TPU v7x, 32 devices: a whole 2x2x4 slice. The times are simulated.
32 devices in a mesh: groups: 2 (over x), seq: 4 (over y, core), tp: 4 (over z).
Axes of the slice: x: 2, y: 2, z: 4, core: 2. Of those that a mesh axis runs over, the one named last changes fastest.
Arguments:
- prefill_states: bfloat16 [8192, 8192], P(('groups', 'seq'), 'tp'), parts along dimension 0, may hold values from -6 to 6
- kv_weight: bfloat16 [8192, 2048], P('tp'), may hold values from -0.0625 to 0.0625
- page_counts: int32 [16], P('groups'), parts along dimension 0, may hold values from 1 to 16, 32 in all
- tail_tokens: int32 [16], P('groups'), parts along dimension 0, may hold values from 1 to 128
- new_query: bfloat16 [16, 2, 8192], P(('groups', 'seq'), None, 'tp'), parts along dimension 0, may hold values from -60 to 60
- new_keyval: bfloat16 [16, 2, 2048], P(('groups', 'seq'), None, 'tp'), parts along dimension 0, may hold values from -6 to 6
- residual: bfloat16 [16, 2, 8192], P('groups', None, 'seq'), parts along dimension 0, may hold values from -6 to 6
- out_weight: bfloat16 [8192, 8192], P('tp', 'seq'), may hold values from -0.0625 to 0.0625
Outputs:
- mixed: float32 [16, 2, 8192], P('groups', None, 'seq'), parts along dimension 0
There are 2 independent parts, one for each index of `groups`. A program takes and returns all parts, laid end to end along the dimension named above; an argument that names none is the same for every part. Nothing has to cross between parts.
Inputs may be any that keep to these rules, and one draw needn't show every extreme that they name: `page_counts`: prompts are laid end to end over the 32 pages of a part in request order; the page counts sum to 32; the longest prompt has exactly 16 pages. Request r is decoded by index r // 2 of seq.
All inputs are finite; a program needn't handle non-finite values.
Results may differ from a plain program's by a relative error of at most 0.025.
Values may be sent and summed in bfloat16 or wider, within the bound.
No kernel may reach another device: no remote copies, remote signals or barrier semaphores. Data moves between devices by JAX's collectives and lax.ppermute only.
A program may use at most 128 MiB of HBM per device.

v0:
```python
import math

import jax
import jax.numpy as jnp
from jax import lax
from jax.sharding import PartitionSpec as P

QH = 64
KVH = 8
HD = 128
PAGE = 128


def rotary(values_in, where_at):
    half_dim = values_in.shape[-1] // 2
    steps = jnp.arange(half_dim, dtype=jnp.float32)
    freqs = jnp.exp(-(steps * (2.0 / values_in.shape[-1])) * math.log(500000.0))
    angles = where_at[..., None] * freqs
    cosine = jnp.cos(angles)
    sine = jnp.sin(angles)
    first = values_in[..., :half_dim]
    second = values_in[..., half_dim:]
    return jnp.concatenate(
        [first * cosine - second * sine, second * cosine + first * sine], axis=-1
    )


def layout(page_counts, tail_tokens):
    page_ends = jnp.cumsum(page_counts)
    starts = page_ends - page_counts
    lengths = (page_counts - 1) * PAGE + tail_tokens
    return (starts, lengths)


def owners(token_index, starts, lengths):
    prompts = starts.shape[0]
    page_index = token_index // PAGE
    covered = (page_index[:, None] >= starts[None, :]).astype(jnp.int32)
    prompt = jnp.sum(covered, axis=1) - 1
    onehot = prompt[:, None] == jnp.arange(prompts, dtype=jnp.int32)[None, :]
    begin_token = jnp.sum(jnp.where(onehot, starts[None, :], 0), axis=1) * PAGE
    limit_len = jnp.sum(jnp.where(onehot, lengths[None, :], 0), axis=1)
    position = token_index - begin_token
    return (prompt, position, position < limit_len)


def absorb(carry_state, query_rows, key_block, value_block, key_mask, scale):
    maxima, totals, summed = carry_state
    scores = (
        jnp.einsum("grqd,gtd->grqt", query_rows, key_block, preferred_element_type=jnp.float32)
        * scale
    )
    scores = jnp.where(key_mask[None, :, None, :], scores, -1e30)
    new_max = jnp.maximum(maxima, jnp.max(scores, axis=-1))
    weights = jnp.where(key_mask[None, :, None, :], jnp.exp(scores - new_max[..., None]), 0.0)
    decay = jnp.exp(maxima - new_max)
    totals = totals * decay + jnp.sum(weights, axis=-1)
    summed = summed * decay[..., None] + jnp.einsum(
        "grqt,gtd->grqd",
        weights.astype(jnp.bfloat16),
        value_block,
        preferred_element_type=jnp.float32,
    )
    return (new_max, totals, summed)


def on_device(
    prefill_states, kv_weight, page_counts, tail_tokens, new_query, new_keyval, residual, out_weight
):
    seq_rank = lax.axis_index("seq")
    n_heads_tp = lax.axis_size("tp")
    local_tokens = prefill_states.shape[0]
    kv_local = KVH // n_heads_tp
    group_size = QH // KVH
    own_rows = new_query.shape[0]
    new_count = new_query.shape[1]
    scale = 1.0 / math.sqrt(HD)
    columns = kv_weight
    columns = columns.reshape(columns.shape[0], lax.axis_size("tp") * kv_local, 2 * HD)
    kv_sum = lax.psum_scatter(
        jnp.einsum(
            "tf,fhc->htc", prefill_states, columns, preferred_element_type=jnp.float32
        ).astype(jnp.bfloat16),
        "tp",
        scatter_dimension=0,
        tiled=True,
    ).astype(jnp.float32)
    starts, lengths = layout(page_counts, tail_tokens)
    token_index = seq_rank * local_tokens + jnp.arange(local_tokens, dtype=jnp.int32)
    prompt, position, is_live = owners(token_index, starts, lengths)
    key_pages = rotary(kv_sum[:, :, :HD], position.astype(jnp.float32)[None, :]).astype(
        jnp.bfloat16
    )
    value_pages = kv_sum[:, :, HD:].astype(jnp.bfloat16)
    own_ids = seq_rank * own_rows + jnp.arange(own_rows, dtype=jnp.int32)
    own_lengths = lax.dynamic_slice_in_dim(lengths, seq_rank * own_rows, own_rows, 0)
    new_pos = (own_lengths[:, None] + jnp.arange(new_count, dtype=jnp.int32)[None, :]).astype(
        jnp.float32
    )
    queries = new_query.astype(jnp.float32).reshape(own_rows, new_count, kv_local, group_size, HD)
    queries = rotary(queries, new_pos[:, :, None, None]).astype(jnp.bfloat16)
    queries = queries.transpose(2, 0, 1, 3, 4).reshape(
        kv_local, own_rows, new_count * group_size, HD
    )
    fresh = new_keyval.astype(jnp.float32).reshape(own_rows, new_count, kv_local, 2, HD)
    fresh_keys = (
        rotary(fresh[:, :, :, 0], new_pos[:, :, None]).astype(jnp.bfloat16).transpose(2, 0, 1, 3)
    )
    fresh_values = fresh[:, :, :, 1].astype(jnp.bfloat16).transpose(2, 0, 1, 3)
    row_step = jnp.arange(new_count * group_size, dtype=jnp.int32) // group_size
    causal = jnp.arange(new_count, dtype=jnp.int32)[None, :] <= row_step[:, None]
    fresh_scores = (
        jnp.einsum("grqd,grmd->grqm", queries, fresh_keys, preferred_element_type=jnp.float32)
        * scale
    )
    fresh_scores = jnp.where(causal[None, None], fresh_scores, -1e30)
    fresh_max = jnp.max(fresh_scores, axis=-1)
    fresh_weights = jnp.where(causal[None, None], jnp.exp(fresh_scores - fresh_max[..., None]), 0.0)
    fresh_totals = jnp.sum(fresh_weights, axis=-1)
    fresh_summed = jnp.einsum(
        "grqm,grmd->grqd",
        fresh_weights.astype(jnp.bfloat16),
        fresh_values,
        preferred_element_type=jnp.float32,
    )
    key_block = lax.all_gather(key_pages, "seq", axis=1, tiled=True)
    value_block = lax.all_gather(value_pages, "seq", axis=1, tiled=True)
    block_index = jnp.arange(key_block.shape[1], dtype=jnp.int32)
    block_prompt, block_pos, block_live = owners(block_index, starts, lengths)
    key_mask = (block_prompt[None, :] == own_ids[:, None]) & block_live[None, :]
    maxima, totals, summed = absorb(
        (fresh_max, fresh_totals, fresh_summed), queries, key_block, value_block, key_mask, scale
    )
    normalized = summed / totals[..., None]
    attended = normalized.reshape(kv_local, own_rows, new_count, group_size, HD).transpose(
        1, 2, 0, 3, 4
    )
    attended = attended.reshape(own_rows, new_count, kv_local * group_size * HD).astype(
        jnp.bfloat16
    )
    partials = jnp.einsum(
        "rnk,kd->rnd",
        lax.all_gather(attended, "seq", axis=0, tiled=True),
        out_weight,
        preferred_element_type=jnp.float32,
    )
    summed_heads = lax.psum(partials, "tp")
    return residual.astype(jnp.float32) + summed_heads


def solution(mesh):
    placed = (
        P(("groups", "seq"), "tp"),
        P("tp", None),
        P("groups"),
        P("groups"),
        P(("groups", "seq"), None, "tp"),
        P(("groups", "seq"), None, "tp"),
        P("groups", None, "seq"),
        P("tp", "seq"),
    )
    return jax.shard_map(
        on_device, mesh=mesh, in_specs=placed, out_specs=P("groups", None, "seq"), check_vma=False
    )
```

profile of v0, /device:TPU:0, one launch (start us, length us, event | category | flops | bytes accessed | tf_op | source)
XLA Modules:
  0.0 218.6 jit_solution(16487618663547934194)
XLA Ops:
  6.5 12.3 %copy.51 = bf16[2048,2048]{0,1:T(8,128)(2,1)} copy(bf16[2048,2048]{1,0:T(8,128)(2,1)} %param.9) | data formatting | bytes 16777216 | tf_op jit(solution)/shard_map/reshape | solution.py:79
  18.9 13.9 %convert_bitcast_fusion = bf16[8,1024,256]{1,2,0:T(8,128)(2,1)} fusion(bf16[2048,8,256]{0,2,1:T(8,128)(2,1)} %bitcast.58, bf16[1024,2048]{1,0:T(8,128)(2,1)} %param.8), kind=kOutput, calls=%fused_computation.6 | convolution fusion | flops 8592031744 | bytes 16777216 | tf_op jit(solution)/shard_map/tf,fhc->htc/dot_general | solution.py:81
  32.8 0.5 copy-done.5
  33.4 0.2 reduce-window.9
  33.6 0.1 convert_reduce_fusion.1
  33.7 0.1 select_reduce_fusion.2
  33.8 1.0 multiply_cosine_fusion
  34.8 77.6 %reduce-scatter.2.cloned.1.call-done = bf16[2,1024,256]{1,2,0:T(8,128)(2,1)} async-done(((bf16[8,1024,256]{1,2,0:T(8,128)(2,1)}), bf16[2,1024,256]{1,2,0:T(8,128)(2,1)}) %reduce-scatter.2.cloned.1.call-update) | async-done | bytes 1048592 | tf_op jit(solution)/shard_map/reduce_scatter | solution.py:80
  112.4 1.5 convert_element_type.71
  113.9 0.2 subtract_convert_fusion
  114.1 0.8 pad_maximum_fusion
  115.1 0.1 dynamic_slice.3
  115.1 0.1 add_convert_fusion.3
  115.2 0.1 multiply_cosine_fusion.1
  115.4 0.1 subtract_convert_fusion.3
  115.5 0.9 slice.50
  116.4 0.1 fusion.36
  116.5 0.2 fusion.38
  116.7 0.1 convert_reduce_fusion
  116.9 0.1 select_reduce_fusion.1
  117.0 0.1 compare_and_fusion
  117.1 21.1 %all-gather.3.cloned.1.call-done = bf16[2,4096,128]{1,2,0:T(8,128)(2,1)} async-done(((bf16[2,1024,128]{1,2,0:T(8,128)(2,1)}), bf16[2,4096,128]{1,2,0:T(8,128)(2,1)}) %all-gather.3.cloned.1.call-update) | async-done | bytes 2097168 | tf_op jit(solution)/shard_map/all_gather | solution.py:126
  138.2 2.2 %fusion.39 = (f32[2,2,16]{2,1,0:T(2,128)S(1)}, f32[2,2,16,4096]{3,2,1,0:T(8,128)S(1)}) fusion(bf16[2,4096,128]{1,2,0:T(8,128)(2,1)} %all-gather.3.cloned.1.call-done, bf16[2,2,2,8,64]{4,3,1,0,2:T(8,128)(2,1)S(1)} %get-tuple-element.12, bf16[2,2,2,8,64]{4,3,1,0,2:T(8,128)(2,1)S(1)} %get-tuple-element.11, pred[2,4096]{1,0:T(4,128)(4,1)S(1)} %compare_and_fusion), kind=kOutput, calls=%fused_computation.92 | convolution fusion | flops 67928000 | bytes 3170560 | tf_op jit(solution)/shard_map/grqd,gtd->grqt/dot_general | solution.py:50
  140.4 0.3 fusion.15
  140.8 21.7 %all-gather.5.cloned.1.call-done = bf16[2,4096,128]{1,2,0:T(8,128)(2,1)} async-done(((bf16[2,1024,128]{1,2,0:T(8,128)(2,1)}), bf16[2,4096,128]{1,2,0:T(8,128)(2,1)}) %all-gather.5.cloned.1.call-update) | async-done | bytes 2097168 | tf_op jit(solution)/shard_map/all_gather | solution.py:127
  162.5 2.4 %fusion.7 = f32[2,2,16,128]{3,2,1,0:T(8,128)S(1)} fusion(bf16[2,4096,128]{1,2,0:T(8,128)(2,1)} %all-gather.5.cloned.1.call-done, f32[2,2,16,4096]{3,2,1,0:T(8,128)S(1)} %get-tuple-element.28, f32[2,2,16]{2,1,0:T(2,128)S(1)} %max.13, pred[2,4096]{1,0:T(4,128)(4,1)S(1)} %compare_and_fusion), kind=kOutput, calls=%fused_computation.7 | convolution fusion | flops 67895296 | bytes 3186944 | tf_op jit(solution)/shard_map/grqt,gtd->grqd/dot_general | solution.py:58
  164.9 0.2 fusion.13
  165.2 5.2 %all_gather.11 = bf16[8,2,2048]{2,1,0:T(2,128)(2,1)S(1)} all-gather(bf16[2,2,2048]{2,1,0:T(2,128)(2,1)S(1)} %convert_element_type.78), channel_id=1, replica_groups=mesh['groups'=2,'seq'=4,'tp'=4] {'seq'}, dimensions={0}, use_global_device_ids=true | all-gather | bytes 81920 | tf_op jit(solution)/shard_map/all_gather | solution.py:143
  170.4 5.3 %fusion = f32[8,2,2048]{2,0,1:T(8,128)} fusion(bf16[2048,2048]{1,0:T(8,128)(2,1)} %param.15, bf16[8,2,2048]{2,1,0:T(2,128)(2,1)S(1)} %all_gather.11), kind=kOutput, calls=%fused_computation | convolution fusion | flops 134217728 | bytes 8585216 | tf_op jit(solution)/shard_map/rnk,kd->rnd/dot_general | solution.py:141
  175.7 34.6 %all-reduce.2.cloned.1.call-done = f32[8,2,2048]{2,0,1:T(8,128)} async-done(((f32[8,2,2048]{2,0,1:T(8,128)}), f32[8,2,2048]{2,0,1:T(8,128)}) %all-reduce.2.cloned.1.call-update) | async-done | bytes 131088 | tf_op jit(solution)/shard_map/psum | solution.py:147
  210.3 0.9 convert_add_fusion
  211.3 0.8 copy.48
  (40 shorter events, 0.4 us)
Async XLA Ops:
  6.5 105.8 %reduce-scatter.2.cloned.1.call-start = ((), (), s32[]{:S(2)}) async-start(), calls=%async_computation.1 | async-start | bytes 5242880 | tf_op jit(solution)/shard_map/reduce_scatter | solution.py:80
  32.7 0.7 copy-start.5
  32.7 0.9 copy-start.4
  32.7 82.3 %copy-start.2 = (bf16[2,2,2048]{2,1,0:T(2,128)(2,1)S(1)}, bf16[2,2,2048]{2,1,0:T(2,128)(2,1)}, u32[]{:S(2)}) copy-start(bf16[2,2,2048]{2,1,0:T(2,128)(2,1)} %param.12) | copy-start | bytes 49156
  32.8 82.3 %copy-start.3 = (bf16[2,2,512]{2,1,0:T(2,128)(2,1)S(1)}, bf16[2,2,512]{2,1,0:T(2,128)(2,1)}, u32[]{:S(2)}) copy-start(bf16[2,2,512]{2,1,0:T(2,128)(2,1)} %param.13) | copy-start | bytes 12292
  32.8 105.4 %all-gather.3.cloned.1.call-start = ((), (), s32[]{:S(2)}) async-start(), calls=%async_computation.2 | async-start | bytes 2621440 | tf_op jit(solution)/shard_map/all_gather | solution.py:126
  112.4 3.1 %copy-start = (bf16[2,1024,256]{1,2,0:T(8,128)(2,1)S(1)}, bf16[2,1024,256]{1,2,0:T(8,128)(2,1)}, u32[]{:S(2)}) copy-start(bf16[2,1024,256]{1,2,0:T(8,128)(2,1)} %reduce-scatter.2.cloned.1.call-done) | copy-start | bytes 3145732
  114.9 47.5 %all-gather.5.cloned.1.call-start = ((), (), s32[]{:S(2)}) async-start(), calls=%async_computation.3 | async-start | bytes 2621440 | tf_op jit(solution)/shard_map/all_gather | solution.py:127
  116.3 94.0 %all-reduce.2.cloned.1.call-start = ((), (), s32[]{:S(2)}) async-start(), calls=%async_computation.4 | async-start | bytes 262144 | tf_op jit(solution)/shard_map/psum | solution.py:147
  170.4 39.9 %copy-start.1 = (bf16[8,2,2048]{2,1,0:T(2,128)(2,1)S(1)}, bf16[8,2,2048]{2,1,0:T(2,128)(2,1)}, u32[]{:S(2)}) copy-start(bf16[8,2,2048]{2,1,0:T(2,128)(2,1)} %param.14) | copy-start | bytes 196612
Sparse Core Ops, SparseCore 0:
  32.9 79.4 reduce-scatter.1
  115.1 23.0 all-gather.2
  139.8 22.5 all-gather.4
  175.8 34.4 all-reduce.1
where the time goes:
time: 219 us
  waiting for transfers between devices  155 us (71%)
  matrix products  24.2 us (11%)
  local copies, waits for them, and re-layouts  14.7 us (7%)
  between operations  13.3 us (6%)
  other arithmetic  5.92 us (3%)
  blocking collectives  5.25 us (2%)
    reduce_scatter x1, waiting for transfers between devices, on_device(): lax.psum_scatter(jnp.einsum('tf,fhc->htc', prefill_states, columns, prefe...  77.6 us
    psum x1, waiting for transfers between devices, on_device(): summed_heads = lax.psum(partials, 'tp')  34.6 us
    all_gather x1, waiting for transfers between devices, on_device(): value_block = lax.all_gather(value_pages, 'seq', axis=1, tiled=True)  21.7 us
    all_gather x1, waiting for transfers between devices, on_device(): key_block = lax.all_gather(key_pages, 'seq', axis=1, tiled=True)  21.1 us
    dot_general x1, matrix products, on_device(): jnp.einsum('tf,fhc->htc', prefill_states, columns, preferred_element_type...  13.9 us
    reshape x1, local copies, waits for them, and re-layouts, on_device(): columns.reshape(columns.shape[0], lax.axis_size('tp') * kv_local, 2 * HD)  12.3 us
    dot_general x1, matrix products, on_device(): jnp.einsum('rnk,kd->rnd', lax.all_gather(attended, 'seq', axis=0, tiled=T...  5.26 us
    all_gather x1, blocking collectives, on_device(): lax.all_gather(attended, 'seq', axis=0, tiled=True)  5.25 us
  transfers between devices with their start and end apart: 4, of which 4 were waited for; matrix products, arithmetic and copies ran while one was open for 3% of the time, Pallas kernels for 0%

commit v1 on v0

v1 whole, which is shorter than its diff:
```python
import functools
import math

import jax
import jax.numpy as jnp
from jax import lax
from jax.experimental import pallas as pl
from jax.experimental.pallas import tpu as pltpu
from jax.sharding import PartitionSpec as P

QH = 64
KVH = 8
HD = 128
PAGE = 128
GROUP = QH // KVH
NEG = -1e30
F32 = jnp.float32
BF16 = jnp.bfloat16
MIB = 1 << 20

VMEM = pl.BlockSpec(memory_space=pltpu.VMEM)
SMEM = pl.BlockSpec(memory_space=pltpu.SMEM)


def shifts(value, axis):
    size = lax.axis_size(axis)
    return [value] + [
        lax.ppermute(value, axis, [(i, (i + d) % size) for i in range(size)])
        for d in range(1, size)
    ]


def exchange(chunks, axis):
    size = lax.axis_size(axis)
    return [chunks[0]] + [
        lax.ppermute(chunks[d], axis, [(i, (i + d) % size) for i in range(size)])
        for d in range(1, size)
    ]


def lane_freqs(rows):
    lane = lax.broadcasted_iota(jnp.int32, (rows, HD), 1) % (HD // 2)
    return jnp.exp(-(lane.astype(F32) * (2.0 / HD)) * math.log(500000.0))


def sine_sign(rows):
    lane = lax.broadcasted_iota(jnp.int32, (rows, HD), 1)
    return jnp.where(lane < HD // 2, -1.0, 1.0)


def ring(axis, back):
    size = lax.axis_size(axis)
    return lax.rem(lax.axis_index(axis) + size - back, size)


def ahead(axis, forward):
    return lax.rem(lax.axis_index(axis) + forward, lax.axis_size(axis))


def keys_kernel(pages, prompts, x_ref, wa_ref, wb_ref, counts, tails, out_ref, meta, cos_s, sin_s):
    step = pl.program_id(0)
    tokens = x_ref.shape[0]
    local_pages = tokens // PAGE

    @pl.when(step == 0)
    def _():
        def one_prompt(r, start):
            length = (counts[r] - 1) * PAGE + tails[r]
            meta[3 * pages + r] = length

            def one_page(i, carry):
                meta[start + i] = r
                meta[pages + start + i] = i * PAGE
                meta[2 * pages + start + i] = jnp.minimum(length - i * PAGE, PAGE)
                return carry

            lax.fori_loop(0, counts[r], one_page, 0)
            return start + counts[r]

        lax.fori_loop(0, prompts, one_prompt, 0)
        freqs = lane_freqs(PAGE)
        offset = lax.broadcasted_iota(jnp.int32, (PAGE, HD), 0).astype(F32) * freqs
        cos_off, sin_off = jnp.cos(offset), jnp.sin(offset)
        row_freqs = lane_freqs(8)
        sign = sine_sign(PAGE)
        first = lax.axis_index("seq") * local_pages
        for p in range(local_pages):
            base = meta[pages + first + p].astype(F32) * row_freqs
            cos_base, sin_base = jnp.cos(base)[:1], jnp.sin(base)[:1]
            cos_s[p * PAGE : (p + 1) * PAGE] = cos_off * cos_base - sin_off * sin_base
            sin_s[p * PAGE : (p + 1) * PAGE] = sign * (sin_off * cos_base + cos_off * sin_base)

    weight = jnp.concatenate([wa_ref[...], wb_ref[...]], axis=1)

    def rows(i, carry):
        at = pl.ds(pl.multiple_of(i * 256, 256), 256)
        product = jnp.dot(x_ref[at], weight, preferred_element_type=F32)
        cosine, sine = cos_s[at], sin_s[at]
        for half in range(2):
            k = product[:, half * HD : (half + 1) * HD]
            k = k * cosine + pltpu.roll(k, HD // 2, 1) * sine
            out_ref[at, half * HD : (half + 1) * HD] = k.astype(BF16)
        return carry

    lax.fori_loop(0, tokens // 256, rows, 0)


def values_kernel(x_ref, wa_ref, wb_ref, out_ref):
    weight = jnp.concatenate([wa_ref[...], wb_ref[...]], axis=1)

    def rows(i, carry):
        at = pl.ds(pl.multiple_of(i * 256, 256), 256)
        out_ref[at] = jnp.dot(x_ref[at], weight, preferred_element_type=F32).astype(BF16)
        return carry

    lax.fori_loop(0, x_ref.shape[0] // 256, rows, 0)


def project_keys(x, kv_weight, counts, tails, pages):
    tokens, depth = x.shape
    prompts = counts.shape[0]
    return pl.pallas_call(
        functools.partial(keys_kernel, pages, prompts),
        grid=(KVH // 2,),
        in_specs=[
            pl.BlockSpec((tokens, depth), lambda i: (0, 0)),
            pl.BlockSpec((depth, HD), lambda i: (0, 4 * i)),
            pl.BlockSpec((depth, HD), lambda i: (0, 4 * i + 2)),
            SMEM,
            SMEM,
        ],
        out_specs=[pl.BlockSpec((tokens, 2 * HD), lambda i: (0, i)), SMEM],
        out_shape=[
            jax.ShapeDtypeStruct((tokens, KVH * HD), BF16),
            jax.ShapeDtypeStruct((3 * pages + prompts,), jnp.int32),
        ],
        scratch_shapes=[pltpu.VMEM((tokens, HD), F32), pltpu.VMEM((tokens, HD), F32)],
        compiler_params=pltpu.CompilerParams(vmem_limit_bytes=40 * MIB),
        cost_estimate=pl.CostEstimate(
            flops=2 * tokens * depth * KVH * HD, bytes_accessed=12 * MIB, transcendentals=0
        ),
        name="keys",
    )(x, kv_weight, kv_weight, counts, tails)


def project_values(x, kv_weight):
    tokens, depth = x.shape
    return pl.pallas_call(
        values_kernel,
        grid=(KVH // 2,),
        in_specs=[
            pl.BlockSpec((tokens, depth), lambda i: (0, 0)),
            pl.BlockSpec((depth, HD), lambda i: (0, 4 * i + 1)),
            pl.BlockSpec((depth, HD), lambda i: (0, 4 * i + 3)),
        ],
        out_specs=pl.BlockSpec((tokens, 2 * HD), lambda i: (0, i)),
        out_shape=jax.ShapeDtypeStruct((tokens, KVH * HD), BF16),
        compiler_params=pltpu.CompilerParams(vmem_limit_bytes=40 * MIB),
        cost_estimate=pl.CostEstimate(
            flops=2 * tokens * depth * KVH * HD, bytes_accessed=12 * MIB, transcendentals=0
        ),
        name="values",
    )(x, kv_weight, kv_weight)


def scores_kernel(pages, own_rows, n_seq, n_tp, *refs):
    pieces = refs[:n_seq]
    k_ref, meta = refs[n_seq : n_seq + 2]
    outs = refs[n_seq + 2 : n_seq + 2 + n_tp]
    own_ref, all_q = refs[n_seq + 2 + n_tp :]
    kv_local = KVH // n_tp
    local_pages = k_ref.shape[0] // PAGE
    new_count = pieces[0].shape[2]
    rows = new_count * GROUP
    freqs = lane_freqs(8)
    sign = sine_sign(8)
    for ds in range(n_seq):
        for rr in range(own_rows):
            request = ring("seq", ds) * own_rows + rr
            length = meta[3 * pages + request]
            cosines, sines = [], []
            for n in range(new_count):
                angle = (length + n).astype(F32) * freqs
                cosines.append(jnp.cos(angle))
                sines.append(jnp.sin(angle) * sign)
            for dt in range(n_tp):
                heads = [pieces[ds][dt, rr, n].astype(F32) for n in range(new_count)]
                for g in range(kv_local):
                    parts = []
                    for n in range(new_count):
                        q = heads[n][g * GROUP : (g + 1) * GROUP]
                        parts.append(q * cosines[n] + pltpu.roll(q, HD // 2, 1) * sines[n])
                    block = jnp.concatenate(parts, axis=0).astype(BF16)
                    at = (ring("tp", dt) * kv_local + g) * rows
                    all_q[request, pl.ds(pl.multiple_of(at, rows), rows)] = block
                    if dt == 0:
                        own_ref[request, g * rows : (g + 1) * rows] = block
    first = lax.axis_index("seq") * local_pages

    def one_page(p, carry):
        request = meta[first + p]
        tokens = pl.ds(pl.multiple_of(p * PAGE, PAGE), PAGE)
        for dt in range(n_tp):
            for g in range(kv_local):
                head = ahead("tp", dt) * kv_local + g
                k = k_ref[tokens, pl.ds(pl.multiple_of(head * HD, HD), HD)]
                q = all_q[request, pl.ds(pl.multiple_of(head * rows, rows), rows)]
                s = lax.dot_general(q, k, (((1,), (1,)), ((), ())), preferred_element_type=F32)
                outs[dt][g * rows : (g + 1) * rows, tokens] = (s * (1.0 / math.sqrt(HD))).astype(
                    BF16
                )
        return carry

    lax.fori_loop(0, local_pages, one_page, 0)


def partial_scores(pieces, k, meta, pages, prompts):
    n_seq, n_tp = lax.axis_size("seq"), lax.axis_size("tp")
    own_rows, new_count = pieces[0].shape[1], pieces[0].shape[2]
    tokens = k.shape[0]
    rows = KVH // n_tp * new_count * GROUP
    return pl.pallas_call(
        functools.partial(scores_kernel, pages, own_rows, n_seq, n_tp),
        in_specs=[VMEM] * (n_seq + 1) + [SMEM],
        out_specs=[VMEM] * (n_tp + 1),
        out_shape=[jax.ShapeDtypeStruct((rows, tokens), BF16)] * n_tp
        + [jax.ShapeDtypeStruct((prompts, rows, HD), BF16)],
        scratch_shapes=[pltpu.VMEM((prompts, rows * n_tp, HD), BF16)],
        compiler_params=pltpu.CompilerParams(vmem_limit_bytes=32 * MIB),
        cost_estimate=pl.CostEstimate(
            flops=2 * tokens * rows * n_tp * HD, bytes_accessed=3 * MIB, transcendentals=0
        ),
        name="scores",
    )(*pieces, k, meta)


def weights_kernel(pages, n_tp, *refs):
    chunks = refs[:n_tp]
    meta, w_ref, stats_ref = refs[n_tp:]
    rows, tokens = w_ref.shape
    local_pages = tokens // PAGE
    first = lax.axis_index("seq") * local_pages
    scores, maxima = [], []
    lane = lax.broadcasted_iota(jnp.int32, (rows, PAGE), 1)
    masks = []
    for p in range(local_pages):
        at = slice(p * PAGE, (p + 1) * PAGE)
        total = chunks[0][:, at].astype(F32)
        for d in range(1, n_tp):
            total = total + chunks[d][:, at].astype(F32)
        mask = lane < meta[2 * pages + first + p]
        total = jnp.where(mask, total, NEG)
        masks.append(mask)
        scores.append(total)
        maxima.append(jnp.max(total, axis=1, keepdims=True))
    stats = jnp.zeros((rows, PAGE), F32)
    for p in range(local_pages):
        top = maxima[p]
        for other in range(local_pages):
            if other != p:
                same = meta[first + p] == meta[first + other]
                top = jnp.where(same, jnp.maximum(top, maxima[other]), top)
        w = jnp.where(masks[p], jnp.exp(scores[p] - top), 0.0)
        w_ref[:, p * PAGE : (p + 1) * PAGE] = w.astype(BF16)
        stats = jnp.where(lane == p, top, stats)
        stats = jnp.where(lane == local_pages + p, jnp.sum(w, axis=1, keepdims=True), stats)
    stats_ref[...] = stats


def softmax_weights(chunks, meta, pages):
    n_tp = len(chunks)
    rows, tokens = chunks[0].shape
    return pl.pallas_call(
        functools.partial(weights_kernel, pages, n_tp),
        in_specs=[VMEM] * n_tp + [SMEM],
        out_specs=[VMEM, VMEM],
        out_shape=[
            jax.ShapeDtypeStruct((rows, tokens), BF16),
            jax.ShapeDtypeStruct((rows, PAGE), F32),
        ],
        name="weights",
    )(*chunks, meta)


def weighted_kernel(pages, n_tp, *refs):
    pieces = refs[:n_tp]
    v_ref, meta = refs[n_tp : n_tp + 2]
    outs = refs[n_tp + 2 : n_tp + 2 + n_tp]
    total = refs[-1]
    kv_local = KVH // n_tp
    rows_local = pieces[0].shape[0]
    rows = rows_local // kv_local
    local_pages = v_ref.shape[0] // PAGE
    first = lax.axis_index("seq") * local_pages
    total[...] = jnp.zeros_like(total)

    def one_page(p, carry):
        request = meta[first + p]
        tokens = pl.ds(pl.multiple_of(p * PAGE, PAGE), PAGE)
        for dt in range(n_tp):
            for g in range(kv_local):
                head = ring("tp", dt) * kv_local + g
                v = v_ref[tokens, pl.ds(pl.multiple_of(head * HD, HD), HD)]
                w = pieces[dt][g * rows : (g + 1) * rows, tokens]
                at = pl.ds(pl.multiple_of(head * rows, rows), rows)
                total[request, at] += jnp.dot(w, v, preferred_element_type=F32)
        return carry

    lax.fori_loop(0, local_pages, one_page, 0)
    for dt in range(n_tp):
        at = pl.ds(pl.multiple_of(ahead("tp", dt) * rows_local, rows_local), rows_local)
        outs[dt][...] = total[:, at].astype(BF16)


def weighted_values(pieces, v, meta, pages, prompts):
    n_tp = len(pieces)
    rows, tokens = pieces[0].shape
    return pl.pallas_call(
        functools.partial(weighted_kernel, pages, n_tp),
        in_specs=[VMEM] * (n_tp + 1) + [SMEM],
        out_specs=[VMEM] * n_tp,
        out_shape=[jax.ShapeDtypeStruct((prompts, rows, HD), BF16)] * n_tp,
        scratch_shapes=[pltpu.VMEM((prompts, rows * n_tp, HD), F32)],
        compiler_params=pltpu.CompilerParams(vmem_limit_bytes=32 * MIB),
        name="weighted",
    )(*pieces, v, meta)


def merge_kernel(pages, own_rows, n_seq, *refs):
    stats = refs[:n_seq]
    fresh = refs[n_seq : 2 * n_seq]
    q_ref, meta, factor_ref, add_ref, all_stats, tops, sums = refs[2 * n_seq :]
    prompts, rows_local, _ = q_ref.shape
    new_count = fresh[0].shape[1]
    rows = new_count * GROUP
    kv_local = rows_local // rows
    local_pages = pages // n_seq
    scale = 1.0 / math.sqrt(HD)
    freqs = lane_freqs(8)
    sign = sine_sign(8)
    step = lax.broadcasted_iota(jnp.int32, (rows, HD), 0) // GROUP
    for ds in range(n_seq):
        all_stats[ring("seq", ds)] = stats[ds][...]
    kept = []
    for ds in range(n_seq):
        for rr in range(own_rows):
            request = ring("seq", ds) * own_rows + rr
            length = meta[3 * pages + request]
            for g in range(kv_local):
                q = q_ref[request, g * rows : (g + 1) * rows].astype(F32)
                points = []
                for n in range(new_count):
                    angle = (length + n).astype(F32) * freqs
                    cosine, sine = jnp.cos(angle)[:1], (jnp.sin(angle) * sign)[:1]
                    both = fresh[ds][rr, n].astype(F32)
                    k = both[2 * g : 2 * g + 1]
                    k = k * cosine + pltpu.roll(k, HD // 2, 1) * sine
                    k = k.astype(BF16).astype(F32)
                    s = jnp.sum(q * k, axis=1, keepdims=True) * scale
                    s = jnp.broadcast_to(s, (rows, HD))
                    points.append((jnp.where(step >= n, s, NEG), both[2 * g + 1 : 2 * g + 2]))
                top = points[0][0]
                for s, _ in points[1:]:
                    top = jnp.maximum(top, s)
                at = slice(g * rows, (g + 1) * rows)
                tops[request, at] = top
                kept.append((request, at, points))

    def grow(page, carry):
        request = meta[page]
        block = all_stats[page // local_pages]
        lane = lax.broadcasted_iota(jnp.int32, block.shape, 1)
        here = lane == page % local_pages
        top = jnp.max(jnp.where(here, block, 2 * NEG), axis=1, keepdims=True)
        tops[request] = jnp.maximum(tops[request], top)
        return carry

    lax.fori_loop(0, pages, grow, 0)
    for request, at, points in kept:
        part = jnp.zeros((rows, HD), F32)
        weighted = jnp.zeros((rows, HD), F32)
        for n, (s, value) in enumerate(points):
            w = jnp.where(step >= n, jnp.exp(s - tops[request, at]), 0.0)
            part = part + w
            weighted = weighted + w * value
        sums[request, at] = part
        add_ref[request, at] = weighted

    def collect(page, carry):
        request = meta[page]
        block = all_stats[page // local_pages]
        lane = lax.broadcasted_iota(jnp.int32, block.shape, 1)
        place = page % local_pages
        top = jnp.sum(jnp.where(lane == place, block, 0.0), axis=1, keepdims=True)
        part = jnp.sum(jnp.where(lane == local_pages + place, block, 0.0), axis=1, keepdims=True)
        sums[request] += part * jnp.exp(top - tops[request])
        return carry

    lax.fori_loop(0, pages, collect, 0)
    factor_ref[...] = jnp.zeros_like(factor_ref)
    first = lax.axis_index("seq") * local_pages
    mine = stats[0][...]

    for p in range(local_pages):
        request = meta[first + p]
        factor_ref[request] = jnp.exp(mine[:, p : p + 1] - tops[request]) / sums[request]
    add_ref[...] = add_ref[...] / sums[...]


def merge(stats, fresh, own_q, meta, pages):
    n_seq = len(stats)
    prompts, rows, _ = own_q.shape
    own_rows = fresh[0].shape[0]
    return pl.pallas_call(
        functools.partial(merge_kernel, pages, own_rows, n_seq),
        in_specs=[VMEM] * (2 * n_seq + 1) + [SMEM],
        out_specs=[VMEM, VMEM],
        out_shape=[jax.ShapeDtypeStruct((prompts, rows, HD), F32)] * 2,
        scratch_shapes=[
            pltpu.VMEM((n_seq,) + stats[0].shape, F32),
            pltpu.VMEM((prompts, rows, HD), F32),
            pltpu.VMEM((prompts, rows, HD), F32),
        ],
        name="merge",
    )(*stats, *fresh, own_q, meta)


def scaled_kernel(n_tp, *refs):
    chunks = refs[:n_tp]
    factor_ref, out_ref = refs[n_tp:]
    total = chunks[0][...].astype(F32)
    for d in range(1, n_tp):
        total = total + chunks[d][...].astype(F32)
    out_ref[...] = (total * factor_ref[...]).astype(BF16)


def scaled_sum(chunks, factor):
    n_tp = len(chunks)
    return pl.pallas_call(
        functools.partial(scaled_kernel, n_tp),
        in_specs=[VMEM] * (n_tp + 1),
        out_specs=VMEM,
        out_shape=jax.ShapeDtypeStruct(chunks[0].shape, BF16),
        name="scaled",
    )(*chunks, factor)


def output_kernel(n_seq, new_count, *refs):
    pieces = refs[:n_seq]
    add_ref, w_ref, out_ref, held = refs[n_seq:]
    prompts, rows_local, _ = add_ref.shape
    rows = new_count * GROUP
    kv_local = rows_local // rows

    @pl.when(pl.program_id(0) == 0)
    def _():
        for r in range(prompts):
            total = add_ref[r]
            for d in range(n_seq):
                total = total + pieces[d][r].astype(F32)
            for g in range(kv_local):
                for n in range(new_count):
                    at = g * rows + n * GROUP
                    held[g * GROUP : (g + 1) * GROUP, r * new_count + n] = total[at : at + GROUP]

    heads = kv_local * GROUP
    left = jnp.concatenate([held[h].astype(BF16) for h in range(heads)], axis=1)
    out_ref[...] = jnp.dot(left, w_ref[...], preferred_element_type=F32).astype(BF16)


def output_partial(pieces, add, out_weight, new_count):
    n_seq = len(pieces)
    prompts, rows, _ = add.shape
    depth, columns = out_weight.shape
    width = min(columns, 512)
    whole = pl.BlockSpec((prompts, rows, HD), lambda i: (0, 0, 0))
    return pl.pallas_call(
        functools.partial(output_kernel, n_seq, new_count),
        grid=(columns // width,),
        in_specs=[whole] * (n_seq + 1) + [pl.BlockSpec((depth, width), lambda i: (0, i))],
        out_specs=pl.BlockSpec((prompts * new_count, width), lambda i: (0, i)),
        out_shape=jax.ShapeDtypeStruct((prompts * new_count, columns), BF16),
        scratch_shapes=[pltpu.VMEM((depth // HD, prompts * new_count, HD), F32)],
        compiler_params=pltpu.CompilerParams(vmem_limit_bytes=32 * MIB),
        name="output",
    )(*pieces, add, out_weight)


def final_kernel(n_tp, *refs):
    pieces = refs[:n_tp]
    res_ref, out_ref = refs[n_tp:]
    prompts, new_count, _ = out_ref.shape
    total = pieces[0][...].astype(F32)
    for d in range(1, n_tp):
        total = total + pieces[d][...].astype(F32)
    for r in range(prompts):
        out_ref[r] = res_ref[r].astype(F32) + total[r * new_count : (r + 1) * new_count]


def final_sum(pieces, residual):
    n_tp = len(pieces)
    return pl.pallas_call(
        functools.partial(final_kernel, n_tp),
        in_specs=[VMEM] * (n_tp + 1),
        out_specs=VMEM,
        out_shape=jax.ShapeDtypeStruct(residual.shape, F32),
        name="final",
    )(*pieces, residual)


def on_device(
    prefill_states, kv_weight, page_counts, tail_tokens, new_query, new_keyval, residual, out_weight
):
    n_seq, n_tp = lax.axis_size("seq"), lax.axis_size("tp")
    own_rows, new_count, _ = new_query.shape
    prompts = page_counts.shape[0]
    pages = prefill_states.shape[0] // PAGE * n_seq
    heads = QH // n_tp
    query = new_query.reshape(own_rows, new_count, heads, HD)
    query = jnp.stack(shifts(query, "tp"))
    fresh = new_keyval.reshape(own_rows, new_count, 2 * KVH // n_tp, HD)
    fresh = shifts(fresh, "seq")
    k, meta = project_keys(prefill_states, kv_weight, page_counts, tail_tokens, pages)
    queries = shifts(query, "seq")
    v = project_values(prefill_states, kv_weight)
    *chunks, own_q = partial_scores(queries, k, meta, pages, prompts)
    weights, stats = softmax_weights(exchange(chunks, "tp"), meta, pages)
    stats = shifts(stats, "seq")
    chunks = weighted_values(shifts(weights, "tp"), v, meta, pages, prompts)
    factor, add = merge(stats, fresh, own_q, meta, pages)
    part = scaled_sum(exchange(chunks, "tp"), factor)
    partial = output_partial(shifts(part, "seq"), add, out_weight, new_count)
    return final_sum(shifts(partial, "tp"), residual)


def solution(mesh):
    placed = (
        P(("groups", "seq"), "tp"),
        P("tp", None),
        P("groups"),
        P("groups"),
        P(("groups", "seq"), None, "tp"),
        P(("groups", "seq"), None, "tp"),
        P("groups", None, "seq"),
        P("tp", "seq"),
    )
    return jax.shard_map(
        on_device, mesh=mesh, in_specs=placed, out_specs=P("groups", None, "seq"), check_vma=False
    )
```

time: 219 us -> 116 us (0.53)
  waiting for transfers between devices: 155 us -> 22.1 us
  Pallas kernels: 0 us -> 42 us
  starting transfers between devices: 0.13 us -> 33.5 us
  matrix products: 24.2 us -> 0 us
  between operations: 13.3 us -> 0.27 us
  other arithmetic: 5.92 us -> 0.01 us
  blocking collectives: 5.25 us -> 0 us
  local copies, waits for them, and re-layouts: 14.7 us -> 17.2 us
    reduce_scatter x1 -> x0, waiting for transfers between devices: 77.6 us -> none  [on_device(): lax.psum_scatter(jnp.einsum('tf,fhc->htc', prefill_states, columns, prefe...]
    all_gather x2 -> x0, waiting for transfers between devices: 42.8 us -> none  [the longest x1 21.7 us: on_device(): value_block = lax.all_gather(value_pages, 'seq', axis=1, tiled=True)]
    pallas_call x0 -> x9, Pallas kernels: none -> 42 us  [the longest x1 11.6 us: project_keys(): pl.pallas_call(functools.partial(keys_kernel, pages, prompts), grid=(KVH...]
    psum x1 -> x0, waiting for transfers between devices: 34.6 us -> none  [on_device(): summed_heads = lax.psum(partials, 'tp')]
    ppermute x0 -> x27, starting transfers between devices: none -> 33.5 us  [the longest x21 24.5 us: shifts(): lax.ppermute(value, axis, [(i, (i + d) % size) for i in range(size)])]
    dot_general x6 -> x0, matrix products: 24.2 us -> none  [the longest x1 13.9 us: on_device(): jnp.einsum('tf,fhc->htc', prefill_states, columns, preferred_element_type...]
    ppermute x0 -> x27, waiting for transfers between devices: none -> 22.1 us  [the longest x21 18.5 us: shifts(): lax.ppermute(value, axis, [(i, (i + d) % size) for i in range(size)])]
    unnamed x12 -> x64, local copies, waits for them, and re-layouts: 0.57 us -> 15.8 us
  transfers between devices with their start and end apart: 4 -> 27, of which waited for: 4 -> 13; matrix products, arithmetic and copies ran while one was open for 3% -> 1% of each run, Pallas kernels for 0% -> 25%
where the time goes in v1:
time: 116 us; the launch traced here: 115 us
  Pallas kernels  42 us (36%)
  starting transfers between devices  33.5 us (29%)
  waiting for transfers between devices  22.1 us (19%)
  local copies, waits for them, and re-layouts  17.2 us (15%)
    ppermute x21, starting transfers between devices, shifts(): lax.ppermute(value, axis, [(i, (i + d) % size) for i in range(size)])  24.5 us
    ppermute x21, waiting for transfers between devices, shifts(): lax.ppermute(value, axis, [(i, (i + d) % size) for i in range(size)])  18.5 us
    unnamed x64, local copies, waits for them, and re-layouts  15.8 us
    pallas_call x1, Pallas kernels, project_keys(): pl.pallas_call(functools.partial(keys_kernel, pages, prompts), grid=(KVH...  11.6 us
    ppermute x6, starting transfers between devices, exchange(): lax.ppermute(chunks[d], axis, [(i, (i + d) % size) for i in range(size)])  9 us
    pallas_call x1, Pallas kernels, project_values(): pl.pallas_call(values_kernel, grid=(KVH // 2,), in_specs=[pl.BlockSpec((t...  8.91 us
    pallas_call x1, Pallas kernels, merge(): pl.pallas_call(functools.partial(merge_kernel, pages, own_rows, n_seq), i...  8.78 us
    ppermute x6, waiting for transfers between devices, exchange(): lax.ppermute(chunks[d], axis, [(i, (i + d) % size) for i in range(size)])  3.62 us
  transfers between devices with their start and end apart: 27, of which 13 were waited for; matrix products, arithmetic and copies ran while one was open for 1% of the time, Pallas kernels for 25%

profile of v1, /device:TPU:0, one launch (start us, length us, event | category | flops | bytes accessed | tf_op | source)
XLA Modules:
  0.0 115.1 jit_solution(12228378219637219358)
XLA Ops:
  0.7 5.1 %collective-permute-start.2 = (bf16[2,2,16,128]{3,2,1,0:T(8,128)(2,1)S(1)}, bf16[2,2,16,128]{3,2,1,0:T(8,128)(2,1)S(1)}, u32[]{:S(2)}, u32[]{:S(2)}) collective-permute-start(bf16[2,2,16,128]{3,2,1,0:T(8,128)(2,1)S(1)} %reshape.6), channel_id=1, source_target_pairs={{0,3},{1,0},{2,1},{3,2},{4,7},{5,4},{6,5},{7,6},{8,11},{9,8},{10,9... | collective-permute-start | bytes 49160 | tf_op jit(solution)/shard_map/ppermute | solution.py:28
  7.6 2.9 %collective-permute-done.1 = bf16[2,2,16,128]{3,2,1,0:T(8,128)(2,1)S(1)} collective-permute-done((bf16[2,2,16,128]{3,2,1,0:T(8,128)(2,1)S(1)}, bf16[2,2,16,128]{3,2,1,0:T(8,128)(2,1)S(1)}, u32[]{:S(2)}, u32[]{:S(2)}) %collective-permute-start.1) | collective-permute-done | bytes 16416 | tf_op jit(solution)/shard_map/ppermute | solution.py:28
  11.5 1.6 %collective-permute-start.4 = (bf16[4,2,2,16,128]{4,3,2,1,0:T(8,128)(2,1)S(1)}, bf16[4,2,2,16,128]{4,3,2,1,0:T(8,128)(2,1)S(1)}, u32[]{:S(2)}, u32[]{:S(2)}) collective-permute-start(bf16[4,2,2,16,128]{4,3,2,1,0:T(8,128)(2,1)S(1)} %pad_maximum_fusion.refs_0_), channel_id=1, source_target_pairs={{0,8},{4,12},{8,0},{12,4},{1,9},{5,13},{9,1},{13,5},{2,10},{6,14},... | collective-permute-start | bytes 196616 | tf_op jit(solution)/shard_map/ppermute | solution.py:28
  13.0 1.4 %collective-permute-start.5 = (bf16[4,2,2,16,128]{4,3,2,1,0:T(8,128)(2,1)S(1)}, bf16[4,2,2,16,128]{4,3,2,1,0:T(8,128)(2,1)S(1)}, u32[]{:S(2)}, u32[]{:S(2)}) collective-permute-start(bf16[4,2,2,16,128]{4,3,2,1,0:T(8,128)(2,1)S(1)} %pad_maximum_fusion.refs_0_), channel_id=1, source_target_pairs={{0,12},{4,0},{8,4},{12,8},{1,13},{5,1},{9,5},{13,9},{2,14},{6,2},{... | collective-permute-start | bytes 196616 | tf_op jit(solution)/shard_map/ppermute | solution.py:28
  14.4 2.2 %copy-done = bf16[1024,2048]{1,0:T(8,128)(2,1)S(1)} copy-done((bf16[1024,2048]{1,0:T(8,128)(2,1)S(1)}, bf16[1024,2048]{1,0:T(8,128)(2,1)}, u32[]{:S(2)}) %copy-start) | copy-done | bytes 4194328
  17.9 11.6 %keys.1 = (bf16[1024,1024]{1,0:T(8,128)(2,1)S(1)}, s32[104]{0:T(128)S(1)}) custom-call(bf16[1024,2048]{1,0:T(8,128)(2,1)S(1)} %copy-done, bf16[2048,2048]{1,0:T(8,128)(2,1)} %wb_ref.3, bf16[2048,2048]{1,0:T(8,128)(2,1)} %wb_ref.3, s32[8]{0:T(128)S(1)} %copy-done.12, s32[8]{0:T(128)S(1)} %copy-done.13), custom_call_target="tpu_custom_call" | custom-call | flops 4294967296 | bytes 12582912 | tf_op jit(solution)/shard_map/keys/pallas_call | solution.py:122
  29.6 3.0 %scores.1 = (bf16[32,1024]{1,0:T(8,128)(2,1)S(1)}, bf16[32,1024]{1,0:T(8,128)(2,1)S(1)}, bf16[32,1024]{1,0:T(8,128)(2,1)S(1)}, bf16[32,1024]{1,0:T(8,128)(2,1)S(1)}, bf16[8,32,128]{2,1,0:T(8,128)(2,1)S(1)}) custom-call(bf16[4,2,2,16,128]{4,3,2,1,0:T(8,128)(2,1)S(1)} %pad_maximum_fusion.refs_0_, ...), custom_call_target="tpu_custom_call" | custom-call | flops 33554432 | bytes 3145728 | tf_op jit(solution)/shard_map/scores/pallas_call | solution.py:222
  34.9 2.9 %collective-permute-start.8 = (bf16[32,1024]{1,0:T(8,128)(2,1)S(1)}, bf16[32,1024]{1,0:T(8,128)(2,1)S(1)}, u32[]{:S(2)}, u32[]{:S(2)}) collective-permute-start(bf16[32,1024]{1,0:T(8,128)(2,1)S(1)} %get-tuple-element.25), channel_id=1, source_target_pairs={{0,3},{1,0},{2,1},{3,2},{4,7},{5,4},{6,5},{7,6},{8,11},{9,8},{10,9... | collective-permute-start | bytes 196616 | tf_op jit(solution)/shard_map/ppermute | solution.py:36
  37.9 2.4 %collective-permute-done.6.refs_1_ = bf16[32,1024]{1,0:T(8,128)(2,1)S(1)} collective-permute-done((bf16[32,1024]{1,0:T(8,128)(2,1)S(1)}, bf16[32,1024]{1,0:T(8,128)(2,1)S(1)}, u32[]{:S(2)}, u32[]{:S(2)}) %collective-permute-start.6) | collective-permute-done | bytes 65568 | tf_op jit(solution)/shard_map/ppermute | solution.py:36
  42.1 1.8 %weights.1 = (bf16[32,1024]{1,0:T(8,128)(2,1)}, f32[32,128]{1,0:T(8,128)}) custom-call(bf16[32,1024]{1,0:T(8,128)(2,1)} %copy-done.9, bf16[32,1024]{1,0:T(8,128)(2,1)} %copy-done.20, bf16[32,1024]{1,0:T(8,128)(2,1)} %copy-done.21, bf16[32,1024]{1,0:T(8,128)(2,1)} %copy-done.22, s32[104]{0:T(128)} %copy-done.10), custom_call_target="tpu_custom_call" | custom-call | tf_op jit(solution)/shard_map/weights/pallas_call | solution.py:273
  44.0 1.3 %collective-permute-start.9 = (bf16[32,1024]{1,0:T(8,128)(2,1)}, bf16[32,1024]{1,0:T(8,128)(2,1)S(1)}, u32[]{:S(2)}, u32[]{:S(2)}) collective-permute-start(bf16[32,1024]{1,0:T(8,128)(2,1)} %get-tuple-element.26.refs_0_), channel_id=1, source_target_pairs={{0,1},{1,2},{2,3},{3,0},{4,5},{5,6},{6,7},{7,4},{8,9},{9,10},{10,1... | collective-permute-start | bytes 196616 | tf_op jit(solution)/shard_map/ppermute | solution.py:28
  45.3 1.7 %collective-permute-start.10 = (bf16[32,1024]{1,0:T(8,128)(2,1)}, bf16[32,1024]{1,0:T(8,128)(2,1)S(1)}, u32[]{:S(2)}, u32[]{:S(2)}) collective-permute-start(bf16[32,1024]{1,0:T(8,128)(2,1)} %get-tuple-element.26.refs_0_), channel_id=1, source_target_pairs={{0,2},{1,3},{2,0},{3,1},{4,6},{5,7},{6,4},{7,5},{8,10},{9,11},{10,... | collective-permute-start | bytes 196616 | tf_op jit(solution)/shard_map/ppermute | solution.py:28
  47.8 2.2 %copy-done.1 = bf16[1024,2048]{1,0:T(8,128)(2,1)S(1)} copy-done((bf16[1024,2048]{1,0:T(8,128)(2,1)S(1)}, bf16[1024,2048]{1,0:T(8,128)(2,1)}, u32[]{:S(2)}) %copy-start.1) | copy-done | bytes 4194328
  50.0 8.9 %values.1.refs_4_ = bf16[1024,1024]{1,0:T(8,128)(2,1)S(1)} custom-call(bf16[1024,2048]{1,0:T(8,128)(2,1)S(1)} %copy-done.1, bf16[2048,2048]{1,0:T(8,128)(2,1)} %wb_ref.3, bf16[2048,2048]{1,0:T(8,128)(2,1)} %wb_ref.3), custom_call_target="tpu_custom_call" | custom-call | flops 4294967296 | bytes 12582912 | tf_op jit(solution)/shard_map/values/pallas_call | solution.py:148
  58.9 2.2 %weighted.1 = (bf16[8,32,128]{2,1,0:T(8,128)(2,1)S(1)}, bf16[8,32,128]{2,1,0:T(8,128)(2,1)S(1)}, bf16[8,32,128]{2,1,0:T(8,128)(2,1)S(1)}, bf16[8,32,128]{2,1,0:T(8,128)(2,1)S(1)}) custom-call(bf16[32,1024]{1,0:T(8,128)(2,1)S(1)} %copy-done.7, bf16[32,1024]{1,0:T(8,128)(2,1)S(1)} %collective-permute-done.9.refs_1_, ...), custom_call_target="tpu_custom_call" | custom-call | tf_op jit(solution)/shard_map/weighted/pallas_call | solution.py:318
  64.2 2.5 %collective-permute-start.14 = (bf16[8,32,128]{2,1,0:T(8,128)(2,1)S(1)}, bf16[8,32,128]{2,1,0:T(8,128)(2,1)S(1)}, u32[]{:S(2)}, u32[]{:S(2)}) collective-permute-start(bf16[8,32,128]{2,1,0:T(8,128)(2,1)S(1)} %get-tuple-element.30), channel_id=1, source_target_pairs={{0,3},{1,0},{2,1},{3,2},{4,7},{5,4},{6,5},{7,6},{8,11},{9,8},{10,9... | collective-permute-start | bytes 196616 | tf_op jit(solution)/shard_map/ppermute | solution.py:36
  66.7 1.4 %collective-permute-start.18 = (bf16[2,2,4,128]{3,2,1,0:T(4,128)(2,1)S(1)}, bf16[2,2,4,128]{3,2,1,0:T(4,128)(2,1)S(1)}, u32[]{:S(2)}, u32[]{:S(2)}) collective-permute-start(bf16[2,2,4,128]{3,2,1,0:T(4,128)(2,1)S(1)} %reshape.7.refs_4_), channel_id=1, source_target_pairs={{0,4},{4,8},{8,12},{12,0},{1,5},{5,9},{9,13},{13,1},{2,6},{6,10},{... | collective-permute-start | bytes 12296 | tf_op jit(solution)/shard_map/ppermute | solution.py:28
  68.1 1.8 %collective-permute-done.18.refs_5_ = bf16[2,2,4,128]{3,2,1,0:T(4,128)(2,1)S(1)} collective-permute-done((bf16[2,2,4,128]{3,2,1,0:T(4,128)(2,1)S(1)}, bf16[2,2,4,128]{3,2,1,0:T(4,128)(2,1)S(1)}, u32[]{:S(2)}, u32[]{:S(2)}) %collective-permute-start.18) | collective-permute-done | bytes 4128 | tf_op jit(solution)/shard_map/ppermute | solution.py:28
  71.1 2.4 %collective-permute-done.19.refs_6_ = bf16[2,2,4,128]{3,2,1,0:T(4,128)(2,1)S(1)} collective-permute-done((bf16[2,2,4,128]{3,2,1,0:T(4,128)(2,1)S(1)}, bf16[2,2,4,128]{3,2,1,0:T(4,128)(2,1)S(1)}, u32[]{:S(2)}, u32[]{:S(2)}) %collective-permute-start.19) | collective-permute-done | bytes 4128 | tf_op jit(solution)/shard_map/ppermute | solution.py:28
  73.5 1.3 %collective-permute-done.20.refs_7_ = bf16[2,2,4,128]{3,2,1,0:T(4,128)(2,1)S(1)} collective-permute-done((bf16[2,2,4,128]{3,2,1,0:T(4,128)(2,1)S(1)}, bf16[2,2,4,128]{3,2,1,0:T(4,128)(2,1)S(1)}, u32[]{:S(2)}, u32[]{:S(2)}) %collective-permute-start.20) | collective-permute-done | bytes 4128 | tf_op jit(solution)/shard_map/ppermute | solution.py:28
  76.1 1.4 %collective-permute-start.17 = (f32[32,128]{1,0:T(8,128)S(1)}, f32[32,128]{1,0:T(8,128)S(1)}, u32[]{:S(2)}, u32[]{:S(2)}) collective-permute-start(f32[32,128]{1,0:T(8,128)S(1)} %copy-done.23), channel_id=1, source_target_pairs={{0,12},{4,0},{8,4},{12,8},{1,13},{5,1},{9,5},{13,9},{2,14},{6,2},{... | collective-permute-start | bytes 49160 | tf_op jit(solution)/shard_map/ppermute | solution.py:28
  79.6 8.8 %merge.1 = (f32[8,32,128]{2,1,0:T(8,128)}, f32[8,32,128]{2,1,0:T(8,128)}) custom-call(f32[32,128]{1,0:T(8,128)} %get-tuple-element.31.refs_0_, f32[32,128]{1,0:T(8,128)} %copy-done.24, f32[32,128]{1,0:T(8,128)} %copy-done.25, f32[32,128]{1,0:T(8,128)} %copy-done.26, bf16[2,2,4,128]{3,2,1,0:T(4,128)(2,1)} %copy-done.27, bf16[2,2,4,128]{3,2,1,0:T(4,128)(2,1)} %copy-done.28, ...), custom_call_target="tpu_custom_call" | custom-call | tf_op jit(solution)/shard_map/merge/pallas_call | solution.py:414
  89.0 1.7 %scaled.1.refs_0_ = bf16[8,32,128]{2,1,0:T(8,128)(2,1)} custom-call(bf16[8,32,128]{2,1,0:T(8,128)(2,1)} %copy-done.6, bf16[8,32,128]{2,1,0:T(8,128)(2,1)} %copy-done.14, bf16[8,32,128]{2,1,0:T(8,128)(2,1)} %copy-done.15, bf16[8,32,128]{2,1,0:T(8,128)(2,1)} %copy-done.16, f32[8,32,128]{2,1,0:T(8,128)} %get-tuple-element.33.refs_4_), custom_call_target="tpu_custom_call" | custom-call | tf_op jit(solution)/shard_map/scaled/pallas_call | solution.py:439
  91.6 1.2 %collective-permute-start.22 = (bf16[8,32,128]{2,1,0:T(8,128)(2,1)}, bf16[8,32,128]{2,1,0:T(8,128)(2,1)S(1)}, u32[]{:S(2)}, u32[]{:S(2)}) collective-permute-start(bf16[8,32,128]{2,1,0:T(8,128)(2,1)} %scaled.1.refs_0_), channel_id=1, source_target_pairs={{0,8},{4,12},{8,0},{12,4},{1,9},{5,13},{9,1},{13,5},{2,10},{6,14},... | collective-permute-start | bytes 196616 | tf_op jit(solution)/shard_map/ppermute | solution.py:28
  93.1 1.5 %collective-permute-done.21.refs_1_ = bf16[8,32,128]{2,1,0:T(8,128)(2,1)S(1)} collective-permute-done((bf16[8,32,128]{2,1,0:T(8,128)(2,1)}, bf16[8,32,128]{2,1,0:T(8,128)(2,1)S(1)}, u32[]{:S(2)}, u32[]{:S(2)}) %collective-permute-start.21) | collective-permute-done | bytes 65568 | tf_op jit(solution)/shard_map/ppermute | solution.py:28
  94.6 1.5 %collective-permute-done.22.refs_2_ = bf16[8,32,128]{2,1,0:T(8,128)(2,1)S(1)} collective-permute-done((bf16[8,32,128]{2,1,0:T(8,128)(2,1)}, bf16[8,32,128]{2,1,0:T(8,128)(2,1)S(1)}, u32[]{:S(2)}, u32[]{:S(2)}) %collective-permute-start.22) | collective-permute-done | bytes 65568 | tf_op jit(solution)/shard_map/ppermute | solution.py:28
  96.1 3.4 %copy-done.2 = bf16[2048,2048]{1,0:T(8,128)(2,1)S(1)} copy-done((bf16[2048,2048]{1,0:T(8,128)(2,1)S(1)}, bf16[2048,2048]{1,0:T(8,128)(2,1)}, u32[]{:S(2)}) %copy-start.2) | copy-done | bytes 8388632
  101.2 2.3 %output.1.refs_0_ = bf16[16,2048]{1,0:T(8,128)(2,1)S(1)} custom-call(bf16[8,32,128]{2,1,0:T(8,128)(2,1)S(1)} %copy-done.3, bf16[8,32,128]{2,1,0:T(8,128)(2,1)S(1)} %collective-permute-done.21.refs_1_, bf16[8,32,128]{2,1,0:T(8,128)(2,1)S(1)} %collective-permute-done.22.refs_2_, bf16[8,32,128]{2,1,0:T(8,128)(2,1)S(1)} %collective-permute-done.23.refs_3_, ...), custom_call_target="tpu_custom_call" | custom-call | tf_op jit(solution)/shard_map/output/pallas_call | solution.py:477
  104.7 2.6 %collective-permute-start.26 = (bf16[16,2048]{1,0:T(8,128)(2,1)S(1)}, bf16[16,2048]{1,0:T(8,128)(2,1)S(1)}, u32[]{:S(2)}, u32[]{:S(2)}) collective-permute-start(bf16[16,2048]{1,0:T(8,128)(2,1)S(1)} %output.1.refs_0_), channel_id=1, source_target_pairs={{0,3},{1,0},{2,1},{3,2},{4,7},{5,4},{6,5},{7,6},{8,11},{9,8},{10,9... | collective-permute-start | bytes 196616 | tf_op jit(solution)/shard_map/ppermute | solution.py:28
  107.4 3.0 %collective-permute-done.24.refs_1_ = bf16[16,2048]{1,0:T(8,128)(2,1)S(1)} collective-permute-done((bf16[16,2048]{1,0:T(8,128)(2,1)S(1)}, bf16[16,2048]{1,0:T(8,128)(2,1)S(1)}, u32[]{:S(2)}, u32[]{:S(2)}) %collective-permute-start.24) | collective-permute-done | bytes 65568 | tf_op jit(solution)/shard_map/ppermute | solution.py:28
  110.3 1.9 %collective-permute-done.25.refs_2_ = bf16[16,2048]{1,0:T(8,128)(2,1)S(1)} collective-permute-done((bf16[16,2048]{1,0:T(8,128)(2,1)S(1)}, bf16[16,2048]{1,0:T(8,128)(2,1)S(1)}, u32[]{:S(2)}, u32[]{:S(2)}) %collective-permute-start.25) | collective-permute-done | bytes 65568 | tf_op jit(solution)/shard_map/ppermute | solution.py:28
  113.4 1.7 %final.1 = f32[8,2,2048]{2,1,0:T(2,128)} custom-call(bf16[16,2048]{1,0:T(8,128)(2,1)} %copy-done.4, bf16[16,2048]{1,0:T(8,128)(2,1)} %copy-done.17, bf16[16,2048]{1,0:T(8,128)(2,1)} %copy-done.18, bf16[16,2048]{1,0:T(8,128)(2,1)} %copy-done.19, bf16[8,2,2048]{2,1,0:T(2,128)(2,1)} %refs_4_.1), custom_call_target="tpu_custom_call" | custom-call | tf_op jit(solution)/shard_map/final/pallas_call | solution.py:502
  (99 shorter events, 23.4 us)
Async XLA Ops:
  0.7 6.9 %collective-permute-start.2 = (bf16[2,2,16,128]{3,2,1,0:T(8,128)(2,1)S(1)}, bf16[2,2,16,128]{3,2,1,0:T(8,128)(2,1)S(1)}, u32[]{:S(2)}, u32[]{:S(2)}) collective-permute-start(bf16[2,2,16,128]{3,2,1,0:T(8,128)(2,1)S(1)} %reshape.6), channel_id=1, source_target_pairs={{0,3},{1,0},{2,1},{3,2},{4,7},{5,4},{6,5},{7,6},{8,11},{9,8},{10,9... | collective-permute-start | bytes 49160 | tf_op jit(solution)/shard_map/ppermute | solution.py:28
  5.8 4.6 %collective-permute-start.1 = (bf16[2,2,16,128]{3,2,1,0:T(8,128)(2,1)S(1)}, bf16[2,2,16,128]{3,2,1,0:T(8,128)(2,1)S(1)}, u32[]{:S(2)}, u32[]{:S(2)}) collective-permute-start(bf16[2,2,16,128]{3,2,1,0:T(8,128)(2,1)S(1)} %reshape.6), channel_id=1, source_target_pairs={{0,2},{1,3},{2,0},{3,1},{4,6},{5,7},{6,4},{7,5},{8,10},{9,11},{10,... | collective-permute-start | bytes 49160 | tf_op jit(solution)/shard_map/ppermute | solution.py:28
  5.8 5.5 %collective-permute-start = (bf16[2,2,16,128]{3,2,1,0:T(8,128)(2,1)S(1)}, bf16[2,2,16,128]{3,2,1,0:T(8,128)(2,1)S(1)}, u32[]{:S(2)}, u32[]{:S(2)}) collective-permute-start(bf16[2,2,16,128]{3,2,1,0:T(8,128)(2,1)S(1)} %reshape.6), channel_id=1, source_target_pairs={{0,1},{1,2},{2,3},{3,0},{4,5},{5,6},{6,7},{7,4},{8,9},{9,10},{10,1... | collective-permute-start | bytes 49160 | tf_op jit(solution)/shard_map/ppermute | solution.py:28
  11.4 18.2 %collective-permute-start.3 = (bf16[4,2,2,16,128]{4,3,2,1,0:T(8,128)(2,1)S(1)}, bf16[4,2,2,16,128]{4,3,2,1,0:T(8,128)(2,1)S(1)}, u32[]{:S(2)}, u32[]{:S(2)}) collective-permute-start(bf16[4,2,2,16,128]{4,3,2,1,0:T(8,128)(2,1)S(1)} %pad_maximum_fusion.refs_0_), channel_id=1, source_target_pairs={{0,4},{4,8},{8,12},{12,0},{1,5},{5,9},{9,13},{13,1},{2,6},{6,10},{... | collective-permute-start | bytes 196616 | tf_op jit(solution)/shard_map/ppermute | solution.py:28
  11.5 18.1 %collective-permute-start.4 = (bf16[4,2,2,16,128]{4,3,2,1,0:T(8,128)(2,1)S(1)}, bf16[4,2,2,16,128]{4,3,2,1,0:T(8,128)(2,1)S(1)}, u32[]{:S(2)}, u32[]{:S(2)}) collective-permute-start(bf16[4,2,2,16,128]{4,3,2,1,0:T(8,128)(2,1)S(1)} %pad_maximum_fusion.refs_0_), channel_id=1, source_target_pairs={{0,8},{4,12},{8,0},{12,4},{1,9},{5,13},{9,1},{13,5},{2,10},{6,14},... | collective-permute-start | bytes 196616 | tf_op jit(solution)/shard_map/ppermute | solution.py:28
  13.0 16.5 %collective-permute-start.5 = (bf16[4,2,2,16,128]{4,3,2,1,0:T(8,128)(2,1)S(1)}, bf16[4,2,2,16,128]{4,3,2,1,0:T(8,128)(2,1)S(1)}, u32[]{:S(2)}, u32[]{:S(2)}) collective-permute-start(bf16[4,2,2,16,128]{4,3,2,1,0:T(8,128)(2,1)S(1)} %pad_maximum_fusion.refs_0_), channel_id=1, source_target_pairs={{0,12},{4,0},{8,4},{12,8},{1,13},{5,1},{9,5},{13,9},{2,14},{6,2},{... | collective-permute-start | bytes 196616 | tf_op jit(solution)/shard_map/ppermute | solution.py:28
  29.6 11.9 %copy-start.10 = (s32[104]{0:T(128)}, s32[104]{0:T(128)S(1)}, u32[]{:S(2)}) copy-start(s32[104]{0:T(128)S(1)} %get-tuple-element.21.refs_5_.refs_4_.refs_9_) | copy-start | bytes 1252
  33.8 6.5 %collective-permute-start.6 = (bf16[32,1024]{1,0:T(8,128)(2,1)S(1)}, bf16[32,1024]{1,0:T(8,128)(2,1)S(1)}, u32[]{:S(2)}, u32[]{:S(2)}) collective-permute-start(bf16[32,1024]{1,0:T(8,128)(2,1)S(1)} %get-tuple-element.23), channel_id=1, source_target_pairs={{0,1},{1,2},{2,3},{3,0},{4,5},{5,6},{6,7},{7,4},{8,9},{9,10},{10,1... | collective-permute-start | bytes 196616 | tf_op jit(solution)/shard_map/ppermute | solution.py:36
  33.8 7.7 %collective-permute-start.7 = (bf16[32,1024]{1,0:T(8,128)(2,1)S(1)}, bf16[32,1024]{1,0:T(8,128)(2,1)S(1)}, u32[]{:S(2)}, u32[]{:S(2)}) collective-permute-start(bf16[32,1024]{1,0:T(8,128)(2,1)S(1)} %get-tuple-element.24), channel_id=1, source_target_pairs={{0,2},{1,3},{2,0},{3,1},{4,6},{5,7},{6,4},{7,5},{8,10},{9,11},{10,... | collective-permute-start | bytes 196616 | tf_op jit(solution)/shard_map/ppermute | solution.py:36
  34.9 6.5 %collective-permute-start.8 = (bf16[32,1024]{1,0:T(8,128)(2,1)S(1)}, bf16[32,1024]{1,0:T(8,128)(2,1)S(1)}, u32[]{:S(2)}, u32[]{:S(2)}) collective-permute-start(bf16[32,1024]{1,0:T(8,128)(2,1)S(1)} %get-tuple-element.25), channel_id=1, source_target_pairs={{0,3},{1,0},{2,1},{3,2},{4,7},{5,4},{6,5},{7,6},{8,11},{9,8},{10,9... | collective-permute-start | bytes 196616 | tf_op jit(solution)/shard_map/ppermute | solution.py:36
  42.1 24.6 %copy-start.31 = (bf16[2,2,512]{2,1,0:T(2,128)(2,1)S(1)}, bf16[2,2,512]{2,1,0:T(2,128)(2,1)}, u32[]{:S(2)}) copy-start(bf16[2,2,512]{2,1,0:T(2,128)(2,1)} %param.13) | copy-start | bytes 12292
  44.0 15.0 %copy-start.11 = (s32[104]{0:T(128)S(1)}, s32[104]{0:T(128)}, u32[]{:S(2)}) copy-start(s32[104]{0:T(128)} %copy-done.10) | copy-start | bytes 1252
  44.0 14.9 %collective-permute-start.9 = (bf16[32,1024]{1,0:T(8,128)(2,1)}, bf16[32,1024]{1,0:T(8,128)(2,1)S(1)}, u32[]{:S(2)}, u32[]{:S(2)}) collective-permute-start(bf16[32,1024]{1,0:T(8,128)(2,1)} %get-tuple-element.26.refs_0_), channel_id=1, source_target_pairs={{0,1},{1,2},{2,3},{3,0},{4,5},{5,6},{6,7},{7,4},{8,9},{9,10},{10,1... | collective-permute-start | bytes 196616 | tf_op jit(solution)/shard_map/ppermute | solution.py:28
  45.3 13.6 %collective-permute-start.10 = (bf16[32,1024]{1,0:T(8,128)(2,1)}, bf16[32,1024]{1,0:T(8,128)(2,1)S(1)}, u32[]{:S(2)}, u32[]{:S(2)}) collective-permute-start(bf16[32,1024]{1,0:T(8,128)(2,1)} %get-tuple-element.26.refs_0_), channel_id=1, source_target_pairs={{0,2},{1,3},{2,0},{3,1},{4,6},{5,7},{6,4},{7,5},{8,10},{9,11},{10,... | collective-permute-start | bytes 196616 | tf_op jit(solution)/shard_map/ppermute | solution.py:28
  47.0 12.0 %collective-permute-start.11 = (bf16[32,1024]{1,0:T(8,128)(2,1)}, bf16[32,1024]{1,0:T(8,128)(2,1)S(1)}, u32[]{:S(2)}, u32[]{:S(2)}) collective-permute-start(bf16[32,1024]{1,0:T(8,128)(2,1)} %get-tuple-element.26.refs_0_), channel_id=1, source_target_pairs={{0,3},{1,0},{2,1},{3,2},{4,7},{5,4},{6,5},{7,6},{8,11},{9,8},{10,9... | collective-permute-start | bytes 196616 | tf_op jit(solution)/shard_map/ppermute | solution.py:28
  50.0 16.7 %copy-start.23 = (f32[32,128]{1,0:T(8,128)S(1)}, f32[32,128]{1,0:T(8,128)}, u32[]{:S(2)}) copy-start(f32[32,128]{1,0:T(8,128)} %get-tuple-element.31.refs_0_) | copy-start | bytes 49156
  61.7 26.6 %collective-permute-start.12 = (bf16[8,32,128]{2,1,0:T(8,128)(2,1)S(1)}, bf16[8,32,128]{2,1,0:T(8,128)(2,1)S(1)}, u32[]{:S(2)}, u32[]{:S(2)}) collective-permute-start(bf16[8,32,128]{2,1,0:T(8,128)(2,1)S(1)} %get-tuple-element.28), channel_id=1, source_target_pairs={{0,1},{1,2},{2,3},{3,0},{4,5},{5,6},{6,7},{7,4},{8,9},{9,10},{10,1... | collective-permute-start | bytes 196616 | tf_op jit(solution)/shard_map/ppermute | solution.py:36
  62.9 25.4 %collective-permute-start.13 = (bf16[8,32,128]{2,1,0:T(8,128)(2,1)S(1)}, bf16[8,32,128]{2,1,0:T(8,128)(2,1)S(1)}, u32[]{:S(2)}, u32[]{:S(2)}) collective-permute-start(bf16[8,32,128]{2,1,0:T(8,128)(2,1)S(1)} %get-tuple-element.29), channel_id=1, source_target_pairs={{0,2},{1,3},{2,0},{3,1},{4,6},{5,7},{6,4},{7,5},{8,10},{9,11},{10,... | collective-permute-start | bytes 196616 | tf_op jit(solution)/shard_map/ppermute | solution.py:36
  64.2 24.2 %collective-permute-start.14 = (bf16[8,32,128]{2,1,0:T(8,128)(2,1)S(1)}, bf16[8,32,128]{2,1,0:T(8,128)(2,1)S(1)}, u32[]{:S(2)}, u32[]{:S(2)}) collective-permute-start(bf16[8,32,128]{2,1,0:T(8,128)(2,1)S(1)} %get-tuple-element.30), channel_id=1, source_target_pairs={{0,3},{1,0},{2,1},{3,2},{4,7},{5,4},{6,5},{7,6},{8,11},{9,8},{10,9... | collective-permute-start | bytes 196616 | tf_op jit(solution)/shard_map/ppermute | solution.py:36
  66.7 9.4 %collective-permute-start.15 = (f32[32,128]{1,0:T(8,128)S(1)}, f32[32,128]{1,0:T(8,128)S(1)}, u32[]{:S(2)}, u32[]{:S(2)}) collective-permute-start(f32[32,128]{1,0:T(8,128)S(1)} %copy-done.23), channel_id=1, source_target_pairs={{0,4},{4,8},{8,12},{12,0},{1,5},{5,9},{9,13},{13,1},{2,6},{6,10},{... | collective-permute-start | bytes 49160 | tf_op jit(solution)/shard_map/ppermute | solution.py:28
  66.7 12.3 %copy-start.27 = (bf16[2,2,4,128]{3,2,1,0:T(4,128)(2,1)}, bf16[2,2,4,128]{3,2,1,0:T(4,128)(2,1)S(1)}, u32[]{:S(2)}) copy-start(bf16[2,2,4,128]{3,2,1,0:T(4,128)(2,1)S(1)} %reshape.7.refs_4_) | copy-start | bytes 12292
  66.7 3.2 %collective-permute-start.18 = (bf16[2,2,4,128]{3,2,1,0:T(4,128)(2,1)S(1)}, bf16[2,2,4,128]{3,2,1,0:T(4,128)(2,1)S(1)}, u32[]{:S(2)}, u32[]{:S(2)}) collective-permute-start(bf16[2,2,4,128]{3,2,1,0:T(4,128)(2,1)S(1)} %reshape.7.refs_4_), channel_id=1, source_target_pairs={{0,4},{4,8},{8,12},{12,0},{1,5},{5,9},{9,13},{13,1},{2,6},{6,10},{... | collective-permute-start | bytes 12296 | tf_op jit(solution)/shard_map/ppermute | solution.py:28
  69.9 3.6 %collective-permute-start.19 = (bf16[2,2,4,128]{3,2,1,0:T(4,128)(2,1)S(1)}, bf16[2,2,4,128]{3,2,1,0:T(4,128)(2,1)S(1)}, u32[]{:S(2)}, u32[]{:S(2)}) collective-permute-start(bf16[2,2,4,128]{3,2,1,0:T(4,128)(2,1)S(1)} %reshape.7.refs_4_), channel_id=1, source_target_pairs={{0,8},{4,12},{8,0},{12,4},{1,9},{5,13},{9,1},{13,5},{2,10},{6,14},... | collective-permute-start | bytes 12296 | tf_op jit(solution)/shard_map/ppermute | solution.py:28
  73.5 1.3 %collective-permute-start.20 = (bf16[2,2,4,128]{3,2,1,0:T(4,128)(2,1)S(1)}, bf16[2,2,4,128]{3,2,1,0:T(4,128)(2,1)S(1)}, u32[]{:S(2)}, u32[]{:S(2)}) collective-permute-start(bf16[2,2,4,128]{3,2,1,0:T(4,128)(2,1)S(1)} %reshape.7.refs_4_), channel_id=1, source_target_pairs={{0,12},{4,0},{8,4},{12,8},{1,13},{5,1},{9,5},{13,9},{2,14},{6,2},{... | collective-permute-start | bytes 12296 | tf_op jit(solution)/shard_map/ppermute | solution.py:28
  74.8 3.7 %collective-permute-start.16 = (f32[32,128]{1,0:T(8,128)S(1)}, f32[32,128]{1,0:T(8,128)S(1)}, u32[]{:S(2)}, u32[]{:S(2)}) collective-permute-start(f32[32,128]{1,0:T(8,128)S(1)} %copy-done.23), channel_id=1, source_target_pairs={{0,8},{4,12},{8,0},{12,4},{1,9},{5,13},{9,1},{13,5},{2,10},{6,14},... | collective-permute-start | bytes 49160 | tf_op jit(solution)/shard_map/ppermute | solution.py:28
  76.1 2.9 %collective-permute-start.17 = (f32[32,128]{1,0:T(8,128)S(1)}, f32[32,128]{1,0:T(8,128)S(1)}, u32[]{:S(2)}, u32[]{:S(2)}) collective-permute-start(f32[32,128]{1,0:T(8,128)S(1)} %copy-done.23), channel_id=1, source_target_pairs={{0,12},{4,0},{8,4},{12,8},{1,13},{5,1},{9,5},{13,9},{2,14},{6,2},{... | collective-permute-start | bytes 49160 | tf_op jit(solution)/shard_map/ppermute | solution.py:28
  90.7 3.9 %collective-permute-start.21 = (bf16[8,32,128]{2,1,0:T(8,128)(2,1)}, bf16[8,32,128]{2,1,0:T(8,128)(2,1)S(1)}, u32[]{:S(2)}, u32[]{:S(2)}) collective-permute-start(bf16[8,32,128]{2,1,0:T(8,128)(2,1)} %scaled.1.refs_0_), channel_id=1, source_target_pairs={{0,4},{4,8},{8,12},{12,0},{1,5},{5,9},{9,13},{13,1},{2,6},{6,10},{... | collective-permute-start | bytes 196616 | tf_op jit(solution)/shard_map/ppermute | solution.py:28
  91.6 4.5 %collective-permute-start.22 = (bf16[8,32,128]{2,1,0:T(8,128)(2,1)}, bf16[8,32,128]{2,1,0:T(8,128)(2,1)S(1)}, u32[]{:S(2)}, u32[]{:S(2)}) collective-permute-start(bf16[8,32,128]{2,1,0:T(8,128)(2,1)} %scaled.1.refs_0_), channel_id=1, source_target_pairs={{0,8},{4,12},{8,0},{12,4},{1,9},{5,13},{9,1},{13,5},{2,10},{6,14},... | collective-permute-start | bytes 196616 | tf_op jit(solution)/shard_map/ppermute | solution.py:28
  92.8 3.2 %collective-permute-start.23 = (bf16[8,32,128]{2,1,0:T(8,128)(2,1)}, bf16[8,32,128]{2,1,0:T(8,128)(2,1)S(1)}, u32[]{:S(2)}, u32[]{:S(2)}) collective-permute-start(bf16[8,32,128]{2,1,0:T(8,128)(2,1)} %scaled.1.refs_0_), channel_id=1, source_target_pairs={{0,12},{4,0},{8,4},{12,8},{1,13},{5,1},{9,5},{13,9},{2,14},{6,2},{... | collective-permute-start | bytes 196616 | tf_op jit(solution)/shard_map/ppermute | solution.py:28
  103.5 6.8 %collective-permute-start.24 = (bf16[16,2048]{1,0:T(8,128)(2,1)S(1)}, bf16[16,2048]{1,0:T(8,128)(2,1)S(1)}, u32[]{:S(2)}, u32[]{:S(2)}) collective-permute-start(bf16[16,2048]{1,0:T(8,128)(2,1)S(1)} %output.1.refs_0_), channel_id=1, source_target_pairs={{0,1},{1,2},{2,3},{3,0},{4,5},{5,6},{6,7},{7,4},{8,9},{9,10},{10,1... | collective-permute-start | bytes 196616 | tf_op jit(solution)/shard_map/ppermute | solution.py:28
  103.5 8.7 %collective-permute-start.25 = (bf16[16,2048]{1,0:T(8,128)(2,1)S(1)}, bf16[16,2048]{1,0:T(8,128)(2,1)S(1)}, u32[]{:S(2)}, u32[]{:S(2)}) collective-permute-start(bf16[16,2048]{1,0:T(8,128)(2,1)S(1)} %output.1.refs_0_), channel_id=1, source_target_pairs={{0,2},{1,3},{2,0},{3,1},{4,6},{5,7},{6,4},{7,5},{8,10},{9,11},{10,... | collective-permute-start | bytes 196616 | tf_op jit(solution)/shard_map/ppermute | solution.py:28
  104.7 7.5 %collective-permute-start.26 = (bf16[16,2048]{1,0:T(8,128)(2,1)S(1)}, bf16[16,2048]{1,0:T(8,128)(2,1)S(1)}, u32[]{:S(2)}, u32[]{:S(2)}) collective-permute-start(bf16[16,2048]{1,0:T(8,128)(2,1)S(1)} %output.1.refs_0_), channel_id=1, source_target_pairs={{0,3},{1,0},{2,1},{3,2},{4,7},{5,4},{6,5},{7,6},{8,11},{9,8},{10,9... | collective-permute-start | bytes 196616 | tf_op jit(solution)/shard_map/ppermute | solution.py:28
  (27 other events, 60.6 us)

commit v2 on v1

v2 whole, which is shorter than its diff:
```python
import functools
import math

import jax
import jax.numpy as jnp
from jax import lax
from jax.experimental import pallas as pl
from jax.experimental.pallas import tpu as pltpu
from jax.sharding import PartitionSpec as P

QH = 64
KVH = 8
HD = 128
PAGE = 128
GROUP = QH // KVH
NEG = -1e30
F32 = jnp.float32
BF16 = jnp.bfloat16
MIB = 1 << 20

VMEM = pl.BlockSpec(memory_space=pltpu.VMEM)
SMEM = pl.BlockSpec(memory_space=pltpu.SMEM)


def exchange(chunks, axis):
    return lax.all_to_all(chunks, axis, 0, 0)


def lane_freqs(rows):
    lane = lax.broadcasted_iota(jnp.int32, (rows, HD), 1) % (HD // 2)
    return jnp.exp(-(lane.astype(F32) * (2.0 / HD)) * math.log(500000.0))


def sine_sign(rows):
    lane = lax.broadcasted_iota(jnp.int32, (rows, HD), 1)
    return jnp.where(lane < HD // 2, -1.0, 1.0)


def keys_kernel(pages, prompts, x_ref, wa_ref, wb_ref, counts, tails, out_ref, meta, cos_s, sin_s):
    step = pl.program_id(0)
    tokens = x_ref.shape[0]
    local_pages = tokens // PAGE

    @pl.when(step == 0)
    def _():
        def one_prompt(r, start):
            length = (counts[r] - 1) * PAGE + tails[r]
            meta[3 * pages + r] = length

            def one_page(i, carry):
                meta[start + i] = r
                meta[pages + start + i] = i * PAGE
                meta[2 * pages + start + i] = jnp.minimum(length - i * PAGE, PAGE)
                return carry

            lax.fori_loop(0, counts[r], one_page, 0)
            return start + counts[r]

        lax.fori_loop(0, prompts, one_prompt, 0)
        freqs = lane_freqs(PAGE)
        offset = lax.broadcasted_iota(jnp.int32, (PAGE, HD), 0).astype(F32) * freqs
        cos_off, sin_off = jnp.cos(offset), jnp.sin(offset)
        row_freqs = lane_freqs(8)
        sign = sine_sign(PAGE)
        first = lax.axis_index("seq") * local_pages
        for p in range(local_pages):
            base = meta[pages + first + p].astype(F32) * row_freqs
            cos_base, sin_base = jnp.cos(base)[:1], jnp.sin(base)[:1]
            cos_s[p * PAGE : (p + 1) * PAGE] = cos_off * cos_base - sin_off * sin_base
            sin_s[p * PAGE : (p + 1) * PAGE] = sign * (sin_off * cos_base + cos_off * sin_base)

    weight = jnp.concatenate([wa_ref[...], wb_ref[...]], axis=1)
    for start in range(0, tokens, 512):
        at = slice(start, start + 512)
        product = jnp.dot(x_ref[at], weight, preferred_element_type=F32)
        cosine, sine = cos_s[at], sin_s[at]
        for half in range(2):
            k = product[:, half * HD : (half + 1) * HD]
            k = k * cosine + pltpu.roll(k, HD // 2, 1) * sine
            out_ref[at, half * HD : (half + 1) * HD] = k.astype(BF16)


def values_kernel(x_ref, wa_ref, wb_ref, out_ref):
    weight = jnp.concatenate([wa_ref[...], wb_ref[...]], axis=1)
    out_ref[...] = jnp.dot(x_ref[...], weight, preferred_element_type=F32).astype(BF16)


def project_keys(x, kv_weight, counts, tails, pages):
    tokens, depth = x.shape
    prompts = counts.shape[0]
    return pl.pallas_call(
        functools.partial(keys_kernel, pages, prompts),
        grid=(KVH // 2,),
        in_specs=[
            pl.BlockSpec((tokens, depth), lambda i: (0, 0)),
            pl.BlockSpec((depth, HD), lambda i: (0, 4 * i)),
            pl.BlockSpec((depth, HD), lambda i: (0, 4 * i + 2)),
            SMEM,
            SMEM,
        ],
        out_specs=[pl.BlockSpec((tokens, 2 * HD), lambda i: (0, i)), SMEM],
        out_shape=[
            jax.ShapeDtypeStruct((tokens, KVH * HD), BF16),
            jax.ShapeDtypeStruct((3 * pages + prompts,), jnp.int32),
        ],
        scratch_shapes=[pltpu.VMEM((tokens, HD), F32), pltpu.VMEM((tokens, HD), F32)],
        compiler_params=pltpu.CompilerParams(vmem_limit_bytes=24 * MIB),
        cost_estimate=pl.CostEstimate(
            flops=2 * tokens * depth * KVH * HD, bytes_accessed=12 * MIB, transcendentals=0
        ),
        name="keys",
    )(x, kv_weight, kv_weight, counts, tails)


def project_values(x, kv_weight):
    tokens, depth = x.shape
    return pl.pallas_call(
        values_kernel,
        grid=(KVH // 2,),
        in_specs=[
            pl.BlockSpec((tokens, depth), lambda i: (0, 0)),
            pl.BlockSpec((depth, HD), lambda i: (0, 4 * i + 1)),
            pl.BlockSpec((depth, HD), lambda i: (0, 4 * i + 3)),
        ],
        out_specs=pl.BlockSpec((tokens, 2 * HD), lambda i: (0, i)),
        out_shape=jax.ShapeDtypeStruct((tokens, KVH * HD), BF16),
        compiler_params=pltpu.CompilerParams(vmem_limit_bytes=24 * MIB),
        cost_estimate=pl.CostEstimate(
            flops=2 * tokens * depth * KVH * HD, bytes_accessed=12 * MIB, transcendentals=0
        ),
        name="values",
    )(x, kv_weight, kv_weight)


def scores_kernel(pages, n_seq, n_tp, new_ref, k_ref, meta, out_ref, fresh_ref, all_q):
    kv_local = KVH // n_tp
    local_pages = k_ref.shape[0] // PAGE
    _, own_rows, new_count, _, _ = new_ref.shape
    rows = new_count * GROUP
    heads = kv_local * GROUP
    scale = 1.0 / math.sqrt(HD)
    freqs = lane_freqs(8)
    sign = sine_sign(8)
    me = lax.axis_index("tp")
    first = lax.axis_index("seq") * local_pages
    step = lax.broadcasted_iota(jnp.int32, (kv_local * rows, HD), 0) % rows // GROUP
    lane = lax.broadcasted_iota(jnp.int32, (kv_local * rows, HD), 1)
    found = [jnp.full((kv_local * rows, HD), NEG, F32) for _ in range(new_count)]
    for ds in range(n_seq):
        for rr in range(own_rows):
            request = ds * own_rows + rr
            length = meta[3 * pages + request]
            cosines, sines = [], []
            for n in range(new_count):
                angle = (length + n).astype(F32) * freqs
                cosines.append(jnp.cos(angle))
                sines.append(jnp.sin(angle) * sign)
            for dt in range(n_tp):
                held = [new_ref[ds * n_tp + dt, rr, n].astype(F32) for n in range(new_count)]
                for g in range(kv_local):
                    parts = []
                    for n in range(new_count):
                        q = held[n][g * GROUP : (g + 1) * GROUP]
                        parts.append(q * cosines[n] + pltpu.roll(q, HD // 2, 1) * sines[n])
                    at = (dt * kv_local + g) * rows
                    all_q[request, at : at + rows] = jnp.concatenate(parts, axis=0).astype(BF16)
            own = pl.ds(pl.multiple_of(me * kv_local * rows, kv_local * rows), kv_local * rows)
            own_q = all_q[request, own].astype(F32)
            for n in range(new_count):
                both = new_ref[ds * n_tp + me, rr, n].astype(F32)
                spread = []
                for g in range(kv_local):
                    k = both[heads + 2 * g : heads + 2 * g + 1]
                    k = k * cosines[n][:1] + pltpu.roll(k, HD // 2, 1) * sines[n][:1]
                    k = k.astype(BF16).astype(F32)
                    spread.append(jnp.broadcast_to(k, (rows, HD)))
                k = jnp.concatenate(spread, axis=0)
                s = jnp.sum(own_q * k, axis=1, keepdims=True) * scale
                found[n] = jnp.where((lane == request) & (step >= n), s, found[n])
    for n in range(new_count):
        fresh_ref[n] = found[n]

    def one_page(p, carry):
        request = meta[first + p]
        tokens = pl.ds(pl.multiple_of(p * PAGE, PAGE), PAGE)
        for head in range(KVH):
            k = k_ref[tokens, head * HD : (head + 1) * HD]
            q = all_q[request, head * rows : (head + 1) * rows]
            s = lax.dot_general(q, k, (((1,), (1,)), ((), ())), preferred_element_type=F32)
            at = head % kv_local * rows
            out_ref[head // kv_local, at : at + rows, tokens] = (s * scale).astype(BF16)
        return carry

    lax.fori_loop(0, local_pages, one_page, 0)


def partial_scores(new, k, meta, pages, prompts, n_seq, n_tp):
    new_count = new.shape[2]
    tokens = k.shape[0]
    rows = KVH // n_tp * new_count * GROUP
    return pl.pallas_call(
        functools.partial(scores_kernel, pages, n_seq, n_tp),
        in_specs=[VMEM, VMEM, SMEM],
        out_specs=[VMEM, VMEM],
        out_shape=[
            jax.ShapeDtypeStruct((n_tp, rows, tokens), BF16),
            jax.ShapeDtypeStruct((new_count, rows, HD), F32),
        ],
        scratch_shapes=[pltpu.VMEM((prompts, rows * n_tp, HD), BF16)],
        compiler_params=pltpu.CompilerParams(vmem_limit_bytes=16 * MIB),
        cost_estimate=pl.CostEstimate(
            flops=2 * tokens * rows * n_tp * HD, bytes_accessed=3 * MIB, transcendentals=0
        ),
        name="scores",
    )(new, k, meta)


def weights_kernel(pages, prompts, in_ref, meta, w_ref, stats_ref):
    n_tp, rows, tokens = in_ref.shape
    local_pages = tokens // PAGE
    first = lax.axis_index("seq") * local_pages
    lane = lax.broadcasted_iota(jnp.int32, (rows, PAGE), 1)
    scores, maxima, masks, owners = [], [], [], []
    for p in range(local_pages):
        at = slice(p * PAGE, (p + 1) * PAGE)
        total = in_ref[0, :, at].astype(F32)
        for d in range(1, n_tp):
            total = total + in_ref[d, :, at].astype(F32)
        mask = lane < meta[2 * pages + first + p]
        total = jnp.where(mask, total, NEG)
        masks.append(mask)
        scores.append(total)
        maxima.append(jnp.max(total, axis=1, keepdims=True))
        owners.append(meta[first + p])
    quarter = lane // prompts
    spot = lane % prompts
    stats = jnp.where(quarter == 0, NEG, 0.0)
    sums = []
    for p in range(local_pages):
        top = maxima[p]
        for other in range(local_pages):
            if other != p:
                top = jnp.where(owners[p] == owners[other], jnp.maximum(top, maxima[other]), top)
        high = top.astype(BF16).astype(F32)
        low = (top - high).astype(BF16).astype(F32)
        w = jnp.where(masks[p], jnp.exp(scores[p] - (high + low)), 0.0)
        for d in range(n_tp):
            w_ref[d, :, p * PAGE : (p + 1) * PAGE] = w.astype(BF16)
        here = spot == owners[p]
        stats = jnp.where(here & (quarter == 0), high, stats)
        stats = jnp.where(here & (quarter == 1), low, stats)
        part = jnp.sum(w, axis=1, keepdims=True)
        stats = stats + jnp.where(here & (quarter == 2), part, 0.0)
    high = stats.astype(BF16).astype(F32)
    low = pltpu.roll(stats - high, prompts, 1)
    stats_ref[...] = jnp.where(quarter == 3, low, stats).astype(BF16)


def softmax_weights(chunks, meta, pages, prompts):
    n_tp, rows, tokens = chunks.shape
    return pl.pallas_call(
        functools.partial(weights_kernel, pages, prompts),
        in_specs=[VMEM, SMEM],
        out_specs=[VMEM, VMEM],
        out_shape=[
            jax.ShapeDtypeStruct((n_tp, rows, tokens), BF16),
            jax.ShapeDtypeStruct((rows, PAGE), BF16),
        ],
        compiler_params=pltpu.CompilerParams(vmem_limit_bytes=8 * MIB),
        name="weights",
    )(chunks, meta)


def weighted_kernel(w_ref, v_ref, meta, out_ref, total):
    n_tp, rows_local, tokens_here = w_ref.shape
    kv_local = KVH // n_tp
    rows = rows_local // kv_local
    local_pages = tokens_here // PAGE
    first = lax.axis_index("seq") * local_pages
    total[...] = jnp.zeros_like(total)

    def one_page(p, carry):
        request = meta[first + p]
        tokens = pl.ds(pl.multiple_of(p * PAGE, PAGE), PAGE)
        for head in range(KVH):
            v = v_ref[tokens, head * HD : (head + 1) * HD]
            at = head % kv_local * rows
            w = w_ref[head // kv_local, at : at + rows, tokens]
            total[request, head * rows : (head + 1) * rows] += jnp.dot(
                w, v, preferred_element_type=F32
            )
        return carry

    lax.fori_loop(0, local_pages, one_page, 0)
    for d in range(n_tp):
        out_ref[d] = total[:, d * rows_local : (d + 1) * rows_local].astype(BF16)


def weighted_values(weights, v, meta, prompts):
    n_tp, rows, _ = weights.shape
    return pl.pallas_call(
        weighted_kernel,
        in_specs=[VMEM, VMEM, SMEM],
        out_specs=VMEM,
        out_shape=jax.ShapeDtypeStruct((n_tp, prompts, rows, HD), BF16),
        scratch_shapes=[pltpu.VMEM((prompts, rows * n_tp, HD), F32)],
        compiler_params=pltpu.CompilerParams(vmem_limit_bytes=24 * MIB),
        name="weighted",
    )(weights, v, meta)


def summed_kernel(in_ref, stats_ref, out_ref):
    n_tp, prompts, _, _ = in_ref.shape
    total = in_ref[0].astype(F32)
    for d in range(1, n_tp):
        total = total + in_ref[d].astype(F32)
    for s in range(out_ref.shape[0]):
        out_ref[s, :prompts] = total.astype(BF16)
        out_ref[s, prompts] = stats_ref[...]


def summed(chunks, stats, n_seq):
    _, prompts, rows, _ = chunks.shape
    return pl.pallas_call(
        summed_kernel,
        in_specs=[VMEM, VMEM],
        out_specs=VMEM,
        out_shape=jax.ShapeDtypeStruct((n_seq, prompts + 1, rows, HD), BF16),
        compiler_params=pltpu.CompilerParams(vmem_limit_bytes=8 * MIB),
        name="summed",
    )(chunks, stats)


def output_kernel(n_tp, in_ref, fresh_ref, new_ref, w_ref, out_ref, held):
    n_seq, more, rows_local, _ = in_ref.shape
    prompts = more - 1
    new_count = fresh_ref.shape[0]
    rows = new_count * GROUP
    kv_local = rows_local // rows
    heads = kv_local * GROUP
    own_rows = prompts // n_seq
    me = lax.axis_index("tp")

    @pl.when(pl.program_id(0) == 0)
    def _():
        tops, parts = [], []
        for s in range(n_seq):
            stats = in_ref[s, prompts].astype(F32)
            folded = stats + pltpu.roll(stats, HD - prompts, 1)
            tops.append(folded)
            parts.append(pltpu.roll(folded, HD - 2 * prompts, 1))
        fresh = [fresh_ref[n] for n in range(new_count)]
        top = fresh[0]
        for other in fresh[1:] + tops:
            top = jnp.maximum(top, other)
        weights = [jnp.exp(f - top) for f in fresh]
        factors = [jnp.exp(t - top) for t in tops]
        total = weights[0]
        for w in weights[1:]:
            total = total + w
        for f, part in zip(factors, parts):
            total = total + f * part
        weights = [w / total for w in weights]
        factors = [f / total for f in factors]
        for r in range(prompts):
            sums = jnp.zeros((rows_local, HD), F32)
            for s in range(n_seq):
                sums = sums + factors[s][:, r : r + 1] * in_ref[s, r].astype(F32)
            for n in range(new_count):
                both = new_ref[r // own_rows * n_tp + me, r % own_rows, n].astype(F32)
                value = jnp.concatenate(
                    [
                        jnp.broadcast_to(both[heads + 2 * g + 1 : heads + 2 * g + 2], (rows, HD))
                        for g in range(kv_local)
                    ],
                    axis=0,
                )
                sums = sums + weights[n][:, r : r + 1] * value
            for g in range(kv_local):
                for n in range(new_count):
                    at = g * rows + n * GROUP
                    held[g * GROUP : (g + 1) * GROUP, r * new_count + n] = sums[at : at + GROUP]

    left = jnp.concatenate([held[h].astype(BF16) for h in range(heads)], axis=1)
    product = jnp.dot(left, w_ref[...], preferred_element_type=F32).astype(BF16)
    for d in range(n_tp):
        out_ref[d] = product


def output_partial(gathered, fresh, new, out_weight, n_tp):
    new_count = fresh.shape[0]
    prompts = gathered.shape[1] - 1
    depth, columns = out_weight.shape
    width = min(columns, 512)
    whole = lambda a: pl.BlockSpec(a.shape, lambda i: (0,) * a.ndim)
    return pl.pallas_call(
        functools.partial(output_kernel, n_tp),
        grid=(columns // width,),
        in_specs=[
            whole(gathered),
            whole(fresh),
            whole(new),
            pl.BlockSpec((depth, width), lambda i: (0, i)),
        ],
        out_specs=pl.BlockSpec((n_tp, prompts * new_count, width), lambda i: (0, 0, i)),
        out_shape=jax.ShapeDtypeStruct((n_tp, prompts * new_count, columns), BF16),
        scratch_shapes=[pltpu.VMEM((depth // HD, prompts * new_count, HD), F32)],
        compiler_params=pltpu.CompilerParams(vmem_limit_bytes=24 * MIB),
        name="output",
    )(gathered, fresh, new, out_weight)


def final_kernel(in_ref, res_ref, out_ref):
    prompts, new_count, _ = out_ref.shape
    total = in_ref[0].astype(F32)
    for d in range(1, in_ref.shape[0]):
        total = total + in_ref[d].astype(F32)
    for r in range(prompts):
        out_ref[r] = res_ref[r].astype(F32) + total[r * new_count : (r + 1) * new_count]


def final_sum(pieces, residual):
    return pl.pallas_call(
        final_kernel,
        in_specs=[VMEM, VMEM],
        out_specs=VMEM,
        out_shape=jax.ShapeDtypeStruct(residual.shape, F32),
        compiler_params=pltpu.CompilerParams(vmem_limit_bytes=8 * MIB),
        name="final",
    )(pieces, residual)


def on_device(
    prefill_states, kv_weight, page_counts, tail_tokens, new_query, new_keyval, residual, out_weight
):
    n_seq, n_tp = lax.axis_size("seq"), lax.axis_size("tp")
    own_rows, new_count, _ = new_query.shape
    prompts = page_counts.shape[0]
    pages = prefill_states.shape[0] // PAGE * n_seq
    new = jnp.concatenate(
        [
            new_query.reshape(own_rows, new_count, QH // n_tp, HD),
            new_keyval.reshape(own_rows, new_count, 2 * KVH // n_tp, HD),
        ],
        axis=2,
    )
    new = exchange(jnp.broadcast_to(new, (n_seq * n_tp,) + new.shape), ("seq", "tp"))
    k, meta = project_keys(prefill_states, kv_weight, page_counts, tail_tokens, pages)
    v = project_values(prefill_states, kv_weight)
    scores, fresh = partial_scores(new, k, meta, pages, prompts, n_seq, n_tp)
    weights, stats = softmax_weights(exchange(scores, "tp"), meta, pages, prompts)
    chunks = weighted_values(exchange(weights, "tp"), v, meta, prompts)
    gathered = exchange(summed(exchange(chunks, "tp"), stats, n_seq), "seq")
    partial = output_partial(gathered, fresh, new, out_weight, n_tp)
    return final_sum(exchange(partial, "tp"), residual)


def solution(mesh):
    placed = (
        P(("groups", "seq"), "tp"),
        P("tp", None),
        P("groups"),
        P("groups"),
        P(("groups", "seq"), None, "tp"),
        P(("groups", "seq"), None, "tp"),
        P("groups", None, "seq"),
        P("tp", "seq"),
    )
    return jax.shard_map(
        on_device, mesh=mesh, in_specs=placed, out_specs=P("groups", None, "seq"), check_vma=False
    )
```

time: 116 us -> 102 us (0.88)
  blocking collectives: 0 us -> 46.6 us
  starting transfers between devices: 33.5 us -> 10.8 us
  waiting for transfers between devices: 22.1 us -> 0.01 us
  Pallas kernels: 42 us -> 26.2 us
    all_to_all x0 -> x4, blocking collectives: none -> 46.6 us  [exchange(): return lax.all_to_all(chunks, axis, 0, 0)]
    ppermute x27 -> x0, starting transfers between devices: 33.5 us -> none  [the longest x21 24.5 us: shifts(): lax.ppermute(value, axis, [(i, (i + d) % size) for i in range(size)])]
    ppermute x27 -> x0, waiting for transfers between devices: 22.1 us -> none  [the longest x21 18.5 us: shifts(): lax.ppermute(value, axis, [(i, (i + d) % size) for i in range(size)])]
    all_to_all x0 -> x2, starting transfers between devices: none -> 10.8 us  [exchange(): return lax.all_to_all(chunks, axis, 0, 0)]
    pallas_call x7 -> x6, Pallas kernels: 21.4 us -> 10.7 us  [the longest x1 3.6 us: partial_scores(): pl.pallas_call(functools.partial(scores_kernel, pages, n_seq, n_tp), in_s...]
    pallas_call x1, Pallas kernels: 11.6 us -> 9.04 us  [project_keys(): pl.pallas_call(functools.partial(keys_kernel, pages, prompts), grid=(KVH...]
    pallas_call x1, Pallas kernels: 8.91 us -> 6.41 us  [project_values(): pl.pallas_call(values_kernel, grid=(KVH // 2,), in_specs=[pl.BlockSpec((t...]
    unnamed x64 -> x16, local copies, waits for them, and re-layouts: 15.8 us -> 15.8 us
  transfers between devices with their start and end apart: 27 -> 2, of which waited for: 13 -> 0; matrix products, arithmetic and copies ran while one was open for 1% -> 0% of each run, Pallas kernels for 25% -> 15%
where the time goes in v2:
time: 102 us; the launch traced here: 101 us
  blocking collectives  46.6 us (46%)
  Pallas kernels  26.2 us (26%)
  local copies, waits for them, and re-layouts  16.8 us (16%)
  starting transfers between devices  10.8 us (11%)
    all_to_all x4, blocking collectives, exchange(): return lax.all_to_all(chunks, axis, 0, 0)  46.6 us
    unnamed x16, local copies, waits for them, and re-layouts  15.8 us
    all_to_all x2, starting transfers between devices, exchange(): return lax.all_to_all(chunks, axis, 0, 0)  10.8 us
    pallas_call x1, Pallas kernels, project_keys(): pl.pallas_call(functools.partial(keys_kernel, pages, prompts), grid=(KVH...  9.04 us
    pallas_call x1, Pallas kernels, project_values(): pl.pallas_call(values_kernel, grid=(KVH // 2,), in_specs=[pl.BlockSpec((t...  6.41 us
    pallas_call x1, Pallas kernels, partial_scores(): pl.pallas_call(functools.partial(scores_kernel, pages, n_seq, n_tp), in_s...  3.6 us
    pallas_call x1, Pallas kernels, output_partial(): pl.pallas_call(functools.partial(output_kernel, n_tp), grid=(columns // w...  2.77 us
    pallas_call x1, Pallas kernels, weighted_values(): pl.pallas_call(weighted_kernel, in_specs=[VMEM, VMEM, SMEM], out_specs=VM...  2.1 us
  transfers between devices with their start and end apart: 2, of which 0 were waited for; matrix products, arithmetic and copies ran while one was open for 0% of the time, Pallas kernels for 15%

profile of v2, /device:TPU:0, one launch (start us, length us, event | category | flops | bytes accessed | tf_op | source)
XLA Modules:
  0.0 101.2 jit_solution(1125102803449619747)
XLA Ops:
  0.0 0.8 pad_maximum_fusion
  0.8 0.9 broadcast_in_dim.3
  1.7 7.4 %all-to-all-start = ((bf16[16,2,2,20,128]{4,2,3,1,0:T(2,128)(2,1)}), bf16[16,2,2,20,128]{4,2,3,1,0:T(2,128)(2,1)S(1)}, u32[]{:S(2)}, u32[]{:S(2)}) async-start(bf16[16,2,2,20,128]{4,2,3,1,0:T(2,128)(2,1)} %broadcast_in_dim.3), calls=%async_computation | async-start | bytes 655360 | tf_op jit(solution)/shard_map/all_to_all | solution.py:26
  9.1 0.0 copy-start
  9.1 3.4 %copy-done = bf16[2048,2048]{1,0:T(8,128)(2,1)S(1)} copy-done((bf16[2048,2048]{1,0:T(8,128)(2,1)S(1)}, bf16[2048,2048]{1,0:T(8,128)(2,1)}, u32[]{:S(2)}) %copy-start) | copy-done | bytes 8388632
  12.4 0.0 copy-start.2
  12.4 2.2 %copy-done.2 = bf16[1024,2048]{1,0:T(8,128)(2,1)S(1)} copy-done((bf16[1024,2048]{1,0:T(8,128)(2,1)S(1)}, bf16[1024,2048]{1,0:T(8,128)(2,1)}, u32[]{:S(2)}) %copy-start.2) | copy-done | bytes 4194328
  14.6 0.0 copy-start.6
  14.6 0.7 copy-done.6
  15.3 0.0 copy-start.7
  15.3 0.7 copy-done.7
  15.9 9.0 %keys.1 = (bf16[1024,1024]{1,0:T(8,128)(2,1)S(1)}, s32[104]{0:T(128)S(1)}) custom-call(bf16[1024,2048]{1,0:T(8,128)(2,1)S(1)} %copy-done.2, bf16[2048,2048]{1,0:T(8,128)(2,1)S(1)} %copy-done, bf16[2048,2048]{1,0:T(8,128)(2,1)S(1)} %copy-done, s32[8]{0:T(128)S(1)} %copy-done.6, s32[8]{0:T(128)S(1)} %copy-done.7), custom_call_target="tpu_custom_call" | custom-call | flops 4294967296 | bytes 12582912 | tf_op jit(solution)/shard_map/keys/pallas_call | solution.py:91
  25.0 0.0 all-to-all-done
  25.0 0.1 copy.11.new_ref
  25.1 3.6 %scores.1 = (bf16[4,32,1024]{2,1,0:T(8,128)(2,1)S(1)}, f32[2,32,128]{2,1,0:T(8,128)S(1)}) custom-call(bf16[16,2,2,20,128]{4,3,2,1,0:T(8,128)(2,1)S(1)} %copy.11.new_ref, bf16[1024,1024]{1,0:T(8,128)(2,1)S(1)} %get-tuple-element.11.k_ref, s32[104]{0:T(128)S(1)} %get-tuple-element.12.meta), custom_call_target="tpu_custom_call" | custom-call | flops 33554432 | bytes 3145728 | tf_op jit(solution)/shard_map/scores/pallas_call | solution.py:201
  28.7 14.0 %all_to_all.30.in_ref = bf16[4,32,1024]{2,1,0:T(8,128)(2,1)S(1)} all-to-all(bf16[4,32,1024]{2,1,0:T(8,128)(2,1)S(1)} %get-tuple-element.13), channel_id=1, replica_groups=mesh['groups'=2,'seq'=4,'tp'=4] {'tp'}, dimensions={0} | all-to-all | bytes 524288 | tf_op jit(solution)/shard_map/all_to_all | solution.py:26
  42.7 1.5 %weights.1 = (bf16[4,32,1024]{2,1,0:T(8,128)(2,1)}, bf16[32,128]{1,0:T(8,128)(2,1)S(1)}) custom-call(bf16[4,32,1024]{2,1,0:T(8,128)(2,1)S(1)} %all_to_all.30.in_ref, s32[104]{0:T(128)S(1)} %get-tuple-element.12.meta), custom_call_target="tpu_custom_call" | custom-call | tf_op jit(solution)/shard_map/weights/pallas_call | solution.py:261
  44.2 3.4 %all-to-all-start.2 = ((bf16[4,32,1024]{2,1,0:T(8,128)(2,1)}), bf16[4,32,1024]{2,1,0:T(8,128)(2,1)S(1)}, u32[]{:S(2)}, u32[]{:S(2)}) async-start(bf16[4,32,1024]{2,1,0:T(8,128)(2,1)} %get-tuple-element.14), calls=%async_computation.2 | async-start | bytes 524288 | tf_op jit(solution)/shard_map/all_to_all | solution.py:26
  47.6 0.0 copy-start.1
  47.6 3.4 %copy-done.1 = bf16[2048,2048]{1,0:T(8,128)(2,1)S(1)} copy-done((bf16[2048,2048]{1,0:T(8,128)(2,1)S(1)}, bf16[2048,2048]{1,0:T(8,128)(2,1)}, u32[]{:S(2)}) %copy-start.1) | copy-done | bytes 8388632
  51.0 0.0 copy-start.3
  51.0 2.2 %copy-done.3 = bf16[1024,2048]{1,0:T(8,128)(2,1)S(1)} copy-done((bf16[1024,2048]{1,0:T(8,128)(2,1)S(1)}, bf16[1024,2048]{1,0:T(8,128)(2,1)}, u32[]{:S(2)}) %copy-start.3) | copy-done | bytes 4194328
  53.2 6.4 %values.1.v_ref = bf16[1024,1024]{1,0:T(8,128)(2,1)S(1)} custom-call(bf16[1024,2048]{1,0:T(8,128)(2,1)S(1)} %copy-done.3, bf16[2048,2048]{1,0:T(8,128)(2,1)S(1)} %copy-done.1, bf16[2048,2048]{1,0:T(8,128)(2,1)S(1)} %copy-done.1), custom_call_target="tpu_custom_call" | custom-call | flops 4294967296 | bytes 12582912 | tf_op jit(solution)/shard_map/values/pallas_call | solution.py:117
  59.6 0.0 all-to-all-done.2.w_ref
  59.6 2.1 %weighted.1 = bf16[4,8,32,128]{3,2,1,0:T(8,128)(2,1)S(1)} custom-call(bf16[4,32,1024]{2,1,0:T(8,128)(2,1)S(1)} %all-to-all-done.2.w_ref, bf16[1024,1024]{1,0:T(8,128)(2,1)S(1)} %values.1.v_ref, s32[104]{0:T(128)S(1)} %get-tuple-element.12.meta), custom_call_target="tpu_custom_call" | custom-call | tf_op jit(solution)/shard_map/weighted/pallas_call | solution.py:301
  61.7 12.0 %all_to_all.31.in_ref = bf16[4,8,32,128]{3,2,1,0:T(8,128)(2,1)S(1)} all-to-all(bf16[4,8,32,128]{3,2,1,0:T(8,128)(2,1)S(1)} %weighted.1), channel_id=1, replica_groups=mesh['groups'=2,'seq'=4,'tp'=4] {'tp'}, dimensions={0} | all-to-all | bytes 524288 | tf_op jit(solution)/shard_map/all_to_all | solution.py:26
  73.7 8.9 %all_to_all.32.in_ref = bf16[4,9,32,128]{3,2,1,0:T(8,128)(2,1)S(1)} all-to-all(bf16[4,9,32,128]{3,2,1,0:T(8,128)(2,1)S(1)} %summed.1), channel_id=1, replica_groups=mesh['groups'=2,'seq'=4,'tp'=4] {'seq'}, dimensions={0} | all-to-all | bytes 589824 | tf_op jit(solution)/shard_map/all_to_all | solution.py:26
  82.7 3.4 %copy-done.4 = bf16[2048,2048]{1,0:T(8,128)(2,1)S(1)} copy-done((bf16[2048,2048]{1,0:T(8,128)(2,1)S(1)}, bf16[2048,2048]{1,0:T(8,128)(2,1)}, u32[]{:S(2)}) %copy-start.4) | copy-done | bytes 8388632
  86.0 2.8 %output.1 = bf16[4,16,2048]{2,1,0:T(8,128)(2,1)S(1)} custom-call(bf16[4,9,32,128]{3,2,1,0:T(8,128)(2,1)S(1)} %all_to_all.32.in_ref, f32[2,32,128]{2,1,0:T(8,128)S(1)} %get-tuple-element.16.fresh_ref, bf16[16,2,2,20,128]{4,3,2,1,0:T(8,128)(2,1)S(1)} %copy.11.new_ref, bf16[2048,2048]{1,0:T(8,128)(2,1)S(1)} %copy-done.4), custom_call_target="tpu_custom_call" | custom-call | tf_op jit(solution)/shard_map/output/pallas_call | solution.py:396
  88.8 11.7 %all_to_all.33.in_ref = bf16[4,16,2048]{2,1,0:T(8,128)(2,1)S(1)} all-to-all(bf16[4,16,2048]{2,1,0:T(8,128)(2,1)S(1)} %output.1), channel_id=1, replica_groups=mesh['groups'=2,'seq'=4,'tp'=4] {'tp'}, dimensions={0} | all-to-all | bytes 524288 | tf_op jit(solution)/shard_map/all_to_all | solution.py:26
  100.5 0.0 copy-done.5
  100.5 0.7 final.1
  (3 shorter events, 0.0 us)
Async XLA Ops:
  1.7 23.3 %all-to-all-start = ((bf16[16,2,2,20,128]{4,2,3,1,0:T(2,128)(2,1)}), bf16[16,2,2,20,128]{4,2,3,1,0:T(2,128)(2,1)S(1)}, u32[]{:S(2)}, u32[]{:S(2)}) async-start(bf16[16,2,2,20,128]{4,2,3,1,0:T(2,128)(2,1)} %broadcast_in_dim.3), calls=%async_computation | async-start | bytes 655360 | tf_op jit(solution)/shard_map/all_to_all | solution.py:26
  9.1 3.4 %copy-start = (bf16[2048,2048]{1,0:T(8,128)(2,1)S(1)}, bf16[2048,2048]{1,0:T(8,128)(2,1)}, u32[]{:S(2)}) copy-start(bf16[2048,2048]{1,0:T(8,128)(2,1)} %wb_ref.3) | copy-start | bytes 25165828
  12.4 2.2 %copy-start.2 = (bf16[1024,2048]{1,0:T(8,128)(2,1)S(1)}, bf16[1024,2048]{1,0:T(8,128)(2,1)}, u32[]{:S(2)}) copy-start(bf16[1024,2048]{1,0:T(8,128)(2,1)} %x_ref.3) | copy-start | bytes 12582916
  14.6 0.7 copy-start.6
  15.3 0.7 copy-start.7
  44.2 15.4 %all-to-all-start.2 = ((bf16[4,32,1024]{2,1,0:T(8,128)(2,1)}), bf16[4,32,1024]{2,1,0:T(8,128)(2,1)S(1)}, u32[]{:S(2)}, u32[]{:S(2)}) async-start(bf16[4,32,1024]{2,1,0:T(8,128)(2,1)} %get-tuple-element.14), calls=%async_computation.2 | async-start | bytes 524288 | tf_op jit(solution)/shard_map/all_to_all | solution.py:26
  47.6 3.4 %copy-start.1 = (bf16[2048,2048]{1,0:T(8,128)(2,1)S(1)}, bf16[2048,2048]{1,0:T(8,128)(2,1)}, u32[]{:S(2)}) copy-start(bf16[2048,2048]{1,0:T(8,128)(2,1)} %wb_ref.3) | copy-start | bytes 25165828
  51.0 2.2 %copy-start.3 = (bf16[1024,2048]{1,0:T(8,128)(2,1)S(1)}, bf16[1024,2048]{1,0:T(8,128)(2,1)}, u32[]{:S(2)}) copy-start(bf16[1024,2048]{1,0:T(8,128)(2,1)} %x_ref.3) | copy-start | bytes 12582916
  82.7 3.4 %copy-start.4 = (bf16[2048,2048]{1,0:T(8,128)(2,1)S(1)}, bf16[2048,2048]{1,0:T(8,128)(2,1)}, u32[]{:S(2)}) copy-start(bf16[2048,2048]{1,0:T(8,128)(2,1)} %w_ref.1) | copy-start | bytes 25165828
  86.0 14.4 %copy-start.5 = (bf16[8,2,2048]{2,1,0:T(2,128)(2,1)S(1)}, bf16[8,2,2048]{2,1,0:T(2,128)(2,1)}, u32[]{:S(2)}) copy-start(bf16[8,2,2048]{2,1,0:T(2,128)(2,1)} %res_ref.1) | copy-start | bytes 196612

commit v3 on v2

v3 whole, which is shorter than its diff:
```python
import functools
import math

import jax
import jax.numpy as jnp
from jax import lax
from jax.experimental import pallas as pl
from jax.experimental.pallas import tpu as pltpu
from jax.sharding import PartitionSpec as P

QH = 64
KVH = 8
HD = 128
PAGE = 128
GROUP = QH // KVH
NEG = -1e30
F32 = jnp.float32
BF16 = jnp.bfloat16
MIB = 1 << 20

VMEM = pl.BlockSpec(memory_space=pltpu.VMEM)
SMEM = pl.BlockSpec(memory_space=pltpu.SMEM)


def pairs(value, axis, d):
    return lax.ppermute(value, axis, [(i, i ^ d) for i in range(lax.axis_size(axis))])


def exchange(chunks, axis):
    return [chunks[0]] + [pairs(chunks[d], axis, d) for d in range(1, len(chunks))]


def gather(value, axis):
    return exchange([value] * lax.axis_size(axis), axis)


def lane_freqs(rows):
    lane = lax.broadcasted_iota(jnp.int32, (rows, HD), 1) % (HD // 2)
    return jnp.exp(-(lane.astype(F32) * (2.0 / HD)) * math.log(500000.0))


def sine_sign(rows):
    lane = lax.broadcasted_iota(jnp.int32, (rows, HD), 1)
    return jnp.where(lane < HD // 2, -1.0, 1.0)


def by_row(rows, numbers):
    row = lax.broadcasted_iota(jnp.int32, (rows, HD), 0)
    out = jnp.zeros((rows, HD), F32)
    for i, number in enumerate(numbers):
        out = jnp.where(row == i, number.astype(F32), out)
    return out


def page_table(pages, prompts, counts, tails, meta):
    def one_prompt(r, start):
        length = (counts[r] - 1) * PAGE + tails[r]
        meta[3 * pages + r] = length

        def one_page(i, carry):
            meta[start + i] = r
            meta[pages + start + i] = i * PAGE
            meta[2 * pages + start + i] = jnp.minimum(length - i * PAGE, PAGE)
            return carry

        lax.fori_loop(0, counts[r], one_page, 0)
        return start + counts[r]

    lax.fori_loop(0, prompts, one_prompt, 0)


def rotation_tables(pages, local_pages, meta, cos_s, sin_s):
    freqs = lane_freqs(8)
    low = lax.broadcasted_iota(jnp.int32, (8, HD), 0).astype(F32) * freqs
    low_cos, low_sin = jnp.cos(low), jnp.sin(low)
    high = lax.broadcasted_iota(jnp.int32, (PAGE // 8, HD), 0).astype(F32) * 8.0
    high = high * lane_freqs(PAGE // 8)
    high_cos, high_sin = jnp.cos(high), jnp.sin(high)
    first = lax.axis_index("seq") * local_pages
    base = by_row(local_pages, [meta[pages + first + p] for p in range(local_pages)])
    base = base * lane_freqs(local_pages)
    base_cos, base_sin = jnp.cos(base), jnp.sin(base)
    sign = sine_sign(8)
    for i in range(PAGE // 8):
        c, s = high_cos[i : i + 1], high_sin[i : i + 1]
        cosine, sine = low_cos * c - low_sin * s, low_sin * c + low_cos * s
        for p in range(local_pages):
            at = slice(p * PAGE + i * 8, p * PAGE + i * 8 + 8)
            c, s = base_cos[p : p + 1], base_sin[p : p + 1]
            cos_s[at] = cosine * c - sine * s
            sin_s[at] = sign * (sine * c + cosine * s)


def accumulate(x_ref, weights, acc, finish):
    step, last = pl.program_id(0), pl.num_programs(0) - 1
    weight = jnp.concatenate([w[...] for w in weights], axis=1)
    tall = 512

    def product(start):
        return jnp.dot(x_ref[start : start + tall], weight, preferred_element_type=F32)

    starts = range(0, x_ref.shape[0], tall)

    @pl.when(step == 0)
    def _():
        for start in starts:
            acc[start : start + tall] = product(start)

    @pl.when((step > 0) & (step < last))
    def _():
        for start in starts:
            acc[start : start + tall] += product(start)

    @pl.when(step == last)
    def _():
        for start in starts:
            finish(slice(start, start + tall), acc[start : start + tall] + product(start))


def keys_kernel(pages, prompts, heads, table, *refs):
    x_ref, *weights = refs[: heads + 1]
    if table:
        counts, tails, out_ref, meta, cos_s, sin_s, acc = refs[heads + 1 :]
    else:
        meta, _, out_ref, cos_s, sin_s, acc = refs[heads + 1 :]

    @pl.when(pl.program_id(0) == 0)
    def _():
        if table:
            page_table(pages, prompts, counts, tails, meta)
        rotation_tables(pages, x_ref.shape[0] // PAGE, meta, cos_s, sin_s)

    def finish(at, product):
        cosine, sine = cos_s[at], sin_s[at]
        for h in range(heads):
            k = product[:, h * HD : (h + 1) * HD]
            k = k * cosine + pltpu.roll(k, HD // 2, 1) * sine
            out_ref[at, h * HD : (h + 1) * HD] = k.astype(BF16)

    accumulate(x_ref, weights, acc, finish)


def values_kernel(heads, *refs):
    x_ref, *weights = refs[: heads + 1]
    _, out_ref, acc = refs[heads + 1 :]

    def finish(at, product):
        out_ref[at] = product.astype(BF16)

    accumulate(x_ref, weights, acc, finish)


BIG = 57 * MIB


def projection_specs(x, heads, columns):
    tokens, depth = x.shape
    block = min(depth // 2, 512)
    at = lambda c: pl.BlockSpec((block, HD), lambda i: (i, c))
    specs = [pl.BlockSpec((tokens, block), lambda i: (0, i))] + [at(c) for c in columns]
    return dict(
        grid=(depth // block,),
        compiler_params=pltpu.CompilerParams(vmem_limit_bytes=BIG),
        cost_estimate=pl.CostEstimate(
            flops=2 * tokens * depth * heads * HD,
            bytes_accessed=2 * depth * (tokens + heads * HD) + 2 * tokens * heads * HD,
            transcendentals=0,
        ),
    ), specs


def project_keys(x, kv_weight, first, heads, pages, prompts, scalars, after=None):
    tokens, _ = x.shape
    table = after is None
    call, specs = projection_specs(x, heads, [2 * (first + h) for h in range(heads)])
    out_specs = [pl.BlockSpec((tokens, heads * HD), lambda i: (0, 0)), SMEM]
    out_shape = [
        jax.ShapeDtypeStruct((tokens, heads * HD), BF16),
        jax.ShapeDtypeStruct((3 * pages + prompts,), jnp.int32),
    ]
    extra = [SMEM, SMEM] if table else [SMEM, pl.BlockSpec(memory_space=pl.ANY)]
    operands = list(scalars) + ([] if table else [after])
    return pl.pallas_call(
        functools.partial(keys_kernel, pages, prompts, heads, table),
        in_specs=specs + extra,
        out_specs=out_specs if table else out_specs[0],
        out_shape=out_shape if table else out_shape[0],
        scratch_shapes=[
            pltpu.VMEM((tokens, HD), F32),
            pltpu.VMEM((tokens, HD), F32),
            pltpu.VMEM((tokens, heads * HD), F32),
        ],
        name="keys",
        **call,
    )(x, *[kv_weight] * heads, *operands)


def project_values(x, kv_weight, first, heads, after):
    tokens, _ = x.shape
    call, specs = projection_specs(x, heads, [2 * (first + h) + 1 for h in range(heads)])
    return pl.pallas_call(
        functools.partial(values_kernel, heads),
        in_specs=specs + [pl.BlockSpec(memory_space=pl.ANY)],
        out_specs=pl.BlockSpec((tokens, heads * HD), lambda i: (0, 0)),
        out_shape=jax.ShapeDtypeStruct((tokens, heads * HD), BF16),
        scratch_shapes=[pltpu.VMEM((tokens, heads * HD), F32)],
        name="values",
        **call,
    )(x, *[kv_weight] * heads, after)


def stacked_kernel(n_tp, *refs):
    for d in range(n_tp):
        refs[-1][d] = refs[d][...]


def stacked(pieces, after):
    n_tp = len(pieces)
    return pl.pallas_call(
        functools.partial(stacked_kernel, n_tp),
        in_specs=[VMEM] * n_tp + [pl.BlockSpec(memory_space=pl.ANY)],
        out_specs=VMEM,
        out_shape=jax.ShapeDtypeStruct((n_tp,) + pieces[0].shape, BF16),
        compiler_params=pltpu.CompilerParams(vmem_limit_bytes=8 * MIB),
        name="stacked",
    )(*pieces, after)


def scores_kernel(pages, n_seq, n_tp, *refs):
    new = refs[:n_seq]
    ka_ref, kb_ref, meta = refs[n_seq : n_seq + 3]
    outs = refs[n_seq + 3 : n_seq + 3 + n_tp]
    fresh_ref, all_q, held, ready, cosines, sines = refs[n_seq + 3 + n_tp :]
    kv_local = KVH // n_tp
    local_pages = ka_ref.shape[0] // PAGE
    _, own_rows, new_count, _, _ = new[0].shape
    prompts = own_rows * n_seq
    rows = new_count * GROUP
    heads = kv_local * GROUP
    scale = 1.0 / math.sqrt(HD)
    me = lax.axis_index("tp")
    seq = lax.axis_index("seq")
    first = seq * local_pages
    step = lax.broadcasted_iota(jnp.int32, (kv_local * rows, HD), 0) % rows // GROUP
    lane = lax.broadcasted_iota(jnp.int32, (kv_local * rows, HD), 1)
    found = [jnp.full((kv_local * rows, HD), NEG, F32) for _ in range(new_count)]
    spots = [meta[3 * pages + r] + n for r in range(prompts) for n in range(new_count)]
    angles = by_row(len(spots), spots) * lane_freqs(len(spots))
    cosines[...] = jnp.cos(angles)
    sines[...] = jnp.sin(angles) * sine_sign(len(spots))
    for ds in range(n_seq):
        for rr in range(own_rows):
            request = (seq ^ ds) * own_rows + rr
            turn = [
                (
                    cosines[pl.ds(request * new_count + n, 1)],
                    sines[pl.ds(request * new_count + n, 1)],
                )
                for n in range(new_count)
            ]
            for dt in range(n_tp):
                block = [new[ds][dt, rr, n].astype(F32) for n in range(new_count)]
                for g in range(kv_local):
                    parts = []
                    for n in range(new_count):
                        q = block[n][g * GROUP : (g + 1) * GROUP]
                        parts.append(q * turn[n][0] + pltpu.roll(q, HD // 2, 1) * turn[n][1])
                    part = jnp.concatenate(parts, axis=0).astype(BF16)
                    at = ((me ^ dt) * kv_local + g) * rows
                    all_q[request, pl.ds(pl.multiple_of(at, rows), rows)] = part
                    if dt == 0:
                        held[g * rows : (g + 1) * rows] = part.astype(F32)
                if dt == 0:
                    for n in range(new_count):
                        spread = []
                        for g in range(kv_local):
                            k = block[n][heads + 2 * g : heads + 2 * g + 1]
                            k = k * turn[n][0] + pltpu.roll(k, HD // 2, 1) * turn[n][1]
                            k = k.astype(BF16).astype(F32)
                            spread.append(jnp.broadcast_to(k, (rows, HD)))
                        k = jnp.concatenate(spread, axis=0)
                        s = jnp.sum(held[...] * k, axis=1, keepdims=True) * scale
                        found[n] = jnp.where((lane == request) & (step >= n), s, found[n])
    for n in range(new_count):
        fresh_ref[n] = found[n]
    half = ka_ref.shape[1] // HD
    for p in range(local_pages):
        request = meta[first + p]
        tokens = slice(p * PAGE, (p + 1) * PAGE)
        for head in range(KVH):
            k_ref = ka_ref if head < half else kb_ref
            k = k_ref[tokens, head % half * HD : (head % half + 1) * HD]
            q = all_q[request, head * rows : (head + 1) * rows]
            s = lax.dot_general(q, k, (((1,), (1,)), ((), ())), preferred_element_type=F32)
            ready[head * rows : (head + 1) * rows, tokens] = (s * scale).astype(BF16)
    count = kv_local * rows
    for d in range(n_tp):
        outs[d][...] = ready[pl.ds(pl.multiple_of((me ^ d) * count, count), count)]


def partial_scores(new, ka, kb, meta, pages, prompts, n_tp):
    n_seq = len(new)
    new_count = new[0].shape[2]
    tokens = ka.shape[0]
    rows = KVH // n_tp * new_count * GROUP
    return pl.pallas_call(
        functools.partial(scores_kernel, pages, n_seq, n_tp),
        in_specs=[VMEM] * (n_seq + 2) + [SMEM],
        out_specs=[VMEM] * (n_tp + 1),
        out_shape=[jax.ShapeDtypeStruct((rows, tokens), BF16)] * n_tp
        + [jax.ShapeDtypeStruct((new_count, rows, HD), F32)],
        scratch_shapes=[
            pltpu.VMEM((prompts, rows * n_tp, HD), BF16),
            pltpu.VMEM((rows, HD), F32),
            pltpu.VMEM((rows * n_tp, tokens), BF16),
            pltpu.VMEM((prompts * new_count, HD), F32),
            pltpu.VMEM((prompts * new_count, HD), F32),
        ],
        compiler_params=pltpu.CompilerParams(vmem_limit_bytes=24 * MIB),
        cost_estimate=pl.CostEstimate(
            flops=2 * tokens * rows * n_tp * HD, bytes_accessed=6 * MIB, transcendentals=0
        ),
        name="scores",
    )(*new, ka, kb, meta)


def weights_kernel(pages, prompts, n_tp, *refs):
    chunks = refs[:n_tp]
    meta, w_ref, stats_ref = refs[n_tp:]
    rows, tokens = w_ref.shape
    local_pages = tokens // PAGE
    first = lax.axis_index("seq") * local_pages
    lane = lax.broadcasted_iota(jnp.int32, (rows, PAGE), 1)
    scores, maxima, masks, owners = [], [], [], []
    for p in range(local_pages):
        at = slice(p * PAGE, (p + 1) * PAGE)
        total = chunks[0][:, at].astype(F32)
        for d in range(1, n_tp):
            total = total + chunks[d][:, at].astype(F32)
        mask = lane < meta[2 * pages + first + p]
        total = jnp.where(mask, total, NEG)
        masks.append(mask)
        scores.append(total)
        maxima.append(jnp.max(total, axis=1, keepdims=True))
        owners.append(meta[first + p])
    quarter = lane // prompts
    spot = lane % prompts
    stats = jnp.where(quarter == 0, NEG, 0.0)
    sums = []
    for p in range(local_pages):
        top = maxima[p]
        for other in range(local_pages):
            if other != p:
                top = jnp.where(owners[p] == owners[other], jnp.maximum(top, maxima[other]), top)
        high = top.astype(BF16).astype(F32)
        low = (top - high).astype(BF16).astype(F32)
        w = jnp.where(masks[p], jnp.exp(scores[p] - (high + low)), 0.0)
        w_ref[:, p * PAGE : (p + 1) * PAGE] = w.astype(BF16)
        here = spot == owners[p]
        stats = jnp.where(here & (quarter == 0), high, stats)
        stats = jnp.where(here & (quarter == 1), low, stats)
        part = jnp.sum(w, axis=1, keepdims=True)
        stats = stats + jnp.where(here & (quarter == 2), part, 0.0)
    high = stats.astype(BF16).astype(F32)
    low = pltpu.roll(stats - high, prompts, 1)
    stats_ref[...] = jnp.where(quarter == 3, low, stats).astype(BF16)


def softmax_weights(chunks, meta, pages, prompts):
    n_tp = len(chunks)
    rows, tokens = chunks[0].shape
    return pl.pallas_call(
        functools.partial(weights_kernel, pages, prompts, n_tp),
        in_specs=[VMEM] * n_tp + [SMEM],
        out_specs=[VMEM, VMEM],
        out_shape=[
            jax.ShapeDtypeStruct((rows, tokens), BF16),
            jax.ShapeDtypeStruct((rows, PAGE), BF16),
        ],
        compiler_params=pltpu.CompilerParams(vmem_limit_bytes=8 * MIB),
        name="weights",
    )(*chunks, meta)


def weighted_kernel(n_tp, *refs):
    pieces = refs[:n_tp]
    va_ref, vb_ref, meta = refs[n_tp : n_tp + 3]
    outs = refs[n_tp + 3 : n_tp + 3 + n_tp]
    ready, total = refs[n_tp + 3 + n_tp :]
    rows_local, tokens_here = pieces[0].shape
    kv_local = KVH // n_tp
    rows = rows_local // kv_local
    local_pages = tokens_here // PAGE
    first = lax.axis_index("seq") * local_pages
    me = lax.axis_index("tp")
    own = [pl.ds(pl.multiple_of((me ^ d) * rows_local, rows_local), rows_local) for d in range(n_tp)]
    for d in range(n_tp):
        ready[own[d]] = pieces[d][...]
    total[...] = jnp.zeros_like(total)
    half = va_ref.shape[1] // HD
    for p in range(local_pages):
        request = meta[first + p]
        tokens = slice(p * PAGE, (p + 1) * PAGE)
        for head in range(KVH):
            v_ref = va_ref if head < half else vb_ref
            v = v_ref[tokens, head % half * HD : (head % half + 1) * HD]
            at = slice(head * rows, (head + 1) * rows)
            total[request, at] += jnp.dot(ready[at, tokens], v, preferred_element_type=F32)
    for d in range(n_tp):
        outs[d][...] = total[:, own[d]].astype(BF16)


def weighted_values(pieces, va, vb, meta, prompts):
    n_tp = len(pieces)
    rows, tokens = pieces[0].shape
    return pl.pallas_call(
        functools.partial(weighted_kernel, n_tp),
        in_specs=[VMEM] * (n_tp + 2) + [SMEM],
        out_specs=[VMEM] * n_tp,
        out_shape=[jax.ShapeDtypeStruct((prompts, rows, HD), BF16)] * n_tp,
        scratch_shapes=[
            pltpu.VMEM((rows * n_tp, tokens), BF16),
            pltpu.VMEM((prompts, rows * n_tp, HD), F32),
        ],
        compiler_params=pltpu.CompilerParams(vmem_limit_bytes=24 * MIB),
        cost_estimate=pl.CostEstimate(
            flops=2 * tokens * rows * n_tp * HD, bytes_accessed=8 * MIB, transcendentals=0
        ),
        name="weighted",
    )(*pieces, va, vb, meta)


def summed_kernel(n_tp, *refs):
    chunks = refs[:n_tp]
    stats_ref, out_ref = refs[n_tp:]
    prompts = chunks[0].shape[0]
    total = chunks[0][...].astype(F32)
    for d in range(1, n_tp):
        total = total + chunks[d][...].astype(F32)
    out_ref[:prompts] = total.astype(BF16)
    out_ref[prompts] = stats_ref[...]


def summed(chunks, stats):
    n_tp = len(chunks)
    prompts, rows, _ = chunks[0].shape
    return pl.pallas_call(
        functools.partial(summed_kernel, n_tp),
        in_specs=[VMEM] * (n_tp + 1),
        out_specs=VMEM,
        out_shape=jax.ShapeDtypeStruct((prompts + 1, rows, HD), BF16),
        compiler_params=pltpu.CompilerParams(vmem_limit_bytes=8 * MIB),
        cost_estimate=pl.CostEstimate(flops=0, bytes_accessed=4 * MIB, transcendentals=0),
        name="summed",
    )(*chunks, stats)


def output_kernel(n_seq, *refs):
    pieces = refs[:n_seq]
    fresh_ref = refs[n_seq]
    new = refs[n_seq + 1 : 2 * n_seq + 1]
    w_ref, out_ref, held = refs[2 * n_seq + 1 :]
    more, rows_local, _ = pieces[0].shape
    prompts = more - 1
    new_count = fresh_ref.shape[0]
    rows = new_count * GROUP
    kv_local = rows_local // rows
    heads = kv_local * GROUP
    own_rows = prompts // n_seq
    seq = lax.axis_index("seq")
    tops, parts = [], []
    for s in range(n_seq):
        stats = pieces[s][prompts].astype(F32)
        folded = stats + pltpu.roll(stats, HD - prompts, 1)
        tops.append(folded)
        parts.append(pltpu.roll(folded, HD - 2 * prompts, 1))
    fresh = [fresh_ref[n] for n in range(new_count)]
    top = fresh[0]
    for other in fresh[1:] + tops:
        top = jnp.maximum(top, other)
    weights = [jnp.exp(f - top) for f in fresh]
    factors = [jnp.exp(t - top) for t in tops]
    total = weights[0]
    for w in weights[1:]:
        total = total + w
    for f, part in zip(factors, parts):
        total = total + f * part
    weights = [w / total for w in weights]
    factors = [f / total for f in factors]
    lane = lax.broadcasted_iota(jnp.int32, (rows_local, HD), 1)
    for r in range(prompts):
        sums = jnp.zeros((rows_local, HD), F32)
        for s in range(n_seq):
            sums = sums + factors[s][:, r : r + 1] * pieces[s][r].astype(F32)
        for g in range(kv_local):
            for n in range(new_count):
                at = g * rows + n * GROUP
                held[g * GROUP : (g + 1) * GROUP, r * new_count + n] = sums[at : at + GROUP]
    for ds in range(n_seq):
        for rr in range(own_rows):
            request = (seq ^ ds) * own_rows + rr
            share = [
                jnp.sum(jnp.where(lane == request, w, 0.0), axis=1, keepdims=True) for w in weights
            ]
            sums = jnp.zeros((rows_local, HD), F32)
            for n in range(new_count):
                both = new[ds][0, rr, n].astype(F32)
                value = [both[heads + 2 * g + 1 : heads + 2 * g + 2] for g in range(kv_local)]
                value = [jnp.broadcast_to(v, (rows, HD)) for v in value]
                sums = sums + share[n] * jnp.concatenate(value, axis=0)
            for g in range(kv_local):
                for n in range(new_count):
                    at = g * rows + n * GROUP
                    held[g * GROUP : (g + 1) * GROUP, request * new_count + n] += sums[
                        at : at + GROUP
                    ]
    left = jnp.concatenate([held[h].astype(BF16) for h in range(heads)], axis=1)
    out_ref[...] = jnp.dot(left, w_ref[...], preferred_element_type=F32).astype(BF16)


def output_partial(pieces, fresh, new, out_weight):
    n_seq = len(pieces)
    new_count = fresh.shape[0]
    prompts = pieces[0].shape[0] - 1
    depth, columns = out_weight.shape
    return pl.pallas_call(
        functools.partial(output_kernel, n_seq),
        in_specs=[VMEM] * (2 * n_seq + 2),
        out_specs=VMEM,
        out_shape=jax.ShapeDtypeStruct((prompts * new_count, columns), BF16),
        scratch_shapes=[pltpu.VMEM((depth // HD, prompts * new_count, HD), F32)],
        compiler_params=pltpu.CompilerParams(vmem_limit_bytes=24 * MIB),
        name="output",
    )(*pieces, fresh, *new, out_weight)


def final_kernel(n_tp, *refs):
    pieces = refs[:n_tp]
    res_ref, out_ref = refs[n_tp:]
    prompts, new_count, _ = out_ref.shape
    total = pieces[0][...].astype(F32)
    for d in range(1, n_tp):
        total = total + pieces[d][...].astype(F32)
    for r in range(prompts):
        out_ref[r] = res_ref[r].astype(F32) + total[r * new_count : (r + 1) * new_count]


def final_sum(pieces, residual):
    n_tp = len(pieces)
    return pl.pallas_call(
        functools.partial(final_kernel, n_tp),
        in_specs=[VMEM] * (n_tp + 1),
        out_specs=VMEM,
        out_shape=jax.ShapeDtypeStruct(residual.shape, F32),
        compiler_params=pltpu.CompilerParams(vmem_limit_bytes=8 * MIB),
        name="final",
    )(*pieces, residual)


def on_device(
    prefill_states, kv_weight, page_counts, tail_tokens, new_query, new_keyval, residual, out_weight
):
    n_seq, n_tp = lax.axis_size("seq"), lax.axis_size("tp")
    own_rows, new_count, _ = new_query.shape
    prompts = page_counts.shape[0]
    pages = prefill_states.shape[0] // PAGE * n_seq
    new = jnp.concatenate(
        [
            new_query.reshape(own_rows, new_count, QH // n_tp, HD),
            new_keyval.reshape(own_rows, new_count, 2 * KVH // n_tp, HD),
        ],
        axis=2,
    )
    half = KVH // 2
    new = gather(new, "tp")
    scalars = (page_counts, tail_tokens)
    ka, meta = project_keys(prefill_states, kv_weight, 0, half, pages, prompts, scalars)
    new = stacked(new, meta)
    kb = project_keys(prefill_states, kv_weight, half, half, pages, prompts, (meta,), new)
    new = gather(new, "seq")
    *scores, fresh = partial_scores(new, ka, kb, meta, pages, prompts, n_tp)
    va = project_values(prefill_states, kv_weight, 0, half, fresh)
    weights, stats = softmax_weights(exchange(scores, "tp"), meta, pages, prompts)
    vb = project_values(prefill_states, kv_weight, half, half, stats)
    chunks = weighted_values(gather(weights, "tp"), va, vb, meta, prompts)
    pieces = gather(summed(exchange(chunks, "tp"), stats), "seq")
    partial = output_partial(pieces, fresh, new, out_weight)
    return final_sum(gather(partial, "tp"), residual)


def solution(mesh):
    placed = (
        P(("groups", "seq"), "tp"),
        P("tp", None),
        P("groups"),
        P("groups"),
        P(("groups", "seq"), None, "tp"),
        P(("groups", "seq"), None, "tp"),
        P("groups", None, "seq"),
        P("tp", "seq"),
    )
    return jax.shard_map(
        on_device, mesh=mesh, in_specs=placed, out_specs=P("groups", None, "seq"), check_vma=False
    )
```

time: 102 us -> 85.1 us (0.83)
  blocking collectives: 46.6 us -> 0 us
  starting transfers between devices: 10.8 us -> 27.3 us
  waiting for transfers between devices: 0.01 us -> 14.2 us
  local copies, waits for them, and re-layouts: 16.8 us -> 10 us
  Pallas kernels: 26.2 us -> 32.8 us
    all_to_all x4 -> x0, blocking collectives: 46.6 us -> none  [exchange(): return lax.all_to_all(chunks, axis, 0, 0)]
    ppermute x0 -> x21, starting transfers between devices: none -> 27.3 us  [pairs(): lax.ppermute(value, axis, [(i, i ^ d) for i in range(lax.axis_size(axis))])]
    ppermute x0 -> x21, waiting for transfers between devices: none -> 14.2 us  [pairs(): lax.ppermute(value, axis, [(i, i ^ d) for i in range(lax.axis_size(axis))])]
    all_to_all x2 -> x0, starting transfers between devices: 10.8 us -> none  [exchange(): return lax.all_to_all(chunks, axis, 0, 0)]
    pallas_call x7 -> x10, Pallas kernels: 22.6 us -> 30.9 us  [the longest x2 13.7 us: project_keys(): pl.pallas_call(functools.partial(keys_kernel, pages, prompts, heads, tabl...]
    unnamed x16 -> x31, local copies, waits for them, and re-layouts: 15.8 us -> 8.6 us
    pallas_call x1, Pallas kernels: 3.6 us -> 1.91 us  [partial_scores(): pl.pallas_call(functools.partial(scores_kernel, pages, n_seq, n_tp), in_s...]
    reshape x0 -> x2, local copies, waits for them, and re-layouts: none -> 1.43 us  [the longest x1 0.73 us: on_device(): new_query.reshape(own_rows, new_count, QH // n_tp, HD)]
  transfers between devices with their start and end apart: 2 -> 21, of which waited for: 0 -> 7; matrix products, arithmetic and copies ran while one was open for 0% -> 0% of each run, Pallas kernels for 15% -> 31%
where the time goes in v3:
time: 85.1 us; the launch traced here: 84.5 us
  Pallas kernels  32.8 us (39%)
  starting transfers between devices  27.3 us (32%)
  waiting for transfers between devices  14.2 us (17%)
  local copies, waits for them, and re-layouts  10 us (12%)
    ppermute x21, starting transfers between devices, pairs(): lax.ppermute(value, axis, [(i, i ^ d) for i in range(lax.axis_size(axis))])  27.3 us
    ppermute x21, waiting for transfers between devices, pairs(): lax.ppermute(value, axis, [(i, i ^ d) for i in range(lax.axis_size(axis))])  14.2 us
    pallas_call x2, Pallas kernels, project_keys(): pl.pallas_call(functools.partial(keys_kernel, pages, prompts, heads, tabl...  13.7 us
    pallas_call x2, Pallas kernels, project_values(): pl.pallas_call(functools.partial(values_kernel, heads), in_specs=specs +...  12.4 us
    unnamed x31, local copies, waits for them, and re-layouts  8.6 us
    pallas_call x1, Pallas kernels, partial_scores(): pl.pallas_call(functools.partial(scores_kernel, pages, n_seq, n_tp), in_s...  1.91 us
    pallas_call x1, Pallas kernels, output_partial(): pl.pallas_call(functools.partial(output_kernel, n_seq), in_specs=[VMEM] *...  1.83 us
  transfers between devices with their start and end apart: 21, of which 7 were waited for; matrix products, arithmetic and copies ran while one was open for 0% of the time, Pallas kernels for 31%

profile of v3, /device:TPU:0, one launch (start us, length us, event | category | flops | bytes accessed | tf_op | source)
XLA Modules:
  0.0 84.5 jit_solution(6953357984161893916)
XLA Ops:
  0.0 0.7 reshape.7
  0.7 0.7 reshape.6
  1.5 5.1 %collective-permute-start.2 = (bf16[2,2,20,128]{3,2,1,0:T(8,128)(2,1)S(1)}, bf16[2,2,20,128]{3,2,1,0:T(8,128)(2,1)S(1)}, u32[]{:S(2)}, u32[]{:S(2)}) collective-permute-start(bf16[2,2,20,128]{3,2,1,0:T(8,128)(2,1)S(1)} %constant_dynamic-update-slice_fusion.refs_0_), channel_id=1, source_target_pairs={{0,3},{1,2},{2,1},{3,0},{4,7},{5,6},{6,5},{7,4},{8,11},{9,10},{10,... | collective-permute-start | bytes 61448 | tf_op jit(solution)/shard_map/ppermute | solution.py:26
  7.2 7.1 %keys.2 = (bf16[1024,512]{1,0:T(8,128)(2,1)}, s32[104]{0:T(128)}) custom-call(bf16[1024,2048]{1,0:T(8,128)(2,1)} %refs_0_.7, bf16[2048,2048]{1,0:T(8,128)(2,1)} %refs_4_.8, bf16[2048,2048]{1,0:T(8,128)(2,1)} %refs_4_.8, bf16[2048,2048]{1,0:T(8,128)(2,1)} %refs_4_.8, bf16[2048,2048]{1,0:T(8,128)(2,1)} %refs_4_.8, s32[8]{0:T(128)} %refs_5_.1, s32[8]{0:T(128)} %refs_6_.1), custom_call_target="tpu_custom_call" | custom-call | flops 2147483648 | bytes 7340032 | tf_op jit(solution)/shard_map/keys/pallas_call | solution.py:183
  15.5 1.3 %collective-permute-start.4 = (bf16[4,2,2,20,128]{4,3,2,1,0:T(8,128)(2,1)S(1)}, bf16[4,2,2,20,128]{4,3,2,1,0:T(8,128)(2,1)S(1)}, u32[]{:S(2)}, u32[]{:S(2)}) collective-permute-start(bf16[4,2,2,20,128]{4,3,2,1,0:T(8,128)(2,1)S(1)} %stacked.1.refs_6_.refs_0_.refs_5_), channel_id=1, source_target_pairs={{0,8},{4,12},{8,0},{12,4},{1,9},{5,13},{9,1},{13,5},{2,10},{6,14},... | collective-permute-start | bytes 245768 | tf_op jit(solution)/shard_map/ppermute | solution.py:26
  17.0 6.7 %keys.3.refs_5_ = bf16[1024,512]{1,0:T(8,128)(2,1)} custom-call(bf16[1024,2048]{1,0:T(8,128)(2,1)} %refs_0_.7, bf16[2048,2048]{1,0:T(8,128)(2,1)} %refs_4_.8, bf16[2048,2048]{1,0:T(8,128)(2,1)} %refs_4_.8, bf16[2048,2048]{1,0:T(8,128)(2,1)} %refs_4_.8, bf16[2048,2048]{1,0:T(8,128)(2,1)} %refs_4_.8, s32[104]{0:T(128)} %get-tuple-element.18.refs_4_.refs_5_.refs_6_, ...), custom_call_target="tpu_custom_call" | custom-call | flops 2147483648 | bytes 7340032 | tf_op jit(solution)/shard_map/keys/pallas_call | solution.py:183
  23.7 1.2 %copy-done.2 = bf16[1024,512]{1,0:T(8,128)(2,1)S(1)} copy-done((bf16[1024,512]{1,0:T(8,128)(2,1)S(1)}, bf16[1024,512]{1,0:T(8,128)(2,1)}, u32[]{:S(2)}) %copy-start.2) | copy-done | bytes 1048600
  24.9 0.9 %copy-done.5 = bf16[4,2,2,20,128]{4,3,2,1,0:T(8,128)(2,1)S(1)} copy-done((bf16[4,2,2,20,128]{4,3,2,1,0:T(8,128)(2,1)S(1)}, bf16[4,2,2,20,128]{4,3,2,1,0:T(8,128)(2,1)}, u32[]{:S(2)}) %copy-start.5) | copy-done | bytes 81944
  25.8 1.9 %scores.1 = (bf16[32,1024]{1,0:T(8,128)(2,1)S(1)}, bf16[32,1024]{1,0:T(8,128)(2,1)S(1)}, bf16[32,1024]{1,0:T(8,128)(2,1)S(1)}, bf16[32,1024]{1,0:T(8,128)(2,1)S(1)}, f32[2,32,128]{2,1,0:T(8,128)S(1)}) custom-call(bf16[4,2,2,20,128]{4,3,2,1,0:T(8,128)(2,1)S(1)} %copy-done.5, bf16[4,2,2,20,128]{4,3,2,1,0:T(8,128)(2,1)S(1)} %collective-permute-done.3.refs_1_.refs_6_, ...), custom_call_target="tpu_custom_call" | custom-call | flops 33554432 | bytes 6291456 | tf_op jit(solution)/shard_map/scores/pallas_call | solution.py:306
  28.3 1.4 %collective-permute-start.6 = (bf16[32,1024]{1,0:T(8,128)(2,1)S(1)}, bf16[32,1024]{1,0:T(8,128)(2,1)S(1)}, u32[]{:S(2)}, u32[]{:S(2)}) collective-permute-start(bf16[32,1024]{1,0:T(8,128)(2,1)S(1)} %get-tuple-element.21), channel_id=1, source_target_pairs={{0,1},{1,0},{2,3},{3,2},{4,5},{5,4},{6,7},{7,6},{8,9},{9,8},{10,11... | collective-permute-start | bytes 196616 | tf_op jit(solution)/shard_map/ppermute | solution.py:26
  29.7 2.9 %collective-permute-start.7 = (bf16[32,1024]{1,0:T(8,128)(2,1)S(1)}, bf16[32,1024]{1,0:T(8,128)(2,1)S(1)}, u32[]{:S(2)}, u32[]{:S(2)}) collective-permute-start(bf16[32,1024]{1,0:T(8,128)(2,1)S(1)} %get-tuple-element.22), channel_id=1, source_target_pairs={{0,2},{1,3},{2,0},{3,1},{4,6},{5,7},{6,4},{7,5},{8,10},{9,11},{10,... | collective-permute-start | bytes 196616 | tf_op jit(solution)/shard_map/ppermute | solution.py:26
  32.7 6.2 %values.2.refs_4_ = bf16[1024,512]{1,0:T(8,128)(2,1)} custom-call(bf16[1024,2048]{1,0:T(8,128)(2,1)} %refs_0_.7, bf16[2048,2048]{1,0:T(8,128)(2,1)} %refs_4_.8, bf16[2048,2048]{1,0:T(8,128)(2,1)} %refs_4_.8, bf16[2048,2048]{1,0:T(8,128)(2,1)} %refs_4_.8, bf16[2048,2048]{1,0:T(8,128)(2,1)} %refs_4_.8, f32[2,32,128]{2,1,0:T(8,128)} %copy-done.8), custom_call_target="tpu_custom_call" | custom-call | flops 2147483648 | bytes 7340032 | tf_op jit(solution)/shard_map/values/pallas_call | solution.py:201
  38.9 0.9 %weights.1 = (bf16[32,1024]{1,0:T(8,128)(2,1)S(1)}, bf16[32,128]{1,0:T(8,128)(2,1)S(1)}) custom-call(bf16[32,1024]{1,0:T(8,128)(2,1)S(1)} %get-tuple-element.20.refs_0_, bf16[32,1024]{1,0:T(8,128)(2,1)S(1)} %collective-permute-done.6.refs_1_, bf16[32,1024]{1,0:T(8,128)(2,1)S(1)} %collective-permute-done.7.refs_2_, ...), custom_call_target="tpu_custom_call" | custom-call | tf_op jit(solution)/shard_map/weights/pallas_call | solution.py:372
  40.4 3.7 %collective-permute-start.11 = (bf16[32,1024]{1,0:T(8,128)(2,1)S(1)}, bf16[32,1024]{1,0:T(8,128)(2,1)S(1)}, u32[]{:S(2)}, u32[]{:S(2)}) collective-permute-start(bf16[32,1024]{1,0:T(8,128)(2,1)S(1)} %get-tuple-element.24.refs_0_), channel_id=1, source_target_pairs={{0,3},{1,2},{2,1},{3,0},{4,7},{5,6},{6,5},{7,4},{8,11},{9,10},{10,... | collective-permute-start | bytes 196616 | tf_op jit(solution)/shard_map/ppermute | solution.py:26
  44.1 0.7 collective-permute-start.9
  44.8 6.3 %values.3.refs_5_ = bf16[1024,512]{1,0:T(8,128)(2,1)} custom-call(bf16[1024,2048]{1,0:T(8,128)(2,1)} %refs_0_.7, bf16[2048,2048]{1,0:T(8,128)(2,1)} %refs_4_.8, bf16[2048,2048]{1,0:T(8,128)(2,1)} %refs_4_.8, bf16[2048,2048]{1,0:T(8,128)(2,1)} %refs_4_.8, bf16[2048,2048]{1,0:T(8,128)(2,1)} %refs_4_.8, bf16[32,128]{1,0:T(8,128)(2,1)} %copy-done.11), custom_call_target="tpu_custom_call" | custom-call | flops 2147483648 | bytes 7340032 | tf_op jit(solution)/shard_map/values/pallas_call | solution.py:201
  51.2 1.2 %copy-done.3 = bf16[1024,512]{1,0:T(8,128)(2,1)S(1)} copy-done((bf16[1024,512]{1,0:T(8,128)(2,1)S(1)}, bf16[1024,512]{1,0:T(8,128)(2,1)}, u32[]{:S(2)}) %copy-start.3) | copy-done | bytes 1048600
  52.4 1.3 %weighted.1 = (bf16[8,32,128]{2,1,0:T(8,128)(2,1)S(1)}, bf16[8,32,128]{2,1,0:T(8,128)(2,1)S(1)}, bf16[8,32,128]{2,1,0:T(8,128)(2,1)S(1)}, bf16[8,32,128]{2,1,0:T(8,128)(2,1)S(1)}) custom-call(bf16[32,1024]{1,0:T(8,128)(2,1)S(1)} %get-tuple-element.24.refs_0_, bf16[32,1024]{1,0:T(8,128)(2,1)S(1)} %collective-permute-done.9.refs_1_, ...), custom_call_target="tpu_custom_call" | custom-call | flops 33554432 | bytes 8388608 | tf_op jit(solution)/shard_map/weighted/pallas_call | solution.py:416
  53.6 1.4 %collective-permute-start.12 = (bf16[8,32,128]{2,1,0:T(8,128)(2,1)S(1)}, bf16[8,32,128]{2,1,0:T(8,128)(2,1)S(1)}, u32[]{:S(2)}, u32[]{:S(2)}) collective-permute-start(bf16[8,32,128]{2,1,0:T(8,128)(2,1)S(1)} %get-tuple-element.28), channel_id=1, source_target_pairs={{0,1},{1,0},{2,3},{3,2},{4,5},{5,4},{6,7},{7,6},{8,9},{9,8},{10,11... | collective-permute-start | bytes 196616 | tf_op jit(solution)/shard_map/ppermute | solution.py:26
  55.1 2.9 %collective-permute-start.13 = (bf16[8,32,128]{2,1,0:T(8,128)(2,1)S(1)}, bf16[8,32,128]{2,1,0:T(8,128)(2,1)S(1)}, u32[]{:S(2)}, u32[]{:S(2)}) collective-permute-start(bf16[8,32,128]{2,1,0:T(8,128)(2,1)S(1)} %get-tuple-element.29), channel_id=1, source_target_pairs={{0,2},{1,3},{2,0},{3,1},{4,6},{5,7},{6,4},{7,5},{8,10},{9,11},{10,... | collective-permute-start | bytes 196616 | tf_op jit(solution)/shard_map/ppermute | solution.py:26
  58.3 3.3 %collective-permute-done.13.refs_2_ = bf16[8,32,128]{2,1,0:T(8,128)(2,1)S(1)} collective-permute-done((bf16[8,32,128]{2,1,0:T(8,128)(2,1)S(1)}, bf16[8,32,128]{2,1,0:T(8,128)(2,1)S(1)}, u32[]{:S(2)}, u32[]{:S(2)}) %collective-permute-start.13) | collective-permute-done | bytes 65568 | tf_op jit(solution)/shard_map/ppermute | solution.py:26
  61.6 2.4 %collective-permute-done.14.refs_3_ = bf16[8,32,128]{2,1,0:T(8,128)(2,1)S(1)} collective-permute-done((bf16[8,32,128]{2,1,0:T(8,128)(2,1)S(1)}, bf16[8,32,128]{2,1,0:T(8,128)(2,1)S(1)}, u32[]{:S(2)}, u32[]{:S(2)}) %collective-permute-start.14) | collective-permute-done | bytes 65568 | tf_op jit(solution)/shard_map/ppermute | solution.py:26
  64.2 1.6 %collective-permute-start.16 = (bf16[9,32,128]{2,1,0:T(8,128)(2,1)S(1)}, bf16[9,32,128]{2,1,0:T(8,128)(2,1)S(1)}, u32[]{:S(2)}, u32[]{:S(2)}) collective-permute-start(bf16[9,32,128]{2,1,0:T(8,128)(2,1)S(1)} %summed.1.refs_0_), channel_id=1, source_target_pairs={{0,8},{4,12},{8,0},{12,4},{1,9},{5,13},{9,1},{13,5},{2,10},{6,14},... | collective-permute-start | bytes 221192 | tf_op jit(solution)/shard_map/ppermute | solution.py:26
  66.0 2.6 %collective-permute-done.17.refs_3_ = bf16[9,32,128]{2,1,0:T(8,128)(2,1)S(1)} collective-permute-done((bf16[9,32,128]{2,1,0:T(8,128)(2,1)S(1)}, bf16[9,32,128]{2,1,0:T(8,128)(2,1)S(1)}, u32[]{:S(2)}, u32[]{:S(2)}) %collective-permute-start.17) | collective-permute-done | bytes 73760 | tf_op jit(solution)/shard_map/ppermute | solution.py:26
  68.6 1.7 %collective-permute-done.16.refs_2_ = bf16[9,32,128]{2,1,0:T(8,128)(2,1)S(1)} collective-permute-done((bf16[9,32,128]{2,1,0:T(8,128)(2,1)S(1)}, bf16[9,32,128]{2,1,0:T(8,128)(2,1)S(1)}, u32[]{:S(2)}, u32[]{:S(2)}) %collective-permute-start.16) | collective-permute-done | bytes 73760 | tf_op jit(solution)/shard_map/ppermute | solution.py:26
  70.3 3.4 %copy-done = bf16[2048,2048]{1,0:T(8,128)(2,1)S(1)} copy-done((bf16[2048,2048]{1,0:T(8,128)(2,1)S(1)}, bf16[2048,2048]{1,0:T(8,128)(2,1)}, u32[]{:S(2)}) %copy-start) | copy-done | bytes 8388632
  73.7 1.8 %output.1.refs_0_ = bf16[16,2048]{1,0:T(8,128)(2,1)S(1)} custom-call(bf16[9,32,128]{2,1,0:T(8,128)(2,1)S(1)} %summed.1.refs_0_, bf16[9,32,128]{2,1,0:T(8,128)(2,1)S(1)} %collective-permute-done.15.refs_1_, bf16[9,32,128]{2,1,0:T(8,128)(2,1)S(1)} %collective-permute-done.16.refs_2_, bf16[9,32,128]{2,1,0:T(8,128)(2,1)S(1)} %collective-permute-done.17.refs_3_, ...), custom_call_target="tpu_custom_call" | custom-call | tf_op jit(solution)/shard_map/output/pallas_call | solution.py:526
  75.5 0.8 collective-permute-start.20
  76.3 3.6 %collective-permute-start.18 = (bf16[16,2048]{1,0:T(8,128)(2,1)S(1)}, bf16[16,2048]{1,0:T(8,128)(2,1)S(1)}, u32[]{:S(2)}, u32[]{:S(2)}) collective-permute-start(bf16[16,2048]{1,0:T(8,128)(2,1)S(1)} %output.1.refs_0_), channel_id=1, source_target_pairs={{0,1},{1,0},{2,3},{3,2},{4,5},{5,4},{6,7},{7,6},{8,9},{9,8},{10,11... | collective-permute-start | bytes 196616 | tf_op jit(solution)/shard_map/ppermute | solution.py:26
  79.9 2.4 %collective-permute-done.20.refs_3_ = bf16[16,2048]{1,0:T(8,128)(2,1)S(1)} collective-permute-done((bf16[16,2048]{1,0:T(8,128)(2,1)S(1)}, bf16[16,2048]{1,0:T(8,128)(2,1)S(1)}, u32[]{:S(2)}, u32[]{:S(2)}) %collective-permute-start.20) | collective-permute-done | bytes 65568 | tf_op jit(solution)/shard_map/ppermute | solution.py:26
  82.4 1.4 %collective-permute-done.19.refs_2_ = bf16[16,2048]{1,0:T(8,128)(2,1)S(1)} collective-permute-done((bf16[16,2048]{1,0:T(8,128)(2,1)S(1)}, bf16[16,2048]{1,0:T(8,128)(2,1)S(1)}, u32[]{:S(2)}, u32[]{:S(2)}) %collective-permute-start.19) | collective-permute-done | bytes 65568 | tf_op jit(solution)/shard_map/ppermute | solution.py:26
  83.8 0.7 final.1
  (55 shorter events, 4.1 us)
Async XLA Ops:
  1.5 12.8 %collective-permute-start.2 = (bf16[2,2,20,128]{3,2,1,0:T(8,128)(2,1)S(1)}, bf16[2,2,20,128]{3,2,1,0:T(8,128)(2,1)S(1)}, u32[]{:S(2)}, u32[]{:S(2)}) collective-permute-start(bf16[2,2,20,128]{3,2,1,0:T(8,128)(2,1)S(1)} %constant_dynamic-update-slice_fusion.refs_0_), channel_id=1, source_target_pairs={{0,3},{1,2},{2,1},{3,0},{4,7},{5,6},{6,5},{7,4},{8,11},{9,10},{10,... | collective-permute-start | bytes 61448 | tf_op jit(solution)/shard_map/ppermute | solution.py:26
  6.6 7.7 %collective-permute-start.1 = (bf16[2,2,20,128]{3,2,1,0:T(8,128)(2,1)S(1)}, bf16[2,2,20,128]{3,2,1,0:T(8,128)(2,1)S(1)}, u32[]{:S(2)}, u32[]{:S(2)}) collective-permute-start(bf16[2,2,20,128]{3,2,1,0:T(8,128)(2,1)S(1)} %constant_dynamic-update-slice_fusion.refs_0_), channel_id=1, source_target_pairs={{0,2},{1,3},{2,0},{3,1},{4,6},{5,7},{6,4},{7,5},{8,10},{9,11},{10,... | collective-permute-start | bytes 61448 | tf_op jit(solution)/shard_map/ppermute | solution.py:26
  6.6 7.7 %collective-permute-start = (bf16[2,2,20,128]{3,2,1,0:T(8,128)(2,1)S(1)}, bf16[2,2,20,128]{3,2,1,0:T(8,128)(2,1)S(1)}, u32[]{:S(2)}, u32[]{:S(2)}) collective-permute-start(bf16[2,2,20,128]{3,2,1,0:T(8,128)(2,1)S(1)} %constant_dynamic-update-slice_fusion.refs_0_), channel_id=1, source_target_pairs={{0,1},{1,0},{2,3},{3,2},{4,5},{5,4},{6,7},{7,6},{8,9},{9,8},{10,11... | collective-permute-start | bytes 61448 | tf_op jit(solution)/shard_map/ppermute | solution.py:26
  15.0 2.0 %copy-start.4 = (bf16[4,2,2,20,128]{4,3,2,1,0:T(8,128)(2,1)}, bf16[4,2,2,20,128]{4,3,2,1,0:T(8,128)(2,1)S(1)}, u32[]{:S(2)}) copy-start(bf16[4,2,2,20,128]{4,3,2,1,0:T(8,128)(2,1)S(1)} %stacked.1.refs_6_.refs_0_.refs_5_) | copy-start | bytes 245764
  15.0 8.7 %copy-start.7 = (bf16[1024,512]{1,0:T(8,128)(2,1)S(1)}, bf16[1024,512]{1,0:T(8,128)(2,1)}, u32[]{:S(2)}) copy-start(bf16[1024,512]{1,0:T(8,128)(2,1)} %get-tuple-element.19.refs_4_) | copy-start | bytes 3145732
  15.0 8.7 %copy-start.14 = (s32[104]{0:T(128)S(1)}, s32[104]{0:T(128)}, u32[]{:S(2)}) copy-start(s32[104]{0:T(128)} %get-tuple-element.18.refs_4_.refs_5_.refs_6_) | copy-start | bytes 1252
  15.0 8.6 %collective-permute-start.5 = (bf16[4,2,2,20,128]{4,3,2,1,0:T(8,128)(2,1)S(1)}, bf16[4,2,2,20,128]{4,3,2,1,0:T(8,128)(2,1)S(1)}, u32[]{:S(2)}, u32[]{:S(2)}) collective-permute-start(bf16[4,2,2,20,128]{4,3,2,1,0:T(8,128)(2,1)S(1)} %stacked.1.refs_6_.refs_0_.refs_5_), channel_id=1, source_target_pairs={{0,12},{4,8},{8,4},{12,0},{1,13},{5,9},{9,5},{13,1},{2,14},{6,10},... | collective-permute-start | bytes 245768 | tf_op jit(solution)/shard_map/ppermute | solution.py:26
  15.5 8.2 %collective-permute-start.4 = (bf16[4,2,2,20,128]{4,3,2,1,0:T(8,128)(2,1)S(1)}, bf16[4,2,2,20,128]{4,3,2,1,0:T(8,128)(2,1)S(1)}, u32[]{:S(2)}, u32[]{:S(2)}) collective-permute-start(bf16[4,2,2,20,128]{4,3,2,1,0:T(8,128)(2,1)S(1)} %stacked.1.refs_6_.refs_0_.refs_5_), channel_id=1, source_target_pairs={{0,8},{4,12},{8,0},{12,4},{1,9},{5,13},{9,1},{13,5},{2,10},{6,14},... | collective-permute-start | bytes 245768 | tf_op jit(solution)/shard_map/ppermute | solution.py:26
  16.8 6.8 %collective-permute-start.3 = (bf16[4,2,2,20,128]{4,3,2,1,0:T(8,128)(2,1)S(1)}, bf16[4,2,2,20,128]{4,3,2,1,0:T(8,128)(2,1)S(1)}, u32[]{:S(2)}, u32[]{:S(2)}) collective-permute-start(bf16[4,2,2,20,128]{4,3,2,1,0:T(8,128)(2,1)S(1)} %stacked.1.refs_6_.refs_0_.refs_5_), channel_id=1, source_target_pairs={{0,4},{4,0},{8,12},{12,8},{1,5},{5,1},{9,13},{13,9},{2,6},{6,2},{1... | collective-permute-start | bytes 245768 | tf_op jit(solution)/shard_map/ppermute | solution.py:26
  23.7 1.2 %copy-start.2 = (bf16[1024,512]{1,0:T(8,128)(2,1)S(1)}, bf16[1024,512]{1,0:T(8,128)(2,1)}, u32[]{:S(2)}) copy-start(bf16[1024,512]{1,0:T(8,128)(2,1)} %keys.3.refs_5_) | copy-start | bytes 3145732
  28.3 10.6 %collective-permute-start.6 = (bf16[32,1024]{1,0:T(8,128)(2,1)S(1)}, bf16[32,1024]{1,0:T(8,128)(2,1)S(1)}, u32[]{:S(2)}, u32[]{:S(2)}) collective-permute-start(bf16[32,1024]{1,0:T(8,128)(2,1)S(1)} %get-tuple-element.21), channel_id=1, source_target_pairs={{0,1},{1,0},{2,3},{3,2},{4,5},{5,4},{6,7},{7,6},{8,9},{9,8},{10,11... | collective-permute-start | bytes 196616 | tf_op jit(solution)/shard_map/ppermute | solution.py:26
  29.7 9.2 %collective-permute-start.7 = (bf16[32,1024]{1,0:T(8,128)(2,1)S(1)}, bf16[32,1024]{1,0:T(8,128)(2,1)S(1)}, u32[]{:S(2)}, u32[]{:S(2)}) collective-permute-start(bf16[32,1024]{1,0:T(8,128)(2,1)S(1)} %get-tuple-element.22), channel_id=1, source_target_pairs={{0,2},{1,3},{2,0},{3,1},{4,6},{5,7},{6,4},{7,5},{8,10},{9,11},{10,... | collective-permute-start | bytes 196616 | tf_op jit(solution)/shard_map/ppermute | solution.py:26
  32.6 6.3 %collective-permute-start.8 = (bf16[32,1024]{1,0:T(8,128)(2,1)S(1)}, bf16[32,1024]{1,0:T(8,128)(2,1)S(1)}, u32[]{:S(2)}, u32[]{:S(2)}) collective-permute-start(bf16[32,1024]{1,0:T(8,128)(2,1)S(1)} %get-tuple-element.23), channel_id=1, source_target_pairs={{0,3},{1,2},{2,1},{3,0},{4,7},{5,6},{6,5},{7,4},{8,11},{9,10},{10,... | collective-permute-start | bytes 196616 | tf_op jit(solution)/shard_map/ppermute | solution.py:26
  40.4 10.7 %collective-permute-start.11 = (bf16[32,1024]{1,0:T(8,128)(2,1)S(1)}, bf16[32,1024]{1,0:T(8,128)(2,1)S(1)}, u32[]{:S(2)}, u32[]{:S(2)}) collective-permute-start(bf16[32,1024]{1,0:T(8,128)(2,1)S(1)} %get-tuple-element.24.refs_0_), channel_id=1, source_target_pairs={{0,3},{1,2},{2,1},{3,0},{4,7},{5,6},{6,5},{7,4},{8,11},{9,10},{10,... | collective-permute-start | bytes 196616 | tf_op jit(solution)/shard_map/ppermute | solution.py:26
  44.1 7.0 %collective-permute-start.10 = (bf16[32,1024]{1,0:T(8,128)(2,1)S(1)}, bf16[32,1024]{1,0:T(8,128)(2,1)S(1)}, u32[]{:S(2)}, u32[]{:S(2)}) collective-permute-start(bf16[32,1024]{1,0:T(8,128)(2,1)S(1)} %get-tuple-element.24.refs_0_), channel_id=1, source_target_pairs={{0,2},{1,3},{2,0},{3,1},{4,6},{5,7},{6,4},{7,5},{8,10},{9,11},{10,... | collective-permute-start | bytes 196616 | tf_op jit(solution)/shard_map/ppermute | solution.py:26
  44.1 7.0 %collective-permute-start.9 = (bf16[32,1024]{1,0:T(8,128)(2,1)S(1)}, bf16[32,1024]{1,0:T(8,128)(2,1)S(1)}, u32[]{:S(2)}, u32[]{:S(2)}) collective-permute-start(bf16[32,1024]{1,0:T(8,128)(2,1)S(1)} %get-tuple-element.24.refs_0_), channel_id=1, source_target_pairs={{0,1},{1,0},{2,3},{3,2},{4,5},{5,4},{6,7},{7,6},{8,9},{9,8},{10,11... | collective-permute-start | bytes 196616 | tf_op jit(solution)/shard_map/ppermute | solution.py:26
  44.8 6.3 %copy-start.1 = (bf16[1024,512]{1,0:T(8,128)(2,1)S(1)}, bf16[1024,512]{1,0:T(8,128)(2,1)}, u32[]{:S(2)}) copy-start(bf16[1024,512]{1,0:T(8,128)(2,1)} %values.2.refs_4_) | copy-start | bytes 3145732
  44.8 19.2 %copy-start.12 = (bf16[32,128]{1,0:T(8,128)(2,1)S(1)}, bf16[32,128]{1,0:T(8,128)(2,1)}, u32[]{:S(2)}) copy-start(bf16[32,128]{1,0:T(8,128)(2,1)} %copy-done.11) | copy-start | bytes 24580
  44.8 25.5 %copy-start.6 = (bf16[4,2,2,20,128]{4,3,2,1,0:T(8,128)(2,1)S(1)}, bf16[4,2,2,20,128]{4,3,2,1,0:T(8,128)(2,1)}, u32[]{:S(2)}) copy-start(bf16[4,2,2,20,128]{4,3,2,1,0:T(8,128)(2,1)} %copy-done.4) | copy-start | bytes 245764
  44.8 25.5 %copy-start.9 = (f32[2,32,128]{2,1,0:T(8,128)S(1)}, f32[2,32,128]{2,1,0:T(8,128)}, u32[]{:S(2)}) copy-start(f32[2,32,128]{2,1,0:T(8,128)} %copy-done.8) | copy-start | bytes 98308
  44.8 39.0 %copy-start.10 = (bf16[8,2,2048]{2,1,0:T(2,128)(2,1)S(1)}, bf16[8,2,2048]{2,1,0:T(2,128)(2,1)}, u32[]{:S(2)}) copy-start(bf16[8,2,2048]{2,1,0:T(2,128)(2,1)} %refs_4_.9) | copy-start | bytes 196612
  51.1 1.2 %copy-start.3 = (bf16[1024,512]{1,0:T(8,128)(2,1)S(1)}, bf16[1024,512]{1,0:T(8,128)(2,1)}, u32[]{:S(2)}) copy-start(bf16[1024,512]{1,0:T(8,128)(2,1)} %values.3.refs_5_) | copy-start | bytes 3145732
  53.6 4.7 %collective-permute-start.12 = (bf16[8,32,128]{2,1,0:T(8,128)(2,1)S(1)}, bf16[8,32,128]{2,1,0:T(8,128)(2,1)S(1)}, u32[]{:S(2)}, u32[]{:S(2)}) collective-permute-start(bf16[8,32,128]{2,1,0:T(8,128)(2,1)S(1)} %get-tuple-element.28), channel_id=1, source_target_pairs={{0,1},{1,0},{2,3},{3,2},{4,5},{5,4},{6,7},{7,6},{8,9},{9,8},{10,11... | collective-permute-start | bytes 196616 | tf_op jit(solution)/shard_map/ppermute | solution.py:26
  55.1 6.6 %collective-permute-start.13 = (bf16[8,32,128]{2,1,0:T(8,128)(2,1)S(1)}, bf16[8,32,128]{2,1,0:T(8,128)(2,1)S(1)}, u32[]{:S(2)}, u32[]{:S(2)}) collective-permute-start(bf16[8,32,128]{2,1,0:T(8,128)(2,1)S(1)} %get-tuple-element.29), channel_id=1, source_target_pairs={{0,2},{1,3},{2,0},{3,1},{4,6},{5,7},{6,4},{7,5},{8,10},{9,11},{10,... | collective-permute-start | bytes 196616 | tf_op jit(solution)/shard_map/ppermute | solution.py:26
  58.0 6.1 %collective-permute-start.14 = (bf16[8,32,128]{2,1,0:T(8,128)(2,1)S(1)}, bf16[8,32,128]{2,1,0:T(8,128)(2,1)S(1)}, u32[]{:S(2)}, u32[]{:S(2)}) collective-permute-start(bf16[8,32,128]{2,1,0:T(8,128)(2,1)S(1)} %get-tuple-element.30), channel_id=1, source_target_pairs={{0,3},{1,2},{2,1},{3,0},{4,7},{5,6},{6,5},{7,4},{8,11},{9,10},{10,... | collective-permute-start | bytes 196616 | tf_op jit(solution)/shard_map/ppermute | solution.py:26
  64.1 4.6 %collective-permute-start.17 = (bf16[9,32,128]{2,1,0:T(8,128)(2,1)S(1)}, bf16[9,32,128]{2,1,0:T(8,128)(2,1)S(1)}, u32[]{:S(2)}, u32[]{:S(2)}) collective-permute-start(bf16[9,32,128]{2,1,0:T(8,128)(2,1)S(1)} %summed.1.refs_0_), channel_id=1, source_target_pairs={{0,12},{4,8},{8,4},{12,0},{1,13},{5,9},{9,5},{13,1},{2,14},{6,10},... | collective-permute-start | bytes 221192 | tf_op jit(solution)/shard_map/ppermute | solution.py:26
  64.2 6.1 %collective-permute-start.16 = (bf16[9,32,128]{2,1,0:T(8,128)(2,1)S(1)}, bf16[9,32,128]{2,1,0:T(8,128)(2,1)S(1)}, u32[]{:S(2)}, u32[]{:S(2)}) collective-permute-start(bf16[9,32,128]{2,1,0:T(8,128)(2,1)S(1)} %summed.1.refs_0_), channel_id=1, source_target_pairs={{0,8},{4,12},{8,0},{12,4},{1,9},{5,13},{9,1},{13,5},{2,10},{6,14},... | collective-permute-start | bytes 221192 | tf_op jit(solution)/shard_map/ppermute | solution.py:26
  65.8 4.6 %collective-permute-start.15 = (bf16[9,32,128]{2,1,0:T(8,128)(2,1)S(1)}, bf16[9,32,128]{2,1,0:T(8,128)(2,1)S(1)}, u32[]{:S(2)}, u32[]{:S(2)}) collective-permute-start(bf16[9,32,128]{2,1,0:T(8,128)(2,1)S(1)} %summed.1.refs_0_), channel_id=1, source_target_pairs={{0,4},{4,0},{8,12},{12,8},{1,5},{5,1},{9,13},{13,9},{2,6},{6,2},{1... | collective-permute-start | bytes 221192 | tf_op jit(solution)/shard_map/ppermute | solution.py:26
  70.3 3.4 %copy-start = (bf16[2048,2048]{1,0:T(8,128)(2,1)S(1)}, bf16[2048,2048]{1,0:T(8,128)(2,1)}, u32[]{:S(2)}) copy-start(bf16[2048,2048]{1,0:T(8,128)(2,1)} %refs_9_.1) | copy-start | bytes 25165828
  75.5 6.8 %collective-permute-start.20 = (bf16[16,2048]{1,0:T(8,128)(2,1)S(1)}, bf16[16,2048]{1,0:T(8,128)(2,1)S(1)}, u32[]{:S(2)}, u32[]{:S(2)}) collective-permute-start(bf16[16,2048]{1,0:T(8,128)(2,1)S(1)} %output.1.refs_0_), channel_id=1, source_target_pairs={{0,3},{1,2},{2,1},{3,0},{4,7},{5,6},{6,5},{7,4},{8,11},{9,10},{10,... | collective-permute-start | bytes 196616 | tf_op jit(solution)/shard_map/ppermute | solution.py:26
  76.3 7.5 %collective-permute-start.19 = (bf16[16,2048]{1,0:T(8,128)(2,1)S(1)}, bf16[16,2048]{1,0:T(8,128)(2,1)S(1)}, u32[]{:S(2)}, u32[]{:S(2)}) collective-permute-start(bf16[16,2048]{1,0:T(8,128)(2,1)S(1)} %output.1.refs_0_), channel_id=1, source_target_pairs={{0,2},{1,3},{2,0},{3,1},{4,6},{5,7},{6,4},{7,5},{8,10},{9,11},{10,... | collective-permute-start | bytes 196616 | tf_op jit(solution)/shard_map/ppermute | solution.py:26
  76.3 7.5 %collective-permute-start.18 = (bf16[16,2048]{1,0:T(8,128)(2,1)S(1)}, bf16[16,2048]{1,0:T(8,128)(2,1)S(1)}, u32[]{:S(2)}, u32[]{:S(2)}) collective-permute-start(bf16[16,2048]{1,0:T(8,128)(2,1)S(1)} %output.1.refs_0_), channel_id=1, source_target_pairs={{0,1},{1,0},{2,3},{3,2},{4,5},{5,4},{6,7},{7,6},{8,9},{9,8},{10,11... | collective-permute-start | bytes 196616 | tf_op jit(solution)/shard_map/ppermute | solution.py:26
  (4 other events, 2.8 us)

commit v4 on v3

--- a/solution.py
+++ b/solution.py
@@ -42,6 +42,10 @@
 def sine_sign(rows):
     lane = lax.broadcasted_iota(jnp.int32, (rows, HD), 1)
     return jnp.where(lane < HD // 2, -1.0, 1.0)
+
+
+def in_hbm(value):
+    return pltpu.with_memory_space_constraint(value, pltpu.HBM)
 
 
 def by_row(rows, numbers):
@@ -91,122 +95,148 @@
             sin_s[at] = sign * (sine * c + cosine * s)
 
 
-def accumulate(x_ref, weights, acc, finish):
-    step, last = pl.program_id(0), pl.num_programs(0) - 1
-    weight = jnp.concatenate([w[...] for w in weights], axis=1)
-    tall = 512
-
-    def product(start):
-        return jnp.dot(x_ref[start : start + tall], weight, preferred_element_type=F32)
-
-    starts = range(0, x_ref.shape[0], tall)
-
-    @pl.when(step == 0)
-    def _():
-        for start in starts:
-            acc[start : start + tall] = product(start)
-
-    @pl.when((step > 0) & (step < last))
-    def _():
-        for start in starts:
-            acc[start : start + tall] += product(start)
-
-    @pl.when(step == last)
-    def _():
-        for start in starts:
-            finish(slice(start, start + tall), acc[start : start + tall] + product(start))
-
-
-def keys_kernel(pages, prompts, heads, table, *refs):
-    x_ref, *weights = refs[: heads + 1]
-    if table:
-        counts, tails, out_ref, meta, cos_s, sin_s, acc = refs[heads + 1 :]
-    else:
-        meta, _, out_ref, cos_s, sin_s, acc = refs[heads + 1 :]
-
-    @pl.when(pl.program_id(0) == 0)
-    def _():
-        if table:
-            page_table(pages, prompts, counts, tails, meta)
-        rotation_tables(pages, x_ref.shape[0] // PAGE, meta, cos_s, sin_s)
-
-    def finish(at, product):
-        cosine, sine = cos_s[at], sin_s[at]
-        for h in range(heads):
-            k = product[:, h * HD : (h + 1) * HD]
-            k = k * cosine + pltpu.roll(k, HD // 2, 1) * sine
-            out_ref[at, h * HD : (h + 1) * HD] = k.astype(BF16)
-
-    accumulate(x_ref, weights, acc, finish)
-
-
-def values_kernel(heads, *refs):
-    x_ref, *weights = refs[: heads + 1]
-    _, out_ref, acc = refs[heads + 1 :]
-
-    def finish(at, product):
-        out_ref[at] = product.astype(BF16)
-
-    accumulate(x_ref, weights, acc, finish)
-
-
-BIG = 57 * MIB
-
-
-def projection_specs(x, heads, columns):
+def keys_kernel(pages, prompts, x_hbm, w_hbm, counts, tails, k_ref, x_ref, v_ref, meta, *scratch):
+    w_ref, cos_s, sin_s, x_sems, k_sems, v_sems = scratch
+    tokens = x_ref.shape[0]
+    tall = tokens // 2
+
+    def x_copy(i):
+        at = pl.ds(i * tall, tall)
+        return pltpu.make_async_copy(x_hbm.at[at], x_ref.at[at], x_sems.at[i])
+
+    def w_copy(head, part):
+        to, sems = (w_ref, k_sems) if part == 0 else (v_ref, v_sems)
+        return pltpu.make_async_copy(
+            w_hbm.at[:, pl.ds((2 * head + part) * HD, HD)],
+            to.at[:, pl.ds(head * HD, HD)],
+            sems.at[head],
+        )
+
+    x_copy(0).start()
+    w_copy(0, 0).start()
+    w_copy(1, 0).start()
+    x_copy(1).start()
+    for head in range(2, KVH):
+        w_copy(head, 0).start()
+    for head in range(KVH):
+        w_copy(head, 1).start()
+    page_table(pages, prompts, counts, tails, meta)
+    rotation_tables(pages, tokens // PAGE, meta, cos_s, sin_s)
+    for pair in range(KVH // 2):
+        w_copy(2 * pair, 0).wait()
+        w_copy(2 * pair + 1, 0).wait()
+        columns = slice(2 * pair * HD, 2 * (pair + 1) * HD)
+        for i in range(2):
+            if pair == 0:
+                x_copy(i).wait()
+            at = slice(i * tall, (i + 1) * tall)
+            product = jnp.dot(x_ref[at], w_ref[:, columns], preferred_element_type=F32)
+            cosine, sine = cos_s[at], sin_s[at]
+            for h in range(2):
+                k = product[:, h * HD : (h + 1) * HD]
+                k = k * cosine + pltpu.roll(k, HD // 2, 1) * sine
+                k_ref[at, (2 * pair + h) * HD : (2 * pair + h + 1) * HD] = k.astype(BF16)
+    for head in range(KVH):
+        w_copy(head, 1).wait()
+
+
+def project_keys(x, kv_weight, counts, tails, pages):
     tokens, depth = x.shape
-    block = min(depth // 2, 512)
-    at = lambda c: pl.BlockSpec((block, HD), lambda i: (i, c))
-    specs = [pl.BlockSpec((tokens, block), lambda i: (0, i))] + [at(c) for c in columns]
-    return dict(
-        grid=(depth // block,),
-        compiler_params=pltpu.CompilerParams(vmem_limit_bytes=BIG),
+    prompts = counts.shape[0]
+    hbm = pl.BlockSpec(memory_space=pltpu.HBM)
+    return pl.pallas_call(
+        functools.partial(keys_kernel, pages, prompts),
+        in_specs=[hbm, hbm, SMEM, SMEM],
+        out_specs=[VMEM, VMEM, VMEM, SMEM],
+        out_shape=[
+            pltpu.VMEM((tokens, KVH * HD), BF16),
+            pltpu.VMEM((tokens, depth), BF16),
+            pltpu.VMEM((depth, KVH * HD), BF16),
+            jax.ShapeDtypeStruct((3 * pages + prompts,), jnp.int32),
+        ],
+        scratch_shapes=[
+            pltpu.VMEM((depth, KVH * HD), BF16),
+            pltpu.VMEM((tokens, HD), F32),
+            pltpu.VMEM((tokens, HD), F32),
+            pltpu.SemaphoreType.DMA((2,)),
+            pltpu.SemaphoreType.DMA((KVH,)),
+            pltpu.SemaphoreType.DMA((KVH,)),
+        ],
+        compiler_params=pltpu.CompilerParams(vmem_limit_bytes=28 * MIB),
         cost_estimate=pl.CostEstimate(
-            flops=2 * tokens * depth * heads * HD,
-            bytes_accessed=2 * depth * (tokens + heads * HD) + 2 * tokens * heads * HD,
+            flops=2 * tokens * depth * KVH * HD,
+            bytes_accessed=2 * depth * (tokens + 2 * KVH * HD) + 2 * tokens * KVH * HD,
             transcendentals=0,
         ),
-    ), specs
-
-
-def project_keys(x, kv_weight, first, heads, pages, prompts, scalars, after=None):
-    tokens, _ = x.shape
-    table = after is None
-    call, specs = projection_specs(x, heads, [2 * (first + h) for h in range(heads)])
-    out_specs = [pl.BlockSpec((tokens, heads * HD), lambda i: (0, 0)), SMEM]
-    out_shape = [
-        jax.ShapeDtypeStruct((tokens, heads * HD), BF16),
-        jax.ShapeDtypeStruct((3 * pages + prompts,), jnp.int32),
-    ]
-    extra = [SMEM, SMEM] if table else [SMEM, pl.BlockSpec(memory_space=pl.ANY)]
-    operands = list(scalars) + ([] if table else [after])
-    return pl.pallas_call(
-        functools.partial(keys_kernel, pages, prompts, heads, table),
-        in_specs=specs + extra,
-        out_specs=out_specs if table else out_specs[0],
-        out_shape=out_shape if table else out_shape[0],
-        scratch_shapes=[
-            pltpu.VMEM((tokens, HD), F32),
-            pltpu.VMEM((tokens, HD), F32),
-            pltpu.VMEM((tokens, heads * HD), F32),
+        name="keys",
+    )(*[in_hbm(a) for a in (x, kv_weight, counts, tails)])
+
+
+def values_kernel(first, x_ref, w_ref, o_hbm, after, v_ref, o_ref, sem):
+    depth = o_ref.shape[0]
+    copy = pltpu.make_async_copy(o_hbm.at[pl.ds(first * depth, depth)], o_ref, sem)
+    copy.start()
+    tokens, columns = v_ref.shape
+    tall = tokens // 2
+    for c in range(0, columns, 2 * HD):
+        for i in range(2):
+            at = slice(i * tall, (i + 1) * tall)
+            weight = w_ref[:, first * columns + c : first * columns + c + 2 * HD]
+            v_ref[at, c : c + 2 * HD] = jnp.dot(
+                x_ref[at], weight, preferred_element_type=F32
+            ).astype(BF16)
+    copy.wait()
+
+
+def project_values(x, weight, out_weight, first, after):
+    tokens, depth = x.shape
+    columns = weight.shape[1] // 2
+    rows = out_weight.shape[0] // 2
+    return pl.pallas_call(
+        functools.partial(values_kernel, first),
+        in_specs=[
+            VMEM,
+            VMEM,
+            pl.BlockSpec(memory_space=pltpu.HBM),
+            pl.BlockSpec(memory_space=pl.ANY),
         ],
-        name="keys",
-        **call,
-    )(x, *[kv_weight] * heads, *operands)
-
-
-def project_values(x, kv_weight, first, heads, after):
-    tokens, _ = x.shape
-    call, specs = projection_specs(x, heads, [2 * (first + h) + 1 for h in range(heads)])
-    return pl.pallas_call(
-        functools.partial(values_kernel, heads),
-        in_specs=specs + [pl.BlockSpec(memory_space=pl.ANY)],
-        out_specs=pl.BlockSpec((tokens, heads * HD), lambda i: (0, 0)),
-        out_shape=jax.ShapeDtypeStruct((tokens, heads * HD), BF16),
-        scratch_shapes=[pltpu.VMEM((tokens, heads * HD), F32)],
+        out_specs=[VMEM, VMEM],
+        out_shape=[
+            pltpu.VMEM((tokens, columns), BF16),
+            pltpu.VMEM((rows, out_weight.shape[1]), BF16),
+        ],
+        scratch_shapes=[pltpu.SemaphoreType.DMA],
+        compiler_params=pltpu.CompilerParams(vmem_limit_bytes=24 * MIB),
+        cost_estimate=pl.CostEstimate(
+            flops=2 * tokens * depth * columns,
+            bytes_accessed=2 * (depth * (tokens + columns) + tokens * columns),
+            transcendentals=0,
+        ),
         name="values",
-        **call,
-    )(x, *[kv_weight] * heads, after)
+    )(x, weight, in_hbm(out_weight), after)
+
+
+def prepare_kernel(q_ref, kv_ref, out_ref):
+    own_rows, new_count, _, _ = out_ref.shape
+    for r in range(own_rows):
+        q, kv = q_ref[r].astype(F32), kv_ref[r].astype(F32)
+        for n in range(new_count):
+            parts = [a[n : n + 1, c : c + HD] for a in (q, kv) for c in range(0, a.shape[1], HD)]
+            out_ref[r, n] = jnp.concatenate(parts, axis=0).astype(BF16)
+
+
+def prepare(new_query, new_keyval):
+    own_rows, new_count, columns = new_query.shape
+    heads = (columns + new_keyval.shape[2]) // HD
+    return pl.pallas_call(
+        prepare_kernel,
+        in_specs=[VMEM, VMEM],
+        out_specs=VMEM,
+        out_shape=jax.ShapeDtypeStruct((own_rows, new_count, heads, HD), BF16),
+        compiler_params=pltpu.CompilerParams(vmem_limit_bytes=8 * MIB),
+        cost_estimate=pl.CostEstimate(flops=0, bytes_accessed=MIB, transcendentals=0),
+        name="prepare",
+    )(in_hbm(new_query), in_hbm(new_keyval))
 
 
 def stacked_kernel(n_tp, *refs):
@@ -228,11 +258,11 @@
 
 def scores_kernel(pages, n_seq, n_tp, *refs):
     new = refs[:n_seq]
-    ka_ref, kb_ref, meta = refs[n_seq : n_seq + 3]
-    outs = refs[n_seq + 3 : n_seq + 3 + n_tp]
-    fresh_ref, all_q, held, ready, cosines, sines = refs[n_seq + 3 + n_tp :]
+    k_ref, meta = refs[n_seq : n_seq + 2]
+    outs = refs[n_seq + 2 : n_seq + 2 + n_tp]
+    fresh_ref, all_q, held, ready, cosines, sines = refs[n_seq + 2 + n_tp :]
     kv_local = KVH // n_tp
-    local_pages = ka_ref.shape[0] // PAGE
+    local_pages = k_ref.shape[0] // PAGE
     _, own_rows, new_count, _, _ = new[0].shape
     prompts = own_rows * n_seq
     rows = new_count * GROUP
@@ -283,13 +313,11 @@
                         found[n] = jnp.where((lane == request) & (step >= n), s, found[n])
     for n in range(new_count):
         fresh_ref[n] = found[n]
-    half = ka_ref.shape[1] // HD
     for p in range(local_pages):
         request = meta[first + p]
         tokens = slice(p * PAGE, (p + 1) * PAGE)
         for head in range(KVH):
-            k_ref = ka_ref if head < half else kb_ref
-            k = k_ref[tokens, head % half * HD : (head % half + 1) * HD]
+            k = k_ref[tokens, head * HD : (head + 1) * HD]
             q = all_q[request, head * rows : (head + 1) * rows]
             s = lax.dot_general(q, k, (((1,), (1,)), ((), ())), preferred_element_type=F32)
             ready[head * rows : (head + 1) * rows, tokens] = (s * scale).astype(BF16)
@@ -298,14 +326,14 @@
         outs[d][...] = ready[pl.ds(pl.multiple_of((me ^ d) * count, count), count)]
 
 
-def partial_scores(new, ka, kb, meta, pages, prompts, n_tp):
+def partial_scores(new, k, meta, pages, prompts, n_tp):
     n_seq = len(new)
     new_count = new[0].shape[2]
-    tokens = ka.shape[0]
+    tokens = k.shape[0]
     rows = KVH // n_tp * new_count * GROUP
     return pl.pallas_call(
         functools.partial(scores_kernel, pages, n_seq, n_tp),
-        in_specs=[VMEM] * (n_seq + 2) + [SMEM],
+        in_specs=[VMEM] * (n_seq + 1) + [SMEM],
         out_specs=[VMEM] * (n_tp + 1),
         out_shape=[jax.ShapeDtypeStruct((rows, tokens), BF16)] * n_tp
         + [jax.ShapeDtypeStruct((new_count, rows, HD), F32)],
@@ -321,7 +349,7 @@
             flops=2 * tokens * rows * n_tp * HD, bytes_accessed=6 * MIB, transcendentals=0
         ),
         name="scores",
-    )(*new, ka, kb, meta)
+    )(*new, k, meta)
 
 
 def weights_kernel(pages, prompts, n_tp, *refs):
@@ -459,7 +487,7 @@
     pieces = refs[:n_seq]
     fresh_ref = refs[n_seq]
     new = refs[n_seq + 1 : 2 * n_seq + 1]
-    w_ref, out_ref, held = refs[2 * n_seq + 1 :]
+    wa_ref, wb_ref, out_ref, held = refs[2 * n_seq + 1 :]
     more, rows_local, _ = pieces[0].shape
     prompts = more - 1
     new_count = fresh_ref.shape[0]
@@ -514,24 +542,29 @@
                     held[g * GROUP : (g + 1) * GROUP, request * new_count + n] += sums[
                         at : at + GROUP
                     ]
-    left = jnp.concatenate([held[h].astype(BF16) for h in range(heads)], axis=1)
-    out_ref[...] = jnp.dot(left, w_ref[...], preferred_element_type=F32).astype(BF16)
-
-
-def output_partial(pieces, fresh, new, out_weight):
+    half = heads // 2
+    product = jnp.zeros(out_ref.shape, F32)
+    for w_ref, at in ((wa_ref, 0), (wb_ref, half)):
+        left = [held[h].astype(BF16) for h in range(at, at + half)]
+        left = jnp.concatenate(left, axis=1)
+        product = product + jnp.dot(left, w_ref[...], preferred_element_type=F32)
+    out_ref[...] = product.astype(BF16)
+
+
+def output_partial(pieces, fresh, new, weights):
     n_seq = len(pieces)
     new_count = fresh.shape[0]
     prompts = pieces[0].shape[0] - 1
-    depth, columns = out_weight.shape
+    depth, columns = weights[0].shape
     return pl.pallas_call(
         functools.partial(output_kernel, n_seq),
-        in_specs=[VMEM] * (2 * n_seq + 2),
+        in_specs=[VMEM] * (2 * n_seq + 3),
         out_specs=VMEM,
         out_shape=jax.ShapeDtypeStruct((prompts * new_count, columns), BF16),
-        scratch_shapes=[pltpu.VMEM((depth // HD, prompts * new_count, HD), F32)],
+        scratch_shapes=[pltpu.VMEM((2 * depth // HD, prompts * new_count, HD), F32)],
         compiler_params=pltpu.CompilerParams(vmem_limit_bytes=24 * MIB),
         name="output",
-    )(*pieces, fresh, *new, out_weight)
+    )(*pieces, fresh, *new, *weights)
 
 
 def final_kernel(n_tp, *refs):
@@ -564,27 +597,17 @@
     own_rows, new_count, _ = new_query.shape
     prompts = page_counts.shape[0]
     pages = prefill_states.shape[0] // PAGE * n_seq
-    new = jnp.concatenate(
-        [
-            new_query.reshape(own_rows, new_count, QH // n_tp, HD),
-            new_keyval.reshape(own_rows, new_count, 2 * KVH // n_tp, HD),
-        ],
-        axis=2,
-    )
-    half = KVH // 2
-    new = gather(new, "tp")
-    scalars = (page_counts, tail_tokens)
-    ka, meta = project_keys(prefill_states, kv_weight, 0, half, pages, prompts, scalars)
+    new = gather(prepare(new_query, new_keyval), "tp")
+    k, x, w, meta = project_keys(prefill_states, kv_weight, page_counts, tail_tokens, pages)
     new = stacked(new, meta)
-    kb = project_keys(prefill_states, kv_weight, half, half, pages, prompts, (meta,), new)
+    va, oa = project_values(x, w, out_weight, 0, new)
     new = gather(new, "seq")
-    *scores, fresh = partial_scores(new, ka, kb, meta, pages, prompts, n_tp)
-    va = project_values(prefill_states, kv_weight, 0, half, fresh)
+    *scores, fresh = partial_scores(new, k, meta, pages, prompts, n_tp)
+    vb, ob = project_values(x, w, out_weight, 1, fresh)
     weights, stats = softmax_weights(exchange(scores, "tp"), meta, pages, prompts)
-    vb = project_values(prefill_states, kv_weight, half, half, stats)
     chunks = weighted_values(gather(weights, "tp"), va, vb, meta, prompts)
     pieces = gather(summed(exchange(chunks, "tp"), stats), "seq")
-    partial = output_partial(pieces, fresh, new, out_weight)
+    partial = output_partial(pieces, fresh, new, (oa, ob))
     return final_sum(gather(partial, "tp"), residual)
 
 

time: 85.1 us -> 73.8 us (0.87)
  local copies, waits for them, and re-layouts: 10 us -> 0.01 us
  Pallas kernels: 32.8 us -> 24.2 us
  waiting for transfers between devices: 14.2 us -> 21.8 us
    unnamed x31 -> x2, local copies, waits for them, and re-layouts: 8.6 us -> 0.01 us
    pallas_call x4, Pallas kernels: 26.2 us -> 17.6 us  [the longest x1 12.1 us: project_keys(): pl.pallas_call(functools.partial(keys_kernel, pages, prompts), in_specs=[...]
    ppermute x21, waiting for transfers between devices: 14.2 us -> 21.8 us  [pairs(): lax.ppermute(value, axis, [(i, i ^ d) for i in range(lax.axis_size(axis))])]
    reshape x2 -> x0, local copies, waits for them, and re-layouts: 1.43 us -> none  [the longest x1 0.73 us: on_device(): new_query.reshape(own_rows, new_count, QH // n_tp, HD)]
  transfers between devices with their start and end apart: 21 -> 21, of which waited for: 7 -> 11; matrix products, arithmetic and copies ran while one was open for 0% -> 0% of each run, Pallas kernels for 31% -> 23%
where the time goes in v4:
time: 73.8 us; the launch traced here: 73.5 us
  starting transfers between devices  27.3 us (37%)
  Pallas kernels  24.2 us (33%)
  waiting for transfers between devices  21.8 us (30%)
    ppermute x21, starting transfers between devices, pairs(): lax.ppermute(value, axis, [(i, i ^ d) for i in range(lax.axis_size(axis))])  27.3 us
    ppermute x21, waiting for transfers between devices, pairs(): lax.ppermute(value, axis, [(i, i ^ d) for i in range(lax.axis_size(axis))])  21.8 us
    pallas_call x1, Pallas kernels, project_keys(): pl.pallas_call(functools.partial(keys_kernel, pages, prompts), in_specs=[...  12.1 us
    pallas_call x2, Pallas kernels, project_values(): pl.pallas_call(functools.partial(values_kernel, first), in_specs=[VMEM, V...  4.69 us
    pallas_call x1, Pallas kernels, partial_scores(): pl.pallas_call(functools.partial(scores_kernel, pages, n_seq, n_tp), in_s...  1.9 us
    pallas_call x1, Pallas kernels, output_partial(): pl.pallas_call(functools.partial(output_kernel, n_seq), in_specs=[VMEM] *...  1.83 us
  transfers between devices with their start and end apart: 21, of which 11 were waited for; matrix products, arithmetic and copies ran while one was open for 0% of the time, Pallas kernels for 23%

profile of v4, /device:TPU:0, one launch (start us, length us, event | category | flops | bytes accessed | tf_op | source)
XLA Modules:
  0.0 73.5 jit_solution(4946982576033701719)
XLA Ops:
  0.0 0.7 %prepare.1.refs_0_ = bf16[2,2,20,128]{3,2,1,0:T(8,128)(2,1)S(1)} custom-call(bf16[2,2,2048]{2,1,0:T(2,128)(2,1)} %q_ref.1, bf16[2,2,512]{2,1,0:T(2,128)(2,1)} %kv_ref.1), custom_call_target="tpu_custom_call" | custom-call | bytes 1048576 | tf_op jit(solution)/shard_map/prepare/pallas_call | solution.py:231
  0.7 5.1 %collective-permute-start.2 = (bf16[2,2,20,128]{3,2,1,0:T(8,128)(2,1)S(1)}, bf16[2,2,20,128]{3,2,1,0:T(8,128)(2,1)S(1)}, u32[]{:S(2)}, u32[]{:S(2)}) collective-permute-start(bf16[2,2,20,128]{3,2,1,0:T(8,128)(2,1)S(1)} %prepare.1.refs_0_), channel_id=1, source_target_pairs={{0,3},{1,2},{2,1},{3,0},{4,7},{5,6},{6,5},{7,4},{8,11},{9,10},{10,... | collective-permute-start | bytes 61448 | tf_op jit(solution)/shard_map/ppermute | solution.py:26
  6.5 12.1 %keys.1 = (bf16[1024,1024]{1,0:T(8,128)(2,1)S(1)}, bf16[1024,2048]{1,0:T(8,128)(2,1)S(1)}, bf16[2048,1024]{1,0:T(8,128)(2,1)S(1)}, s32[104]{0:T(128)S(1)}) custom-call(bf16[1024,2048]{1,0:T(8,128)(2,1)} %x_hbm.1, bf16[2048,2048]{1,0:T(8,128)(2,1)} %w_hbm.1, s32[8]{0:T(128)} %counts.1, s32[8]{0:T(128)} %tails.1), custom_call_target="tpu_custom_call" | custom-call | flops 4294967296 | bytes 14680064 | tf_op jit(solution)/shard_map/keys/pallas_call | solution.py:147
  19.2 1.3 %collective-permute-start.4 = (bf16[4,2,2,20,128]{4,3,2,1,0:T(8,128)(2,1)S(1)}, bf16[4,2,2,20,128]{4,3,2,1,0:T(8,128)(2,1)S(1)}, u32[]{:S(2)}, u32[]{:S(2)}) collective-permute-start(bf16[4,2,2,20,128]{4,3,2,1,0:T(8,128)(2,1)S(1)} %stacked.1.refs_0_.after.refs_5_), channel_id=1, source_target_pairs={{0,8},{4,12},{8,0},{12,4},{1,9},{5,13},{9,1},{13,5},{2,10},{6,14},... | collective-permute-start | bytes 245768 | tf_op jit(solution)/shard_map/ppermute | solution.py:26
  20.7 3.0 %collective-permute-done.5.refs_3_.refs_8_ = bf16[4,2,2,20,128]{4,3,2,1,0:T(8,128)(2,1)S(1)} collective-permute-done((bf16[4,2,2,20,128]{4,3,2,1,0:T(8,128)(2,1)S(1)}, bf16[4,2,2,20,128]{4,3,2,1,0:T(8,128)(2,1)S(1)}, u32[]{:S(2)}, u32[]{:S(2)}) %collective-permute-start.5) | collective-permute-done | bytes 81952 | tf_op jit(solution)/shard_map/ppermute | solution.py:26
  23.7 2.3 %collective-permute-done.4.refs_2_.refs_7_ = bf16[4,2,2,20,128]{4,3,2,1,0:T(8,128)(2,1)S(1)} collective-permute-done((bf16[4,2,2,20,128]{4,3,2,1,0:T(8,128)(2,1)S(1)}, bf16[4,2,2,20,128]{4,3,2,1,0:T(8,128)(2,1)S(1)}, u32[]{:S(2)}, u32[]{:S(2)}) %collective-permute-start.4) | collective-permute-done | bytes 81952 | tf_op jit(solution)/shard_map/ppermute | solution.py:26
  26.0 1.9 %scores.1 = (bf16[32,1024]{1,0:T(8,128)(2,1)S(1)}, bf16[32,1024]{1,0:T(8,128)(2,1)S(1)}, bf16[32,1024]{1,0:T(8,128)(2,1)S(1)}, bf16[32,1024]{1,0:T(8,128)(2,1)S(1)}, f32[2,32,128]{2,1,0:T(8,128)S(1)}) custom-call(bf16[4,2,2,20,128]{4,3,2,1,0:T(8,128)(2,1)S(1)} %stacked.1.refs_0_.after.refs_5_, ...), custom_call_target="tpu_custom_call" | custom-call | flops 33554432 | bytes 6291456 | tf_op jit(solution)/shard_map/scores/pallas_call | solution.py:334
  27.9 1.4 %collective-permute-start.6 = (bf16[32,1024]{1,0:T(8,128)(2,1)S(1)}, bf16[32,1024]{1,0:T(8,128)(2,1)S(1)}, u32[]{:S(2)}, u32[]{:S(2)}) collective-permute-start(bf16[32,1024]{1,0:T(8,128)(2,1)S(1)} %get-tuple-element.27), channel_id=1, source_target_pairs={{0,1},{1,0},{2,3},{3,2},{4,5},{5,4},{6,7},{7,6},{8,9},{9,8},{10,11... | collective-permute-start | bytes 196616 | tf_op jit(solution)/shard_map/ppermute | solution.py:26
  29.3 2.9 %collective-permute-start.7 = (bf16[32,1024]{1,0:T(8,128)(2,1)S(1)}, bf16[32,1024]{1,0:T(8,128)(2,1)S(1)}, u32[]{:S(2)}, u32[]{:S(2)}) collective-permute-start(bf16[32,1024]{1,0:T(8,128)(2,1)S(1)} %get-tuple-element.28), channel_id=1, source_target_pairs={{0,2},{1,3},{2,0},{3,1},{4,6},{5,7},{6,4},{7,5},{8,10},{9,11},{10,... | collective-permute-start | bytes 196616 | tf_op jit(solution)/shard_map/ppermute | solution.py:26
  32.3 2.3 %values.2 = (bf16[1024,512]{1,0:T(8,128)(2,1)S(1)}, bf16[1024,2048]{1,0:T(8,128)(2,1)S(1)}) custom-call(bf16[1024,2048]{1,0:T(8,128)(2,1)S(1)} %get-tuple-element.31.x_ref, bf16[2048,1024]{1,0:T(8,128)(2,1)S(1)} %get-tuple-element.32.w_ref, bf16[2048,2048]{1,0:T(8,128)(2,1)} %o_hbm.3, bf16[4,2,2,20,128]{4,3,2,1,0:T(8,128)(2,1)S(1)} %stacked.1.refs_0_.after.refs_5_), custom_call_target="tpu_custom_call" | custom-call | flops 2147483648 | bytes 7340032 | tf_op jit(solution)/shard_map/values/pallas_call | solution.py:195
  34.7 2.2 %collective-permute-done.7.refs_2_ = bf16[32,1024]{1,0:T(8,128)(2,1)S(1)} collective-permute-done((bf16[32,1024]{1,0:T(8,128)(2,1)S(1)}, bf16[32,1024]{1,0:T(8,128)(2,1)S(1)}, u32[]{:S(2)}, u32[]{:S(2)}) %collective-permute-start.7) | collective-permute-done | bytes 65568 | tf_op jit(solution)/shard_map/ppermute | solution.py:26
  37.0 1.5 %collective-permute-done.8.refs_3_ = bf16[32,1024]{1,0:T(8,128)(2,1)S(1)} collective-permute-done((bf16[32,1024]{1,0:T(8,128)(2,1)S(1)}, bf16[32,1024]{1,0:T(8,128)(2,1)S(1)}, u32[]{:S(2)}, u32[]{:S(2)}) %collective-permute-start.8) | collective-permute-done | bytes 65568 | tf_op jit(solution)/shard_map/ppermute | solution.py:26
  38.4 0.9 %weights.1 = (bf16[32,1024]{1,0:T(8,128)(2,1)S(1)}, bf16[32,128]{1,0:T(8,128)(2,1)S(1)}) custom-call(bf16[32,1024]{1,0:T(8,128)(2,1)S(1)} %get-tuple-element.26.refs_0_, bf16[32,1024]{1,0:T(8,128)(2,1)S(1)} %collective-permute-done.6.refs_1_, bf16[32,1024]{1,0:T(8,128)(2,1)S(1)} %collective-permute-done.7.refs_2_, ...), custom_call_target="tpu_custom_call" | custom-call | tf_op jit(solution)/shard_map/weights/pallas_call | solution.py:400
  39.4 1.8 %collective-permute-start.11 = (bf16[32,1024]{1,0:T(8,128)(2,1)S(1)}, bf16[32,1024]{1,0:T(8,128)(2,1)S(1)}, u32[]{:S(2)}, u32[]{:S(2)}) collective-permute-start(bf16[32,1024]{1,0:T(8,128)(2,1)S(1)} %get-tuple-element.30.refs_0_), channel_id=1, source_target_pairs={{0,3},{1,2},{2,1},{3,0},{4,7},{5,6},{6,5},{7,4},{8,11},{9,10},{10,... | collective-permute-start | bytes 196616 | tf_op jit(solution)/shard_map/ppermute | solution.py:26
  41.5 2.3 %collective-permute-start.9 = (bf16[32,1024]{1,0:T(8,128)(2,1)S(1)}, bf16[32,1024]{1,0:T(8,128)(2,1)S(1)}, u32[]{:S(2)}, u32[]{:S(2)}) collective-permute-start(bf16[32,1024]{1,0:T(8,128)(2,1)S(1)} %get-tuple-element.30.refs_0_), channel_id=1, source_target_pairs={{0,1},{1,0},{2,3},{3,2},{4,5},{5,4},{6,7},{7,6},{8,9},{9,8},{10,11... | collective-permute-start | bytes 196616 | tf_op jit(solution)/shard_map/ppermute | solution.py:26
  43.7 2.3 %values.3 = (bf16[1024,512]{1,0:T(8,128)(2,1)S(1)}, bf16[1024,2048]{1,0:T(8,128)(2,1)S(1)}) custom-call(bf16[1024,2048]{1,0:T(8,128)(2,1)S(1)} %get-tuple-element.31.x_ref, bf16[2048,1024]{1,0:T(8,128)(2,1)S(1)} %get-tuple-element.32.w_ref, bf16[2048,2048]{1,0:T(8,128)(2,1)} %o_hbm.3, f32[2,32,128]{2,1,0:T(8,128)S(1)} %get-tuple-element.34.after.refs_4_), custom_call_target="tpu_custom_call" | custom-call | flops 2147483648 | bytes 7340032 | tf_op jit(solution)/shard_map/values/pallas_call | solution.py:195
  46.1 0.9 %collective-permute-done.10.refs_2_ = bf16[32,1024]{1,0:T(8,128)(2,1)S(1)} collective-permute-done((bf16[32,1024]{1,0:T(8,128)(2,1)S(1)}, bf16[32,1024]{1,0:T(8,128)(2,1)S(1)}, u32[]{:S(2)}, u32[]{:S(2)}) %collective-permute-start.10) | collective-permute-done | bytes 65568 | tf_op jit(solution)/shard_map/ppermute | solution.py:26
  47.0 1.3 %weighted.1 = (bf16[8,32,128]{2,1,0:T(8,128)(2,1)S(1)}, bf16[8,32,128]{2,1,0:T(8,128)(2,1)S(1)}, bf16[8,32,128]{2,1,0:T(8,128)(2,1)S(1)}, bf16[8,32,128]{2,1,0:T(8,128)(2,1)S(1)}) custom-call(bf16[32,1024]{1,0:T(8,128)(2,1)S(1)} %get-tuple-element.30.refs_0_, bf16[32,1024]{1,0:T(8,128)(2,1)S(1)} %collective-permute-done.9.refs_1_, ...), custom_call_target="tpu_custom_call" | custom-call | flops 33554432 | bytes 8388608 | tf_op jit(solution)/shard_map/weighted/pallas_call | solution.py:444
  48.3 1.1 %collective-permute-start.12 = (bf16[8,32,128]{2,1,0:T(8,128)(2,1)S(1)}, bf16[8,32,128]{2,1,0:T(8,128)(2,1)S(1)}, u32[]{:S(2)}, u32[]{:S(2)}) collective-permute-start(bf16[8,32,128]{2,1,0:T(8,128)(2,1)S(1)} %get-tuple-element.37), channel_id=1, source_target_pairs={{0,1},{1,0},{2,3},{3,2},{4,5},{5,4},{6,7},{7,6},{8,9},{9,8},{10,11... | collective-permute-start | bytes 196616 | tf_op jit(solution)/shard_map/ppermute | solution.py:26
  49.4 1.4 %collective-permute-start.13 = (bf16[8,32,128]{2,1,0:T(8,128)(2,1)S(1)}, bf16[8,32,128]{2,1,0:T(8,128)(2,1)S(1)}, u32[]{:S(2)}, u32[]{:S(2)}) collective-permute-start(bf16[8,32,128]{2,1,0:T(8,128)(2,1)S(1)} %get-tuple-element.38), channel_id=1, source_target_pairs={{0,2},{1,3},{2,0},{3,1},{4,6},{5,7},{6,4},{7,5},{8,10},{9,11},{10,... | collective-permute-start | bytes 196616 | tf_op jit(solution)/shard_map/ppermute | solution.py:26
  50.8 1.9 %collective-permute-start.14 = (bf16[8,32,128]{2,1,0:T(8,128)(2,1)S(1)}, bf16[8,32,128]{2,1,0:T(8,128)(2,1)S(1)}, u32[]{:S(2)}, u32[]{:S(2)}) collective-permute-start(bf16[8,32,128]{2,1,0:T(8,128)(2,1)S(1)} %get-tuple-element.39), channel_id=1, source_target_pairs={{0,3},{1,2},{2,1},{3,0},{4,7},{5,6},{6,5},{7,4},{8,11},{9,10},{10,... | collective-permute-start | bytes 196616 | tf_op jit(solution)/shard_map/ppermute | solution.py:26
  52.7 3.0 %collective-permute-done.13.refs_2_ = bf16[8,32,128]{2,1,0:T(8,128)(2,1)S(1)} collective-permute-done((bf16[8,32,128]{2,1,0:T(8,128)(2,1)S(1)}, bf16[8,32,128]{2,1,0:T(8,128)(2,1)S(1)}, u32[]{:S(2)}, u32[]{:S(2)}) %collective-permute-start.13) | collective-permute-done | bytes 65568 | tf_op jit(solution)/shard_map/ppermute | solution.py:26
  55.7 1.2 %collective-permute-done.14.refs_3_ = bf16[8,32,128]{2,1,0:T(8,128)(2,1)S(1)} collective-permute-done((bf16[8,32,128]{2,1,0:T(8,128)(2,1)S(1)}, bf16[8,32,128]{2,1,0:T(8,128)(2,1)S(1)}, u32[]{:S(2)}, u32[]{:S(2)}) %collective-permute-start.14) | collective-permute-done | bytes 65568 | tf_op jit(solution)/shard_map/ppermute | solution.py:26
  57.7 1.3 %collective-permute-start.15 = (bf16[9,32,128]{2,1,0:T(8,128)(2,1)S(1)}, bf16[9,32,128]{2,1,0:T(8,128)(2,1)S(1)}, u32[]{:S(2)}, u32[]{:S(2)}) collective-permute-start(bf16[9,32,128]{2,1,0:T(8,128)(2,1)S(1)} %summed.1.refs_0_), channel_id=1, source_target_pairs={{0,4},{4,0},{8,12},{12,8},{1,5},{5,1},{9,13},{13,9},{2,6},{6,2},{1... | collective-permute-start | bytes 221192 | tf_op jit(solution)/shard_map/ppermute | solution.py:26
  58.9 2.1 %collective-permute-done.17.refs_3_ = bf16[9,32,128]{2,1,0:T(8,128)(2,1)S(1)} collective-permute-done((bf16[9,32,128]{2,1,0:T(8,128)(2,1)S(1)}, bf16[9,32,128]{2,1,0:T(8,128)(2,1)S(1)}, u32[]{:S(2)}, u32[]{:S(2)}) %collective-permute-start.17) | collective-permute-done | bytes 73760 | tf_op jit(solution)/shard_map/ppermute | solution.py:26
  61.0 1.2 %collective-permute-done.16.refs_2_ = bf16[9,32,128]{2,1,0:T(8,128)(2,1)S(1)} collective-permute-done((bf16[9,32,128]{2,1,0:T(8,128)(2,1)S(1)}, bf16[9,32,128]{2,1,0:T(8,128)(2,1)S(1)}, u32[]{:S(2)}, u32[]{:S(2)}) %collective-permute-start.16) | collective-permute-done | bytes 73760 | tf_op jit(solution)/shard_map/ppermute | solution.py:26
  62.3 1.8 %output.1.refs_0_ = bf16[16,2048]{1,0:T(8,128)(2,1)S(1)} custom-call(bf16[9,32,128]{2,1,0:T(8,128)(2,1)S(1)} %summed.1.refs_0_, bf16[9,32,128]{2,1,0:T(8,128)(2,1)S(1)} %collective-permute-done.15.refs_1_, bf16[9,32,128]{2,1,0:T(8,128)(2,1)S(1)} %collective-permute-done.16.refs_2_, bf16[9,32,128]{2,1,0:T(8,128)(2,1)S(1)} %collective-permute-done.17.refs_3_, ...), custom_call_target="tpu_custom_call" | custom-call | tf_op jit(solution)/shard_map/output/pallas_call | solution.py:559
  64.1 1.8 %collective-permute-start.20 = (bf16[16,2048]{1,0:T(8,128)(2,1)S(1)}, bf16[16,2048]{1,0:T(8,128)(2,1)S(1)}, u32[]{:S(2)}, u32[]{:S(2)}) collective-permute-start(bf16[16,2048]{1,0:T(8,128)(2,1)S(1)} %output.1.refs_0_), channel_id=1, source_target_pairs={{0,3},{1,2},{2,1},{3,0},{4,7},{5,6},{6,5},{7,4},{8,11},{9,10},{10,... | collective-permute-start | bytes 196616 | tf_op jit(solution)/shard_map/ppermute | solution.py:26
  66.3 2.2 %collective-permute-start.18 = (bf16[16,2048]{1,0:T(8,128)(2,1)S(1)}, bf16[16,2048]{1,0:T(8,128)(2,1)S(1)}, u32[]{:S(2)}, u32[]{:S(2)}) collective-permute-start(bf16[16,2048]{1,0:T(8,128)(2,1)S(1)} %output.1.refs_0_), channel_id=1, source_target_pairs={{0,1},{1,0},{2,3},{3,2},{4,5},{5,4},{6,7},{7,6},{8,9},{9,8},{10,11... | collective-permute-start | bytes 196616 | tf_op jit(solution)/shard_map/ppermute | solution.py:26
  68.5 2.4 %collective-permute-done.20.refs_3_ = bf16[16,2048]{1,0:T(8,128)(2,1)S(1)} collective-permute-done((bf16[16,2048]{1,0:T(8,128)(2,1)S(1)}, bf16[16,2048]{1,0:T(8,128)(2,1)S(1)}, u32[]{:S(2)}, u32[]{:S(2)}) %collective-permute-start.20) | collective-permute-done | bytes 65568 | tf_op jit(solution)/shard_map/ppermute | solution.py:26
  70.8 2.0 %collective-permute-done.19.refs_2_ = bf16[16,2048]{1,0:T(8,128)(2,1)S(1)} collective-permute-done((bf16[16,2048]{1,0:T(8,128)(2,1)S(1)}, bf16[16,2048]{1,0:T(8,128)(2,1)S(1)}, u32[]{:S(2)}, u32[]{:S(2)}) %collective-permute-start.19) | collective-permute-done | bytes 65568 | tf_op jit(solution)/shard_map/ppermute | solution.py:26
  72.8 0.7 final.1
  (23 shorter events, 2.8 us)
Async XLA Ops:
  0.7 17.9 %collective-permute-start.2 = (bf16[2,2,20,128]{3,2,1,0:T(8,128)(2,1)S(1)}, bf16[2,2,20,128]{3,2,1,0:T(8,128)(2,1)S(1)}, u32[]{:S(2)}, u32[]{:S(2)}) collective-permute-start(bf16[2,2,20,128]{3,2,1,0:T(8,128)(2,1)S(1)} %prepare.1.refs_0_), channel_id=1, source_target_pairs={{0,3},{1,2},{2,1},{3,0},{4,7},{5,6},{6,5},{7,4},{8,11},{9,10},{10,... | collective-permute-start | bytes 61448 | tf_op jit(solution)/shard_map/ppermute | solution.py:26
  5.9 12.8 %collective-permute-start.1 = (bf16[2,2,20,128]{3,2,1,0:T(8,128)(2,1)S(1)}, bf16[2,2,20,128]{3,2,1,0:T(8,128)(2,1)S(1)}, u32[]{:S(2)}, u32[]{:S(2)}) collective-permute-start(bf16[2,2,20,128]{3,2,1,0:T(8,128)(2,1)S(1)} %prepare.1.refs_0_), channel_id=1, source_target_pairs={{0,2},{1,3},{2,0},{3,1},{4,6},{5,7},{6,4},{7,5},{8,10},{9,11},{10,... | collective-permute-start | bytes 61448 | tf_op jit(solution)/shard_map/ppermute | solution.py:26
  5.9 12.8 %collective-permute-start = (bf16[2,2,20,128]{3,2,1,0:T(8,128)(2,1)S(1)}, bf16[2,2,20,128]{3,2,1,0:T(8,128)(2,1)S(1)}, u32[]{:S(2)}, u32[]{:S(2)}) collective-permute-start(bf16[2,2,20,128]{3,2,1,0:T(8,128)(2,1)S(1)} %prepare.1.refs_0_), channel_id=1, source_target_pairs={{0,1},{1,0},{2,3},{3,2},{4,5},{5,4},{6,7},{7,6},{8,9},{9,8},{10,11... | collective-permute-start | bytes 61448 | tf_op jit(solution)/shard_map/ppermute | solution.py:26
  18.7 4.9 %collective-permute-start.5 = (bf16[4,2,2,20,128]{4,3,2,1,0:T(8,128)(2,1)S(1)}, bf16[4,2,2,20,128]{4,3,2,1,0:T(8,128)(2,1)S(1)}, u32[]{:S(2)}, u32[]{:S(2)}) collective-permute-start(bf16[4,2,2,20,128]{4,3,2,1,0:T(8,128)(2,1)S(1)} %stacked.1.refs_0_.after.refs_5_), channel_id=1, source_target_pairs={{0,12},{4,8},{8,4},{12,0},{1,13},{5,9},{9,5},{13,1},{2,14},{6,10},... | collective-permute-start | bytes 245768 | tf_op jit(solution)/shard_map/ppermute | solution.py:26
  19.2 6.8 %collective-permute-start.4 = (bf16[4,2,2,20,128]{4,3,2,1,0:T(8,128)(2,1)S(1)}, bf16[4,2,2,20,128]{4,3,2,1,0:T(8,128)(2,1)S(1)}, u32[]{:S(2)}, u32[]{:S(2)}) collective-permute-start(bf16[4,2,2,20,128]{4,3,2,1,0:T(8,128)(2,1)S(1)} %stacked.1.refs_0_.after.refs_5_), channel_id=1, source_target_pairs={{0,8},{4,12},{8,0},{12,4},{1,9},{5,13},{9,1},{13,5},{2,10},{6,14},... | collective-permute-start | bytes 245768 | tf_op jit(solution)/shard_map/ppermute | solution.py:26
  20.5 5.5 %collective-permute-start.3 = (bf16[4,2,2,20,128]{4,3,2,1,0:T(8,128)(2,1)S(1)}, bf16[4,2,2,20,128]{4,3,2,1,0:T(8,128)(2,1)S(1)}, u32[]{:S(2)}, u32[]{:S(2)}) collective-permute-start(bf16[4,2,2,20,128]{4,3,2,1,0:T(8,128)(2,1)S(1)} %stacked.1.refs_0_.after.refs_5_), channel_id=1, source_target_pairs={{0,4},{4,0},{8,12},{12,8},{1,5},{5,1},{9,13},{13,9},{2,6},{6,2},{1... | collective-permute-start | bytes 245768 | tf_op jit(solution)/shard_map/ppermute | solution.py:26
  27.9 6.8 %collective-permute-start.6 = (bf16[32,1024]{1,0:T(8,128)(2,1)S(1)}, bf16[32,1024]{1,0:T(8,128)(2,1)S(1)}, u32[]{:S(2)}, u32[]{:S(2)}) collective-permute-start(bf16[32,1024]{1,0:T(8,128)(2,1)S(1)} %get-tuple-element.27), channel_id=1, source_target_pairs={{0,1},{1,0},{2,3},{3,2},{4,5},{5,4},{6,7},{7,6},{8,9},{9,8},{10,11... | collective-permute-start | bytes 196616 | tf_op jit(solution)/shard_map/ppermute | solution.py:26
  29.3 7.6 %collective-permute-start.7 = (bf16[32,1024]{1,0:T(8,128)(2,1)S(1)}, bf16[32,1024]{1,0:T(8,128)(2,1)S(1)}, u32[]{:S(2)}, u32[]{:S(2)}) collective-permute-start(bf16[32,1024]{1,0:T(8,128)(2,1)S(1)} %get-tuple-element.28), channel_id=1, source_target_pairs={{0,2},{1,3},{2,0},{3,1},{4,6},{5,7},{6,4},{7,5},{8,10},{9,11},{10,... | collective-permute-start | bytes 196616 | tf_op jit(solution)/shard_map/ppermute | solution.py:26
  32.3 6.2 %collective-permute-start.8 = (bf16[32,1024]{1,0:T(8,128)(2,1)S(1)}, bf16[32,1024]{1,0:T(8,128)(2,1)S(1)}, u32[]{:S(2)}, u32[]{:S(2)}) collective-permute-start(bf16[32,1024]{1,0:T(8,128)(2,1)S(1)} %get-tuple-element.29), channel_id=1, source_target_pairs={{0,3},{1,2},{2,1},{3,0},{4,7},{5,6},{6,5},{7,4},{8,11},{9,10},{10,... | collective-permute-start | bytes 196616 | tf_op jit(solution)/shard_map/ppermute | solution.py:26
  39.4 6.7 %collective-permute-start.11 = (bf16[32,1024]{1,0:T(8,128)(2,1)S(1)}, bf16[32,1024]{1,0:T(8,128)(2,1)S(1)}, u32[]{:S(2)}, u32[]{:S(2)}) collective-permute-start(bf16[32,1024]{1,0:T(8,128)(2,1)S(1)} %get-tuple-element.30.refs_0_), channel_id=1, source_target_pairs={{0,3},{1,2},{2,1},{3,0},{4,7},{5,6},{6,5},{7,4},{8,11},{9,10},{10,... | collective-permute-start | bytes 196616 | tf_op jit(solution)/shard_map/ppermute | solution.py:26
  41.2 5.8 %collective-permute-start.10 = (bf16[32,1024]{1,0:T(8,128)(2,1)S(1)}, bf16[32,1024]{1,0:T(8,128)(2,1)S(1)}, u32[]{:S(2)}, u32[]{:S(2)}) collective-permute-start(bf16[32,1024]{1,0:T(8,128)(2,1)S(1)} %get-tuple-element.30.refs_0_), channel_id=1, source_target_pairs={{0,2},{1,3},{2,0},{3,1},{4,6},{5,7},{6,4},{7,5},{8,10},{9,11},{10,... | collective-permute-start | bytes 196616 | tf_op jit(solution)/shard_map/ppermute | solution.py:26
  41.5 5.5 %collective-permute-start.9 = (bf16[32,1024]{1,0:T(8,128)(2,1)S(1)}, bf16[32,1024]{1,0:T(8,128)(2,1)S(1)}, u32[]{:S(2)}, u32[]{:S(2)}) collective-permute-start(bf16[32,1024]{1,0:T(8,128)(2,1)S(1)} %get-tuple-element.30.refs_0_), channel_id=1, source_target_pairs={{0,1},{1,0},{2,3},{3,2},{4,5},{5,4},{6,7},{7,6},{8,9},{9,8},{10,11... | collective-permute-start | bytes 196616 | tf_op jit(solution)/shard_map/ppermute | solution.py:26
  48.3 4.5 %collective-permute-start.12 = (bf16[8,32,128]{2,1,0:T(8,128)(2,1)S(1)}, bf16[8,32,128]{2,1,0:T(8,128)(2,1)S(1)}, u32[]{:S(2)}, u32[]{:S(2)}) collective-permute-start(bf16[8,32,128]{2,1,0:T(8,128)(2,1)S(1)} %get-tuple-element.37), channel_id=1, source_target_pairs={{0,1},{1,0},{2,3},{3,2},{4,5},{5,4},{6,7},{7,6},{8,9},{9,8},{10,11... | collective-permute-start | bytes 196616 | tf_op jit(solution)/shard_map/ppermute | solution.py:26
  49.4 6.4 %collective-permute-start.13 = (bf16[8,32,128]{2,1,0:T(8,128)(2,1)S(1)}, bf16[8,32,128]{2,1,0:T(8,128)(2,1)S(1)}, u32[]{:S(2)}, u32[]{:S(2)}) collective-permute-start(bf16[8,32,128]{2,1,0:T(8,128)(2,1)S(1)} %get-tuple-element.38), channel_id=1, source_target_pairs={{0,2},{1,3},{2,0},{3,1},{4,6},{5,7},{6,4},{7,5},{8,10},{9,11},{10,... | collective-permute-start | bytes 196616 | tf_op jit(solution)/shard_map/ppermute | solution.py:26
  50.8 6.2 %collective-permute-start.14 = (bf16[8,32,128]{2,1,0:T(8,128)(2,1)S(1)}, bf16[8,32,128]{2,1,0:T(8,128)(2,1)S(1)}, u32[]{:S(2)}, u32[]{:S(2)}) collective-permute-start(bf16[8,32,128]{2,1,0:T(8,128)(2,1)S(1)} %get-tuple-element.39), channel_id=1, source_target_pairs={{0,3},{1,2},{2,1},{3,0},{4,7},{5,6},{6,5},{7,4},{8,11},{9,10},{10,... | collective-permute-start | bytes 196616 | tf_op jit(solution)/shard_map/ppermute | solution.py:26
  57.0 4.0 %collective-permute-start.17 = (bf16[9,32,128]{2,1,0:T(8,128)(2,1)S(1)}, bf16[9,32,128]{2,1,0:T(8,128)(2,1)S(1)}, u32[]{:S(2)}, u32[]{:S(2)}) collective-permute-start(bf16[9,32,128]{2,1,0:T(8,128)(2,1)S(1)} %summed.1.refs_0_), channel_id=1, source_target_pairs={{0,12},{4,8},{8,4},{12,0},{1,13},{5,9},{9,5},{13,1},{2,14},{6,10},... | collective-permute-start | bytes 221192 | tf_op jit(solution)/shard_map/ppermute | solution.py:26
  57.1 5.2 %collective-permute-start.16 = (bf16[9,32,128]{2,1,0:T(8,128)(2,1)S(1)}, bf16[9,32,128]{2,1,0:T(8,128)(2,1)S(1)}, u32[]{:S(2)}, u32[]{:S(2)}) collective-permute-start(bf16[9,32,128]{2,1,0:T(8,128)(2,1)S(1)} %summed.1.refs_0_), channel_id=1, source_target_pairs={{0,8},{4,12},{8,0},{12,4},{1,9},{5,13},{9,1},{13,5},{2,10},{6,14},... | collective-permute-start | bytes 221192 | tf_op jit(solution)/shard_map/ppermute | solution.py:26
  57.7 4.6 %collective-permute-start.15 = (bf16[9,32,128]{2,1,0:T(8,128)(2,1)S(1)}, bf16[9,32,128]{2,1,0:T(8,128)(2,1)S(1)}, u32[]{:S(2)}, u32[]{:S(2)}) collective-permute-start(bf16[9,32,128]{2,1,0:T(8,128)(2,1)S(1)} %summed.1.refs_0_), channel_id=1, source_target_pairs={{0,4},{4,0},{8,12},{12,8},{1,5},{5,1},{9,13},{13,9},{2,6},{6,2},{1... | collective-permute-start | bytes 221192 | tf_op jit(solution)/shard_map/ppermute | solution.py:26
  62.3 10.6 %copy-start = (bf16[8,2,2048]{2,1,0:T(2,128)(2,1)S(1)}, bf16[8,2,2048]{2,1,0:T(2,128)(2,1)}, u32[]{:S(2)}) copy-start(bf16[8,2,2048]{2,1,0:T(2,128)(2,1)} %refs_4_.1) | copy-start | bytes 196612
  64.1 6.8 %collective-permute-start.20 = (bf16[16,2048]{1,0:T(8,128)(2,1)S(1)}, bf16[16,2048]{1,0:T(8,128)(2,1)S(1)}, u32[]{:S(2)}, u32[]{:S(2)}) collective-permute-start(bf16[16,2048]{1,0:T(8,128)(2,1)S(1)} %output.1.refs_0_), channel_id=1, source_target_pairs={{0,3},{1,2},{2,1},{3,0},{4,7},{5,6},{6,5},{7,4},{8,11},{9,10},{10,... | collective-permute-start | bytes 196616 | tf_op jit(solution)/shard_map/ppermute | solution.py:26
  65.9 6.9 %collective-permute-start.19 = (bf16[16,2048]{1,0:T(8,128)(2,1)S(1)}, bf16[16,2048]{1,0:T(8,128)(2,1)S(1)}, u32[]{:S(2)}, u32[]{:S(2)}) collective-permute-start(bf16[16,2048]{1,0:T(8,128)(2,1)S(1)} %output.1.refs_0_), channel_id=1, source_target_pairs={{0,2},{1,3},{2,0},{3,1},{4,6},{5,7},{6,4},{7,5},{8,10},{9,11},{10,... | collective-permute-start | bytes 196616 | tf_op jit(solution)/shard_map/ppermute | solution.py:26
  66.3 6.5 %collective-permute-start.18 = (bf16[16,2048]{1,0:T(8,128)(2,1)S(1)}, bf16[16,2048]{1,0:T(8,128)(2,1)S(1)}, u32[]{:S(2)}, u32[]{:S(2)}) collective-permute-start(bf16[16,2048]{1,0:T(8,128)(2,1)S(1)} %output.1.refs_0_), channel_id=1, source_target_pairs={{0,1},{1,0},{2,3},{3,2},{4,5},{5,4},{6,7},{7,6},{8,9},{9,8},{10,11... | collective-permute-start | bytes 196616 | tf_op jit(solution)/shard_map/ppermute | solution.py:26

commit v5 on v4

--- a/solution.py
+++ b/solution.py
@@ -27,11 +27,13 @@
 
 
 def exchange(chunks, axis):
-    return [chunks[0]] + [pairs(chunks[d], axis, d) for d in range(1, len(chunks))]
+    got = {d: pairs(chunks[d], axis, d) for d in reversed(range(1, len(chunks)))}
+    return [chunks[0]] + [got[d] for d in range(1, len(chunks))]
 
 
 def gather(value, axis):
-    return exchange([value] * lax.axis_size(axis), axis)
+    size = lax.axis_size(axis)
+    return [value] + [pairs(value, axis, d) for d in range(1, size)]
 
 
 def lane_freqs(rows):
@@ -95,81 +97,105 @@
             sin_s[at] = sign * (sine * c + cosine * s)
 
 
-def keys_kernel(pages, prompts, x_hbm, w_hbm, counts, tails, k_ref, x_ref, v_ref, meta, *scratch):
-    w_ref, cos_s, sin_s, x_sems, k_sems, v_sems = scratch
-    tokens = x_ref.shape[0]
+def pair_columns(w_ref, rows, pair, part):
+    at = [(2 * head + part) * HD for head in (2 * pair, 2 * pair + 1)]
+    return jnp.concatenate([w_ref[rows, c : c + HD] for c in at], axis=1)
+
+
+def load_kernel(pages, prompts, new_count, x_hbm, w_hbm, counts, tails, *refs):
+    acc, x_ref, w_ref, cos_ref, sin_ref, cos_q, sin_q, meta, x_sems, w_sems = refs
+    tokens, depth = x_ref.shape
+    half, tall = depth // 2, tokens // 2
+    copies = []
+    for i in range(2):
+        at = pl.ds(i * half, half)
+        x_copy = pltpu.make_async_copy(x_hbm.at[:, at], x_ref.at[:, at], x_sems.at[i])
+        w_copy = pltpu.make_async_copy(w_hbm.at[at], w_ref.at[at], w_sems.at[i])
+        x_copy.start()
+        w_copy.start()
+        copies.append((x_copy, w_copy))
+    page_table(pages, prompts, counts, tails, meta)
+    rotation_tables(pages, tokens // PAGE, meta, cos_ref, sin_ref)
+    spots = [meta[3 * pages + r] + n for r in range(prompts) for n in range(new_count)]
+    angles = by_row(len(spots), spots) * lane_freqs(len(spots))
+    cos_q[...] = jnp.cos(angles)
+    sin_q[...] = jnp.sin(angles) * sine_sign(len(spots))
+    for copy in copies[0]:
+        copy.wait()
+    rows = slice(0, half)
+    for pair in range(KVH // 2):
+        weight = pair_columns(w_ref, rows, pair, 0)
+        for start in range(0, tokens, tall):
+            at = slice(start, start + tall)
+            acc[at, 2 * pair * HD : 2 * (pair + 1) * HD] = jnp.dot(
+                x_ref[at, rows], weight, preferred_element_type=F32
+            )
+    for copy in copies[1]:
+        copy.wait()
+
+
+def load(x, kv_weight, counts, tails, pages, new_count):
+    tokens, depth = x.shape
+    columns = kv_weight.shape[1]
+    prompts = counts.shape[0]
+    hbm = pl.BlockSpec(memory_space=pltpu.HBM)
+    return pl.pallas_call(
+        functools.partial(load_kernel, pages, prompts, new_count),
+        in_specs=[hbm, hbm, SMEM, SMEM],
+        out_specs=[VMEM] * 7 + [SMEM],
+        out_shape=[
+            pltpu.VMEM((tokens, KVH * HD), F32),
+            pltpu.VMEM((tokens, depth), BF16),
+            pltpu.VMEM((depth, columns), BF16),
+            pltpu.VMEM((tokens, HD), F32),
+            pltpu.VMEM((tokens, HD), F32),
+            pltpu.VMEM((prompts * new_count, HD), F32),
+            pltpu.VMEM((prompts * new_count, HD), F32),
+            jax.ShapeDtypeStruct((3 * pages + prompts,), jnp.int32),
+        ],
+        scratch_shapes=[pltpu.SemaphoreType.DMA((2,)), pltpu.SemaphoreType.DMA((2,))],
+        compiler_params=pltpu.CompilerParams(vmem_limit_bytes=28 * MIB),
+        cost_estimate=pl.CostEstimate(
+            flops=tokens * depth * KVH * HD,
+            bytes_accessed=2 * depth * (tokens + columns),
+            transcendentals=0,
+        ),
+        name="load",
+    )(*[in_hbm(a) for a in (x, kv_weight, counts, tails)])
+
+
+def keys_kernel(acc, x_ref, w_ref, cos_ref, sin_ref, after, k_ref):
+    tokens, depth = x_ref.shape
     tall = tokens // 2
-
-    def x_copy(i):
-        at = pl.ds(i * tall, tall)
-        return pltpu.make_async_copy(x_hbm.at[at], x_ref.at[at], x_sems.at[i])
-
-    def w_copy(head, part):
-        to, sems = (w_ref, k_sems) if part == 0 else (v_ref, v_sems)
-        return pltpu.make_async_copy(
-            w_hbm.at[:, pl.ds((2 * head + part) * HD, HD)],
-            to.at[:, pl.ds(head * HD, HD)],
-            sems.at[head],
-        )
-
-    x_copy(0).start()
-    w_copy(0, 0).start()
-    w_copy(1, 0).start()
-    x_copy(1).start()
-    for head in range(2, KVH):
-        w_copy(head, 0).start()
-    for head in range(KVH):
-        w_copy(head, 1).start()
-    page_table(pages, prompts, counts, tails, meta)
-    rotation_tables(pages, tokens // PAGE, meta, cos_s, sin_s)
+    rows = slice(depth // 2, depth)
     for pair in range(KVH // 2):
-        w_copy(2 * pair, 0).wait()
-        w_copy(2 * pair + 1, 0).wait()
+        weight = pair_columns(w_ref, rows, pair, 0)
         columns = slice(2 * pair * HD, 2 * (pair + 1) * HD)
-        for i in range(2):
-            if pair == 0:
-                x_copy(i).wait()
-            at = slice(i * tall, (i + 1) * tall)
-            product = jnp.dot(x_ref[at], w_ref[:, columns], preferred_element_type=F32)
-            cosine, sine = cos_s[at], sin_s[at]
+        for start in range(0, tokens, tall):
+            at = slice(start, start + tall)
+            product = acc[at, columns] + jnp.dot(
+                x_ref[at, rows], weight, preferred_element_type=F32
+            )
+            cosine, sine = cos_ref[at], sin_ref[at]
             for h in range(2):
                 k = product[:, h * HD : (h + 1) * HD]
                 k = k * cosine + pltpu.roll(k, HD // 2, 1) * sine
                 k_ref[at, (2 * pair + h) * HD : (2 * pair + h + 1) * HD] = k.astype(BF16)
-    for head in range(KVH):
-        w_copy(head, 1).wait()
-
-
-def project_keys(x, kv_weight, counts, tails, pages):
+
+
+def rotated_keys(acc, x, weight, cosine, sine, after):
     tokens, depth = x.shape
-    prompts = counts.shape[0]
-    hbm = pl.BlockSpec(memory_space=pltpu.HBM)
-    return pl.pallas_call(
-        functools.partial(keys_kernel, pages, prompts),
-        in_specs=[hbm, hbm, SMEM, SMEM],
-        out_specs=[VMEM, VMEM, VMEM, SMEM],
-        out_shape=[
-            pltpu.VMEM((tokens, KVH * HD), BF16),
-            pltpu.VMEM((tokens, depth), BF16),
-            pltpu.VMEM((depth, KVH * HD), BF16),
-            jax.ShapeDtypeStruct((3 * pages + prompts,), jnp.int32),
-        ],
-        scratch_shapes=[
-            pltpu.VMEM((depth, KVH * HD), BF16),
-            pltpu.VMEM((tokens, HD), F32),
-            pltpu.VMEM((tokens, HD), F32),
-            pltpu.SemaphoreType.DMA((2,)),
-            pltpu.SemaphoreType.DMA((KVH,)),
-            pltpu.SemaphoreType.DMA((KVH,)),
-        ],
-        compiler_params=pltpu.CompilerParams(vmem_limit_bytes=28 * MIB),
+    return pl.pallas_call(
+        keys_kernel,
+        in_specs=[VMEM] * 5 + [pl.BlockSpec(memory_space=pl.ANY)],
+        out_specs=VMEM,
+        out_shape=pltpu.VMEM((tokens, KVH * HD), BF16),
+        compiler_params=pltpu.CompilerParams(vmem_limit_bytes=24 * MIB),
         cost_estimate=pl.CostEstimate(
-            flops=2 * tokens * depth * KVH * HD,
-            bytes_accessed=2 * depth * (tokens + 2 * KVH * HD) + 2 * tokens * KVH * HD,
-            transcendentals=0,
+            flops=tokens * depth * KVH * HD, bytes_accessed=8 * MIB, transcendentals=0
         ),
         name="keys",
-    )(*[in_hbm(a) for a in (x, kv_weight, counts, tails)])
+    )(acc, x, weight, cosine, sine, after)
 
 
 def values_kernel(first, x_ref, w_ref, o_hbm, after, v_ref, o_ref, sem):
@@ -178,11 +204,12 @@
     copy.start()
     tokens, columns = v_ref.shape
     tall = tokens // 2
-    for c in range(0, columns, 2 * HD):
+    pairs_here = columns // (2 * HD)
+    for pair in range(pairs_here):
+        weight = pair_columns(w_ref, slice(None), first * pairs_here + pair, 1)
         for i in range(2):
             at = slice(i * tall, (i + 1) * tall)
-            weight = w_ref[:, first * columns + c : first * columns + c + 2 * HD]
-            v_ref[at, c : c + 2 * HD] = jnp.dot(
+            v_ref[at, 2 * pair * HD : 2 * (pair + 1) * HD] = jnp.dot(
                 x_ref[at], weight, preferred_element_type=F32
             ).astype(BF16)
     copy.wait()
@@ -190,7 +217,7 @@
 
 def project_values(x, weight, out_weight, first, after):
     tokens, depth = x.shape
-    columns = weight.shape[1] // 2
+    columns = KVH // 2 * HD
     rows = out_weight.shape[0] // 2
     return pl.pallas_call(
         functools.partial(values_kernel, first),
@@ -208,9 +235,7 @@
         scratch_shapes=[pltpu.SemaphoreType.DMA],
         compiler_params=pltpu.CompilerParams(vmem_limit_bytes=24 * MIB),
         cost_estimate=pl.CostEstimate(
-            flops=2 * tokens * depth * columns,
-            bytes_accessed=2 * (depth * (tokens + columns) + tokens * columns),
-            transcendentals=0,
+            flops=2 * tokens * depth * columns, bytes_accessed=8 * MIB, transcendentals=0
         ),
         name="values",
     )(x, weight, in_hbm(out_weight), after)
@@ -256,38 +281,25 @@
     )(*pieces, after)
 
 
-def scores_kernel(pages, n_seq, n_tp, *refs):
+def scores_kernel(n_seq, n_tp, *refs):
     new = refs[:n_seq]
-    k_ref, meta = refs[n_seq : n_seq + 2]
-    outs = refs[n_seq + 2 : n_seq + 2 + n_tp]
-    fresh_ref, all_q, held, ready, cosines, sines = refs[n_seq + 2 + n_tp :]
+    k_ref, cos_q, sin_q, meta = refs[n_seq : n_seq + 4]
+    outs = refs[n_seq + 4 : n_seq + 4 + n_tp]
+    own_q, all_q, ready = refs[n_seq + 4 + n_tp :]
     kv_local = KVH // n_tp
     local_pages = k_ref.shape[0] // PAGE
     _, own_rows, new_count, _, _ = new[0].shape
-    prompts = own_rows * n_seq
     rows = new_count * GROUP
-    heads = kv_local * GROUP
+    count = kv_local * rows
     scale = 1.0 / math.sqrt(HD)
     me = lax.axis_index("tp")
     seq = lax.axis_index("seq")
     first = seq * local_pages
-    step = lax.broadcasted_iota(jnp.int32, (kv_local * rows, HD), 0) % rows // GROUP
-    lane = lax.broadcasted_iota(jnp.int32, (kv_local * rows, HD), 1)
-    found = [jnp.full((kv_local * rows, HD), NEG, F32) for _ in range(new_count)]
-    spots = [meta[3 * pages + r] + n for r in range(prompts) for n in range(new_count)]
-    angles = by_row(len(spots), spots) * lane_freqs(len(spots))
-    cosines[...] = jnp.cos(angles)
-    sines[...] = jnp.sin(angles) * sine_sign(len(spots))
     for ds in range(n_seq):
         for rr in range(own_rows):
             request = (seq ^ ds) * own_rows + rr
-            turn = [
-                (
-                    cosines[pl.ds(request * new_count + n, 1)],
-                    sines[pl.ds(request * new_count + n, 1)],
-                )
-                for n in range(new_count)
-            ]
+            spots = [pl.ds(request * new_count + n, 1) for n in range(new_count)]
+            turn = [(cos_q[spot], sin_q[spot]) for spot in spots]
             for dt in range(n_tp):
                 block = [new[ds][dt, rr, n].astype(F32) for n in range(new_count)]
                 for g in range(kv_local):
@@ -299,20 +311,7 @@
                     at = ((me ^ dt) * kv_local + g) * rows
                     all_q[request, pl.ds(pl.multiple_of(at, rows), rows)] = part
                     if dt == 0:
-                        held[g * rows : (g + 1) * rows] = part.astype(F32)
-                if dt == 0:
-                    for n in range(new_count):
-                        spread = []
-                        for g in range(kv_local):
-                            k = block[n][heads + 2 * g : heads + 2 * g + 1]
-                            k = k * turn[n][0] + pltpu.roll(k, HD // 2, 1) * turn[n][1]
-                            k = k.astype(BF16).astype(F32)
-                            spread.append(jnp.broadcast_to(k, (rows, HD)))
-                        k = jnp.concatenate(spread, axis=0)
-                        s = jnp.sum(held[...] * k, axis=1, keepdims=True) * scale
-                        found[n] = jnp.where((lane == request) & (step >= n), s, found[n])
-    for n in range(new_count):
-        fresh_ref[n] = found[n]
+                        own_q[request, g * rows : (g + 1) * rows] = part
     for p in range(local_pages):
         request = meta[first + p]
         tokens = slice(p * PAGE, (p + 1) * PAGE)
@@ -321,35 +320,85 @@
             q = all_q[request, head * rows : (head + 1) * rows]
             s = lax.dot_general(q, k, (((1,), (1,)), ((), ())), preferred_element_type=F32)
             ready[head * rows : (head + 1) * rows, tokens] = (s * scale).astype(BF16)
-    count = kv_local * rows
     for d in range(n_tp):
         outs[d][...] = ready[pl.ds(pl.multiple_of((me ^ d) * count, count), count)]
 
 
-def partial_scores(new, k, meta, pages, prompts, n_tp):
+def partial_scores(new, k, cos_q, sin_q, meta, prompts, n_tp):
     n_seq = len(new)
     new_count = new[0].shape[2]
     tokens = k.shape[0]
     rows = KVH // n_tp * new_count * GROUP
     return pl.pallas_call(
-        functools.partial(scores_kernel, pages, n_seq, n_tp),
-        in_specs=[VMEM] * (n_seq + 1) + [SMEM],
+        functools.partial(scores_kernel, n_seq, n_tp),
+        in_specs=[VMEM] * (n_seq + 3) + [SMEM],
         out_specs=[VMEM] * (n_tp + 1),
         out_shape=[jax.ShapeDtypeStruct((rows, tokens), BF16)] * n_tp
-        + [jax.ShapeDtypeStruct((new_count, rows, HD), F32)],
+        + [jax.ShapeDtypeStruct((prompts, rows, HD), BF16)],
         scratch_shapes=[
             pltpu.VMEM((prompts, rows * n_tp, HD), BF16),
-            pltpu.VMEM((rows, HD), F32),
             pltpu.VMEM((rows * n_tp, tokens), BF16),
-            pltpu.VMEM((prompts * new_count, HD), F32),
-            pltpu.VMEM((prompts * new_count, HD), F32),
         ],
         compiler_params=pltpu.CompilerParams(vmem_limit_bytes=24 * MIB),
         cost_estimate=pl.CostEstimate(
             flops=2 * tokens * rows * n_tp * HD, bytes_accessed=6 * MIB, transcendentals=0
         ),
         name="scores",
-    )(*new, k, meta)
+    )(*new, k, cos_q, sin_q, meta)
+
+
+def fresh_kernel(n_seq, *refs):
+    new = refs[:n_seq]
+    q_ref, cos_q, sin_q, score_ref, value_ref = refs[n_seq:]
+    prompts, rows_local, _ = q_ref.shape
+    _, own_rows, new_count, _, _ = new[0].shape
+    rows = new_count * GROUP
+    kv_local = rows_local // rows
+    heads = kv_local * GROUP
+    scale = 1.0 / math.sqrt(HD)
+    seq = lax.axis_index("seq")
+    step = lax.broadcasted_iota(jnp.int32, (rows_local, HD), 0) % rows // GROUP
+    lane = lax.broadcasted_iota(jnp.int32, (rows_local, HD), 1)
+    found = [jnp.full((rows_local, HD), NEG, F32) for _ in range(new_count)]
+    for ds in range(n_seq):
+        for rr in range(own_rows):
+            request = (seq ^ ds) * own_rows + rr
+            q = q_ref[request].astype(F32)
+            for n in range(new_count):
+                spot = pl.ds(request * new_count + n, 1)
+                cosine, sine = cos_q[spot], sin_q[spot]
+                both = new[ds][0, rr, n].astype(F32)
+                keys, values = [], []
+                for g in range(kv_local):
+                    k = both[heads + 2 * g : heads + 2 * g + 1]
+                    k = k * cosine + pltpu.roll(k, HD // 2, 1) * sine
+                    k = k.astype(BF16).astype(F32)
+                    keys.append(jnp.broadcast_to(k, (rows, HD)))
+                    v = both[heads + 2 * g + 1 : heads + 2 * g + 2]
+                    values.append(jnp.broadcast_to(v, (rows, HD)))
+                s = jnp.sum(q * jnp.concatenate(keys, axis=0), axis=1, keepdims=True) * scale
+                found[n] = jnp.where((lane == request) & (step >= n), s, found[n])
+                value_ref[request * new_count + n] = jnp.concatenate(values, axis=0)
+    for n in range(new_count):
+        score_ref[n] = found[n]
+
+
+def fresh_scores(new, own_q, cos_q, sin_q):
+    n_seq = len(new)
+    new_count = new[0].shape[2]
+    prompts, rows, _ = own_q.shape
+    return pl.pallas_call(
+        functools.partial(fresh_kernel, n_seq),
+        in_specs=[VMEM] * (n_seq + 3),
+        out_specs=[VMEM, VMEM],
+        out_shape=[
+            jax.ShapeDtypeStruct((new_count, rows, HD), F32),
+            jax.ShapeDtypeStruct((prompts * new_count, rows, HD), F32),
+        ],
+        compiler_params=pltpu.CompilerParams(vmem_limit_bytes=16 * MIB),
+        cost_estimate=pl.CostEstimate(flops=0, bytes_accessed=2 * MIB, transcendentals=0),
+        name="fresh",
+    )(*new, own_q, cos_q, sin_q)
 
 
 def weights_kernel(pages, prompts, n_tp, *refs):
@@ -485,17 +534,13 @@
 
 def output_kernel(n_seq, *refs):
     pieces = refs[:n_seq]
-    fresh_ref = refs[n_seq]
-    new = refs[n_seq + 1 : 2 * n_seq + 1]
-    wa_ref, wb_ref, out_ref, held = refs[2 * n_seq + 1 :]
+    fresh_ref, value_ref, wa_ref, wb_ref, out_ref, held = refs[n_seq:]
     more, rows_local, _ = pieces[0].shape
     prompts = more - 1
     new_count = fresh_ref.shape[0]
     rows = new_count * GROUP
     kv_local = rows_local // rows
     heads = kv_local * GROUP
-    own_rows = prompts // n_seq
-    seq = lax.axis_index("seq")
     tops, parts = [], []
     for s in range(n_seq):
         stats = pieces[s][prompts].astype(F32)
@@ -515,33 +560,16 @@
         total = total + f * part
     weights = [w / total for w in weights]
     factors = [f / total for f in factors]
-    lane = lax.broadcasted_iota(jnp.int32, (rows_local, HD), 1)
     for r in range(prompts):
         sums = jnp.zeros((rows_local, HD), F32)
         for s in range(n_seq):
             sums = sums + factors[s][:, r : r + 1] * pieces[s][r].astype(F32)
+        for n in range(new_count):
+            sums = sums + weights[n][:, r : r + 1] * value_ref[r * new_count + n]
         for g in range(kv_local):
             for n in range(new_count):
                 at = g * rows + n * GROUP
                 held[g * GROUP : (g + 1) * GROUP, r * new_count + n] = sums[at : at + GROUP]
-    for ds in range(n_seq):
-        for rr in range(own_rows):
-            request = (seq ^ ds) * own_rows + rr
-            share = [
-                jnp.sum(jnp.where(lane == request, w, 0.0), axis=1, keepdims=True) for w in weights
-            ]
-            sums = jnp.zeros((rows_local, HD), F32)
-            for n in range(new_count):
-                both = new[ds][0, rr, n].astype(F32)
-                value = [both[heads + 2 * g + 1 : heads + 2 * g + 2] for g in range(kv_local)]
-                value = [jnp.broadcast_to(v, (rows, HD)) for v in value]
-                sums = sums + share[n] * jnp.concatenate(value, axis=0)
-            for g in range(kv_local):
-                for n in range(new_count):
-                    at = g * rows + n * GROUP
-                    held[g * GROUP : (g + 1) * GROUP, request * new_count + n] += sums[
-                        at : at + GROUP
-                    ]
     half = heads // 2
     product = jnp.zeros(out_ref.shape, F32)
     for w_ref, at in ((wa_ref, 0), (wb_ref, half)):
@@ -551,20 +579,20 @@
     out_ref[...] = product.astype(BF16)
 
 
-def output_partial(pieces, fresh, new, weights):
+def output_partial(pieces, fresh, values, weights):
     n_seq = len(pieces)
     new_count = fresh.shape[0]
     prompts = pieces[0].shape[0] - 1
     depth, columns = weights[0].shape
     return pl.pallas_call(
         functools.partial(output_kernel, n_seq),
-        in_specs=[VMEM] * (2 * n_seq + 3),
+        in_specs=[VMEM] * (n_seq + 4),
         out_specs=VMEM,
         out_shape=jax.ShapeDtypeStruct((prompts * new_count, columns), BF16),
         scratch_shapes=[pltpu.VMEM((2 * depth // HD, prompts * new_count, HD), F32)],
         compiler_params=pltpu.CompilerParams(vmem_limit_bytes=24 * MIB),
         name="output",
-    )(*pieces, fresh, *new, *weights)
+    )(*pieces, fresh, values, *weights)
 
 
 def final_kernel(n_tp, *refs):
@@ -598,16 +626,20 @@
     prompts = page_counts.shape[0]
     pages = prefill_states.shape[0] // PAGE * n_seq
     new = gather(prepare(new_query, new_keyval), "tp")
-    k, x, w, meta = project_keys(prefill_states, kv_weight, page_counts, tail_tokens, pages)
+    acc, x, w, cosine, sine, cos_q, sin_q, meta = load(
+        prefill_states, kv_weight, page_counts, tail_tokens, pages, new_count
+    )
     new = stacked(new, meta)
-    va, oa = project_values(x, w, out_weight, 0, new)
+    k = rotated_keys(acc, x, w, cosine, sine, new)
     new = gather(new, "seq")
-    *scores, fresh = partial_scores(new, k, meta, pages, prompts, n_tp)
-    vb, ob = project_values(x, w, out_weight, 1, fresh)
+    *scores, own_q = partial_scores(new, k, cos_q, sin_q, meta, prompts, n_tp)
+    va, oa = project_values(x, w, out_weight, 0, own_q)
+    fresh, values = fresh_scores(new, own_q, cos_q, sin_q)
     weights, stats = softmax_weights(exchange(scores, "tp"), meta, pages, prompts)
+    vb, ob = project_values(x, w, out_weight, 1, stats)
     chunks = weighted_values(gather(weights, "tp"), va, vb, meta, prompts)
     pieces = gather(summed(exchange(chunks, "tp"), stats), "seq")
-    partial = output_partial(pieces, fresh, new, (oa, ob))
+    partial = output_partial(pieces, fresh, values, (oa, ob))
     return final_sum(gather(partial, "tp"), residual)
 
 

time: 73.8 us -> 68.8 us (0.932)
  Pallas kernels: 24.2 us -> 22 us
  waiting for transfers between devices: 21.8 us -> 20.1 us
  starting transfers between devices: 27.3 us -> 26.3 us
    pallas_call x2 -> x4, Pallas kernels: 14 us -> 12 us  [the longest x1 6.52 us: load(): pl.pallas_call(functools.partial(load_kernel, pages, prompts, new_count),...]
    ppermute x21, waiting for transfers between devices: 21.8 us -> 20.1 us  [pairs(): lax.ppermute(value, axis, [(i, i ^ d) for i in range(lax.axis_size(axis))])]
    ppermute x21, starting transfers between devices: 27.3 us -> 26.3 us  [pairs(): lax.ppermute(value, axis, [(i, i ^ d) for i in range(lax.axis_size(axis))])]
  transfers between devices with their start and end apart: 21 -> 21, of which waited for: 11 -> 14; matrix products, arithmetic and copies ran while one was open for 0% -> 0% of each run, Pallas kernels for 23% -> 22%
where the time goes in v5:
time: 68.8 us; the launch traced here: 68.5 us
  starting transfers between devices  26.3 us (38%)
  Pallas kernels  22 us (32%)
  waiting for transfers between devices  20.1 us (29%)
    ppermute x21, starting transfers between devices, pairs(): lax.ppermute(value, axis, [(i, i ^ d) for i in range(lax.axis_size(axis))])  26.3 us
    ppermute x21, waiting for transfers between devices, pairs(): lax.ppermute(value, axis, [(i, i ^ d) for i in range(lax.axis_size(axis))])  20.1 us
    pallas_call x1, Pallas kernels, load(): pl.pallas_call(functools.partial(load_kernel, pages, prompts, new_count),...  6.52 us
    pallas_call x2, Pallas kernels, project_values(): pl.pallas_call(functools.partial(values_kernel, first), in_specs=[VMEM, V...  4.75 us
    pallas_call x1, Pallas kernels, rotated_keys(): pl.pallas_call(keys_kernel, in_specs=[VMEM] * 5 + [pl.BlockSpec(memory_sp...  2.74 us
    pallas_call x1, Pallas kernels, partial_scores(): pl.pallas_call(functools.partial(scores_kernel, n_seq, n_tp), in_specs=[V...  1.88 us
    pallas_call x1, Pallas kernels, output_partial(): pl.pallas_call(functools.partial(output_kernel, n_seq), in_specs=[VMEM] *...  1.58 us
  transfers between devices with their start and end apart: 21, of which 14 were waited for; matrix products, arithmetic and copies ran while one was open for 0% of the time, Pallas kernels for 22%

profile of v5, /device:TPU:0, one launch (start us, length us, event | category | flops | bytes accessed | tf_op | source)
XLA Modules:
  0.0 68.5 jit_solution(15878117334784271984)
XLA Ops:
  0.7 3.1 %collective-permute-start = (bf16[2,2,20,128]{3,2,1,0:T(8,128)(2,1)S(1)}, bf16[2,2,20,128]{3,2,1,0:T(8,128)(2,1)S(1)}, u32[]{:S(2)}, u32[]{:S(2)}) collective-permute-start(bf16[2,2,20,128]{3,2,1,0:T(8,128)(2,1)S(1)} %prepare.1.refs_0_), channel_id=1, source_target_pairs={{0,1},{1,0},{2,3},{3,2},{4,5},{5,4},{6,7},{7,6},{8,9},{9,8},{10,11... | collective-permute-start | bytes 61448 | tf_op jit(solution)/shard_map/ppermute | solution.py:26
  3.8 2.6 %collective-permute-start.1 = (bf16[2,2,20,128]{3,2,1,0:T(8,128)(2,1)S(1)}, bf16[2,2,20,128]{3,2,1,0:T(8,128)(2,1)S(1)}, u32[]{:S(2)}, u32[]{:S(2)}) collective-permute-start(bf16[2,2,20,128]{3,2,1,0:T(8,128)(2,1)S(1)} %prepare.1.refs_0_), channel_id=1, source_target_pairs={{0,2},{1,3},{2,0},{3,1},{4,6},{5,7},{6,4},{7,5},{8,10},{9,11},{10,... | collective-permute-start | bytes 61448 | tf_op jit(solution)/shard_map/ppermute | solution.py:26
  6.4 6.5 %load.1 = (f32[1024,1024]{1,0:T(8,128)S(1)}, bf16[1024,2048]{1,0:T(8,128)(2,1)S(1)}, bf16[2048,2048]{1,0:T(8,128)(2,1)S(1)}, f32[1024,128]{1,0:T(8,128)S(1)}, f3...) custom-call(bf16[1024,2048]{1,0:T(8,128)(2,1)} %x_hbm.1, ...), custom_call_target="tpu_custom_call" | custom-call | flops 2147483648 | bytes 12582912 | tf_op jit(solution)/shard_map/load/pallas_call | solution.py:142
  13.1 1.8 %collective-permute-start.4 = (bf16[4,2,2,20,128]{4,3,2,1,0:T(8,128)(2,1)S(1)}, bf16[4,2,2,20,128]{4,3,2,1,0:T(8,128)(2,1)S(1)}, u32[]{:S(2)}, u32[]{:S(2)}) collective-permute-start(bf16[4,2,2,20,128]{4,3,2,1,0:T(8,128)(2,1)S(1)} %stacked.1.after.refs_0_), channel_id=1, source_target_pairs={{0,8},{4,12},{8,0},{12,4},{1,9},{5,13},{9,1},{13,5},{2,10},{6,14},... | collective-permute-start | bytes 245768 | tf_op jit(solution)/shard_map/ppermute | solution.py:26
  15.0 2.7 %keys.1.refs_4_ = bf16[1024,1024]{1,0:T(8,128)(2,1)S(1)} custom-call(f32[1024,1024]{1,0:T(8,128)S(1)} %get-tuple-element.31.acc, bf16[1024,2048]{1,0:T(8,128)(2,1)S(1)} %get-tuple-element.32.x_ref, bf16[2048,2048]{1,0:T(8,128)(2,1)S(1)} %get-tuple-element.33.w_ref, f32[1024,128]{1,0:T(8,128)S(1)} %get-tuple-element.34.cos_ref, ...), custom_call_target="tpu_custom_call" | custom-call | flops 2147483648 | bytes 8388608 | tf_op jit(solution)/shard_map/keys/pallas_call | solution.py:188
  17.7 1.0 %collective-permute-done.4.refs_2_ = bf16[4,2,2,20,128]{4,3,2,1,0:T(8,128)(2,1)S(1)} collective-permute-done((bf16[4,2,2,20,128]{4,3,2,1,0:T(8,128)(2,1)S(1)}, bf16[4,2,2,20,128]{4,3,2,1,0:T(8,128)(2,1)S(1)}, u32[]{:S(2)}, u32[]{:S(2)}) %collective-permute-start.4) | collective-permute-done | bytes 81952 | tf_op jit(solution)/shard_map/ppermute | solution.py:26
  18.7 1.3 %collective-permute-done.5.refs_3_ = bf16[4,2,2,20,128]{4,3,2,1,0:T(8,128)(2,1)S(1)} collective-permute-done((bf16[4,2,2,20,128]{4,3,2,1,0:T(8,128)(2,1)S(1)}, bf16[4,2,2,20,128]{4,3,2,1,0:T(8,128)(2,1)S(1)}, u32[]{:S(2)}, u32[]{:S(2)}) %collective-permute-start.5) | collective-permute-done | bytes 81952 | tf_op jit(solution)/shard_map/ppermute | solution.py:26
  20.0 1.9 %scores.1 = (bf16[32,1024]{1,0:T(8,128)(2,1)S(1)}, bf16[32,1024]{1,0:T(8,128)(2,1)S(1)}, bf16[32,1024]{1,0:T(8,128)(2,1)S(1)}, bf16[32,1024]{1,0:T(8,128)(2,1)S(1)}, bf16[8,32,128]{2,1,0:T(8,128)(2,1)S(1)}) custom-call(bf16[4,2,2,20,128]{4,3,2,1,0:T(8,128)(2,1)S(1)} %stacked.1.after.refs_0_, bf16[4,2,2,20,128]{4,3,2,1,0:T(8,128)(2,1)S(1)} %collective-permute-done.3.refs_1_, ...), custom_call_target="tpu_custom_call" | custom-call | flops 33554432 | bytes 6291456 | tf_op jit(solution)/shard_map/scores/pallas_call | solution.py:332
  21.9 0.9 %collective-permute-start.6 = (bf16[32,1024]{1,0:T(8,128)(2,1)S(1)}, bf16[32,1024]{1,0:T(8,128)(2,1)S(1)}, u32[]{:S(2)}, u32[]{:S(2)}) collective-permute-start(bf16[32,1024]{1,0:T(8,128)(2,1)S(1)} %get-tuple-element.39), channel_id=1, source_target_pairs={{0,1},{1,0},{2,3},{3,2},{4,5},{5,4},{6,7},{7,6},{8,9},{9,8},{10,11... | collective-permute-start | bytes 196616 | tf_op jit(solution)/shard_map/ppermute | solution.py:26
  22.8 3.5 %collective-permute-start.7 = (bf16[32,1024]{1,0:T(8,128)(2,1)S(1)}, bf16[32,1024]{1,0:T(8,128)(2,1)S(1)}, u32[]{:S(2)}, u32[]{:S(2)}) collective-permute-start(bf16[32,1024]{1,0:T(8,128)(2,1)S(1)} %get-tuple-element.40), channel_id=1, source_target_pairs={{0,2},{1,3},{2,0},{3,1},{4,6},{5,7},{6,4},{7,5},{8,10},{9,11},{10,... | collective-permute-start | bytes 196616 | tf_op jit(solution)/shard_map/ppermute | solution.py:26
  26.3 2.4 %values.2 = (bf16[1024,512]{1,0:T(8,128)(2,1)S(1)}, bf16[1024,2048]{1,0:T(8,128)(2,1)S(1)}) custom-call(bf16[1024,2048]{1,0:T(8,128)(2,1)S(1)} %get-tuple-element.32.x_ref, bf16[2048,2048]{1,0:T(8,128)(2,1)S(1)} %get-tuple-element.33.w_ref, bf16[2048,2048]{1,0:T(8,128)(2,1)} %o_hbm.3, bf16[8,32,128]{2,1,0:T(8,128)(2,1)S(1)} %get-tuple-element.43.after.refs_4_), custom_call_target="tpu_custom_call" | custom-call | flops 2147483648 | bytes 8388608 | tf_op jit(solution)/shard_map/values/pallas_call | solution.py:222
  28.7 1.6 %collective-permute-done.7.refs_2_ = bf16[32,1024]{1,0:T(8,128)(2,1)S(1)} collective-permute-done((bf16[32,1024]{1,0:T(8,128)(2,1)S(1)}, bf16[32,1024]{1,0:T(8,128)(2,1)S(1)}, u32[]{:S(2)}, u32[]{:S(2)}) %collective-permute-start.7) | collective-permute-done | bytes 65568 | tf_op jit(solution)/shard_map/ppermute | solution.py:26
  30.3 2.1 %collective-permute-done.8.refs_3_ = bf16[32,1024]{1,0:T(8,128)(2,1)S(1)} collective-permute-done((bf16[32,1024]{1,0:T(8,128)(2,1)S(1)}, bf16[32,1024]{1,0:T(8,128)(2,1)S(1)}, u32[]{:S(2)}, u32[]{:S(2)}) %collective-permute-start.8) | collective-permute-done | bytes 65568 | tf_op jit(solution)/shard_map/ppermute | solution.py:26
  32.5 0.9 %weights.1 = (bf16[32,1024]{1,0:T(8,128)(2,1)S(1)}, bf16[32,128]{1,0:T(8,128)(2,1)S(1)}) custom-call(bf16[32,1024]{1,0:T(8,128)(2,1)S(1)} %get-tuple-element.38.refs_0_, bf16[32,1024]{1,0:T(8,128)(2,1)S(1)} %collective-permute-done.6.refs_1_, bf16[32,1024]{1,0:T(8,128)(2,1)S(1)} %collective-permute-done.7.refs_2_, ...), custom_call_target="tpu_custom_call" | custom-call | tf_op jit(solution)/shard_map/weights/pallas_call | solution.py:449
  33.4 1.8 %collective-permute-start.10 = (bf16[32,1024]{1,0:T(8,128)(2,1)S(1)}, bf16[32,1024]{1,0:T(8,128)(2,1)S(1)}, u32[]{:S(2)}, u32[]{:S(2)}) collective-permute-start(bf16[32,1024]{1,0:T(8,128)(2,1)S(1)} %get-tuple-element.42.refs_0_), channel_id=1, source_target_pairs={{0,2},{1,3},{2,0},{3,1},{4,6},{5,7},{6,4},{7,5},{8,10},{9,11},{10,... | collective-permute-start | bytes 196616 | tf_op jit(solution)/shard_map/ppermute | solution.py:26
  35.2 1.4 %collective-permute-start.11 = (bf16[32,1024]{1,0:T(8,128)(2,1)S(1)}, bf16[32,1024]{1,0:T(8,128)(2,1)S(1)}, u32[]{:S(2)}, u32[]{:S(2)}) collective-permute-start(bf16[32,1024]{1,0:T(8,128)(2,1)S(1)} %get-tuple-element.42.refs_0_), channel_id=1, source_target_pairs={{0,3},{1,2},{2,1},{3,0},{4,7},{5,6},{6,5},{7,4},{8,11},{9,10},{10,... | collective-permute-start | bytes 196616 | tf_op jit(solution)/shard_map/ppermute | solution.py:26
  36.9 2.4 %values.3 = (bf16[1024,512]{1,0:T(8,128)(2,1)S(1)}, bf16[1024,2048]{1,0:T(8,128)(2,1)S(1)}) custom-call(bf16[1024,2048]{1,0:T(8,128)(2,1)S(1)} %get-tuple-element.32.x_ref, bf16[2048,2048]{1,0:T(8,128)(2,1)S(1)} %get-tuple-element.33.w_ref, bf16[2048,2048]{1,0:T(8,128)(2,1)} %o_hbm.3, bf16[32,128]{1,0:T(8,128)(2,1)S(1)} %get-tuple-element.45.after.refs_4_), custom_call_target="tpu_custom_call" | custom-call | flops 2147483648 | bytes 8388608 | tf_op jit(solution)/shard_map/values/pallas_call | solution.py:222
  40.0 1.5 %collective-permute-done.11.refs_3_ = bf16[32,1024]{1,0:T(8,128)(2,1)S(1)} collective-permute-done((bf16[32,1024]{1,0:T(8,128)(2,1)S(1)}, bf16[32,1024]{1,0:T(8,128)(2,1)S(1)}, u32[]{:S(2)}, u32[]{:S(2)}) %collective-permute-start.11) | collective-permute-done | bytes 65568 | tf_op jit(solution)/shard_map/ppermute | solution.py:26
  41.6 1.3 %weighted.1 = (bf16[8,32,128]{2,1,0:T(8,128)(2,1)S(1)}, bf16[8,32,128]{2,1,0:T(8,128)(2,1)S(1)}, bf16[8,32,128]{2,1,0:T(8,128)(2,1)S(1)}, bf16[8,32,128]{2,1,0:T(8,128)(2,1)S(1)}) custom-call(bf16[32,1024]{1,0:T(8,128)(2,1)S(1)} %get-tuple-element.42.refs_0_, bf16[32,1024]{1,0:T(8,128)(2,1)S(1)} %collective-permute-done.9.refs_1_, ...), custom_call_target="tpu_custom_call" | custom-call | flops 33554432 | bytes 8388608 | tf_op jit(solution)/shard_map/weighted/pallas_call | solution.py:493
  42.9 2.4 %collective-permute-start.13 = (bf16[8,32,128]{2,1,0:T(8,128)(2,1)S(1)}, bf16[8,32,128]{2,1,0:T(8,128)(2,1)S(1)}, u32[]{:S(2)}, u32[]{:S(2)}) collective-permute-start(bf16[8,32,128]{2,1,0:T(8,128)(2,1)S(1)} %get-tuple-element.49), channel_id=1, source_target_pairs={{0,2},{1,3},{2,0},{3,1},{4,6},{5,7},{6,4},{7,5},{8,10},{9,11},{10,... | collective-permute-start | bytes 196616 | tf_op jit(solution)/shard_map/ppermute | solution.py:26
  45.3 2.0 %collective-permute-start.14 = (bf16[8,32,128]{2,1,0:T(8,128)(2,1)S(1)}, bf16[8,32,128]{2,1,0:T(8,128)(2,1)S(1)}, u32[]{:S(2)}, u32[]{:S(2)}) collective-permute-start(bf16[8,32,128]{2,1,0:T(8,128)(2,1)S(1)} %get-tuple-element.50), channel_id=1, source_target_pairs={{0,3},{1,2},{2,1},{3,0},{4,7},{5,6},{6,5},{7,4},{8,11},{9,10},{10,... | collective-permute-start | bytes 196616 | tf_op jit(solution)/shard_map/ppermute | solution.py:26
  47.3 2.3 %collective-permute-done.13.refs_2_ = bf16[8,32,128]{2,1,0:T(8,128)(2,1)S(1)} collective-permute-done((bf16[8,32,128]{2,1,0:T(8,128)(2,1)S(1)}, bf16[8,32,128]{2,1,0:T(8,128)(2,1)S(1)}, u32[]{:S(2)}, u32[]{:S(2)}) %collective-permute-start.13) | collective-permute-done | bytes 65568 | tf_op jit(solution)/shard_map/ppermute | solution.py:26
  49.6 1.8 %collective-permute-done.14.refs_3_ = bf16[8,32,128]{2,1,0:T(8,128)(2,1)S(1)} collective-permute-done((bf16[8,32,128]{2,1,0:T(8,128)(2,1)S(1)}, bf16[8,32,128]{2,1,0:T(8,128)(2,1)S(1)}, u32[]{:S(2)}, u32[]{:S(2)}) %collective-permute-start.14) | collective-permute-done | bytes 65568 | tf_op jit(solution)/shard_map/ppermute | solution.py:26
  51.5 1.6 %collective-permute-start.16 = (bf16[9,32,128]{2,1,0:T(8,128)(2,1)S(1)}, bf16[9,32,128]{2,1,0:T(8,128)(2,1)S(1)}, u32[]{:S(2)}, u32[]{:S(2)}) collective-permute-start(bf16[9,32,128]{2,1,0:T(8,128)(2,1)S(1)} %summed.1.refs_0_), channel_id=1, source_target_pairs={{0,8},{4,12},{8,0},{12,4},{1,9},{5,13},{9,1},{13,5},{2,10},{6,14},... | collective-permute-start | bytes 221192 | tf_op jit(solution)/shard_map/ppermute | solution.py:26
  53.4 0.8 %fresh.1 = (f32[2,32,128]{2,1,0:T(8,128)S(1)}, f32[16,32,128]{2,1,0:T(8,128)S(1)}) custom-call(bf16[4,2,2,20,128]{4,3,2,1,0:T(8,128)(2,1)S(1)} %stacked.1.after.refs_0_, bf16[4,2,2,20,128]{4,3,2,1,0:T(8,128)(2,1)S(1)} %collective-permute-done.3.refs_1_, bf16[4,2,2,20,128]{4,3,2,1,0:T(8,128)(2,1)S(1)} %collective-permute-done.4.refs_2_, ...), custom_call_target="tpu_custom_call" | custom-call | bytes 2097152 | tf_op jit(solution)/shard_map/fresh/pallas_call | solution.py:390
  54.2 2.1 %collective-permute-done.16.refs_2_ = bf16[9,32,128]{2,1,0:T(8,128)(2,1)S(1)} collective-permute-done((bf16[9,32,128]{2,1,0:T(8,128)(2,1)S(1)}, bf16[9,32,128]{2,1,0:T(8,128)(2,1)S(1)}, u32[]{:S(2)}, u32[]{:S(2)}) %collective-permute-start.16) | collective-permute-done | bytes 73760 | tf_op jit(solution)/shard_map/ppermute | solution.py:26
  56.3 1.2 %collective-permute-done.17.refs_3_ = bf16[9,32,128]{2,1,0:T(8,128)(2,1)S(1)} collective-permute-done((bf16[9,32,128]{2,1,0:T(8,128)(2,1)S(1)}, bf16[9,32,128]{2,1,0:T(8,128)(2,1)S(1)}, u32[]{:S(2)}, u32[]{:S(2)}) %collective-permute-start.17) | collective-permute-done | bytes 73760 | tf_op jit(solution)/shard_map/ppermute | solution.py:26
  57.5 1.6 %output.1.refs_0_ = bf16[16,2048]{1,0:T(8,128)(2,1)S(1)} custom-call(bf16[9,32,128]{2,1,0:T(8,128)(2,1)S(1)} %summed.1.refs_0_, bf16[9,32,128]{2,1,0:T(8,128)(2,1)S(1)} %collective-permute-done.15.refs_1_, bf16[9,32,128]{2,1,0:T(8,128)(2,1)S(1)} %collective-permute-done.16.refs_2_, bf16[9,32,128]{2,1,0:T(8,128)(2,1)S(1)} %collective-permute-done.17.refs_3_, ...), custom_call_target="tpu_custom_call" | custom-call | tf_op jit(solution)/shard_map/output/pallas_call | solution.py:587
  59.1 2.5 %collective-permute-start.19 = (bf16[16,2048]{1,0:T(8,128)(2,1)S(1)}, bf16[16,2048]{1,0:T(8,128)(2,1)S(1)}, u32[]{:S(2)}, u32[]{:S(2)}) collective-permute-start(bf16[16,2048]{1,0:T(8,128)(2,1)S(1)} %output.1.refs_0_), channel_id=1, source_target_pairs={{0,2},{1,3},{2,0},{3,1},{4,6},{5,7},{6,4},{7,5},{8,10},{9,11},{10,... | collective-permute-start | bytes 196616 | tf_op jit(solution)/shard_map/ppermute | solution.py:26
  61.7 1.9 %collective-permute-start.20 = (bf16[16,2048]{1,0:T(8,128)(2,1)S(1)}, bf16[16,2048]{1,0:T(8,128)(2,1)S(1)}, u32[]{:S(2)}, u32[]{:S(2)}) collective-permute-start(bf16[16,2048]{1,0:T(8,128)(2,1)S(1)} %output.1.refs_0_), channel_id=1, source_target_pairs={{0,3},{1,2},{2,1},{3,0},{4,7},{5,6},{6,5},{7,4},{8,11},{9,10},{10,... | collective-permute-start | bytes 196616 | tf_op jit(solution)/shard_map/ppermute | solution.py:26
  63.5 0.8 %collective-permute-done.18.refs_1_ = bf16[16,2048]{1,0:T(8,128)(2,1)S(1)} collective-permute-done((bf16[16,2048]{1,0:T(8,128)(2,1)S(1)}, bf16[16,2048]{1,0:T(8,128)(2,1)S(1)}, u32[]{:S(2)}, u32[]{:S(2)}) %collective-permute-start.18) | collective-permute-done | bytes 65568 | tf_op jit(solution)/shard_map/ppermute | solution.py:26
  64.3 2.8 %collective-permute-done.19.refs_2_ = bf16[16,2048]{1,0:T(8,128)(2,1)S(1)} collective-permute-done((bf16[16,2048]{1,0:T(8,128)(2,1)S(1)}, bf16[16,2048]{1,0:T(8,128)(2,1)S(1)}, u32[]{:S(2)}, u32[]{:S(2)}) %collective-permute-start.19) | collective-permute-done | bytes 65568 | tf_op jit(solution)/shard_map/ppermute | solution.py:26
  (25 shorter events, 4.0 us)
Async XLA Ops:
  0.7 12.2 %collective-permute-start = (bf16[2,2,20,128]{3,2,1,0:T(8,128)(2,1)S(1)}, bf16[2,2,20,128]{3,2,1,0:T(8,128)(2,1)S(1)}, u32[]{:S(2)}, u32[]{:S(2)}) collective-permute-start(bf16[2,2,20,128]{3,2,1,0:T(8,128)(2,1)S(1)} %prepare.1.refs_0_), channel_id=1, source_target_pairs={{0,1},{1,0},{2,3},{3,2},{4,5},{5,4},{6,7},{7,6},{8,9},{9,8},{10,11... | collective-permute-start | bytes 61448 | tf_op jit(solution)/shard_map/ppermute | solution.py:26
  3.8 9.1 %collective-permute-start.1 = (bf16[2,2,20,128]{3,2,1,0:T(8,128)(2,1)S(1)}, bf16[2,2,20,128]{3,2,1,0:T(8,128)(2,1)S(1)}, u32[]{:S(2)}, u32[]{:S(2)}) collective-permute-start(bf16[2,2,20,128]{3,2,1,0:T(8,128)(2,1)S(1)} %prepare.1.refs_0_), channel_id=1, source_target_pairs={{0,2},{1,3},{2,0},{3,1},{4,6},{5,7},{6,4},{7,5},{8,10},{9,11},{10,... | collective-permute-start | bytes 61448 | tf_op jit(solution)/shard_map/ppermute | solution.py:26
  6.4 6.6 %collective-permute-start.2 = (bf16[2,2,20,128]{3,2,1,0:T(8,128)(2,1)S(1)}, bf16[2,2,20,128]{3,2,1,0:T(8,128)(2,1)S(1)}, u32[]{:S(2)}, u32[]{:S(2)}) collective-permute-start(bf16[2,2,20,128]{3,2,1,0:T(8,128)(2,1)S(1)} %prepare.1.refs_0_), channel_id=1, source_target_pairs={{0,3},{1,2},{2,1},{3,0},{4,7},{5,6},{6,5},{7,4},{8,11},{9,10},{10,... | collective-permute-start | bytes 61448 | tf_op jit(solution)/shard_map/ppermute | solution.py:26
  13.0 4.7 %collective-permute-start.3 = (bf16[4,2,2,20,128]{4,3,2,1,0:T(8,128)(2,1)S(1)}, bf16[4,2,2,20,128]{4,3,2,1,0:T(8,128)(2,1)S(1)}, u32[]{:S(2)}, u32[]{:S(2)}) collective-permute-start(bf16[4,2,2,20,128]{4,3,2,1,0:T(8,128)(2,1)S(1)} %stacked.1.after.refs_0_), channel_id=1, source_target_pairs={{0,4},{4,0},{8,12},{12,8},{1,5},{5,1},{9,13},{13,9},{2,6},{6,2},{1... | collective-permute-start | bytes 245768 | tf_op jit(solution)/shard_map/ppermute | solution.py:26
  13.1 5.6 %collective-permute-start.4 = (bf16[4,2,2,20,128]{4,3,2,1,0:T(8,128)(2,1)S(1)}, bf16[4,2,2,20,128]{4,3,2,1,0:T(8,128)(2,1)S(1)}, u32[]{:S(2)}, u32[]{:S(2)}) collective-permute-start(bf16[4,2,2,20,128]{4,3,2,1,0:T(8,128)(2,1)S(1)} %stacked.1.after.refs_0_), channel_id=1, source_target_pairs={{0,8},{4,12},{8,0},{12,4},{1,9},{5,13},{9,1},{13,5},{2,10},{6,14},... | collective-permute-start | bytes 245768 | tf_op jit(solution)/shard_map/ppermute | solution.py:26
  14.9 5.1 %collective-permute-start.5 = (bf16[4,2,2,20,128]{4,3,2,1,0:T(8,128)(2,1)S(1)}, bf16[4,2,2,20,128]{4,3,2,1,0:T(8,128)(2,1)S(1)}, u32[]{:S(2)}, u32[]{:S(2)}) collective-permute-start(bf16[4,2,2,20,128]{4,3,2,1,0:T(8,128)(2,1)S(1)} %stacked.1.after.refs_0_), channel_id=1, source_target_pairs={{0,12},{4,8},{8,4},{12,0},{1,13},{5,9},{9,5},{13,1},{2,14},{6,10},... | collective-permute-start | bytes 245768 | tf_op jit(solution)/shard_map/ppermute | solution.py:26
  21.9 6.8 %collective-permute-start.6 = (bf16[32,1024]{1,0:T(8,128)(2,1)S(1)}, bf16[32,1024]{1,0:T(8,128)(2,1)S(1)}, u32[]{:S(2)}, u32[]{:S(2)}) collective-permute-start(bf16[32,1024]{1,0:T(8,128)(2,1)S(1)} %get-tuple-element.39), channel_id=1, source_target_pairs={{0,1},{1,0},{2,3},{3,2},{4,5},{5,4},{6,7},{7,6},{8,9},{9,8},{10,11... | collective-permute-start | bytes 196616 | tf_op jit(solution)/shard_map/ppermute | solution.py:26
  22.8 7.5 %collective-permute-start.7 = (bf16[32,1024]{1,0:T(8,128)(2,1)S(1)}, bf16[32,1024]{1,0:T(8,128)(2,1)S(1)}, u32[]{:S(2)}, u32[]{:S(2)}) collective-permute-start(bf16[32,1024]{1,0:T(8,128)(2,1)S(1)} %get-tuple-element.40), channel_id=1, source_target_pairs={{0,2},{1,3},{2,0},{3,1},{4,6},{5,7},{6,4},{7,5},{8,10},{9,11},{10,... | collective-permute-start | bytes 196616 | tf_op jit(solution)/shard_map/ppermute | solution.py:26
  26.3 6.2 %collective-permute-start.8 = (bf16[32,1024]{1,0:T(8,128)(2,1)S(1)}, bf16[32,1024]{1,0:T(8,128)(2,1)S(1)}, u32[]{:S(2)}, u32[]{:S(2)}) collective-permute-start(bf16[32,1024]{1,0:T(8,128)(2,1)S(1)} %get-tuple-element.41), channel_id=1, source_target_pairs={{0,3},{1,2},{2,1},{3,0},{4,7},{5,6},{6,5},{7,4},{8,11},{9,10},{10,... | collective-permute-start | bytes 196616 | tf_op jit(solution)/shard_map/ppermute | solution.py:26
  33.4 6.6 %collective-permute-start.10 = (bf16[32,1024]{1,0:T(8,128)(2,1)S(1)}, bf16[32,1024]{1,0:T(8,128)(2,1)S(1)}, u32[]{:S(2)}, u32[]{:S(2)}) collective-permute-start(bf16[32,1024]{1,0:T(8,128)(2,1)S(1)} %get-tuple-element.42.refs_0_), channel_id=1, source_target_pairs={{0,2},{1,3},{2,0},{3,1},{4,6},{5,7},{6,4},{7,5},{8,10},{9,11},{10,... | collective-permute-start | bytes 196616 | tf_op jit(solution)/shard_map/ppermute | solution.py:26
  35.2 6.2 %collective-permute-start.11 = (bf16[32,1024]{1,0:T(8,128)(2,1)S(1)}, bf16[32,1024]{1,0:T(8,128)(2,1)S(1)}, u32[]{:S(2)}, u32[]{:S(2)}) collective-permute-start(bf16[32,1024]{1,0:T(8,128)(2,1)S(1)} %get-tuple-element.42.refs_0_), channel_id=1, source_target_pairs={{0,3},{1,2},{2,1},{3,0},{4,7},{5,6},{6,5},{7,4},{8,11},{9,10},{10,... | collective-permute-start | bytes 196616 | tf_op jit(solution)/shard_map/ppermute | solution.py:26
  36.6 5.0 %collective-permute-start.9 = (bf16[32,1024]{1,0:T(8,128)(2,1)S(1)}, bf16[32,1024]{1,0:T(8,128)(2,1)S(1)}, u32[]{:S(2)}, u32[]{:S(2)}) collective-permute-start(bf16[32,1024]{1,0:T(8,128)(2,1)S(1)} %get-tuple-element.42.refs_0_), channel_id=1, source_target_pairs={{0,1},{1,0},{2,3},{3,2},{4,5},{5,4},{6,7},{7,6},{8,9},{9,8},{10,11... | collective-permute-start | bytes 196616 | tf_op jit(solution)/shard_map/ppermute | solution.py:26
  42.8 4.5 %collective-permute-start.12 = (bf16[8,32,128]{2,1,0:T(8,128)(2,1)S(1)}, bf16[8,32,128]{2,1,0:T(8,128)(2,1)S(1)}, u32[]{:S(2)}, u32[]{:S(2)}) collective-permute-start(bf16[8,32,128]{2,1,0:T(8,128)(2,1)S(1)} %get-tuple-element.48), channel_id=1, source_target_pairs={{0,1},{1,0},{2,3},{3,2},{4,5},{5,4},{6,7},{7,6},{8,9},{9,8},{10,11... | collective-permute-start | bytes 196616 | tf_op jit(solution)/shard_map/ppermute | solution.py:26
  42.9 6.6 %collective-permute-start.13 = (bf16[8,32,128]{2,1,0:T(8,128)(2,1)S(1)}, bf16[8,32,128]{2,1,0:T(8,128)(2,1)S(1)}, u32[]{:S(2)}, u32[]{:S(2)}) collective-permute-start(bf16[8,32,128]{2,1,0:T(8,128)(2,1)S(1)} %get-tuple-element.49), channel_id=1, source_target_pairs={{0,2},{1,3},{2,0},{3,1},{4,6},{5,7},{6,4},{7,5},{8,10},{9,11},{10,... | collective-permute-start | bytes 196616 | tf_op jit(solution)/shard_map/ppermute | solution.py:26
  45.3 6.1 %collective-permute-start.14 = (bf16[8,32,128]{2,1,0:T(8,128)(2,1)S(1)}, bf16[8,32,128]{2,1,0:T(8,128)(2,1)S(1)}, u32[]{:S(2)}, u32[]{:S(2)}) collective-permute-start(bf16[8,32,128]{2,1,0:T(8,128)(2,1)S(1)} %get-tuple-element.50), channel_id=1, source_target_pairs={{0,3},{1,2},{2,1},{3,0},{4,7},{5,6},{6,5},{7,4},{8,11},{9,10},{10,... | collective-permute-start | bytes 196616 | tf_op jit(solution)/shard_map/ppermute | solution.py:26
  51.4 2.8 %collective-permute-start.15 = (bf16[9,32,128]{2,1,0:T(8,128)(2,1)S(1)}, bf16[9,32,128]{2,1,0:T(8,128)(2,1)S(1)}, u32[]{:S(2)}, u32[]{:S(2)}) collective-permute-start(bf16[9,32,128]{2,1,0:T(8,128)(2,1)S(1)} %summed.1.refs_0_), channel_id=1, source_target_pairs={{0,4},{4,0},{8,12},{12,8},{1,5},{5,1},{9,13},{13,9},{2,6},{6,2},{1... | collective-permute-start | bytes 221192 | tf_op jit(solution)/shard_map/ppermute | solution.py:26
  51.5 4.8 %collective-permute-start.16 = (bf16[9,32,128]{2,1,0:T(8,128)(2,1)S(1)}, bf16[9,32,128]{2,1,0:T(8,128)(2,1)S(1)}, u32[]{:S(2)}, u32[]{:S(2)}) collective-permute-start(bf16[9,32,128]{2,1,0:T(8,128)(2,1)S(1)} %summed.1.refs_0_), channel_id=1, source_target_pairs={{0,8},{4,12},{8,0},{12,4},{1,9},{5,13},{9,1},{13,5},{2,10},{6,14},... | collective-permute-start | bytes 221192 | tf_op jit(solution)/shard_map/ppermute | solution.py:26
  53.1 4.4 %collective-permute-start.17 = (bf16[9,32,128]{2,1,0:T(8,128)(2,1)S(1)}, bf16[9,32,128]{2,1,0:T(8,128)(2,1)S(1)}, u32[]{:S(2)}, u32[]{:S(2)}) collective-permute-start(bf16[9,32,128]{2,1,0:T(8,128)(2,1)S(1)} %summed.1.refs_0_), channel_id=1, source_target_pairs={{0,12},{4,8},{8,4},{12,0},{1,13},{5,9},{9,5},{13,1},{2,14},{6,10},... | collective-permute-start | bytes 221192 | tf_op jit(solution)/shard_map/ppermute | solution.py:26
  57.5 10.3 %copy-start = (bf16[8,2,2048]{2,1,0:T(2,128)(2,1)S(1)}, bf16[8,2,2048]{2,1,0:T(2,128)(2,1)}, u32[]{:S(2)}) copy-start(bf16[8,2,2048]{2,1,0:T(2,128)(2,1)} %refs_4_.1) | copy-start | bytes 196612
  59.1 5.2 %collective-permute-start.18 = (bf16[16,2048]{1,0:T(8,128)(2,1)S(1)}, bf16[16,2048]{1,0:T(8,128)(2,1)S(1)}, u32[]{:S(2)}, u32[]{:S(2)}) collective-permute-start(bf16[16,2048]{1,0:T(8,128)(2,1)S(1)} %output.1.refs_0_), channel_id=1, source_target_pairs={{0,1},{1,0},{2,3},{3,2},{4,5},{5,4},{6,7},{7,6},{8,9},{9,8},{10,11... | collective-permute-start | bytes 196616 | tf_op jit(solution)/shard_map/ppermute | solution.py:26
  59.1 8.0 %collective-permute-start.19 = (bf16[16,2048]{1,0:T(8,128)(2,1)S(1)}, bf16[16,2048]{1,0:T(8,128)(2,1)S(1)}, u32[]{:S(2)}, u32[]{:S(2)}) collective-permute-start(bf16[16,2048]{1,0:T(8,128)(2,1)S(1)} %output.1.refs_0_), channel_id=1, source_target_pairs={{0,2},{1,3},{2,0},{3,1},{4,6},{5,7},{6,4},{7,5},{8,10},{9,11},{10,... | collective-permute-start | bytes 196616 | tf_op jit(solution)/shard_map/ppermute | solution.py:26
  61.7 6.2 %collective-permute-start.20 = (bf16[16,2048]{1,0:T(8,128)(2,1)S(1)}, bf16[16,2048]{1,0:T(8,128)(2,1)S(1)}, u32[]{:S(2)}, u32[]{:S(2)}) collective-permute-start(bf16[16,2048]{1,0:T(8,128)(2,1)S(1)} %output.1.refs_0_), channel_id=1, source_target_pairs={{0,3},{1,2},{2,1},{3,0},{4,7},{5,6},{6,5},{7,4},{8,11},{9,10},{10,... | collective-permute-start | bytes 196616 | tf_op jit(solution)/shard_map/ppermute | solution.py:26

commit v6 on v5

--- a/solution.py
+++ b/solution.py
@@ -26,14 +26,36 @@
     return lax.ppermute(value, axis, [(i, i ^ d) for i in range(lax.axis_size(axis))])
 
 
-def exchange(chunks, axis):
-    got = {d: pairs(chunks[d], axis, d) for d in reversed(range(1, len(chunks)))}
-    return [chunks[0]] + [got[d] for d in range(1, len(chunks))]
+def repeat_kernel(in_ref, out_ref):
+    out_ref[...] = in_ref[...]
+
+
+def repeated(value):
+    return pl.pallas_call(
+        repeat_kernel,
+        in_specs=[VMEM],
+        out_specs=VMEM,
+        out_shape=jax.ShapeDtypeStruct(value.shape, value.dtype),
+        compiler_params=pltpu.CompilerParams(vmem_limit_bytes=8 * MIB),
+        name="repeat",
+    )(value)
+
+
+def far_first(size):
+    return list(range(size // 2, size)) + list(range(1, size // 2))
 
 
 def gather(value, axis):
     size = lax.axis_size(axis)
-    return [value] + [pairs(value, axis, d) for d in range(1, size)]
+    got = {0: value}
+    near = repeated(value)
+    for d in far_first(size):
+        got[d] = pairs(value if d >= size // 2 else near, axis, d)
+    return [got[d] for d in range(size)]
+
+
+def own_copy(value, axis):
+    return pairs(value, axis, 0)
 
 
 def lane_freqs(rows):
@@ -48,6 +70,10 @@
 
 def in_hbm(value):
     return pltpu.with_memory_space_constraint(value, pltpu.HBM)
+
+
+def in_vmem(value):
+    return pltpu.with_memory_space_constraint(value, pltpu.VMEM)
 
 
 def by_row(rows, numbers):
@@ -102,100 +128,48 @@
     return jnp.concatenate([w_ref[rows, c : c + HD] for c in at], axis=1)
 
 
-def load_kernel(pages, prompts, new_count, x_hbm, w_hbm, counts, tails, *refs):
-    acc, x_ref, w_ref, cos_ref, sin_ref, cos_q, sin_q, meta, x_sems, w_sems = refs
-    tokens, depth = x_ref.shape
-    half, tall = depth // 2, tokens // 2
-    copies = []
-    for i in range(2):
-        at = pl.ds(i * half, half)
-        x_copy = pltpu.make_async_copy(x_hbm.at[:, at], x_ref.at[:, at], x_sems.at[i])
-        w_copy = pltpu.make_async_copy(w_hbm.at[at], w_ref.at[at], w_sems.at[i])
-        x_copy.start()
-        w_copy.start()
-        copies.append((x_copy, w_copy))
+def keys_kernel(pages, prompts, x_ref, w_ref, counts, tails, k_ref, cos_q, sin_q, meta, cos_s, sin_s):
+    tokens = x_ref.shape[0]
+    tall = tokens // 2
     page_table(pages, prompts, counts, tails, meta)
-    rotation_tables(pages, tokens // PAGE, meta, cos_ref, sin_ref)
+    rotation_tables(pages, tokens // PAGE, meta, cos_s, sin_s)
+    new_count = cos_q.shape[0] // prompts
     spots = [meta[3 * pages + r] + n for r in range(prompts) for n in range(new_count)]
     angles = by_row(len(spots), spots) * lane_freqs(len(spots))
     cos_q[...] = jnp.cos(angles)
     sin_q[...] = jnp.sin(angles) * sine_sign(len(spots))
-    for copy in copies[0]:
-        copy.wait()
-    rows = slice(0, half)
     for pair in range(KVH // 2):
-        weight = pair_columns(w_ref, rows, pair, 0)
+        weight = pair_columns(w_ref, slice(None), pair, 0)
         for start in range(0, tokens, tall):
             at = slice(start, start + tall)
-            acc[at, 2 * pair * HD : 2 * (pair + 1) * HD] = jnp.dot(
-                x_ref[at, rows], weight, preferred_element_type=F32
-            )
-    for copy in copies[1]:
-        copy.wait()
-
-
-def load(x, kv_weight, counts, tails, pages, new_count):
+            product = jnp.dot(x_ref[at], weight, preferred_element_type=F32)
+            cosine, sine = cos_s[at], sin_s[at]
+            for h in range(2):
+                k = product[:, h * HD : (h + 1) * HD]
+                k = k * cosine + pltpu.roll(k, HD // 2, 1) * sine
+                k_ref[at, (2 * pair + h) * HD : (2 * pair + h + 1) * HD] = k.astype(BF16)
+
+
+def project_keys(x, kv_weight, counts, tails, pages, new_count):
     tokens, depth = x.shape
-    columns = kv_weight.shape[1]
     prompts = counts.shape[0]
-    hbm = pl.BlockSpec(memory_space=pltpu.HBM)
-    return pl.pallas_call(
-        functools.partial(load_kernel, pages, prompts, new_count),
-        in_specs=[hbm, hbm, SMEM, SMEM],
-        out_specs=[VMEM] * 7 + [SMEM],
+    return pl.pallas_call(
+        functools.partial(keys_kernel, pages, prompts),
+        in_specs=[VMEM, VMEM, SMEM, SMEM],
+        out_specs=[VMEM, VMEM, VMEM, SMEM],
         out_shape=[
-            pltpu.VMEM((tokens, KVH * HD), F32),
-            pltpu.VMEM((tokens, depth), BF16),
-            pltpu.VMEM((depth, columns), BF16),
-            pltpu.VMEM((tokens, HD), F32),
-            pltpu.VMEM((tokens, HD), F32),
+            pltpu.VMEM((tokens, KVH * HD), BF16),
             pltpu.VMEM((prompts * new_count, HD), F32),
             pltpu.VMEM((prompts * new_count, HD), F32),
             jax.ShapeDtypeStruct((3 * pages + prompts,), jnp.int32),
         ],
-        scratch_shapes=[pltpu.SemaphoreType.DMA((2,)), pltpu.SemaphoreType.DMA((2,))],
-        compiler_params=pltpu.CompilerParams(vmem_limit_bytes=28 * MIB),
-        cost_estimate=pl.CostEstimate(
-            flops=tokens * depth * KVH * HD,
-            bytes_accessed=2 * depth * (tokens + columns),
-            transcendentals=0,
-        ),
-        name="load",
-    )(*[in_hbm(a) for a in (x, kv_weight, counts, tails)])
-
-
-def keys_kernel(acc, x_ref, w_ref, cos_ref, sin_ref, after, k_ref):
-    tokens, depth = x_ref.shape
-    tall = tokens // 2
-    rows = slice(depth // 2, depth)
-    for pair in range(KVH // 2):
-        weight = pair_columns(w_ref, rows, pair, 0)
-        columns = slice(2 * pair * HD, 2 * (pair + 1) * HD)
-        for start in range(0, tokens, tall):
-            at = slice(start, start + tall)
-            product = acc[at, columns] + jnp.dot(
-                x_ref[at, rows], weight, preferred_element_type=F32
-            )
-            cosine, sine = cos_ref[at], sin_ref[at]
-            for h in range(2):
-                k = product[:, h * HD : (h + 1) * HD]
-                k = k * cosine + pltpu.roll(k, HD // 2, 1) * sine
-                k_ref[at, (2 * pair + h) * HD : (2 * pair + h + 1) * HD] = k.astype(BF16)
-
-
-def rotated_keys(acc, x, weight, cosine, sine, after):
-    tokens, depth = x.shape
-    return pl.pallas_call(
-        keys_kernel,
-        in_specs=[VMEM] * 5 + [pl.BlockSpec(memory_space=pl.ANY)],
-        out_specs=VMEM,
-        out_shape=pltpu.VMEM((tokens, KVH * HD), BF16),
+        scratch_shapes=[pltpu.VMEM((tokens, HD), F32), pltpu.VMEM((tokens, HD), F32)],
         compiler_params=pltpu.CompilerParams(vmem_limit_bytes=24 * MIB),
         cost_estimate=pl.CostEstimate(
-            flops=tokens * depth * KVH * HD, bytes_accessed=8 * MIB, transcendentals=0
+            flops=2 * tokens * depth * KVH * HD, bytes_accessed=12 * MIB, transcendentals=0
         ),
         name="keys",
-    )(acc, x, weight, cosine, sine, after)
+    )(in_vmem(x), in_vmem(kv_weight), in_hbm(counts), in_hbm(tails))
 
 
 def values_kernel(first, x_ref, w_ref, o_hbm, after, v_ref, o_ref, sem):
@@ -238,136 +212,136 @@
             flops=2 * tokens * depth * columns, bytes_accessed=8 * MIB, transcendentals=0
         ),
         name="values",
-    )(x, weight, in_hbm(out_weight), after)
+    )(in_vmem(x), in_vmem(weight), in_hbm(out_weight), after)
 
 
 def prepare_kernel(q_ref, kv_ref, out_ref):
-    own_rows, new_count, _, _ = out_ref.shape
+    copies, own_rows, new_count, _, _ = out_ref.shape
     for r in range(own_rows):
         q, kv = q_ref[r].astype(F32), kv_ref[r].astype(F32)
         for n in range(new_count):
             parts = [a[n : n + 1, c : c + HD] for a in (q, kv) for c in range(0, a.shape[1], HD)]
-            out_ref[r, n] = jnp.concatenate(parts, axis=0).astype(BF16)
-
-
-def prepare(new_query, new_keyval):
+            block = jnp.concatenate(parts, axis=0).astype(BF16)
+            for i in range(copies):
+                out_ref[i, r, n] = block
+
+
+def prepare(new_query, new_keyval, copies):
     own_rows, new_count, columns = new_query.shape
     heads = (columns + new_keyval.shape[2]) // HD
     return pl.pallas_call(
         prepare_kernel,
         in_specs=[VMEM, VMEM],
         out_specs=VMEM,
-        out_shape=jax.ShapeDtypeStruct((own_rows, new_count, heads, HD), BF16),
+        out_shape=jax.ShapeDtypeStruct((copies, own_rows, new_count, heads, HD), BF16),
         compiler_params=pltpu.CompilerParams(vmem_limit_bytes=8 * MIB),
         cost_estimate=pl.CostEstimate(flops=0, bytes_accessed=MIB, transcendentals=0),
         name="prepare",
     )(in_hbm(new_query), in_hbm(new_keyval))
 
 
-def stacked_kernel(n_tp, *refs):
-    for d in range(n_tp):
-        refs[-1][d] = refs[d][...]
-
-
-def stacked(pieces, after):
-    n_tp = len(pieces)
-    return pl.pallas_call(
-        functools.partial(stacked_kernel, n_tp),
-        in_specs=[VMEM] * n_tp + [pl.BlockSpec(memory_space=pl.ANY)],
-        out_specs=VMEM,
-        out_shape=jax.ShapeDtypeStruct((n_tp,) + pieces[0].shape, BF16),
-        compiler_params=pltpu.CompilerParams(vmem_limit_bytes=8 * MIB),
-        name="stacked",
-    )(*pieces, after)
-
-
-def scores_kernel(n_seq, n_tp, *refs):
-    new = refs[:n_seq]
-    k_ref, cos_q, sin_q, meta = refs[n_seq : n_seq + 4]
-    outs = refs[n_seq + 4 : n_seq + 4 + n_tp]
-    own_q, all_q, ready = refs[n_seq + 4 + n_tp :]
+def turned_queries(new_ref, cos_q, sin_q, all_q, n_seq, n_tp):
+    _, own_rows, new_count, _, _ = new_ref.shape
     kv_local = KVH // n_tp
-    local_pages = k_ref.shape[0] // PAGE
-    _, own_rows, new_count, _, _ = new[0].shape
     rows = new_count * GROUP
-    count = kv_local * rows
-    scale = 1.0 / math.sqrt(HD)
-    me = lax.axis_index("tp")
-    seq = lax.axis_index("seq")
-    first = seq * local_pages
     for ds in range(n_seq):
         for rr in range(own_rows):
-            request = (seq ^ ds) * own_rows + rr
-            spots = [pl.ds(request * new_count + n, 1) for n in range(new_count)]
+            request = ds * own_rows + rr
+            spots = [slice(request * new_count + n, request * new_count + n + 1) for n in range(new_count)]
             turn = [(cos_q[spot], sin_q[spot]) for spot in spots]
             for dt in range(n_tp):
-                block = [new[ds][dt, rr, n].astype(F32) for n in range(new_count)]
+                block = [new_ref[ds * n_tp + dt, rr, n].astype(F32) for n in range(new_count)]
                 for g in range(kv_local):
                     parts = []
                     for n in range(new_count):
                         q = block[n][g * GROUP : (g + 1) * GROUP]
                         parts.append(q * turn[n][0] + pltpu.roll(q, HD // 2, 1) * turn[n][1])
-                    part = jnp.concatenate(parts, axis=0).astype(BF16)
-                    at = ((me ^ dt) * kv_local + g) * rows
-                    all_q[request, pl.ds(pl.multiple_of(at, rows), rows)] = part
-                    if dt == 0:
-                        own_q[request, g * rows : (g + 1) * rows] = part
+                    at = (dt * kv_local + g) * rows
+                    all_q[request, at : at + rows] = jnp.concatenate(parts, axis=0).astype(BF16)
+
+
+def page_scores(all_q, k_ref, meta, outs, entries, rows):
+    local_pages = k_ref.shape[0] // PAGE
+    kv_local = outs[0].shape[0] // rows
+    scale = 1.0 / math.sqrt(HD)
+    me = lax.axis_index("tp")
+    first = lax.axis_index("seq") * local_pages
     for p in range(local_pages):
         request = meta[first + p]
         tokens = slice(p * PAGE, (p + 1) * PAGE)
-        for head in range(KVH):
-            k = k_ref[tokens, head * HD : (head + 1) * HD]
-            q = all_q[request, head * rows : (head + 1) * rows]
-            s = lax.dot_general(q, k, (((1,), (1,)), ((), ())), preferred_element_type=F32)
-            ready[head * rows : (head + 1) * rows, tokens] = (s * scale).astype(BF16)
-    for d in range(n_tp):
-        outs[d][...] = ready[pl.ds(pl.multiple_of((me ^ d) * count, count), count)]
-
-
-def partial_scores(new, k, cos_q, sin_q, meta, prompts, n_tp):
-    n_seq = len(new)
-    new_count = new[0].shape[2]
+        for out, d in zip(outs, entries):
+            for g in range(kv_local):
+                head = (me ^ d) * kv_local + g
+                k = k_ref[tokens, pl.ds(pl.multiple_of(head * HD, HD), HD)]
+                q = all_q[request, pl.ds(pl.multiple_of(head * rows, rows), rows)]
+                s = lax.dot_general(q, k, (((1,), (1,)), ((), ())), preferred_element_type=F32)
+                out[g * rows : (g + 1) * rows, tokens] = (s * scale).astype(BF16)
+
+
+def far_kernel(n_seq, n_tp, entries, new_ref, k_ref, cos_q, sin_q, meta, all_q, *outs):
+    turned_queries(new_ref, cos_q, sin_q, all_q, n_seq, n_tp)
+    page_scores(all_q, k_ref, meta, outs, entries, new_ref.shape[2] * GROUP)
+
+
+def near_kernel(rows, entries, all_q, k_ref, meta, *outs):
+    page_scores(all_q, k_ref, meta, outs, entries, rows)
+
+
+def partial_scores(new, k, cos_q, sin_q, meta, prompts, n_seq, n_tp):
+    new_count = new.shape[2]
     tokens = k.shape[0]
-    rows = KVH // n_tp * new_count * GROUP
-    return pl.pallas_call(
-        functools.partial(scores_kernel, n_seq, n_tp),
-        in_specs=[VMEM] * (n_seq + 3) + [SMEM],
-        out_specs=[VMEM] * (n_tp + 1),
-        out_shape=[jax.ShapeDtypeStruct((rows, tokens), BF16)] * n_tp
-        + [jax.ShapeDtypeStruct((prompts, rows, HD), BF16)],
-        scratch_shapes=[
-            pltpu.VMEM((prompts, rows * n_tp, HD), BF16),
-            pltpu.VMEM((rows * n_tp, tokens), BF16),
-        ],
+    rows = new_count * GROUP
+    count = KVH // n_tp * rows
+    chunk = jax.ShapeDtypeStruct((count, tokens), BF16)
+    params = dict(
         compiler_params=pltpu.CompilerParams(vmem_limit_bytes=24 * MIB),
         cost_estimate=pl.CostEstimate(
-            flops=2 * tokens * rows * n_tp * HD, bytes_accessed=6 * MIB, transcendentals=0
+            flops=tokens * count * n_tp * HD, bytes_accessed=3 * MIB, transcendentals=0
         ),
-        name="scores",
-    )(*new, k, cos_q, sin_q, meta)
-
-
-def fresh_kernel(n_seq, *refs):
-    new = refs[:n_seq]
-    q_ref, cos_q, sin_q, score_ref, value_ref = refs[n_seq:]
-    prompts, rows_local, _ = q_ref.shape
-    _, own_rows, new_count, _, _ = new[0].shape
+    )
+    far, near = list(range(n_tp // 2, n_tp)), list(range(n_tp // 2))
+    all_q, *outs = pl.pallas_call(
+        functools.partial(far_kernel, n_seq, n_tp, far),
+        in_specs=[VMEM] * 4 + [SMEM],
+        out_specs=[VMEM] * (1 + len(far)),
+        out_shape=[pltpu.VMEM((prompts, count * n_tp, HD), BF16)] + [chunk] * len(far),
+        name="far_scores",
+        **params,
+    )(new, k, cos_q, sin_q, meta)
+    got = {d: pairs(out, "tp", d) for d, out in zip(far, outs)}
+    outs = pl.pallas_call(
+        functools.partial(near_kernel, rows, near),
+        in_specs=[VMEM] * 2 + [SMEM],
+        out_specs=[VMEM] * len(near),
+        out_shape=[chunk] * len(near),
+        name="near_scores",
+        **params,
+    )(all_q, k, meta)
+    for d, out in zip(near, outs):
+        got[d] = pairs(out, "tp", d) if d else out
+    return all_q, [got[d] for d in range(n_tp)]
+
+
+def fresh_kernel(n_seq, n_tp, new_ref, all_q, cos_q, sin_q, score_ref, value_ref):
+    rows_local = score_ref.shape[1]
+    _, own_rows, new_count, _, _ = new_ref.shape
     rows = new_count * GROUP
     kv_local = rows_local // rows
     heads = kv_local * GROUP
     scale = 1.0 / math.sqrt(HD)
-    seq = lax.axis_index("seq")
+    me = lax.axis_index("tp")
+    own = pl.ds(pl.multiple_of(me * rows_local, rows_local), rows_local)
     step = lax.broadcasted_iota(jnp.int32, (rows_local, HD), 0) % rows // GROUP
     lane = lax.broadcasted_iota(jnp.int32, (rows_local, HD), 1)
     found = [jnp.full((rows_local, HD), NEG, F32) for _ in range(new_count)]
     for ds in range(n_seq):
         for rr in range(own_rows):
-            request = (seq ^ ds) * own_rows + rr
-            q = q_ref[request].astype(F32)
+            request = ds * own_rows + rr
+            q = all_q[request, own].astype(F32)
             for n in range(new_count):
-                spot = pl.ds(request * new_count + n, 1)
+                spot = slice(request * new_count + n, request * new_count + n + 1)
                 cosine, sine = cos_q[spot], sin_q[spot]
-                both = new[ds][0, rr, n].astype(F32)
+                both = new_ref[ds * n_tp + me, rr, n].astype(F32)
                 keys, values = [], []
                 for g in range(kv_local):
                     k = both[heads + 2 * g : heads + 2 * g + 1]
@@ -383,13 +357,13 @@
         score_ref[n] = found[n]
 
 
-def fresh_scores(new, own_q, cos_q, sin_q):
-    n_seq = len(new)
-    new_count = new[0].shape[2]
-    prompts, rows, _ = own_q.shape
-    return pl.pallas_call(
-        functools.partial(fresh_kernel, n_seq),
-        in_specs=[VMEM] * (n_seq + 3),
+def fresh_scores(new, all_q, cos_q, sin_q, n_seq, n_tp):
+    new_count = new.shape[2]
+    prompts, rows, _ = all_q.shape
+    rows = rows // n_tp
+    return pl.pallas_call(
+        functools.partial(fresh_kernel, n_seq, n_tp),
+        in_specs=[VMEM] * 4,
         out_specs=[VMEM, VMEM],
         out_shape=[
             jax.ShapeDtypeStruct((new_count, rows, HD), F32),
@@ -398,7 +372,7 @@
         compiler_params=pltpu.CompilerParams(vmem_limit_bytes=16 * MIB),
         cost_estimate=pl.CostEstimate(flops=0, bytes_accessed=2 * MIB, transcendentals=0),
         name="fresh",
-    )(*new, own_q, cos_q, sin_q)
+    )(new, all_q, cos_q, sin_q)
 
 
 def weights_kernel(pages, prompts, n_tp, *refs):
@@ -459,52 +433,59 @@
     )(*chunks, meta)
 
 
-def weighted_kernel(n_tp, *refs):
-    pieces = refs[:n_tp]
-    va_ref, vb_ref, meta = refs[n_tp : n_tp + 3]
-    outs = refs[n_tp + 3 : n_tp + 3 + n_tp]
-    ready, total = refs[n_tp + 3 + n_tp :]
+def weighted_kernel(n_tp, entries, *refs):
+    pieces = refs[: len(entries)]
+    va_ref, vb_ref, meta = refs[len(entries) : len(entries) + 3]
+    outs, total = refs[len(entries) + 3 : -1], refs[-1]
     rows_local, tokens_here = pieces[0].shape
     kv_local = KVH // n_tp
     rows = rows_local // kv_local
     local_pages = tokens_here // PAGE
     first = lax.axis_index("seq") * local_pages
+    half = va_ref.shape[1] // HD
     me = lax.axis_index("tp")
-    own = [pl.ds(pl.multiple_of((me ^ d) * rows_local, rows_local), rows_local) for d in range(n_tp)]
-    for d in range(n_tp):
-        ready[own[d]] = pieces[d][...]
     total[...] = jnp.zeros_like(total)
-    half = va_ref.shape[1] // HD
     for p in range(local_pages):
         request = meta[first + p]
         tokens = slice(p * PAGE, (p + 1) * PAGE)
-        for head in range(KVH):
-            v_ref = va_ref if head < half else vb_ref
-            v = v_ref[tokens, head % half * HD : (head % half + 1) * HD]
-            at = slice(head * rows, (head + 1) * rows)
-            total[request, at] += jnp.dot(ready[at, tokens], v, preferred_element_type=F32)
-    for d in range(n_tp):
-        outs[d][...] = total[:, own[d]].astype(BF16)
+        for i, (piece, d) in enumerate(zip(pieces, entries)):
+            for g in range(kv_local):
+                head = (me ^ d) * kv_local + g
+                at = pl.ds(pl.multiple_of(head % half * HD, HD), HD)
+                v = jnp.where(head < half, va_ref[tokens, at], vb_ref[tokens, at])
+                to = slice((i * kv_local + g) * rows, (i * kv_local + g + 1) * rows)
+                total[request, to] += jnp.dot(
+                    piece[g * rows : (g + 1) * rows, tokens], v, preferred_element_type=F32
+                )
+    for i, out in enumerate(outs):
+        out[...] = total[:, i * rows_local : (i + 1) * rows_local].astype(BF16)
 
 
 def weighted_values(pieces, va, vb, meta, prompts):
     n_tp = len(pieces)
     rows, tokens = pieces[0].shape
-    return pl.pallas_call(
-        functools.partial(weighted_kernel, n_tp),
-        in_specs=[VMEM] * (n_tp + 2) + [SMEM],
-        out_specs=[VMEM] * n_tp,
-        out_shape=[jax.ShapeDtypeStruct((prompts, rows, HD), BF16)] * n_tp,
-        scratch_shapes=[
-            pltpu.VMEM((rows * n_tp, tokens), BF16),
-            pltpu.VMEM((prompts, rows * n_tp, HD), F32),
-        ],
-        compiler_params=pltpu.CompilerParams(vmem_limit_bytes=24 * MIB),
-        cost_estimate=pl.CostEstimate(
-            flops=2 * tokens * rows * n_tp * HD, bytes_accessed=8 * MIB, transcendentals=0
-        ),
-        name="weighted",
-    )(*pieces, va, vb, meta)
+
+    def call(entries):
+        return pl.pallas_call(
+            functools.partial(weighted_kernel, n_tp, entries),
+            in_specs=[VMEM] * (len(entries) + 2) + [SMEM],
+            out_specs=[VMEM] * len(entries),
+            out_shape=[jax.ShapeDtypeStruct((prompts, rows, HD), BF16)] * len(entries),
+            scratch_shapes=[pltpu.VMEM((prompts, rows * len(entries), HD), F32)],
+            compiler_params=pltpu.CompilerParams(vmem_limit_bytes=24 * MIB),
+            cost_estimate=pl.CostEstimate(
+                flops=tokens * rows * n_tp * HD, bytes_accessed=4 * MIB, transcendentals=0
+            ),
+            name="weighted",
+        )(*[pieces[d] for d in entries], va, vb, meta)
+
+    got = {}
+    far, near = list(range(n_tp // 2, n_tp)), list(range(n_tp // 2))
+    for d, out in zip(far, call(far)):
+        got[d] = pairs(out, "tp", d)
+    for d, out in zip(near, call(near)):
+        got[d] = pairs(out, "tp", d) if d else out
+    return [got[d] for d in range(n_tp)]
 
 
 def summed_kernel(n_tp, *refs):
@@ -625,20 +606,17 @@
     own_rows, new_count, _ = new_query.shape
     prompts = page_counts.shape[0]
     pages = prefill_states.shape[0] // PAGE * n_seq
-    new = gather(prepare(new_query, new_keyval), "tp")
-    acc, x, w, cosine, sine, cos_q, sin_q, meta = load(
-        prefill_states, kv_weight, page_counts, tail_tokens, pages, new_count
-    )
-    new = stacked(new, meta)
-    k = rotated_keys(acc, x, w, cosine, sine, new)
-    new = gather(new, "seq")
-    *scores, own_q = partial_scores(new, k, cos_q, sin_q, meta, prompts, n_tp)
-    va, oa = project_values(x, w, out_weight, 0, own_q)
-    fresh, values = fresh_scores(new, own_q, cos_q, sin_q)
-    weights, stats = softmax_weights(exchange(scores, "tp"), meta, pages, prompts)
+    x, w = own_copy(prefill_states, "tp"), own_copy(kv_weight, "tp")
+    new = prepare(new_query, new_keyval, n_seq * n_tp)
+    new = lax.all_to_all(new, ("seq", "tp"), 0, 0)
+    k, cos_q, sin_q, meta = project_keys(x, w, page_counts, tail_tokens, pages, new_count)
+    all_q, scores = partial_scores(new, k, cos_q, sin_q, meta, prompts, n_seq, n_tp)
+    va, oa = project_values(x, w, out_weight, 0, all_q)
+    fresh, values = fresh_scores(new, all_q, cos_q, sin_q, n_seq, n_tp)
+    weights, stats = softmax_weights(scores, meta, pages, prompts)
     vb, ob = project_values(x, w, out_weight, 1, stats)
     chunks = weighted_values(gather(weights, "tp"), va, vb, meta, prompts)
-    pieces = gather(summed(exchange(chunks, "tp"), stats), "seq")
+    pieces = gather(summed(chunks, stats), "seq")
     partial = output_partial(pieces, fresh, values, (oa, ob))
     return final_sum(gather(partial, "tp"), residual)
 

time: 68.8 us -> 79.6 us (1.16)
  blocking collectives: 0 us -> 18.7 us
  waiting for transfers between devices: 20.1 us -> 15.9 us
  Pallas kernels: 22 us -> 19.8 us
  starting transfers between devices: 26.3 us -> 24.6 us
    all_to_all x0 -> x1, blocking collectives: none -> 18.7 us  [on_device(): new = lax.all_to_all(new, ('seq', 'tp'), 0, 0)]
    ppermute x21 -> x17, waiting for transfers between devices: 20.1 us -> 15.9 us  [pairs(): lax.ppermute(value, axis, [(i, i ^ d) for i in range(lax.axis_size(axis))])]
    pallas_call x6 -> x9, Pallas kernels: 13.2 us -> 11.1 us  [the longest x1 5.8 us: project_keys(): pl.pallas_call(functools.partial(keys_kernel, pages, prompts), in_specs=[...]
    ppermute x21 -> x17, starting transfers between devices: 26.3 us -> 24.6 us  [pairs(): lax.ppermute(value, axis, [(i, i ^ d) for i in range(lax.axis_size(axis))])]
  transfers between devices with their start and end apart: 21 -> 17, of which waited for: 14 -> 9; matrix products, arithmetic and copies ran while one was open for 0% -> 0% of each run, Pallas kernels for 22% -> 10%
where the time goes in v6:
time: 79.6 us; the launch traced here: 79.3 us
  starting transfers between devices  24.6 us (31%)
  Pallas kernels  19.8 us (25%)
  blocking collectives  18.7 us (23%)
  waiting for transfers between devices  15.9 us (20%)
    ppermute x17, starting transfers between devices, pairs(): lax.ppermute(value, axis, [(i, i ^ d) for i in range(lax.axis_size(axis))])  24.6 us
    all_to_all x1, blocking collectives, on_device(): new = lax.all_to_all(new, ('seq', 'tp'), 0, 0)  18.7 us
    ppermute x17, waiting for transfers between devices, pairs(): lax.ppermute(value, axis, [(i, i ^ d) for i in range(lax.axis_size(axis))])  15.9 us
    pallas_call x1, Pallas kernels, project_keys(): pl.pallas_call(functools.partial(keys_kernel, pages, prompts), in_specs=[...  5.8 us
    pallas_call x2, Pallas kernels, project_values(): pl.pallas_call(functools.partial(values_kernel, first), in_specs=[VMEM, V...  4.7 us
    pallas_call x2, Pallas kernels, call(): pl.pallas_call(functools.partial(weighted_kernel, n_tp, entries), in_spec...  1.97 us
  transfers between devices with their start and end apart: 17, of which 9 were waited for; matrix products, arithmetic and copies ran while one was open for 0% of the time, Pallas kernels for 10%

profile of v6, /device:TPU:0, one launch (start us, length us, event | category | flops | bytes accessed | tf_op | source)
XLA Modules:
  0.0 79.3 jit_solution(143645837746001411)
XLA Ops:
  0.0 3.4 %collective-permute-start.1 = (bf16[2048,2048]{1,0:T(8,128)(2,1)}, bf16[2048,2048]{1,0:T(8,128)(2,1)S(1)}, u32[]{:S(2)}, u32[]{:S(2)}) collective-permute-start(bf16[2048,2048]{1,0:T(8,128)(2,1)} %param.9), channel_id=1, source_target_pairs={{0,0},{1,1},{2,2},{3,3},{4,4},{5,5},{6,6},{7,7},{8,8},{9,9},{10,10... | collective-permute-start | bytes 25165832 | tf_op jit(solution)/shard_map/ppermute | solution.py:26
  3.4 2.2 %collective-permute-start = (bf16[1024,2048]{1,0:T(8,128)(2,1)}, bf16[1024,2048]{1,0:T(8,128)(2,1)S(1)}, u32[]{:S(2)}, u32[]{:S(2)}) collective-permute-start(bf16[1024,2048]{1,0:T(8,128)(2,1)} %param.8), channel_id=1, source_target_pairs={{0,0},{1,1},{2,2},{3,3},{4,4},{5,5},{6,6},{7,7},{8,8},{9,9},{10,10... | collective-permute-start | bytes 12582920 | tf_op jit(solution)/shard_map/ppermute | solution.py:26
  5.6 0.8 prepare.1
  6.6 18.7 %all_to_all.5 = bf16[16,2,2,20,128]{4,2,3,1,0:T(2,128)(2,1)S(1)} all-to-all(bf16[16,2,2,20,128]{4,2,3,1,0:T(2,128)(2,1)S(1)} %copy.9), channel_id=1, replica_groups=mesh['groups'=2,'seq'=4,'tp'=4] {'seq','tp'}, dimensions={0} | all-to-all | bytes 655360 | tf_op jit(solution)/shard_map/all_to_all | solution.py:611
  25.3 5.8 %keys.1 = (bf16[1024,1024]{1,0:T(8,128)(2,1)S(1)}, f32[16,128]{1,0:T(8,128)S(1)}, f32[16,128]{1,0:T(8,128)S(1)}, s32[104]{0:T(128)S(1)}) custom-call(bf16[1024,2048]{1,0:T(8,128)(2,1)S(1)} %collective-permute-done.x_ref, bf16[2048,2048]{1,0:T(8,128)(2,1)S(1)} %collective-permute-done.1.w_ref, s32[8]{0:T(128)} %counts.1, s32[8]{0:T(128)} %tails.1), custom_call_target="tpu_custom_call" | custom-call | flops 4294967296 | bytes 12582912 | tf_op jit(solution)/shard_map/keys/pallas_call | solution.py:156
  31.2 1.3 %far_scores.1 = (bf16[8,128,128]{2,1,0:T(8,128)(2,1)S(1)}, bf16[32,1024]{1,0:T(8,128)(2,1)S(1)}, bf16[32,1024]{1,0:T(8,128)(2,1)S(1)}) custom-call(bf16[16,2,2,20,128]{4,3,2,1,0:T(8,128)(2,1)S(1)} %copy.10.new_ref, bf16[1024,1024]{1,0:T(8,128)(2,1)S(1)} %get-tuple-element.26.k_ref, f32[16,128]{1,0:T(8,128)S(1)} %get-tuple-element.27.cos_q, ...), custom_call_target="tpu_custom_call" | custom-call | flops 16777216 | bytes 3145728 | tf_op jit(solution)/shard_map/far_scores/pallas_call | solution.py:303
  32.5 1.2 %near_scores.1 = (bf16[32,1024]{1,0:T(8,128)(2,1)S(1)}, bf16[32,1024]{1,0:T(8,128)(2,1)S(1)}) custom-call(bf16[8,128,128]{2,1,0:T(8,128)(2,1)S(1)} %get-tuple-element.30.all_q.after, bf16[1024,1024]{1,0:T(8,128)(2,1)S(1)} %get-tuple-element.26.k_ref, s32[104]{0:T(128)S(1)} %get-tuple-element.29.meta.refs_4_), custom_call_target="tpu_custom_call" | custom-call | flops 16777216 | bytes 3145728 | tf_op jit(solution)/shard_map/near_scores/pallas_call | solution.py:312
  33.7 1.4 %collective-permute-start.3 = (bf16[32,1024]{1,0:T(8,128)(2,1)S(1)}, bf16[32,1024]{1,0:T(8,128)(2,1)S(1)}, u32[]{:S(2)}, u32[]{:S(2)}) collective-permute-start(bf16[32,1024]{1,0:T(8,128)(2,1)S(1)} %get-tuple-element.33), channel_id=1, source_target_pairs={{0,2},{1,3},{2,0},{3,1},{4,6},{5,7},{6,4},{7,5},{8,10},{9,11},{10,... | collective-permute-start | bytes 196616 | tf_op jit(solution)/shard_map/ppermute | solution.py:26
  35.2 2.9 %collective-permute-start.4 = (bf16[32,1024]{1,0:T(8,128)(2,1)S(1)}, bf16[32,1024]{1,0:T(8,128)(2,1)S(1)}, u32[]{:S(2)}, u32[]{:S(2)}) collective-permute-start(bf16[32,1024]{1,0:T(8,128)(2,1)S(1)} %get-tuple-element.34), channel_id=1, source_target_pairs={{0,3},{1,2},{2,1},{3,0},{4,7},{5,6},{6,5},{7,4},{8,11},{9,10},{10,... | collective-permute-start | bytes 196616 | tf_op jit(solution)/shard_map/ppermute | solution.py:26
  38.1 2.3 %values.2 = (bf16[1024,512]{1,0:T(8,128)(2,1)S(1)}, bf16[1024,2048]{1,0:T(8,128)(2,1)S(1)}) custom-call(bf16[1024,2048]{1,0:T(8,128)(2,1)S(1)} %collective-permute-done.x_ref, bf16[2048,2048]{1,0:T(8,128)(2,1)S(1)} %collective-permute-done.1.w_ref, bf16[2048,2048]{1,0:T(8,128)(2,1)} %o_hbm.3, bf16[8,128,128]{2,1,0:T(8,128)(2,1)S(1)} %get-tuple-element.30.all_q.after), custom_call_target="tpu_custom_call" | custom-call | flops 2147483648 | bytes 8388608 | tf_op jit(solution)/shard_map/values/pallas_call | solution.py:196
  40.5 1.8 %collective-permute-done.3.refs_2_ = bf16[32,1024]{1,0:T(8,128)(2,1)S(1)} collective-permute-done((bf16[32,1024]{1,0:T(8,128)(2,1)S(1)}, bf16[32,1024]{1,0:T(8,128)(2,1)S(1)}, u32[]{:S(2)}, u32[]{:S(2)}) %collective-permute-start.3) | collective-permute-done | bytes 65568 | tf_op jit(solution)/shard_map/ppermute | solution.py:26
  42.3 0.9 %weights.1 = (bf16[32,1024]{1,0:T(8,128)(2,1)S(1)}, bf16[32,128]{1,0:T(8,128)(2,1)S(1)}) custom-call(bf16[32,1024]{1,0:T(8,128)(2,1)S(1)} %get-tuple-element.31.refs_0_, bf16[32,1024]{1,0:T(8,128)(2,1)S(1)} %collective-permute-done.2.refs_1_, bf16[32,1024]{1,0:T(8,128)(2,1)S(1)} %collective-permute-done.3.refs_2_, ...), custom_call_target="tpu_custom_call" | custom-call | tf_op jit(solution)/shard_map/weights/pallas_call | solution.py:423
  43.2 1.5 %collective-permute-start.7 = (bf16[32,1024]{1,0:T(8,128)(2,1)S(1)}, bf16[32,1024]{1,0:T(8,128)(2,1)S(1)}, u32[]{:S(2)}, u32[]{:S(2)}) collective-permute-start(bf16[32,1024]{1,0:T(8,128)(2,1)S(1)} %get-tuple-element.35.in_ref.refs_0_), channel_id=1, source_target_pairs={{0,2},{1,3},{2,0},{3,1},{4,6},{5,7},{6,4},{7,5},{8,10},{9,11},{10,... | collective-permute-start | bytes 196616 | tf_op jit(solution)/shard_map/ppermute | solution.py:26
  44.7 2.2 %collective-permute-start.8 = (bf16[32,1024]{1,0:T(8,128)(2,1)S(1)}, bf16[32,1024]{1,0:T(8,128)(2,1)S(1)}, u32[]{:S(2)}, u32[]{:S(2)}) collective-permute-start(bf16[32,1024]{1,0:T(8,128)(2,1)S(1)} %get-tuple-element.35.in_ref.refs_0_), channel_id=1, source_target_pairs={{0,3},{1,2},{2,1},{3,0},{4,7},{5,6},{6,5},{7,4},{8,11},{9,10},{10,... | collective-permute-start | bytes 196616 | tf_op jit(solution)/shard_map/ppermute | solution.py:26
  46.9 2.3 %values.3 = (bf16[1024,512]{1,0:T(8,128)(2,1)S(1)}, bf16[1024,2048]{1,0:T(8,128)(2,1)S(1)}) custom-call(bf16[1024,2048]{1,0:T(8,128)(2,1)S(1)} %collective-permute-done.x_ref, bf16[2048,2048]{1,0:T(8,128)(2,1)S(1)} %collective-permute-done.1.w_ref, bf16[2048,2048]{1,0:T(8,128)(2,1)} %o_hbm.3, bf16[32,128]{1,0:T(8,128)(2,1)S(1)} %get-tuple-element.37.after.refs_4_), custom_call_target="tpu_custom_call" | custom-call | flops 2147483648 | bytes 8388608 | tf_op jit(solution)/shard_map/values/pallas_call | solution.py:196
  49.2 2.2 %collective-permute-done.5.refs_1_ = bf16[32,1024]{1,0:T(8,128)(2,1)S(1)} collective-permute-done((bf16[32,1024]{1,0:T(8,128)(2,1)S(1)}, bf16[32,1024]{1,0:T(8,128)(2,1)S(1)}, u32[]{:S(2)}, u32[]{:S(2)}) %collective-permute-start.5) | collective-permute-done | bytes 65568 | tf_op jit(solution)/shard_map/ppermute | solution.py:26
  51.5 1.0 %weighted.2 = (bf16[8,32,128]{2,1,0:T(8,128)(2,1)S(1)}, bf16[8,32,128]{2,1,0:T(8,128)(2,1)S(1)}) custom-call(bf16[32,1024]{1,0:T(8,128)(2,1)S(1)} %get-tuple-element.35.in_ref.refs_0_, bf16[32,1024]{1,0:T(8,128)(2,1)S(1)} %collective-permute-done.5.refs_1_, bf16[1024,512]{1,0:T(8,128)(2,1)S(1)} %get-tuple-element.36.refs_2_, ...), custom_call_target="tpu_custom_call" | custom-call | flops 16777216 | bytes 4194304 | tf_op jit(solution)/shard_map/weighted/pallas_call | solution.py:469
  52.9 1.0 %weighted.3 = (bf16[8,32,128]{2,1,0:T(8,128)(2,1)S(1)}, bf16[8,32,128]{2,1,0:T(8,128)(2,1)S(1)}) custom-call(bf16[32,1024]{1,0:T(8,128)(2,1)S(1)} %collective-permute-done.7.refs_0_, bf16[32,1024]{1,0:T(8,128)(2,1)S(1)} %collective-permute-done.8.refs_1_, bf16[1024,512]{1,0:T(8,128)(2,1)S(1)} %get-tuple-element.36.refs_2_, ...), custom_call_target="tpu_custom_call" | custom-call | flops 16777216 | bytes 4194304 | tf_op jit(solution)/shard_map/weighted/pallas_call | solution.py:469
  53.9 2.2 %collective-permute-start.9 = (bf16[8,32,128]{2,1,0:T(8,128)(2,1)S(1)}, bf16[8,32,128]{2,1,0:T(8,128)(2,1)S(1)}, u32[]{:S(2)}, u32[]{:S(2)}) collective-permute-start(bf16[8,32,128]{2,1,0:T(8,128)(2,1)S(1)} %get-tuple-element.41), channel_id=1, source_target_pairs={{0,2},{1,3},{2,0},{3,1},{4,6},{5,7},{6,4},{7,5},{8,10},{9,11},{10,... | collective-permute-start | bytes 196616 | tf_op jit(solution)/shard_map/ppermute | solution.py:26
  56.2 1.8 %collective-permute-start.10 = (bf16[8,32,128]{2,1,0:T(8,128)(2,1)S(1)}, bf16[8,32,128]{2,1,0:T(8,128)(2,1)S(1)}, u32[]{:S(2)}, u32[]{:S(2)}) collective-permute-start(bf16[8,32,128]{2,1,0:T(8,128)(2,1)S(1)} %get-tuple-element.42), channel_id=1, source_target_pairs={{0,3},{1,2},{2,1},{3,0},{4,7},{5,6},{6,5},{7,4},{8,11},{9,10},{10,... | collective-permute-start | bytes 196616 | tf_op jit(solution)/shard_map/ppermute | solution.py:26
  58.0 1.3 %collective-permute-done.9.refs_2_ = bf16[8,32,128]{2,1,0:T(8,128)(2,1)S(1)} collective-permute-done((bf16[8,32,128]{2,1,0:T(8,128)(2,1)S(1)}, bf16[8,32,128]{2,1,0:T(8,128)(2,1)S(1)}, u32[]{:S(2)}, u32[]{:S(2)}) %collective-permute-start.9) | collective-permute-done | bytes 65568 | tf_op jit(solution)/shard_map/ppermute | solution.py:26
  59.3 2.9 %collective-permute-done.10.refs_3_ = bf16[8,32,128]{2,1,0:T(8,128)(2,1)S(1)} collective-permute-done((bf16[8,32,128]{2,1,0:T(8,128)(2,1)S(1)}, bf16[8,32,128]{2,1,0:T(8,128)(2,1)S(1)}, u32[]{:S(2)}, u32[]{:S(2)}) %collective-permute-start.10) | collective-permute-done | bytes 65568 | tf_op jit(solution)/shard_map/ppermute | solution.py:26
  62.4 1.0 %collective-permute-start.12 = (bf16[9,32,128]{2,1,0:T(8,128)(2,1)S(1)}, bf16[9,32,128]{2,1,0:T(8,128)(2,1)S(1)}, u32[]{:S(2)}, u32[]{:S(2)}) collective-permute-start(bf16[9,32,128]{2,1,0:T(8,128)(2,1)S(1)} %summed.1.in_ref.refs_0_), channel_id=1, source_target_pairs={{0,8},{4,12},{8,0},{12,4},{1,9},{5,13},{9,1},{13,5},{2,10},{6,14},... | collective-permute-start | bytes 221192 | tf_op jit(solution)/shard_map/ppermute | solution.py:26
  63.4 0.8 %collective-permute-start.13 = (bf16[9,32,128]{2,1,0:T(8,128)(2,1)S(1)}, bf16[9,32,128]{2,1,0:T(8,128)(2,1)S(1)}, u32[]{:S(2)}, u32[]{:S(2)}) collective-permute-start(bf16[9,32,128]{2,1,0:T(8,128)(2,1)S(1)} %summed.1.in_ref.refs_0_), channel_id=1, source_target_pairs={{0,12},{4,8},{8,4},{12,0},{1,13},{5,9},{9,5},{13,1},{2,14},{6,10},... | collective-permute-start | bytes 221192 | tf_op jit(solution)/shard_map/ppermute | solution.py:26
  64.2 0.7 fresh.1
  65.0 2.5 %collective-permute-done.12.refs_2_ = bf16[9,32,128]{2,1,0:T(8,128)(2,1)S(1)} collective-permute-done((bf16[9,32,128]{2,1,0:T(8,128)(2,1)S(1)}, bf16[9,32,128]{2,1,0:T(8,128)(2,1)S(1)}, u32[]{:S(2)}, u32[]{:S(2)}) %collective-permute-start.12) | collective-permute-done | bytes 73760 | tf_op jit(solution)/shard_map/ppermute | solution.py:26
  68.2 1.6 %output.1.in_ref.refs_0_ = bf16[16,2048]{1,0:T(8,128)(2,1)S(1)} custom-call(bf16[9,32,128]{2,1,0:T(8,128)(2,1)S(1)} %summed.1.in_ref.refs_0_, bf16[9,32,128]{2,1,0:T(8,128)(2,1)S(1)} %collective-permute-done.11.refs_1_, bf16[9,32,128]{2,1,0:T(8,128)(2,1)S(1)} %collective-permute-done.12.refs_2_, bf16[9,32,128]{2,1,0:T(8,128)(2,1)S(1)} %collective-permute-done.13.refs_3_, ...), custom_call_target="tpu_custom_call" | custom-call | tf_op jit(solution)/shard_map/output/pallas_call | solution.py:568
  69.8 2.6 %collective-permute-start.15 = (bf16[16,2048]{1,0:T(8,128)(2,1)S(1)}, bf16[16,2048]{1,0:T(8,128)(2,1)S(1)}, u32[]{:S(2)}, u32[]{:S(2)}) collective-permute-start(bf16[16,2048]{1,0:T(8,128)(2,1)S(1)} %output.1.in_ref.refs_0_), channel_id=1, source_target_pairs={{0,2},{1,3},{2,0},{3,1},{4,6},{5,7},{6,4},{7,5},{8,10},{9,11},{10,... | collective-permute-start | bytes 196616 | tf_op jit(solution)/shard_map/ppermute | solution.py:26
  72.4 1.8 %collective-permute-start.16 = (bf16[16,2048]{1,0:T(8,128)(2,1)S(1)}, bf16[16,2048]{1,0:T(8,128)(2,1)S(1)}, u32[]{:S(2)}, u32[]{:S(2)}) collective-permute-start(bf16[16,2048]{1,0:T(8,128)(2,1)S(1)} %output.1.in_ref.refs_0_), channel_id=1, source_target_pairs={{0,3},{1,2},{2,1},{3,0},{4,7},{5,6},{6,5},{7,4},{8,11},{9,10},{10,... | collective-permute-start | bytes 196616 | tf_op jit(solution)/shard_map/ppermute | solution.py:26
  74.2 0.9 %collective-permute-done.14.refs_1_ = bf16[16,2048]{1,0:T(8,128)(2,1)S(1)} collective-permute-done((bf16[16,2048]{1,0:T(8,128)(2,1)S(1)}, bf16[16,2048]{1,0:T(8,128)(2,1)S(1)}, u32[]{:S(2)}, u32[]{:S(2)}) %collective-permute-start.14) | collective-permute-done | bytes 65568 | tf_op jit(solution)/shard_map/ppermute | solution.py:26
  75.1 2.8 %collective-permute-done.15.refs_2_ = bf16[16,2048]{1,0:T(8,128)(2,1)S(1)} collective-permute-done((bf16[16,2048]{1,0:T(8,128)(2,1)S(1)}, bf16[16,2048]{1,0:T(8,128)(2,1)S(1)}, u32[]{:S(2)}, u32[]{:S(2)}) %collective-permute-start.15) | collective-permute-done | bytes 65568 | tf_op jit(solution)/shard_map/ppermute | solution.py:26
  77.8 0.8 collective-permute-done.16.refs_3_
  (23 shorter events, 2.4 us)
Async XLA Ops:
  0.0 25.3 %collective-permute-start.1 = (bf16[2048,2048]{1,0:T(8,128)(2,1)}, bf16[2048,2048]{1,0:T(8,128)(2,1)S(1)}, u32[]{:S(2)}, u32[]{:S(2)}) collective-permute-start(bf16[2048,2048]{1,0:T(8,128)(2,1)} %param.9), channel_id=1, source_target_pairs={{0,0},{1,1},{2,2},{3,3},{4,4},{5,5},{6,6},{7,7},{8,8},{9,9},{10,10... | collective-permute-start | bytes 25165832 | tf_op jit(solution)/shard_map/ppermute | solution.py:26
  3.4 21.9 %collective-permute-start = (bf16[1024,2048]{1,0:T(8,128)(2,1)}, bf16[1024,2048]{1,0:T(8,128)(2,1)S(1)}, u32[]{:S(2)}, u32[]{:S(2)}) collective-permute-start(bf16[1024,2048]{1,0:T(8,128)(2,1)} %param.8), channel_id=1, source_target_pairs={{0,0},{1,1},{2,2},{3,3},{4,4},{5,5},{6,6},{7,7},{8,8},{9,9},{10,10... | collective-permute-start | bytes 12582920 | tf_op jit(solution)/shard_map/ppermute | solution.py:26
  33.7 6.8 %collective-permute-start.2 = (bf16[32,1024]{1,0:T(8,128)(2,1)S(1)}, bf16[32,1024]{1,0:T(8,128)(2,1)S(1)}, u32[]{:S(2)}, u32[]{:S(2)}) collective-permute-start(bf16[32,1024]{1,0:T(8,128)(2,1)S(1)} %get-tuple-element.32), channel_id=1, source_target_pairs={{0,1},{1,0},{2,3},{3,2},{4,5},{5,4},{6,7},{7,6},{8,9},{9,8},{10,11... | collective-permute-start | bytes 196616 | tf_op jit(solution)/shard_map/ppermute | solution.py:26
  33.7 8.5 %collective-permute-start.3 = (bf16[32,1024]{1,0:T(8,128)(2,1)S(1)}, bf16[32,1024]{1,0:T(8,128)(2,1)S(1)}, u32[]{:S(2)}, u32[]{:S(2)}) collective-permute-start(bf16[32,1024]{1,0:T(8,128)(2,1)S(1)} %get-tuple-element.33), channel_id=1, source_target_pairs={{0,2},{1,3},{2,0},{3,1},{4,6},{5,7},{6,4},{7,5},{8,10},{9,11},{10,... | collective-permute-start | bytes 196616 | tf_op jit(solution)/shard_map/ppermute | solution.py:26
  35.2 7.1 %collective-permute-start.4 = (bf16[32,1024]{1,0:T(8,128)(2,1)S(1)}, bf16[32,1024]{1,0:T(8,128)(2,1)S(1)}, u32[]{:S(2)}, u32[]{:S(2)}) collective-permute-start(bf16[32,1024]{1,0:T(8,128)(2,1)S(1)} %get-tuple-element.34), channel_id=1, source_target_pairs={{0,3},{1,2},{2,1},{3,0},{4,7},{5,6},{6,5},{7,4},{8,11},{9,10},{10,... | collective-permute-start | bytes 196616 | tf_op jit(solution)/shard_map/ppermute | solution.py:26
  43.2 9.7 %collective-permute-start.7 = (bf16[32,1024]{1,0:T(8,128)(2,1)S(1)}, bf16[32,1024]{1,0:T(8,128)(2,1)S(1)}, u32[]{:S(2)}, u32[]{:S(2)}) collective-permute-start(bf16[32,1024]{1,0:T(8,128)(2,1)S(1)} %get-tuple-element.35.in_ref.refs_0_), channel_id=1, source_target_pairs={{0,2},{1,3},{2,0},{3,1},{4,6},{5,7},{6,4},{7,5},{8,10},{9,11},{10,... | collective-permute-start | bytes 196616 | tf_op jit(solution)/shard_map/ppermute | solution.py:26
  44.7 8.2 %collective-permute-start.8 = (bf16[32,1024]{1,0:T(8,128)(2,1)S(1)}, bf16[32,1024]{1,0:T(8,128)(2,1)S(1)}, u32[]{:S(2)}, u32[]{:S(2)}) collective-permute-start(bf16[32,1024]{1,0:T(8,128)(2,1)S(1)} %get-tuple-element.35.in_ref.refs_0_), channel_id=1, source_target_pairs={{0,3},{1,2},{2,1},{3,0},{4,7},{5,6},{6,5},{7,4},{8,11},{9,10},{10,... | collective-permute-start | bytes 196616 | tf_op jit(solution)/shard_map/ppermute | solution.py:26
  46.9 4.6 %collective-permute-start.5 = (bf16[32,1024]{1,0:T(8,128)(2,1)S(1)}, bf16[32,1024]{1,0:T(8,128)(2,1)S(1)}, u32[]{:S(2)}, u32[]{:S(2)}) collective-permute-start(bf16[32,1024]{1,0:T(8,128)(2,1)S(1)} %repeat.3), channel_id=1, source_target_pairs={{0,1},{1,0},{2,3},{3,2},{4,5},{5,4},{6,7},{7,6},{8,9},{9,8},{10,11... | collective-permute-start | bytes 196616 | tf_op jit(solution)/shard_map/ppermute | solution.py:26
  52.5 5.5 %collective-permute-start.6 = (bf16[8,32,128]{2,1,0:T(8,128)(2,1)S(1)}, bf16[8,32,128]{2,1,0:T(8,128)(2,1)S(1)}, u32[]{:S(2)}, u32[]{:S(2)}) collective-permute-start(bf16[8,32,128]{2,1,0:T(8,128)(2,1)S(1)} %get-tuple-element.40), channel_id=1, source_target_pairs={{0,1},{1,0},{2,3},{3,2},{4,5},{5,4},{6,7},{7,6},{8,9},{9,8},{10,11... | collective-permute-start | bytes 196616 | tf_op jit(solution)/shard_map/ppermute | solution.py:26
  53.9 5.4 %collective-permute-start.9 = (bf16[8,32,128]{2,1,0:T(8,128)(2,1)S(1)}, bf16[8,32,128]{2,1,0:T(8,128)(2,1)S(1)}, u32[]{:S(2)}, u32[]{:S(2)}) collective-permute-start(bf16[8,32,128]{2,1,0:T(8,128)(2,1)S(1)} %get-tuple-element.41), channel_id=1, source_target_pairs={{0,2},{1,3},{2,0},{3,1},{4,6},{5,7},{6,4},{7,5},{8,10},{9,11},{10,... | collective-permute-start | bytes 196616 | tf_op jit(solution)/shard_map/ppermute | solution.py:26
  56.2 6.1 %collective-permute-start.10 = (bf16[8,32,128]{2,1,0:T(8,128)(2,1)S(1)}, bf16[8,32,128]{2,1,0:T(8,128)(2,1)S(1)}, u32[]{:S(2)}, u32[]{:S(2)}) collective-permute-start(bf16[8,32,128]{2,1,0:T(8,128)(2,1)S(1)} %get-tuple-element.42), channel_id=1, source_target_pairs={{0,3},{1,2},{2,1},{3,0},{4,7},{5,6},{6,5},{7,4},{8,11},{9,10},{10,... | collective-permute-start | bytes 196616 | tf_op jit(solution)/shard_map/ppermute | solution.py:26
  62.3 2.7 %collective-permute-start.11 = (bf16[9,32,128]{2,1,0:T(8,128)(2,1)S(1)}, bf16[9,32,128]{2,1,0:T(8,128)(2,1)S(1)}, u32[]{:S(2)}, u32[]{:S(2)}) collective-permute-start(bf16[9,32,128]{2,1,0:T(8,128)(2,1)S(1)} %repeat.4), channel_id=1, source_target_pairs={{0,4},{4,0},{8,12},{12,8},{1,5},{5,1},{9,13},{13,9},{2,6},{6,2},{1... | collective-permute-start | bytes 221192 | tf_op jit(solution)/shard_map/ppermute | solution.py:26
  62.4 5.1 %collective-permute-start.12 = (bf16[9,32,128]{2,1,0:T(8,128)(2,1)S(1)}, bf16[9,32,128]{2,1,0:T(8,128)(2,1)S(1)}, u32[]{:S(2)}, u32[]{:S(2)}) collective-permute-start(bf16[9,32,128]{2,1,0:T(8,128)(2,1)S(1)} %summed.1.in_ref.refs_0_), channel_id=1, source_target_pairs={{0,8},{4,12},{8,0},{12,4},{1,9},{5,13},{9,1},{13,5},{2,10},{6,14},... | collective-permute-start | bytes 221192 | tf_op jit(solution)/shard_map/ppermute | solution.py:26
  63.4 4.8 %collective-permute-start.13 = (bf16[9,32,128]{2,1,0:T(8,128)(2,1)S(1)}, bf16[9,32,128]{2,1,0:T(8,128)(2,1)S(1)}, u32[]{:S(2)}, u32[]{:S(2)}) collective-permute-start(bf16[9,32,128]{2,1,0:T(8,128)(2,1)S(1)} %summed.1.in_ref.refs_0_), channel_id=1, source_target_pairs={{0,12},{4,8},{8,4},{12,0},{1,13},{5,9},{9,5},{13,1},{2,14},{6,10},... | collective-permute-start | bytes 221192 | tf_op jit(solution)/shard_map/ppermute | solution.py:26
  68.2 10.4 %copy-start = (bf16[8,2,2048]{2,1,0:T(2,128)(2,1)S(1)}, bf16[8,2,2048]{2,1,0:T(2,128)(2,1)}, u32[]{:S(2)}) copy-start(bf16[8,2,2048]{2,1,0:T(2,128)(2,1)} %refs_4_.1) | copy-start | bytes 196612
  69.8 5.3 %collective-permute-start.14 = (bf16[16,2048]{1,0:T(8,128)(2,1)S(1)}, bf16[16,2048]{1,0:T(8,128)(2,1)S(1)}, u32[]{:S(2)}, u32[]{:S(2)}) collective-permute-start(bf16[16,2048]{1,0:T(8,128)(2,1)S(1)} %repeat.5), channel_id=1, source_target_pairs={{0,1},{1,0},{2,3},{3,2},{4,5},{5,4},{6,7},{7,6},{8,9},{9,8},{10,11... | collective-permute-start | bytes 196616 | tf_op jit(solution)/shard_map/ppermute | solution.py:26
  69.8 8.0 %collective-permute-start.15 = (bf16[16,2048]{1,0:T(8,128)(2,1)S(1)}, bf16[16,2048]{1,0:T(8,128)(2,1)S(1)}, u32[]{:S(2)}, u32[]{:S(2)}) collective-permute-start(bf16[16,2048]{1,0:T(8,128)(2,1)S(1)} %output.1.in_ref.refs_0_), channel_id=1, source_target_pairs={{0,2},{1,3},{2,0},{3,1},{4,6},{5,7},{6,4},{7,5},{8,10},{9,11},{10,... | collective-permute-start | bytes 196616 | tf_op jit(solution)/shard_map/ppermute | solution.py:26
  72.4 6.2 %collective-permute-start.16 = (bf16[16,2048]{1,0:T(8,128)(2,1)S(1)}, bf16[16,2048]{1,0:T(8,128)(2,1)S(1)}, u32[]{:S(2)}, u32[]{:S(2)}) collective-permute-start(bf16[16,2048]{1,0:T(8,128)(2,1)S(1)} %output.1.in_ref.refs_0_), channel_id=1, source_target_pairs={{0,3},{1,2},{2,1},{3,0},{4,7},{5,6},{6,5},{7,4},{8,11},{9,10},{10,... | collective-permute-start | bytes 196616 | tf_op jit(solution)/shard_map/ppermute | solution.py:26

commit v7 on v5

--- a/solution.py
+++ b/solution.py
@@ -20,20 +20,24 @@
 
 VMEM = pl.BlockSpec(memory_space=pltpu.VMEM)
 SMEM = pl.BlockSpec(memory_space=pltpu.SMEM)
-
-
-def pairs(value, axis, d):
-    return lax.ppermute(value, axis, [(i, i ^ d) for i in range(lax.axis_size(axis))])
+ANY = pl.BlockSpec(memory_space=pl.ANY)
+
+
+def partner(me, entry, size):
+    return me ^ ((size - entry) % size)
+
+
+def pairs(value, axis, entry):
+    size = lax.axis_size(axis)
+    return lax.ppermute(value, axis, [(i, partner(i, entry, size)) for i in range(size)])
 
 
 def exchange(chunks, axis):
-    got = {d: pairs(chunks[d], axis, d) for d in reversed(range(1, len(chunks)))}
-    return [chunks[0]] + [got[d] for d in range(1, len(chunks))]
+    return [chunks[0]] + [pairs(chunks[i], axis, i) for i in range(1, len(chunks))]
 
 
 def gather(value, axis):
-    size = lax.axis_size(axis)
-    return [value] + [pairs(value, axis, d) for d in range(1, size)]
+    return exchange([value] * lax.axis_size(axis), axis)
 
 
 def lane_freqs(rows):
@@ -102,13 +106,16 @@
     return jnp.concatenate([w_ref[rows, c : c + HD] for c in at], axis=1)
 
 
+PARTS = 4
+
+
 def load_kernel(pages, prompts, new_count, x_hbm, w_hbm, counts, tails, *refs):
     acc, x_ref, w_ref, cos_ref, sin_ref, cos_q, sin_q, meta, x_sems, w_sems = refs
     tokens, depth = x_ref.shape
-    half, tall = depth // 2, tokens // 2
+    size, tall = depth // PARTS, tokens // 2
     copies = []
-    for i in range(2):
-        at = pl.ds(i * half, half)
+    for i in range(PARTS):
+        at = pl.ds(i * size, size)
         x_copy = pltpu.make_async_copy(x_hbm.at[:, at], x_ref.at[:, at], x_sems.at[i])
         w_copy = pltpu.make_async_copy(w_hbm.at[at], w_ref.at[at], w_sems.at[i])
         x_copy.start()
@@ -120,17 +127,18 @@
     angles = by_row(len(spots), spots) * lane_freqs(len(spots))
     cos_q[...] = jnp.cos(angles)
     sin_q[...] = jnp.sin(angles) * sine_sign(len(spots))
-    for copy in copies[0]:
-        copy.wait()
-    rows = slice(0, half)
-    for pair in range(KVH // 2):
-        weight = pair_columns(w_ref, rows, pair, 0)
-        for start in range(0, tokens, tall):
-            at = slice(start, start + tall)
-            acc[at, 2 * pair * HD : 2 * (pair + 1) * HD] = jnp.dot(
-                x_ref[at, rows], weight, preferred_element_type=F32
-            )
-    for copy in copies[1]:
+    for i in range(PARTS - 1):
+        for copy in copies[i]:
+            copy.wait()
+        rows = slice(i * size, (i + 1) * size)
+        for pair in range(KVH // 2):
+            weight = pair_columns(w_ref, rows, pair, 0)
+            columns = slice(2 * pair * HD, 2 * (pair + 1) * HD)
+            for start in range(0, tokens, tall):
+                at = slice(start, start + tall)
+                product = jnp.dot(x_ref[at, rows], weight, preferred_element_type=F32)
+                acc[at, columns] = product if i == 0 else acc[at, columns] + product
+    for copy in copies[-1]:
         copy.wait()
 
 
@@ -153,10 +161,10 @@
             pltpu.VMEM((prompts * new_count, HD), F32),
             jax.ShapeDtypeStruct((3 * pages + prompts,), jnp.int32),
         ],
-        scratch_shapes=[pltpu.SemaphoreType.DMA((2,)), pltpu.SemaphoreType.DMA((2,))],
+        scratch_shapes=[pltpu.SemaphoreType.DMA((PARTS,)), pltpu.SemaphoreType.DMA((PARTS,))],
         compiler_params=pltpu.CompilerParams(vmem_limit_bytes=28 * MIB),
         cost_estimate=pl.CostEstimate(
-            flops=tokens * depth * KVH * HD,
+            flops=3 * tokens * depth // 2 * KVH * HD,
             bytes_accessed=2 * depth * (tokens + columns),
             transcendentals=0,
         ),
@@ -167,7 +175,7 @@
 def keys_kernel(acc, x_ref, w_ref, cos_ref, sin_ref, after, k_ref):
     tokens, depth = x_ref.shape
     tall = tokens // 2
-    rows = slice(depth // 2, depth)
+    rows = slice(depth - depth // PARTS, depth)
     for pair in range(KVH // 2):
         weight = pair_columns(w_ref, rows, pair, 0)
         columns = slice(2 * pair * HD, 2 * (pair + 1) * HD)
@@ -187,12 +195,12 @@
     tokens, depth = x.shape
     return pl.pallas_call(
         keys_kernel,
-        in_specs=[VMEM] * 5 + [pl.BlockSpec(memory_space=pl.ANY)],
+        in_specs=[VMEM] * 5 + [ANY],
         out_specs=VMEM,
         out_shape=pltpu.VMEM((tokens, KVH * HD), BF16),
         compiler_params=pltpu.CompilerParams(vmem_limit_bytes=24 * MIB),
         cost_estimate=pl.CostEstimate(
-            flops=tokens * depth * KVH * HD, bytes_accessed=8 * MIB, transcendentals=0
+            flops=tokens * depth // 2 * KVH * HD, bytes_accessed=8 * MIB, transcendentals=0
         ),
         name="keys",
     )(acc, x, weight, cosine, sine, after)
@@ -225,7 +233,7 @@
             VMEM,
             VMEM,
             pl.BlockSpec(memory_space=pltpu.HBM),
-            pl.BlockSpec(memory_space=pl.ANY),
+            ANY,
         ],
         out_specs=[VMEM, VMEM],
         out_shape=[
@@ -273,7 +281,7 @@
     n_tp = len(pieces)
     return pl.pallas_call(
         functools.partial(stacked_kernel, n_tp),
-        in_specs=[VMEM] * n_tp + [pl.BlockSpec(memory_space=pl.ANY)],
+        in_specs=[VMEM] * n_tp + [ANY],
         out_specs=VMEM,
         out_shape=jax.ShapeDtypeStruct((n_tp,) + pieces[0].shape, BF16),
         compiler_params=pltpu.CompilerParams(vmem_limit_bytes=8 * MIB),
@@ -284,8 +292,8 @@
 def scores_kernel(n_seq, n_tp, *refs):
     new = refs[:n_seq]
     k_ref, cos_q, sin_q, meta = refs[n_seq : n_seq + 4]
-    outs = refs[n_seq + 4 : n_seq + 4 + n_tp]
-    own_q, all_q, ready = refs[n_seq + 4 + n_tp :]
+    outs = refs[n_seq + 5 : n_seq + 5 + n_tp]
+    own_q, all_q, ready = refs[n_seq + 5 + n_tp :]
     kv_local = KVH // n_tp
     local_pages = k_ref.shape[0] // PAGE
     _, own_rows, new_count, _, _ = new[0].shape
@@ -297,7 +305,7 @@
     first = seq * local_pages
     for ds in range(n_seq):
         for rr in range(own_rows):
-            request = (seq ^ ds) * own_rows + rr
+            request = partner(seq, ds, n_seq) * own_rows + rr
             spots = [pl.ds(request * new_count + n, 1) for n in range(new_count)]
             turn = [(cos_q[spot], sin_q[spot]) for spot in spots]
             for dt in range(n_tp):
@@ -308,7 +316,7 @@
                         q = block[n][g * GROUP : (g + 1) * GROUP]
                         parts.append(q * turn[n][0] + pltpu.roll(q, HD // 2, 1) * turn[n][1])
                     part = jnp.concatenate(parts, axis=0).astype(BF16)
-                    at = ((me ^ dt) * kv_local + g) * rows
+                    at = (partner(me, dt, n_tp) * kv_local + g) * rows
                     all_q[request, pl.ds(pl.multiple_of(at, rows), rows)] = part
                     if dt == 0:
                         own_q[request, g * rows : (g + 1) * rows] = part
@@ -321,17 +329,17 @@
             s = lax.dot_general(q, k, (((1,), (1,)), ((), ())), preferred_element_type=F32)
             ready[head * rows : (head + 1) * rows, tokens] = (s * scale).astype(BF16)
     for d in range(n_tp):
-        outs[d][...] = ready[pl.ds(pl.multiple_of((me ^ d) * count, count), count)]
-
-
-def partial_scores(new, k, cos_q, sin_q, meta, prompts, n_tp):
+        outs[d][...] = ready[pl.ds(pl.multiple_of(partner(me, d, n_tp) * count, count), count)]
+
+
+def partial_scores(new, k, cos_q, sin_q, meta, after, prompts, n_tp):
     n_seq = len(new)
     new_count = new[0].shape[2]
     tokens = k.shape[0]
     rows = KVH // n_tp * new_count * GROUP
     return pl.pallas_call(
         functools.partial(scores_kernel, n_seq, n_tp),
-        in_specs=[VMEM] * (n_seq + 3) + [SMEM],
+        in_specs=[VMEM] * (n_seq + 3) + [SMEM, ANY],
         out_specs=[VMEM] * (n_tp + 1),
         out_shape=[jax.ShapeDtypeStruct((rows, tokens), BF16)] * n_tp
         + [jax.ShapeDtypeStruct((prompts, rows, HD), BF16)],
@@ -344,7 +352,7 @@
             flops=2 * tokens * rows * n_tp * HD, bytes_accessed=6 * MIB, transcendentals=0
         ),
         name="scores",
-    )(*new, k, cos_q, sin_q, meta)
+    )(*new, k, cos_q, sin_q, meta, after)
 
 
 def fresh_kernel(n_seq, *refs):
@@ -362,7 +370,7 @@
     found = [jnp.full((rows_local, HD), NEG, F32) for _ in range(new_count)]
     for ds in range(n_seq):
         for rr in range(own_rows):
-            request = (seq ^ ds) * own_rows + rr
+            request = partner(seq, ds, n_seq) * own_rows + rr
             q = q_ref[request].astype(F32)
             for n in range(new_count):
                 spot = pl.ds(request * new_count + n, 1)
@@ -403,7 +411,7 @@
 
 def weights_kernel(pages, prompts, n_tp, *refs):
     chunks = refs[:n_tp]
-    meta, w_ref, stats_ref = refs[n_tp:]
+    meta, _, w_ref, stats_ref = refs[n_tp:]
     rows, tokens = w_ref.shape
     local_pages = tokens // PAGE
     first = lax.axis_index("seq") * local_pages
@@ -443,12 +451,12 @@
     stats_ref[...] = jnp.where(quarter == 3, low, stats).astype(BF16)
 
 
-def softmax_weights(chunks, meta, pages, prompts):
+def softmax_weights(chunks, meta, after, pages, prompts):
     n_tp = len(chunks)
     rows, tokens = chunks[0].shape
     return pl.pallas_call(
         functools.partial(weights_kernel, pages, prompts, n_tp),
-        in_specs=[VMEM] * n_tp + [SMEM],
+        in_specs=[VMEM] * n_tp + [SMEM, ANY],
         out_specs=[VMEM, VMEM],
         out_shape=[
             jax.ShapeDtypeStruct((rows, tokens), BF16),
@@ -456,7 +464,7 @@
         ],
         compiler_params=pltpu.CompilerParams(vmem_limit_bytes=8 * MIB),
         name="weights",
-    )(*chunks, meta)
+    )(*chunks, meta, after)
 
 
 def weighted_kernel(n_tp, *refs):
@@ -470,7 +478,7 @@
     local_pages = tokens_here // PAGE
     first = lax.axis_index("seq") * local_pages
     me = lax.axis_index("tp")
-    own = [pl.ds(pl.multiple_of((me ^ d) * rows_local, rows_local), rows_local) for d in range(n_tp)]
+    own = [pl.ds(pl.multiple_of(partner(me, d, n_tp) * rows_local, rows_local), rows_local) for d in range(n_tp)]
     for d in range(n_tp):
         ready[own[d]] = pieces[d][...]
     total[...] = jnp.zeros_like(total)
@@ -631,12 +639,12 @@
     )
     new = stacked(new, meta)
     k = rotated_keys(acc, x, w, cosine, sine, new)
+    va, oa = project_values(x, w, out_weight, 0, new)
     new = gather(new, "seq")
-    *scores, own_q = partial_scores(new, k, cos_q, sin_q, meta, prompts, n_tp)
-    va, oa = project_values(x, w, out_weight, 0, own_q)
+    *scores, own_q = partial_scores(new, k, cos_q, sin_q, meta, va, prompts, n_tp)
+    vb, ob = project_values(x, w, out_weight, 1, own_q)
     fresh, values = fresh_scores(new, own_q, cos_q, sin_q)
-    weights, stats = softmax_weights(exchange(scores, "tp"), meta, pages, prompts)
-    vb, ob = project_values(x, w, out_weight, 1, stats)
+    weights, stats = softmax_weights(exchange(scores, "tp"), meta, vb, pages, prompts)
     chunks = weighted_values(gather(weights, "tp"), va, vb, meta, prompts)
     pieces = gather(summed(exchange(chunks, "tp"), stats), "seq")
     partial = output_partial(pieces, fresh, values, (oa, ob))

time: 68.8 us -> 68 us (0.988)
  waiting for transfers between devices: 20.1 us -> 18.7 us
  starting transfers between devices: 26.3 us -> 27.3 us
    ppermute x21, waiting for transfers between devices: 20.1 us -> 18.7 us  [pairs(): lax.ppermute(value, axis, [(i, partner(i, entry, size)) for i in range(si...]
    pallas_call x1, Pallas kernels: 2.74 us -> 1.63 us  [rotated_keys(): pl.pallas_call(keys_kernel, in_specs=[VMEM] * 5 + [ANY], out_specs=VMEM,...]
    ppermute x21, starting transfers between devices: 26.3 us -> 27.3 us  [pairs(): lax.ppermute(value, axis, [(i, partner(i, entry, size)) for i in range(si...]
  transfers between devices with their start and end apart: 21 -> 21, of which waited for: 14 -> 10; matrix products, arithmetic and copies ran while one was open for 0% -> 0% of each run, Pallas kernels for 22% -> 21%
where the time goes in v7:
time: 68 us; the launch traced here: 67.7 us
  starting transfers between devices  27.3 us (40%)
  Pallas kernels  21.5 us (32%)
  waiting for transfers between devices  18.7 us (28%)
    ppermute x21, starting transfers between devices, pairs(): lax.ppermute(value, axis, [(i, partner(i, entry, size)) for i in range(si...  27.3 us
    ppermute x21, waiting for transfers between devices, pairs(): lax.ppermute(value, axis, [(i, partner(i, entry, size)) for i in range(si...  18.7 us
    pallas_call x1, Pallas kernels, load(): pl.pallas_call(functools.partial(load_kernel, pages, prompts, new_count),...  7.16 us
    pallas_call x2, Pallas kernels, project_values(): pl.pallas_call(functools.partial(values_kernel, first), in_specs=[VMEM, V...  4.76 us
    pallas_call x1, Pallas kernels, partial_scores(): pl.pallas_call(functools.partial(scores_kernel, n_seq, n_tp), in_specs=[V...  1.88 us
    pallas_call x1, Pallas kernels, rotated_keys(): pl.pallas_call(keys_kernel, in_specs=[VMEM] * 5 + [ANY], out_specs=VMEM,...  1.63 us
    pallas_call x1, Pallas kernels, output_partial(): pl.pallas_call(functools.partial(output_kernel, n_seq), in_specs=[VMEM] *...  1.58 us
  transfers between devices with their start and end apart: 21, of which 10 were waited for; matrix products, arithmetic and copies ran while one was open for 0% of the time, Pallas kernels for 21%

profile of v7, /device:TPU:0, one launch (start us, length us, event | category | flops | bytes accessed | tf_op | source)
XLA Modules:
  0.0 67.7 jit_solution(14876818029066507350)
XLA Ops:
  0.0 0.7 %prepare.1.refs_0_ = bf16[2,2,20,128]{3,2,1,0:T(8,128)(2,1)S(1)} custom-call(bf16[2,2,2048]{2,1,0:T(2,128)(2,1)} %q_ref.1, bf16[2,2,512]{2,1,0:T(2,128)(2,1)} %kv_ref.1), custom_call_target="tpu_custom_call" | custom-call | bytes 1048576 | tf_op jit(solution)/shard_map/prepare/pallas_call | solution.py:264
  0.7 5.1 %collective-permute-start = (bf16[2,2,20,128]{3,2,1,0:T(8,128)(2,1)S(1)}, bf16[2,2,20,128]{3,2,1,0:T(8,128)(2,1)S(1)}, u32[]{:S(2)}, u32[]{:S(2)}) collective-permute-start(bf16[2,2,20,128]{3,2,1,0:T(8,128)(2,1)S(1)} %prepare.1.refs_0_), channel_id=1, source_target_pairs={{0,3},{1,2},{2,1},{3,0},{4,7},{5,6},{6,5},{7,4},{8,11},{9,10},{10,... | collective-permute-start | bytes 61448 | tf_op jit(solution)/shard_map/ppermute | solution.py:32
  6.5 7.2 %load.1 = (f32[1024,1024]{1,0:T(8,128)S(1)}, bf16[1024,2048]{1,0:T(8,128)(2,1)S(1)}, bf16[2048,2048]{1,0:T(8,128)(2,1)S(1)}, f32[1024,128]{1,0:T(8,128)S(1)}, f3...) custom-call(bf16[1024,2048]{1,0:T(8,128)(2,1)} %x_hbm.1, ...), custom_call_target="tpu_custom_call" | custom-call | flops 3221225472 | bytes 12582912 | tf_op jit(solution)/shard_map/load/pallas_call | solution.py:150
  14.2 1.4 %collective-permute-start.4 = (bf16[4,2,2,20,128]{4,3,2,1,0:T(8,128)(2,1)S(1)}, bf16[4,2,2,20,128]{4,3,2,1,0:T(8,128)(2,1)S(1)}, u32[]{:S(2)}, u32[]{:S(2)}) collective-permute-start(bf16[4,2,2,20,128]{4,3,2,1,0:T(8,128)(2,1)S(1)} %stacked.1.after.refs_0_), channel_id=1, source_target_pairs={{0,8},{4,12},{8,0},{12,4},{1,9},{5,13},{9,1},{13,5},{2,10},{6,14},... | collective-permute-start | bytes 245768 | tf_op jit(solution)/shard_map/ppermute | solution.py:32
  15.7 2.4 %values.2 = (bf16[1024,512]{1,0:T(8,128)(2,1)S(1)}, bf16[1024,2048]{1,0:T(8,128)(2,1)S(1)}) custom-call(bf16[1024,2048]{1,0:T(8,128)(2,1)S(1)} %get-tuple-element.32.x_ref, bf16[2048,2048]{1,0:T(8,128)(2,1)S(1)} %get-tuple-element.33.w_ref, bf16[2048,2048]{1,0:T(8,128)(2,1)} %o_hbm.3, bf16[4,2,2,20,128]{4,3,2,1,0:T(8,128)(2,1)S(1)} %stacked.1.after.refs_0_), custom_call_target="tpu_custom_call" | custom-call | flops 2147483648 | bytes 8388608 | tf_op jit(solution)/shard_map/values/pallas_call | solution.py:230
  18.0 1.6 %keys.1.refs_4_ = bf16[1024,1024]{1,0:T(8,128)(2,1)S(1)} custom-call(f32[1024,1024]{1,0:T(8,128)S(1)} %get-tuple-element.31.acc, bf16[1024,2048]{1,0:T(8,128)(2,1)S(1)} %get-tuple-element.32.x_ref, bf16[2048,2048]{1,0:T(8,128)(2,1)S(1)} %get-tuple-element.33.w_ref, f32[1024,128]{1,0:T(8,128)S(1)} %get-tuple-element.34.cos_ref, ...), custom_call_target="tpu_custom_call" | custom-call | flops 1073741824 | bytes 8388608 | tf_op jit(solution)/shard_map/keys/pallas_call | solution.py:196
  19.7 1.3 %collective-permute-done.4.refs_2_ = bf16[4,2,2,20,128]{4,3,2,1,0:T(8,128)(2,1)S(1)} collective-permute-done((bf16[4,2,2,20,128]{4,3,2,1,0:T(8,128)(2,1)S(1)}, bf16[4,2,2,20,128]{4,3,2,1,0:T(8,128)(2,1)S(1)}, u32[]{:S(2)}, u32[]{:S(2)}) %collective-permute-start.4) | collective-permute-done | bytes 81952 | tf_op jit(solution)/shard_map/ppermute | solution.py:32
  21.0 1.9 %scores.1 = (bf16[32,1024]{1,0:T(8,128)(2,1)S(1)}, bf16[32,1024]{1,0:T(8,128)(2,1)S(1)}, bf16[32,1024]{1,0:T(8,128)(2,1)S(1)}, bf16[32,1024]{1,0:T(8,128)(2,1)S(1)}, bf16[8,32,128]{2,1,0:T(8,128)(2,1)S(1)}) custom-call(bf16[4,2,2,20,128]{4,3,2,1,0:T(8,128)(2,1)S(1)} %stacked.1.after.refs_0_, bf16[4,2,2,20,128]{4,3,2,1,0:T(8,128)(2,1)S(1)} %collective-permute-done.3.refs_1_, ...), custom_call_target="tpu_custom_call" | custom-call | flops 33554432 | bytes 6291456 | tf_op jit(solution)/shard_map/scores/pallas_call | solution.py:340
  22.9 3.8 %collective-permute-start.6 = (bf16[32,1024]{1,0:T(8,128)(2,1)S(1)}, bf16[32,1024]{1,0:T(8,128)(2,1)S(1)}, u32[]{:S(2)}, u32[]{:S(2)}) collective-permute-start(bf16[32,1024]{1,0:T(8,128)(2,1)S(1)} %get-tuple-element.40), channel_id=1, source_target_pairs={{0,3},{1,2},{2,1},{3,0},{4,7},{5,6},{6,5},{7,4},{8,11},{9,10},{10,... | collective-permute-start | bytes 196616 | tf_op jit(solution)/shard_map/ppermute | solution.py:32
  27.3 2.4 %values.3 = (bf16[1024,512]{1,0:T(8,128)(2,1)S(1)}, bf16[1024,2048]{1,0:T(8,128)(2,1)S(1)}) custom-call(bf16[1024,2048]{1,0:T(8,128)(2,1)S(1)} %get-tuple-element.32.x_ref, bf16[2048,2048]{1,0:T(8,128)(2,1)S(1)} %get-tuple-element.33.w_ref, bf16[2048,2048]{1,0:T(8,128)(2,1)} %o_hbm.3, bf16[8,32,128]{2,1,0:T(8,128)(2,1)S(1)} %get-tuple-element.43.after.refs_4_), custom_call_target="tpu_custom_call" | custom-call | flops 2147483648 | bytes 8388608 | tf_op jit(solution)/shard_map/values/pallas_call | solution.py:230
  29.7 2.6 %collective-permute-done.7.refs_2_ = bf16[32,1024]{1,0:T(8,128)(2,1)S(1)} collective-permute-done((bf16[32,1024]{1,0:T(8,128)(2,1)S(1)}, bf16[32,1024]{1,0:T(8,128)(2,1)S(1)}, u32[]{:S(2)}, u32[]{:S(2)}) %collective-permute-start.7) | collective-permute-done | bytes 65568 | tf_op jit(solution)/shard_map/ppermute | solution.py:32
  32.4 0.9 %weights.1 = (bf16[32,1024]{1,0:T(8,128)(2,1)S(1)}, bf16[32,128]{1,0:T(8,128)(2,1)S(1)}) custom-call(bf16[32,1024]{1,0:T(8,128)(2,1)S(1)} %get-tuple-element.39.refs_0_, bf16[32,1024]{1,0:T(8,128)(2,1)S(1)} %collective-permute-done.6.refs_1_, bf16[32,1024]{1,0:T(8,128)(2,1)S(1)} %collective-permute-done.7.refs_2_, ...), custom_call_target="tpu_custom_call" | custom-call | tf_op jit(solution)/shard_map/weights/pallas_call | solution.py:457
  33.3 1.5 %collective-permute-start.10 = (bf16[32,1024]{1,0:T(8,128)(2,1)S(1)}, bf16[32,1024]{1,0:T(8,128)(2,1)S(1)}, u32[]{:S(2)}, u32[]{:S(2)}) collective-permute-start(bf16[32,1024]{1,0:T(8,128)(2,1)S(1)} %get-tuple-element.45.refs_0_), channel_id=1, source_target_pairs={{0,2},{1,3},{2,0},{3,1},{4,6},{5,7},{6,4},{7,5},{8,10},{9,11},{10,... | collective-permute-start | bytes 196616 | tf_op jit(solution)/shard_map/ppermute | solution.py:32
  34.8 1.3 %collective-permute-start.11 = (bf16[32,1024]{1,0:T(8,128)(2,1)S(1)}, bf16[32,1024]{1,0:T(8,128)(2,1)S(1)}, u32[]{:S(2)}, u32[]{:S(2)}) collective-permute-start(bf16[32,1024]{1,0:T(8,128)(2,1)S(1)} %get-tuple-element.45.refs_0_), channel_id=1, source_target_pairs={{0,1},{1,0},{2,3},{3,2},{4,5},{5,4},{6,7},{7,6},{8,9},{9,8},{10,11... | collective-permute-start | bytes 196616 | tf_op jit(solution)/shard_map/ppermute | solution.py:32
  36.1 1.6 %collective-permute-start.9 = (bf16[32,1024]{1,0:T(8,128)(2,1)S(1)}, bf16[32,1024]{1,0:T(8,128)(2,1)S(1)}, u32[]{:S(2)}, u32[]{:S(2)}) collective-permute-start(bf16[32,1024]{1,0:T(8,128)(2,1)S(1)} %get-tuple-element.45.refs_0_), channel_id=1, source_target_pairs={{0,3},{1,2},{2,1},{3,0},{4,7},{5,6},{6,5},{7,4},{8,11},{9,10},{10,... | collective-permute-start | bytes 196616 | tf_op jit(solution)/shard_map/ppermute | solution.py:32
  37.7 2.6 %collective-permute-done.10.refs_2_ = bf16[32,1024]{1,0:T(8,128)(2,1)S(1)} collective-permute-done((bf16[32,1024]{1,0:T(8,128)(2,1)S(1)}, bf16[32,1024]{1,0:T(8,128)(2,1)S(1)}, u32[]{:S(2)}, u32[]{:S(2)}) %collective-permute-start.10) | collective-permute-done | bytes 65568 | tf_op jit(solution)/shard_map/ppermute | solution.py:32
  40.3 1.9 %collective-permute-done.9.refs_1_ = bf16[32,1024]{1,0:T(8,128)(2,1)S(1)} collective-permute-done((bf16[32,1024]{1,0:T(8,128)(2,1)S(1)}, bf16[32,1024]{1,0:T(8,128)(2,1)S(1)}, u32[]{:S(2)}, u32[]{:S(2)}) %collective-permute-start.9) | collective-permute-done | bytes 65568 | tf_op jit(solution)/shard_map/ppermute | solution.py:32
  42.2 1.3 %weighted.1 = (bf16[8,32,128]{2,1,0:T(8,128)(2,1)S(1)}, bf16[8,32,128]{2,1,0:T(8,128)(2,1)S(1)}, bf16[8,32,128]{2,1,0:T(8,128)(2,1)S(1)}, bf16[8,32,128]{2,1,0:T(8,128)(2,1)S(1)}) custom-call(bf16[32,1024]{1,0:T(8,128)(2,1)S(1)} %get-tuple-element.45.refs_0_, bf16[32,1024]{1,0:T(8,128)(2,1)S(1)} %collective-permute-done.9.refs_1_, ...), custom_call_target="tpu_custom_call" | custom-call | flops 33554432 | bytes 8388608 | tf_op jit(solution)/shard_map/weighted/pallas_call | solution.py:501
  43.4 1.6 %collective-permute-start.12 = (bf16[8,32,128]{2,1,0:T(8,128)(2,1)S(1)}, bf16[8,32,128]{2,1,0:T(8,128)(2,1)S(1)}, u32[]{:S(2)}, u32[]{:S(2)}) collective-permute-start(bf16[8,32,128]{2,1,0:T(8,128)(2,1)S(1)} %get-tuple-element.47), channel_id=1, source_target_pairs={{0,3},{1,2},{2,1},{3,0},{4,7},{5,6},{6,5},{7,4},{8,11},{9,10},{10,... | collective-permute-start | bytes 196616 | tf_op jit(solution)/shard_map/ppermute | solution.py:32
  45.1 2.8 %collective-permute-start.14 = (bf16[8,32,128]{2,1,0:T(8,128)(2,1)S(1)}, bf16[8,32,128]{2,1,0:T(8,128)(2,1)S(1)}, u32[]{:S(2)}, u32[]{:S(2)}) collective-permute-start(bf16[8,32,128]{2,1,0:T(8,128)(2,1)S(1)} %get-tuple-element.49), channel_id=1, source_target_pairs={{0,1},{1,0},{2,3},{3,2},{4,5},{5,4},{6,7},{7,6},{8,9},{9,8},{10,11... | collective-permute-start | bytes 196616 | tf_op jit(solution)/shard_map/ppermute | solution.py:32
  47.9 1.7 %collective-permute-done.12.refs_1_ = bf16[8,32,128]{2,1,0:T(8,128)(2,1)S(1)} collective-permute-done((bf16[8,32,128]{2,1,0:T(8,128)(2,1)S(1)}, bf16[8,32,128]{2,1,0:T(8,128)(2,1)S(1)}, u32[]{:S(2)}, u32[]{:S(2)}) %collective-permute-start.12) | collective-permute-done | bytes 65568 | tf_op jit(solution)/shard_map/ppermute | solution.py:32
  49.7 1.4 %collective-permute-done.13.refs_2_ = bf16[8,32,128]{2,1,0:T(8,128)(2,1)S(1)} collective-permute-done((bf16[8,32,128]{2,1,0:T(8,128)(2,1)S(1)}, bf16[8,32,128]{2,1,0:T(8,128)(2,1)S(1)}, u32[]{:S(2)}, u32[]{:S(2)}) %collective-permute-start.13) | collective-permute-done | bytes 65568 | tf_op jit(solution)/shard_map/ppermute | solution.py:32
  51.8 1.2 %collective-permute-start.17 = (bf16[9,32,128]{2,1,0:T(8,128)(2,1)S(1)}, bf16[9,32,128]{2,1,0:T(8,128)(2,1)S(1)}, u32[]{:S(2)}, u32[]{:S(2)}) collective-permute-start(bf16[9,32,128]{2,1,0:T(8,128)(2,1)S(1)} %summed.1.refs_0_), channel_id=1, source_target_pairs={{0,4},{4,0},{8,12},{12,8},{1,5},{5,1},{9,13},{13,9},{2,6},{6,2},{1... | collective-permute-start | bytes 221192 | tf_op jit(solution)/shard_map/ppermute | solution.py:32
  53.0 0.8 %fresh.1 = (f32[2,32,128]{2,1,0:T(8,128)S(1)}, f32[16,32,128]{2,1,0:T(8,128)S(1)}) custom-call(bf16[4,2,2,20,128]{4,3,2,1,0:T(8,128)(2,1)S(1)} %stacked.1.after.refs_0_, bf16[4,2,2,20,128]{4,3,2,1,0:T(8,128)(2,1)S(1)} %collective-permute-done.3.refs_1_, bf16[4,2,2,20,128]{4,3,2,1,0:T(8,128)(2,1)S(1)} %collective-permute-done.4.refs_2_, ...), custom_call_target="tpu_custom_call" | custom-call | bytes 2097152 | tf_op jit(solution)/shard_map/fresh/pallas_call | solution.py:398
  53.8 1.3 %collective-permute-done.15.refs_1_ = bf16[9,32,128]{2,1,0:T(8,128)(2,1)S(1)} collective-permute-done((bf16[9,32,128]{2,1,0:T(8,128)(2,1)S(1)}, bf16[9,32,128]{2,1,0:T(8,128)(2,1)S(1)}, u32[]{:S(2)}, u32[]{:S(2)}) %collective-permute-start.15) | collective-permute-done | bytes 73760 | tf_op jit(solution)/shard_map/ppermute | solution.py:32
  55.1 1.2 %collective-permute-done.16.refs_2_ = bf16[9,32,128]{2,1,0:T(8,128)(2,1)S(1)} collective-permute-done((bf16[9,32,128]{2,1,0:T(8,128)(2,1)S(1)}, bf16[9,32,128]{2,1,0:T(8,128)(2,1)S(1)}, u32[]{:S(2)}, u32[]{:S(2)}) %collective-permute-start.16) | collective-permute-done | bytes 73760 | tf_op jit(solution)/shard_map/ppermute | solution.py:32
  56.3 1.6 %output.1.refs_0_ = bf16[16,2048]{1,0:T(8,128)(2,1)S(1)} custom-call(bf16[9,32,128]{2,1,0:T(8,128)(2,1)S(1)} %summed.1.refs_0_, bf16[9,32,128]{2,1,0:T(8,128)(2,1)S(1)} %collective-permute-done.15.refs_1_, bf16[9,32,128]{2,1,0:T(8,128)(2,1)S(1)} %collective-permute-done.16.refs_2_, bf16[9,32,128]{2,1,0:T(8,128)(2,1)S(1)} %collective-permute-done.17.refs_3_, ...), custom_call_target="tpu_custom_call" | custom-call | tf_op jit(solution)/shard_map/output/pallas_call | solution.py:595
  57.9 1.8 %collective-permute-start.18 = (bf16[16,2048]{1,0:T(8,128)(2,1)S(1)}, bf16[16,2048]{1,0:T(8,128)(2,1)S(1)}, u32[]{:S(2)}, u32[]{:S(2)}) collective-permute-start(bf16[16,2048]{1,0:T(8,128)(2,1)S(1)} %output.1.refs_0_), channel_id=1, source_target_pairs={{0,3},{1,2},{2,1},{3,0},{4,7},{5,6},{6,5},{7,4},{8,11},{9,10},{10,... | collective-permute-start | bytes 196616 | tf_op jit(solution)/shard_map/ppermute | solution.py:32
  59.7 0.8 %collective-permute-start.19 = (bf16[16,2048]{1,0:T(8,128)(2,1)S(1)}, bf16[16,2048]{1,0:T(8,128)(2,1)S(1)}, u32[]{:S(2)}, u32[]{:S(2)}) collective-permute-start(bf16[16,2048]{1,0:T(8,128)(2,1)S(1)} %output.1.refs_0_), channel_id=1, source_target_pairs={{0,2},{1,3},{2,0},{3,1},{4,6},{5,7},{6,4},{7,5},{8,10},{9,11},{10,... | collective-permute-start | bytes 196616 | tf_op jit(solution)/shard_map/ppermute | solution.py:32
  60.5 1.8 %collective-permute-start.20 = (bf16[16,2048]{1,0:T(8,128)(2,1)S(1)}, bf16[16,2048]{1,0:T(8,128)(2,1)S(1)}, u32[]{:S(2)}, u32[]{:S(2)}) collective-permute-start(bf16[16,2048]{1,0:T(8,128)(2,1)S(1)} %output.1.refs_0_), channel_id=1, source_target_pairs={{0,1},{1,0},{2,3},{3,2},{4,5},{5,4},{6,7},{7,6},{8,9},{9,8},{10,11... | collective-permute-start | bytes 196616 | tf_op jit(solution)/shard_map/ppermute | solution.py:32
  62.3 2.4 %collective-permute-done.18.refs_1_ = bf16[16,2048]{1,0:T(8,128)(2,1)S(1)} collective-permute-done((bf16[16,2048]{1,0:T(8,128)(2,1)S(1)}, bf16[16,2048]{1,0:T(8,128)(2,1)S(1)}, u32[]{:S(2)}, u32[]{:S(2)}) %collective-permute-start.18) | collective-permute-done | bytes 65568 | tf_op jit(solution)/shard_map/ppermute | solution.py:32
  64.7 2.3 %collective-permute-done.19.refs_2_ = bf16[16,2048]{1,0:T(8,128)(2,1)S(1)} collective-permute-done((bf16[16,2048]{1,0:T(8,128)(2,1)S(1)}, bf16[16,2048]{1,0:T(8,128)(2,1)S(1)}, u32[]{:S(2)}, u32[]{:S(2)}) %collective-permute-start.19) | collective-permute-done | bytes 65568 | tf_op jit(solution)/shard_map/ppermute | solution.py:32
  (25 shorter events, 3.4 us)
Async XLA Ops:
  0.7 12.9 %collective-permute-start = (bf16[2,2,20,128]{3,2,1,0:T(8,128)(2,1)S(1)}, bf16[2,2,20,128]{3,2,1,0:T(8,128)(2,1)S(1)}, u32[]{:S(2)}, u32[]{:S(2)}) collective-permute-start(bf16[2,2,20,128]{3,2,1,0:T(8,128)(2,1)S(1)} %prepare.1.refs_0_), channel_id=1, source_target_pairs={{0,3},{1,2},{2,1},{3,0},{4,7},{5,6},{6,5},{7,4},{8,11},{9,10},{10,... | collective-permute-start | bytes 61448 | tf_op jit(solution)/shard_map/ppermute | solution.py:32
  5.9 7.8 %collective-permute-start.1 = (bf16[2,2,20,128]{3,2,1,0:T(8,128)(2,1)S(1)}, bf16[2,2,20,128]{3,2,1,0:T(8,128)(2,1)S(1)}, u32[]{:S(2)}, u32[]{:S(2)}) collective-permute-start(bf16[2,2,20,128]{3,2,1,0:T(8,128)(2,1)S(1)} %prepare.1.refs_0_), channel_id=1, source_target_pairs={{0,2},{1,3},{2,0},{3,1},{4,6},{5,7},{6,4},{7,5},{8,10},{9,11},{10,... | collective-permute-start | bytes 61448 | tf_op jit(solution)/shard_map/ppermute | solution.py:32
  5.9 7.8 %collective-permute-start.2 = (bf16[2,2,20,128]{3,2,1,0:T(8,128)(2,1)S(1)}, bf16[2,2,20,128]{3,2,1,0:T(8,128)(2,1)S(1)}, u32[]{:S(2)}, u32[]{:S(2)}) collective-permute-start(bf16[2,2,20,128]{3,2,1,0:T(8,128)(2,1)S(1)} %prepare.1.refs_0_), channel_id=1, source_target_pairs={{0,1},{1,0},{2,3},{3,2},{4,5},{5,4},{6,7},{7,6},{8,9},{9,8},{10,11... | collective-permute-start | bytes 61448 | tf_op jit(solution)/shard_map/ppermute | solution.py:32
  13.7 5.9 %collective-permute-start.3 = (bf16[4,2,2,20,128]{4,3,2,1,0:T(8,128)(2,1)S(1)}, bf16[4,2,2,20,128]{4,3,2,1,0:T(8,128)(2,1)S(1)}, u32[]{:S(2)}, u32[]{:S(2)}) collective-permute-start(bf16[4,2,2,20,128]{4,3,2,1,0:T(8,128)(2,1)S(1)} %stacked.1.after.refs_0_), channel_id=1, source_target_pairs={{0,12},{4,8},{8,4},{12,0},{1,13},{5,9},{9,5},{13,1},{2,14},{6,10},... | collective-permute-start | bytes 245768 | tf_op jit(solution)/shard_map/ppermute | solution.py:32
  14.2 6.8 %collective-permute-start.4 = (bf16[4,2,2,20,128]{4,3,2,1,0:T(8,128)(2,1)S(1)}, bf16[4,2,2,20,128]{4,3,2,1,0:T(8,128)(2,1)S(1)}, u32[]{:S(2)}, u32[]{:S(2)}) collective-permute-start(bf16[4,2,2,20,128]{4,3,2,1,0:T(8,128)(2,1)S(1)} %stacked.1.after.refs_0_), channel_id=1, source_target_pairs={{0,8},{4,12},{8,0},{12,4},{1,9},{5,13},{9,1},{13,5},{2,10},{6,14},... | collective-permute-start | bytes 245768 | tf_op jit(solution)/shard_map/ppermute | solution.py:32
  15.6 5.4 %collective-permute-start.5 = (bf16[4,2,2,20,128]{4,3,2,1,0:T(8,128)(2,1)S(1)}, bf16[4,2,2,20,128]{4,3,2,1,0:T(8,128)(2,1)S(1)}, u32[]{:S(2)}, u32[]{:S(2)}) collective-permute-start(bf16[4,2,2,20,128]{4,3,2,1,0:T(8,128)(2,1)S(1)} %stacked.1.after.refs_0_), channel_id=1, source_target_pairs={{0,4},{4,0},{8,12},{12,8},{1,5},{5,1},{9,13},{13,9},{2,6},{6,2},{1... | collective-permute-start | bytes 245768 | tf_op jit(solution)/shard_map/ppermute | solution.py:32
  22.9 6.8 %collective-permute-start.6 = (bf16[32,1024]{1,0:T(8,128)(2,1)S(1)}, bf16[32,1024]{1,0:T(8,128)(2,1)S(1)}, u32[]{:S(2)}, u32[]{:S(2)}) collective-permute-start(bf16[32,1024]{1,0:T(8,128)(2,1)S(1)} %get-tuple-element.40), channel_id=1, source_target_pairs={{0,3},{1,2},{2,1},{3,0},{4,7},{5,6},{6,5},{7,4},{8,11},{9,10},{10,... | collective-permute-start | bytes 196616 | tf_op jit(solution)/shard_map/ppermute | solution.py:32
  26.7 5.7 %collective-permute-start.7 = (bf16[32,1024]{1,0:T(8,128)(2,1)S(1)}, bf16[32,1024]{1,0:T(8,128)(2,1)S(1)}, u32[]{:S(2)}, u32[]{:S(2)}) collective-permute-start(bf16[32,1024]{1,0:T(8,128)(2,1)S(1)} %get-tuple-element.41), channel_id=1, source_target_pairs={{0,2},{1,3},{2,0},{3,1},{4,6},{5,7},{6,4},{7,5},{8,10},{9,11},{10,... | collective-permute-start | bytes 196616 | tf_op jit(solution)/shard_map/ppermute | solution.py:32
  26.7 5.7 %collective-permute-start.8 = (bf16[32,1024]{1,0:T(8,128)(2,1)S(1)}, bf16[32,1024]{1,0:T(8,128)(2,1)S(1)}, u32[]{:S(2)}, u32[]{:S(2)}) collective-permute-start(bf16[32,1024]{1,0:T(8,128)(2,1)S(1)} %get-tuple-element.42), channel_id=1, source_target_pairs={{0,1},{1,0},{2,3},{3,2},{4,5},{5,4},{6,7},{7,6},{8,9},{9,8},{10,11... | collective-permute-start | bytes 196616 | tf_op jit(solution)/shard_map/ppermute | solution.py:32
  33.3 7.0 %collective-permute-start.10 = (bf16[32,1024]{1,0:T(8,128)(2,1)S(1)}, bf16[32,1024]{1,0:T(8,128)(2,1)S(1)}, u32[]{:S(2)}, u32[]{:S(2)}) collective-permute-start(bf16[32,1024]{1,0:T(8,128)(2,1)S(1)} %get-tuple-element.45.refs_0_), channel_id=1, source_target_pairs={{0,2},{1,3},{2,0},{3,1},{4,6},{5,7},{6,4},{7,5},{8,10},{9,11},{10,... | collective-permute-start | bytes 196616 | tf_op jit(solution)/shard_map/ppermute | solution.py:32
  34.8 5.5 %collective-permute-start.11 = (bf16[32,1024]{1,0:T(8,128)(2,1)S(1)}, bf16[32,1024]{1,0:T(8,128)(2,1)S(1)}, u32[]{:S(2)}, u32[]{:S(2)}) collective-permute-start(bf16[32,1024]{1,0:T(8,128)(2,1)S(1)} %get-tuple-element.45.refs_0_), channel_id=1, source_target_pairs={{0,1},{1,0},{2,3},{3,2},{4,5},{5,4},{6,7},{7,6},{8,9},{9,8},{10,11... | collective-permute-start | bytes 196616 | tf_op jit(solution)/shard_map/ppermute | solution.py:32
  36.1 6.1 %collective-permute-start.9 = (bf16[32,1024]{1,0:T(8,128)(2,1)S(1)}, bf16[32,1024]{1,0:T(8,128)(2,1)S(1)}, u32[]{:S(2)}, u32[]{:S(2)}) collective-permute-start(bf16[32,1024]{1,0:T(8,128)(2,1)S(1)} %get-tuple-element.45.refs_0_), channel_id=1, source_target_pairs={{0,3},{1,2},{2,1},{3,0},{4,7},{5,6},{6,5},{7,4},{8,11},{9,10},{10,... | collective-permute-start | bytes 196616 | tf_op jit(solution)/shard_map/ppermute | solution.py:32
  43.4 6.2 %collective-permute-start.12 = (bf16[8,32,128]{2,1,0:T(8,128)(2,1)S(1)}, bf16[8,32,128]{2,1,0:T(8,128)(2,1)S(1)}, u32[]{:S(2)}, u32[]{:S(2)}) collective-permute-start(bf16[8,32,128]{2,1,0:T(8,128)(2,1)S(1)} %get-tuple-element.47), channel_id=1, source_target_pairs={{0,3},{1,2},{2,1},{3,0},{4,7},{5,6},{6,5},{7,4},{8,11},{9,10},{10,... | collective-permute-start | bytes 196616 | tf_op jit(solution)/shard_map/ppermute | solution.py:32
  45.1 6.0 %collective-permute-start.13 = (bf16[8,32,128]{2,1,0:T(8,128)(2,1)S(1)}, bf16[8,32,128]{2,1,0:T(8,128)(2,1)S(1)}, u32[]{:S(2)}, u32[]{:S(2)}) collective-permute-start(bf16[8,32,128]{2,1,0:T(8,128)(2,1)S(1)} %get-tuple-element.48), channel_id=1, source_target_pairs={{0,2},{1,3},{2,0},{3,1},{4,6},{5,7},{6,4},{7,5},{8,10},{9,11},{10,... | collective-permute-start | bytes 196616 | tf_op jit(solution)/shard_map/ppermute | solution.py:32
  45.1 6.0 %collective-permute-start.14 = (bf16[8,32,128]{2,1,0:T(8,128)(2,1)S(1)}, bf16[8,32,128]{2,1,0:T(8,128)(2,1)S(1)}, u32[]{:S(2)}, u32[]{:S(2)}) collective-permute-start(bf16[8,32,128]{2,1,0:T(8,128)(2,1)S(1)} %get-tuple-element.49), channel_id=1, source_target_pairs={{0,1},{1,0},{2,3},{3,2},{4,5},{5,4},{6,7},{7,6},{8,9},{9,8},{10,11... | collective-permute-start | bytes 196616 | tf_op jit(solution)/shard_map/ppermute | solution.py:32
  51.1 4.0 %collective-permute-start.15 = (bf16[9,32,128]{2,1,0:T(8,128)(2,1)S(1)}, bf16[9,32,128]{2,1,0:T(8,128)(2,1)S(1)}, u32[]{:S(2)}, u32[]{:S(2)}) collective-permute-start(bf16[9,32,128]{2,1,0:T(8,128)(2,1)S(1)} %summed.1.refs_0_), channel_id=1, source_target_pairs={{0,12},{4,8},{8,4},{12,0},{1,13},{5,9},{9,5},{13,1},{2,14},{6,10},... | collective-permute-start | bytes 221192 | tf_op jit(solution)/shard_map/ppermute | solution.py:32
  51.2 5.2 %collective-permute-start.16 = (bf16[9,32,128]{2,1,0:T(8,128)(2,1)S(1)}, bf16[9,32,128]{2,1,0:T(8,128)(2,1)S(1)}, u32[]{:S(2)}, u32[]{:S(2)}) collective-permute-start(bf16[9,32,128]{2,1,0:T(8,128)(2,1)S(1)} %summed.1.refs_0_), channel_id=1, source_target_pairs={{0,8},{4,12},{8,0},{12,4},{1,9},{5,13},{9,1},{13,5},{2,10},{6,14},... | collective-permute-start | bytes 221192 | tf_op jit(solution)/shard_map/ppermute | solution.py:32
  51.8 4.5 %collective-permute-start.17 = (bf16[9,32,128]{2,1,0:T(8,128)(2,1)S(1)}, bf16[9,32,128]{2,1,0:T(8,128)(2,1)S(1)}, u32[]{:S(2)}, u32[]{:S(2)}) collective-permute-start(bf16[9,32,128]{2,1,0:T(8,128)(2,1)S(1)} %summed.1.refs_0_), channel_id=1, source_target_pairs={{0,4},{4,0},{8,12},{12,8},{1,5},{5,1},{9,13},{13,9},{2,6},{6,2},{1... | collective-permute-start | bytes 221192 | tf_op jit(solution)/shard_map/ppermute | solution.py:32
  56.3 10.6 %copy-start = (bf16[8,2,2048]{2,1,0:T(2,128)(2,1)S(1)}, bf16[8,2,2048]{2,1,0:T(2,128)(2,1)}, u32[]{:S(2)}) copy-start(bf16[8,2,2048]{2,1,0:T(2,128)(2,1)} %refs_4_.1) | copy-start | bytes 196612
  57.9 6.8 %collective-permute-start.18 = (bf16[16,2048]{1,0:T(8,128)(2,1)S(1)}, bf16[16,2048]{1,0:T(8,128)(2,1)S(1)}, u32[]{:S(2)}, u32[]{:S(2)}) collective-permute-start(bf16[16,2048]{1,0:T(8,128)(2,1)S(1)} %output.1.refs_0_), channel_id=1, source_target_pairs={{0,3},{1,2},{2,1},{3,0},{4,7},{5,6},{6,5},{7,4},{8,11},{9,10},{10,... | collective-permute-start | bytes 196616 | tf_op jit(solution)/shard_map/ppermute | solution.py:32
  59.7 7.3 %collective-permute-start.19 = (bf16[16,2048]{1,0:T(8,128)(2,1)S(1)}, bf16[16,2048]{1,0:T(8,128)(2,1)S(1)}, u32[]{:S(2)}, u32[]{:S(2)}) collective-permute-start(bf16[16,2048]{1,0:T(8,128)(2,1)S(1)} %output.1.refs_0_), channel_id=1, source_target_pairs={{0,2},{1,3},{2,0},{3,1},{4,6},{5,7},{6,4},{7,5},{8,10},{9,11},{10,... | collective-permute-start | bytes 196616 | tf_op jit(solution)/shard_map/ppermute | solution.py:32
  60.5 6.5 %collective-permute-start.20 = (bf16[16,2048]{1,0:T(8,128)(2,1)S(1)}, bf16[16,2048]{1,0:T(8,128)(2,1)S(1)}, u32[]{:S(2)}, u32[]{:S(2)}) collective-permute-start(bf16[16,2048]{1,0:T(8,128)(2,1)S(1)} %output.1.refs_0_), channel_id=1, source_target_pairs={{0,1},{1,0},{2,3},{3,2},{4,5},{5,4},{6,7},{7,6},{8,9},{9,8},{10,11... | collective-permute-start | bytes 196616 | tf_op jit(solution)/shard_map/ppermute | solution.py:32

commit v8 on v7

--- a/solution.py
+++ b/solution.py
@@ -38,6 +38,11 @@
 
 def gather(value, axis):
     return exchange([value] * lax.axis_size(axis), axis)
+
+
+def gather_by_index(value, axis):
+    size = lax.axis_size(axis)
+    return [value] + [pairs(value, axis, size - d) for d in range(1, size)]
 
 
 def lane_freqs(rows):
@@ -127,7 +132,7 @@
     angles = by_row(len(spots), spots) * lane_freqs(len(spots))
     cos_q[...] = jnp.cos(angles)
     sin_q[...] = jnp.sin(angles) * sine_sign(len(spots))
-    for i in range(PARTS - 1):
+    for i in range(PARTS // 2):
         for copy in copies[i]:
             copy.wait()
         rows = slice(i * size, (i + 1) * size)
@@ -138,8 +143,9 @@
                 at = slice(start, start + tall)
                 product = jnp.dot(x_ref[at, rows], weight, preferred_element_type=F32)
                 acc[at, columns] = product if i == 0 else acc[at, columns] + product
-    for copy in copies[-1]:
-        copy.wait()
+    for pair_of_copies in copies[PARTS // 2 :]:
+        for copy in pair_of_copies:
+            copy.wait()
 
 
 def load(x, kv_weight, counts, tails, pages, new_count):
@@ -175,7 +181,7 @@
 def keys_kernel(acc, x_ref, w_ref, cos_ref, sin_ref, after, k_ref):
     tokens, depth = x_ref.shape
     tall = tokens // 2
-    rows = slice(depth - depth // PARTS, depth)
+    rows = slice(depth // 2, depth)
     for pair in range(KVH // 2):
         weight = pair_columns(w_ref, rows, pair, 0)
         columns = slice(2 * pair * HD, 2 * (pair + 1) * HD)
@@ -249,23 +255,29 @@
     )(x, weight, in_hbm(out_weight), after)
 
 
-def prepare_kernel(q_ref, kv_ref, out_ref):
-    own_rows, new_count, _, _ = out_ref.shape
-    for r in range(own_rows):
+def by_heads(row):
+    return jnp.concatenate([row[:, c : c + HD] for c in range(0, row.shape[1], HD)], axis=0)
+
+
+def prepare_kernel(q_ref, kv_ref, q_out, kv_out):
+    for r in range(q_ref.shape[0]):
         q, kv = q_ref[r].astype(F32), kv_ref[r].astype(F32)
-        for n in range(new_count):
-            parts = [a[n : n + 1, c : c + HD] for a in (q, kv) for c in range(0, a.shape[1], HD)]
-            out_ref[r, n] = jnp.concatenate(parts, axis=0).astype(BF16)
+        for n in range(q_ref.shape[1]):
+            q_out[r, n] = by_heads(q[n : n + 1]).astype(BF16)
+            kv_out[r, n] = by_heads(kv[n : n + 1])
 
 
 def prepare(new_query, new_keyval):
     own_rows, new_count, columns = new_query.shape
-    heads = (columns + new_keyval.shape[2]) // HD
+    shape = lambda a: (own_rows, new_count, a.shape[2] // HD, HD)
     return pl.pallas_call(
         prepare_kernel,
         in_specs=[VMEM, VMEM],
-        out_specs=VMEM,
-        out_shape=jax.ShapeDtypeStruct((own_rows, new_count, heads, HD), BF16),
+        out_specs=[VMEM, VMEM],
+        out_shape=[
+            jax.ShapeDtypeStruct(shape(new_query), BF16),
+            jax.ShapeDtypeStruct(shape(new_keyval), F32),
+        ],
         compiler_params=pltpu.CompilerParams(vmem_limit_bytes=8 * MIB),
         cost_estimate=pl.CostEstimate(flops=0, bytes_accessed=MIB, transcendentals=0),
         name="prepare",
@@ -273,20 +285,27 @@
 
 
 def stacked_kernel(n_tp, *refs):
-    for d in range(n_tp):
-        refs[-1][d] = refs[d][...]
-
-
-def stacked(pieces, after):
+    kv_ref, _, out_ref = refs[n_tp:]
+    own_rows, new_count, heads, _ = refs[0].shape
+    for r in range(own_rows):
+        for n in range(new_count):
+            rows = [refs[d][r, n].astype(F32) for d in range(n_tp)] + [kv_ref[r, n]]
+            rows.append(jnp.zeros((out_ref.shape[2] - n_tp * heads - kv_ref.shape[2], HD), F32))
+            out_ref[r, n] = jnp.concatenate(rows, axis=0).astype(BF16)
+
+
+def stacked(pieces, fresh, after):
     n_tp = len(pieces)
+    own_rows, new_count, heads, _ = pieces[0].shape
+    rows = n_tp * heads + 16
     return pl.pallas_call(
         functools.partial(stacked_kernel, n_tp),
-        in_specs=[VMEM] * n_tp + [ANY],
+        in_specs=[VMEM] * (n_tp + 1) + [ANY],
         out_specs=VMEM,
-        out_shape=jax.ShapeDtypeStruct((n_tp,) + pieces[0].shape, BF16),
+        out_shape=jax.ShapeDtypeStruct((own_rows, new_count, rows, HD), BF16),
         compiler_params=pltpu.CompilerParams(vmem_limit_bytes=8 * MIB),
         name="stacked",
-    )(*pieces, after)
+    )(*pieces, fresh, after)
 
 
 def scores_kernel(n_seq, n_tp, *refs):
@@ -296,7 +315,7 @@
     own_q, all_q, ready = refs[n_seq + 5 + n_tp :]
     kv_local = KVH // n_tp
     local_pages = k_ref.shape[0] // PAGE
-    _, own_rows, new_count, _, _ = new[0].shape
+    own_rows, new_count, _, _ = new[0].shape
     rows = new_count * GROUP
     count = kv_local * rows
     scale = 1.0 / math.sqrt(HD)
@@ -308,12 +327,13 @@
             request = partner(seq, ds, n_seq) * own_rows + rr
             spots = [pl.ds(request * new_count + n, 1) for n in range(new_count)]
             turn = [(cos_q[spot], sin_q[spot]) for spot in spots]
+            held = [new[ds][rr, n].astype(F32) for n in range(new_count)]
             for dt in range(n_tp):
-                block = [new[ds][dt, rr, n].astype(F32) for n in range(new_count)]
                 for g in range(kv_local):
                     parts = []
                     for n in range(new_count):
-                        q = block[n][g * GROUP : (g + 1) * GROUP]
+                        row = (dt * kv_local + g) * GROUP
+                        q = held[n][row : row + GROUP]
                         parts.append(q * turn[n][0] + pltpu.roll(q, HD // 2, 1) * turn[n][1])
                     part = jnp.concatenate(parts, axis=0).astype(BF16)
                     at = (partner(me, dt, n_tp) * kv_local + g) * rows
@@ -334,7 +354,7 @@
 
 def partial_scores(new, k, cos_q, sin_q, meta, after, prompts, n_tp):
     n_seq = len(new)
-    new_count = new[0].shape[2]
+    new_count = new[0].shape[1]
     tokens = k.shape[0]
     rows = KVH // n_tp * new_count * GROUP
     return pl.pallas_call(
@@ -359,10 +379,10 @@
     new = refs[:n_seq]
     q_ref, cos_q, sin_q, score_ref, value_ref = refs[n_seq:]
     prompts, rows_local, _ = q_ref.shape
-    _, own_rows, new_count, _, _ = new[0].shape
+    own_rows, new_count, _, _ = new[0].shape
     rows = new_count * GROUP
     kv_local = rows_local // rows
-    heads = kv_local * GROUP
+    heads = QH
     scale = 1.0 / math.sqrt(HD)
     seq = lax.axis_index("seq")
     step = lax.broadcasted_iota(jnp.int32, (rows_local, HD), 0) % rows // GROUP
@@ -375,7 +395,7 @@
             for n in range(new_count):
                 spot = pl.ds(request * new_count + n, 1)
                 cosine, sine = cos_q[spot], sin_q[spot]
-                both = new[ds][0, rr, n].astype(F32)
+                both = new[ds][rr, n].astype(F32)
                 keys, values = [], []
                 for g in range(kv_local):
                     k = both[heads + 2 * g : heads + 2 * g + 1]
@@ -393,7 +413,7 @@
 
 def fresh_scores(new, own_q, cos_q, sin_q):
     n_seq = len(new)
-    new_count = new[0].shape[2]
+    new_count = new[0].shape[1]
     prompts, rows, _ = own_q.shape
     return pl.pallas_call(
         functools.partial(fresh_kernel, n_seq),
@@ -480,7 +500,8 @@
     me = lax.axis_index("tp")
     own = [pl.ds(pl.multiple_of(partner(me, d, n_tp) * rows_local, rows_local), rows_local) for d in range(n_tp)]
     for d in range(n_tp):
-        ready[own[d]] = pieces[d][...]
+        at = pl.multiple_of((me ^ d) * rows_local, rows_local)
+        ready[pl.ds(at, rows_local)] = pieces[d][...]
     total[...] = jnp.zeros_like(total)
     half = va_ref.shape[1] // HD
     for p in range(local_pages):
@@ -633,11 +654,12 @@
     own_rows, new_count, _ = new_query.shape
     prompts = page_counts.shape[0]
     pages = prefill_states.shape[0] // PAGE * n_seq
-    new = gather(prepare(new_query, new_keyval), "tp")
+    query, new_kv = prepare(new_query, new_keyval)
+    query = gather(query, "tp")
     acc, x, w, cosine, sine, cos_q, sin_q, meta = load(
         prefill_states, kv_weight, page_counts, tail_tokens, pages, new_count
     )
-    new = stacked(new, meta)
+    new = stacked(query, new_kv, meta)
     k = rotated_keys(acc, x, w, cosine, sine, new)
     va, oa = project_values(x, w, out_weight, 0, new)
     new = gather(new, "seq")
@@ -645,7 +667,7 @@
     vb, ob = project_values(x, w, out_weight, 1, own_q)
     fresh, values = fresh_scores(new, own_q, cos_q, sin_q)
     weights, stats = softmax_weights(exchange(scores, "tp"), meta, vb, pages, prompts)
-    chunks = weighted_values(gather(weights, "tp"), va, vb, meta, prompts)
+    chunks = weighted_values(gather_by_index(weights, "tp"), va, vb, meta, prompts)
     pieces = gather(summed(exchange(chunks, "tp"), stats), "seq")
     partial = output_partial(pieces, fresh, values, (oa, ob))
     return final_sum(gather(partial, "tp"), residual)

time: 68 us -> 67 us (0.985)
    pallas_call x1, Pallas kernels: 7.16 us -> 6.04 us  [load(): pl.pallas_call(functools.partial(load_kernel, pages, prompts, new_count),...]
    pallas_call x1, Pallas kernels: 1.63 us -> 2.73 us  [rotated_keys(): pl.pallas_call(keys_kernel, in_specs=[VMEM] * 5 + [ANY], out_specs=VMEM,...]
  transfers between devices with their start and end apart: 21 -> 21, of which waited for: 10 -> 9; matrix products, arithmetic and copies ran while one was open for 0% -> 0% of each run, Pallas kernels for 21% -> 21%
where the time goes in v8:
time: 67 us; the launch traced here: 66.8 us
  starting transfers between devices  26.7 us (40%)
  Pallas kernels  21.5 us (32%)
  waiting for transfers between devices  18.4 us (27%)
    ppermute x21, starting transfers between devices, pairs(): lax.ppermute(value, axis, [(i, partner(i, entry, size)) for i in range(si...  26.7 us
    ppermute x21, waiting for transfers between devices, pairs(): lax.ppermute(value, axis, [(i, partner(i, entry, size)) for i in range(si...  18.4 us
    pallas_call x1, Pallas kernels, load(): pl.pallas_call(functools.partial(load_kernel, pages, prompts, new_count),...  6.04 us
    pallas_call x2, Pallas kernels, project_values(): pl.pallas_call(functools.partial(values_kernel, first), in_specs=[VMEM, V...  4.75 us
    pallas_call x1, Pallas kernels, rotated_keys(): pl.pallas_call(keys_kernel, in_specs=[VMEM] * 5 + [ANY], out_specs=VMEM,...  2.73 us
    pallas_call x1, Pallas kernels, partial_scores(): pl.pallas_call(functools.partial(scores_kernel, n_seq, n_tp), in_specs=[V...  1.88 us
    pallas_call x1, Pallas kernels, output_partial(): pl.pallas_call(functools.partial(output_kernel, n_seq), in_specs=[VMEM] *...  1.58 us
  transfers between devices with their start and end apart: 21, of which 9 were waited for; matrix products, arithmetic and copies ran while one was open for 0% of the time, Pallas kernels for 21%

profile of v8, /device:TPU:0, one launch (start us, length us, event | category | flops | bytes accessed | tf_op | source)
XLA Modules:
  0.0 66.8 jit_solution(11741956207866296056)
XLA Ops:
  0.0 0.7 %prepare.1 = (bf16[2,2,16,128]{3,2,1,0:T(8,128)(2,1)S(1)}, f32[2,2,4,128]{3,2,1,0:T(4,128)S(1)}) custom-call(bf16[2,2,2048]{2,1,0:T(2,128)(2,1)} %q_ref.1, bf16[2,2,512]{2,1,0:T(2,128)(2,1)} %kv_ref.1), custom_call_target="tpu_custom_call" | custom-call | bytes 1048576 | tf_op jit(solution)/shard_map/prepare/pallas_call | solution.py:273
  0.7 5.1 %collective-permute-start = (bf16[2,2,16,128]{3,2,1,0:T(8,128)(2,1)S(1)}, bf16[2,2,16,128]{3,2,1,0:T(8,128)(2,1)S(1)}, u32[]{:S(2)}, u32[]{:S(2)}) collective-permute-start(bf16[2,2,16,128]{3,2,1,0:T(8,128)(2,1)S(1)} %get-tuple-element.32.refs_0_), channel_id=1, source_target_pairs={{0,3},{1,2},{2,1},{3,0},{4,7},{5,6},{6,5},{7,4},{8,11},{9,10},{10,... | collective-permute-start | bytes 49160 | tf_op jit(solution)/shard_map/ppermute | solution.py:32
  5.9 0.6 collective-permute-start.2
  6.5 6.0 %load.1 = (f32[1024,1024]{1,0:T(8,128)S(1)}, bf16[1024,2048]{1,0:T(8,128)(2,1)S(1)}, bf16[2048,2048]{1,0:T(8,128)(2,1)S(1)}, f32[1024,128]{1,0:T(8,128)S(1)}, f3...) custom-call(bf16[1024,2048]{1,0:T(8,128)(2,1)} %x_hbm.1, ...), custom_call_target="tpu_custom_call" | custom-call | flops 3221225472 | bytes 12582912 | tf_op jit(solution)/shard_map/load/pallas_call | solution.py:156
  13.1 1.3 %collective-permute-start.4 = (bf16[2,2,80,128]{3,2,1,0:T(8,128)(2,1)S(1)}, bf16[2,2,80,128]{3,2,1,0:T(8,128)(2,1)S(1)}, u32[]{:S(2)}, u32[]{:S(2)}) collective-permute-start(bf16[2,2,80,128]{3,2,1,0:T(8,128)(2,1)S(1)} %stacked.1.after.refs_0_), channel_id=1, source_target_pairs={{0,8},{4,12},{8,0},{12,4},{1,9},{5,13},{9,1},{13,5},{2,10},{6,14},... | collective-permute-start | bytes 245768 | tf_op jit(solution)/shard_map/ppermute | solution.py:32
  14.6 2.4 %values.2 = (bf16[1024,512]{1,0:T(8,128)(2,1)S(1)}, bf16[1024,2048]{1,0:T(8,128)(2,1)S(1)}) custom-call(bf16[1024,2048]{1,0:T(8,128)(2,1)S(1)} %get-tuple-element.36.x_ref, bf16[2048,2048]{1,0:T(8,128)(2,1)S(1)} %get-tuple-element.37.w_ref, bf16[2048,2048]{1,0:T(8,128)(2,1)} %o_hbm.3, bf16[2,2,80,128]{3,2,1,0:T(8,128)(2,1)S(1)} %stacked.1.after.refs_0_), custom_call_target="tpu_custom_call" | custom-call | flops 2147483648 | bytes 8388608 | tf_op jit(solution)/shard_map/values/pallas_call | solution.py:236
  17.0 2.7 %keys.1.refs_4_ = bf16[1024,1024]{1,0:T(8,128)(2,1)S(1)} custom-call(f32[1024,1024]{1,0:T(8,128)S(1)} %get-tuple-element.35.acc, bf16[1024,2048]{1,0:T(8,128)(2,1)S(1)} %get-tuple-element.36.x_ref, bf16[2048,2048]{1,0:T(8,128)(2,1)S(1)} %get-tuple-element.37.w_ref, f32[1024,128]{1,0:T(8,128)S(1)} %get-tuple-element.38.cos_ref, ...), custom_call_target="tpu_custom_call" | custom-call | flops 1073741824 | bytes 8388608 | tf_op jit(solution)/shard_map/keys/pallas_call | solution.py:202
  19.7 1.9 %scores.1 = (bf16[32,1024]{1,0:T(8,128)(2,1)S(1)}, bf16[32,1024]{1,0:T(8,128)(2,1)S(1)}, bf16[32,1024]{1,0:T(8,128)(2,1)S(1)}, bf16[32,1024]{1,0:T(8,128)(2,1)S(1)}, bf16[8,32,128]{2,1,0:T(8,128)(2,1)S(1)}) custom-call(bf16[2,2,80,128]{3,2,1,0:T(8,128)(2,1)S(1)} %stacked.1.after.refs_0_, bf16[2,2,80,128]{3,2,1,0:T(8,128)(2,1)S(1)} %collective-permute-done.3.refs_1_, ...), custom_call_target="tpu_custom_call" | custom-call | flops 33554432 | bytes 6291456 | tf_op jit(solution)/shard_map/scores/pallas_call | solution.py:360
  21.6 3.8 %collective-permute-start.6 = (bf16[32,1024]{1,0:T(8,128)(2,1)S(1)}, bf16[32,1024]{1,0:T(8,128)(2,1)S(1)}, u32[]{:S(2)}, u32[]{:S(2)}) collective-permute-start(bf16[32,1024]{1,0:T(8,128)(2,1)S(1)} %get-tuple-element.44), channel_id=1, source_target_pairs={{0,3},{1,2},{2,1},{3,0},{4,7},{5,6},{6,5},{7,4},{8,11},{9,10},{10,... | collective-permute-start | bytes 196616 | tf_op jit(solution)/shard_map/ppermute | solution.py:32
  25.4 0.7 %collective-permute-start.8 = (bf16[32,1024]{1,0:T(8,128)(2,1)S(1)}, bf16[32,1024]{1,0:T(8,128)(2,1)S(1)}, u32[]{:S(2)}, u32[]{:S(2)}) collective-permute-start(bf16[32,1024]{1,0:T(8,128)(2,1)S(1)} %get-tuple-element.46), channel_id=1, source_target_pairs={{0,1},{1,0},{2,3},{3,2},{4,5},{5,4},{6,7},{7,6},{8,9},{9,8},{10,11... | collective-permute-start | bytes 196616 | tf_op jit(solution)/shard_map/ppermute | solution.py:32
  26.1 2.4 %values.3 = (bf16[1024,512]{1,0:T(8,128)(2,1)S(1)}, bf16[1024,2048]{1,0:T(8,128)(2,1)S(1)}) custom-call(bf16[1024,2048]{1,0:T(8,128)(2,1)S(1)} %get-tuple-element.36.x_ref, bf16[2048,2048]{1,0:T(8,128)(2,1)S(1)} %get-tuple-element.37.w_ref, bf16[2048,2048]{1,0:T(8,128)(2,1)} %o_hbm.3, bf16[8,32,128]{2,1,0:T(8,128)(2,1)S(1)} %get-tuple-element.47.after.refs_4_), custom_call_target="tpu_custom_call" | custom-call | flops 2147483648 | bytes 8388608 | tf_op jit(solution)/shard_map/values/pallas_call | solution.py:236
  28.5 2.6 %collective-permute-done.7.refs_2_ = bf16[32,1024]{1,0:T(8,128)(2,1)S(1)} collective-permute-done((bf16[32,1024]{1,0:T(8,128)(2,1)S(1)}, bf16[32,1024]{1,0:T(8,128)(2,1)S(1)}, u32[]{:S(2)}, u32[]{:S(2)}) %collective-permute-start.7) | collective-permute-done | bytes 65568 | tf_op jit(solution)/shard_map/ppermute | solution.py:32
  31.1 0.9 %weights.1 = (bf16[32,1024]{1,0:T(8,128)(2,1)S(1)}, bf16[32,128]{1,0:T(8,128)(2,1)S(1)}) custom-call(bf16[32,1024]{1,0:T(8,128)(2,1)S(1)} %get-tuple-element.43.refs_0_, bf16[32,1024]{1,0:T(8,128)(2,1)S(1)} %collective-permute-done.6.refs_1_, bf16[32,1024]{1,0:T(8,128)(2,1)S(1)} %collective-permute-done.7.refs_2_, ...), custom_call_target="tpu_custom_call" | custom-call | tf_op jit(solution)/shard_map/weights/pallas_call | solution.py:477
  32.0 1.6 %collective-permute-start.10 = (bf16[32,1024]{1,0:T(8,128)(2,1)S(1)}, bf16[32,1024]{1,0:T(8,128)(2,1)S(1)}, u32[]{:S(2)}, u32[]{:S(2)}) collective-permute-start(bf16[32,1024]{1,0:T(8,128)(2,1)S(1)} %get-tuple-element.49.refs_0_), channel_id=1, source_target_pairs={{0,2},{1,3},{2,0},{3,1},{4,6},{5,7},{6,4},{7,5},{8,10},{9,11},{10,... | collective-permute-start | bytes 196616 | tf_op jit(solution)/shard_map/ppermute | solution.py:32
  33.6 2.2 %collective-permute-start.11 = (bf16[32,1024]{1,0:T(8,128)(2,1)S(1)}, bf16[32,1024]{1,0:T(8,128)(2,1)S(1)}, u32[]{:S(2)}, u32[]{:S(2)}) collective-permute-start(bf16[32,1024]{1,0:T(8,128)(2,1)S(1)} %get-tuple-element.49.refs_0_), channel_id=1, source_target_pairs={{0,3},{1,2},{2,1},{3,0},{4,7},{5,6},{6,5},{7,4},{8,11},{9,10},{10,... | collective-permute-start | bytes 196616 | tf_op jit(solution)/shard_map/ppermute | solution.py:32
  35.8 4.3 %collective-permute-done.10.refs_2_ = bf16[32,1024]{1,0:T(8,128)(2,1)S(1)} collective-permute-done((bf16[32,1024]{1,0:T(8,128)(2,1)S(1)}, bf16[32,1024]{1,0:T(8,128)(2,1)S(1)}, u32[]{:S(2)}, u32[]{:S(2)}) %collective-permute-start.10) | collective-permute-done | bytes 65568 | tf_op jit(solution)/shard_map/ppermute | solution.py:32
  40.6 1.3 %weighted.1 = (bf16[8,32,128]{2,1,0:T(8,128)(2,1)S(1)}, bf16[8,32,128]{2,1,0:T(8,128)(2,1)S(1)}, bf16[8,32,128]{2,1,0:T(8,128)(2,1)S(1)}, bf16[8,32,128]{2,1,0:T(8,128)(2,1)S(1)}) custom-call(bf16[32,1024]{1,0:T(8,128)(2,1)S(1)} %get-tuple-element.49.refs_0_, bf16[32,1024]{1,0:T(8,128)(2,1)S(1)} %collective-permute-done.9.refs_1_, ...), custom_call_target="tpu_custom_call" | custom-call | flops 33554432 | bytes 8388608 | tf_op jit(solution)/shard_map/weighted/pallas_call | solution.py:522
  41.9 2.0 %collective-permute-start.12 = (bf16[8,32,128]{2,1,0:T(8,128)(2,1)S(1)}, bf16[8,32,128]{2,1,0:T(8,128)(2,1)S(1)}, u32[]{:S(2)}, u32[]{:S(2)}) collective-permute-start(bf16[8,32,128]{2,1,0:T(8,128)(2,1)S(1)} %get-tuple-element.51), channel_id=1, source_target_pairs={{0,3},{1,2},{2,1},{3,0},{4,7},{5,6},{6,5},{7,4},{8,11},{9,10},{10,... | collective-permute-start | bytes 196616 | tf_op jit(solution)/shard_map/ppermute | solution.py:32
  44.2 2.2 %collective-permute-start.14 = (bf16[8,32,128]{2,1,0:T(8,128)(2,1)S(1)}, bf16[8,32,128]{2,1,0:T(8,128)(2,1)S(1)}, u32[]{:S(2)}, u32[]{:S(2)}) collective-permute-start(bf16[8,32,128]{2,1,0:T(8,128)(2,1)S(1)} %get-tuple-element.53), channel_id=1, source_target_pairs={{0,1},{1,0},{2,3},{3,2},{4,5},{5,4},{6,7},{7,6},{8,9},{9,8},{10,11... | collective-permute-start | bytes 196616 | tf_op jit(solution)/shard_map/ppermute | solution.py:32
  46.4 1.8 %collective-permute-done.12.refs_1_ = bf16[8,32,128]{2,1,0:T(8,128)(2,1)S(1)} collective-permute-done((bf16[8,32,128]{2,1,0:T(8,128)(2,1)S(1)}, bf16[8,32,128]{2,1,0:T(8,128)(2,1)S(1)}, u32[]{:S(2)}, u32[]{:S(2)}) %collective-permute-start.12) | collective-permute-done | bytes 65568 | tf_op jit(solution)/shard_map/ppermute | solution.py:32
  48.2 1.5 %collective-permute-done.13.refs_2_ = bf16[8,32,128]{2,1,0:T(8,128)(2,1)S(1)} collective-permute-done((bf16[8,32,128]{2,1,0:T(8,128)(2,1)S(1)}, bf16[8,32,128]{2,1,0:T(8,128)(2,1)S(1)}, u32[]{:S(2)}, u32[]{:S(2)}) %collective-permute-start.13) | collective-permute-done | bytes 65568 | tf_op jit(solution)/shard_map/ppermute | solution.py:32
  50.2 0.9 %collective-permute-start.16 = (bf16[9,32,128]{2,1,0:T(8,128)(2,1)S(1)}, bf16[9,32,128]{2,1,0:T(8,128)(2,1)S(1)}, u32[]{:S(2)}, u32[]{:S(2)}) collective-permute-start(bf16[9,32,128]{2,1,0:T(8,128)(2,1)S(1)} %summed.1.refs_0_), channel_id=1, source_target_pairs={{0,8},{4,12},{8,0},{12,4},{1,9},{5,13},{9,1},{13,5},{2,10},{6,14},... | collective-permute-start | bytes 221192 | tf_op jit(solution)/shard_map/ppermute | solution.py:32
  51.6 0.8 %fresh.1 = (f32[2,32,128]{2,1,0:T(8,128)S(1)}, f32[16,32,128]{2,1,0:T(8,128)S(1)}) custom-call(bf16[2,2,80,128]{3,2,1,0:T(8,128)(2,1)S(1)} %stacked.1.after.refs_0_, bf16[2,2,80,128]{3,2,1,0:T(8,128)(2,1)S(1)} %collective-permute-done.3.refs_1_, bf16[2,2,80,128]{3,2,1,0:T(8,128)(2,1)S(1)} %collective-permute-done.4.refs_2_, ...), custom_call_target="tpu_custom_call" | custom-call | bytes 2097152 | tf_op jit(solution)/shard_map/fresh/pallas_call | solution.py:418
  52.4 1.9 %collective-permute-done.15.refs_1_ = bf16[9,32,128]{2,1,0:T(8,128)(2,1)S(1)} collective-permute-done((bf16[9,32,128]{2,1,0:T(8,128)(2,1)S(1)}, bf16[9,32,128]{2,1,0:T(8,128)(2,1)S(1)}, u32[]{:S(2)}, u32[]{:S(2)}) %collective-permute-start.15) | collective-permute-done | bytes 73760 | tf_op jit(solution)/shard_map/ppermute | solution.py:32
  54.3 1.4 %collective-permute-done.16.refs_2_ = bf16[9,32,128]{2,1,0:T(8,128)(2,1)S(1)} collective-permute-done((bf16[9,32,128]{2,1,0:T(8,128)(2,1)S(1)}, bf16[9,32,128]{2,1,0:T(8,128)(2,1)S(1)}, u32[]{:S(2)}, u32[]{:S(2)}) %collective-permute-start.16) | collective-permute-done | bytes 73760 | tf_op jit(solution)/shard_map/ppermute | solution.py:32
  55.7 1.6 %output.1.refs_0_ = bf16[16,2048]{1,0:T(8,128)(2,1)S(1)} custom-call(bf16[9,32,128]{2,1,0:T(8,128)(2,1)S(1)} %summed.1.refs_0_, bf16[9,32,128]{2,1,0:T(8,128)(2,1)S(1)} %collective-permute-done.15.refs_1_, bf16[9,32,128]{2,1,0:T(8,128)(2,1)S(1)} %collective-permute-done.16.refs_2_, bf16[9,32,128]{2,1,0:T(8,128)(2,1)S(1)} %collective-permute-done.17.refs_3_, ...), custom_call_target="tpu_custom_call" | custom-call | tf_op jit(solution)/shard_map/output/pallas_call | solution.py:616
  57.3 1.5 %collective-permute-start.18 = (bf16[16,2048]{1,0:T(8,128)(2,1)S(1)}, bf16[16,2048]{1,0:T(8,128)(2,1)S(1)}, u32[]{:S(2)}, u32[]{:S(2)}) collective-permute-start(bf16[16,2048]{1,0:T(8,128)(2,1)S(1)} %output.1.refs_0_), channel_id=1, source_target_pairs={{0,3},{1,2},{2,1},{3,0},{4,7},{5,6},{6,5},{7,4},{8,11},{9,10},{10,... | collective-permute-start | bytes 196616 | tf_op jit(solution)/shard_map/ppermute | solution.py:32
  58.8 0.7 %collective-permute-start.19 = (bf16[16,2048]{1,0:T(8,128)(2,1)S(1)}, bf16[16,2048]{1,0:T(8,128)(2,1)S(1)}, u32[]{:S(2)}, u32[]{:S(2)}) collective-permute-start(bf16[16,2048]{1,0:T(8,128)(2,1)S(1)} %output.1.refs_0_), channel_id=1, source_target_pairs={{0,2},{1,3},{2,0},{3,1},{4,6},{5,7},{6,4},{7,5},{8,10},{9,11},{10,... | collective-permute-start | bytes 196616 | tf_op jit(solution)/shard_map/ppermute | solution.py:32
  59.6 2.1 %collective-permute-start.20 = (bf16[16,2048]{1,0:T(8,128)(2,1)S(1)}, bf16[16,2048]{1,0:T(8,128)(2,1)S(1)}, u32[]{:S(2)}, u32[]{:S(2)}) collective-permute-start(bf16[16,2048]{1,0:T(8,128)(2,1)S(1)} %output.1.refs_0_), channel_id=1, source_target_pairs={{0,1},{1,0},{2,3},{3,2},{4,5},{5,4},{6,7},{7,6},{8,9},{9,8},{10,11... | collective-permute-start | bytes 196616 | tf_op jit(solution)/shard_map/ppermute | solution.py:32
  61.7 2.4 %collective-permute-done.18.refs_1_ = bf16[16,2048]{1,0:T(8,128)(2,1)S(1)} collective-permute-done((bf16[16,2048]{1,0:T(8,128)(2,1)S(1)}, bf16[16,2048]{1,0:T(8,128)(2,1)S(1)}, u32[]{:S(2)}, u32[]{:S(2)}) %collective-permute-start.18) | collective-permute-done | bytes 65568 | tf_op jit(solution)/shard_map/ppermute | solution.py:32
  64.1 1.9 %collective-permute-done.19.refs_2_ = bf16[16,2048]{1,0:T(8,128)(2,1)S(1)} collective-permute-done((bf16[16,2048]{1,0:T(8,128)(2,1)S(1)}, bf16[16,2048]{1,0:T(8,128)(2,1)S(1)}, u32[]{:S(2)}, u32[]{:S(2)}) %collective-permute-start.19) | collective-permute-done | bytes 65568 | tf_op jit(solution)/shard_map/ppermute | solution.py:32
  66.0 0.7 %final.1 = f32[8,2,2048]{2,1,0:T(2,128)} custom-call(bf16[16,2048]{1,0:T(8,128)(2,1)S(1)} %output.1.refs_0_, bf16[16,2048]{1,0:T(8,128)(2,1)S(1)} %collective-permute-done.18.refs_1_, bf16[16,2048]{1,0:T(8,128)(2,1)S(1)} %collective-permute-done.19.refs_2_, bf16[16,2048]{1,0:T(8,128)(2,1)S(1)} %collective-permute-done.20.refs_3_, bf16[8,2,2048]{2,1,0:T(2,128)(2,1)S(1)} %copy-done), custom_call_target="tpu_custom_call" | custom-call | tf_op jit(solution)/shard_map/final/pallas_call | solution.py:640
  (25 shorter events, 2.6 us)
Async XLA Ops:
  0.7 11.8 %collective-permute-start = (bf16[2,2,16,128]{3,2,1,0:T(8,128)(2,1)S(1)}, bf16[2,2,16,128]{3,2,1,0:T(8,128)(2,1)S(1)}, u32[]{:S(2)}, u32[]{:S(2)}) collective-permute-start(bf16[2,2,16,128]{3,2,1,0:T(8,128)(2,1)S(1)} %get-tuple-element.32.refs_0_), channel_id=1, source_target_pairs={{0,3},{1,2},{2,1},{3,0},{4,7},{5,6},{6,5},{7,4},{8,11},{9,10},{10,... | collective-permute-start | bytes 49160 | tf_op jit(solution)/shard_map/ppermute | solution.py:32
  5.9 6.7 %collective-permute-start.1 = (bf16[2,2,16,128]{3,2,1,0:T(8,128)(2,1)S(1)}, bf16[2,2,16,128]{3,2,1,0:T(8,128)(2,1)S(1)}, u32[]{:S(2)}, u32[]{:S(2)}) collective-permute-start(bf16[2,2,16,128]{3,2,1,0:T(8,128)(2,1)S(1)} %get-tuple-element.32.refs_0_), channel_id=1, source_target_pairs={{0,2},{1,3},{2,0},{3,1},{4,6},{5,7},{6,4},{7,5},{8,10},{9,11},{10,... | collective-permute-start | bytes 49160 | tf_op jit(solution)/shard_map/ppermute | solution.py:32
  5.9 6.7 %collective-permute-start.2 = (bf16[2,2,16,128]{3,2,1,0:T(8,128)(2,1)S(1)}, bf16[2,2,16,128]{3,2,1,0:T(8,128)(2,1)S(1)}, u32[]{:S(2)}, u32[]{:S(2)}) collective-permute-start(bf16[2,2,16,128]{3,2,1,0:T(8,128)(2,1)S(1)} %get-tuple-element.32.refs_0_), channel_id=1, source_target_pairs={{0,1},{1,0},{2,3},{3,2},{4,5},{5,4},{6,7},{7,6},{8,9},{9,8},{10,11... | collective-permute-start | bytes 49160 | tf_op jit(solution)/shard_map/ppermute | solution.py:32
  12.6 7.1 %collective-permute-start.3 = (bf16[2,2,80,128]{3,2,1,0:T(8,128)(2,1)S(1)}, bf16[2,2,80,128]{3,2,1,0:T(8,128)(2,1)S(1)}, u32[]{:S(2)}, u32[]{:S(2)}) collective-permute-start(bf16[2,2,80,128]{3,2,1,0:T(8,128)(2,1)S(1)} %stacked.1.after.refs_0_), channel_id=1, source_target_pairs={{0,12},{4,8},{8,4},{12,0},{1,13},{5,9},{9,5},{13,1},{2,14},{6,10},... | collective-permute-start | bytes 245768 | tf_op jit(solution)/shard_map/ppermute | solution.py:32
  13.1 6.6 %collective-permute-start.4 = (bf16[2,2,80,128]{3,2,1,0:T(8,128)(2,1)S(1)}, bf16[2,2,80,128]{3,2,1,0:T(8,128)(2,1)S(1)}, u32[]{:S(2)}, u32[]{:S(2)}) collective-permute-start(bf16[2,2,80,128]{3,2,1,0:T(8,128)(2,1)S(1)} %stacked.1.after.refs_0_), channel_id=1, source_target_pairs={{0,8},{4,12},{8,0},{12,4},{1,9},{5,13},{9,1},{13,5},{2,10},{6,14},... | collective-permute-start | bytes 245768 | tf_op jit(solution)/shard_map/ppermute | solution.py:32
  14.4 5.3 %collective-permute-start.5 = (bf16[2,2,80,128]{3,2,1,0:T(8,128)(2,1)S(1)}, bf16[2,2,80,128]{3,2,1,0:T(8,128)(2,1)S(1)}, u32[]{:S(2)}, u32[]{:S(2)}) collective-permute-start(bf16[2,2,80,128]{3,2,1,0:T(8,128)(2,1)S(1)} %stacked.1.after.refs_0_), channel_id=1, source_target_pairs={{0,4},{4,0},{8,12},{12,8},{1,5},{5,1},{9,13},{13,9},{2,6},{6,2},{1... | collective-permute-start | bytes 245768 | tf_op jit(solution)/shard_map/ppermute | solution.py:32
  21.6 6.9 %collective-permute-start.6 = (bf16[32,1024]{1,0:T(8,128)(2,1)S(1)}, bf16[32,1024]{1,0:T(8,128)(2,1)S(1)}, u32[]{:S(2)}, u32[]{:S(2)}) collective-permute-start(bf16[32,1024]{1,0:T(8,128)(2,1)S(1)} %get-tuple-element.44), channel_id=1, source_target_pairs={{0,3},{1,2},{2,1},{3,0},{4,7},{5,6},{6,5},{7,4},{8,11},{9,10},{10,... | collective-permute-start | bytes 196616 | tf_op jit(solution)/shard_map/ppermute | solution.py:32
  25.4 5.7 %collective-permute-start.7 = (bf16[32,1024]{1,0:T(8,128)(2,1)S(1)}, bf16[32,1024]{1,0:T(8,128)(2,1)S(1)}, u32[]{:S(2)}, u32[]{:S(2)}) collective-permute-start(bf16[32,1024]{1,0:T(8,128)(2,1)S(1)} %get-tuple-element.45), channel_id=1, source_target_pairs={{0,2},{1,3},{2,0},{3,1},{4,6},{5,7},{6,4},{7,5},{8,10},{9,11},{10,... | collective-permute-start | bytes 196616 | tf_op jit(solution)/shard_map/ppermute | solution.py:32
  25.4 5.7 %collective-permute-start.8 = (bf16[32,1024]{1,0:T(8,128)(2,1)S(1)}, bf16[32,1024]{1,0:T(8,128)(2,1)S(1)}, u32[]{:S(2)}, u32[]{:S(2)}) collective-permute-start(bf16[32,1024]{1,0:T(8,128)(2,1)S(1)} %get-tuple-element.46), channel_id=1, source_target_pairs={{0,1},{1,0},{2,3},{3,2},{4,5},{5,4},{6,7},{7,6},{8,9},{9,8},{10,11... | collective-permute-start | bytes 196616 | tf_op jit(solution)/shard_map/ppermute | solution.py:32
  32.0 8.1 %collective-permute-start.10 = (bf16[32,1024]{1,0:T(8,128)(2,1)S(1)}, bf16[32,1024]{1,0:T(8,128)(2,1)S(1)}, u32[]{:S(2)}, u32[]{:S(2)}) collective-permute-start(bf16[32,1024]{1,0:T(8,128)(2,1)S(1)} %get-tuple-element.49.refs_0_), channel_id=1, source_target_pairs={{0,2},{1,3},{2,0},{3,1},{4,6},{5,7},{6,4},{7,5},{8,10},{9,11},{10,... | collective-permute-start | bytes 196616 | tf_op jit(solution)/shard_map/ppermute | solution.py:32
  33.6 6.5 %collective-permute-start.11 = (bf16[32,1024]{1,0:T(8,128)(2,1)S(1)}, bf16[32,1024]{1,0:T(8,128)(2,1)S(1)}, u32[]{:S(2)}, u32[]{:S(2)}) collective-permute-start(bf16[32,1024]{1,0:T(8,128)(2,1)S(1)} %get-tuple-element.49.refs_0_), channel_id=1, source_target_pairs={{0,3},{1,2},{2,1},{3,0},{4,7},{5,6},{6,5},{7,4},{8,11},{9,10},{10,... | collective-permute-start | bytes 196616 | tf_op jit(solution)/shard_map/ppermute | solution.py:32
  35.8 4.9 %collective-permute-start.9 = (bf16[32,1024]{1,0:T(8,128)(2,1)S(1)}, bf16[32,1024]{1,0:T(8,128)(2,1)S(1)}, u32[]{:S(2)}, u32[]{:S(2)}) collective-permute-start(bf16[32,1024]{1,0:T(8,128)(2,1)S(1)} %get-tuple-element.49.refs_0_), channel_id=1, source_target_pairs={{0,1},{1,0},{2,3},{3,2},{4,5},{5,4},{6,7},{7,6},{8,9},{9,8},{10,11... | collective-permute-start | bytes 196616 | tf_op jit(solution)/shard_map/ppermute | solution.py:32
  41.9 6.3 %collective-permute-start.12 = (bf16[8,32,128]{2,1,0:T(8,128)(2,1)S(1)}, bf16[8,32,128]{2,1,0:T(8,128)(2,1)S(1)}, u32[]{:S(2)}, u32[]{:S(2)}) collective-permute-start(bf16[8,32,128]{2,1,0:T(8,128)(2,1)S(1)} %get-tuple-element.51), channel_id=1, source_target_pairs={{0,3},{1,2},{2,1},{3,0},{4,7},{5,6},{6,5},{7,4},{8,11},{9,10},{10,... | collective-permute-start | bytes 196616 | tf_op jit(solution)/shard_map/ppermute | solution.py:32
  43.9 5.7 %collective-permute-start.13 = (bf16[8,32,128]{2,1,0:T(8,128)(2,1)S(1)}, bf16[8,32,128]{2,1,0:T(8,128)(2,1)S(1)}, u32[]{:S(2)}, u32[]{:S(2)}) collective-permute-start(bf16[8,32,128]{2,1,0:T(8,128)(2,1)S(1)} %get-tuple-element.52), channel_id=1, source_target_pairs={{0,2},{1,3},{2,0},{3,1},{4,6},{5,7},{6,4},{7,5},{8,10},{9,11},{10,... | collective-permute-start | bytes 196616 | tf_op jit(solution)/shard_map/ppermute | solution.py:32
  44.2 5.4 %collective-permute-start.14 = (bf16[8,32,128]{2,1,0:T(8,128)(2,1)S(1)}, bf16[8,32,128]{2,1,0:T(8,128)(2,1)S(1)}, u32[]{:S(2)}, u32[]{:S(2)}) collective-permute-start(bf16[8,32,128]{2,1,0:T(8,128)(2,1)S(1)} %get-tuple-element.53), channel_id=1, source_target_pairs={{0,1},{1,0},{2,3},{3,2},{4,5},{5,4},{6,7},{7,6},{8,9},{9,8},{10,11... | collective-permute-start | bytes 196616 | tf_op jit(solution)/shard_map/ppermute | solution.py:32
  49.7 4.6 %collective-permute-start.15 = (bf16[9,32,128]{2,1,0:T(8,128)(2,1)S(1)}, bf16[9,32,128]{2,1,0:T(8,128)(2,1)S(1)}, u32[]{:S(2)}, u32[]{:S(2)}) collective-permute-start(bf16[9,32,128]{2,1,0:T(8,128)(2,1)S(1)} %summed.1.refs_0_), channel_id=1, source_target_pairs={{0,12},{4,8},{8,4},{12,0},{1,13},{5,9},{9,5},{13,1},{2,14},{6,10},... | collective-permute-start | bytes 221192 | tf_op jit(solution)/shard_map/ppermute | solution.py:32
  50.2 5.5 %collective-permute-start.16 = (bf16[9,32,128]{2,1,0:T(8,128)(2,1)S(1)}, bf16[9,32,128]{2,1,0:T(8,128)(2,1)S(1)}, u32[]{:S(2)}, u32[]{:S(2)}) collective-permute-start(bf16[9,32,128]{2,1,0:T(8,128)(2,1)S(1)} %summed.1.refs_0_), channel_id=1, source_target_pairs={{0,8},{4,12},{8,0},{12,4},{1,9},{5,13},{9,1},{13,5},{2,10},{6,14},... | collective-permute-start | bytes 221192 | tf_op jit(solution)/shard_map/ppermute | solution.py:32
  51.2 4.6 %collective-permute-start.17 = (bf16[9,32,128]{2,1,0:T(8,128)(2,1)S(1)}, bf16[9,32,128]{2,1,0:T(8,128)(2,1)S(1)}, u32[]{:S(2)}, u32[]{:S(2)}) collective-permute-start(bf16[9,32,128]{2,1,0:T(8,128)(2,1)S(1)} %summed.1.refs_0_), channel_id=1, source_target_pairs={{0,4},{4,0},{8,12},{12,8},{1,5},{5,1},{9,13},{13,9},{2,6},{6,2},{1... | collective-permute-start | bytes 221192 | tf_op jit(solution)/shard_map/ppermute | solution.py:32
  55.7 10.3 %copy-start = (bf16[8,2,2048]{2,1,0:T(2,128)(2,1)S(1)}, bf16[8,2,2048]{2,1,0:T(2,128)(2,1)}, u32[]{:S(2)}) copy-start(bf16[8,2,2048]{2,1,0:T(2,128)(2,1)} %refs_4_.1) | copy-start | bytes 196612
  57.3 6.8 %collective-permute-start.18 = (bf16[16,2048]{1,0:T(8,128)(2,1)S(1)}, bf16[16,2048]{1,0:T(8,128)(2,1)S(1)}, u32[]{:S(2)}, u32[]{:S(2)}) collective-permute-start(bf16[16,2048]{1,0:T(8,128)(2,1)S(1)} %output.1.refs_0_), channel_id=1, source_target_pairs={{0,3},{1,2},{2,1},{3,0},{4,7},{5,6},{6,5},{7,4},{8,11},{9,10},{10,... | collective-permute-start | bytes 196616 | tf_op jit(solution)/shard_map/ppermute | solution.py:32
  58.8 7.2 %collective-permute-start.19 = (bf16[16,2048]{1,0:T(8,128)(2,1)S(1)}, bf16[16,2048]{1,0:T(8,128)(2,1)S(1)}, u32[]{:S(2)}, u32[]{:S(2)}) collective-permute-start(bf16[16,2048]{1,0:T(8,128)(2,1)S(1)} %output.1.refs_0_), channel_id=1, source_target_pairs={{0,2},{1,3},{2,0},{3,1},{4,6},{5,7},{6,4},{7,5},{8,10},{9,11},{10,... | collective-permute-start | bytes 196616 | tf_op jit(solution)/shard_map/ppermute | solution.py:32
  59.6 6.5 %collective-permute-start.20 = (bf16[16,2048]{1,0:T(8,128)(2,1)S(1)}, bf16[16,2048]{1,0:T(8,128)(2,1)S(1)}, u32[]{:S(2)}, u32[]{:S(2)}) collective-permute-start(bf16[16,2048]{1,0:T(8,128)(2,1)S(1)} %output.1.refs_0_), channel_id=1, source_target_pairs={{0,1},{1,0},{2,3},{3,2},{4,5},{5,4},{6,7},{7,6},{8,9},{9,8},{10,11... | collective-permute-start | bytes 196616 | tf_op jit(solution)/shard_map/ppermute | solution.py:32

commit v9 on v8

--- a/solution.py
+++ b/solution.py
@@ -37,10 +37,6 @@
 
 
 def gather(value, axis):
-    return exchange([value] * lax.axis_size(axis), axis)
-
-
-def gather_by_index(value, axis):
     size = lax.axis_size(axis)
     return [value] + [pairs(value, axis, size - d) for d in range(1, size)]
 
@@ -311,8 +307,8 @@
 def scores_kernel(n_seq, n_tp, *refs):
     new = refs[:n_seq]
     k_ref, cos_q, sin_q, meta = refs[n_seq : n_seq + 4]
-    outs = refs[n_seq + 5 : n_seq + 5 + n_tp]
-    own_q, all_q, ready = refs[n_seq + 5 + n_tp :]
+    outs = refs[n_seq + 4 : n_seq + 4 + n_tp]
+    own_q, all_q, ready = refs[n_seq + 4 + n_tp :]
     kv_local = KVH // n_tp
     local_pages = k_ref.shape[0] // PAGE
     own_rows, new_count, _, _ = new[0].shape
@@ -324,7 +320,7 @@
     first = seq * local_pages
     for ds in range(n_seq):
         for rr in range(own_rows):
-            request = partner(seq, ds, n_seq) * own_rows + rr
+            request = (seq ^ ds) * own_rows + rr
             spots = [pl.ds(request * new_count + n, 1) for n in range(new_count)]
             turn = [(cos_q[spot], sin_q[spot]) for spot in spots]
             held = [new[ds][rr, n].astype(F32) for n in range(new_count)]
@@ -336,7 +332,7 @@
                         q = held[n][row : row + GROUP]
                         parts.append(q * turn[n][0] + pltpu.roll(q, HD // 2, 1) * turn[n][1])
                     part = jnp.concatenate(parts, axis=0).astype(BF16)
-                    at = (partner(me, dt, n_tp) * kv_local + g) * rows
+                    at = ((me ^ dt) * kv_local + g) * rows
                     all_q[request, pl.ds(pl.multiple_of(at, rows), rows)] = part
                     if dt == 0:
                         own_q[request, g * rows : (g + 1) * rows] = part
@@ -352,14 +348,14 @@
         outs[d][...] = ready[pl.ds(pl.multiple_of(partner(me, d, n_tp) * count, count), count)]
 
 
-def partial_scores(new, k, cos_q, sin_q, meta, after, prompts, n_tp):
+def partial_scores(new, k, cos_q, sin_q, meta, prompts, n_tp):
     n_seq = len(new)
     new_count = new[0].shape[1]
     tokens = k.shape[0]
     rows = KVH // n_tp * new_count * GROUP
     return pl.pallas_call(
         functools.partial(scores_kernel, n_seq, n_tp),
-        in_specs=[VMEM] * (n_seq + 3) + [SMEM, ANY],
+        in_specs=[VMEM] * (n_seq + 3) + [SMEM],
         out_specs=[VMEM] * (n_tp + 1),
         out_shape=[jax.ShapeDtypeStruct((rows, tokens), BF16)] * n_tp
         + [jax.ShapeDtypeStruct((prompts, rows, HD), BF16)],
@@ -372,7 +368,7 @@
             flops=2 * tokens * rows * n_tp * HD, bytes_accessed=6 * MIB, transcendentals=0
         ),
         name="scores",
-    )(*new, k, cos_q, sin_q, meta, after)
+    )(*new, k, cos_q, sin_q, meta)
 
 
 def fresh_kernel(n_seq, *refs):
@@ -390,7 +386,7 @@
     found = [jnp.full((rows_local, HD), NEG, F32) for _ in range(new_count)]
     for ds in range(n_seq):
         for rr in range(own_rows):
-            request = partner(seq, ds, n_seq) * own_rows + rr
+            request = (seq ^ ds) * own_rows + rr
             q = q_ref[request].astype(F32)
             for n in range(new_count):
                 spot = pl.ds(request * new_count + n, 1)
@@ -661,13 +657,13 @@
     )
     new = stacked(query, new_kv, meta)
     k = rotated_keys(acc, x, w, cosine, sine, new)
-    va, oa = project_values(x, w, out_weight, 0, new)
     new = gather(new, "seq")
-    *scores, own_q = partial_scores(new, k, cos_q, sin_q, meta, va, prompts, n_tp)
-    vb, ob = project_values(x, w, out_weight, 1, own_q)
+    *scores, own_q = partial_scores(new, k, cos_q, sin_q, meta, prompts, n_tp)
+    va, oa = project_values(x, w, out_weight, 0, own_q)
     fresh, values = fresh_scores(new, own_q, cos_q, sin_q)
-    weights, stats = softmax_weights(exchange(scores, "tp"), meta, vb, pages, prompts)
-    chunks = weighted_values(gather_by_index(weights, "tp"), va, vb, meta, prompts)
+    weights, stats = softmax_weights(exchange(scores, "tp"), meta, va, pages, prompts)
+    vb, ob = project_values(x, w, out_weight, 1, stats)
+    chunks = weighted_values(gather(weights, "tp"), va, vb, meta, prompts)
     pieces = gather(summed(exchange(chunks, "tp"), stats), "seq")
     partial = output_partial(pieces, fresh, values, (oa, ob))
     return final_sum(gather(partial, "tp"), residual)

time: 67 us -> 67.1 us (level)
  no operation moved by 1% of the time
where the time goes in v9:
time: 67.1 us; the launch traced here: 66.8 us
  starting transfers between devices  27.3 us (41%)
  Pallas kernels  21.5 us (32%)
  waiting for transfers between devices  17.9 us (27%)
    ppermute x21, starting transfers between devices, pairs(): lax.ppermute(value, axis, [(i, partner(i, entry, size)) for i in range(si...  27.3 us
    ppermute x21, waiting for transfers between devices, pairs(): lax.ppermute(value, axis, [(i, partner(i, entry, size)) for i in range(si...  17.9 us
    pallas_call x1, Pallas kernels, load(): pl.pallas_call(functools.partial(load_kernel, pages, prompts, new_count),...  6.04 us
    pallas_call x2, Pallas kernels, project_values(): pl.pallas_call(functools.partial(values_kernel, first), in_specs=[VMEM, V...  4.75 us
    pallas_call x1, Pallas kernels, rotated_keys(): pl.pallas_call(keys_kernel, in_specs=[VMEM] * 5 + [ANY], out_specs=VMEM,...  2.73 us
    pallas_call x1, Pallas kernels, partial_scores(): pl.pallas_call(functools.partial(scores_kernel, n_seq, n_tp), in_specs=[V...  1.88 us
    pallas_call x1, Pallas kernels, output_partial(): pl.pallas_call(functools.partial(output_kernel, n_seq), in_specs=[VMEM] *...  1.58 us
  transfers between devices with their start and end apart: 21, of which 9 were waited for; matrix products, arithmetic and copies ran while one was open for 0% of the time, Pallas kernels for 21%

profile of v9, /device:TPU:0, one launch (start us, length us, event | category | flops | bytes accessed | tf_op | source)
XLA Modules:
  0.0 66.8 jit_solution(8520882792581827081)
XLA Ops:
  0.0 0.7 %prepare.1 = (bf16[2,2,16,128]{3,2,1,0:T(8,128)(2,1)S(1)}, f32[2,2,4,128]{3,2,1,0:T(4,128)S(1)}) custom-call(bf16[2,2,2048]{2,1,0:T(2,128)(2,1)} %q_ref.1, bf16[2,2,512]{2,1,0:T(2,128)(2,1)} %kv_ref.1), custom_call_target="tpu_custom_call" | custom-call | bytes 1048576 | tf_op jit(solution)/shard_map/prepare/pallas_call | solution.py:269
  0.7 5.1 %collective-permute-start.2 = (bf16[2,2,16,128]{3,2,1,0:T(8,128)(2,1)S(1)}, bf16[2,2,16,128]{3,2,1,0:T(8,128)(2,1)S(1)}, u32[]{:S(2)}, u32[]{:S(2)}) collective-permute-start(bf16[2,2,16,128]{3,2,1,0:T(8,128)(2,1)S(1)} %get-tuple-element.32.refs_0_), channel_id=1, source_target_pairs={{0,3},{1,2},{2,1},{3,0},{4,7},{5,6},{6,5},{7,4},{8,11},{9,10},{10,... | collective-permute-start | bytes 49160 | tf_op jit(solution)/shard_map/ppermute | solution.py:32
  5.9 0.6 collective-permute-start
  6.5 6.0 %load.1 = (f32[1024,1024]{1,0:T(8,128)S(1)}, bf16[1024,2048]{1,0:T(8,128)(2,1)S(1)}, bf16[2048,2048]{1,0:T(8,128)(2,1)S(1)}, f32[1024,128]{1,0:T(8,128)S(1)}, f3...) custom-call(bf16[1024,2048]{1,0:T(8,128)(2,1)} %x_hbm.1, ...), custom_call_target="tpu_custom_call" | custom-call | flops 3221225472 | bytes 12582912 | tf_op jit(solution)/shard_map/load/pallas_call | solution.py:152
  13.1 1.3 %collective-permute-start.4 = (bf16[2,2,80,128]{3,2,1,0:T(8,128)(2,1)S(1)}, bf16[2,2,80,128]{3,2,1,0:T(8,128)(2,1)S(1)}, u32[]{:S(2)}, u32[]{:S(2)}) collective-permute-start(bf16[2,2,80,128]{3,2,1,0:T(8,128)(2,1)S(1)} %stacked.1.after.refs_0_), channel_id=1, source_target_pairs={{0,8},{4,12},{8,0},{12,4},{1,9},{5,13},{9,1},{13,5},{2,10},{6,14},... | collective-permute-start | bytes 245768 | tf_op jit(solution)/shard_map/ppermute | solution.py:32
  14.6 2.7 %keys.1.refs_4_ = bf16[1024,1024]{1,0:T(8,128)(2,1)S(1)} custom-call(f32[1024,1024]{1,0:T(8,128)S(1)} %get-tuple-element.35.acc, bf16[1024,2048]{1,0:T(8,128)(2,1)S(1)} %get-tuple-element.36.x_ref, bf16[2048,2048]{1,0:T(8,128)(2,1)S(1)} %get-tuple-element.37.w_ref, f32[1024,128]{1,0:T(8,128)S(1)} %get-tuple-element.38.cos_ref, ...), custom_call_target="tpu_custom_call" | custom-call | flops 1073741824 | bytes 8388608 | tf_op jit(solution)/shard_map/keys/pallas_call | solution.py:198
  17.3 1.9 %collective-permute-done.4.refs_2_ = bf16[2,2,80,128]{3,2,1,0:T(8,128)(2,1)S(1)} collective-permute-done((bf16[2,2,80,128]{3,2,1,0:T(8,128)(2,1)S(1)}, bf16[2,2,80,128]{3,2,1,0:T(8,128)(2,1)S(1)}, u32[]{:S(2)}, u32[]{:S(2)}) %collective-permute-start.4) | collective-permute-done | bytes 81952 | tf_op jit(solution)/shard_map/ppermute | solution.py:32
  19.2 1.9 %scores.1 = (bf16[32,1024]{1,0:T(8,128)(2,1)S(1)}, bf16[32,1024]{1,0:T(8,128)(2,1)S(1)}, bf16[32,1024]{1,0:T(8,128)(2,1)S(1)}, bf16[32,1024]{1,0:T(8,128)(2,1)S(1)}, bf16[8,32,128]{2,1,0:T(8,128)(2,1)S(1)}) custom-call(bf16[2,2,80,128]{3,2,1,0:T(8,128)(2,1)S(1)} %stacked.1.after.refs_0_, bf16[2,2,80,128]{3,2,1,0:T(8,128)(2,1)S(1)} %collective-permute-done.3.refs_1_, ...), custom_call_target="tpu_custom_call" | custom-call | flops 33554432 | bytes 6291456 | tf_op jit(solution)/shard_map/scores/pallas_call | solution.py:356
  21.1 3.8 %collective-permute-start.6 = (bf16[32,1024]{1,0:T(8,128)(2,1)S(1)}, bf16[32,1024]{1,0:T(8,128)(2,1)S(1)}, u32[]{:S(2)}, u32[]{:S(2)}) collective-permute-start(bf16[32,1024]{1,0:T(8,128)(2,1)S(1)} %get-tuple-element.43), channel_id=1, source_target_pairs={{0,3},{1,2},{2,1},{3,0},{4,7},{5,6},{6,5},{7,4},{8,11},{9,10},{10,... | collective-permute-start | bytes 196616 | tf_op jit(solution)/shard_map/ppermute | solution.py:32
  24.9 0.6 collective-permute-start.8
  25.5 2.4 %values.2 = (bf16[1024,512]{1,0:T(8,128)(2,1)S(1)}, bf16[1024,2048]{1,0:T(8,128)(2,1)S(1)}) custom-call(bf16[1024,2048]{1,0:T(8,128)(2,1)S(1)} %get-tuple-element.36.x_ref, bf16[2048,2048]{1,0:T(8,128)(2,1)S(1)} %get-tuple-element.37.w_ref, bf16[2048,2048]{1,0:T(8,128)(2,1)} %o_hbm.3, bf16[8,32,128]{2,1,0:T(8,128)(2,1)S(1)} %get-tuple-element.46.after.refs_4_), custom_call_target="tpu_custom_call" | custom-call | flops 2147483648 | bytes 8388608 | tf_op jit(solution)/shard_map/values/pallas_call | solution.py:232
  27.9 2.6 %collective-permute-done.7.refs_2_ = bf16[32,1024]{1,0:T(8,128)(2,1)S(1)} collective-permute-done((bf16[32,1024]{1,0:T(8,128)(2,1)S(1)}, bf16[32,1024]{1,0:T(8,128)(2,1)S(1)}, u32[]{:S(2)}, u32[]{:S(2)}) %collective-permute-start.7) | collective-permute-done | bytes 65568 | tf_op jit(solution)/shard_map/ppermute | solution.py:32
  30.6 0.9 %weights.1 = (bf16[32,1024]{1,0:T(8,128)(2,1)S(1)}, bf16[32,128]{1,0:T(8,128)(2,1)S(1)}) custom-call(bf16[32,1024]{1,0:T(8,128)(2,1)S(1)} %get-tuple-element.42.refs_0_, bf16[32,1024]{1,0:T(8,128)(2,1)S(1)} %collective-permute-done.6.refs_1_, bf16[32,1024]{1,0:T(8,128)(2,1)S(1)} %collective-permute-done.7.refs_2_, ...), custom_call_target="tpu_custom_call" | custom-call | tf_op jit(solution)/shard_map/weights/pallas_call | solution.py:473
  31.5 2.3 %collective-permute-start.11 = (bf16[32,1024]{1,0:T(8,128)(2,1)S(1)}, bf16[32,1024]{1,0:T(8,128)(2,1)S(1)}, u32[]{:S(2)}, u32[]{:S(2)}) collective-permute-start(bf16[32,1024]{1,0:T(8,128)(2,1)S(1)} %get-tuple-element.48.refs_0_), channel_id=1, source_target_pairs={{0,3},{1,2},{2,1},{3,0},{4,7},{5,6},{6,5},{7,4},{8,11},{9,10},{10,... | collective-permute-start | bytes 196616 | tf_op jit(solution)/shard_map/ppermute | solution.py:32
  34.1 1.7 %collective-permute-start.9 = (bf16[32,1024]{1,0:T(8,128)(2,1)S(1)}, bf16[32,1024]{1,0:T(8,128)(2,1)S(1)}, u32[]{:S(2)}, u32[]{:S(2)}) collective-permute-start(bf16[32,1024]{1,0:T(8,128)(2,1)S(1)} %get-tuple-element.48.refs_0_), channel_id=1, source_target_pairs={{0,1},{1,0},{2,3},{3,2},{4,5},{5,4},{6,7},{7,6},{8,9},{9,8},{10,11... | collective-permute-start | bytes 196616 | tf_op jit(solution)/shard_map/ppermute | solution.py:32
  35.9 2.4 %values.3 = (bf16[1024,512]{1,0:T(8,128)(2,1)S(1)}, bf16[1024,2048]{1,0:T(8,128)(2,1)S(1)}) custom-call(bf16[1024,2048]{1,0:T(8,128)(2,1)S(1)} %get-tuple-element.36.x_ref, bf16[2048,2048]{1,0:T(8,128)(2,1)S(1)} %get-tuple-element.37.w_ref, bf16[2048,2048]{1,0:T(8,128)(2,1)} %o_hbm.3, bf16[32,128]{1,0:T(8,128)(2,1)S(1)} %get-tuple-element.49.after.refs_4_), custom_call_target="tpu_custom_call" | custom-call | flops 2147483648 | bytes 8388608 | tf_op jit(solution)/shard_map/values/pallas_call | solution.py:232
  38.3 2.2 %collective-permute-done.10.refs_2_ = bf16[32,1024]{1,0:T(8,128)(2,1)S(1)} collective-permute-done((bf16[32,1024]{1,0:T(8,128)(2,1)S(1)}, bf16[32,1024]{1,0:T(8,128)(2,1)S(1)}, u32[]{:S(2)}, u32[]{:S(2)}) %collective-permute-start.10) | collective-permute-done | bytes 65568 | tf_op jit(solution)/shard_map/ppermute | solution.py:32
  40.5 1.3 %weighted.1 = (bf16[8,32,128]{2,1,0:T(8,128)(2,1)S(1)}, bf16[8,32,128]{2,1,0:T(8,128)(2,1)S(1)}, bf16[8,32,128]{2,1,0:T(8,128)(2,1)S(1)}, bf16[8,32,128]{2,1,0:T(8,128)(2,1)S(1)}) custom-call(bf16[32,1024]{1,0:T(8,128)(2,1)S(1)} %get-tuple-element.48.refs_0_, bf16[32,1024]{1,0:T(8,128)(2,1)S(1)} %collective-permute-done.9.refs_1_, ...), custom_call_target="tpu_custom_call" | custom-call | flops 33554432 | bytes 8388608 | tf_op jit(solution)/shard_map/weighted/pallas_call | solution.py:518
  41.7 2.0 %collective-permute-start.12 = (bf16[8,32,128]{2,1,0:T(8,128)(2,1)S(1)}, bf16[8,32,128]{2,1,0:T(8,128)(2,1)S(1)}, u32[]{:S(2)}, u32[]{:S(2)}) collective-permute-start(bf16[8,32,128]{2,1,0:T(8,128)(2,1)S(1)} %get-tuple-element.52), channel_id=1, source_target_pairs={{0,3},{1,2},{2,1},{3,0},{4,7},{5,6},{6,5},{7,4},{8,11},{9,10},{10,... | collective-permute-start | bytes 196616 | tf_op jit(solution)/shard_map/ppermute | solution.py:32
  43.7 2.5 %collective-permute-start.14 = (bf16[8,32,128]{2,1,0:T(8,128)(2,1)S(1)}, bf16[8,32,128]{2,1,0:T(8,128)(2,1)S(1)}, u32[]{:S(2)}, u32[]{:S(2)}) collective-permute-start(bf16[8,32,128]{2,1,0:T(8,128)(2,1)S(1)} %get-tuple-element.54), channel_id=1, source_target_pairs={{0,1},{1,0},{2,3},{3,2},{4,5},{5,4},{6,7},{7,6},{8,9},{9,8},{10,11... | collective-permute-start | bytes 196616 | tf_op jit(solution)/shard_map/ppermute | solution.py:32
  46.2 2.0 %collective-permute-done.12.refs_1_ = bf16[8,32,128]{2,1,0:T(8,128)(2,1)S(1)} collective-permute-done((bf16[8,32,128]{2,1,0:T(8,128)(2,1)S(1)}, bf16[8,32,128]{2,1,0:T(8,128)(2,1)S(1)}, u32[]{:S(2)}, u32[]{:S(2)}) %collective-permute-start.12) | collective-permute-done | bytes 65568 | tf_op jit(solution)/shard_map/ppermute | solution.py:32
  48.2 1.7 %collective-permute-done.13.refs_2_ = bf16[8,32,128]{2,1,0:T(8,128)(2,1)S(1)} collective-permute-done((bf16[8,32,128]{2,1,0:T(8,128)(2,1)S(1)}, bf16[8,32,128]{2,1,0:T(8,128)(2,1)S(1)}, u32[]{:S(2)}, u32[]{:S(2)}) %collective-permute-start.13) | collective-permute-done | bytes 65568 | tf_op jit(solution)/shard_map/ppermute | solution.py:32
  50.1 1.2 %collective-permute-start.16 = (bf16[9,32,128]{2,1,0:T(8,128)(2,1)S(1)}, bf16[9,32,128]{2,1,0:T(8,128)(2,1)S(1)}, u32[]{:S(2)}, u32[]{:S(2)}) collective-permute-start(bf16[9,32,128]{2,1,0:T(8,128)(2,1)S(1)} %summed.1.refs_0_), channel_id=1, source_target_pairs={{0,8},{4,12},{8,0},{12,4},{1,9},{5,13},{9,1},{13,5},{2,10},{6,14},... | collective-permute-start | bytes 221192 | tf_op jit(solution)/shard_map/ppermute | solution.py:32
  51.8 0.8 %fresh.1 = (f32[2,32,128]{2,1,0:T(8,128)S(1)}, f32[16,32,128]{2,1,0:T(8,128)S(1)}) custom-call(bf16[2,2,80,128]{3,2,1,0:T(8,128)(2,1)S(1)} %stacked.1.after.refs_0_, bf16[2,2,80,128]{3,2,1,0:T(8,128)(2,1)S(1)} %collective-permute-done.3.refs_1_, bf16[2,2,80,128]{3,2,1,0:T(8,128)(2,1)S(1)} %collective-permute-done.4.refs_2_, ...), custom_call_target="tpu_custom_call" | custom-call | bytes 2097152 | tf_op jit(solution)/shard_map/fresh/pallas_call | solution.py:414
  52.7 1.9 %collective-permute-done.17.refs_3_ = bf16[9,32,128]{2,1,0:T(8,128)(2,1)S(1)} collective-permute-done((bf16[9,32,128]{2,1,0:T(8,128)(2,1)S(1)}, bf16[9,32,128]{2,1,0:T(8,128)(2,1)S(1)}, u32[]{:S(2)}, u32[]{:S(2)}) %collective-permute-start.17) | collective-permute-done | bytes 73760 | tf_op jit(solution)/shard_map/ppermute | solution.py:32
  54.6 1.3 %collective-permute-done.16.refs_2_ = bf16[9,32,128]{2,1,0:T(8,128)(2,1)S(1)} collective-permute-done((bf16[9,32,128]{2,1,0:T(8,128)(2,1)S(1)}, bf16[9,32,128]{2,1,0:T(8,128)(2,1)S(1)}, u32[]{:S(2)}, u32[]{:S(2)}) %collective-permute-start.16) | collective-permute-done | bytes 73760 | tf_op jit(solution)/shard_map/ppermute | solution.py:32
  55.8 1.6 %output.1.refs_0_ = bf16[16,2048]{1,0:T(8,128)(2,1)S(1)} custom-call(bf16[9,32,128]{2,1,0:T(8,128)(2,1)S(1)} %summed.1.refs_0_, bf16[9,32,128]{2,1,0:T(8,128)(2,1)S(1)} %collective-permute-done.15.refs_1_, bf16[9,32,128]{2,1,0:T(8,128)(2,1)S(1)} %collective-permute-done.16.refs_2_, bf16[9,32,128]{2,1,0:T(8,128)(2,1)S(1)} %collective-permute-done.17.refs_3_, ...), custom_call_target="tpu_custom_call" | custom-call | tf_op jit(solution)/shard_map/output/pallas_call | solution.py:612
  57.4 2.2 %collective-permute-start.20 = (bf16[16,2048]{1,0:T(8,128)(2,1)S(1)}, bf16[16,2048]{1,0:T(8,128)(2,1)S(1)}, u32[]{:S(2)}, u32[]{:S(2)}) collective-permute-start(bf16[16,2048]{1,0:T(8,128)(2,1)S(1)} %output.1.refs_0_), channel_id=1, source_target_pairs={{0,3},{1,2},{2,1},{3,0},{4,7},{5,6},{6,5},{7,4},{8,11},{9,10},{10,... | collective-permute-start | bytes 196616 | tf_op jit(solution)/shard_map/ppermute | solution.py:32
  59.6 2.1 %collective-permute-start.18 = (bf16[16,2048]{1,0:T(8,128)(2,1)S(1)}, bf16[16,2048]{1,0:T(8,128)(2,1)S(1)}, u32[]{:S(2)}, u32[]{:S(2)}) collective-permute-start(bf16[16,2048]{1,0:T(8,128)(2,1)S(1)} %output.1.refs_0_), channel_id=1, source_target_pairs={{0,1},{1,0},{2,3},{3,2},{4,5},{5,4},{6,7},{7,6},{8,9},{9,8},{10,11... | collective-permute-start | bytes 196616 | tf_op jit(solution)/shard_map/ppermute | solution.py:32
  61.8 2.3 %collective-permute-done.20.refs_3_ = bf16[16,2048]{1,0:T(8,128)(2,1)S(1)} collective-permute-done((bf16[16,2048]{1,0:T(8,128)(2,1)S(1)}, bf16[16,2048]{1,0:T(8,128)(2,1)S(1)}, u32[]{:S(2)}, u32[]{:S(2)}) %collective-permute-start.20) | collective-permute-done | bytes 65568 | tf_op jit(solution)/shard_map/ppermute | solution.py:32
  64.1 2.0 %collective-permute-done.19.refs_2_ = bf16[16,2048]{1,0:T(8,128)(2,1)S(1)} collective-permute-done((bf16[16,2048]{1,0:T(8,128)(2,1)S(1)}, bf16[16,2048]{1,0:T(8,128)(2,1)S(1)}, u32[]{:S(2)}, u32[]{:S(2)}) %collective-permute-start.19) | collective-permute-done | bytes 65568 | tf_op jit(solution)/shard_map/ppermute | solution.py:32
  66.1 0.7 %final.1 = f32[8,2,2048]{2,1,0:T(2,128)} custom-call(bf16[16,2048]{1,0:T(8,128)(2,1)S(1)} %output.1.refs_0_, bf16[16,2048]{1,0:T(8,128)(2,1)S(1)} %collective-permute-done.18.refs_1_, bf16[16,2048]{1,0:T(8,128)(2,1)S(1)} %collective-permute-done.19.refs_2_, bf16[16,2048]{1,0:T(8,128)(2,1)S(1)} %collective-permute-done.20.refs_3_, bf16[8,2,2048]{2,1,0:T(2,128)(2,1)S(1)} %copy-done), custom_call_target="tpu_custom_call" | custom-call | tf_op jit(solution)/shard_map/final/pallas_call | solution.py:636
  (25 shorter events, 1.9 us)
Async XLA Ops:
  0.7 11.8 %collective-permute-start.2 = (bf16[2,2,16,128]{3,2,1,0:T(8,128)(2,1)S(1)}, bf16[2,2,16,128]{3,2,1,0:T(8,128)(2,1)S(1)}, u32[]{:S(2)}, u32[]{:S(2)}) collective-permute-start(bf16[2,2,16,128]{3,2,1,0:T(8,128)(2,1)S(1)} %get-tuple-element.32.refs_0_), channel_id=1, source_target_pairs={{0,3},{1,2},{2,1},{3,0},{4,7},{5,6},{6,5},{7,4},{8,11},{9,10},{10,... | collective-permute-start | bytes 49160 | tf_op jit(solution)/shard_map/ppermute | solution.py:32
  5.9 6.7 %collective-permute-start.1 = (bf16[2,2,16,128]{3,2,1,0:T(8,128)(2,1)S(1)}, bf16[2,2,16,128]{3,2,1,0:T(8,128)(2,1)S(1)}, u32[]{:S(2)}, u32[]{:S(2)}) collective-permute-start(bf16[2,2,16,128]{3,2,1,0:T(8,128)(2,1)S(1)} %get-tuple-element.32.refs_0_), channel_id=1, source_target_pairs={{0,2},{1,3},{2,0},{3,1},{4,6},{5,7},{6,4},{7,5},{8,10},{9,11},{10,... | collective-permute-start | bytes 49160 | tf_op jit(solution)/shard_map/ppermute | solution.py:32
  5.9 6.7 %collective-permute-start = (bf16[2,2,16,128]{3,2,1,0:T(8,128)(2,1)S(1)}, bf16[2,2,16,128]{3,2,1,0:T(8,128)(2,1)S(1)}, u32[]{:S(2)}, u32[]{:S(2)}) collective-permute-start(bf16[2,2,16,128]{3,2,1,0:T(8,128)(2,1)S(1)} %get-tuple-element.32.refs_0_), channel_id=1, source_target_pairs={{0,1},{1,0},{2,3},{3,2},{4,5},{5,4},{6,7},{7,6},{8,9},{9,8},{10,11... | collective-permute-start | bytes 49160 | tf_op jit(solution)/shard_map/ppermute | solution.py:32
  12.6 4.7 %collective-permute-start.5 = (bf16[2,2,80,128]{3,2,1,0:T(8,128)(2,1)S(1)}, bf16[2,2,80,128]{3,2,1,0:T(8,128)(2,1)S(1)}, u32[]{:S(2)}, u32[]{:S(2)}) collective-permute-start(bf16[2,2,80,128]{3,2,1,0:T(8,128)(2,1)S(1)} %stacked.1.after.refs_0_), channel_id=1, source_target_pairs={{0,12},{4,8},{8,4},{12,0},{1,13},{5,9},{9,5},{13,1},{2,14},{6,10},... | collective-permute-start | bytes 245768 | tf_op jit(solution)/shard_map/ppermute | solution.py:32
  13.1 6.1 %collective-permute-start.4 = (bf16[2,2,80,128]{3,2,1,0:T(8,128)(2,1)S(1)}, bf16[2,2,80,128]{3,2,1,0:T(8,128)(2,1)S(1)}, u32[]{:S(2)}, u32[]{:S(2)}) collective-permute-start(bf16[2,2,80,128]{3,2,1,0:T(8,128)(2,1)S(1)} %stacked.1.after.refs_0_), channel_id=1, source_target_pairs={{0,8},{4,12},{8,0},{12,4},{1,9},{5,13},{9,1},{13,5},{2,10},{6,14},... | collective-permute-start | bytes 245768 | tf_op jit(solution)/shard_map/ppermute | solution.py:32
  14.4 4.8 %collective-permute-start.3 = (bf16[2,2,80,128]{3,2,1,0:T(8,128)(2,1)S(1)}, bf16[2,2,80,128]{3,2,1,0:T(8,128)(2,1)S(1)}, u32[]{:S(2)}, u32[]{:S(2)}) collective-permute-start(bf16[2,2,80,128]{3,2,1,0:T(8,128)(2,1)S(1)} %stacked.1.after.refs_0_), channel_id=1, source_target_pairs={{0,4},{4,0},{8,12},{12,8},{1,5},{5,1},{9,13},{13,9},{2,6},{6,2},{1... | collective-permute-start | bytes 245768 | tf_op jit(solution)/shard_map/ppermute | solution.py:32
  21.1 6.8 %collective-permute-start.6 = (bf16[32,1024]{1,0:T(8,128)(2,1)S(1)}, bf16[32,1024]{1,0:T(8,128)(2,1)S(1)}, u32[]{:S(2)}, u32[]{:S(2)}) collective-permute-start(bf16[32,1024]{1,0:T(8,128)(2,1)S(1)} %get-tuple-element.43), channel_id=1, source_target_pairs={{0,3},{1,2},{2,1},{3,0},{4,7},{5,6},{6,5},{7,4},{8,11},{9,10},{10,... | collective-permute-start | bytes 196616 | tf_op jit(solution)/shard_map/ppermute | solution.py:32
  24.9 5.7 %collective-permute-start.7 = (bf16[32,1024]{1,0:T(8,128)(2,1)S(1)}, bf16[32,1024]{1,0:T(8,128)(2,1)S(1)}, u32[]{:S(2)}, u32[]{:S(2)}) collective-permute-start(bf16[32,1024]{1,0:T(8,128)(2,1)S(1)} %get-tuple-element.44), channel_id=1, source_target_pairs={{0,2},{1,3},{2,0},{3,1},{4,6},{5,7},{6,4},{7,5},{8,10},{9,11},{10,... | collective-permute-start | bytes 196616 | tf_op jit(solution)/shard_map/ppermute | solution.py:32
  24.9 5.7 %collective-permute-start.8 = (bf16[32,1024]{1,0:T(8,128)(2,1)S(1)}, bf16[32,1024]{1,0:T(8,128)(2,1)S(1)}, u32[]{:S(2)}, u32[]{:S(2)}) collective-permute-start(bf16[32,1024]{1,0:T(8,128)(2,1)S(1)} %get-tuple-element.45), channel_id=1, source_target_pairs={{0,1},{1,0},{2,3},{3,2},{4,5},{5,4},{6,7},{7,6},{8,9},{9,8},{10,11... | collective-permute-start | bytes 196616 | tf_op jit(solution)/shard_map/ppermute | solution.py:32
  31.5 6.8 %collective-permute-start.11 = (bf16[32,1024]{1,0:T(8,128)(2,1)S(1)}, bf16[32,1024]{1,0:T(8,128)(2,1)S(1)}, u32[]{:S(2)}, u32[]{:S(2)}) collective-permute-start(bf16[32,1024]{1,0:T(8,128)(2,1)S(1)} %get-tuple-element.48.refs_0_), channel_id=1, source_target_pairs={{0,3},{1,2},{2,1},{3,0},{4,7},{5,6},{6,5},{7,4},{8,11},{9,10},{10,... | collective-permute-start | bytes 196616 | tf_op jit(solution)/shard_map/ppermute | solution.py:32
  33.7 6.7 %collective-permute-start.10 = (bf16[32,1024]{1,0:T(8,128)(2,1)S(1)}, bf16[32,1024]{1,0:T(8,128)(2,1)S(1)}, u32[]{:S(2)}, u32[]{:S(2)}) collective-permute-start(bf16[32,1024]{1,0:T(8,128)(2,1)S(1)} %get-tuple-element.48.refs_0_), channel_id=1, source_target_pairs={{0,2},{1,3},{2,0},{3,1},{4,6},{5,7},{6,4},{7,5},{8,10},{9,11},{10,... | collective-permute-start | bytes 196616 | tf_op jit(solution)/shard_map/ppermute | solution.py:32
  34.1 6.3 %collective-permute-start.9 = (bf16[32,1024]{1,0:T(8,128)(2,1)S(1)}, bf16[32,1024]{1,0:T(8,128)(2,1)S(1)}, u32[]{:S(2)}, u32[]{:S(2)}) collective-permute-start(bf16[32,1024]{1,0:T(8,128)(2,1)S(1)} %get-tuple-element.48.refs_0_), channel_id=1, source_target_pairs={{0,1},{1,0},{2,3},{3,2},{4,5},{5,4},{6,7},{7,6},{8,9},{9,8},{10,11... | collective-permute-start | bytes 196616 | tf_op jit(solution)/shard_map/ppermute | solution.py:32
  41.7 6.4 %collective-permute-start.12 = (bf16[8,32,128]{2,1,0:T(8,128)(2,1)S(1)}, bf16[8,32,128]{2,1,0:T(8,128)(2,1)S(1)}, u32[]{:S(2)}, u32[]{:S(2)}) collective-permute-start(bf16[8,32,128]{2,1,0:T(8,128)(2,1)S(1)} %get-tuple-element.52), channel_id=1, source_target_pairs={{0,3},{1,2},{2,1},{3,0},{4,7},{5,6},{6,5},{7,4},{8,11},{9,10},{10,... | collective-permute-start | bytes 196616 | tf_op jit(solution)/shard_map/ppermute | solution.py:32
  43.7 6.2 %collective-permute-start.13 = (bf16[8,32,128]{2,1,0:T(8,128)(2,1)S(1)}, bf16[8,32,128]{2,1,0:T(8,128)(2,1)S(1)}, u32[]{:S(2)}, u32[]{:S(2)}) collective-permute-start(bf16[8,32,128]{2,1,0:T(8,128)(2,1)S(1)} %get-tuple-element.53), channel_id=1, source_target_pairs={{0,2},{1,3},{2,0},{3,1},{4,6},{5,7},{6,4},{7,5},{8,10},{9,11},{10,... | collective-permute-start | bytes 196616 | tf_op jit(solution)/shard_map/ppermute | solution.py:32
  43.7 6.2 %collective-permute-start.14 = (bf16[8,32,128]{2,1,0:T(8,128)(2,1)S(1)}, bf16[8,32,128]{2,1,0:T(8,128)(2,1)S(1)}, u32[]{:S(2)}, u32[]{:S(2)}) collective-permute-start(bf16[8,32,128]{2,1,0:T(8,128)(2,1)S(1)} %get-tuple-element.54), channel_id=1, source_target_pairs={{0,1},{1,0},{2,3},{3,2},{4,5},{5,4},{6,7},{7,6},{8,9},{9,8},{10,11... | collective-permute-start | bytes 196616 | tf_op jit(solution)/shard_map/ppermute | solution.py:32
  49.9 4.6 %collective-permute-start.17 = (bf16[9,32,128]{2,1,0:T(8,128)(2,1)S(1)}, bf16[9,32,128]{2,1,0:T(8,128)(2,1)S(1)}, u32[]{:S(2)}, u32[]{:S(2)}) collective-permute-start(bf16[9,32,128]{2,1,0:T(8,128)(2,1)S(1)} %summed.1.refs_0_), channel_id=1, source_target_pairs={{0,12},{4,8},{8,4},{12,0},{1,13},{5,9},{9,5},{13,1},{2,14},{6,10},... | collective-permute-start | bytes 221192 | tf_op jit(solution)/shard_map/ppermute | solution.py:32
  50.1 5.7 %collective-permute-start.16 = (bf16[9,32,128]{2,1,0:T(8,128)(2,1)S(1)}, bf16[9,32,128]{2,1,0:T(8,128)(2,1)S(1)}, u32[]{:S(2)}, u32[]{:S(2)}) collective-permute-start(bf16[9,32,128]{2,1,0:T(8,128)(2,1)S(1)} %summed.1.refs_0_), channel_id=1, source_target_pairs={{0,8},{4,12},{8,0},{12,4},{1,9},{5,13},{9,1},{13,5},{2,10},{6,14},... | collective-permute-start | bytes 221192 | tf_op jit(solution)/shard_map/ppermute | solution.py:32
  51.3 4.5 %collective-permute-start.15 = (bf16[9,32,128]{2,1,0:T(8,128)(2,1)S(1)}, bf16[9,32,128]{2,1,0:T(8,128)(2,1)S(1)}, u32[]{:S(2)}, u32[]{:S(2)}) collective-permute-start(bf16[9,32,128]{2,1,0:T(8,128)(2,1)S(1)} %summed.1.refs_0_), channel_id=1, source_target_pairs={{0,4},{4,0},{8,12},{12,8},{1,5},{5,1},{9,13},{13,9},{2,6},{6,2},{1... | collective-permute-start | bytes 221192 | tf_op jit(solution)/shard_map/ppermute | solution.py:32
  55.8 10.3 %copy-start = (bf16[8,2,2048]{2,1,0:T(2,128)(2,1)S(1)}, bf16[8,2,2048]{2,1,0:T(2,128)(2,1)}, u32[]{:S(2)}) copy-start(bf16[8,2,2048]{2,1,0:T(2,128)(2,1)} %refs_4_.1) | copy-start | bytes 196612
  57.4 6.7 %collective-permute-start.20 = (bf16[16,2048]{1,0:T(8,128)(2,1)S(1)}, bf16[16,2048]{1,0:T(8,128)(2,1)S(1)}, u32[]{:S(2)}, u32[]{:S(2)}) collective-permute-start(bf16[16,2048]{1,0:T(8,128)(2,1)S(1)} %output.1.refs_0_), channel_id=1, source_target_pairs={{0,3},{1,2},{2,1},{3,0},{4,7},{5,6},{6,5},{7,4},{8,11},{9,10},{10,... | collective-permute-start | bytes 196616 | tf_op jit(solution)/shard_map/ppermute | solution.py:32
  59.6 6.5 %collective-permute-start.19 = (bf16[16,2048]{1,0:T(8,128)(2,1)S(1)}, bf16[16,2048]{1,0:T(8,128)(2,1)S(1)}, u32[]{:S(2)}, u32[]{:S(2)}) collective-permute-start(bf16[16,2048]{1,0:T(8,128)(2,1)S(1)} %output.1.refs_0_), channel_id=1, source_target_pairs={{0,2},{1,3},{2,0},{3,1},{4,6},{5,7},{6,4},{7,5},{8,10},{9,11},{10,... | collective-permute-start | bytes 196616 | tf_op jit(solution)/shard_map/ppermute | solution.py:32
  59.6 6.5 %collective-permute-start.18 = (bf16[16,2048]{1,0:T(8,128)(2,1)S(1)}, bf16[16,2048]{1,0:T(8,128)(2,1)S(1)}, u32[]{:S(2)}, u32[]{:S(2)}) collective-permute-start(bf16[16,2048]{1,0:T(8,128)(2,1)S(1)} %output.1.refs_0_), channel_id=1, source_target_pairs={{0,1},{1,0},{2,3},{3,2},{4,5},{5,4},{6,7},{7,6},{8,9},{9,8},{10,11... | collective-permute-start | bytes 196616 | tf_op jit(solution)/shard_map/ppermute | solution.py:32

commit v10 on v9

--- a/solution.py
+++ b/solution.py
@@ -107,47 +107,54 @@
     return jnp.concatenate([w_ref[rows, c : c + HD] for c in at], axis=1)
 
 
-PARTS = 4
-
-
-def load_kernel(pages, prompts, new_count, x_hbm, w_hbm, counts, tails, *refs):
-    acc, x_ref, w_ref, cos_ref, sin_ref, cos_q, sin_q, meta, x_sems, w_sems = refs
-    tokens, depth = x_ref.shape
-    size, tall = depth // PARTS, tokens // 2
-    copies = []
-    for i in range(PARTS):
-        at = pl.ds(i * size, size)
-        x_copy = pltpu.make_async_copy(x_hbm.at[:, at], x_ref.at[:, at], x_sems.at[i])
-        w_copy = pltpu.make_async_copy(w_hbm.at[at], w_ref.at[at], w_sems.at[i])
+def copies_of(x_hbm, w_hbm, x_ref, w_ref, sems, first, size, count):
+    pairs_of = []
+    for i in range(count):
+        source, to = pl.ds(first + i * size, size), pl.ds(i * size, size)
+        x_copy = pltpu.make_async_copy(x_hbm.at[:, source], x_ref.at[:, to], sems.at[2 * i])
+        w_copy = pltpu.make_async_copy(w_hbm.at[source], w_ref.at[to], sems.at[2 * i + 1])
         x_copy.start()
         w_copy.start()
-        copies.append((x_copy, w_copy))
+        pairs_of.append((x_copy, w_copy))
+    return pairs_of
+
+
+def add_block(x_ref, w_ref, rows, acc, out, fresh):
+    tokens = x_ref.shape[0]
+    tall = tokens // 2
+    for pair in range(KVH // 2):
+        weight = pair_columns(w_ref, rows, pair, 0)
+        columns = slice(2 * pair * HD, 2 * (pair + 1) * HD)
+        for start in range(0, tokens, tall):
+            at = slice(start, start + tall)
+            product = jnp.dot(x_ref[at, rows], weight, preferred_element_type=F32)
+            out[at, columns] = product if fresh else acc[at, columns] + product
+
+
+def load_kernel(pages, prompts, new_count, x_hbm, w_hbm, counts, tails, *refs):
+    acc, x_ref, w_ref, cos_ref, sin_ref, cos_q, sin_q, meta, sems = refs
+    tokens = x_ref.shape[0]
+    size = x_ref.shape[1] // 3
+    copies = copies_of(x_hbm, w_hbm, x_ref, w_ref, sems, 0, size, 3)
     page_table(pages, prompts, counts, tails, meta)
     rotation_tables(pages, tokens // PAGE, meta, cos_ref, sin_ref)
     spots = [meta[3 * pages + r] + n for r in range(prompts) for n in range(new_count)]
     angles = by_row(len(spots), spots) * lane_freqs(len(spots))
     cos_q[...] = jnp.cos(angles)
     sin_q[...] = jnp.sin(angles) * sine_sign(len(spots))
-    for i in range(PARTS // 2):
+    for i in range(2):
         for copy in copies[i]:
             copy.wait()
-        rows = slice(i * size, (i + 1) * size)
-        for pair in range(KVH // 2):
-            weight = pair_columns(w_ref, rows, pair, 0)
-            columns = slice(2 * pair * HD, 2 * (pair + 1) * HD)
-            for start in range(0, tokens, tall):
-                at = slice(start, start + tall)
-                product = jnp.dot(x_ref[at, rows], weight, preferred_element_type=F32)
-                acc[at, columns] = product if i == 0 else acc[at, columns] + product
-    for pair_of_copies in copies[PARTS // 2 :]:
-        for copy in pair_of_copies:
-            copy.wait()
+        add_block(x_ref, w_ref, slice(i * size, (i + 1) * size), acc, acc, i == 0)
+    for copy in copies[2]:
+        copy.wait()
 
 
 def load(x, kv_weight, counts, tails, pages, new_count):
     tokens, depth = x.shape
     columns = kv_weight.shape[1]
     prompts = counts.shape[0]
+    part = depth // 4 * 3
     hbm = pl.BlockSpec(memory_space=pltpu.HBM)
     return pl.pallas_call(
         functools.partial(load_kernel, pages, prompts, new_count),
@@ -155,37 +162,38 @@
         out_specs=[VMEM] * 7 + [SMEM],
         out_shape=[
             pltpu.VMEM((tokens, KVH * HD), F32),
-            pltpu.VMEM((tokens, depth), BF16),
-            pltpu.VMEM((depth, columns), BF16),
+            pltpu.VMEM((tokens, part), BF16),
+            pltpu.VMEM((part, columns), BF16),
             pltpu.VMEM((tokens, HD), F32),
             pltpu.VMEM((tokens, HD), F32),
             pltpu.VMEM((prompts * new_count, HD), F32),
             pltpu.VMEM((prompts * new_count, HD), F32),
             jax.ShapeDtypeStruct((3 * pages + prompts,), jnp.int32),
         ],
-        scratch_shapes=[pltpu.SemaphoreType.DMA((PARTS,)), pltpu.SemaphoreType.DMA((PARTS,))],
+        scratch_shapes=[pltpu.SemaphoreType.DMA((6,))],
         compiler_params=pltpu.CompilerParams(vmem_limit_bytes=28 * MIB),
         cost_estimate=pl.CostEstimate(
-            flops=3 * tokens * depth // 2 * KVH * HD,
-            bytes_accessed=2 * depth * (tokens + columns),
+            flops=tokens * depth * KVH * HD,
+            bytes_accessed=2 * part * (tokens + columns),
             transcendentals=0,
         ),
         name="load",
     )(*[in_hbm(a) for a in (x, kv_weight, counts, tails)])
 
 
-def keys_kernel(acc, x_ref, w_ref, cos_ref, sin_ref, after, k_ref):
-    tokens, depth = x_ref.shape
+def keys_kernel(acc, xa_ref, wa_ref, x_hbm, w_hbm, cos_ref, sin_ref, after, k_ref, x_ref, w_ref, total, sems):
+    tokens, size = x_ref.shape
     tall = tokens // 2
-    rows = slice(depth // 2, depth)
+    ((x_copy, w_copy),) = copies_of(x_hbm, w_hbm, x_ref, w_ref, sems, 3 * size, size, 1)
+    add_block(xa_ref, wa_ref, slice(2 * size, 3 * size), acc, total, False)
+    x_copy.wait()
+    w_copy.wait()
     for pair in range(KVH // 2):
-        weight = pair_columns(w_ref, rows, pair, 0)
+        weight = pair_columns(w_ref, slice(None), pair, 0)
         columns = slice(2 * pair * HD, 2 * (pair + 1) * HD)
         for start in range(0, tokens, tall):
             at = slice(start, start + tall)
-            product = acc[at, columns] + jnp.dot(
-                x_ref[at, rows], weight, preferred_element_type=F32
-            )
+            product = total[at, columns] + jnp.dot(x_ref[at], weight, preferred_element_type=F32)
             cosine, sine = cos_ref[at], sin_ref[at]
             for h in range(2):
                 k = product[:, h * HD : (h + 1) * HD]
@@ -193,22 +201,32 @@
                 k_ref[at, (2 * pair + h) * HD : (2 * pair + h + 1) * HD] = k.astype(BF16)
 
 
-def rotated_keys(acc, x, weight, cosine, sine, after):
+def rotated_keys(acc, xa, wa, x, kv_weight, cosine, sine, after):
     tokens, depth = x.shape
+    columns = kv_weight.shape[1]
+    hbm = pl.BlockSpec(memory_space=pltpu.HBM)
     return pl.pallas_call(
         keys_kernel,
-        in_specs=[VMEM] * 5 + [ANY],
-        out_specs=VMEM,
-        out_shape=pltpu.VMEM((tokens, KVH * HD), BF16),
+        in_specs=[VMEM] * 3 + [hbm] * 2 + [VMEM] * 2 + [ANY],
+        out_specs=[VMEM] * 3,
+        out_shape=[
+            pltpu.VMEM((tokens, KVH * HD), BF16),
+            pltpu.VMEM((tokens, depth // 4), BF16),
+            pltpu.VMEM((depth // 4, columns), BF16),
+        ],
+        scratch_shapes=[
+            pltpu.VMEM((tokens, KVH * HD), F32),
+            pltpu.SemaphoreType.DMA((2,)),
+        ],
         compiler_params=pltpu.CompilerParams(vmem_limit_bytes=24 * MIB),
         cost_estimate=pl.CostEstimate(
-            flops=tokens * depth // 2 * KVH * HD, bytes_accessed=8 * MIB, transcendentals=0
+            flops=tokens * depth * KVH * HD, bytes_accessed=8 * MIB, transcendentals=0
         ),
         name="keys",
-    )(acc, x, weight, cosine, sine, after)
-
-
-def values_kernel(first, x_ref, w_ref, o_hbm, after, v_ref, o_ref, sem):
+    )(acc, xa, wa, in_hbm(x), in_hbm(kv_weight), cosine, sine, after)
+
+
+def values_kernel(first, xa_ref, wa_ref, xb_ref, wb_ref, o_hbm, after, v_ref, o_ref, sem):
     depth = o_ref.shape[0]
     copy = pltpu.make_async_copy(o_hbm.at[pl.ds(first * depth, depth)], o_ref, sem)
     copy.start()
@@ -216,27 +234,22 @@
     tall = tokens // 2
     pairs_here = columns // (2 * HD)
     for pair in range(pairs_here):
-        weight = pair_columns(w_ref, slice(None), first * pairs_here + pair, 1)
+        weights = [pair_columns(w, slice(None), first * pairs_here + pair, 1) for w in (wa_ref, wb_ref)]
         for i in range(2):
             at = slice(i * tall, (i + 1) * tall)
-            v_ref[at, 2 * pair * HD : 2 * (pair + 1) * HD] = jnp.dot(
-                x_ref[at], weight, preferred_element_type=F32
-            ).astype(BF16)
+            product = jnp.dot(xa_ref[at], weights[0], preferred_element_type=F32)
+            product = product + jnp.dot(xb_ref[at], weights[1], preferred_element_type=F32)
+            v_ref[at, 2 * pair * HD : 2 * (pair + 1) * HD] = product.astype(BF16)
     copy.wait()
 
 
-def project_values(x, weight, out_weight, first, after):
-    tokens, depth = x.shape
+def project_values(blocks, out_weight, first, after):
+    tokens, depth = blocks[0].shape
     columns = KVH // 2 * HD
     rows = out_weight.shape[0] // 2
     return pl.pallas_call(
         functools.partial(values_kernel, first),
-        in_specs=[
-            VMEM,
-            VMEM,
-            pl.BlockSpec(memory_space=pltpu.HBM),
-            ANY,
-        ],
+        in_specs=[VMEM] * 4 + [pl.BlockSpec(memory_space=pltpu.HBM), ANY],
         out_specs=[VMEM, VMEM],
         out_shape=[
             pltpu.VMEM((tokens, columns), BF16),
@@ -248,7 +261,7 @@
             flops=2 * tokens * depth * columns, bytes_accessed=8 * MIB, transcendentals=0
         ),
         name="values",
-    )(x, weight, in_hbm(out_weight), after)
+    )(*blocks, in_hbm(out_weight), after)
 
 
 def by_heads(row):
@@ -280,62 +293,67 @@
     )(in_hbm(new_query), in_hbm(new_keyval))
 
 
-def stacked_kernel(n_tp, *refs):
-    kv_ref, _, out_ref = refs[n_tp:]
+def turned_kernel(n_tp, *refs):
+    kv_ref, cos_q, sin_q, out_ref = refs[n_tp:]
     own_rows, new_count, heads, _ = refs[0].shape
+    rows = new_count * GROUP
+    kv_local = heads // GROUP
+    me, seq = lax.axis_index("tp"), lax.axis_index("seq")
     for r in range(own_rows):
+        spots = [pl.ds((seq * own_rows + r) * new_count + n, 1) for n in range(new_count)]
+        turns = [(cos_q[spot], sin_q[spot]) for spot in spots]
+
+        def turn(value, n):
+            return value * turns[n][0] + pltpu.roll(value, HD // 2, 1) * turns[n][1]
+
+        for d in range(n_tp):
+            blocks = [refs[d][r, n].astype(F32) for n in range(new_count)]
+            for g in range(kv_local):
+                parts = [turn(q[g * GROUP : (g + 1) * GROUP], n) for n, q in enumerate(blocks)]
+                at = ((me ^ d) * kv_local + g) * rows
+                at = pl.ds(pl.multiple_of(at, rows), rows)
+                out_ref[r, at] = jnp.concatenate(parts, axis=0).astype(BF16)
+        fresh = []
         for n in range(new_count):
-            rows = [refs[d][r, n].astype(F32) for d in range(n_tp)] + [kv_ref[r, n]]
-            rows.append(jnp.zeros((out_ref.shape[2] - n_tp * heads - kv_ref.shape[2], HD), F32))
-            out_ref[r, n] = jnp.concatenate(rows, axis=0).astype(BF16)
-
-
-def stacked(pieces, fresh, after):
+            row = lax.broadcasted_iota(jnp.int32, kv_ref.shape[2:], 0)
+            fresh.append(jnp.where(row % 2 == 0, turn(kv_ref[r, n], n), kv_ref[r, n]))
+        fresh.append(jnp.zeros((FRESH - new_count * 2 * kv_local, HD), F32))
+        out_ref[r, KVH * rows :] = jnp.concatenate(fresh, axis=0).astype(BF16)
+
+
+FRESH = 16
+
+
+def turned(pieces, fresh, cos_q, sin_q):
     n_tp = len(pieces)
-    own_rows, new_count, heads, _ = pieces[0].shape
-    rows = n_tp * heads + 16
-    return pl.pallas_call(
-        functools.partial(stacked_kernel, n_tp),
-        in_specs=[VMEM] * (n_tp + 1) + [ANY],
+    own_rows, new_count, _, _ = pieces[0].shape
+    rows = KVH * GROUP * new_count + FRESH
+    return pl.pallas_call(
+        functools.partial(turned_kernel, n_tp),
+        in_specs=[VMEM] * (n_tp + 3),
         out_specs=VMEM,
-        out_shape=jax.ShapeDtypeStruct((own_rows, new_count, rows, HD), BF16),
+        out_shape=jax.ShapeDtypeStruct((own_rows, rows, HD), BF16),
         compiler_params=pltpu.CompilerParams(vmem_limit_bytes=8 * MIB),
-        name="stacked",
-    )(*pieces, fresh, after)
+        name="turned",
+    )(*pieces, fresh, cos_q, sin_q)
 
 
 def scores_kernel(n_seq, n_tp, *refs):
     new = refs[:n_seq]
-    k_ref, cos_q, sin_q, meta = refs[n_seq : n_seq + 4]
-    outs = refs[n_seq + 4 : n_seq + 4 + n_tp]
-    own_q, all_q, ready = refs[n_seq + 4 + n_tp :]
-    kv_local = KVH // n_tp
+    k_ref, meta = refs[n_seq : n_seq + 2]
+    outs = refs[n_seq + 2 : n_seq + 2 + n_tp]
+    all_q, ready = refs[n_seq + 2 + n_tp :]
+    own_rows = new[0].shape[0]
     local_pages = k_ref.shape[0] // PAGE
-    own_rows, new_count, _, _ = new[0].shape
-    rows = new_count * GROUP
-    count = kv_local * rows
+    rows = all_q.shape[1] // KVH
+    count = all_q.shape[1] // n_tp
     scale = 1.0 / math.sqrt(HD)
     me = lax.axis_index("tp")
     seq = lax.axis_index("seq")
     first = seq * local_pages
     for ds in range(n_seq):
         for rr in range(own_rows):
-            request = (seq ^ ds) * own_rows + rr
-            spots = [pl.ds(request * new_count + n, 1) for n in range(new_count)]
-            turn = [(cos_q[spot], sin_q[spot]) for spot in spots]
-            held = [new[ds][rr, n].astype(F32) for n in range(new_count)]
-            for dt in range(n_tp):
-                for g in range(kv_local):
-                    parts = []
-                    for n in range(new_count):
-                        row = (dt * kv_local + g) * GROUP
-                        q = held[n][row : row + GROUP]
-                        parts.append(q * turn[n][0] + pltpu.roll(q, HD // 2, 1) * turn[n][1])
-                    part = jnp.concatenate(parts, axis=0).astype(BF16)
-                    at = ((me ^ dt) * kv_local + g) * rows
-                    all_q[request, pl.ds(pl.multiple_of(at, rows), rows)] = part
-                    if dt == 0:
-                        own_q[request, g * rows : (g + 1) * rows] = part
+            all_q[(seq ^ ds) * own_rows + rr] = new[ds][rr, : KVH * rows]
     for p in range(local_pages):
         request = meta[first + p]
         tokens = slice(p * PAGE, (p + 1) * PAGE)
@@ -348,72 +366,66 @@
         outs[d][...] = ready[pl.ds(pl.multiple_of(partner(me, d, n_tp) * count, count), count)]
 
 
-def partial_scores(new, k, cos_q, sin_q, meta, prompts, n_tp):
+def partial_scores(new, k, meta, prompts, n_tp):
     n_seq = len(new)
-    new_count = new[0].shape[1]
+    all_rows = new[0].shape[1] - FRESH
     tokens = k.shape[0]
-    rows = KVH // n_tp * new_count * GROUP
+    rows = all_rows // n_tp
     return pl.pallas_call(
         functools.partial(scores_kernel, n_seq, n_tp),
-        in_specs=[VMEM] * (n_seq + 3) + [SMEM],
-        out_specs=[VMEM] * (n_tp + 1),
-        out_shape=[jax.ShapeDtypeStruct((rows, tokens), BF16)] * n_tp
-        + [jax.ShapeDtypeStruct((prompts, rows, HD), BF16)],
+        in_specs=[VMEM] * (n_seq + 1) + [SMEM],
+        out_specs=[VMEM] * n_tp,
+        out_shape=[jax.ShapeDtypeStruct((rows, tokens), BF16)] * n_tp,
         scratch_shapes=[
-            pltpu.VMEM((prompts, rows * n_tp, HD), BF16),
-            pltpu.VMEM((rows * n_tp, tokens), BF16),
+            pltpu.VMEM((prompts, all_rows, HD), BF16),
+            pltpu.VMEM((all_rows, tokens), BF16),
         ],
         compiler_params=pltpu.CompilerParams(vmem_limit_bytes=24 * MIB),
         cost_estimate=pl.CostEstimate(
-            flops=2 * tokens * rows * n_tp * HD, bytes_accessed=6 * MIB, transcendentals=0
+            flops=2 * tokens * all_rows * HD, bytes_accessed=6 * MIB, transcendentals=0
         ),
         name="scores",
-    )(*new, k, cos_q, sin_q, meta)
+    )(*new, k, meta)
 
 
 def fresh_kernel(n_seq, *refs):
     new = refs[:n_seq]
-    q_ref, cos_q, sin_q, score_ref, value_ref = refs[n_seq:]
-    prompts, rows_local, _ = q_ref.shape
-    own_rows, new_count, _, _ = new[0].shape
+    _, score_ref, value_ref = refs[n_seq:]
+    new_count, rows_local, _ = score_ref.shape
+    own_rows = new[0].shape[0]
     rows = new_count * GROUP
     kv_local = rows_local // rows
-    heads = QH
     scale = 1.0 / math.sqrt(HD)
     seq = lax.axis_index("seq")
+    own = pl.ds(pl.multiple_of(lax.axis_index("tp") * rows_local, rows_local), rows_local)
     step = lax.broadcasted_iota(jnp.int32, (rows_local, HD), 0) % rows // GROUP
     lane = lax.broadcasted_iota(jnp.int32, (rows_local, HD), 1)
     found = [jnp.full((rows_local, HD), NEG, F32) for _ in range(new_count)]
+
+    def spread(block, first):
+        parts = [block[first + 2 * g : first + 2 * g + 1] for g in range(kv_local)]
+        return jnp.concatenate([jnp.broadcast_to(a, (rows, HD)) for a in parts], axis=0)
+
     for ds in range(n_seq):
         for rr in range(own_rows):
             request = (seq ^ ds) * own_rows + rr
-            q = q_ref[request].astype(F32)
+            q = new[ds][rr, own].astype(F32)
+            both = new[ds][rr, KVH * rows :].astype(F32)
             for n in range(new_count):
-                spot = pl.ds(request * new_count + n, 1)
-                cosine, sine = cos_q[spot], sin_q[spot]
-                both = new[ds][rr, n].astype(F32)
-                keys, values = [], []
-                for g in range(kv_local):
-                    k = both[heads + 2 * g : heads + 2 * g + 1]
-                    k = k * cosine + pltpu.roll(k, HD // 2, 1) * sine
-                    k = k.astype(BF16).astype(F32)
-                    keys.append(jnp.broadcast_to(k, (rows, HD)))
-                    v = both[heads + 2 * g + 1 : heads + 2 * g + 2]
-                    values.append(jnp.broadcast_to(v, (rows, HD)))
-                s = jnp.sum(q * jnp.concatenate(keys, axis=0), axis=1, keepdims=True) * scale
+                first = n * 2 * kv_local
+                s = jnp.sum(q * spread(both, first), axis=1, keepdims=True) * scale
                 found[n] = jnp.where((lane == request) & (step >= n), s, found[n])
-                value_ref[request * new_count + n] = jnp.concatenate(values, axis=0)
+                value_ref[request * new_count + n] = spread(both, first + 1)
     for n in range(new_count):
         score_ref[n] = found[n]
 
 
-def fresh_scores(new, own_q, cos_q, sin_q):
+def fresh_scores(new, after, prompts, new_count, n_tp):
     n_seq = len(new)
-    new_count = new[0].shape[1]
-    prompts, rows, _ = own_q.shape
+    rows = (new[0].shape[1] - FRESH) // n_tp
     return pl.pallas_call(
         functools.partial(fresh_kernel, n_seq),
-        in_specs=[VMEM] * (n_seq + 3),
+        in_specs=[VMEM] * n_seq + [ANY],
         out_specs=[VMEM, VMEM],
         out_shape=[
             jax.ShapeDtypeStruct((new_count, rows, HD), F32),
@@ -422,7 +434,7 @@
         compiler_params=pltpu.CompilerParams(vmem_limit_bytes=16 * MIB),
         cost_estimate=pl.CostEstimate(flops=0, bytes_accessed=2 * MIB, transcendentals=0),
         name="fresh",
-    )(*new, own_q, cos_q, sin_q)
+    )(*new, after)
 
 
 def weights_kernel(pages, prompts, n_tp, *refs):
@@ -652,17 +664,17 @@
     pages = prefill_states.shape[0] // PAGE * n_seq
     query, new_kv = prepare(new_query, new_keyval)
     query = gather(query, "tp")
-    acc, x, w, cosine, sine, cos_q, sin_q, meta = load(
+    acc, xa, wa, cosine, sine, cos_q, sin_q, meta = load(
         prefill_states, kv_weight, page_counts, tail_tokens, pages, new_count
     )
-    new = stacked(query, new_kv, meta)
-    k = rotated_keys(acc, x, w, cosine, sine, new)
+    new = turned(query, new_kv, cos_q, sin_q)
+    k, xb, wb = rotated_keys(acc, xa, wa, prefill_states, kv_weight, cosine, sine, new)
     new = gather(new, "seq")
-    *scores, own_q = partial_scores(new, k, cos_q, sin_q, meta, prompts, n_tp)
-    va, oa = project_values(x, w, out_weight, 0, own_q)
-    fresh, values = fresh_scores(new, own_q, cos_q, sin_q)
+    scores = partial_scores(new, k, meta, prompts, n_tp)
+    va, oa = project_values((xa, wa, xb, wb), out_weight, 0, scores[0])
     weights, stats = softmax_weights(exchange(scores, "tp"), meta, va, pages, prompts)
-    vb, ob = project_values(x, w, out_weight, 1, stats)
+    vb, ob = project_values((xa, wa, xb, wb), out_weight, 1, stats)
+    fresh, values = fresh_scores(new, stats, prompts, new_count, n_tp)
     chunks = weighted_values(gather(weights, "tp"), va, vb, meta, prompts)
     pieces = gather(summed(exchange(chunks, "tp"), stats), "seq")
     partial = output_partial(pieces, fresh, values, (oa, ob))

time: 67.1 us -> 66.4 us (0.990)
    pallas_call x4, Pallas kernels: 7.5 us -> 8.4 us  [the longest x2 4.68 us: project_values(): pl.pallas_call(functools.partial(values_kernel, first), in_specs=[VMEM] *...]
    pallas_call x1, Pallas kernels: 0.82 us -> 0.14 us  [fresh_scores(): pl.pallas_call(functools.partial(fresh_kernel, n_seq), in_specs=[VMEM] *...]
where the time goes in v10:
time: 66.4 us; the launch traced here: 66.1 us
  starting transfers between devices  27.3 us (41%)
  Pallas kernels  21.2 us (32%)
  waiting for transfers between devices  17.4 us (26%)
    ppermute x21, starting transfers between devices, pairs(): lax.ppermute(value, axis, [(i, partner(i, entry, size)) for i in range(si...  27.3 us
    ppermute x21, waiting for transfers between devices, pairs(): lax.ppermute(value, axis, [(i, partner(i, entry, size)) for i in range(si...  17.4 us
    pallas_call x1, Pallas kernels, load(): pl.pallas_call(functools.partial(load_kernel, pages, prompts, new_count),...  5.68 us
    pallas_call x2, Pallas kernels, project_values(): pl.pallas_call(functools.partial(values_kernel, first), in_specs=[VMEM] *...  4.68 us
    pallas_call x1, Pallas kernels, rotated_keys(): pl.pallas_call(keys_kernel, in_specs=[VMEM] * 3 + [hbm] * 2 + [VMEM] * 2...  3.62 us
    pallas_call x1, Pallas kernels, partial_scores(): pl.pallas_call(functools.partial(scores_kernel, n_seq, n_tp), in_specs=[V...  1.76 us
    pallas_call x1, Pallas kernels, output_partial(): pl.pallas_call(functools.partial(output_kernel, n_seq), in_specs=[VMEM] *...  1.58 us
  transfers between devices with their start and end apart: 21, of which 9 were waited for; matrix products, arithmetic and copies ran while one was open for 0% of the time, Pallas kernels for 21%

profile of v10, /device:TPU:0, one launch (start us, length us, event | category | flops | bytes accessed | tf_op | source)
XLA Modules:
  0.0 66.1 jit_solution(6463089543932212114)
XLA Ops:
  0.0 0.7 %prepare.1 = (bf16[2,2,16,128]{3,2,1,0:T(8,128)(2,1)S(1)}, f32[2,2,4,128]{3,2,1,0:T(4,128)S(1)}) custom-call(bf16[2,2,2048]{2,1,0:T(2,128)(2,1)} %q_ref.1, bf16[2,2,512]{2,1,0:T(2,128)(2,1)} %kv_ref.1), custom_call_target="tpu_custom_call" | custom-call | bytes 1048576 | tf_op jit(solution)/shard_map/prepare/pallas_call | solution.py:282
  0.7 5.1 %collective-permute-start.2 = (bf16[2,2,16,128]{3,2,1,0:T(8,128)(2,1)S(1)}, bf16[2,2,16,128]{3,2,1,0:T(8,128)(2,1)S(1)}, u32[]{:S(2)}, u32[]{:S(2)}) collective-permute-start(bf16[2,2,16,128]{3,2,1,0:T(8,128)(2,1)S(1)} %get-tuple-element.34.refs_0_), channel_id=1, source_target_pairs={{0,3},{1,2},{2,1},{3,0},{4,7},{5,6},{6,5},{7,4},{8,11},{9,10},{10,... | collective-permute-start | bytes 49160 | tf_op jit(solution)/shard_map/ppermute | solution.py:32
  5.9 0.6 collective-permute-start
  6.5 5.7 %load.1 = (f32[1024,1024]{1,0:T(8,128)S(1)}, bf16[1024,1536]{1,0:T(8,128)(2,1)S(1)}, bf16[1536,2048]{1,0:T(8,128)(2,1)S(1)}, f32[1024,128]{1,0:T(8,128)S(1)}, f3...) custom-call(bf16[1024,2048]{1,0:T(8,128)(2,1)} %x_hbm.3, ...), custom_call_target="tpu_custom_call" | custom-call | flops 2147483648 | bytes 9437184 | tf_op jit(solution)/shard_map/load/pallas_call | solution.py:159
  12.8 1.3 %collective-permute-start.4 = (bf16[2,144,128]{2,1,0:T(8,128)(2,1)S(1)}, bf16[2,144,128]{2,1,0:T(8,128)(2,1)S(1)}, u32[]{:S(2)}, u32[]{:S(2)}) collective-permute-start(bf16[2,144,128]{2,1,0:T(8,128)(2,1)S(1)} %turned.1.after.refs_0_), channel_id=1, source_target_pairs={{0,8},{4,12},{8,0},{12,4},{1,9},{5,13},{9,1},{13,5},{2,10},{6,14},... | collective-permute-start | bytes 221192 | tf_op jit(solution)/shard_map/ppermute | solution.py:32
  14.3 3.6 %keys.1 = (bf16[1024,1024]{1,0:T(8,128)(2,1)S(1)}, bf16[1024,512]{1,0:T(8,128)(2,1)S(1)}, bf16[512,2048]{1,0:T(8,128)(2,1)S(1)}) custom-call(f32[1024,1024]{1,0:T(8,128)S(1)} %get-tuple-element.38.acc, bf16[1024,1536]{1,0:T(8,128)(2,1)S(1)} %get-tuple-element.39.xa_ref, bf16[1536,2048]{1,0:T(8,128)(2,1)S(1)} %get-tuple-element.40.wa_ref, ...), custom_call_target="tpu_custom_call" | custom-call | flops 2147483648 | bytes 8388608 | tf_op jit(solution)/shard_map/keys/pallas_call | solution.py:208
  17.9 0.6 collective-permute-done.4.refs_2_
  18.5 1.8 %scores.1 = (bf16[32,1024]{1,0:T(8,128)(2,1)S(1)}, bf16[32,1024]{1,0:T(8,128)(2,1)S(1)}, bf16[32,1024]{1,0:T(8,128)(2,1)S(1)}, bf16[32,1024]{1,0:T(8,128)(2,1)S(1)}) custom-call(bf16[2,144,128]{2,1,0:T(8,128)(2,1)S(1)} %turned.1.after.refs_0_, bf16[2,144,128]{2,1,0:T(8,128)(2,1)S(1)} %collective-permute-done.3.refs_1_, ...), custom_call_target="tpu_custom_call" | custom-call | flops 33554432 | bytes 6291456 | tf_op jit(solution)/shard_map/scores/pallas_call | solution.py:374
  20.3 3.8 %collective-permute-start.6 = (bf16[32,1024]{1,0:T(8,128)(2,1)S(1)}, bf16[32,1024]{1,0:T(8,128)(2,1)S(1)}, u32[]{:S(2)}, u32[]{:S(2)}) collective-permute-start(bf16[32,1024]{1,0:T(8,128)(2,1)S(1)} %get-tuple-element.46), channel_id=1, source_target_pairs={{0,3},{1,2},{2,1},{3,0},{4,7},{5,6},{6,5},{7,4},{8,11},{9,10},{10,... | collective-permute-start | bytes 196616 | tf_op jit(solution)/shard_map/ppermute | solution.py:32
  24.1 0.6 collective-permute-start.8
  24.8 2.3 %values.2 = (bf16[1024,512]{1,0:T(8,128)(2,1)S(1)}, bf16[1024,2048]{1,0:T(8,128)(2,1)S(1)}) custom-call(bf16[1024,1536]{1,0:T(8,128)(2,1)S(1)} %get-tuple-element.39.xa_ref, bf16[1536,2048]{1,0:T(8,128)(2,1)S(1)} %get-tuple-element.40.wa_ref, bf16[1024,512]{1,0:T(8,128)(2,1)S(1)} %get-tuple-element.49.xb_ref, ...), custom_call_target="tpu_custom_call" | custom-call | flops 1610612736 | bytes 8388608 | tf_op jit(solution)/shard_map/values/pallas_call | solution.py:250
  27.1 2.7 %collective-permute-done.7.refs_2_ = bf16[32,1024]{1,0:T(8,128)(2,1)S(1)} collective-permute-done((bf16[32,1024]{1,0:T(8,128)(2,1)S(1)}, bf16[32,1024]{1,0:T(8,128)(2,1)S(1)}, u32[]{:S(2)}, u32[]{:S(2)}) %collective-permute-start.7) | collective-permute-done | bytes 65568 | tf_op jit(solution)/shard_map/ppermute | solution.py:32
  29.8 0.9 %weights.1 = (bf16[32,1024]{1,0:T(8,128)(2,1)S(1)}, bf16[32,128]{1,0:T(8,128)(2,1)S(1)}) custom-call(bf16[32,1024]{1,0:T(8,128)(2,1)S(1)} %get-tuple-element.45.after.refs_0_, bf16[32,1024]{1,0:T(8,128)(2,1)S(1)} %collective-permute-done.6.refs_1_, bf16[32,1024]{1,0:T(8,128)(2,1)S(1)} %collective-permute-done.7.refs_2_, ...), custom_call_target="tpu_custom_call" | custom-call | tf_op jit(solution)/shard_map/weights/pallas_call | solution.py:485
  30.7 2.3 %collective-permute-start.11 = (bf16[32,1024]{1,0:T(8,128)(2,1)S(1)}, bf16[32,1024]{1,0:T(8,128)(2,1)S(1)}, u32[]{:S(2)}, u32[]{:S(2)}) collective-permute-start(bf16[32,1024]{1,0:T(8,128)(2,1)S(1)} %get-tuple-element.52.refs_0_), channel_id=1, source_target_pairs={{0,3},{1,2},{2,1},{3,0},{4,7},{5,6},{6,5},{7,4},{8,11},{9,10},{10,... | collective-permute-start | bytes 196616 | tf_op jit(solution)/shard_map/ppermute | solution.py:32
  33.4 1.7 %collective-permute-start.9 = (bf16[32,1024]{1,0:T(8,128)(2,1)S(1)}, bf16[32,1024]{1,0:T(8,128)(2,1)S(1)}, u32[]{:S(2)}, u32[]{:S(2)}) collective-permute-start(bf16[32,1024]{1,0:T(8,128)(2,1)S(1)} %get-tuple-element.52.refs_0_), channel_id=1, source_target_pairs={{0,1},{1,0},{2,3},{3,2},{4,5},{5,4},{6,7},{7,6},{8,9},{9,8},{10,11... | collective-permute-start | bytes 196616 | tf_op jit(solution)/shard_map/ppermute | solution.py:32
  35.1 2.3 %values.3 = (bf16[1024,512]{1,0:T(8,128)(2,1)S(1)}, bf16[1024,2048]{1,0:T(8,128)(2,1)S(1)}) custom-call(bf16[1024,1536]{1,0:T(8,128)(2,1)S(1)} %get-tuple-element.39.xa_ref, bf16[1536,2048]{1,0:T(8,128)(2,1)S(1)} %get-tuple-element.40.wa_ref, bf16[1024,512]{1,0:T(8,128)(2,1)S(1)} %get-tuple-element.49.xb_ref, ...), custom_call_target="tpu_custom_call" | custom-call | flops 1610612736 | bytes 8388608 | tf_op jit(solution)/shard_map/values/pallas_call | solution.py:250
  37.5 2.2 %collective-permute-done.10.refs_2_ = bf16[32,1024]{1,0:T(8,128)(2,1)S(1)} collective-permute-done((bf16[32,1024]{1,0:T(8,128)(2,1)S(1)}, bf16[32,1024]{1,0:T(8,128)(2,1)S(1)}, u32[]{:S(2)}, u32[]{:S(2)}) %collective-permute-start.10) | collective-permute-done | bytes 65568 | tf_op jit(solution)/shard_map/ppermute | solution.py:32
  39.7 1.3 %weighted.1 = (bf16[8,32,128]{2,1,0:T(8,128)(2,1)S(1)}, bf16[8,32,128]{2,1,0:T(8,128)(2,1)S(1)}, bf16[8,32,128]{2,1,0:T(8,128)(2,1)S(1)}, bf16[8,32,128]{2,1,0:T(8,128)(2,1)S(1)}) custom-call(bf16[32,1024]{1,0:T(8,128)(2,1)S(1)} %get-tuple-element.52.refs_0_, bf16[32,1024]{1,0:T(8,128)(2,1)S(1)} %collective-permute-done.9.refs_1_, ...), custom_call_target="tpu_custom_call" | custom-call | flops 33554432 | bytes 8388608 | tf_op jit(solution)/shard_map/weighted/pallas_call | solution.py:530
  41.0 2.0 %collective-permute-start.12 = (bf16[8,32,128]{2,1,0:T(8,128)(2,1)S(1)}, bf16[8,32,128]{2,1,0:T(8,128)(2,1)S(1)}, u32[]{:S(2)}, u32[]{:S(2)}) collective-permute-start(bf16[8,32,128]{2,1,0:T(8,128)(2,1)S(1)} %get-tuple-element.56), channel_id=1, source_target_pairs={{0,3},{1,2},{2,1},{3,0},{4,7},{5,6},{6,5},{7,4},{8,11},{9,10},{10,... | collective-permute-start | bytes 196616 | tf_op jit(solution)/shard_map/ppermute | solution.py:32
  43.0 2.5 %collective-permute-start.14 = (bf16[8,32,128]{2,1,0:T(8,128)(2,1)S(1)}, bf16[8,32,128]{2,1,0:T(8,128)(2,1)S(1)}, u32[]{:S(2)}, u32[]{:S(2)}) collective-permute-start(bf16[8,32,128]{2,1,0:T(8,128)(2,1)S(1)} %get-tuple-element.58), channel_id=1, source_target_pairs={{0,1},{1,0},{2,3},{3,2},{4,5},{5,4},{6,7},{7,6},{8,9},{9,8},{10,11... | collective-permute-start | bytes 196616 | tf_op jit(solution)/shard_map/ppermute | solution.py:32
  45.4 2.0 %collective-permute-done.12.refs_1_ = bf16[8,32,128]{2,1,0:T(8,128)(2,1)S(1)} collective-permute-done((bf16[8,32,128]{2,1,0:T(8,128)(2,1)S(1)}, bf16[8,32,128]{2,1,0:T(8,128)(2,1)S(1)}, u32[]{:S(2)}, u32[]{:S(2)}) %collective-permute-start.12) | collective-permute-done | bytes 65568 | tf_op jit(solution)/shard_map/ppermute | solution.py:32
  47.4 1.7 %collective-permute-done.13.refs_2_ = bf16[8,32,128]{2,1,0:T(8,128)(2,1)S(1)} collective-permute-done((bf16[8,32,128]{2,1,0:T(8,128)(2,1)S(1)}, bf16[8,32,128]{2,1,0:T(8,128)(2,1)S(1)}, u32[]{:S(2)}, u32[]{:S(2)}) %collective-permute-start.13) | collective-permute-done | bytes 65568 | tf_op jit(solution)/shard_map/ppermute | solution.py:32
  49.3 1.2 %collective-permute-start.16 = (bf16[9,32,128]{2,1,0:T(8,128)(2,1)S(1)}, bf16[9,32,128]{2,1,0:T(8,128)(2,1)S(1)}, u32[]{:S(2)}, u32[]{:S(2)}) collective-permute-start(bf16[9,32,128]{2,1,0:T(8,128)(2,1)S(1)} %summed.1.refs_0_), channel_id=1, source_target_pairs={{0,8},{4,12},{8,0},{12,4},{1,9},{5,13},{9,1},{13,5},{2,10},{6,14},... | collective-permute-start | bytes 221192 | tf_op jit(solution)/shard_map/ppermute | solution.py:32
  50.5 0.6 collective-permute-start.15
  51.2 2.6 %collective-permute-done.17.refs_3_ = bf16[9,32,128]{2,1,0:T(8,128)(2,1)S(1)} collective-permute-done((bf16[9,32,128]{2,1,0:T(8,128)(2,1)S(1)}, bf16[9,32,128]{2,1,0:T(8,128)(2,1)S(1)}, u32[]{:S(2)}, u32[]{:S(2)}) %collective-permute-start.17) | collective-permute-done | bytes 73760 | tf_op jit(solution)/shard_map/ppermute | solution.py:32
  53.8 1.3 %collective-permute-done.16.refs_2_ = bf16[9,32,128]{2,1,0:T(8,128)(2,1)S(1)} collective-permute-done((bf16[9,32,128]{2,1,0:T(8,128)(2,1)S(1)}, bf16[9,32,128]{2,1,0:T(8,128)(2,1)S(1)}, u32[]{:S(2)}, u32[]{:S(2)}) %collective-permute-start.16) | collective-permute-done | bytes 73760 | tf_op jit(solution)/shard_map/ppermute | solution.py:32
  55.1 1.6 %output.1.refs_0_ = bf16[16,2048]{1,0:T(8,128)(2,1)S(1)} custom-call(bf16[9,32,128]{2,1,0:T(8,128)(2,1)S(1)} %summed.1.refs_0_, bf16[9,32,128]{2,1,0:T(8,128)(2,1)S(1)} %collective-permute-done.15.refs_1_, bf16[9,32,128]{2,1,0:T(8,128)(2,1)S(1)} %collective-permute-done.16.refs_2_, bf16[9,32,128]{2,1,0:T(8,128)(2,1)S(1)} %collective-permute-done.17.refs_3_, ...), custom_call_target="tpu_custom_call" | custom-call | tf_op jit(solution)/shard_map/output/pallas_call | solution.py:624
  56.7 2.2 %collective-permute-start.20 = (bf16[16,2048]{1,0:T(8,128)(2,1)S(1)}, bf16[16,2048]{1,0:T(8,128)(2,1)S(1)}, u32[]{:S(2)}, u32[]{:S(2)}) collective-permute-start(bf16[16,2048]{1,0:T(8,128)(2,1)S(1)} %output.1.refs_0_), channel_id=1, source_target_pairs={{0,3},{1,2},{2,1},{3,0},{4,7},{5,6},{6,5},{7,4},{8,11},{9,10},{10,... | collective-permute-start | bytes 196616 | tf_op jit(solution)/shard_map/ppermute | solution.py:32
  58.9 2.1 %collective-permute-start.18 = (bf16[16,2048]{1,0:T(8,128)(2,1)S(1)}, bf16[16,2048]{1,0:T(8,128)(2,1)S(1)}, u32[]{:S(2)}, u32[]{:S(2)}) collective-permute-start(bf16[16,2048]{1,0:T(8,128)(2,1)S(1)} %output.1.refs_0_), channel_id=1, source_target_pairs={{0,1},{1,0},{2,3},{3,2},{4,5},{5,4},{6,7},{7,6},{8,9},{9,8},{10,11... | collective-permute-start | bytes 196616 | tf_op jit(solution)/shard_map/ppermute | solution.py:32
  61.0 2.3 %collective-permute-done.20.refs_3_ = bf16[16,2048]{1,0:T(8,128)(2,1)S(1)} collective-permute-done((bf16[16,2048]{1,0:T(8,128)(2,1)S(1)}, bf16[16,2048]{1,0:T(8,128)(2,1)S(1)}, u32[]{:S(2)}, u32[]{:S(2)}) %collective-permute-start.20) | collective-permute-done | bytes 65568 | tf_op jit(solution)/shard_map/ppermute | solution.py:32
  63.4 2.0 %collective-permute-done.19.refs_2_ = bf16[16,2048]{1,0:T(8,128)(2,1)S(1)} collective-permute-done((bf16[16,2048]{1,0:T(8,128)(2,1)S(1)}, bf16[16,2048]{1,0:T(8,128)(2,1)S(1)}, u32[]{:S(2)}, u32[]{:S(2)}) %collective-permute-start.19) | collective-permute-done | bytes 65568 | tf_op jit(solution)/shard_map/ppermute | solution.py:32
  65.4 0.7 %final.1 = f32[8,2,2048]{2,1,0:T(2,128)} custom-call(bf16[16,2048]{1,0:T(8,128)(2,1)S(1)} %output.1.refs_0_, bf16[16,2048]{1,0:T(8,128)(2,1)S(1)} %collective-permute-done.18.refs_1_, bf16[16,2048]{1,0:T(8,128)(2,1)S(1)} %collective-permute-done.19.refs_2_, bf16[16,2048]{1,0:T(8,128)(2,1)S(1)} %collective-permute-done.20.refs_3_, bf16[8,2,2048]{2,1,0:T(2,128)(2,1)S(1)} %copy-done), custom_call_target="tpu_custom_call" | custom-call | tf_op jit(solution)/shard_map/final/pallas_call | solution.py:648
  (25 shorter events, 1.5 us)
Async XLA Ops:
  0.7 11.4 %collective-permute-start.2 = (bf16[2,2,16,128]{3,2,1,0:T(8,128)(2,1)S(1)}, bf16[2,2,16,128]{3,2,1,0:T(8,128)(2,1)S(1)}, u32[]{:S(2)}, u32[]{:S(2)}) collective-permute-start(bf16[2,2,16,128]{3,2,1,0:T(8,128)(2,1)S(1)} %get-tuple-element.34.refs_0_), channel_id=1, source_target_pairs={{0,3},{1,2},{2,1},{3,0},{4,7},{5,6},{6,5},{7,4},{8,11},{9,10},{10,... | collective-permute-start | bytes 49160 | tf_op jit(solution)/shard_map/ppermute | solution.py:32
  5.9 6.3 %collective-permute-start.1 = (bf16[2,2,16,128]{3,2,1,0:T(8,128)(2,1)S(1)}, bf16[2,2,16,128]{3,2,1,0:T(8,128)(2,1)S(1)}, u32[]{:S(2)}, u32[]{:S(2)}) collective-permute-start(bf16[2,2,16,128]{3,2,1,0:T(8,128)(2,1)S(1)} %get-tuple-element.34.refs_0_), channel_id=1, source_target_pairs={{0,2},{1,3},{2,0},{3,1},{4,6},{5,7},{6,4},{7,5},{8,10},{9,11},{10,... | collective-permute-start | bytes 49160 | tf_op jit(solution)/shard_map/ppermute | solution.py:32
  5.9 6.4 %collective-permute-start = (bf16[2,2,16,128]{3,2,1,0:T(8,128)(2,1)S(1)}, bf16[2,2,16,128]{3,2,1,0:T(8,128)(2,1)S(1)}, u32[]{:S(2)}, u32[]{:S(2)}) collective-permute-start(bf16[2,2,16,128]{3,2,1,0:T(8,128)(2,1)S(1)} %get-tuple-element.34.refs_0_), channel_id=1, source_target_pairs={{0,1},{1,0},{2,3},{3,2},{4,5},{5,4},{6,7},{7,6},{8,9},{9,8},{10,11... | collective-permute-start | bytes 49160 | tf_op jit(solution)/shard_map/ppermute | solution.py:32
  12.3 5.6 %collective-permute-start.5 = (bf16[2,144,128]{2,1,0:T(8,128)(2,1)S(1)}, bf16[2,144,128]{2,1,0:T(8,128)(2,1)S(1)}, u32[]{:S(2)}, u32[]{:S(2)}) collective-permute-start(bf16[2,144,128]{2,1,0:T(8,128)(2,1)S(1)} %turned.1.after.refs_0_), channel_id=1, source_target_pairs={{0,12},{4,8},{8,4},{12,0},{1,13},{5,9},{9,5},{13,1},{2,14},{6,10},... | collective-permute-start | bytes 221192 | tf_op jit(solution)/shard_map/ppermute | solution.py:32
  12.8 5.7 %collective-permute-start.4 = (bf16[2,144,128]{2,1,0:T(8,128)(2,1)S(1)}, bf16[2,144,128]{2,1,0:T(8,128)(2,1)S(1)}, u32[]{:S(2)}, u32[]{:S(2)}) collective-permute-start(bf16[2,144,128]{2,1,0:T(8,128)(2,1)S(1)} %turned.1.after.refs_0_), channel_id=1, source_target_pairs={{0,8},{4,12},{8,0},{12,4},{1,9},{5,13},{9,1},{13,5},{2,10},{6,14},... | collective-permute-start | bytes 221192 | tf_op jit(solution)/shard_map/ppermute | solution.py:32
  14.1 4.4 %collective-permute-start.3 = (bf16[2,144,128]{2,1,0:T(8,128)(2,1)S(1)}, bf16[2,144,128]{2,1,0:T(8,128)(2,1)S(1)}, u32[]{:S(2)}, u32[]{:S(2)}) collective-permute-start(bf16[2,144,128]{2,1,0:T(8,128)(2,1)S(1)} %turned.1.after.refs_0_), channel_id=1, source_target_pairs={{0,4},{4,0},{8,12},{12,8},{1,5},{5,1},{9,13},{13,9},{2,6},{6,2},{1... | collective-permute-start | bytes 221192 | tf_op jit(solution)/shard_map/ppermute | solution.py:32
  20.3 6.8 %collective-permute-start.6 = (bf16[32,1024]{1,0:T(8,128)(2,1)S(1)}, bf16[32,1024]{1,0:T(8,128)(2,1)S(1)}, u32[]{:S(2)}, u32[]{:S(2)}) collective-permute-start(bf16[32,1024]{1,0:T(8,128)(2,1)S(1)} %get-tuple-element.46), channel_id=1, source_target_pairs={{0,3},{1,2},{2,1},{3,0},{4,7},{5,6},{6,5},{7,4},{8,11},{9,10},{10,... | collective-permute-start | bytes 196616 | tf_op jit(solution)/shard_map/ppermute | solution.py:32
  24.1 5.7 %collective-permute-start.7 = (bf16[32,1024]{1,0:T(8,128)(2,1)S(1)}, bf16[32,1024]{1,0:T(8,128)(2,1)S(1)}, u32[]{:S(2)}, u32[]{:S(2)}) collective-permute-start(bf16[32,1024]{1,0:T(8,128)(2,1)S(1)} %get-tuple-element.47), channel_id=1, source_target_pairs={{0,2},{1,3},{2,0},{3,1},{4,6},{5,7},{6,4},{7,5},{8,10},{9,11},{10,... | collective-permute-start | bytes 196616 | tf_op jit(solution)/shard_map/ppermute | solution.py:32
  24.1 5.7 %collective-permute-start.8 = (bf16[32,1024]{1,0:T(8,128)(2,1)S(1)}, bf16[32,1024]{1,0:T(8,128)(2,1)S(1)}, u32[]{:S(2)}, u32[]{:S(2)}) collective-permute-start(bf16[32,1024]{1,0:T(8,128)(2,1)S(1)} %get-tuple-element.48), channel_id=1, source_target_pairs={{0,1},{1,0},{2,3},{3,2},{4,5},{5,4},{6,7},{7,6},{8,9},{9,8},{10,11... | collective-permute-start | bytes 196616 | tf_op jit(solution)/shard_map/ppermute | solution.py:32
  30.7 6.7 %collective-permute-start.11 = (bf16[32,1024]{1,0:T(8,128)(2,1)S(1)}, bf16[32,1024]{1,0:T(8,128)(2,1)S(1)}, u32[]{:S(2)}, u32[]{:S(2)}) collective-permute-start(bf16[32,1024]{1,0:T(8,128)(2,1)S(1)} %get-tuple-element.52.refs_0_), channel_id=1, source_target_pairs={{0,3},{1,2},{2,1},{3,0},{4,7},{5,6},{6,5},{7,4},{8,11},{9,10},{10,... | collective-permute-start | bytes 196616 | tf_op jit(solution)/shard_map/ppermute | solution.py:32
  33.0 6.7 %collective-permute-start.10 = (bf16[32,1024]{1,0:T(8,128)(2,1)S(1)}, bf16[32,1024]{1,0:T(8,128)(2,1)S(1)}, u32[]{:S(2)}, u32[]{:S(2)}) collective-permute-start(bf16[32,1024]{1,0:T(8,128)(2,1)S(1)} %get-tuple-element.52.refs_0_), channel_id=1, source_target_pairs={{0,2},{1,3},{2,0},{3,1},{4,6},{5,7},{6,4},{7,5},{8,10},{9,11},{10,... | collective-permute-start | bytes 196616 | tf_op jit(solution)/shard_map/ppermute | solution.py:32
  33.4 6.3 %collective-permute-start.9 = (bf16[32,1024]{1,0:T(8,128)(2,1)S(1)}, bf16[32,1024]{1,0:T(8,128)(2,1)S(1)}, u32[]{:S(2)}, u32[]{:S(2)}) collective-permute-start(bf16[32,1024]{1,0:T(8,128)(2,1)S(1)} %get-tuple-element.52.refs_0_), channel_id=1, source_target_pairs={{0,1},{1,0},{2,3},{3,2},{4,5},{5,4},{6,7},{7,6},{8,9},{9,8},{10,11... | collective-permute-start | bytes 196616 | tf_op jit(solution)/shard_map/ppermute | solution.py:32
  41.0 6.4 %collective-permute-start.12 = (bf16[8,32,128]{2,1,0:T(8,128)(2,1)S(1)}, bf16[8,32,128]{2,1,0:T(8,128)(2,1)S(1)}, u32[]{:S(2)}, u32[]{:S(2)}) collective-permute-start(bf16[8,32,128]{2,1,0:T(8,128)(2,1)S(1)} %get-tuple-element.56), channel_id=1, source_target_pairs={{0,3},{1,2},{2,1},{3,0},{4,7},{5,6},{6,5},{7,4},{8,11},{9,10},{10,... | collective-permute-start | bytes 196616 | tf_op jit(solution)/shard_map/ppermute | solution.py:32
  43.0 6.2 %collective-permute-start.13 = (bf16[8,32,128]{2,1,0:T(8,128)(2,1)S(1)}, bf16[8,32,128]{2,1,0:T(8,128)(2,1)S(1)}, u32[]{:S(2)}, u32[]{:S(2)}) collective-permute-start(bf16[8,32,128]{2,1,0:T(8,128)(2,1)S(1)} %get-tuple-element.57), channel_id=1, source_target_pairs={{0,2},{1,3},{2,0},{3,1},{4,6},{5,7},{6,4},{7,5},{8,10},{9,11},{10,... | collective-permute-start | bytes 196616 | tf_op jit(solution)/shard_map/ppermute | solution.py:32
  43.0 6.2 %collective-permute-start.14 = (bf16[8,32,128]{2,1,0:T(8,128)(2,1)S(1)}, bf16[8,32,128]{2,1,0:T(8,128)(2,1)S(1)}, u32[]{:S(2)}, u32[]{:S(2)}) collective-permute-start(bf16[8,32,128]{2,1,0:T(8,128)(2,1)S(1)} %get-tuple-element.58), channel_id=1, source_target_pairs={{0,1},{1,0},{2,3},{3,2},{4,5},{5,4},{6,7},{7,6},{8,9},{9,8},{10,11... | collective-permute-start | bytes 196616 | tf_op jit(solution)/shard_map/ppermute | solution.py:32
  49.2 4.6 %collective-permute-start.17 = (bf16[9,32,128]{2,1,0:T(8,128)(2,1)S(1)}, bf16[9,32,128]{2,1,0:T(8,128)(2,1)S(1)}, u32[]{:S(2)}, u32[]{:S(2)}) collective-permute-start(bf16[9,32,128]{2,1,0:T(8,128)(2,1)S(1)} %summed.1.refs_0_), channel_id=1, source_target_pairs={{0,12},{4,8},{8,4},{12,0},{1,13},{5,9},{9,5},{13,1},{2,14},{6,10},... | collective-permute-start | bytes 221192 | tf_op jit(solution)/shard_map/ppermute | solution.py:32
  49.3 5.7 %collective-permute-start.16 = (bf16[9,32,128]{2,1,0:T(8,128)(2,1)S(1)}, bf16[9,32,128]{2,1,0:T(8,128)(2,1)S(1)}, u32[]{:S(2)}, u32[]{:S(2)}) collective-permute-start(bf16[9,32,128]{2,1,0:T(8,128)(2,1)S(1)} %summed.1.refs_0_), channel_id=1, source_target_pairs={{0,8},{4,12},{8,0},{12,4},{1,9},{5,13},{9,1},{13,5},{2,10},{6,14},... | collective-permute-start | bytes 221192 | tf_op jit(solution)/shard_map/ppermute | solution.py:32
  50.5 4.5 %collective-permute-start.15 = (bf16[9,32,128]{2,1,0:T(8,128)(2,1)S(1)}, bf16[9,32,128]{2,1,0:T(8,128)(2,1)S(1)}, u32[]{:S(2)}, u32[]{:S(2)}) collective-permute-start(bf16[9,32,128]{2,1,0:T(8,128)(2,1)S(1)} %summed.1.refs_0_), channel_id=1, source_target_pairs={{0,4},{4,0},{8,12},{12,8},{1,5},{5,1},{9,13},{13,9},{2,6},{6,2},{1... | collective-permute-start | bytes 221192 | tf_op jit(solution)/shard_map/ppermute | solution.py:32
  55.1 10.3 %copy-start = (bf16[8,2,2048]{2,1,0:T(2,128)(2,1)S(1)}, bf16[8,2,2048]{2,1,0:T(2,128)(2,1)}, u32[]{:S(2)}) copy-start(bf16[8,2,2048]{2,1,0:T(2,128)(2,1)} %refs_4_.1) | copy-start | bytes 196612
  56.7 6.7 %collective-permute-start.20 = (bf16[16,2048]{1,0:T(8,128)(2,1)S(1)}, bf16[16,2048]{1,0:T(8,128)(2,1)S(1)}, u32[]{:S(2)}, u32[]{:S(2)}) collective-permute-start(bf16[16,2048]{1,0:T(8,128)(2,1)S(1)} %output.1.refs_0_), channel_id=1, source_target_pairs={{0,3},{1,2},{2,1},{3,0},{4,7},{5,6},{6,5},{7,4},{8,11},{9,10},{10,... | collective-permute-start | bytes 196616 | tf_op jit(solution)/shard_map/ppermute | solution.py:32
  58.9 6.5 %collective-permute-start.19 = (bf16[16,2048]{1,0:T(8,128)(2,1)S(1)}, bf16[16,2048]{1,0:T(8,128)(2,1)S(1)}, u32[]{:S(2)}, u32[]{:S(2)}) collective-permute-start(bf16[16,2048]{1,0:T(8,128)(2,1)S(1)} %output.1.refs_0_), channel_id=1, source_target_pairs={{0,2},{1,3},{2,0},{3,1},{4,6},{5,7},{6,4},{7,5},{8,10},{9,11},{10,... | collective-permute-start | bytes 196616 | tf_op jit(solution)/shard_map/ppermute | solution.py:32
  58.9 6.5 %collective-permute-start.18 = (bf16[16,2048]{1,0:T(8,128)(2,1)S(1)}, bf16[16,2048]{1,0:T(8,128)(2,1)S(1)}, u32[]{:S(2)}, u32[]{:S(2)}) collective-permute-start(bf16[16,2048]{1,0:T(8,128)(2,1)S(1)} %output.1.refs_0_), channel_id=1, source_target_pairs={{0,1},{1,0},{2,3},{3,2},{4,5},{5,4},{6,7},{7,6},{8,9},{9,8},{10,11... | collective-permute-start | bytes 196616 | tf_op jit(solution)/shard_map/ppermute | solution.py:32

commit v11 on v10

--- a/solution.py
+++ b/solution.py
@@ -23,22 +23,28 @@
 ANY = pl.BlockSpec(memory_space=pl.ANY)
 
 
+def pairs(value, axis, d):
+    return lax.ppermute(value, axis, [(i, i ^ d) for i in range(lax.axis_size(axis))])
+
+
 def partner(me, entry, size):
     return me ^ ((size - entry) % size)
 
 
-def pairs(value, axis, entry):
-    size = lax.axis_size(axis)
-    return lax.ppermute(value, axis, [(i, partner(i, entry, size)) for i in range(size)])
-
-
 def exchange(chunks, axis):
-    return [chunks[0]] + [pairs(chunks[i], axis, i) for i in range(1, len(chunks))]
+    size = len(chunks)
+    return [chunks[0]] + [pairs(chunks[i], axis, size - i) for i in range(1, size)]
 
 
 def gather(value, axis):
-    size = lax.axis_size(axis)
-    return [value] + [pairs(value, axis, size - d) for d in range(1, size)]
+    return [value] + [pairs(value, axis, d) for d in range(1, lax.axis_size(axis))]
+
+
+def gather_by_chips(value, axis):
+    got = [value]
+    for d in range(1, lax.axis_size(axis)):
+        got.append(pairs(got[d - 1], axis, 1) if d % 2 else pairs(value, axis, d))
+    return got
 
 
 def lane_freqs(rows):
@@ -142,10 +148,9 @@
     angles = by_row(len(spots), spots) * lane_freqs(len(spots))
     cos_q[...] = jnp.cos(angles)
     sin_q[...] = jnp.sin(angles) * sine_sign(len(spots))
-    for i in range(2):
-        for copy in copies[i]:
-            copy.wait()
-        add_block(x_ref, w_ref, slice(i * size, (i + 1) * size), acc, acc, i == 0)
+    for copy in copies[0] + copies[1]:
+        copy.wait()
+    add_block(x_ref, w_ref, slice(0, 2 * size), acc, acc, True)
     for copy in copies[2]:
         copy.wait()
 
@@ -676,7 +681,7 @@
     vb, ob = project_values((xa, wa, xb, wb), out_weight, 1, stats)
     fresh, values = fresh_scores(new, stats, prompts, new_count, n_tp)
     chunks = weighted_values(gather(weights, "tp"), va, vb, meta, prompts)
-    pieces = gather(summed(exchange(chunks, "tp"), stats), "seq")
+    pieces = gather_by_chips(summed(exchange(chunks, "tp"), stats), "seq")
     partial = output_partial(pieces, fresh, values, (oa, ob))
     return final_sum(gather(partial, "tp"), residual)
 

time: 66.4 us -> 67.1 us (1.011)
  Pallas kernels: 21.2 us -> 22.1 us
  starting transfers between devices: 27.3 us -> 26.4 us
  waiting for transfers between devices: 17.4 us -> 18.2 us
    ppermute x21, starting transfers between devices: 27.3 us -> 26.4 us  [pairs(): lax.ppermute(value, axis, [(i, i ^ d) for i in range(lax.axis_size(axis))])]
    pallas_call x1, Pallas kernels: 5.68 us -> 6.54 us  [load(): pl.pallas_call(functools.partial(load_kernel, pages, prompts, new_count),...]
    ppermute x21, waiting for transfers between devices: 17.4 us -> 18.2 us  [pairs(): lax.ppermute(value, axis, [(i, i ^ d) for i in range(lax.axis_size(axis))])]
  transfers between devices with their start and end apart: 21 -> 21, of which waited for: 9 -> 9; matrix products, arithmetic and copies ran while one was open for 0% -> 0% of each run, Pallas kernels for 21% -> 22%
where the time goes in v11:
time: 67.1 us; the launch traced here: 66.8 us
  starting transfers between devices  26.4 us (39%)
  Pallas kernels  22.1 us (33%)
  waiting for transfers between devices  18.2 us (27%)
    ppermute x21, starting transfers between devices, pairs(): lax.ppermute(value, axis, [(i, i ^ d) for i in range(lax.axis_size(axis))])  26.4 us
    ppermute x21, waiting for transfers between devices, pairs(): lax.ppermute(value, axis, [(i, i ^ d) for i in range(lax.axis_size(axis))])  18.2 us
    pallas_call x1, Pallas kernels, load(): pl.pallas_call(functools.partial(load_kernel, pages, prompts, new_count),...  6.54 us
    pallas_call x2, Pallas kernels, project_values(): pl.pallas_call(functools.partial(values_kernel, first), in_specs=[VMEM] *...  4.68 us
    pallas_call x1, Pallas kernels, rotated_keys(): pl.pallas_call(keys_kernel, in_specs=[VMEM] * 3 + [hbm] * 2 + [VMEM] * 2...  3.61 us
    pallas_call x1, Pallas kernels, partial_scores(): pl.pallas_call(functools.partial(scores_kernel, n_seq, n_tp), in_specs=[V...  1.76 us
    pallas_call x1, Pallas kernels, output_partial(): pl.pallas_call(functools.partial(output_kernel, n_seq), in_specs=[VMEM] *...  1.58 us
  transfers between devices with their start and end apart: 21, of which 9 were waited for; matrix products, arithmetic and copies ran while one was open for 0% of the time, Pallas kernels for 22%

profile of v11, /device:TPU:0, one launch (start us, length us, event | category | flops | bytes accessed | tf_op | source)
XLA Modules:
  0.0 66.8 jit_solution(11569897838996713270)
XLA Ops:
  0.0 0.7 %prepare.1 = (bf16[2,2,16,128]{3,2,1,0:T(8,128)(2,1)S(1)}, f32[2,2,4,128]{3,2,1,0:T(4,128)S(1)}) custom-call(bf16[2,2,2048]{2,1,0:T(2,128)(2,1)} %q_ref.1, bf16[2,2,512]{2,1,0:T(2,128)(2,1)} %kv_ref.1), custom_call_target="tpu_custom_call" | custom-call | bytes 1048576 | tf_op jit(solution)/shard_map/prepare/pallas_call | solution.py:287
  0.7 5.1 %collective-permute-start.2 = (bf16[2,2,16,128]{3,2,1,0:T(8,128)(2,1)S(1)}, bf16[2,2,16,128]{3,2,1,0:T(8,128)(2,1)S(1)}, u32[]{:S(2)}, u32[]{:S(2)}) collective-permute-start(bf16[2,2,16,128]{3,2,1,0:T(8,128)(2,1)S(1)} %get-tuple-element.34.refs_0_), channel_id=1, source_target_pairs={{0,3},{1,2},{2,1},{3,0},{4,7},{5,6},{6,5},{7,4},{8,11},{9,10},{10,... | collective-permute-start | bytes 49160 | tf_op jit(solution)/shard_map/ppermute | solution.py:27
  5.9 0.6 collective-permute-start
  6.5 6.5 %load.1 = (f32[1024,1024]{1,0:T(8,128)S(1)}, bf16[1024,1536]{1,0:T(8,128)(2,1)S(1)}, bf16[1536,2048]{1,0:T(8,128)(2,1)S(1)}, f32[1024,128]{1,0:T(8,128)S(1)}, f3...) custom-call(bf16[1024,2048]{1,0:T(8,128)(2,1)} %x_hbm.3, ...), custom_call_target="tpu_custom_call" | custom-call | flops 2147483648 | bytes 9437184 | tf_op jit(solution)/shard_map/load/pallas_call | solution.py:164
  13.2 0.5 collective-permute-start.5
  13.7 1.3 %collective-permute-start.4 = (bf16[2,144,128]{2,1,0:T(8,128)(2,1)S(1)}, bf16[2,144,128]{2,1,0:T(8,128)(2,1)S(1)}, u32[]{:S(2)}, u32[]{:S(2)}) collective-permute-start(bf16[2,144,128]{2,1,0:T(8,128)(2,1)S(1)} %turned.1.after.refs_0_), channel_id=1, source_target_pairs={{0,8},{4,12},{8,0},{12,4},{1,9},{5,13},{9,1},{13,5},{2,10},{6,14},... | collective-permute-start | bytes 221192 | tf_op jit(solution)/shard_map/ppermute | solution.py:27
  15.1 3.6 %keys.1 = (bf16[1024,1024]{1,0:T(8,128)(2,1)S(1)}, bf16[1024,512]{1,0:T(8,128)(2,1)S(1)}, bf16[512,2048]{1,0:T(8,128)(2,1)S(1)}) custom-call(f32[1024,1024]{1,0:T(8,128)S(1)} %get-tuple-element.38.acc, bf16[1024,1536]{1,0:T(8,128)(2,1)S(1)} %get-tuple-element.39.xa_ref, bf16[1536,2048]{1,0:T(8,128)(2,1)S(1)} %get-tuple-element.40.wa_ref, ...), custom_call_target="tpu_custom_call" | custom-call | flops 2147483648 | bytes 8388608 | tf_op jit(solution)/shard_map/keys/pallas_call | solution.py:213
  18.8 0.6 collective-permute-done.4.refs_2_
  19.4 1.8 %scores.1 = (bf16[32,1024]{1,0:T(8,128)(2,1)S(1)}, bf16[32,1024]{1,0:T(8,128)(2,1)S(1)}, bf16[32,1024]{1,0:T(8,128)(2,1)S(1)}, bf16[32,1024]{1,0:T(8,128)(2,1)S(1)}) custom-call(bf16[2,144,128]{2,1,0:T(8,128)(2,1)S(1)} %turned.1.after.refs_0_, bf16[2,144,128]{2,1,0:T(8,128)(2,1)S(1)} %collective-permute-done.3.refs_1_, ...), custom_call_target="tpu_custom_call" | custom-call | flops 33554432 | bytes 6291456 | tf_op jit(solution)/shard_map/scores/pallas_call | solution.py:379
  21.2 3.8 %collective-permute-start.6 = (bf16[32,1024]{1,0:T(8,128)(2,1)S(1)}, bf16[32,1024]{1,0:T(8,128)(2,1)S(1)}, u32[]{:S(2)}, u32[]{:S(2)}) collective-permute-start(bf16[32,1024]{1,0:T(8,128)(2,1)S(1)} %get-tuple-element.46), channel_id=1, source_target_pairs={{0,3},{1,2},{2,1},{3,0},{4,7},{5,6},{6,5},{7,4},{8,11},{9,10},{10,... | collective-permute-start | bytes 196616 | tf_op jit(solution)/shard_map/ppermute | solution.py:27
  25.0 0.6 collective-permute-start.8
  25.6 2.3 %values.2 = (bf16[1024,512]{1,0:T(8,128)(2,1)S(1)}, bf16[1024,2048]{1,0:T(8,128)(2,1)S(1)}) custom-call(bf16[1024,1536]{1,0:T(8,128)(2,1)S(1)} %get-tuple-element.39.xa_ref, bf16[1536,2048]{1,0:T(8,128)(2,1)S(1)} %get-tuple-element.40.wa_ref, bf16[1024,512]{1,0:T(8,128)(2,1)S(1)} %get-tuple-element.49.xb_ref, ...), custom_call_target="tpu_custom_call" | custom-call | flops 1610612736 | bytes 8388608 | tf_op jit(solution)/shard_map/values/pallas_call | solution.py:255
  28.0 2.7 %collective-permute-done.7.refs_2_ = bf16[32,1024]{1,0:T(8,128)(2,1)S(1)} collective-permute-done((bf16[32,1024]{1,0:T(8,128)(2,1)S(1)}, bf16[32,1024]{1,0:T(8,128)(2,1)S(1)}, u32[]{:S(2)}, u32[]{:S(2)}) %collective-permute-start.7) | collective-permute-done | bytes 65568 | tf_op jit(solution)/shard_map/ppermute | solution.py:27
  30.7 0.9 %weights.1 = (bf16[32,1024]{1,0:T(8,128)(2,1)S(1)}, bf16[32,128]{1,0:T(8,128)(2,1)S(1)}) custom-call(bf16[32,1024]{1,0:T(8,128)(2,1)S(1)} %get-tuple-element.45.after.refs_0_, bf16[32,1024]{1,0:T(8,128)(2,1)S(1)} %collective-permute-done.6.refs_1_, bf16[32,1024]{1,0:T(8,128)(2,1)S(1)} %collective-permute-done.7.refs_2_, ...), custom_call_target="tpu_custom_call" | custom-call | tf_op jit(solution)/shard_map/weights/pallas_call | solution.py:490
  31.6 2.3 %collective-permute-start.11 = (bf16[32,1024]{1,0:T(8,128)(2,1)S(1)}, bf16[32,1024]{1,0:T(8,128)(2,1)S(1)}, u32[]{:S(2)}, u32[]{:S(2)}) collective-permute-start(bf16[32,1024]{1,0:T(8,128)(2,1)S(1)} %get-tuple-element.52.refs_0_), channel_id=1, source_target_pairs={{0,3},{1,2},{2,1},{3,0},{4,7},{5,6},{6,5},{7,4},{8,11},{9,10},{10,... | collective-permute-start | bytes 196616 | tf_op jit(solution)/shard_map/ppermute | solution.py:27
  34.2 1.7 %collective-permute-start.9 = (bf16[32,1024]{1,0:T(8,128)(2,1)S(1)}, bf16[32,1024]{1,0:T(8,128)(2,1)S(1)}, u32[]{:S(2)}, u32[]{:S(2)}) collective-permute-start(bf16[32,1024]{1,0:T(8,128)(2,1)S(1)} %get-tuple-element.52.refs_0_), channel_id=1, source_target_pairs={{0,1},{1,0},{2,3},{3,2},{4,5},{5,4},{6,7},{7,6},{8,9},{9,8},{10,11... | collective-permute-start | bytes 196616 | tf_op jit(solution)/shard_map/ppermute | solution.py:27
  36.0 2.3 %values.3 = (bf16[1024,512]{1,0:T(8,128)(2,1)S(1)}, bf16[1024,2048]{1,0:T(8,128)(2,1)S(1)}) custom-call(bf16[1024,1536]{1,0:T(8,128)(2,1)S(1)} %get-tuple-element.39.xa_ref, bf16[1536,2048]{1,0:T(8,128)(2,1)S(1)} %get-tuple-element.40.wa_ref, bf16[1024,512]{1,0:T(8,128)(2,1)S(1)} %get-tuple-element.49.xb_ref, ...), custom_call_target="tpu_custom_call" | custom-call | flops 1610612736 | bytes 8388608 | tf_op jit(solution)/shard_map/values/pallas_call | solution.py:255
  38.3 2.2 %collective-permute-done.10.refs_2_ = bf16[32,1024]{1,0:T(8,128)(2,1)S(1)} collective-permute-done((bf16[32,1024]{1,0:T(8,128)(2,1)S(1)}, bf16[32,1024]{1,0:T(8,128)(2,1)S(1)}, u32[]{:S(2)}, u32[]{:S(2)}) %collective-permute-start.10) | collective-permute-done | bytes 65568 | tf_op jit(solution)/shard_map/ppermute | solution.py:27
  40.6 1.3 %weighted.1 = (bf16[8,32,128]{2,1,0:T(8,128)(2,1)S(1)}, bf16[8,32,128]{2,1,0:T(8,128)(2,1)S(1)}, bf16[8,32,128]{2,1,0:T(8,128)(2,1)S(1)}, bf16[8,32,128]{2,1,0:T(8,128)(2,1)S(1)}) custom-call(bf16[32,1024]{1,0:T(8,128)(2,1)S(1)} %get-tuple-element.52.refs_0_, bf16[32,1024]{1,0:T(8,128)(2,1)S(1)} %collective-permute-done.9.refs_1_, ...), custom_call_target="tpu_custom_call" | custom-call | flops 33554432 | bytes 8388608 | tf_op jit(solution)/shard_map/weighted/pallas_call | solution.py:535
  41.8 2.0 %collective-permute-start.12 = (bf16[8,32,128]{2,1,0:T(8,128)(2,1)S(1)}, bf16[8,32,128]{2,1,0:T(8,128)(2,1)S(1)}, u32[]{:S(2)}, u32[]{:S(2)}) collective-permute-start(bf16[8,32,128]{2,1,0:T(8,128)(2,1)S(1)} %get-tuple-element.56), channel_id=1, source_target_pairs={{0,3},{1,2},{2,1},{3,0},{4,7},{5,6},{6,5},{7,4},{8,11},{9,10},{10,... | collective-permute-start | bytes 196616 | tf_op jit(solution)/shard_map/ppermute | solution.py:27
  43.8 2.5 %collective-permute-start.14 = (bf16[8,32,128]{2,1,0:T(8,128)(2,1)S(1)}, bf16[8,32,128]{2,1,0:T(8,128)(2,1)S(1)}, u32[]{:S(2)}, u32[]{:S(2)}) collective-permute-start(bf16[8,32,128]{2,1,0:T(8,128)(2,1)S(1)} %get-tuple-element.58), channel_id=1, source_target_pairs={{0,1},{1,0},{2,3},{3,2},{4,5},{5,4},{6,7},{7,6},{8,9},{9,8},{10,11... | collective-permute-start | bytes 196616 | tf_op jit(solution)/shard_map/ppermute | solution.py:27
  46.3 2.0 %collective-permute-done.12.refs_1_ = bf16[8,32,128]{2,1,0:T(8,128)(2,1)S(1)} collective-permute-done((bf16[8,32,128]{2,1,0:T(8,128)(2,1)S(1)}, bf16[8,32,128]{2,1,0:T(8,128)(2,1)S(1)}, u32[]{:S(2)}, u32[]{:S(2)}) %collective-permute-start.12) | collective-permute-done | bytes 65568 | tf_op jit(solution)/shard_map/ppermute | solution.py:27
  48.3 1.7 %collective-permute-done.13.refs_2_ = bf16[8,32,128]{2,1,0:T(8,128)(2,1)S(1)} collective-permute-done((bf16[8,32,128]{2,1,0:T(8,128)(2,1)S(1)}, bf16[8,32,128]{2,1,0:T(8,128)(2,1)S(1)}, u32[]{:S(2)}, u32[]{:S(2)}) %collective-permute-start.13) | collective-permute-done | bytes 65568 | tf_op jit(solution)/shard_map/ppermute | solution.py:27
  50.0 0.9 %collective-permute-start.16 = (bf16[9,32,128]{2,1,0:T(8,128)(2,1)S(1)}, bf16[9,32,128]{2,1,0:T(8,128)(2,1)S(1)}, u32[]{:S(2)}, u32[]{:S(2)}) collective-permute-start(bf16[9,32,128]{2,1,0:T(8,128)(2,1)S(1)} %summed.1.refs_0_), channel_id=1, source_target_pairs={{0,8},{4,12},{8,0},{12,4},{1,9},{5,13},{9,1},{13,5},{2,10},{6,14},... | collective-permute-start | bytes 221192 | tf_op jit(solution)/shard_map/ppermute | solution.py:27
  51.0 3.5 %collective-permute-done.16.refs_2_ = bf16[9,32,128]{2,1,0:T(8,128)(2,1)S(1)} collective-permute-done((bf16[9,32,128]{2,1,0:T(8,128)(2,1)S(1)}, bf16[9,32,128]{2,1,0:T(8,128)(2,1)S(1)}, u32[]{:S(2)}, u32[]{:S(2)}) %collective-permute-start.16) | collective-permute-done | bytes 73760 | tf_op jit(solution)/shard_map/ppermute | solution.py:27
  54.6 1.1 %collective-permute-done.17.refs_3_ = bf16[9,32,128]{2,1,0:T(8,128)(2,1)S(1)} collective-permute-done((bf16[9,32,128]{2,1,0:T(8,128)(2,1)S(1)}, bf16[9,32,128]{2,1,0:T(8,128)(2,1)S(1)}, u32[]{:S(2)}, u32[]{:S(2)}) %collective-permute-start.17) | collective-permute-done | bytes 73760 | tf_op jit(solution)/shard_map/ppermute | solution.py:27
  55.7 1.6 %output.1.refs_0_ = bf16[16,2048]{1,0:T(8,128)(2,1)S(1)} custom-call(bf16[9,32,128]{2,1,0:T(8,128)(2,1)S(1)} %summed.1.refs_0_, bf16[9,32,128]{2,1,0:T(8,128)(2,1)S(1)} %collective-permute-done.15.refs_1_, bf16[9,32,128]{2,1,0:T(8,128)(2,1)S(1)} %collective-permute-done.16.refs_2_, bf16[9,32,128]{2,1,0:T(8,128)(2,1)S(1)} %collective-permute-done.17.refs_3_, ...), custom_call_target="tpu_custom_call" | custom-call | tf_op jit(solution)/shard_map/output/pallas_call | solution.py:629
  57.3 2.0 %collective-permute-start.20 = (bf16[16,2048]{1,0:T(8,128)(2,1)S(1)}, bf16[16,2048]{1,0:T(8,128)(2,1)S(1)}, u32[]{:S(2)}, u32[]{:S(2)}) collective-permute-start(bf16[16,2048]{1,0:T(8,128)(2,1)S(1)} %output.1.refs_0_), channel_id=1, source_target_pairs={{0,3},{1,2},{2,1},{3,0},{4,7},{5,6},{6,5},{7,4},{8,11},{9,10},{10,... | collective-permute-start | bytes 196616 | tf_op jit(solution)/shard_map/ppermute | solution.py:27
  59.3 2.3 %collective-permute-start.18 = (bf16[16,2048]{1,0:T(8,128)(2,1)S(1)}, bf16[16,2048]{1,0:T(8,128)(2,1)S(1)}, u32[]{:S(2)}, u32[]{:S(2)}) collective-permute-start(bf16[16,2048]{1,0:T(8,128)(2,1)S(1)} %output.1.refs_0_), channel_id=1, source_target_pairs={{0,1},{1,0},{2,3},{3,2},{4,5},{5,4},{6,7},{7,6},{8,9},{9,8},{10,11... | collective-permute-start | bytes 196616 | tf_op jit(solution)/shard_map/ppermute | solution.py:27
  61.7 2.4 %collective-permute-done.20.refs_3_ = bf16[16,2048]{1,0:T(8,128)(2,1)S(1)} collective-permute-done((bf16[16,2048]{1,0:T(8,128)(2,1)S(1)}, bf16[16,2048]{1,0:T(8,128)(2,1)S(1)}, u32[]{:S(2)}, u32[]{:S(2)}) %collective-permute-start.20) | collective-permute-done | bytes 65568 | tf_op jit(solution)/shard_map/ppermute | solution.py:27
  64.1 2.0 %collective-permute-done.19.refs_2_ = bf16[16,2048]{1,0:T(8,128)(2,1)S(1)} collective-permute-done((bf16[16,2048]{1,0:T(8,128)(2,1)S(1)}, bf16[16,2048]{1,0:T(8,128)(2,1)S(1)}, u32[]{:S(2)}, u32[]{:S(2)}) %collective-permute-start.19) | collective-permute-done | bytes 65568 | tf_op jit(solution)/shard_map/ppermute | solution.py:27
  66.1 0.7 %final.1 = f32[8,2,2048]{2,1,0:T(2,128)} custom-call(bf16[16,2048]{1,0:T(8,128)(2,1)S(1)} %output.1.refs_0_, bf16[16,2048]{1,0:T(8,128)(2,1)S(1)} %collective-permute-done.18.refs_1_, bf16[16,2048]{1,0:T(8,128)(2,1)S(1)} %collective-permute-done.19.refs_2_, bf16[16,2048]{1,0:T(8,128)(2,1)S(1)} %collective-permute-done.20.refs_3_, bf16[8,2,2048]{2,1,0:T(2,128)(2,1)S(1)} %copy-done), custom_call_target="tpu_custom_call" | custom-call | tf_op jit(solution)/shard_map/final/pallas_call | solution.py:653
  (25 shorter events, 0.9 us)
Async XLA Ops:
  0.7 12.3 %collective-permute-start.2 = (bf16[2,2,16,128]{3,2,1,0:T(8,128)(2,1)S(1)}, bf16[2,2,16,128]{3,2,1,0:T(8,128)(2,1)S(1)}, u32[]{:S(2)}, u32[]{:S(2)}) collective-permute-start(bf16[2,2,16,128]{3,2,1,0:T(8,128)(2,1)S(1)} %get-tuple-element.34.refs_0_), channel_id=1, source_target_pairs={{0,3},{1,2},{2,1},{3,0},{4,7},{5,6},{6,5},{7,4},{8,11},{9,10},{10,... | collective-permute-start | bytes 49160 | tf_op jit(solution)/shard_map/ppermute | solution.py:27
  5.9 7.2 %collective-permute-start.1 = (bf16[2,2,16,128]{3,2,1,0:T(8,128)(2,1)S(1)}, bf16[2,2,16,128]{3,2,1,0:T(8,128)(2,1)S(1)}, u32[]{:S(2)}, u32[]{:S(2)}) collective-permute-start(bf16[2,2,16,128]{3,2,1,0:T(8,128)(2,1)S(1)} %get-tuple-element.34.refs_0_), channel_id=1, source_target_pairs={{0,2},{1,3},{2,0},{3,1},{4,6},{5,7},{6,4},{7,5},{8,10},{9,11},{10,... | collective-permute-start | bytes 49160 | tf_op jit(solution)/shard_map/ppermute | solution.py:27
  5.9 7.2 %collective-permute-start = (bf16[2,2,16,128]{3,2,1,0:T(8,128)(2,1)S(1)}, bf16[2,2,16,128]{3,2,1,0:T(8,128)(2,1)S(1)}, u32[]{:S(2)}, u32[]{:S(2)}) collective-permute-start(bf16[2,2,16,128]{3,2,1,0:T(8,128)(2,1)S(1)} %get-tuple-element.34.refs_0_), channel_id=1, source_target_pairs={{0,1},{1,0},{2,3},{3,2},{4,5},{5,4},{6,7},{7,6},{8,9},{9,8},{10,11... | collective-permute-start | bytes 49160 | tf_op jit(solution)/shard_map/ppermute | solution.py:27
  13.2 5.6 %collective-permute-start.5 = (bf16[2,144,128]{2,1,0:T(8,128)(2,1)S(1)}, bf16[2,144,128]{2,1,0:T(8,128)(2,1)S(1)}, u32[]{:S(2)}, u32[]{:S(2)}) collective-permute-start(bf16[2,144,128]{2,1,0:T(8,128)(2,1)S(1)} %turned.1.after.refs_0_), channel_id=1, source_target_pairs={{0,12},{4,8},{8,4},{12,0},{1,13},{5,9},{9,5},{13,1},{2,14},{6,10},... | collective-permute-start | bytes 221192 | tf_op jit(solution)/shard_map/ppermute | solution.py:27
  13.7 5.7 %collective-permute-start.4 = (bf16[2,144,128]{2,1,0:T(8,128)(2,1)S(1)}, bf16[2,144,128]{2,1,0:T(8,128)(2,1)S(1)}, u32[]{:S(2)}, u32[]{:S(2)}) collective-permute-start(bf16[2,144,128]{2,1,0:T(8,128)(2,1)S(1)} %turned.1.after.refs_0_), channel_id=1, source_target_pairs={{0,8},{4,12},{8,0},{12,4},{1,9},{5,13},{9,1},{13,5},{2,10},{6,14},... | collective-permute-start | bytes 221192 | tf_op jit(solution)/shard_map/ppermute | solution.py:27
  15.0 4.4 %collective-permute-start.3 = (bf16[2,144,128]{2,1,0:T(8,128)(2,1)S(1)}, bf16[2,144,128]{2,1,0:T(8,128)(2,1)S(1)}, u32[]{:S(2)}, u32[]{:S(2)}) collective-permute-start(bf16[2,144,128]{2,1,0:T(8,128)(2,1)S(1)} %turned.1.after.refs_0_), channel_id=1, source_target_pairs={{0,4},{4,0},{8,12},{12,8},{1,5},{5,1},{9,13},{13,9},{2,6},{6,2},{1... | collective-permute-start | bytes 221192 | tf_op jit(solution)/shard_map/ppermute | solution.py:27
  21.2 6.8 %collective-permute-start.6 = (bf16[32,1024]{1,0:T(8,128)(2,1)S(1)}, bf16[32,1024]{1,0:T(8,128)(2,1)S(1)}, u32[]{:S(2)}, u32[]{:S(2)}) collective-permute-start(bf16[32,1024]{1,0:T(8,128)(2,1)S(1)} %get-tuple-element.46), channel_id=1, source_target_pairs={{0,3},{1,2},{2,1},{3,0},{4,7},{5,6},{6,5},{7,4},{8,11},{9,10},{10,... | collective-permute-start | bytes 196616 | tf_op jit(solution)/shard_map/ppermute | solution.py:27
  25.0 5.7 %collective-permute-start.7 = (bf16[32,1024]{1,0:T(8,128)(2,1)S(1)}, bf16[32,1024]{1,0:T(8,128)(2,1)S(1)}, u32[]{:S(2)}, u32[]{:S(2)}) collective-permute-start(bf16[32,1024]{1,0:T(8,128)(2,1)S(1)} %get-tuple-element.47), channel_id=1, source_target_pairs={{0,2},{1,3},{2,0},{3,1},{4,6},{5,7},{6,4},{7,5},{8,10},{9,11},{10,... | collective-permute-start | bytes 196616 | tf_op jit(solution)/shard_map/ppermute | solution.py:27
  25.0 5.7 %collective-permute-start.8 = (bf16[32,1024]{1,0:T(8,128)(2,1)S(1)}, bf16[32,1024]{1,0:T(8,128)(2,1)S(1)}, u32[]{:S(2)}, u32[]{:S(2)}) collective-permute-start(bf16[32,1024]{1,0:T(8,128)(2,1)S(1)} %get-tuple-element.48), channel_id=1, source_target_pairs={{0,1},{1,0},{2,3},{3,2},{4,5},{5,4},{6,7},{7,6},{8,9},{9,8},{10,11... | collective-permute-start | bytes 196616 | tf_op jit(solution)/shard_map/ppermute | solution.py:27
  31.6 6.7 %collective-permute-start.11 = (bf16[32,1024]{1,0:T(8,128)(2,1)S(1)}, bf16[32,1024]{1,0:T(8,128)(2,1)S(1)}, u32[]{:S(2)}, u32[]{:S(2)}) collective-permute-start(bf16[32,1024]{1,0:T(8,128)(2,1)S(1)} %get-tuple-element.52.refs_0_), channel_id=1, source_target_pairs={{0,3},{1,2},{2,1},{3,0},{4,7},{5,6},{6,5},{7,4},{8,11},{9,10},{10,... | collective-permute-start | bytes 196616 | tf_op jit(solution)/shard_map/ppermute | solution.py:27
  33.9 6.7 %collective-permute-start.10 = (bf16[32,1024]{1,0:T(8,128)(2,1)S(1)}, bf16[32,1024]{1,0:T(8,128)(2,1)S(1)}, u32[]{:S(2)}, u32[]{:S(2)}) collective-permute-start(bf16[32,1024]{1,0:T(8,128)(2,1)S(1)} %get-tuple-element.52.refs_0_), channel_id=1, source_target_pairs={{0,2},{1,3},{2,0},{3,1},{4,6},{5,7},{6,4},{7,5},{8,10},{9,11},{10,... | collective-permute-start | bytes 196616 | tf_op jit(solution)/shard_map/ppermute | solution.py:27
  34.2 6.3 %collective-permute-start.9 = (bf16[32,1024]{1,0:T(8,128)(2,1)S(1)}, bf16[32,1024]{1,0:T(8,128)(2,1)S(1)}, u32[]{:S(2)}, u32[]{:S(2)}) collective-permute-start(bf16[32,1024]{1,0:T(8,128)(2,1)S(1)} %get-tuple-element.52.refs_0_), channel_id=1, source_target_pairs={{0,1},{1,0},{2,3},{3,2},{4,5},{5,4},{6,7},{7,6},{8,9},{9,8},{10,11... | collective-permute-start | bytes 196616 | tf_op jit(solution)/shard_map/ppermute | solution.py:27
  41.8 6.4 %collective-permute-start.12 = (bf16[8,32,128]{2,1,0:T(8,128)(2,1)S(1)}, bf16[8,32,128]{2,1,0:T(8,128)(2,1)S(1)}, u32[]{:S(2)}, u32[]{:S(2)}) collective-permute-start(bf16[8,32,128]{2,1,0:T(8,128)(2,1)S(1)} %get-tuple-element.56), channel_id=1, source_target_pairs={{0,3},{1,2},{2,1},{3,0},{4,7},{5,6},{6,5},{7,4},{8,11},{9,10},{10,... | collective-permute-start | bytes 196616 | tf_op jit(solution)/shard_map/ppermute | solution.py:27
  43.8 6.2 %collective-permute-start.13 = (bf16[8,32,128]{2,1,0:T(8,128)(2,1)S(1)}, bf16[8,32,128]{2,1,0:T(8,128)(2,1)S(1)}, u32[]{:S(2)}, u32[]{:S(2)}) collective-permute-start(bf16[8,32,128]{2,1,0:T(8,128)(2,1)S(1)} %get-tuple-element.57), channel_id=1, source_target_pairs={{0,2},{1,3},{2,0},{3,1},{4,6},{5,7},{6,4},{7,5},{8,10},{9,11},{10,... | collective-permute-start | bytes 196616 | tf_op jit(solution)/shard_map/ppermute | solution.py:27
  43.8 6.2 %collective-permute-start.14 = (bf16[8,32,128]{2,1,0:T(8,128)(2,1)S(1)}, bf16[8,32,128]{2,1,0:T(8,128)(2,1)S(1)}, u32[]{:S(2)}, u32[]{:S(2)}) collective-permute-start(bf16[8,32,128]{2,1,0:T(8,128)(2,1)S(1)} %get-tuple-element.58), channel_id=1, source_target_pairs={{0,1},{1,0},{2,3},{3,2},{4,5},{5,4},{6,7},{7,6},{8,9},{9,8},{10,11... | collective-permute-start | bytes 196616 | tf_op jit(solution)/shard_map/ppermute | solution.py:27
  50.0 4.4 %collective-permute-start.16 = (bf16[9,32,128]{2,1,0:T(8,128)(2,1)S(1)}, bf16[9,32,128]{2,1,0:T(8,128)(2,1)S(1)}, u32[]{:S(2)}, u32[]{:S(2)}) collective-permute-start(bf16[9,32,128]{2,1,0:T(8,128)(2,1)S(1)} %summed.1.refs_0_), channel_id=1, source_target_pairs={{0,8},{4,12},{8,0},{12,4},{1,9},{5,13},{9,1},{13,5},{2,10},{6,14},... | collective-permute-start | bytes 221192 | tf_op jit(solution)/shard_map/ppermute | solution.py:27
  51.0 3.6 %collective-permute-start.15 = (bf16[9,32,128]{2,1,0:T(8,128)(2,1)S(1)}, bf16[9,32,128]{2,1,0:T(8,128)(2,1)S(1)}, u32[]{:S(2)}, u32[]{:S(2)}) collective-permute-start(bf16[9,32,128]{2,1,0:T(8,128)(2,1)S(1)} %summed.1.refs_0_), channel_id=1, source_target_pairs={{0,4},{4,0},{8,12},{12,8},{1,5},{5,1},{9,13},{13,9},{2,6},{6,2},{1... | collective-permute-start | bytes 221192 | tf_op jit(solution)/shard_map/ppermute | solution.py:27
  54.4 1.3 %collective-permute-start.17 = (bf16[9,32,128]{2,1,0:T(8,128)(2,1)S(1)}, bf16[9,32,128]{2,1,0:T(8,128)(2,1)S(1)}, u32[]{:S(2)}, u32[]{:S(2)}) collective-permute-start(bf16[9,32,128]{2,1,0:T(8,128)(2,1)S(1)} %collective-permute-done.16.refs_2_), channel_id=1, source_target_pairs={{0,4},{4,0},{8,12},{12,8},{1,5},{5,1},{9,13},{13,9},{2,6},{6,2},{1... | collective-permute-start | bytes 221192 | tf_op jit(solution)/shard_map/ppermute | solution.py:27
  55.7 10.4 %copy-start = (bf16[8,2,2048]{2,1,0:T(2,128)(2,1)S(1)}, bf16[8,2,2048]{2,1,0:T(2,128)(2,1)}, u32[]{:S(2)}) copy-start(bf16[8,2,2048]{2,1,0:T(2,128)(2,1)} %refs_4_.1) | copy-start | bytes 196612
  57.3 6.8 %collective-permute-start.20 = (bf16[16,2048]{1,0:T(8,128)(2,1)S(1)}, bf16[16,2048]{1,0:T(8,128)(2,1)S(1)}, u32[]{:S(2)}, u32[]{:S(2)}) collective-permute-start(bf16[16,2048]{1,0:T(8,128)(2,1)S(1)} %output.1.refs_0_), channel_id=1, source_target_pairs={{0,3},{1,2},{2,1},{3,0},{4,7},{5,6},{6,5},{7,4},{8,11},{9,10},{10,... | collective-permute-start | bytes 196616 | tf_op jit(solution)/shard_map/ppermute | solution.py:27
  59.3 6.7 %collective-permute-start.19 = (bf16[16,2048]{1,0:T(8,128)(2,1)S(1)}, bf16[16,2048]{1,0:T(8,128)(2,1)S(1)}, u32[]{:S(2)}, u32[]{:S(2)}) collective-permute-start(bf16[16,2048]{1,0:T(8,128)(2,1)S(1)} %output.1.refs_0_), channel_id=1, source_target_pairs={{0,2},{1,3},{2,0},{3,1},{4,6},{5,7},{6,4},{7,5},{8,10},{9,11},{10,... | collective-permute-start | bytes 196616 | tf_op jit(solution)/shard_map/ppermute | solution.py:27
  59.3 6.7 %collective-permute-start.18 = (bf16[16,2048]{1,0:T(8,128)(2,1)S(1)}, bf16[16,2048]{1,0:T(8,128)(2,1)S(1)}, u32[]{:S(2)}, u32[]{:S(2)}) collective-permute-start(bf16[16,2048]{1,0:T(8,128)(2,1)S(1)} %output.1.refs_0_), channel_id=1, source_target_pairs={{0,1},{1,0},{2,3},{3,2},{4,5},{5,4},{6,7},{7,6},{8,9},{9,8},{10,11... | collective-permute-start | bytes 196616 | tf_op jit(solution)/shard_map/ppermute | solution.py:27

commit v12 on v11

--- a/solution.py
+++ b/solution.py
@@ -38,13 +38,6 @@
 
 def gather(value, axis):
     return [value] + [pairs(value, axis, d) for d in range(1, lax.axis_size(axis))]
-
-
-def gather_by_chips(value, axis):
-    got = [value]
-    for d in range(1, lax.axis_size(axis)):
-        got.append(pairs(got[d - 1], axis, 1) if d % 2 else pairs(value, axis, d))
-    return got
 
 
 def lane_freqs(rows):
@@ -119,10 +112,18 @@
         source, to = pl.ds(first + i * size, size), pl.ds(i * size, size)
         x_copy = pltpu.make_async_copy(x_hbm.at[:, source], x_ref.at[:, to], sems.at[2 * i])
         w_copy = pltpu.make_async_copy(w_hbm.at[source], w_ref.at[to], sems.at[2 * i + 1])
-        x_copy.start()
-        w_copy.start()
         pairs_of.append((x_copy, w_copy))
     return pairs_of
+
+
+def start(copies):
+    for copy in copies:
+        copy.start()
+
+
+def wait(copies):
+    for copy in copies:
+        copy.wait()
 
 
 def add_block(x_ref, w_ref, rows, acc, out, fresh):
@@ -131,8 +132,8 @@
     for pair in range(KVH // 2):
         weight = pair_columns(w_ref, rows, pair, 0)
         columns = slice(2 * pair * HD, 2 * (pair + 1) * HD)
-        for start in range(0, tokens, tall):
-            at = slice(start, start + tall)
+        for top in range(0, tokens, tall):
+            at = slice(top, top + tall)
             product = jnp.dot(x_ref[at, rows], weight, preferred_element_type=F32)
             out[at, columns] = product if fresh else acc[at, columns] + product
 
@@ -142,17 +143,20 @@
     tokens = x_ref.shape[0]
     size = x_ref.shape[1] // 3
     copies = copies_of(x_hbm, w_hbm, x_ref, w_ref, sems, 0, size, 3)
+    start(copies[0])
     page_table(pages, prompts, counts, tails, meta)
     rotation_tables(pages, tokens // PAGE, meta, cos_ref, sin_ref)
     spots = [meta[3 * pages + r] + n for r in range(prompts) for n in range(new_count)]
     angles = by_row(len(spots), spots) * lane_freqs(len(spots))
     cos_q[...] = jnp.cos(angles)
     sin_q[...] = jnp.sin(angles) * sine_sign(len(spots))
-    for copy in copies[0] + copies[1]:
-        copy.wait()
-    add_block(x_ref, w_ref, slice(0, 2 * size), acc, acc, True)
-    for copy in copies[2]:
-        copy.wait()
+    start(copies[1])
+    for i in range(2):
+        wait(copies[i])
+        if i == 0:
+            start(copies[2])
+        add_block(x_ref, w_ref, slice(i * size, (i + 1) * size), acc, acc, i == 0)
+    wait(copies[2])
 
 
 def load(x, kv_weight, counts, tails, pages, new_count):
@@ -189,15 +193,15 @@
 def keys_kernel(acc, xa_ref, wa_ref, x_hbm, w_hbm, cos_ref, sin_ref, after, k_ref, x_ref, w_ref, total, sems):
     tokens, size = x_ref.shape
     tall = tokens // 2
-    ((x_copy, w_copy),) = copies_of(x_hbm, w_hbm, x_ref, w_ref, sems, 3 * size, size, 1)
+    (copies,) = copies_of(x_hbm, w_hbm, x_ref, w_ref, sems, 3 * size, size, 1)
+    start(copies)
     add_block(xa_ref, wa_ref, slice(2 * size, 3 * size), acc, total, False)
-    x_copy.wait()
-    w_copy.wait()
+    wait(copies)
     for pair in range(KVH // 2):
         weight = pair_columns(w_ref, slice(None), pair, 0)
         columns = slice(2 * pair * HD, 2 * (pair + 1) * HD)
-        for start in range(0, tokens, tall):
-            at = slice(start, start + tall)
+        for top in range(0, tokens, tall):
+            at = slice(top, top + tall)
             product = total[at, columns] + jnp.dot(x_ref[at], weight, preferred_element_type=F32)
             cosine, sine = cos_ref[at], sin_ref[at]
             for h in range(2):
@@ -444,8 +448,8 @@
 
 def weights_kernel(pages, prompts, n_tp, *refs):
     chunks = refs[:n_tp]
-    meta, _, w_ref, stats_ref = refs[n_tp:]
-    rows, tokens = w_ref.shape
+    meta, _, w_ref = refs[n_tp:]
+    rows, tokens = chunks[0].shape
     local_pages = tokens // PAGE
     first = lax.axis_index("seq") * local_pages
     lane = lax.broadcasted_iota(jnp.int32, (rows, PAGE), 1)
@@ -481,7 +485,7 @@
         stats = stats + jnp.where(here & (quarter == 2), part, 0.0)
     high = stats.astype(BF16).astype(F32)
     low = pltpu.roll(stats - high, prompts, 1)
-    stats_ref[...] = jnp.where(quarter == 3, low, stats).astype(BF16)
+    w_ref[:, tokens:] = jnp.where(quarter == 3, low, stats).astype(BF16)
 
 
 def softmax_weights(chunks, meta, after, pages, prompts):
@@ -490,86 +494,144 @@
     return pl.pallas_call(
         functools.partial(weights_kernel, pages, prompts, n_tp),
         in_specs=[VMEM] * n_tp + [SMEM, ANY],
-        out_specs=[VMEM, VMEM],
-        out_shape=[
-            jax.ShapeDtypeStruct((rows, tokens), BF16),
-            jax.ShapeDtypeStruct((rows, PAGE), BF16),
-        ],
+        out_specs=VMEM,
+        out_shape=jax.ShapeDtypeStruct((rows, tokens + HD), BF16),
         compiler_params=pltpu.CompilerParams(vmem_limit_bytes=8 * MIB),
         name="weights",
     )(*chunks, meta, after)
 
 
+def unpacked(stats, prompts):
+    stats = stats.astype(F32)
+    folded = stats + pltpu.roll(stats, HD - prompts, 1)
+    return folded, pltpu.roll(folded, HD - 2 * prompts, 1)
+
+
+def packed(top, total, prompts):
+    lane = lax.broadcasted_iota(jnp.int32, top.shape, 1)
+    out = jnp.zeros(top.shape, F32)
+    for i, value in enumerate((top, total)):
+        high = value.astype(BF16).astype(F32)
+        for j, piece in enumerate((high, value - high)):
+            at = (2 * i + j) * prompts
+            piece = pltpu.roll(piece, at, 1) if at else piece
+            out = jnp.where((lane >= at) & (lane < at + prompts), piece, out)
+    return out.astype(BF16)
+
+
 def weighted_kernel(n_tp, *refs):
     pieces = refs[:n_tp]
-    va_ref, vb_ref, meta = refs[n_tp : n_tp + 3]
-    outs = refs[n_tp + 3 : n_tp + 3 + n_tp]
-    ready, total = refs[n_tp + 3 + n_tp :]
-    rows_local, tokens_here = pieces[0].shape
+    va_ref, vb_ref, meta, keep_ref, send_ref, ready, total = refs[n_tp:]
+    rows_local = pieces[0].shape[0]
+    tokens_here = va_ref.shape[0]
     kv_local = KVH // n_tp
     rows = rows_local // kv_local
     local_pages = tokens_here // PAGE
-    first = lax.axis_index("seq") * local_pages
-    me = lax.axis_index("tp")
-    own = [pl.ds(pl.multiple_of(partner(me, d, n_tp) * rows_local, rows_local), rows_local) for d in range(n_tp)]
+    half = keep_ref.shape[0] - 1
+    seq, me = lax.axis_index("seq"), lax.axis_index("tp")
+    first = seq * local_pages
+    core = seq % 2
     for d in range(n_tp):
-        at = pl.multiple_of((me ^ d) * rows_local, rows_local)
-        ready[pl.ds(at, rows_local)] = pieces[d][...]
+        at = pl.ds(pl.multiple_of((me ^ d) * rows_local, rows_local), rows_local)
+        ready[at] = pieces[d][:, :tokens_here]
+        keep_ref[half, at] = pieces[d][:, tokens_here:]
+        send_ref[half, at] = pieces[d][:, tokens_here:]
     total[...] = jnp.zeros_like(total)
-    half = va_ref.shape[1] // HD
+    columns = va_ref.shape[1] // HD
     for p in range(local_pages):
         request = meta[first + p]
         tokens = slice(p * PAGE, (p + 1) * PAGE)
         for head in range(KVH):
-            v_ref = va_ref if head < half else vb_ref
-            v = v_ref[tokens, head % half * HD : (head % half + 1) * HD]
+            v_ref = va_ref if head < columns else vb_ref
+            v = v_ref[tokens, head % columns * HD : (head % columns + 1) * HD]
             at = slice(head * rows, (head + 1) * rows)
             total[request, at] += jnp.dot(ready[at, tokens], v, preferred_element_type=F32)
-    for d in range(n_tp):
-        outs[d][...] = total[:, own[d]].astype(BF16)
+    for i in range(half):
+        keep_ref[i] = total[core * half + i].astype(BF16)
+        send_ref[i] = total[(1 - core) * half + i].astype(BF16)
 
 
 def weighted_values(pieces, va, vb, meta, prompts):
     n_tp = len(pieces)
-    rows, tokens = pieces[0].shape
+    rows = pieces[0].shape[0] * n_tp
     return pl.pallas_call(
         functools.partial(weighted_kernel, n_tp),
         in_specs=[VMEM] * (n_tp + 2) + [SMEM],
-        out_specs=[VMEM] * n_tp,
-        out_shape=[jax.ShapeDtypeStruct((prompts, rows, HD), BF16)] * n_tp,
+        out_specs=[VMEM] * 2,
+        out_shape=[jax.ShapeDtypeStruct((prompts // 2 + 1, rows, HD), BF16)] * 2,
         scratch_shapes=[
-            pltpu.VMEM((rows * n_tp, tokens), BF16),
-            pltpu.VMEM((prompts, rows * n_tp, HD), F32),
+            pltpu.VMEM((rows, va.shape[0]), BF16),
+            pltpu.VMEM((prompts, rows, HD), F32),
         ],
         compiler_params=pltpu.CompilerParams(vmem_limit_bytes=24 * MIB),
         cost_estimate=pl.CostEstimate(
-            flops=2 * tokens * rows * n_tp * HD, bytes_accessed=8 * MIB, transcendentals=0
+            flops=2 * va.shape[0] * rows * HD, bytes_accessed=8 * MIB, transcendentals=0
         ),
         name="weighted",
     )(*pieces, va, vb, meta)
 
 
+def joined_kernel(n_tp, keep_ref, got_ref, *refs):
+    outs, stats_ref, ready, facts = refs[:n_tp], refs[n_tp], refs[n_tp + 1], refs[n_tp + 2]
+    more, rows, _ = keep_ref.shape
+    half = more - 1
+    prompts = 2 * half
+    count = rows // n_tp
+    me = lax.axis_index("tp")
+    core = lax.axis_index("seq") % 2
+    (top_a, sum_a), (top_b, sum_b) = [unpacked(r[half], prompts) for r in (keep_ref, got_ref)]
+    top = jnp.maximum(top_a, top_b)
+    factors = [jnp.exp(top_a - top), jnp.exp(top_b - top)]
+    facts[...] = packed(top, sum_a * factors[0] + sum_b * factors[1], prompts).astype(F32)
+    own = pl.ds(pl.multiple_of(me * count, count), count)
+    stats_ref[...] = facts[own].astype(BF16)
+    factors = [jnp.where(core == 0, f, pltpu.roll(f, HD - half, 1)) for f in factors]
+    for i in range(half):
+        total = factors[0][:, i : i + 1] * keep_ref[i].astype(F32)
+        total = total + factors[1][:, i : i + 1] * got_ref[i].astype(F32)
+        ready[i] = total.astype(BF16)
+    for d in range(n_tp):
+        at = pl.ds(pl.multiple_of(partner(me, d, n_tp) * count, count), count)
+        outs[d][...] = ready[:, at]
+
+
+def joined(keep, got, n_tp):
+    more, rows, _ = keep.shape
+    count = rows // n_tp
+    return pl.pallas_call(
+        functools.partial(joined_kernel, n_tp),
+        in_specs=[VMEM, VMEM],
+        out_specs=[VMEM] * (n_tp + 1),
+        out_shape=[jax.ShapeDtypeStruct((more - 1, count, HD), BF16)] * n_tp
+        + [jax.ShapeDtypeStruct((count, HD), BF16)],
+        scratch_shapes=[pltpu.VMEM((more - 1, rows, HD), BF16), pltpu.VMEM((rows, HD), F32)],
+        compiler_params=pltpu.CompilerParams(vmem_limit_bytes=16 * MIB),
+        cost_estimate=pl.CostEstimate(flops=0, bytes_accessed=2 * MIB, transcendentals=0),
+        name="joined",
+    )(keep, got)
+
+
 def summed_kernel(n_tp, *refs):
     chunks = refs[:n_tp]
     stats_ref, out_ref = refs[n_tp:]
-    prompts = chunks[0].shape[0]
+    half = chunks[0].shape[0]
     total = chunks[0][...].astype(F32)
     for d in range(1, n_tp):
         total = total + chunks[d][...].astype(F32)
-    out_ref[:prompts] = total.astype(BF16)
-    out_ref[prompts] = stats_ref[...]
+    out_ref[:half] = total.astype(BF16)
+    out_ref[half] = stats_ref[...]
 
 
 def summed(chunks, stats):
     n_tp = len(chunks)
-    prompts, rows, _ = chunks[0].shape
+    half, rows, _ = chunks[0].shape
     return pl.pallas_call(
         functools.partial(summed_kernel, n_tp),
         in_specs=[VMEM] * (n_tp + 1),
         out_specs=VMEM,
-        out_shape=jax.ShapeDtypeStruct((prompts + 1, rows, HD), BF16),
+        out_shape=jax.ShapeDtypeStruct((half + 1, rows, HD), BF16),
         compiler_params=pltpu.CompilerParams(vmem_limit_bytes=8 * MIB),
-        cost_estimate=pl.CostEstimate(flops=0, bytes_accessed=4 * MIB, transcendentals=0),
+        cost_estimate=pl.CostEstimate(flops=0, bytes_accessed=16 * MIB, transcendentals=0),
         name="summed",
     )(*chunks, stats)
 
@@ -578,20 +640,17 @@
     pieces = refs[:n_seq]
     fresh_ref, value_ref, wa_ref, wb_ref, out_ref, held = refs[n_seq:]
     more, rows_local, _ = pieces[0].shape
-    prompts = more - 1
+    own = more - 1
+    prompts = 2 * own
     new_count = fresh_ref.shape[0]
     rows = new_count * GROUP
     kv_local = rows_local // rows
     heads = kv_local * GROUP
-    tops, parts = [], []
-    for s in range(n_seq):
-        stats = pieces[s][prompts].astype(F32)
-        folded = stats + pltpu.roll(stats, HD - prompts, 1)
-        tops.append(folded)
-        parts.append(pltpu.roll(folded, HD - 2 * prompts, 1))
+    core = lax.axis_index("seq") % 2
+    tops, parts = zip(*[unpacked(pieces[s][own], prompts) for s in range(0, n_seq, 2)])
     fresh = [fresh_ref[n] for n in range(new_count)]
     top = fresh[0]
-    for other in fresh[1:] + tops:
+    for other in fresh[1:] + list(tops):
         top = jnp.maximum(top, other)
     weights = [jnp.exp(f - top) for f in fresh]
     factors = [jnp.exp(t - top) for t in tops]
@@ -600,18 +659,27 @@
         total = total + w
     for f, part in zip(factors, parts):
         total = total + f * part
-    weights = [w / total for w in weights]
-    factors = [f / total for f in factors]
-    for r in range(prompts):
+    lane = lax.broadcasted_iota(jnp.int32, (rows_local, HD), 1)
+
+    def own_first(value):
+        other = jnp.where(lane < own, pltpu.roll(value, HD - own, 1), pltpu.roll(value, own, 1))
+        return jnp.where(core == 0, value, other)
+
+    weights = [own_first(w / total) for w in weights]
+    factors = [own_first(f / total) for f in factors]
+    for i in range(prompts):
+        side = i // own
+        request = (core ^ side) * own + i % own
         sums = jnp.zeros((rows_local, HD), F32)
-        for s in range(n_seq):
-            sums = sums + factors[s][:, r : r + 1] * pieces[s][r].astype(F32)
+        for chip in range(n_seq // 2):
+            piece = pieces[2 * chip + side][i % own].astype(F32)
+            sums = sums + factors[chip][:, i : i + 1] * piece
         for n in range(new_count):
-            sums = sums + weights[n][:, r : r + 1] * value_ref[r * new_count + n]
+            sums = sums + weights[n][:, i : i + 1] * value_ref[request * new_count + n]
         for g in range(kv_local):
             for n in range(new_count):
                 at = g * rows + n * GROUP
-                held[g * GROUP : (g + 1) * GROUP, r * new_count + n] = sums[at : at + GROUP]
+                held[g * GROUP : (g + 1) * GROUP, request * new_count + n] = sums[at : at + GROUP]
     half = heads // 2
     product = jnp.zeros(out_ref.shape, F32)
     for w_ref, at in ((wa_ref, 0), (wb_ref, half)):
@@ -624,7 +692,7 @@
 def output_partial(pieces, fresh, values, weights):
     n_seq = len(pieces)
     new_count = fresh.shape[0]
-    prompts = pieces[0].shape[0] - 1
+    prompts = 2 * (pieces[0].shape[0] - 1)
     depth, columns = weights[0].shape
     return pl.pallas_call(
         functools.partial(output_kernel, n_seq),
@@ -677,11 +745,12 @@
     new = gather(new, "seq")
     scores = partial_scores(new, k, meta, prompts, n_tp)
     va, oa = project_values((xa, wa, xb, wb), out_weight, 0, scores[0])
-    weights, stats = softmax_weights(exchange(scores, "tp"), meta, va, pages, prompts)
-    vb, ob = project_values((xa, wa, xb, wb), out_weight, 1, stats)
-    fresh, values = fresh_scores(new, stats, prompts, new_count, n_tp)
-    chunks = weighted_values(gather(weights, "tp"), va, vb, meta, prompts)
-    pieces = gather_by_chips(summed(exchange(chunks, "tp"), stats), "seq")
+    weights = softmax_weights(exchange(scores, "tp"), meta, va, pages, prompts)
+    vb, ob = project_values((xa, wa, xb, wb), out_weight, 1, weights)
+    fresh, values = fresh_scores(new, weights, prompts, new_count, n_tp)
+    keep, send = weighted_values(gather(weights, "tp"), va, vb, meta, prompts)
+    *chunks, stats = joined(keep, pairs(send, "seq", 1), n_tp)
+    pieces = gather(summed(exchange(chunks, "tp"), stats), "seq")
     partial = output_partial(pieces, fresh, values, (oa, ob))
     return final_sum(gather(partial, "tp"), residual)
 

time: 67.1 us -> 66.9 us (level)
  starting transfers between devices: 26.4 us -> 27.4 us
  waiting for transfers between devices: 18.2 us -> 17.3 us
    ppermute x21 -> x22, starting transfers between devices: 26.4 us -> 27.4 us  [pairs(): lax.ppermute(value, axis, [(i, i ^ d) for i in range(lax.axis_size(axis))])]
    pallas_call x1, Pallas kernels: 6.54 us -> 5.68 us  [load(): pl.pallas_call(functools.partial(load_kernel, pages, prompts, new_count),...]
    ppermute x21 -> x22, waiting for transfers between devices: 18.2 us -> 17.3 us  [pairs(): lax.ppermute(value, axis, [(i, i ^ d) for i in range(lax.axis_size(axis))])]
  transfers between devices with their start and end apart: 21 -> 22, of which waited for: 9 -> 11; matrix products, arithmetic and copies ran while one was open for 0% -> 0% of each run, Pallas kernels for 22% -> 21%
where the time goes in v12:
time: 66.9 us; the launch traced here: 66.6 us
  starting transfers between devices  27.4 us (41%)
  Pallas kernels  21.7 us (32%)
  waiting for transfers between devices  17.3 us (26%)
    ppermute x22, starting transfers between devices, pairs(): lax.ppermute(value, axis, [(i, i ^ d) for i in range(lax.axis_size(axis))])  27.4 us
    ppermute x22, waiting for transfers between devices, pairs(): lax.ppermute(value, axis, [(i, i ^ d) for i in range(lax.axis_size(axis))])  17.3 us
    pallas_call x1, Pallas kernels, load(): pl.pallas_call(functools.partial(load_kernel, pages, prompts, new_count),...  5.68 us
    pallas_call x2, Pallas kernels, project_values(): pl.pallas_call(functools.partial(values_kernel, first), in_specs=[VMEM] *...  4.68 us
    pallas_call x1, Pallas kernels, rotated_keys(): pl.pallas_call(keys_kernel, in_specs=[VMEM] * 3 + [hbm] * 2 + [VMEM] * 2...  3.62 us
    pallas_call x1, Pallas kernels, partial_scores(): pl.pallas_call(functools.partial(scores_kernel, n_seq, n_tp), in_specs=[V...  1.76 us
    pallas_call x1, Pallas kernels, output_partial(): pl.pallas_call(functools.partial(output_kernel, n_seq), in_specs=[VMEM] *...  1.66 us
  transfers between devices with their start and end apart: 22, of which 11 were waited for; matrix products, arithmetic and copies ran while one was open for 0% of the time, Pallas kernels for 21%

profile of v12, /device:TPU:0, one launch (start us, length us, event | category | flops | bytes accessed | tf_op | source)
XLA Modules:
  0.0 66.6 jit_solution(12402497283490679401)
XLA Ops:
  0.0 0.7 %prepare.1 = (bf16[2,2,16,128]{3,2,1,0:T(8,128)(2,1)S(1)}, f32[2,2,4,128]{3,2,1,0:T(4,128)S(1)}) custom-call(bf16[2,2,2048]{2,1,0:T(2,128)(2,1)} %q_ref.1, bf16[2,2,512]{2,1,0:T(2,128)(2,1)} %kv_ref.1), custom_call_target="tpu_custom_call" | custom-call | bytes 1048576 | tf_op jit(solution)/shard_map/prepare/pallas_call | solution.py:291
  0.7 5.1 %collective-permute-start.2 = (bf16[2,2,16,128]{3,2,1,0:T(8,128)(2,1)S(1)}, bf16[2,2,16,128]{3,2,1,0:T(8,128)(2,1)S(1)}, u32[]{:S(2)}, u32[]{:S(2)}) collective-permute-start(bf16[2,2,16,128]{3,2,1,0:T(8,128)(2,1)S(1)} %get-tuple-element.35.refs_0_), channel_id=1, source_target_pairs={{0,3},{1,2},{2,1},{3,0},{4,7},{5,6},{6,5},{7,4},{8,11},{9,10},{10,... | collective-permute-start | bytes 49160 | tf_op jit(solution)/shard_map/ppermute | solution.py:27
  5.9 0.6 collective-permute-start
  6.5 5.7 %load.1 = (f32[1024,1024]{1,0:T(8,128)S(1)}, bf16[1024,1536]{1,0:T(8,128)(2,1)S(1)}, bf16[1536,2048]{1,0:T(8,128)(2,1)S(1)}, f32[1024,128]{1,0:T(8,128)S(1)}, f3...) custom-call(bf16[1024,2048]{1,0:T(8,128)(2,1)} %x_hbm.3, ...), custom_call_target="tpu_custom_call" | custom-call | flops 2147483648 | bytes 9437184 | tf_op jit(solution)/shard_map/load/pallas_call | solution.py:168
  12.8 1.3 %collective-permute-start.4 = (bf16[2,144,128]{2,1,0:T(8,128)(2,1)S(1)}, bf16[2,144,128]{2,1,0:T(8,128)(2,1)S(1)}, u32[]{:S(2)}, u32[]{:S(2)}) collective-permute-start(bf16[2,144,128]{2,1,0:T(8,128)(2,1)S(1)} %turned.1.after.refs_0_), channel_id=1, source_target_pairs={{0,8},{4,12},{8,0},{12,4},{1,9},{5,13},{9,1},{13,5},{2,10},{6,14},... | collective-permute-start | bytes 221192 | tf_op jit(solution)/shard_map/ppermute | solution.py:27
  14.3 3.6 %keys.1 = (bf16[1024,1024]{1,0:T(8,128)(2,1)S(1)}, bf16[1024,512]{1,0:T(8,128)(2,1)S(1)}, bf16[512,2048]{1,0:T(8,128)(2,1)S(1)}) custom-call(f32[1024,1024]{1,0:T(8,128)S(1)} %get-tuple-element.39.acc, bf16[1024,1536]{1,0:T(8,128)(2,1)S(1)} %get-tuple-element.40.xa_ref, bf16[1536,2048]{1,0:T(8,128)(2,1)S(1)} %get-tuple-element.41.wa_ref, ...), custom_call_target="tpu_custom_call" | custom-call | flops 2147483648 | bytes 8388608 | tf_op jit(solution)/shard_map/keys/pallas_call | solution.py:217
  18.5 1.8 %scores.1 = (bf16[32,1024]{1,0:T(8,128)(2,1)S(1)}, bf16[32,1024]{1,0:T(8,128)(2,1)S(1)}, bf16[32,1024]{1,0:T(8,128)(2,1)S(1)}, bf16[32,1024]{1,0:T(8,128)(2,1)S(1)}) custom-call(bf16[2,144,128]{2,1,0:T(8,128)(2,1)S(1)} %turned.1.after.refs_0_, bf16[2,144,128]{2,1,0:T(8,128)(2,1)S(1)} %collective-permute-done.3.refs_1_, ...), custom_call_target="tpu_custom_call" | custom-call | flops 33554432 | bytes 6291456 | tf_op jit(solution)/shard_map/scores/pallas_call | solution.py:383
  20.3 3.8 %collective-permute-start.6 = (bf16[32,1024]{1,0:T(8,128)(2,1)S(1)}, bf16[32,1024]{1,0:T(8,128)(2,1)S(1)}, u32[]{:S(2)}, u32[]{:S(2)}) collective-permute-start(bf16[32,1024]{1,0:T(8,128)(2,1)S(1)} %get-tuple-element.47), channel_id=1, source_target_pairs={{0,3},{1,2},{2,1},{3,0},{4,7},{5,6},{6,5},{7,4},{8,11},{9,10},{10,... | collective-permute-start | bytes 196616 | tf_op jit(solution)/shard_map/ppermute | solution.py:27
  24.8 2.3 %values.2 = (bf16[1024,512]{1,0:T(8,128)(2,1)S(1)}, bf16[1024,2048]{1,0:T(8,128)(2,1)S(1)}) custom-call(bf16[1024,1536]{1,0:T(8,128)(2,1)S(1)} %get-tuple-element.40.xa_ref, bf16[1536,2048]{1,0:T(8,128)(2,1)S(1)} %get-tuple-element.41.wa_ref, bf16[1024,512]{1,0:T(8,128)(2,1)S(1)} %get-tuple-element.50.xb_ref, ...), custom_call_target="tpu_custom_call" | custom-call | flops 1610612736 | bytes 8388608 | tf_op jit(solution)/shard_map/values/pallas_call | solution.py:259
  27.1 2.7 %collective-permute-done.7.refs_2_ = bf16[32,1024]{1,0:T(8,128)(2,1)S(1)} collective-permute-done((bf16[32,1024]{1,0:T(8,128)(2,1)S(1)}, bf16[32,1024]{1,0:T(8,128)(2,1)S(1)}, u32[]{:S(2)}, u32[]{:S(2)}) %collective-permute-start.7) | collective-permute-done | bytes 65568 | tf_op jit(solution)/shard_map/ppermute | solution.py:27
  29.8 0.9 %weights.1.after.refs_0_.refs_4_ = bf16[32,1152]{1,0:T(8,128)(2,1)S(1)} custom-call(bf16[32,1024]{1,0:T(8,128)(2,1)S(1)} %get-tuple-element.46.after.refs_0_, bf16[32,1024]{1,0:T(8,128)(2,1)S(1)} %collective-permute-done.6.refs_1_, bf16[32,1024]{1,0:T(8,128)(2,1)S(1)} %collective-permute-done.7.refs_2_, bf16[32,1024]{1,0:T(8,128)(2,1)S(1)} %collective-permute-done.8.refs_3_, ...), custom_call_target="tpu_custom_call" | custom-call | tf_op jit(solution)/shard_map/weights/pallas_call | solution.py:494
  30.7 2.3 %collective-permute-start.11 = (bf16[32,1152]{1,0:T(8,128)(2,1)S(1)}, bf16[32,1152]{1,0:T(8,128)(2,1)S(1)}, u32[]{:S(2)}, u32[]{:S(2)}) collective-permute-start(bf16[32,1152]{1,0:T(8,128)(2,1)S(1)} %weights.1.after.refs_0_.refs_4_), channel_id=1, source_target_pairs={{0,3},{1,2},{2,1},{3,0},{4,7},{5,6},{6,5},{7,4},{8,11},{9,10},{10,... | collective-permute-start | bytes 221192 | tf_op jit(solution)/shard_map/ppermute | solution.py:27
  33.4 1.7 %collective-permute-start.9 = (bf16[32,1152]{1,0:T(8,128)(2,1)S(1)}, bf16[32,1152]{1,0:T(8,128)(2,1)S(1)}, u32[]{:S(2)}, u32[]{:S(2)}) collective-permute-start(bf16[32,1152]{1,0:T(8,128)(2,1)S(1)} %weights.1.after.refs_0_.refs_4_), channel_id=1, source_target_pairs={{0,1},{1,0},{2,3},{3,2},{4,5},{5,4},{6,7},{7,6},{8,9},{9,8},{10,11... | collective-permute-start | bytes 221192 | tf_op jit(solution)/shard_map/ppermute | solution.py:27
  35.1 2.3 %values.3 = (bf16[1024,512]{1,0:T(8,128)(2,1)S(1)}, bf16[1024,2048]{1,0:T(8,128)(2,1)S(1)}) custom-call(bf16[1024,1536]{1,0:T(8,128)(2,1)S(1)} %get-tuple-element.40.xa_ref, bf16[1536,2048]{1,0:T(8,128)(2,1)S(1)} %get-tuple-element.41.wa_ref, bf16[1024,512]{1,0:T(8,128)(2,1)S(1)} %get-tuple-element.50.xb_ref, ...), custom_call_target="tpu_custom_call" | custom-call | flops 1610612736 | bytes 8388608 | tf_op jit(solution)/shard_map/values/pallas_call | solution.py:259
  37.7 2.6 %collective-permute-done.10.refs_2_ = bf16[32,1152]{1,0:T(8,128)(2,1)S(1)} collective-permute-done((bf16[32,1152]{1,0:T(8,128)(2,1)S(1)}, bf16[32,1152]{1,0:T(8,128)(2,1)S(1)}, u32[]{:S(2)}, u32[]{:S(2)}) %collective-permute-start.10) | collective-permute-done | bytes 73760 | tf_op jit(solution)/shard_map/ppermute | solution.py:27
  40.3 1.3 %weighted.1 = (bf16[5,128,128]{2,1,0:T(8,128)(2,1)S(1)}, bf16[5,128,128]{2,1,0:T(8,128)(2,1)S(1)}) custom-call(bf16[32,1152]{1,0:T(8,128)(2,1)S(1)} %weights.1.after.refs_0_.refs_4_, bf16[32,1152]{1,0:T(8,128)(2,1)S(1)} %collective-permute-done.9.refs_1_, bf16[32,1152]{1,0:T(8,128)(2,1)S(1)} %collective-permute-done.10.refs_2_, ...), custom_call_target="tpu_custom_call" | custom-call | flops 33554432 | bytes 8388608 | tf_op jit(solution)/shard_map/weighted/pallas_call | solution.py:557
  41.7 1.4 %collective-permute-done.12.got_ref = bf16[5,128,128]{2,1,0:T(8,128)(2,1)S(1)} collective-permute-done((bf16[5,128,128]{2,1,0:T(8,128)(2,1)S(1)}, bf16[5,128,128]{2,1,0:T(8,128)(2,1)S(1)}, u32[]{:S(2)}, u32[]{:S(2)}) %collective-permute-start.12) | collective-permute-done | bytes 163872 | tf_op jit(solution)/shard_map/ppermute | solution.py:27
  43.5 2.0 %collective-permute-start.13 = (bf16[4,32,128]{2,1,0:T(8,128)(2,1)S(1)}, bf16[4,32,128]{2,1,0:T(8,128)(2,1)S(1)}, u32[]{:S(2)}, u32[]{:S(2)}) collective-permute-start(bf16[4,32,128]{2,1,0:T(8,128)(2,1)S(1)} %get-tuple-element.57), channel_id=1, source_target_pairs={{0,3},{1,2},{2,1},{3,0},{4,7},{5,6},{6,5},{7,4},{8,11},{9,10},{10,... | collective-permute-start | bytes 98312 | tf_op jit(solution)/shard_map/ppermute | solution.py:27
  45.5 2.5 %collective-permute-start.15 = (bf16[4,32,128]{2,1,0:T(8,128)(2,1)S(1)}, bf16[4,32,128]{2,1,0:T(8,128)(2,1)S(1)}, u32[]{:S(2)}, u32[]{:S(2)}) collective-permute-start(bf16[4,32,128]{2,1,0:T(8,128)(2,1)S(1)} %get-tuple-element.59), channel_id=1, source_target_pairs={{0,1},{1,0},{2,3},{3,2},{4,5},{5,4},{6,7},{7,6},{8,9},{9,8},{10,11... | collective-permute-start | bytes 98312 | tf_op jit(solution)/shard_map/ppermute | solution.py:27
  47.9 1.4 %collective-permute-done.13.refs_1_ = bf16[4,32,128]{2,1,0:T(8,128)(2,1)S(1)} collective-permute-done((bf16[4,32,128]{2,1,0:T(8,128)(2,1)S(1)}, bf16[4,32,128]{2,1,0:T(8,128)(2,1)S(1)}, u32[]{:S(2)}, u32[]{:S(2)}) %collective-permute-start.13) | collective-permute-done | bytes 32800 | tf_op jit(solution)/shard_map/ppermute | solution.py:27
  49.4 1.0 %collective-permute-done.14.refs_2_ = bf16[4,32,128]{2,1,0:T(8,128)(2,1)S(1)} collective-permute-done((bf16[4,32,128]{2,1,0:T(8,128)(2,1)S(1)}, bf16[4,32,128]{2,1,0:T(8,128)(2,1)S(1)}, u32[]{:S(2)}, u32[]{:S(2)}) %collective-permute-start.14) | collective-permute-done | bytes 32800 | tf_op jit(solution)/shard_map/ppermute | solution.py:27
  50.4 1.0 %collective-permute-start.17 = (bf16[5,32,128]{2,1,0:T(8,128)(2,1)S(1)}, bf16[5,32,128]{2,1,0:T(8,128)(2,1)S(1)}, u32[]{:S(2)}, u32[]{:S(2)}) collective-permute-start(bf16[5,32,128]{2,1,0:T(8,128)(2,1)S(1)} %summed.1.refs_0_), channel_id=1, source_target_pairs={{0,8},{4,12},{8,0},{12,4},{1,9},{5,13},{9,1},{13,5},{2,10},{6,14},... | collective-permute-start | bytes 122888 | tf_op jit(solution)/shard_map/ppermute | solution.py:27
  51.4 0.8 %collective-permute-start.16 = (bf16[5,32,128]{2,1,0:T(8,128)(2,1)S(1)}, bf16[5,32,128]{2,1,0:T(8,128)(2,1)S(1)}, u32[]{:S(2)}, u32[]{:S(2)}) collective-permute-start(bf16[5,32,128]{2,1,0:T(8,128)(2,1)S(1)} %summed.1.refs_0_), channel_id=1, source_target_pairs={{0,4},{4,0},{8,12},{12,8},{1,5},{5,1},{9,13},{13,9},{2,6},{6,2},{1... | collective-permute-start | bytes 122888 | tf_op jit(solution)/shard_map/ppermute | solution.py:27
  52.4 1.4 %collective-permute-done.18.refs_3_ = bf16[5,32,128]{2,1,0:T(8,128)(2,1)S(1)} collective-permute-done((bf16[5,32,128]{2,1,0:T(8,128)(2,1)S(1)}, bf16[5,32,128]{2,1,0:T(8,128)(2,1)S(1)}, u32[]{:S(2)}, u32[]{:S(2)}) %collective-permute-start.18) | collective-permute-done | bytes 40992 | tf_op jit(solution)/shard_map/ppermute | solution.py:27
  53.9 1.0 %collective-permute-done.17.refs_2_ = bf16[5,32,128]{2,1,0:T(8,128)(2,1)S(1)} collective-permute-done((bf16[5,32,128]{2,1,0:T(8,128)(2,1)S(1)}, bf16[5,32,128]{2,1,0:T(8,128)(2,1)S(1)}, u32[]{:S(2)}, u32[]{:S(2)}) %collective-permute-start.17) | collective-permute-done | bytes 40992 | tf_op jit(solution)/shard_map/ppermute | solution.py:27
  54.9 1.7 %output.1.refs_0_ = bf16[16,2048]{1,0:T(8,128)(2,1)S(1)} custom-call(bf16[5,32,128]{2,1,0:T(8,128)(2,1)S(1)} %summed.1.refs_0_, bf16[5,32,128]{2,1,0:T(8,128)(2,1)S(1)} %collective-permute-done.16.refs_1_, bf16[5,32,128]{2,1,0:T(8,128)(2,1)S(1)} %collective-permute-done.17.refs_2_, bf16[5,32,128]{2,1,0:T(8,128)(2,1)S(1)} %collective-permute-done.18.refs_3_, ...), custom_call_target="tpu_custom_call" | custom-call | tf_op jit(solution)/shard_map/output/pallas_call | solution.py:697
  56.5 1.9 %collective-permute-start.21 = (bf16[16,2048]{1,0:T(8,128)(2,1)S(1)}, bf16[16,2048]{1,0:T(8,128)(2,1)S(1)}, u32[]{:S(2)}, u32[]{:S(2)}) collective-permute-start(bf16[16,2048]{1,0:T(8,128)(2,1)S(1)} %output.1.refs_0_), channel_id=1, source_target_pairs={{0,3},{1,2},{2,1},{3,0},{4,7},{5,6},{6,5},{7,4},{8,11},{9,10},{10,... | collective-permute-start | bytes 196616 | tf_op jit(solution)/shard_map/ppermute | solution.py:27
  58.5 1.1 %collective-permute-start.20 = (bf16[16,2048]{1,0:T(8,128)(2,1)S(1)}, bf16[16,2048]{1,0:T(8,128)(2,1)S(1)}, u32[]{:S(2)}, u32[]{:S(2)}) collective-permute-start(bf16[16,2048]{1,0:T(8,128)(2,1)S(1)} %output.1.refs_0_), channel_id=1, source_target_pairs={{0,2},{1,3},{2,0},{3,1},{4,6},{5,7},{6,4},{7,5},{8,10},{9,11},{10,... | collective-permute-start | bytes 196616 | tf_op jit(solution)/shard_map/ppermute | solution.py:27
  59.5 1.4 %collective-permute-start.19 = (bf16[16,2048]{1,0:T(8,128)(2,1)S(1)}, bf16[16,2048]{1,0:T(8,128)(2,1)S(1)}, u32[]{:S(2)}, u32[]{:S(2)}) collective-permute-start(bf16[16,2048]{1,0:T(8,128)(2,1)S(1)} %output.1.refs_0_), channel_id=1, source_target_pairs={{0,1},{1,0},{2,3},{3,2},{4,5},{5,4},{6,7},{7,6},{8,9},{9,8},{10,11... | collective-permute-start | bytes 196616 | tf_op jit(solution)/shard_map/ppermute | solution.py:27
  60.9 2.4 %collective-permute-done.21.refs_3_ = bf16[16,2048]{1,0:T(8,128)(2,1)S(1)} collective-permute-done((bf16[16,2048]{1,0:T(8,128)(2,1)S(1)}, bf16[16,2048]{1,0:T(8,128)(2,1)S(1)}, u32[]{:S(2)}, u32[]{:S(2)}) %collective-permute-start.21) | collective-permute-done | bytes 65568 | tf_op jit(solution)/shard_map/ppermute | solution.py:27
  63.3 2.6 %collective-permute-done.20.refs_2_ = bf16[16,2048]{1,0:T(8,128)(2,1)S(1)} collective-permute-done((bf16[16,2048]{1,0:T(8,128)(2,1)S(1)}, bf16[16,2048]{1,0:T(8,128)(2,1)S(1)}, u32[]{:S(2)}, u32[]{:S(2)}) %collective-permute-start.20) | collective-permute-done | bytes 65568 | tf_op jit(solution)/shard_map/ppermute | solution.py:27
  65.9 0.7 %final.1 = f32[8,2,2048]{2,1,0:T(2,128)} custom-call(bf16[16,2048]{1,0:T(8,128)(2,1)S(1)} %output.1.refs_0_, bf16[16,2048]{1,0:T(8,128)(2,1)S(1)} %collective-permute-done.19.refs_1_, bf16[16,2048]{1,0:T(8,128)(2,1)S(1)} %collective-permute-done.20.refs_2_, bf16[16,2048]{1,0:T(8,128)(2,1)S(1)} %collective-permute-done.21.refs_3_, bf16[8,2,2048]{2,1,0:T(2,128)(2,1)S(1)} %copy-done), custom_call_target="tpu_custom_call" | custom-call | tf_op jit(solution)/shard_map/final/pallas_call | solution.py:721
  (28 shorter events, 3.4 us)
Async XLA Ops:
  0.7 11.5 %collective-permute-start.2 = (bf16[2,2,16,128]{3,2,1,0:T(8,128)(2,1)S(1)}, bf16[2,2,16,128]{3,2,1,0:T(8,128)(2,1)S(1)}, u32[]{:S(2)}, u32[]{:S(2)}) collective-permute-start(bf16[2,2,16,128]{3,2,1,0:T(8,128)(2,1)S(1)} %get-tuple-element.35.refs_0_), channel_id=1, source_target_pairs={{0,3},{1,2},{2,1},{3,0},{4,7},{5,6},{6,5},{7,4},{8,11},{9,10},{10,... | collective-permute-start | bytes 49160 | tf_op jit(solution)/shard_map/ppermute | solution.py:27
  5.9 6.3 %collective-permute-start.1 = (bf16[2,2,16,128]{3,2,1,0:T(8,128)(2,1)S(1)}, bf16[2,2,16,128]{3,2,1,0:T(8,128)(2,1)S(1)}, u32[]{:S(2)}, u32[]{:S(2)}) collective-permute-start(bf16[2,2,16,128]{3,2,1,0:T(8,128)(2,1)S(1)} %get-tuple-element.35.refs_0_), channel_id=1, source_target_pairs={{0,2},{1,3},{2,0},{3,1},{4,6},{5,7},{6,4},{7,5},{8,10},{9,11},{10,... | collective-permute-start | bytes 49160 | tf_op jit(solution)/shard_map/ppermute | solution.py:27
  5.9 6.4 %collective-permute-start = (bf16[2,2,16,128]{3,2,1,0:T(8,128)(2,1)S(1)}, bf16[2,2,16,128]{3,2,1,0:T(8,128)(2,1)S(1)}, u32[]{:S(2)}, u32[]{:S(2)}) collective-permute-start(bf16[2,2,16,128]{3,2,1,0:T(8,128)(2,1)S(1)} %get-tuple-element.35.refs_0_), channel_id=1, source_target_pairs={{0,1},{1,0},{2,3},{3,2},{4,5},{5,4},{6,7},{7,6},{8,9},{9,8},{10,11... | collective-permute-start | bytes 49160 | tf_op jit(solution)/shard_map/ppermute | solution.py:27
  12.3 5.6 %collective-permute-start.5 = (bf16[2,144,128]{2,1,0:T(8,128)(2,1)S(1)}, bf16[2,144,128]{2,1,0:T(8,128)(2,1)S(1)}, u32[]{:S(2)}, u32[]{:S(2)}) collective-permute-start(bf16[2,144,128]{2,1,0:T(8,128)(2,1)S(1)} %turned.1.after.refs_0_), channel_id=1, source_target_pairs={{0,12},{4,8},{8,4},{12,0},{1,13},{5,9},{9,5},{13,1},{2,14},{6,10},... | collective-permute-start | bytes 221192 | tf_op jit(solution)/shard_map/ppermute | solution.py:27
  12.8 5.7 %collective-permute-start.4 = (bf16[2,144,128]{2,1,0:T(8,128)(2,1)S(1)}, bf16[2,144,128]{2,1,0:T(8,128)(2,1)S(1)}, u32[]{:S(2)}, u32[]{:S(2)}) collective-permute-start(bf16[2,144,128]{2,1,0:T(8,128)(2,1)S(1)} %turned.1.after.refs_0_), channel_id=1, source_target_pairs={{0,8},{4,12},{8,0},{12,4},{1,9},{5,13},{9,1},{13,5},{2,10},{6,14},... | collective-permute-start | bytes 221192 | tf_op jit(solution)/shard_map/ppermute | solution.py:27
  14.1 4.4 %collective-permute-start.3 = (bf16[2,144,128]{2,1,0:T(8,128)(2,1)S(1)}, bf16[2,144,128]{2,1,0:T(8,128)(2,1)S(1)}, u32[]{:S(2)}, u32[]{:S(2)}) collective-permute-start(bf16[2,144,128]{2,1,0:T(8,128)(2,1)S(1)} %turned.1.after.refs_0_), channel_id=1, source_target_pairs={{0,4},{4,0},{8,12},{12,8},{1,5},{5,1},{9,13},{13,9},{2,6},{6,2},{1... | collective-permute-start | bytes 221192 | tf_op jit(solution)/shard_map/ppermute | solution.py:27
  20.3 6.8 %collective-permute-start.6 = (bf16[32,1024]{1,0:T(8,128)(2,1)S(1)}, bf16[32,1024]{1,0:T(8,128)(2,1)S(1)}, u32[]{:S(2)}, u32[]{:S(2)}) collective-permute-start(bf16[32,1024]{1,0:T(8,128)(2,1)S(1)} %get-tuple-element.47), channel_id=1, source_target_pairs={{0,3},{1,2},{2,1},{3,0},{4,7},{5,6},{6,5},{7,4},{8,11},{9,10},{10,... | collective-permute-start | bytes 196616 | tf_op jit(solution)/shard_map/ppermute | solution.py:27
  24.1 5.7 %collective-permute-start.7 = (bf16[32,1024]{1,0:T(8,128)(2,1)S(1)}, bf16[32,1024]{1,0:T(8,128)(2,1)S(1)}, u32[]{:S(2)}, u32[]{:S(2)}) collective-permute-start(bf16[32,1024]{1,0:T(8,128)(2,1)S(1)} %get-tuple-element.48), channel_id=1, source_target_pairs={{0,2},{1,3},{2,0},{3,1},{4,6},{5,7},{6,4},{7,5},{8,10},{9,11},{10,... | collective-permute-start | bytes 196616 | tf_op jit(solution)/shard_map/ppermute | solution.py:27
  24.1 5.7 %collective-permute-start.8 = (bf16[32,1024]{1,0:T(8,128)(2,1)S(1)}, bf16[32,1024]{1,0:T(8,128)(2,1)S(1)}, u32[]{:S(2)}, u32[]{:S(2)}) collective-permute-start(bf16[32,1024]{1,0:T(8,128)(2,1)S(1)} %get-tuple-element.49), channel_id=1, source_target_pairs={{0,1},{1,0},{2,3},{3,2},{4,5},{5,4},{6,7},{7,6},{8,9},{9,8},{10,11... | collective-permute-start | bytes 196616 | tf_op jit(solution)/shard_map/ppermute | solution.py:27
  30.7 7.0 %collective-permute-start.11 = (bf16[32,1152]{1,0:T(8,128)(2,1)S(1)}, bf16[32,1152]{1,0:T(8,128)(2,1)S(1)}, u32[]{:S(2)}, u32[]{:S(2)}) collective-permute-start(bf16[32,1152]{1,0:T(8,128)(2,1)S(1)} %weights.1.after.refs_0_.refs_4_), channel_id=1, source_target_pairs={{0,3},{1,2},{2,1},{3,0},{4,7},{5,6},{6,5},{7,4},{8,11},{9,10},{10,... | collective-permute-start | bytes 221192 | tf_op jit(solution)/shard_map/ppermute | solution.py:27
  33.0 7.3 %collective-permute-start.10 = (bf16[32,1152]{1,0:T(8,128)(2,1)S(1)}, bf16[32,1152]{1,0:T(8,128)(2,1)S(1)}, u32[]{:S(2)}, u32[]{:S(2)}) collective-permute-start(bf16[32,1152]{1,0:T(8,128)(2,1)S(1)} %weights.1.after.refs_0_.refs_4_), channel_id=1, source_target_pairs={{0,2},{1,3},{2,0},{3,1},{4,6},{5,7},{6,4},{7,5},{8,10},{9,11},{10,... | collective-permute-start | bytes 221192 | tf_op jit(solution)/shard_map/ppermute | solution.py:27
  33.4 6.9 %collective-permute-start.9 = (bf16[32,1152]{1,0:T(8,128)(2,1)S(1)}, bf16[32,1152]{1,0:T(8,128)(2,1)S(1)}, u32[]{:S(2)}, u32[]{:S(2)}) collective-permute-start(bf16[32,1152]{1,0:T(8,128)(2,1)S(1)} %weights.1.after.refs_0_.refs_4_), channel_id=1, source_target_pairs={{0,1},{1,0},{2,3},{3,2},{4,5},{5,4},{6,7},{7,6},{8,9},{9,8},{10,11... | collective-permute-start | bytes 221192 | tf_op jit(solution)/shard_map/ppermute | solution.py:27
  41.6 1.5 %collective-permute-start.12 = (bf16[5,128,128]{2,1,0:T(8,128)(2,1)S(1)}, bf16[5,128,128]{2,1,0:T(8,128)(2,1)S(1)}, u32[]{:S(2)}, u32[]{:S(2)}) collective-permute-start(bf16[5,128,128]{2,1,0:T(8,128)(2,1)S(1)} %get-tuple-element.55), channel_id=1, source_target_pairs={{0,4},{4,0},{8,12},{12,8},{1,5},{5,1},{9,13},{13,9},{2,6},{6,2},{1... | collective-permute-start | bytes 491528 | tf_op jit(solution)/shard_map/ppermute | solution.py:27
  43.5 5.9 %collective-permute-start.13 = (bf16[4,32,128]{2,1,0:T(8,128)(2,1)S(1)}, bf16[4,32,128]{2,1,0:T(8,128)(2,1)S(1)}, u32[]{:S(2)}, u32[]{:S(2)}) collective-permute-start(bf16[4,32,128]{2,1,0:T(8,128)(2,1)S(1)} %get-tuple-element.57), channel_id=1, source_target_pairs={{0,3},{1,2},{2,1},{3,0},{4,7},{5,6},{6,5},{7,4},{8,11},{9,10},{10,... | collective-permute-start | bytes 98312 | tf_op jit(solution)/shard_map/ppermute | solution.py:27
  45.5 4.9 %collective-permute-start.14 = (bf16[4,32,128]{2,1,0:T(8,128)(2,1)S(1)}, bf16[4,32,128]{2,1,0:T(8,128)(2,1)S(1)}, u32[]{:S(2)}, u32[]{:S(2)}) collective-permute-start(bf16[4,32,128]{2,1,0:T(8,128)(2,1)S(1)} %get-tuple-element.58), channel_id=1, source_target_pairs={{0,2},{1,3},{2,0},{3,1},{4,6},{5,7},{6,4},{7,5},{8,10},{9,11},{10,... | collective-permute-start | bytes 98312 | tf_op jit(solution)/shard_map/ppermute | solution.py:27
  45.5 4.9 %collective-permute-start.15 = (bf16[4,32,128]{2,1,0:T(8,128)(2,1)S(1)}, bf16[4,32,128]{2,1,0:T(8,128)(2,1)S(1)}, u32[]{:S(2)}, u32[]{:S(2)}) collective-permute-start(bf16[4,32,128]{2,1,0:T(8,128)(2,1)S(1)} %get-tuple-element.59), channel_id=1, source_target_pairs={{0,1},{1,0},{2,3},{3,2},{4,5},{5,4},{6,7},{7,6},{8,9},{9,8},{10,11... | collective-permute-start | bytes 98312 | tf_op jit(solution)/shard_map/ppermute | solution.py:27
  50.4 3.5 %collective-permute-start.18 = (bf16[5,32,128]{2,1,0:T(8,128)(2,1)S(1)}, bf16[5,32,128]{2,1,0:T(8,128)(2,1)S(1)}, u32[]{:S(2)}, u32[]{:S(2)}) collective-permute-start(bf16[5,32,128]{2,1,0:T(8,128)(2,1)S(1)} %summed.1.refs_0_), channel_id=1, source_target_pairs={{0,12},{4,8},{8,4},{12,0},{1,13},{5,9},{9,5},{13,1},{2,14},{6,10},... | collective-permute-start | bytes 122888 | tf_op jit(solution)/shard_map/ppermute | solution.py:27
  50.4 4.4 %collective-permute-start.17 = (bf16[5,32,128]{2,1,0:T(8,128)(2,1)S(1)}, bf16[5,32,128]{2,1,0:T(8,128)(2,1)S(1)}, u32[]{:S(2)}, u32[]{:S(2)}) collective-permute-start(bf16[5,32,128]{2,1,0:T(8,128)(2,1)S(1)} %summed.1.refs_0_), channel_id=1, source_target_pairs={{0,8},{4,12},{8,0},{12,4},{1,9},{5,13},{9,1},{13,5},{2,10},{6,14},... | collective-permute-start | bytes 122888 | tf_op jit(solution)/shard_map/ppermute | solution.py:27
  51.4 3.4 %collective-permute-start.16 = (bf16[5,32,128]{2,1,0:T(8,128)(2,1)S(1)}, bf16[5,32,128]{2,1,0:T(8,128)(2,1)S(1)}, u32[]{:S(2)}, u32[]{:S(2)}) collective-permute-start(bf16[5,32,128]{2,1,0:T(8,128)(2,1)S(1)} %summed.1.refs_0_), channel_id=1, source_target_pairs={{0,4},{4,0},{8,12},{12,8},{1,5},{5,1},{9,13},{13,9},{2,6},{6,2},{1... | collective-permute-start | bytes 122888 | tf_op jit(solution)/shard_map/ppermute | solution.py:27
  54.9 11.0 %copy-start = (bf16[8,2,2048]{2,1,0:T(2,128)(2,1)S(1)}, bf16[8,2,2048]{2,1,0:T(2,128)(2,1)}, u32[]{:S(2)}) copy-start(bf16[8,2,2048]{2,1,0:T(2,128)(2,1)} %refs_4_.1) | copy-start | bytes 196612
  56.5 6.8 %collective-permute-start.21 = (bf16[16,2048]{1,0:T(8,128)(2,1)S(1)}, bf16[16,2048]{1,0:T(8,128)(2,1)S(1)}, u32[]{:S(2)}, u32[]{:S(2)}) collective-permute-start(bf16[16,2048]{1,0:T(8,128)(2,1)S(1)} %output.1.refs_0_), channel_id=1, source_target_pairs={{0,3},{1,2},{2,1},{3,0},{4,7},{5,6},{6,5},{7,4},{8,11},{9,10},{10,... | collective-permute-start | bytes 196616 | tf_op jit(solution)/shard_map/ppermute | solution.py:27
  58.5 7.4 %collective-permute-start.20 = (bf16[16,2048]{1,0:T(8,128)(2,1)S(1)}, bf16[16,2048]{1,0:T(8,128)(2,1)S(1)}, u32[]{:S(2)}, u32[]{:S(2)}) collective-permute-start(bf16[16,2048]{1,0:T(8,128)(2,1)S(1)} %output.1.refs_0_), channel_id=1, source_target_pairs={{0,2},{1,3},{2,0},{3,1},{4,6},{5,7},{6,4},{7,5},{8,10},{9,11},{10,... | collective-permute-start | bytes 196616 | tf_op jit(solution)/shard_map/ppermute | solution.py:27
  59.5 6.3 %collective-permute-start.19 = (bf16[16,2048]{1,0:T(8,128)(2,1)S(1)}, bf16[16,2048]{1,0:T(8,128)(2,1)S(1)}, u32[]{:S(2)}, u32[]{:S(2)}) collective-permute-start(bf16[16,2048]{1,0:T(8,128)(2,1)S(1)} %output.1.refs_0_), channel_id=1, source_target_pairs={{0,1},{1,0},{2,3},{3,2},{4,5},{5,4},{6,7},{7,6},{8,9},{9,8},{10,11... | collective-permute-start | bytes 196616 | tf_op jit(solution)/shard_map/ppermute | solution.py:27

commit v13 on v10

--- a/solution.py
+++ b/solution.py
@@ -102,131 +102,113 @@
             sin_s[at] = sign * (sine * c + cosine * s)
 
 
-def pair_columns(w_ref, rows, pair, part):
+def pair_columns(w_ref, pair, part):
     at = [(2 * head + part) * HD for head in (2 * pair, 2 * pair + 1)]
-    return jnp.concatenate([w_ref[rows, c : c + HD] for c in at], axis=1)
-
-
-def copies_of(x_hbm, w_hbm, x_ref, w_ref, sems, first, size, count):
-    pairs_of = []
-    for i in range(count):
-        source, to = pl.ds(first + i * size, size), pl.ds(i * size, size)
-        x_copy = pltpu.make_async_copy(x_hbm.at[:, source], x_ref.at[:, to], sems.at[2 * i])
-        w_copy = pltpu.make_async_copy(w_hbm.at[source], w_ref.at[to], sems.at[2 * i + 1])
-        x_copy.start()
-        w_copy.start()
-        pairs_of.append((x_copy, w_copy))
-    return pairs_of
-
-
-def add_block(x_ref, w_ref, rows, acc, out, fresh):
+    return jnp.concatenate([w_ref[:, c : c + HD] for c in at], axis=1)
+
+
+def pair_keys(x_ref, w_ref, cos_ref, sin_ref, pair, rows, k_ref, column):
+    product = jnp.dot(x_ref[rows], pair_columns(w_ref, pair, 0), preferred_element_type=F32)
+    cosine, sine = cos_ref[rows], sin_ref[rows]
+    for h in range(2):
+        k = product[:, h * HD : (h + 1) * HD]
+        k = k * cosine + pltpu.roll(k, HD // 2, 1) * sine
+        k_ref[rows, column + h * HD : column + (h + 1) * HD] = k.astype(BF16)
+
+
+def load_kernel(pages, prompts, new_count, x_hbm, w_hbm, counts, tails, *refs):
+    k_ref, x_ref, w_ref, cos_ref, sin_ref, cos_q, sin_q, meta, x_sems, w_sems = refs
     tokens = x_ref.shape[0]
-    tall = tokens // 2
-    for pair in range(KVH // 2):
-        weight = pair_columns(w_ref, rows, pair, 0)
-        columns = slice(2 * pair * HD, 2 * (pair + 1) * HD)
-        for start in range(0, tokens, tall):
-            at = slice(start, start + tall)
-            product = jnp.dot(x_ref[at, rows], weight, preferred_element_type=F32)
-            out[at, columns] = product if fresh else acc[at, columns] + product
-
-
-def load_kernel(pages, prompts, new_count, x_hbm, w_hbm, counts, tails, *refs):
-    acc, x_ref, w_ref, cos_ref, sin_ref, cos_q, sin_q, meta, sems = refs
-    tokens = x_ref.shape[0]
-    size = x_ref.shape[1] // 3
-    copies = copies_of(x_hbm, w_hbm, x_ref, w_ref, sems, 0, size, 3)
+    tall, wide = tokens // 2, 4 * HD
+
+    def x_copy(i):
+        at = pl.ds(i * tall, tall)
+        return pltpu.make_async_copy(x_hbm.at[at], x_ref.at[at], x_sems.at[i])
+
+    def w_copy(pair):
+        at = pl.ds(pair * wide, wide)
+        return pltpu.make_async_copy(w_hbm.at[:, at], w_ref.at[:, at], w_sems.at[pair])
+
+    x_copy(0).start()
+    w_copy(0).start()
     page_table(pages, prompts, counts, tails, meta)
+    x_copy(1).start()
     rotation_tables(pages, tokens // PAGE, meta, cos_ref, sin_ref)
     spots = [meta[3 * pages + r] + n for r in range(prompts) for n in range(new_count)]
     angles = by_row(len(spots), spots) * lane_freqs(len(spots))
     cos_q[...] = jnp.cos(angles)
     sin_q[...] = jnp.sin(angles) * sine_sign(len(spots))
-    for i in range(2):
-        for copy in copies[i]:
-            copy.wait()
-        add_block(x_ref, w_ref, slice(i * size, (i + 1) * size), acc, acc, i == 0)
-    for copy in copies[2]:
-        copy.wait()
+    w_copy(1).start()
+    count = KVH // 2
+    for pair in range(count // 2):
+        w_copy(pair).wait()
+        if pair + 2 < count:
+            w_copy(pair + 2).start()
+        for i in range(2):
+            if pair == 0:
+                x_copy(i).wait()
+            rows = slice(i * tall, (i + 1) * tall)
+            pair_keys(x_ref, w_ref, cos_ref, sin_ref, pair, rows, k_ref, 2 * pair * HD)
+    for pair in range(count // 2, count):
+        w_copy(pair).wait()
 
 
 def load(x, kv_weight, counts, tails, pages, new_count):
     tokens, depth = x.shape
     columns = kv_weight.shape[1]
     prompts = counts.shape[0]
-    part = depth // 4 * 3
     hbm = pl.BlockSpec(memory_space=pltpu.HBM)
     return pl.pallas_call(
         functools.partial(load_kernel, pages, prompts, new_count),
         in_specs=[hbm, hbm, SMEM, SMEM],
         out_specs=[VMEM] * 7 + [SMEM],
         out_shape=[
-            pltpu.VMEM((tokens, KVH * HD), F32),
-            pltpu.VMEM((tokens, part), BF16),
-            pltpu.VMEM((part, columns), BF16),
+            pltpu.VMEM((tokens, KVH // 2 * HD), BF16),
+            pltpu.VMEM((tokens, depth), BF16),
+            pltpu.VMEM((depth, columns), BF16),
             pltpu.VMEM((tokens, HD), F32),
             pltpu.VMEM((tokens, HD), F32),
             pltpu.VMEM((prompts * new_count, HD), F32),
             pltpu.VMEM((prompts * new_count, HD), F32),
             jax.ShapeDtypeStruct((3 * pages + prompts,), jnp.int32),
         ],
-        scratch_shapes=[pltpu.SemaphoreType.DMA((6,))],
+        scratch_shapes=[pltpu.SemaphoreType.DMA((2,)), pltpu.SemaphoreType.DMA((KVH // 2,))],
         compiler_params=pltpu.CompilerParams(vmem_limit_bytes=28 * MIB),
         cost_estimate=pl.CostEstimate(
             flops=tokens * depth * KVH * HD,
-            bytes_accessed=2 * part * (tokens + columns),
+            bytes_accessed=2 * depth * (tokens + columns),
             transcendentals=0,
         ),
         name="load",
     )(*[in_hbm(a) for a in (x, kv_weight, counts, tails)])
 
 
-def keys_kernel(acc, xa_ref, wa_ref, x_hbm, w_hbm, cos_ref, sin_ref, after, k_ref, x_ref, w_ref, total, sems):
-    tokens, size = x_ref.shape
+def keys_kernel(x_ref, w_ref, cos_ref, sin_ref, after, k_ref):
+    tokens = x_ref.shape[0]
     tall = tokens // 2
-    ((x_copy, w_copy),) = copies_of(x_hbm, w_hbm, x_ref, w_ref, sems, 3 * size, size, 1)
-    add_block(xa_ref, wa_ref, slice(2 * size, 3 * size), acc, total, False)
-    x_copy.wait()
-    w_copy.wait()
-    for pair in range(KVH // 2):
-        weight = pair_columns(w_ref, slice(None), pair, 0)
-        columns = slice(2 * pair * HD, 2 * (pair + 1) * HD)
-        for start in range(0, tokens, tall):
-            at = slice(start, start + tall)
-            product = total[at, columns] + jnp.dot(x_ref[at], weight, preferred_element_type=F32)
-            cosine, sine = cos_ref[at], sin_ref[at]
-            for h in range(2):
-                k = product[:, h * HD : (h + 1) * HD]
-                k = k * cosine + pltpu.roll(k, HD // 2, 1) * sine
-                k_ref[at, (2 * pair + h) * HD : (2 * pair + h + 1) * HD] = k.astype(BF16)
-
-
-def rotated_keys(acc, xa, wa, x, kv_weight, cosine, sine, after):
+    for pair in range(KVH // 4, KVH // 2):
+        for i in range(2):
+            rows = slice(i * tall, (i + 1) * tall)
+            column = (2 * pair - KVH // 2) * HD
+            pair_keys(x_ref, w_ref, cos_ref, sin_ref, pair, rows, k_ref, column)
+
+
+def rotated_keys(x, weight, cosine, sine, after):
     tokens, depth = x.shape
-    columns = kv_weight.shape[1]
-    hbm = pl.BlockSpec(memory_space=pltpu.HBM)
     return pl.pallas_call(
         keys_kernel,
-        in_specs=[VMEM] * 3 + [hbm] * 2 + [VMEM] * 2 + [ANY],
-        out_specs=[VMEM] * 3,
-        out_shape=[
-            pltpu.VMEM((tokens, KVH * HD), BF16),
-            pltpu.VMEM((tokens, depth // 4), BF16),
-            pltpu.VMEM((depth // 4, columns), BF16),
-        ],
-        scratch_shapes=[
-            pltpu.VMEM((tokens, KVH * HD), F32),
-            pltpu.SemaphoreType.DMA((2,)),
-        ],
+        in_specs=[VMEM] * 4 + [ANY],
+        out_specs=VMEM,
+        out_shape=pltpu.VMEM((tokens, KVH // 2 * HD), BF16),
         compiler_params=pltpu.CompilerParams(vmem_limit_bytes=24 * MIB),
         cost_estimate=pl.CostEstimate(
             flops=tokens * depth * KVH * HD, bytes_accessed=8 * MIB, transcendentals=0
         ),
         name="keys",
-    )(acc, xa, wa, in_hbm(x), in_hbm(kv_weight), cosine, sine, after)
-
-
-def values_kernel(first, xa_ref, wa_ref, xb_ref, wb_ref, o_hbm, after, v_ref, o_ref, sem):
+    )(x, weight, cosine, sine, after)
+
+
+def values_kernel(first, x_ref, w_ref, o_hbm, after, v_ref, o_ref, sem):
     depth = o_ref.shape[0]
     copy = pltpu.make_async_copy(o_hbm.at[pl.ds(first * depth, depth)], o_ref, sem)
     copy.start()
@@ -234,22 +216,21 @@
     tall = tokens // 2
     pairs_here = columns // (2 * HD)
     for pair in range(pairs_here):
-        weights = [pair_columns(w, slice(None), first * pairs_here + pair, 1) for w in (wa_ref, wb_ref)]
+        weight = pair_columns(w_ref, first * pairs_here + pair, 1)
         for i in range(2):
             at = slice(i * tall, (i + 1) * tall)
-            product = jnp.dot(xa_ref[at], weights[0], preferred_element_type=F32)
-            product = product + jnp.dot(xb_ref[at], weights[1], preferred_element_type=F32)
+            product = jnp.dot(x_ref[at], weight, preferred_element_type=F32)
             v_ref[at, 2 * pair * HD : 2 * (pair + 1) * HD] = product.astype(BF16)
     copy.wait()
 
 
-def project_values(blocks, out_weight, first, after):
-    tokens, depth = blocks[0].shape
+def project_values(x, weight, out_weight, first, after):
+    tokens, depth = x.shape
     columns = KVH // 2 * HD
     rows = out_weight.shape[0] // 2
     return pl.pallas_call(
         functools.partial(values_kernel, first),
-        in_specs=[VMEM] * 4 + [pl.BlockSpec(memory_space=pltpu.HBM), ANY],
+        in_specs=[VMEM] * 2 + [pl.BlockSpec(memory_space=pltpu.HBM), ANY],
         out_specs=[VMEM, VMEM],
         out_shape=[
             pltpu.VMEM((tokens, columns), BF16),
@@ -261,7 +242,7 @@
             flops=2 * tokens * depth * columns, bytes_accessed=8 * MIB, transcendentals=0
         ),
         name="values",
-    )(*blocks, in_hbm(out_weight), after)
+    )(x, weight, in_hbm(out_weight), after)
 
 
 def by_heads(row):
@@ -340,11 +321,12 @@
 
 def scores_kernel(n_seq, n_tp, *refs):
     new = refs[:n_seq]
-    k_ref, meta = refs[n_seq : n_seq + 2]
-    outs = refs[n_seq + 2 : n_seq + 2 + n_tp]
-    all_q, ready = refs[n_seq + 2 + n_tp :]
+    ka_ref, kb_ref, meta = refs[n_seq : n_seq + 3]
+    outs = refs[n_seq + 3 : n_seq + 3 + n_tp]
+    all_q, ready = refs[n_seq + 3 + n_tp :]
     own_rows = new[0].shape[0]
-    local_pages = k_ref.shape[0] // PAGE
+    local_pages = ka_ref.shape[0] // PAGE
+    half = ka_ref.shape[1] // HD
     rows = all_q.shape[1] // KVH
     count = all_q.shape[1] // n_tp
     scale = 1.0 / math.sqrt(HD)
@@ -358,7 +340,8 @@
         request = meta[first + p]
         tokens = slice(p * PAGE, (p + 1) * PAGE)
         for head in range(KVH):
-            k = k_ref[tokens, head * HD : (head + 1) * HD]
+            k_ref = ka_ref if head < half else kb_ref
+            k = k_ref[tokens, head % half * HD : (head % half + 1) * HD]
             q = all_q[request, head * rows : (head + 1) * rows]
             s = lax.dot_general(q, k, (((1,), (1,)), ((), ())), preferred_element_type=F32)
             ready[head * rows : (head + 1) * rows, tokens] = (s * scale).astype(BF16)
@@ -366,14 +349,14 @@
         outs[d][...] = ready[pl.ds(pl.multiple_of(partner(me, d, n_tp) * count, count), count)]
 
 
-def partial_scores(new, k, meta, prompts, n_tp):
+def partial_scores(new, ka, kb, meta, prompts, n_tp):
     n_seq = len(new)
     all_rows = new[0].shape[1] - FRESH
-    tokens = k.shape[0]
+    tokens = ka.shape[0]
     rows = all_rows // n_tp
     return pl.pallas_call(
         functools.partial(scores_kernel, n_seq, n_tp),
-        in_specs=[VMEM] * (n_seq + 1) + [SMEM],
+        in_specs=[VMEM] * (n_seq + 2) + [SMEM],
         out_specs=[VMEM] * n_tp,
         out_shape=[jax.ShapeDtypeStruct((rows, tokens), BF16)] * n_tp,
         scratch_shapes=[
@@ -385,7 +368,7 @@
             flops=2 * tokens * all_rows * HD, bytes_accessed=6 * MIB, transcendentals=0
         ),
         name="scores",
-    )(*new, k, meta)
+    )(*new, ka, kb, meta)
 
 
 def fresh_kernel(n_seq, *refs):
@@ -664,16 +647,16 @@
     pages = prefill_states.shape[0] // PAGE * n_seq
     query, new_kv = prepare(new_query, new_keyval)
     query = gather(query, "tp")
-    acc, xa, wa, cosine, sine, cos_q, sin_q, meta = load(
+    ka, x, w, cosine, sine, cos_q, sin_q, meta = load(
         prefill_states, kv_weight, page_counts, tail_tokens, pages, new_count
     )
     new = turned(query, new_kv, cos_q, sin_q)
-    k, xb, wb = rotated_keys(acc, xa, wa, prefill_states, kv_weight, cosine, sine, new)
+    kb = rotated_keys(x, w, cosine, sine, new)
     new = gather(new, "seq")
-    scores = partial_scores(new, k, meta, prompts, n_tp)
-    va, oa = project_values((xa, wa, xb, wb), out_weight, 0, scores[0])
+    scores = partial_scores(new, ka, kb, meta, prompts, n_tp)
+    va, oa = project_values(x, w, out_weight, 0, scores[0])
     weights, stats = softmax_weights(exchange(scores, "tp"), meta, va, pages, prompts)
-    vb, ob = project_values((xa, wa, xb, wb), out_weight, 1, stats)
+    vb, ob = project_values(x, w, out_weight, 1, stats)
     fresh, values = fresh_scores(new, stats, prompts, new_count, n_tp)
     chunks = weighted_values(gather(weights, "tp"), va, vb, meta, prompts)
     pieces = gather(summed(exchange(chunks, "tp"), stats), "seq")

time: 66.4 us -> 68.5 us (1.032)
  Pallas kernels: 21.2 us -> 22.3 us
  waiting for transfers between devices: 17.4 us -> 18.4 us
    pallas_call x1, Pallas kernels: 5.68 us -> 7.75 us  [load(): pl.pallas_call(functools.partial(load_kernel, pages, prompts, new_count),...]
    pallas_call x1, Pallas kernels: 3.62 us -> 2.59 us  [rotated_keys(): pl.pallas_call(keys_kernel, in_specs=[VMEM] * 4 + [ANY], out_specs=VMEM,...]
    ppermute x21, waiting for transfers between devices: 17.4 us -> 18.4 us  [pairs(): lax.ppermute(value, axis, [(i, partner(i, entry, size)) for i in range(si...]
  transfers between devices with their start and end apart: 21 -> 21, of which waited for: 9 -> 9; matrix products, arithmetic and copies ran while one was open for 0% -> 0% of each run, Pallas kernels for 21% -> 22%
where the time goes in v13:
time: 68.5 us; the launch traced here: 68.2 us
  starting transfers between devices  27.3 us (40%)
  Pallas kernels  22.3 us (33%)
  waiting for transfers between devices  18.4 us (27%)
    ppermute x21, starting transfers between devices, pairs(): lax.ppermute(value, axis, [(i, partner(i, entry, size)) for i in range(si...  27.3 us
    ppermute x21, waiting for transfers between devices, pairs(): lax.ppermute(value, axis, [(i, partner(i, entry, size)) for i in range(si...  18.4 us
    pallas_call x1, Pallas kernels, load(): pl.pallas_call(functools.partial(load_kernel, pages, prompts, new_count),...  7.75 us
    pallas_call x2, Pallas kernels, project_values(): pl.pallas_call(functools.partial(values_kernel, first), in_specs=[VMEM] *...  4.75 us
    pallas_call x1, Pallas kernels, rotated_keys(): pl.pallas_call(keys_kernel, in_specs=[VMEM] * 4 + [ANY], out_specs=VMEM,...  2.59 us
    pallas_call x1, Pallas kernels, partial_scores(): pl.pallas_call(functools.partial(scores_kernel, n_seq, n_tp), in_specs=[V...  1.76 us
    pallas_call x1, Pallas kernels, output_partial(): pl.pallas_call(functools.partial(output_kernel, n_seq), in_specs=[VMEM] *...  1.58 us
  transfers between devices with their start and end apart: 21, of which 9 were waited for; matrix products, arithmetic and copies ran while one was open for 0% of the time, Pallas kernels for 22%

profile of v13, /device:TPU:0, one launch (start us, length us, event | category | flops | bytes accessed | tf_op | source)
XLA Modules:
  0.0 68.2 jit_solution(13564786860195409440)
XLA Ops:
  0.0 0.7 %prepare.1 = (bf16[2,2,16,128]{3,2,1,0:T(8,128)(2,1)S(1)}, f32[2,2,4,128]{3,2,1,0:T(4,128)S(1)}) custom-call(bf16[2,2,2048]{2,1,0:T(2,128)(2,1)} %q_ref.1, bf16[2,2,512]{2,1,0:T(2,128)(2,1)} %kv_ref.1), custom_call_target="tpu_custom_call" | custom-call | bytes 1048576 | tf_op jit(solution)/shard_map/prepare/pallas_call | solution.py:263
  0.7 5.1 %collective-permute-start.2 = (bf16[2,2,16,128]{3,2,1,0:T(8,128)(2,1)S(1)}, bf16[2,2,16,128]{3,2,1,0:T(8,128)(2,1)S(1)}, u32[]{:S(2)}, u32[]{:S(2)}) collective-permute-start(bf16[2,2,16,128]{3,2,1,0:T(8,128)(2,1)S(1)} %get-tuple-element.31.refs_0_), channel_id=1, source_target_pairs={{0,3},{1,2},{2,1},{3,0},{4,7},{5,6},{6,5},{7,4},{8,11},{9,10},{10,... | collective-permute-start | bytes 49160 | tf_op jit(solution)/shard_map/ppermute | solution.py:32
  5.9 0.6 collective-permute-start
  6.5 7.7 %load.1 = (bf16[1024,512]{1,0:T(8,128)(2,1)S(1)}, bf16[1024,2048]{1,0:T(8,128)(2,1)S(1)}, bf16[2048,2048]{1,0:T(8,128)(2,1)S(1)}, f32[1024,128]{1,0:T(8,128)S(1)...) custom-call(bf16[1024,2048]{1,0:T(8,128)(2,1)} %x_hbm.1, ...), custom_call_target="tpu_custom_call" | custom-call | flops 2147483648 | bytes 12582912 | tf_op jit(solution)/shard_map/load/pallas_call | solution.py:161
  14.9 1.3 %collective-permute-start.4 = (bf16[2,144,128]{2,1,0:T(8,128)(2,1)S(1)}, bf16[2,144,128]{2,1,0:T(8,128)(2,1)S(1)}, u32[]{:S(2)}, u32[]{:S(2)}) collective-permute-start(bf16[2,144,128]{2,1,0:T(8,128)(2,1)S(1)} %turned.1.after.refs_0_), channel_id=1, source_target_pairs={{0,8},{4,12},{8,0},{12,4},{1,9},{5,13},{9,1},{13,5},{2,10},{6,14},... | collective-permute-start | bytes 221192 | tf_op jit(solution)/shard_map/ppermute | solution.py:32
  16.3 2.6 %keys.1.refs_5_ = bf16[1024,512]{1,0:T(8,128)(2,1)S(1)} custom-call(bf16[1024,2048]{1,0:T(8,128)(2,1)S(1)} %get-tuple-element.36.x_ref, bf16[2048,2048]{1,0:T(8,128)(2,1)S(1)} %get-tuple-element.37.w_ref, f32[1024,128]{1,0:T(8,128)S(1)} %get-tuple-element.38.cos_ref, f32[1024,128]{1,0:T(8,128)S(1)} %get-tuple-element.39.sin_ref, ...), custom_call_target="tpu_custom_call" | custom-call | flops 2147483648 | bytes 8388608 | tf_op jit(solution)/shard_map/keys/pallas_call | solution.py:198
  19.0 1.7 %collective-permute-done.4.refs_2_ = bf16[2,144,128]{2,1,0:T(8,128)(2,1)S(1)} collective-permute-done((bf16[2,144,128]{2,1,0:T(8,128)(2,1)S(1)}, bf16[2,144,128]{2,1,0:T(8,128)(2,1)S(1)}, u32[]{:S(2)}, u32[]{:S(2)}) %collective-permute-start.4) | collective-permute-done | bytes 73760 | tf_op jit(solution)/shard_map/ppermute | solution.py:32
  20.6 1.8 %scores.1 = (bf16[32,1024]{1,0:T(8,128)(2,1)S(1)}, bf16[32,1024]{1,0:T(8,128)(2,1)S(1)}, bf16[32,1024]{1,0:T(8,128)(2,1)S(1)}, bf16[32,1024]{1,0:T(8,128)(2,1)S(1)}) custom-call(bf16[2,144,128]{2,1,0:T(8,128)(2,1)S(1)} %turned.1.after.refs_0_, bf16[2,144,128]{2,1,0:T(8,128)(2,1)S(1)} %collective-permute-done.3.refs_1_, ...), custom_call_target="tpu_custom_call" | custom-call | flops 33554432 | bytes 6291456 | tf_op jit(solution)/shard_map/scores/pallas_call | solution.py:357
  22.4 3.8 %collective-permute-start.6 = (bf16[32,1024]{1,0:T(8,128)(2,1)S(1)}, bf16[32,1024]{1,0:T(8,128)(2,1)S(1)}, u32[]{:S(2)}, u32[]{:S(2)}) collective-permute-start(bf16[32,1024]{1,0:T(8,128)(2,1)S(1)} %get-tuple-element.42), channel_id=1, source_target_pairs={{0,3},{1,2},{2,1},{3,0},{4,7},{5,6},{6,5},{7,4},{8,11},{9,10},{10,... | collective-permute-start | bytes 196616 | tf_op jit(solution)/shard_map/ppermute | solution.py:32
  26.2 0.6 collective-permute-start.8
  26.8 2.4 %values.2 = (bf16[1024,512]{1,0:T(8,128)(2,1)S(1)}, bf16[1024,2048]{1,0:T(8,128)(2,1)S(1)}) custom-call(bf16[1024,2048]{1,0:T(8,128)(2,1)S(1)} %get-tuple-element.36.x_ref, bf16[2048,2048]{1,0:T(8,128)(2,1)S(1)} %get-tuple-element.37.w_ref, bf16[2048,2048]{1,0:T(8,128)(2,1)} %o_hbm.3, bf16[32,1024]{1,0:T(8,128)(2,1)S(1)} %get-tuple-element.41.after.refs_0_), custom_call_target="tpu_custom_call" | custom-call | flops 2147483648 | bytes 8388608 | tf_op jit(solution)/shard_map/values/pallas_call | solution.py:231
  29.2 2.6 %collective-permute-done.7.refs_2_ = bf16[32,1024]{1,0:T(8,128)(2,1)S(1)} collective-permute-done((bf16[32,1024]{1,0:T(8,128)(2,1)S(1)}, bf16[32,1024]{1,0:T(8,128)(2,1)S(1)}, u32[]{:S(2)}, u32[]{:S(2)}) %collective-permute-start.7) | collective-permute-done | bytes 65568 | tf_op jit(solution)/shard_map/ppermute | solution.py:32
  31.9 0.9 %weights.1 = (bf16[32,1024]{1,0:T(8,128)(2,1)S(1)}, bf16[32,128]{1,0:T(8,128)(2,1)S(1)}) custom-call(bf16[32,1024]{1,0:T(8,128)(2,1)S(1)} %get-tuple-element.41.after.refs_0_, bf16[32,1024]{1,0:T(8,128)(2,1)S(1)} %collective-permute-done.6.refs_1_, bf16[32,1024]{1,0:T(8,128)(2,1)S(1)} %collective-permute-done.7.refs_2_, ...), custom_call_target="tpu_custom_call" | custom-call | tf_op jit(solution)/shard_map/weights/pallas_call | solution.py:468
  32.8 2.3 %collective-permute-start.11 = (bf16[32,1024]{1,0:T(8,128)(2,1)S(1)}, bf16[32,1024]{1,0:T(8,128)(2,1)S(1)}, u32[]{:S(2)}, u32[]{:S(2)}) collective-permute-start(bf16[32,1024]{1,0:T(8,128)(2,1)S(1)} %get-tuple-element.46.refs_0_), channel_id=1, source_target_pairs={{0,3},{1,2},{2,1},{3,0},{4,7},{5,6},{6,5},{7,4},{8,11},{9,10},{10,... | collective-permute-start | bytes 196616 | tf_op jit(solution)/shard_map/ppermute | solution.py:32
  35.5 1.7 %collective-permute-start.9 = (bf16[32,1024]{1,0:T(8,128)(2,1)S(1)}, bf16[32,1024]{1,0:T(8,128)(2,1)S(1)}, u32[]{:S(2)}, u32[]{:S(2)}) collective-permute-start(bf16[32,1024]{1,0:T(8,128)(2,1)S(1)} %get-tuple-element.46.refs_0_), channel_id=1, source_target_pairs={{0,1},{1,0},{2,3},{3,2},{4,5},{5,4},{6,7},{7,6},{8,9},{9,8},{10,11... | collective-permute-start | bytes 196616 | tf_op jit(solution)/shard_map/ppermute | solution.py:32
  37.2 2.4 %values.3 = (bf16[1024,512]{1,0:T(8,128)(2,1)S(1)}, bf16[1024,2048]{1,0:T(8,128)(2,1)S(1)}) custom-call(bf16[1024,2048]{1,0:T(8,128)(2,1)S(1)} %get-tuple-element.36.x_ref, bf16[2048,2048]{1,0:T(8,128)(2,1)S(1)} %get-tuple-element.37.w_ref, bf16[2048,2048]{1,0:T(8,128)(2,1)} %o_hbm.3, bf16[32,128]{1,0:T(8,128)(2,1)S(1)} %get-tuple-element.47.after.refs_4_), custom_call_target="tpu_custom_call" | custom-call | flops 2147483648 | bytes 8388608 | tf_op jit(solution)/shard_map/values/pallas_call | solution.py:231
  39.6 2.2 %collective-permute-done.10.refs_2_ = bf16[32,1024]{1,0:T(8,128)(2,1)S(1)} collective-permute-done((bf16[32,1024]{1,0:T(8,128)(2,1)S(1)}, bf16[32,1024]{1,0:T(8,128)(2,1)S(1)}, u32[]{:S(2)}, u32[]{:S(2)}) %collective-permute-start.10) | collective-permute-done | bytes 65568 | tf_op jit(solution)/shard_map/ppermute | solution.py:32
  41.8 1.3 %weighted.1 = (bf16[8,32,128]{2,1,0:T(8,128)(2,1)S(1)}, bf16[8,32,128]{2,1,0:T(8,128)(2,1)S(1)}, bf16[8,32,128]{2,1,0:T(8,128)(2,1)S(1)}, bf16[8,32,128]{2,1,0:T(8,128)(2,1)S(1)}) custom-call(bf16[32,1024]{1,0:T(8,128)(2,1)S(1)} %get-tuple-element.46.refs_0_, bf16[32,1024]{1,0:T(8,128)(2,1)S(1)} %collective-permute-done.9.refs_1_, ...), custom_call_target="tpu_custom_call" | custom-call | flops 33554432 | bytes 8388608 | tf_op jit(solution)/shard_map/weighted/pallas_call | solution.py:513
  43.1 2.0 %collective-permute-start.12 = (bf16[8,32,128]{2,1,0:T(8,128)(2,1)S(1)}, bf16[8,32,128]{2,1,0:T(8,128)(2,1)S(1)}, u32[]{:S(2)}, u32[]{:S(2)}) collective-permute-start(bf16[8,32,128]{2,1,0:T(8,128)(2,1)S(1)} %get-tuple-element.50), channel_id=1, source_target_pairs={{0,3},{1,2},{2,1},{3,0},{4,7},{5,6},{6,5},{7,4},{8,11},{9,10},{10,... | collective-permute-start | bytes 196616 | tf_op jit(solution)/shard_map/ppermute | solution.py:32
  45.0 2.5 %collective-permute-start.14 = (bf16[8,32,128]{2,1,0:T(8,128)(2,1)S(1)}, bf16[8,32,128]{2,1,0:T(8,128)(2,1)S(1)}, u32[]{:S(2)}, u32[]{:S(2)}) collective-permute-start(bf16[8,32,128]{2,1,0:T(8,128)(2,1)S(1)} %get-tuple-element.52), channel_id=1, source_target_pairs={{0,1},{1,0},{2,3},{3,2},{4,5},{5,4},{6,7},{7,6},{8,9},{9,8},{10,11... | collective-permute-start | bytes 196616 | tf_op jit(solution)/shard_map/ppermute | solution.py:32
  47.5 2.0 %collective-permute-done.12.refs_1_ = bf16[8,32,128]{2,1,0:T(8,128)(2,1)S(1)} collective-permute-done((bf16[8,32,128]{2,1,0:T(8,128)(2,1)S(1)}, bf16[8,32,128]{2,1,0:T(8,128)(2,1)S(1)}, u32[]{:S(2)}, u32[]{:S(2)}) %collective-permute-start.12) | collective-permute-done | bytes 65568 | tf_op jit(solution)/shard_map/ppermute | solution.py:32
  49.5 1.7 %collective-permute-done.13.refs_2_ = bf16[8,32,128]{2,1,0:T(8,128)(2,1)S(1)} collective-permute-done((bf16[8,32,128]{2,1,0:T(8,128)(2,1)S(1)}, bf16[8,32,128]{2,1,0:T(8,128)(2,1)S(1)}, u32[]{:S(2)}, u32[]{:S(2)}) %collective-permute-start.13) | collective-permute-done | bytes 65568 | tf_op jit(solution)/shard_map/ppermute | solution.py:32
  51.3 1.3 %collective-permute-start.16 = (bf16[9,32,128]{2,1,0:T(8,128)(2,1)S(1)}, bf16[9,32,128]{2,1,0:T(8,128)(2,1)S(1)}, u32[]{:S(2)}, u32[]{:S(2)}) collective-permute-start(bf16[9,32,128]{2,1,0:T(8,128)(2,1)S(1)} %summed.1.refs_0_), channel_id=1, source_target_pairs={{0,8},{4,12},{8,0},{12,4},{1,9},{5,13},{9,1},{13,5},{2,10},{6,14},... | collective-permute-start | bytes 221192 | tf_op jit(solution)/shard_map/ppermute | solution.py:32
  52.6 0.6 collective-permute-start.15
  53.3 2.6 %collective-permute-done.17.refs_3_ = bf16[9,32,128]{2,1,0:T(8,128)(2,1)S(1)} collective-permute-done((bf16[9,32,128]{2,1,0:T(8,128)(2,1)S(1)}, bf16[9,32,128]{2,1,0:T(8,128)(2,1)S(1)}, u32[]{:S(2)}, u32[]{:S(2)}) %collective-permute-start.17) | collective-permute-done | bytes 73760 | tf_op jit(solution)/shard_map/ppermute | solution.py:32
  55.9 1.3 %collective-permute-done.16.refs_2_ = bf16[9,32,128]{2,1,0:T(8,128)(2,1)S(1)} collective-permute-done((bf16[9,32,128]{2,1,0:T(8,128)(2,1)S(1)}, bf16[9,32,128]{2,1,0:T(8,128)(2,1)S(1)}, u32[]{:S(2)}, u32[]{:S(2)}) %collective-permute-start.16) | collective-permute-done | bytes 73760 | tf_op jit(solution)/shard_map/ppermute | solution.py:32
  57.2 1.6 %output.1.refs_0_ = bf16[16,2048]{1,0:T(8,128)(2,1)S(1)} custom-call(bf16[9,32,128]{2,1,0:T(8,128)(2,1)S(1)} %summed.1.refs_0_, bf16[9,32,128]{2,1,0:T(8,128)(2,1)S(1)} %collective-permute-done.15.refs_1_, bf16[9,32,128]{2,1,0:T(8,128)(2,1)S(1)} %collective-permute-done.16.refs_2_, bf16[9,32,128]{2,1,0:T(8,128)(2,1)S(1)} %collective-permute-done.17.refs_3_, ...), custom_call_target="tpu_custom_call" | custom-call | tf_op jit(solution)/shard_map/output/pallas_call | solution.py:607
  58.7 2.2 %collective-permute-start.20 = (bf16[16,2048]{1,0:T(8,128)(2,1)S(1)}, bf16[16,2048]{1,0:T(8,128)(2,1)S(1)}, u32[]{:S(2)}, u32[]{:S(2)}) collective-permute-start(bf16[16,2048]{1,0:T(8,128)(2,1)S(1)} %output.1.refs_0_), channel_id=1, source_target_pairs={{0,3},{1,2},{2,1},{3,0},{4,7},{5,6},{6,5},{7,4},{8,11},{9,10},{10,... | collective-permute-start | bytes 196616 | tf_op jit(solution)/shard_map/ppermute | solution.py:32
  61.0 2.2 %collective-permute-start.18 = (bf16[16,2048]{1,0:T(8,128)(2,1)S(1)}, bf16[16,2048]{1,0:T(8,128)(2,1)S(1)}, u32[]{:S(2)}, u32[]{:S(2)}) collective-permute-start(bf16[16,2048]{1,0:T(8,128)(2,1)S(1)} %output.1.refs_0_), channel_id=1, source_target_pairs={{0,1},{1,0},{2,3},{3,2},{4,5},{5,4},{6,7},{7,6},{8,9},{9,8},{10,11... | collective-permute-start | bytes 196616 | tf_op jit(solution)/shard_map/ppermute | solution.py:32
  63.1 2.3 %collective-permute-done.20.refs_3_ = bf16[16,2048]{1,0:T(8,128)(2,1)S(1)} collective-permute-done((bf16[16,2048]{1,0:T(8,128)(2,1)S(1)}, bf16[16,2048]{1,0:T(8,128)(2,1)S(1)}, u32[]{:S(2)}, u32[]{:S(2)}) %collective-permute-start.20) | collective-permute-done | bytes 65568 | tf_op jit(solution)/shard_map/ppermute | solution.py:32
  65.5 2.0 %collective-permute-done.19.refs_2_ = bf16[16,2048]{1,0:T(8,128)(2,1)S(1)} collective-permute-done((bf16[16,2048]{1,0:T(8,128)(2,1)S(1)}, bf16[16,2048]{1,0:T(8,128)(2,1)S(1)}, u32[]{:S(2)}, u32[]{:S(2)}) %collective-permute-start.19) | collective-permute-done | bytes 65568 | tf_op jit(solution)/shard_map/ppermute | solution.py:32
  67.5 0.7 %final.1 = f32[8,2,2048]{2,1,0:T(2,128)} custom-call(bf16[16,2048]{1,0:T(8,128)(2,1)S(1)} %output.1.refs_0_, bf16[16,2048]{1,0:T(8,128)(2,1)S(1)} %collective-permute-done.18.refs_1_, bf16[16,2048]{1,0:T(8,128)(2,1)S(1)} %collective-permute-done.19.refs_2_, bf16[16,2048]{1,0:T(8,128)(2,1)S(1)} %collective-permute-done.20.refs_3_, bf16[8,2,2048]{2,1,0:T(2,128)(2,1)S(1)} %copy-done), custom_call_target="tpu_custom_call" | custom-call | tf_op jit(solution)/shard_map/final/pallas_call | solution.py:631
  (25 shorter events, 1.4 us)
Async XLA Ops:
  0.7 13.5 %collective-permute-start.2 = (bf16[2,2,16,128]{3,2,1,0:T(8,128)(2,1)S(1)}, bf16[2,2,16,128]{3,2,1,0:T(8,128)(2,1)S(1)}, u32[]{:S(2)}, u32[]{:S(2)}) collective-permute-start(bf16[2,2,16,128]{3,2,1,0:T(8,128)(2,1)S(1)} %get-tuple-element.31.refs_0_), channel_id=1, source_target_pairs={{0,3},{1,2},{2,1},{3,0},{4,7},{5,6},{6,5},{7,4},{8,11},{9,10},{10,... | collective-permute-start | bytes 49160 | tf_op jit(solution)/shard_map/ppermute | solution.py:32
  5.9 8.4 %collective-permute-start.1 = (bf16[2,2,16,128]{3,2,1,0:T(8,128)(2,1)S(1)}, bf16[2,2,16,128]{3,2,1,0:T(8,128)(2,1)S(1)}, u32[]{:S(2)}, u32[]{:S(2)}) collective-permute-start(bf16[2,2,16,128]{3,2,1,0:T(8,128)(2,1)S(1)} %get-tuple-element.31.refs_0_), channel_id=1, source_target_pairs={{0,2},{1,3},{2,0},{3,1},{4,6},{5,7},{6,4},{7,5},{8,10},{9,11},{10,... | collective-permute-start | bytes 49160 | tf_op jit(solution)/shard_map/ppermute | solution.py:32
  5.9 8.4 %collective-permute-start = (bf16[2,2,16,128]{3,2,1,0:T(8,128)(2,1)S(1)}, bf16[2,2,16,128]{3,2,1,0:T(8,128)(2,1)S(1)}, u32[]{:S(2)}, u32[]{:S(2)}) collective-permute-start(bf16[2,2,16,128]{3,2,1,0:T(8,128)(2,1)S(1)} %get-tuple-element.31.refs_0_), channel_id=1, source_target_pairs={{0,1},{1,0},{2,3},{3,2},{4,5},{5,4},{6,7},{7,6},{8,9},{9,8},{10,11... | collective-permute-start | bytes 49160 | tf_op jit(solution)/shard_map/ppermute | solution.py:32
  14.4 4.6 %collective-permute-start.5 = (bf16[2,144,128]{2,1,0:T(8,128)(2,1)S(1)}, bf16[2,144,128]{2,1,0:T(8,128)(2,1)S(1)}, u32[]{:S(2)}, u32[]{:S(2)}) collective-permute-start(bf16[2,144,128]{2,1,0:T(8,128)(2,1)S(1)} %turned.1.after.refs_0_), channel_id=1, source_target_pairs={{0,12},{4,8},{8,4},{12,0},{1,13},{5,9},{9,5},{13,1},{2,14},{6,10},... | collective-permute-start | bytes 221192 | tf_op jit(solution)/shard_map/ppermute | solution.py:32
  14.9 5.7 %collective-permute-start.4 = (bf16[2,144,128]{2,1,0:T(8,128)(2,1)S(1)}, bf16[2,144,128]{2,1,0:T(8,128)(2,1)S(1)}, u32[]{:S(2)}, u32[]{:S(2)}) collective-permute-start(bf16[2,144,128]{2,1,0:T(8,128)(2,1)S(1)} %turned.1.after.refs_0_), channel_id=1, source_target_pairs={{0,8},{4,12},{8,0},{12,4},{1,9},{5,13},{9,1},{13,5},{2,10},{6,14},... | collective-permute-start | bytes 221192 | tf_op jit(solution)/shard_map/ppermute | solution.py:32
  16.2 4.4 %collective-permute-start.3 = (bf16[2,144,128]{2,1,0:T(8,128)(2,1)S(1)}, bf16[2,144,128]{2,1,0:T(8,128)(2,1)S(1)}, u32[]{:S(2)}, u32[]{:S(2)}) collective-permute-start(bf16[2,144,128]{2,1,0:T(8,128)(2,1)S(1)} %turned.1.after.refs_0_), channel_id=1, source_target_pairs={{0,4},{4,0},{8,12},{12,8},{1,5},{5,1},{9,13},{13,9},{2,6},{6,2},{1... | collective-permute-start | bytes 221192 | tf_op jit(solution)/shard_map/ppermute | solution.py:32
  22.4 6.8 %collective-permute-start.6 = (bf16[32,1024]{1,0:T(8,128)(2,1)S(1)}, bf16[32,1024]{1,0:T(8,128)(2,1)S(1)}, u32[]{:S(2)}, u32[]{:S(2)}) collective-permute-start(bf16[32,1024]{1,0:T(8,128)(2,1)S(1)} %get-tuple-element.42), channel_id=1, source_target_pairs={{0,3},{1,2},{2,1},{3,0},{4,7},{5,6},{6,5},{7,4},{8,11},{9,10},{10,... | collective-permute-start | bytes 196616 | tf_op jit(solution)/shard_map/ppermute | solution.py:32
  26.2 5.7 %collective-permute-start.7 = (bf16[32,1024]{1,0:T(8,128)(2,1)S(1)}, bf16[32,1024]{1,0:T(8,128)(2,1)S(1)}, u32[]{:S(2)}, u32[]{:S(2)}) collective-permute-start(bf16[32,1024]{1,0:T(8,128)(2,1)S(1)} %get-tuple-element.43), channel_id=1, source_target_pairs={{0,2},{1,3},{2,0},{3,1},{4,6},{5,7},{6,4},{7,5},{8,10},{9,11},{10,... | collective-permute-start | bytes 196616 | tf_op jit(solution)/shard_map/ppermute | solution.py:32
  26.2 5.7 %collective-permute-start.8 = (bf16[32,1024]{1,0:T(8,128)(2,1)S(1)}, bf16[32,1024]{1,0:T(8,128)(2,1)S(1)}, u32[]{:S(2)}, u32[]{:S(2)}) collective-permute-start(bf16[32,1024]{1,0:T(8,128)(2,1)S(1)} %get-tuple-element.44), channel_id=1, source_target_pairs={{0,1},{1,0},{2,3},{3,2},{4,5},{5,4},{6,7},{7,6},{8,9},{9,8},{10,11... | collective-permute-start | bytes 196616 | tf_op jit(solution)/shard_map/ppermute | solution.py:32
  32.8 6.8 %collective-permute-start.11 = (bf16[32,1024]{1,0:T(8,128)(2,1)S(1)}, bf16[32,1024]{1,0:T(8,128)(2,1)S(1)}, u32[]{:S(2)}, u32[]{:S(2)}) collective-permute-start(bf16[32,1024]{1,0:T(8,128)(2,1)S(1)} %get-tuple-element.46.refs_0_), channel_id=1, source_target_pairs={{0,3},{1,2},{2,1},{3,0},{4,7},{5,6},{6,5},{7,4},{8,11},{9,10},{10,... | collective-permute-start | bytes 196616 | tf_op jit(solution)/shard_map/ppermute | solution.py:32
  35.1 6.7 %collective-permute-start.10 = (bf16[32,1024]{1,0:T(8,128)(2,1)S(1)}, bf16[32,1024]{1,0:T(8,128)(2,1)S(1)}, u32[]{:S(2)}, u32[]{:S(2)}) collective-permute-start(bf16[32,1024]{1,0:T(8,128)(2,1)S(1)} %get-tuple-element.46.refs_0_), channel_id=1, source_target_pairs={{0,2},{1,3},{2,0},{3,1},{4,6},{5,7},{6,4},{7,5},{8,10},{9,11},{10,... | collective-permute-start | bytes 196616 | tf_op jit(solution)/shard_map/ppermute | solution.py:32
  35.5 6.3 %collective-permute-start.9 = (bf16[32,1024]{1,0:T(8,128)(2,1)S(1)}, bf16[32,1024]{1,0:T(8,128)(2,1)S(1)}, u32[]{:S(2)}, u32[]{:S(2)}) collective-permute-start(bf16[32,1024]{1,0:T(8,128)(2,1)S(1)} %get-tuple-element.46.refs_0_), channel_id=1, source_target_pairs={{0,1},{1,0},{2,3},{3,2},{4,5},{5,4},{6,7},{7,6},{8,9},{9,8},{10,11... | collective-permute-start | bytes 196616 | tf_op jit(solution)/shard_map/ppermute | solution.py:32
  43.1 6.4 %collective-permute-start.12 = (bf16[8,32,128]{2,1,0:T(8,128)(2,1)S(1)}, bf16[8,32,128]{2,1,0:T(8,128)(2,1)S(1)}, u32[]{:S(2)}, u32[]{:S(2)}) collective-permute-start(bf16[8,32,128]{2,1,0:T(8,128)(2,1)S(1)} %get-tuple-element.50), channel_id=1, source_target_pairs={{0,3},{1,2},{2,1},{3,0},{4,7},{5,6},{6,5},{7,4},{8,11},{9,10},{10,... | collective-permute-start | bytes 196616 | tf_op jit(solution)/shard_map/ppermute | solution.py:32
  45.0 6.2 %collective-permute-start.13 = (bf16[8,32,128]{2,1,0:T(8,128)(2,1)S(1)}, bf16[8,32,128]{2,1,0:T(8,128)(2,1)S(1)}, u32[]{:S(2)}, u32[]{:S(2)}) collective-permute-start(bf16[8,32,128]{2,1,0:T(8,128)(2,1)S(1)} %get-tuple-element.51), channel_id=1, source_target_pairs={{0,2},{1,3},{2,0},{3,1},{4,6},{5,7},{6,4},{7,5},{8,10},{9,11},{10,... | collective-permute-start | bytes 196616 | tf_op jit(solution)/shard_map/ppermute | solution.py:32
  45.0 6.2 %collective-permute-start.14 = (bf16[8,32,128]{2,1,0:T(8,128)(2,1)S(1)}, bf16[8,32,128]{2,1,0:T(8,128)(2,1)S(1)}, u32[]{:S(2)}, u32[]{:S(2)}) collective-permute-start(bf16[8,32,128]{2,1,0:T(8,128)(2,1)S(1)} %get-tuple-element.52), channel_id=1, source_target_pairs={{0,1},{1,0},{2,3},{3,2},{4,5},{5,4},{6,7},{7,6},{8,9},{9,8},{10,11... | collective-permute-start | bytes 196616 | tf_op jit(solution)/shard_map/ppermute | solution.py:32
  51.2 4.6 %collective-permute-start.17 = (bf16[9,32,128]{2,1,0:T(8,128)(2,1)S(1)}, bf16[9,32,128]{2,1,0:T(8,128)(2,1)S(1)}, u32[]{:S(2)}, u32[]{:S(2)}) collective-permute-start(bf16[9,32,128]{2,1,0:T(8,128)(2,1)S(1)} %summed.1.refs_0_), channel_id=1, source_target_pairs={{0,12},{4,8},{8,4},{12,0},{1,13},{5,9},{9,5},{13,1},{2,14},{6,10},... | collective-permute-start | bytes 221192 | tf_op jit(solution)/shard_map/ppermute | solution.py:32
  51.3 5.8 %collective-permute-start.16 = (bf16[9,32,128]{2,1,0:T(8,128)(2,1)S(1)}, bf16[9,32,128]{2,1,0:T(8,128)(2,1)S(1)}, u32[]{:S(2)}, u32[]{:S(2)}) collective-permute-start(bf16[9,32,128]{2,1,0:T(8,128)(2,1)S(1)} %summed.1.refs_0_), channel_id=1, source_target_pairs={{0,8},{4,12},{8,0},{12,4},{1,9},{5,13},{9,1},{13,5},{2,10},{6,14},... | collective-permute-start | bytes 221192 | tf_op jit(solution)/shard_map/ppermute | solution.py:32
  52.6 4.5 %collective-permute-start.15 = (bf16[9,32,128]{2,1,0:T(8,128)(2,1)S(1)}, bf16[9,32,128]{2,1,0:T(8,128)(2,1)S(1)}, u32[]{:S(2)}, u32[]{:S(2)}) collective-permute-start(bf16[9,32,128]{2,1,0:T(8,128)(2,1)S(1)} %summed.1.refs_0_), channel_id=1, source_target_pairs={{0,4},{4,0},{8,12},{12,8},{1,5},{5,1},{9,13},{13,9},{2,6},{6,2},{1... | collective-permute-start | bytes 221192 | tf_op jit(solution)/shard_map/ppermute | solution.py:32
  57.2 10.3 %copy-start = (bf16[8,2,2048]{2,1,0:T(2,128)(2,1)S(1)}, bf16[8,2,2048]{2,1,0:T(2,128)(2,1)}, u32[]{:S(2)}) copy-start(bf16[8,2,2048]{2,1,0:T(2,128)(2,1)} %refs_4_.1) | copy-start | bytes 196612
  58.7 6.7 %collective-permute-start.20 = (bf16[16,2048]{1,0:T(8,128)(2,1)S(1)}, bf16[16,2048]{1,0:T(8,128)(2,1)S(1)}, u32[]{:S(2)}, u32[]{:S(2)}) collective-permute-start(bf16[16,2048]{1,0:T(8,128)(2,1)S(1)} %output.1.refs_0_), channel_id=1, source_target_pairs={{0,3},{1,2},{2,1},{3,0},{4,7},{5,6},{6,5},{7,4},{8,11},{9,10},{10,... | collective-permute-start | bytes 196616 | tf_op jit(solution)/shard_map/ppermute | solution.py:32
  61.0 6.5 %collective-permute-start.19 = (bf16[16,2048]{1,0:T(8,128)(2,1)S(1)}, bf16[16,2048]{1,0:T(8,128)(2,1)S(1)}, u32[]{:S(2)}, u32[]{:S(2)}) collective-permute-start(bf16[16,2048]{1,0:T(8,128)(2,1)S(1)} %output.1.refs_0_), channel_id=1, source_target_pairs={{0,2},{1,3},{2,0},{3,1},{4,6},{5,7},{6,4},{7,5},{8,10},{9,11},{10,... | collective-permute-start | bytes 196616 | tf_op jit(solution)/shard_map/ppermute | solution.py:32
  61.0 6.5 %collective-permute-start.18 = (bf16[16,2048]{1,0:T(8,128)(2,1)S(1)}, bf16[16,2048]{1,0:T(8,128)(2,1)S(1)}, u32[]{:S(2)}, u32[]{:S(2)}) collective-permute-start(bf16[16,2048]{1,0:T(8,128)(2,1)S(1)} %output.1.refs_0_), channel_id=1, source_target_pairs={{0,1},{1,0},{2,3},{3,2},{4,5},{5,4},{6,7},{7,6},{8,9},{9,8},{10,11... | collective-permute-start | bytes 196616 | tf_op jit(solution)/shard_map/ppermute | solution.py:32

commit v14 on v10

--- a/solution.py
+++ b/solution.py
@@ -113,10 +113,18 @@
         source, to = pl.ds(first + i * size, size), pl.ds(i * size, size)
         x_copy = pltpu.make_async_copy(x_hbm.at[:, source], x_ref.at[:, to], sems.at[2 * i])
         w_copy = pltpu.make_async_copy(w_hbm.at[source], w_ref.at[to], sems.at[2 * i + 1])
-        x_copy.start()
-        w_copy.start()
         pairs_of.append((x_copy, w_copy))
     return pairs_of
+
+
+def start(copies):
+    for copy in copies:
+        copy.start()
+
+
+def wait(copies):
+    for copy in copies:
+        copy.wait()
 
 
 def add_block(x_ref, w_ref, rows, acc, out, fresh):
@@ -125,8 +133,8 @@
     for pair in range(KVH // 2):
         weight = pair_columns(w_ref, rows, pair, 0)
         columns = slice(2 * pair * HD, 2 * (pair + 1) * HD)
-        for start in range(0, tokens, tall):
-            at = slice(start, start + tall)
+        for top in range(0, tokens, tall):
+            at = slice(top, top + tall)
             product = jnp.dot(x_ref[at, rows], weight, preferred_element_type=F32)
             out[at, columns] = product if fresh else acc[at, columns] + product
 
@@ -136,18 +144,20 @@
     tokens = x_ref.shape[0]
     size = x_ref.shape[1] // 3
     copies = copies_of(x_hbm, w_hbm, x_ref, w_ref, sems, 0, size, 3)
+    start(copies[0])
     page_table(pages, prompts, counts, tails, meta)
     rotation_tables(pages, tokens // PAGE, meta, cos_ref, sin_ref)
     spots = [meta[3 * pages + r] + n for r in range(prompts) for n in range(new_count)]
     angles = by_row(len(spots), spots) * lane_freqs(len(spots))
     cos_q[...] = jnp.cos(angles)
     sin_q[...] = jnp.sin(angles) * sine_sign(len(spots))
+    start(copies[1])
     for i in range(2):
-        for copy in copies[i]:
-            copy.wait()
+        wait(copies[i])
+        if i == 0:
+            start(copies[2])
         add_block(x_ref, w_ref, slice(i * size, (i + 1) * size), acc, acc, i == 0)
-    for copy in copies[2]:
-        copy.wait()
+    wait(copies[2])
 
 
 def load(x, kv_weight, counts, tails, pages, new_count):
@@ -184,15 +194,15 @@
 def keys_kernel(acc, xa_ref, wa_ref, x_hbm, w_hbm, cos_ref, sin_ref, after, k_ref, x_ref, w_ref, total, sems):
     tokens, size = x_ref.shape
     tall = tokens // 2
-    ((x_copy, w_copy),) = copies_of(x_hbm, w_hbm, x_ref, w_ref, sems, 3 * size, size, 1)
+    (copies,) = copies_of(x_hbm, w_hbm, x_ref, w_ref, sems, 3 * size, size, 1)
+    start(copies)
     add_block(xa_ref, wa_ref, slice(2 * size, 3 * size), acc, total, False)
-    x_copy.wait()
-    w_copy.wait()
+    wait(copies)
     for pair in range(KVH // 2):
         weight = pair_columns(w_ref, slice(None), pair, 0)
         columns = slice(2 * pair * HD, 2 * (pair + 1) * HD)
-        for start in range(0, tokens, tall):
-            at = slice(start, start + tall)
+        for top in range(0, tokens, tall):
+            at = slice(top, top + tall)
             product = total[at, columns] + jnp.dot(x_ref[at], weight, preferred_element_type=F32)
             cosine, sine = cos_ref[at], sin_ref[at]
             for h in range(2):
@@ -345,23 +355,32 @@
     all_q, ready = refs[n_seq + 2 + n_tp :]
     own_rows = new[0].shape[0]
     local_pages = k_ref.shape[0] // PAGE
-    rows = all_q.shape[1] // KVH
-    count = all_q.shape[1] // n_tp
+    all_rows = all_q.shape[1]
+    rows = all_rows // KVH
+    count = all_rows // n_tp
     scale = 1.0 / math.sqrt(HD)
     me = lax.axis_index("tp")
     seq = lax.axis_index("seq")
     first = seq * local_pages
+    even = lax.broadcasted_iota(jnp.int32, (all_rows, HD), 0) // rows % 2 == 0
     for ds in range(n_seq):
         for rr in range(own_rows):
-            all_q[(seq ^ ds) * own_rows + rr] = new[ds][rr, : KVH * rows]
-    for p in range(local_pages):
-        request = meta[first + p]
-        tokens = slice(p * PAGE, (p + 1) * PAGE)
-        for head in range(KVH):
-            k = k_ref[tokens, head * HD : (head + 1) * HD]
-            q = all_q[request, head * rows : (head + 1) * rows]
+            q = new[ds][rr, :all_rows].astype(F32)
+            request = (seq ^ ds) * own_rows + rr
+            all_q[request, :, :HD] = jnp.where(even, q, 0.0).astype(BF16)
+            all_q[request, :, HD:] = jnp.where(even, 0.0, q).astype(BF16)
+    for p in range(0, local_pages, 2):
+        requests = [meta[first + p], meta[first + p + 1]]
+        tokens = slice(p * PAGE, (p + 2) * PAGE)
+        for pair in range(KVH // 2):
+            k = k_ref[tokens, 2 * pair * HD : 2 * (pair + 1) * HD]
+            at = slice(2 * pair * rows, 2 * (pair + 1) * rows)
+            q = jnp.concatenate([all_q[request, at] for request in requests], axis=0)
             s = lax.dot_general(q, k, (((1,), (1,)), ((), ())), preferred_element_type=F32)
-            ready[head * rows : (head + 1) * rows, tokens] = (s * scale).astype(BF16)
+            for i in range(2):
+                part = s[2 * i * rows : 2 * (i + 1) * rows, i * PAGE : (i + 1) * PAGE]
+                here = slice((p + i) * PAGE, (p + i + 1) * PAGE)
+                ready[at, here] = (part * scale).astype(BF16)
     for d in range(n_tp):
         outs[d][...] = ready[pl.ds(pl.multiple_of(partner(me, d, n_tp) * count, count), count)]
 
@@ -377,7 +396,7 @@
         out_specs=[VMEM] * n_tp,
         out_shape=[jax.ShapeDtypeStruct((rows, tokens), BF16)] * n_tp,
         scratch_shapes=[
-            pltpu.VMEM((prompts, all_rows, HD), BF16),
+            pltpu.VMEM((prompts, all_rows, 2 * HD), BF16),
             pltpu.VMEM((all_rows, tokens), BF16),
         ],
         compiler_params=pltpu.CompilerParams(vmem_limit_bytes=24 * MIB),
@@ -512,14 +531,23 @@
         ready[pl.ds(at, rows_local)] = pieces[d][...]
     total[...] = jnp.zeros_like(total)
     half = va_ref.shape[1] // HD
-    for p in range(local_pages):
-        request = meta[first + p]
-        tokens = slice(p * PAGE, (p + 1) * PAGE)
-        for head in range(KVH):
+    none = jnp.zeros((2 * rows, PAGE), BF16)
+    for p in range(0, local_pages, 2):
+        requests = [meta[first + p], meta[first + p + 1]]
+        tokens = slice(p * PAGE, (p + 2) * PAGE)
+        for pair in range(KVH // 2):
+            head = 2 * pair
             v_ref = va_ref if head < half else vb_ref
-            v = v_ref[tokens, head % half * HD : (head % half + 1) * HD]
-            at = slice(head * rows, (head + 1) * rows)
-            total[request, at] += jnp.dot(ready[at, tokens], v, preferred_element_type=F32)
+            v = v_ref[tokens, head % half * HD : (head % half + 2) * HD]
+            at = slice(head * rows, (head + 2) * rows)
+            w = [ready[at, (p + i) * PAGE : (p + i + 1) * PAGE] for i in range(2)]
+            w = [jnp.concatenate([w[0], none], axis=1), jnp.concatenate([none, w[1]], axis=1)]
+            sums = jnp.dot(jnp.concatenate(w, axis=0), v, preferred_element_type=F32)
+            for i, request in enumerate(requests):
+                for h in range(2):
+                    row = (2 * i + h) * rows
+                    part = sums[row : row + rows, h * HD : (h + 1) * HD]
+                    total[request, (head + h) * rows : (head + h + 1) * rows] += part
     for d in range(n_tp):
         outs[d][...] = total[:, own[d]].astype(BF16)
 

time: 66.4 us -> 65.9 us (level)
  transfers between devices with their start and end apart: 21 -> 21, of which waited for: 9 -> 9; matrix products, arithmetic and copies ran while one was open for 0% -> 0% of each run, Pallas kernels for 21% -> 22%
where the time goes in v14:
time: 65.9 us; the launch traced here: 65.6 us
  starting transfers between devices  27.3 us (41%)
  Pallas kernels  20.6 us (31%)
  waiting for transfers between devices  17.5 us (27%)
    ppermute x21, starting transfers between devices, pairs(): lax.ppermute(value, axis, [(i, partner(i, entry, size)) for i in range(si...  27.3 us
    ppermute x21, waiting for transfers between devices, pairs(): lax.ppermute(value, axis, [(i, partner(i, entry, size)) for i in range(si...  17.5 us
    pallas_call x1, Pallas kernels, load(): pl.pallas_call(functools.partial(load_kernel, pages, prompts, new_count),...  5.68 us
    pallas_call x2, Pallas kernels, project_values(): pl.pallas_call(functools.partial(values_kernel, first), in_specs=[VMEM] *...  4.68 us
    pallas_call x1, Pallas kernels, rotated_keys(): pl.pallas_call(keys_kernel, in_specs=[VMEM] * 3 + [hbm] * 2 + [VMEM] * 2...  3.62 us
    pallas_call x1, Pallas kernels, output_partial(): pl.pallas_call(functools.partial(output_kernel, n_seq), in_specs=[VMEM] *...  1.58 us
    pallas_call x1, Pallas kernels, partial_scores(): pl.pallas_call(functools.partial(scores_kernel, n_seq, n_tp), in_specs=[V...  1.35 us
  transfers between devices with their start and end apart: 21, of which 9 were waited for; matrix products, arithmetic and copies ran while one was open for 0% of the time, Pallas kernels for 22%

profile of v14, /device:TPU:0, one launch (start us, length us, event | category | flops | bytes accessed | tf_op | source)
XLA Modules:
  0.0 65.6 jit_solution(16407720625477805946)
XLA Ops:
  0.0 0.7 %prepare.1 = (bf16[2,2,16,128]{3,2,1,0:T(8,128)(2,1)S(1)}, f32[2,2,4,128]{3,2,1,0:T(4,128)S(1)}) custom-call(bf16[2,2,2048]{2,1,0:T(2,128)(2,1)} %q_ref.1, bf16[2,2,512]{2,1,0:T(2,128)(2,1)} %kv_ref.1), custom_call_target="tpu_custom_call" | custom-call | bytes 1048576 | tf_op jit(solution)/shard_map/prepare/pallas_call | solution.py:292
  0.7 5.1 %collective-permute-start.2 = (bf16[2,2,16,128]{3,2,1,0:T(8,128)(2,1)S(1)}, bf16[2,2,16,128]{3,2,1,0:T(8,128)(2,1)S(1)}, u32[]{:S(2)}, u32[]{:S(2)}) collective-permute-start(bf16[2,2,16,128]{3,2,1,0:T(8,128)(2,1)S(1)} %get-tuple-element.34.refs_0_), channel_id=1, source_target_pairs={{0,3},{1,2},{2,1},{3,0},{4,7},{5,6},{6,5},{7,4},{8,11},{9,10},{10,... | collective-permute-start | bytes 49160 | tf_op jit(solution)/shard_map/ppermute | solution.py:32
  5.9 0.6 collective-permute-start
  6.5 5.7 %load.1 = (f32[1024,1024]{1,0:T(8,128)S(1)}, bf16[1024,1536]{1,0:T(8,128)(2,1)S(1)}, bf16[1536,2048]{1,0:T(8,128)(2,1)S(1)}, f32[1024,128]{1,0:T(8,128)S(1)}, f3...) custom-call(bf16[1024,2048]{1,0:T(8,128)(2,1)} %x_hbm.3, ...), custom_call_target="tpu_custom_call" | custom-call | flops 2147483648 | bytes 9437184 | tf_op jit(solution)/shard_map/load/pallas_call | solution.py:169
  12.8 1.3 %collective-permute-start.4 = (bf16[2,144,128]{2,1,0:T(8,128)(2,1)S(1)}, bf16[2,144,128]{2,1,0:T(8,128)(2,1)S(1)}, u32[]{:S(2)}, u32[]{:S(2)}) collective-permute-start(bf16[2,144,128]{2,1,0:T(8,128)(2,1)S(1)} %turned.1.after.refs_0_), channel_id=1, source_target_pairs={{0,8},{4,12},{8,0},{12,4},{1,9},{5,13},{9,1},{13,5},{2,10},{6,14},... | collective-permute-start | bytes 221192 | tf_op jit(solution)/shard_map/ppermute | solution.py:32
  14.3 3.6 %keys.1 = (bf16[1024,1024]{1,0:T(8,128)(2,1)S(1)}, bf16[1024,512]{1,0:T(8,128)(2,1)S(1)}, bf16[512,2048]{1,0:T(8,128)(2,1)S(1)}) custom-call(f32[1024,1024]{1,0:T(8,128)S(1)} %get-tuple-element.38.acc, bf16[1024,1536]{1,0:T(8,128)(2,1)S(1)} %get-tuple-element.39.xa_ref, bf16[1536,2048]{1,0:T(8,128)(2,1)S(1)} %get-tuple-element.40.wa_ref, ...), custom_call_target="tpu_custom_call" | custom-call | flops 2147483648 | bytes 8388608 | tf_op jit(solution)/shard_map/keys/pallas_call | solution.py:218
  17.9 0.6 collective-permute-done.4.refs_2_
  18.5 1.3 %scores.1 = (bf16[32,1024]{1,0:T(8,128)(2,1)S(1)}, bf16[32,1024]{1,0:T(8,128)(2,1)S(1)}, bf16[32,1024]{1,0:T(8,128)(2,1)S(1)}, bf16[32,1024]{1,0:T(8,128)(2,1)S(1)}) custom-call(bf16[2,144,128]{2,1,0:T(8,128)(2,1)S(1)} %turned.1.after.refs_0_, bf16[2,144,128]{2,1,0:T(8,128)(2,1)S(1)} %collective-permute-done.3.refs_1_, ...), custom_call_target="tpu_custom_call" | custom-call | flops 33554432 | bytes 6291456 | tf_op jit(solution)/shard_map/scores/pallas_call | solution.py:393
  19.9 3.8 %collective-permute-start.6 = (bf16[32,1024]{1,0:T(8,128)(2,1)S(1)}, bf16[32,1024]{1,0:T(8,128)(2,1)S(1)}, u32[]{:S(2)}, u32[]{:S(2)}) collective-permute-start(bf16[32,1024]{1,0:T(8,128)(2,1)S(1)} %get-tuple-element.46), channel_id=1, source_target_pairs={{0,3},{1,2},{2,1},{3,0},{4,7},{5,6},{6,5},{7,4},{8,11},{9,10},{10,... | collective-permute-start | bytes 196616 | tf_op jit(solution)/shard_map/ppermute | solution.py:32
  23.7 0.6 collective-permute-start.8
  24.4 2.3 %values.2 = (bf16[1024,512]{1,0:T(8,128)(2,1)S(1)}, bf16[1024,2048]{1,0:T(8,128)(2,1)S(1)}) custom-call(bf16[1024,1536]{1,0:T(8,128)(2,1)S(1)} %get-tuple-element.39.xa_ref, bf16[1536,2048]{1,0:T(8,128)(2,1)S(1)} %get-tuple-element.40.wa_ref, bf16[1024,512]{1,0:T(8,128)(2,1)S(1)} %get-tuple-element.49.xb_ref, ...), custom_call_target="tpu_custom_call" | custom-call | flops 1610612736 | bytes 8388608 | tf_op jit(solution)/shard_map/values/pallas_call | solution.py:260
  26.7 2.7 %collective-permute-done.7.refs_2_ = bf16[32,1024]{1,0:T(8,128)(2,1)S(1)} collective-permute-done((bf16[32,1024]{1,0:T(8,128)(2,1)S(1)}, bf16[32,1024]{1,0:T(8,128)(2,1)S(1)}, u32[]{:S(2)}, u32[]{:S(2)}) %collective-permute-start.7) | collective-permute-done | bytes 65568 | tf_op jit(solution)/shard_map/ppermute | solution.py:32
  29.4 0.9 %weights.1 = (bf16[32,1024]{1,0:T(8,128)(2,1)S(1)}, bf16[32,128]{1,0:T(8,128)(2,1)S(1)}) custom-call(bf16[32,1024]{1,0:T(8,128)(2,1)S(1)} %get-tuple-element.45.after.refs_0_, bf16[32,1024]{1,0:T(8,128)(2,1)S(1)} %collective-permute-done.6.refs_1_, bf16[32,1024]{1,0:T(8,128)(2,1)S(1)} %collective-permute-done.7.refs_2_, ...), custom_call_target="tpu_custom_call" | custom-call | tf_op jit(solution)/shard_map/weights/pallas_call | solution.py:504
  30.3 2.3 %collective-permute-start.11 = (bf16[32,1024]{1,0:T(8,128)(2,1)S(1)}, bf16[32,1024]{1,0:T(8,128)(2,1)S(1)}, u32[]{:S(2)}, u32[]{:S(2)}) collective-permute-start(bf16[32,1024]{1,0:T(8,128)(2,1)S(1)} %get-tuple-element.52.refs_0_), channel_id=1, source_target_pairs={{0,3},{1,2},{2,1},{3,0},{4,7},{5,6},{6,5},{7,4},{8,11},{9,10},{10,... | collective-permute-start | bytes 196616 | tf_op jit(solution)/shard_map/ppermute | solution.py:32
  33.0 1.7 %collective-permute-start.9 = (bf16[32,1024]{1,0:T(8,128)(2,1)S(1)}, bf16[32,1024]{1,0:T(8,128)(2,1)S(1)}, u32[]{:S(2)}, u32[]{:S(2)}) collective-permute-start(bf16[32,1024]{1,0:T(8,128)(2,1)S(1)} %get-tuple-element.52.refs_0_), channel_id=1, source_target_pairs={{0,1},{1,0},{2,3},{3,2},{4,5},{5,4},{6,7},{7,6},{8,9},{9,8},{10,11... | collective-permute-start | bytes 196616 | tf_op jit(solution)/shard_map/ppermute | solution.py:32
  34.7 2.3 %values.3 = (bf16[1024,512]{1,0:T(8,128)(2,1)S(1)}, bf16[1024,2048]{1,0:T(8,128)(2,1)S(1)}) custom-call(bf16[1024,1536]{1,0:T(8,128)(2,1)S(1)} %get-tuple-element.39.xa_ref, bf16[1536,2048]{1,0:T(8,128)(2,1)S(1)} %get-tuple-element.40.wa_ref, bf16[1024,512]{1,0:T(8,128)(2,1)S(1)} %get-tuple-element.49.xb_ref, ...), custom_call_target="tpu_custom_call" | custom-call | flops 1610612736 | bytes 8388608 | tf_op jit(solution)/shard_map/values/pallas_call | solution.py:260
  37.1 2.2 %collective-permute-done.10.refs_2_ = bf16[32,1024]{1,0:T(8,128)(2,1)S(1)} collective-permute-done((bf16[32,1024]{1,0:T(8,128)(2,1)S(1)}, bf16[32,1024]{1,0:T(8,128)(2,1)S(1)}, u32[]{:S(2)}, u32[]{:S(2)}) %collective-permute-start.10) | collective-permute-done | bytes 65568 | tf_op jit(solution)/shard_map/ppermute | solution.py:32
  39.3 1.1 %weighted.1 = (bf16[8,32,128]{2,1,0:T(8,128)(2,1)S(1)}, bf16[8,32,128]{2,1,0:T(8,128)(2,1)S(1)}, bf16[8,32,128]{2,1,0:T(8,128)(2,1)S(1)}, bf16[8,32,128]{2,1,0:T(8,128)(2,1)S(1)}) custom-call(bf16[32,1024]{1,0:T(8,128)(2,1)S(1)} %get-tuple-element.52.refs_0_, bf16[32,1024]{1,0:T(8,128)(2,1)S(1)} %collective-permute-done.9.refs_1_, ...), custom_call_target="tpu_custom_call" | custom-call | flops 33554432 | bytes 8388608 | tf_op jit(solution)/shard_map/weighted/pallas_call | solution.py:558
  40.4 2.0 %collective-permute-start.12 = (bf16[8,32,128]{2,1,0:T(8,128)(2,1)S(1)}, bf16[8,32,128]{2,1,0:T(8,128)(2,1)S(1)}, u32[]{:S(2)}, u32[]{:S(2)}) collective-permute-start(bf16[8,32,128]{2,1,0:T(8,128)(2,1)S(1)} %get-tuple-element.56), channel_id=1, source_target_pairs={{0,3},{1,2},{2,1},{3,0},{4,7},{5,6},{6,5},{7,4},{8,11},{9,10},{10,... | collective-permute-start | bytes 196616 | tf_op jit(solution)/shard_map/ppermute | solution.py:32
  42.4 2.5 %collective-permute-start.14 = (bf16[8,32,128]{2,1,0:T(8,128)(2,1)S(1)}, bf16[8,32,128]{2,1,0:T(8,128)(2,1)S(1)}, u32[]{:S(2)}, u32[]{:S(2)}) collective-permute-start(bf16[8,32,128]{2,1,0:T(8,128)(2,1)S(1)} %get-tuple-element.58), channel_id=1, source_target_pairs={{0,1},{1,0},{2,3},{3,2},{4,5},{5,4},{6,7},{7,6},{8,9},{9,8},{10,11... | collective-permute-start | bytes 196616 | tf_op jit(solution)/shard_map/ppermute | solution.py:32
  44.8 2.0 %collective-permute-done.12.refs_1_ = bf16[8,32,128]{2,1,0:T(8,128)(2,1)S(1)} collective-permute-done((bf16[8,32,128]{2,1,0:T(8,128)(2,1)S(1)}, bf16[8,32,128]{2,1,0:T(8,128)(2,1)S(1)}, u32[]{:S(2)}, u32[]{:S(2)}) %collective-permute-start.12) | collective-permute-done | bytes 65568 | tf_op jit(solution)/shard_map/ppermute | solution.py:32
  46.8 1.7 %collective-permute-done.13.refs_2_ = bf16[8,32,128]{2,1,0:T(8,128)(2,1)S(1)} collective-permute-done((bf16[8,32,128]{2,1,0:T(8,128)(2,1)S(1)}, bf16[8,32,128]{2,1,0:T(8,128)(2,1)S(1)}, u32[]{:S(2)}, u32[]{:S(2)}) %collective-permute-start.13) | collective-permute-done | bytes 65568 | tf_op jit(solution)/shard_map/ppermute | solution.py:32
  48.7 1.2 %collective-permute-start.16 = (bf16[9,32,128]{2,1,0:T(8,128)(2,1)S(1)}, bf16[9,32,128]{2,1,0:T(8,128)(2,1)S(1)}, u32[]{:S(2)}, u32[]{:S(2)}) collective-permute-start(bf16[9,32,128]{2,1,0:T(8,128)(2,1)S(1)} %summed.1.refs_0_), channel_id=1, source_target_pairs={{0,8},{4,12},{8,0},{12,4},{1,9},{5,13},{9,1},{13,5},{2,10},{6,14},... | collective-permute-start | bytes 221192 | tf_op jit(solution)/shard_map/ppermute | solution.py:32
  50.0 0.5 collective-permute-start.15
  50.7 2.6 %collective-permute-done.17.refs_3_ = bf16[9,32,128]{2,1,0:T(8,128)(2,1)S(1)} collective-permute-done((bf16[9,32,128]{2,1,0:T(8,128)(2,1)S(1)}, bf16[9,32,128]{2,1,0:T(8,128)(2,1)S(1)}, u32[]{:S(2)}, u32[]{:S(2)}) %collective-permute-start.17) | collective-permute-done | bytes 73760 | tf_op jit(solution)/shard_map/ppermute | solution.py:32
  53.2 1.3 %collective-permute-done.16.refs_2_ = bf16[9,32,128]{2,1,0:T(8,128)(2,1)S(1)} collective-permute-done((bf16[9,32,128]{2,1,0:T(8,128)(2,1)S(1)}, bf16[9,32,128]{2,1,0:T(8,128)(2,1)S(1)}, u32[]{:S(2)}, u32[]{:S(2)}) %collective-permute-start.16) | collective-permute-done | bytes 73760 | tf_op jit(solution)/shard_map/ppermute | solution.py:32
  54.5 1.6 %output.1.refs_0_ = bf16[16,2048]{1,0:T(8,128)(2,1)S(1)} custom-call(bf16[9,32,128]{2,1,0:T(8,128)(2,1)S(1)} %summed.1.refs_0_, bf16[9,32,128]{2,1,0:T(8,128)(2,1)S(1)} %collective-permute-done.15.refs_1_, bf16[9,32,128]{2,1,0:T(8,128)(2,1)S(1)} %collective-permute-done.16.refs_2_, bf16[9,32,128]{2,1,0:T(8,128)(2,1)S(1)} %collective-permute-done.17.refs_3_, ...), custom_call_target="tpu_custom_call" | custom-call | tf_op jit(solution)/shard_map/output/pallas_call | solution.py:652
  56.1 2.2 %collective-permute-start.20 = (bf16[16,2048]{1,0:T(8,128)(2,1)S(1)}, bf16[16,2048]{1,0:T(8,128)(2,1)S(1)}, u32[]{:S(2)}, u32[]{:S(2)}) collective-permute-start(bf16[16,2048]{1,0:T(8,128)(2,1)S(1)} %output.1.refs_0_), channel_id=1, source_target_pairs={{0,3},{1,2},{2,1},{3,0},{4,7},{5,6},{6,5},{7,4},{8,11},{9,10},{10,... | collective-permute-start | bytes 196616 | tf_op jit(solution)/shard_map/ppermute | solution.py:32
  58.3 2.2 %collective-permute-start.18 = (bf16[16,2048]{1,0:T(8,128)(2,1)S(1)}, bf16[16,2048]{1,0:T(8,128)(2,1)S(1)}, u32[]{:S(2)}, u32[]{:S(2)}) collective-permute-start(bf16[16,2048]{1,0:T(8,128)(2,1)S(1)} %output.1.refs_0_), channel_id=1, source_target_pairs={{0,1},{1,0},{2,3},{3,2},{4,5},{5,4},{6,7},{7,6},{8,9},{9,8},{10,11... | collective-permute-start | bytes 196616 | tf_op jit(solution)/shard_map/ppermute | solution.py:32
  60.5 2.3 %collective-permute-done.20.refs_3_ = bf16[16,2048]{1,0:T(8,128)(2,1)S(1)} collective-permute-done((bf16[16,2048]{1,0:T(8,128)(2,1)S(1)}, bf16[16,2048]{1,0:T(8,128)(2,1)S(1)}, u32[]{:S(2)}, u32[]{:S(2)}) %collective-permute-start.20) | collective-permute-done | bytes 65568 | tf_op jit(solution)/shard_map/ppermute | solution.py:32
  62.9 2.0 %collective-permute-done.19.refs_2_ = bf16[16,2048]{1,0:T(8,128)(2,1)S(1)} collective-permute-done((bf16[16,2048]{1,0:T(8,128)(2,1)S(1)}, bf16[16,2048]{1,0:T(8,128)(2,1)S(1)}, u32[]{:S(2)}, u32[]{:S(2)}) %collective-permute-start.19) | collective-permute-done | bytes 65568 | tf_op jit(solution)/shard_map/ppermute | solution.py:32
  64.9 0.7 %final.1 = f32[8,2,2048]{2,1,0:T(2,128)} custom-call(bf16[16,2048]{1,0:T(8,128)(2,1)S(1)} %output.1.refs_0_, bf16[16,2048]{1,0:T(8,128)(2,1)S(1)} %collective-permute-done.18.refs_1_, bf16[16,2048]{1,0:T(8,128)(2,1)S(1)} %collective-permute-done.19.refs_2_, bf16[16,2048]{1,0:T(8,128)(2,1)S(1)} %collective-permute-done.20.refs_3_, bf16[8,2,2048]{2,1,0:T(2,128)(2,1)S(1)} %copy-done), custom_call_target="tpu_custom_call" | custom-call | tf_op jit(solution)/shard_map/final/pallas_call | solution.py:676
  (25 shorter events, 1.5 us)
Async XLA Ops:
  0.7 11.5 %collective-permute-start.2 = (bf16[2,2,16,128]{3,2,1,0:T(8,128)(2,1)S(1)}, bf16[2,2,16,128]{3,2,1,0:T(8,128)(2,1)S(1)}, u32[]{:S(2)}, u32[]{:S(2)}) collective-permute-start(bf16[2,2,16,128]{3,2,1,0:T(8,128)(2,1)S(1)} %get-tuple-element.34.refs_0_), channel_id=1, source_target_pairs={{0,3},{1,2},{2,1},{3,0},{4,7},{5,6},{6,5},{7,4},{8,11},{9,10},{10,... | collective-permute-start | bytes 49160 | tf_op jit(solution)/shard_map/ppermute | solution.py:32
  5.9 6.3 %collective-permute-start.1 = (bf16[2,2,16,128]{3,2,1,0:T(8,128)(2,1)S(1)}, bf16[2,2,16,128]{3,2,1,0:T(8,128)(2,1)S(1)}, u32[]{:S(2)}, u32[]{:S(2)}) collective-permute-start(bf16[2,2,16,128]{3,2,1,0:T(8,128)(2,1)S(1)} %get-tuple-element.34.refs_0_), channel_id=1, source_target_pairs={{0,2},{1,3},{2,0},{3,1},{4,6},{5,7},{6,4},{7,5},{8,10},{9,11},{10,... | collective-permute-start | bytes 49160 | tf_op jit(solution)/shard_map/ppermute | solution.py:32
  5.9 6.4 %collective-permute-start = (bf16[2,2,16,128]{3,2,1,0:T(8,128)(2,1)S(1)}, bf16[2,2,16,128]{3,2,1,0:T(8,128)(2,1)S(1)}, u32[]{:S(2)}, u32[]{:S(2)}) collective-permute-start(bf16[2,2,16,128]{3,2,1,0:T(8,128)(2,1)S(1)} %get-tuple-element.34.refs_0_), channel_id=1, source_target_pairs={{0,1},{1,0},{2,3},{3,2},{4,5},{5,4},{6,7},{7,6},{8,9},{9,8},{10,11... | collective-permute-start | bytes 49160 | tf_op jit(solution)/shard_map/ppermute | solution.py:32
  12.3 5.6 %collective-permute-start.5 = (bf16[2,144,128]{2,1,0:T(8,128)(2,1)S(1)}, bf16[2,144,128]{2,1,0:T(8,128)(2,1)S(1)}, u32[]{:S(2)}, u32[]{:S(2)}) collective-permute-start(bf16[2,144,128]{2,1,0:T(8,128)(2,1)S(1)} %turned.1.after.refs_0_), channel_id=1, source_target_pairs={{0,12},{4,8},{8,4},{12,0},{1,13},{5,9},{9,5},{13,1},{2,14},{6,10},... | collective-permute-start | bytes 221192 | tf_op jit(solution)/shard_map/ppermute | solution.py:32
  12.8 5.7 %collective-permute-start.4 = (bf16[2,144,128]{2,1,0:T(8,128)(2,1)S(1)}, bf16[2,144,128]{2,1,0:T(8,128)(2,1)S(1)}, u32[]{:S(2)}, u32[]{:S(2)}) collective-permute-start(bf16[2,144,128]{2,1,0:T(8,128)(2,1)S(1)} %turned.1.after.refs_0_), channel_id=1, source_target_pairs={{0,8},{4,12},{8,0},{12,4},{1,9},{5,13},{9,1},{13,5},{2,10},{6,14},... | collective-permute-start | bytes 221192 | tf_op jit(solution)/shard_map/ppermute | solution.py:32
  14.1 4.4 %collective-permute-start.3 = (bf16[2,144,128]{2,1,0:T(8,128)(2,1)S(1)}, bf16[2,144,128]{2,1,0:T(8,128)(2,1)S(1)}, u32[]{:S(2)}, u32[]{:S(2)}) collective-permute-start(bf16[2,144,128]{2,1,0:T(8,128)(2,1)S(1)} %turned.1.after.refs_0_), channel_id=1, source_target_pairs={{0,4},{4,0},{8,12},{12,8},{1,5},{5,1},{9,13},{13,9},{2,6},{6,2},{1... | collective-permute-start | bytes 221192 | tf_op jit(solution)/shard_map/ppermute | solution.py:32
  19.9 6.8 %collective-permute-start.6 = (bf16[32,1024]{1,0:T(8,128)(2,1)S(1)}, bf16[32,1024]{1,0:T(8,128)(2,1)S(1)}, u32[]{:S(2)}, u32[]{:S(2)}) collective-permute-start(bf16[32,1024]{1,0:T(8,128)(2,1)S(1)} %get-tuple-element.46), channel_id=1, source_target_pairs={{0,3},{1,2},{2,1},{3,0},{4,7},{5,6},{6,5},{7,4},{8,11},{9,10},{10,... | collective-permute-start | bytes 196616 | tf_op jit(solution)/shard_map/ppermute | solution.py:32
  23.7 5.7 %collective-permute-start.7 = (bf16[32,1024]{1,0:T(8,128)(2,1)S(1)}, bf16[32,1024]{1,0:T(8,128)(2,1)S(1)}, u32[]{:S(2)}, u32[]{:S(2)}) collective-permute-start(bf16[32,1024]{1,0:T(8,128)(2,1)S(1)} %get-tuple-element.47), channel_id=1, source_target_pairs={{0,2},{1,3},{2,0},{3,1},{4,6},{5,7},{6,4},{7,5},{8,10},{9,11},{10,... | collective-permute-start | bytes 196616 | tf_op jit(solution)/shard_map/ppermute | solution.py:32
  23.7 5.7 %collective-permute-start.8 = (bf16[32,1024]{1,0:T(8,128)(2,1)S(1)}, bf16[32,1024]{1,0:T(8,128)(2,1)S(1)}, u32[]{:S(2)}, u32[]{:S(2)}) collective-permute-start(bf16[32,1024]{1,0:T(8,128)(2,1)S(1)} %get-tuple-element.48), channel_id=1, source_target_pairs={{0,1},{1,0},{2,3},{3,2},{4,5},{5,4},{6,7},{7,6},{8,9},{9,8},{10,11... | collective-permute-start | bytes 196616 | tf_op jit(solution)/shard_map/ppermute | solution.py:32
  30.3 6.7 %collective-permute-start.11 = (bf16[32,1024]{1,0:T(8,128)(2,1)S(1)}, bf16[32,1024]{1,0:T(8,128)(2,1)S(1)}, u32[]{:S(2)}, u32[]{:S(2)}) collective-permute-start(bf16[32,1024]{1,0:T(8,128)(2,1)S(1)} %get-tuple-element.52.refs_0_), channel_id=1, source_target_pairs={{0,3},{1,2},{2,1},{3,0},{4,7},{5,6},{6,5},{7,4},{8,11},{9,10},{10,... | collective-permute-start | bytes 196616 | tf_op jit(solution)/shard_map/ppermute | solution.py:32
  32.6 6.7 %collective-permute-start.10 = (bf16[32,1024]{1,0:T(8,128)(2,1)S(1)}, bf16[32,1024]{1,0:T(8,128)(2,1)S(1)}, u32[]{:S(2)}, u32[]{:S(2)}) collective-permute-start(bf16[32,1024]{1,0:T(8,128)(2,1)S(1)} %get-tuple-element.52.refs_0_), channel_id=1, source_target_pairs={{0,2},{1,3},{2,0},{3,1},{4,6},{5,7},{6,4},{7,5},{8,10},{9,11},{10,... | collective-permute-start | bytes 196616 | tf_op jit(solution)/shard_map/ppermute | solution.py:32
  33.0 6.3 %collective-permute-start.9 = (bf16[32,1024]{1,0:T(8,128)(2,1)S(1)}, bf16[32,1024]{1,0:T(8,128)(2,1)S(1)}, u32[]{:S(2)}, u32[]{:S(2)}) collective-permute-start(bf16[32,1024]{1,0:T(8,128)(2,1)S(1)} %get-tuple-element.52.refs_0_), channel_id=1, source_target_pairs={{0,1},{1,0},{2,3},{3,2},{4,5},{5,4},{6,7},{7,6},{8,9},{9,8},{10,11... | collective-permute-start | bytes 196616 | tf_op jit(solution)/shard_map/ppermute | solution.py:32
  40.4 6.4 %collective-permute-start.12 = (bf16[8,32,128]{2,1,0:T(8,128)(2,1)S(1)}, bf16[8,32,128]{2,1,0:T(8,128)(2,1)S(1)}, u32[]{:S(2)}, u32[]{:S(2)}) collective-permute-start(bf16[8,32,128]{2,1,0:T(8,128)(2,1)S(1)} %get-tuple-element.56), channel_id=1, source_target_pairs={{0,3},{1,2},{2,1},{3,0},{4,7},{5,6},{6,5},{7,4},{8,11},{9,10},{10,... | collective-permute-start | bytes 196616 | tf_op jit(solution)/shard_map/ppermute | solution.py:32
  42.4 6.2 %collective-permute-start.13 = (bf16[8,32,128]{2,1,0:T(8,128)(2,1)S(1)}, bf16[8,32,128]{2,1,0:T(8,128)(2,1)S(1)}, u32[]{:S(2)}, u32[]{:S(2)}) collective-permute-start(bf16[8,32,128]{2,1,0:T(8,128)(2,1)S(1)} %get-tuple-element.57), channel_id=1, source_target_pairs={{0,2},{1,3},{2,0},{3,1},{4,6},{5,7},{6,4},{7,5},{8,10},{9,11},{10,... | collective-permute-start | bytes 196616 | tf_op jit(solution)/shard_map/ppermute | solution.py:32
  42.4 6.2 %collective-permute-start.14 = (bf16[8,32,128]{2,1,0:T(8,128)(2,1)S(1)}, bf16[8,32,128]{2,1,0:T(8,128)(2,1)S(1)}, u32[]{:S(2)}, u32[]{:S(2)}) collective-permute-start(bf16[8,32,128]{2,1,0:T(8,128)(2,1)S(1)} %get-tuple-element.58), channel_id=1, source_target_pairs={{0,1},{1,0},{2,3},{3,2},{4,5},{5,4},{6,7},{7,6},{8,9},{9,8},{10,11... | collective-permute-start | bytes 196616 | tf_op jit(solution)/shard_map/ppermute | solution.py:32
  48.6 4.6 %collective-permute-start.17 = (bf16[9,32,128]{2,1,0:T(8,128)(2,1)S(1)}, bf16[9,32,128]{2,1,0:T(8,128)(2,1)S(1)}, u32[]{:S(2)}, u32[]{:S(2)}) collective-permute-start(bf16[9,32,128]{2,1,0:T(8,128)(2,1)S(1)} %summed.1.refs_0_), channel_id=1, source_target_pairs={{0,12},{4,8},{8,4},{12,0},{1,13},{5,9},{9,5},{13,1},{2,14},{6,10},... | collective-permute-start | bytes 221192 | tf_op jit(solution)/shard_map/ppermute | solution.py:32
  48.7 5.8 %collective-permute-start.16 = (bf16[9,32,128]{2,1,0:T(8,128)(2,1)S(1)}, bf16[9,32,128]{2,1,0:T(8,128)(2,1)S(1)}, u32[]{:S(2)}, u32[]{:S(2)}) collective-permute-start(bf16[9,32,128]{2,1,0:T(8,128)(2,1)S(1)} %summed.1.refs_0_), channel_id=1, source_target_pairs={{0,8},{4,12},{8,0},{12,4},{1,9},{5,13},{9,1},{13,5},{2,10},{6,14},... | collective-permute-start | bytes 221192 | tf_op jit(solution)/shard_map/ppermute | solution.py:32
  50.0 4.6 %collective-permute-start.15 = (bf16[9,32,128]{2,1,0:T(8,128)(2,1)S(1)}, bf16[9,32,128]{2,1,0:T(8,128)(2,1)S(1)}, u32[]{:S(2)}, u32[]{:S(2)}) collective-permute-start(bf16[9,32,128]{2,1,0:T(8,128)(2,1)S(1)} %summed.1.refs_0_), channel_id=1, source_target_pairs={{0,4},{4,0},{8,12},{12,8},{1,5},{5,1},{9,13},{13,9},{2,6},{6,2},{1... | collective-permute-start | bytes 221192 | tf_op jit(solution)/shard_map/ppermute | solution.py:32
  54.5 10.3 %copy-start = (bf16[8,2,2048]{2,1,0:T(2,128)(2,1)S(1)}, bf16[8,2,2048]{2,1,0:T(2,128)(2,1)}, u32[]{:S(2)}) copy-start(bf16[8,2,2048]{2,1,0:T(2,128)(2,1)} %refs_4_.1) | copy-start | bytes 196612
  56.1 6.7 %collective-permute-start.20 = (bf16[16,2048]{1,0:T(8,128)(2,1)S(1)}, bf16[16,2048]{1,0:T(8,128)(2,1)S(1)}, u32[]{:S(2)}, u32[]{:S(2)}) collective-permute-start(bf16[16,2048]{1,0:T(8,128)(2,1)S(1)} %output.1.refs_0_), channel_id=1, source_target_pairs={{0,3},{1,2},{2,1},{3,0},{4,7},{5,6},{6,5},{7,4},{8,11},{9,10},{10,... | collective-permute-start | bytes 196616 | tf_op jit(solution)/shard_map/ppermute | solution.py:32
  58.3 6.5 %collective-permute-start.19 = (bf16[16,2048]{1,0:T(8,128)(2,1)S(1)}, bf16[16,2048]{1,0:T(8,128)(2,1)S(1)}, u32[]{:S(2)}, u32[]{:S(2)}) collective-permute-start(bf16[16,2048]{1,0:T(8,128)(2,1)S(1)} %output.1.refs_0_), channel_id=1, source_target_pairs={{0,2},{1,3},{2,0},{3,1},{4,6},{5,7},{6,4},{7,5},{8,10},{9,11},{10,... | collective-permute-start | bytes 196616 | tf_op jit(solution)/shard_map/ppermute | solution.py:32
  58.3 6.5 %collective-permute-start.18 = (bf16[16,2048]{1,0:T(8,128)(2,1)S(1)}, bf16[16,2048]{1,0:T(8,128)(2,1)S(1)}, u32[]{:S(2)}, u32[]{:S(2)}) collective-permute-start(bf16[16,2048]{1,0:T(8,128)(2,1)S(1)} %output.1.refs_0_), channel_id=1, source_target_pairs={{0,1},{1,0},{2,3},{3,2},{4,5},{5,4},{6,7},{7,6},{8,9},{9,8},{10,11... | collective-permute-start | bytes 196616 | tf_op jit(solution)/shard_map/ppermute | solution.py:32

commit v15 on v14

--- a/solution.py
+++ b/solution.py
@@ -23,22 +23,29 @@
 ANY = pl.BlockSpec(memory_space=pl.ANY)
 
 
-def partner(me, entry, size):
-    return me ^ ((size - entry) % size)
-
-
-def pairs(value, axis, entry):
-    size = lax.axis_size(axis)
-    return lax.ppermute(value, axis, [(i, partner(i, entry, size)) for i in range(size)])
+def pairs(value, axis, d):
+    return lax.ppermute(value, axis, [(i, i ^ d) for i in range(lax.axis_size(axis))])
+
+
+def order(size):
+    found, top = [0], size // 2
+    while top:
+        found += range(top, 2 * top)
+        top //= 2
+    return found
+
+
+def reverse(size):
+    return [0] + order(size)[:0:-1]
 
 
 def exchange(chunks, axis):
-    return [chunks[0]] + [pairs(chunks[i], axis, i) for i in range(1, len(chunks))]
+    offsets = order(len(chunks))
+    return [chunks[0]] + [pairs(c, axis, d) for c, d in zip(chunks[1:], offsets[1:])]
 
 
 def gather(value, axis):
-    size = lax.axis_size(axis)
-    return [value] + [pairs(value, axis, size - d) for d in range(1, size)]
+    return [value] + [pairs(value, axis, d) for d in reverse(lax.axis_size(axis))[1:]]
 
 
 def lane_freqs(rows):
@@ -320,7 +327,7 @@
             blocks = [refs[d][r, n].astype(F32) for n in range(new_count)]
             for g in range(kv_local):
                 parts = [turn(q[g * GROUP : (g + 1) * GROUP], n) for n, q in enumerate(blocks)]
-                at = ((me ^ d) * kv_local + g) * rows
+                at = ((me ^ reverse(n_tp)[d]) * kv_local + g) * rows
                 at = pl.ds(pl.multiple_of(at, rows), rows)
                 out_ref[r, at] = jnp.concatenate(parts, axis=0).astype(BF16)
         fresh = []
@@ -366,7 +373,7 @@
     for ds in range(n_seq):
         for rr in range(own_rows):
             q = new[ds][rr, :all_rows].astype(F32)
-            request = (seq ^ ds) * own_rows + rr
+            request = (seq ^ reverse(n_seq)[ds]) * own_rows + rr
             all_q[request, :, :HD] = jnp.where(even, q, 0.0).astype(BF16)
             all_q[request, :, HD:] = jnp.where(even, 0.0, q).astype(BF16)
     for p in range(0, local_pages, 2):
@@ -382,7 +389,7 @@
                 here = slice((p + i) * PAGE, (p + i + 1) * PAGE)
                 ready[at, here] = (part * scale).astype(BF16)
     for d in range(n_tp):
-        outs[d][...] = ready[pl.ds(pl.multiple_of(partner(me, d, n_tp) * count, count), count)]
+        outs[d][...] = ready[pl.ds(pl.multiple_of((me ^ order(n_tp)[d]) * count, count), count)]
 
 
 def partial_scores(new, k, meta, prompts, n_tp):
@@ -427,7 +434,7 @@
 
     for ds in range(n_seq):
         for rr in range(own_rows):
-            request = (seq ^ ds) * own_rows + rr
+            request = (seq ^ reverse(n_seq)[ds]) * own_rows + rr
             q = new[ds][rr, own].astype(F32)
             both = new[ds][rr, KVH * rows :].astype(F32)
             for n in range(new_count):
@@ -478,12 +485,13 @@
     quarter = lane // prompts
     spot = lane % prompts
     stats = jnp.where(quarter == 0, NEG, 0.0)
-    sums = []
+    same = [owners[p] == owners[p - 1] for p in range(1, local_pages)]
+    for p in range(1, local_pages):
+        maxima[p] = jnp.where(same[p - 1], jnp.maximum(maxima[p - 1], maxima[p]), maxima[p])
+    for p in reversed(range(local_pages - 1)):
+        maxima[p] = jnp.where(same[p], maxima[p + 1], maxima[p])
     for p in range(local_pages):
         top = maxima[p]
-        for other in range(local_pages):
-            if other != p:
-                top = jnp.where(owners[p] == owners[other], jnp.maximum(top, maxima[other]), top)
         high = top.astype(BF16).astype(F32)
         low = (top - high).astype(BF16).astype(F32)
         w = jnp.where(masks[p], jnp.exp(scores[p] - (high + low)), 0.0)
@@ -525,9 +533,9 @@
     local_pages = tokens_here // PAGE
     first = lax.axis_index("seq") * local_pages
     me = lax.axis_index("tp")
-    own = [pl.ds(pl.multiple_of(partner(me, d, n_tp) * rows_local, rows_local), rows_local) for d in range(n_tp)]
+    own = [pl.ds(pl.multiple_of((me ^ order(n_tp)[d]) * rows_local, rows_local), rows_local) for d in range(n_tp)]
     for d in range(n_tp):
-        at = pl.multiple_of((me ^ d) * rows_local, rows_local)
+        at = pl.multiple_of((me ^ reverse(n_tp)[d]) * rows_local, rows_local)
         ready[pl.ds(at, rows_local)] = pieces[d][...]
     total[...] = jnp.zeros_like(total)
     half = va_ref.shape[1] // HD

time: 65.9 us -> 64.5 us (0.979)
  starting transfers between devices: 27.3 us -> 24.9 us
  waiting for transfers between devices: 17.5 us -> 18.6 us
    ppermute x21, starting transfers between devices: 27.3 us -> 24.9 us  [pairs(): lax.ppermute(value, axis, [(i, i ^ d) for i in range(lax.axis_size(axis))])]
    ppermute x21, waiting for transfers between devices: 17.5 us -> 18.6 us  [pairs(): lax.ppermute(value, axis, [(i, i ^ d) for i in range(lax.axis_size(axis))])]
  transfers between devices with their start and end apart: 21 -> 21, of which waited for: 9 -> 14; matrix products, arithmetic and copies ran while one was open for 0% -> 0% of each run, Pallas kernels for 22% -> 22%
where the time goes in v15:
time: 64.5 us; the launch traced here: 64.2 us
  starting transfers between devices  24.9 us (39%)
  Pallas kernels  20.6 us (32%)
  waiting for transfers between devices  18.6 us (29%)
    ppermute x21, starting transfers between devices, pairs(): lax.ppermute(value, axis, [(i, i ^ d) for i in range(lax.axis_size(axis))])  24.9 us
    ppermute x21, waiting for transfers between devices, pairs(): lax.ppermute(value, axis, [(i, i ^ d) for i in range(lax.axis_size(axis))])  18.6 us
    pallas_call x1, Pallas kernels, load(): pl.pallas_call(functools.partial(load_kernel, pages, prompts, new_count),...  5.68 us
    pallas_call x2, Pallas kernels, project_values(): pl.pallas_call(functools.partial(values_kernel, first), in_specs=[VMEM] *...  4.68 us
    pallas_call x1, Pallas kernels, rotated_keys(): pl.pallas_call(keys_kernel, in_specs=[VMEM] * 3 + [hbm] * 2 + [VMEM] * 2...  3.62 us
    pallas_call x1, Pallas kernels, output_partial(): pl.pallas_call(functools.partial(output_kernel, n_seq), in_specs=[VMEM] *...  1.58 us
    pallas_call x1, Pallas kernels, partial_scores(): pl.pallas_call(functools.partial(scores_kernel, n_seq, n_tp), in_specs=[V...  1.35 us
  transfers between devices with their start and end apart: 21, of which 14 were waited for; matrix products, arithmetic and copies ran while one was open for 0% of the time, Pallas kernels for 22%

profile of v15, /device:TPU:0, one launch (start us, length us, event | category | flops | bytes accessed | tf_op | source)
XLA Modules:
  0.0 64.2 jit_solution(7777251578402897519)
XLA Ops:
  0.0 0.7 %prepare.1 = (bf16[2,2,16,128]{3,2,1,0:T(8,128)(2,1)S(1)}, f32[2,2,4,128]{3,2,1,0:T(4,128)S(1)}) custom-call(bf16[2,2,2048]{2,1,0:T(2,128)(2,1)} %q_ref.1, bf16[2,2,512]{2,1,0:T(2,128)(2,1)} %kv_ref.1), custom_call_target="tpu_custom_call" | custom-call | bytes 1048576 | tf_op jit(solution)/shard_map/prepare/pallas_call | solution.py:299
  0.7 4.1 %collective-permute-start.2 = (bf16[2,2,16,128]{3,2,1,0:T(8,128)(2,1)S(1)}, bf16[2,2,16,128]{3,2,1,0:T(8,128)(2,1)S(1)}, u32[]{:S(2)}, u32[]{:S(2)}) collective-permute-start(bf16[2,2,16,128]{3,2,1,0:T(8,128)(2,1)S(1)} %get-tuple-element.34.refs_0_), channel_id=1, source_target_pairs={{0,2},{1,3},{2,0},{3,1},{4,6},{5,7},{6,4},{7,5},{8,10},{9,11},{10,... | collective-permute-start | bytes 49160 | tf_op jit(solution)/shard_map/ppermute | solution.py:27
  4.8 1.3 %collective-permute-start.1 = (bf16[2,2,16,128]{3,2,1,0:T(8,128)(2,1)S(1)}, bf16[2,2,16,128]{3,2,1,0:T(8,128)(2,1)S(1)}, u32[]{:S(2)}, u32[]{:S(2)}) collective-permute-start(bf16[2,2,16,128]{3,2,1,0:T(8,128)(2,1)S(1)} %get-tuple-element.34.refs_0_), channel_id=1, source_target_pairs={{0,3},{1,2},{2,1},{3,0},{4,7},{5,6},{6,5},{7,4},{8,11},{9,10},{10,... | collective-permute-start | bytes 49160 | tf_op jit(solution)/shard_map/ppermute | solution.py:27
  6.4 5.7 %load.1 = (f32[1024,1024]{1,0:T(8,128)S(1)}, bf16[1024,1536]{1,0:T(8,128)(2,1)S(1)}, bf16[1536,2048]{1,0:T(8,128)(2,1)S(1)}, f32[1024,128]{1,0:T(8,128)S(1)}, f3...) custom-call(bf16[1024,2048]{1,0:T(8,128)(2,1)} %x_hbm.3, ...), custom_call_target="tpu_custom_call" | custom-call | flops 2147483648 | bytes 9437184 | tf_op jit(solution)/shard_map/load/pallas_call | solution.py:176
  12.3 1.6 %collective-permute-start.5 = (bf16[2,144,128]{2,1,0:T(8,128)(2,1)S(1)}, bf16[2,144,128]{2,1,0:T(8,128)(2,1)S(1)}, u32[]{:S(2)}, u32[]{:S(2)}) collective-permute-start(bf16[2,144,128]{2,1,0:T(8,128)(2,1)S(1)} %turned.1.after.refs_0_), channel_id=1, source_target_pairs={{0,8},{4,12},{8,0},{12,4},{1,9},{5,13},{9,1},{13,5},{2,10},{6,14},... | collective-permute-start | bytes 221192 | tf_op jit(solution)/shard_map/ppermute | solution.py:27
  13.8 0.6 collective-permute-start.3
  14.5 3.6 %keys.1 = (bf16[1024,1024]{1,0:T(8,128)(2,1)S(1)}, bf16[1024,512]{1,0:T(8,128)(2,1)S(1)}, bf16[512,2048]{1,0:T(8,128)(2,1)S(1)}) custom-call(f32[1024,1024]{1,0:T(8,128)S(1)} %get-tuple-element.38.acc, bf16[1024,1536]{1,0:T(8,128)(2,1)S(1)} %get-tuple-element.39.xa_ref, bf16[1536,2048]{1,0:T(8,128)(2,1)S(1)} %get-tuple-element.40.wa_ref, ...), custom_call_target="tpu_custom_call" | custom-call | flops 2147483648 | bytes 8388608 | tf_op jit(solution)/shard_map/keys/pallas_call | solution.py:225
  18.3 1.3 %scores.1 = (bf16[32,1024]{1,0:T(8,128)(2,1)S(1)}, bf16[32,1024]{1,0:T(8,128)(2,1)S(1)}, bf16[32,1024]{1,0:T(8,128)(2,1)S(1)}, bf16[32,1024]{1,0:T(8,128)(2,1)S(1)}) custom-call(bf16[2,144,128]{2,1,0:T(8,128)(2,1)S(1)} %turned.1.after.refs_0_, bf16[2,144,128]{2,1,0:T(8,128)(2,1)S(1)} %collective-permute-done.3.refs_1_, ...), custom_call_target="tpu_custom_call" | custom-call | flops 33554432 | bytes 6291456 | tf_op jit(solution)/shard_map/scores/pallas_call | solution.py:400
  19.6 2.9 %collective-permute-start.6 = (bf16[32,1024]{1,0:T(8,128)(2,1)S(1)}, bf16[32,1024]{1,0:T(8,128)(2,1)S(1)}, u32[]{:S(2)}, u32[]{:S(2)}) collective-permute-start(bf16[32,1024]{1,0:T(8,128)(2,1)S(1)} %get-tuple-element.46), channel_id=1, source_target_pairs={{0,2},{1,3},{2,0},{3,1},{4,6},{5,7},{6,4},{7,5},{8,10},{9,11},{10,... | collective-permute-start | bytes 196616 | tf_op jit(solution)/shard_map/ppermute | solution.py:27
  22.5 1.3 %collective-permute-start.7 = (bf16[32,1024]{1,0:T(8,128)(2,1)S(1)}, bf16[32,1024]{1,0:T(8,128)(2,1)S(1)}, u32[]{:S(2)}, u32[]{:S(2)}) collective-permute-start(bf16[32,1024]{1,0:T(8,128)(2,1)S(1)} %get-tuple-element.47), channel_id=1, source_target_pairs={{0,3},{1,2},{2,1},{3,0},{4,7},{5,6},{6,5},{7,4},{8,11},{9,10},{10,... | collective-permute-start | bytes 196616 | tf_op jit(solution)/shard_map/ppermute | solution.py:27
  23.8 2.3 %values.2 = (bf16[1024,512]{1,0:T(8,128)(2,1)S(1)}, bf16[1024,2048]{1,0:T(8,128)(2,1)S(1)}) custom-call(bf16[1024,1536]{1,0:T(8,128)(2,1)S(1)} %get-tuple-element.39.xa_ref, bf16[1536,2048]{1,0:T(8,128)(2,1)S(1)} %get-tuple-element.40.wa_ref, bf16[1024,512]{1,0:T(8,128)(2,1)S(1)} %get-tuple-element.49.xb_ref, ...), custom_call_target="tpu_custom_call" | custom-call | flops 1610612736 | bytes 8388608 | tf_op jit(solution)/shard_map/values/pallas_call | solution.py:267
  26.7 2.1 %collective-permute-done.7.refs_2_ = bf16[32,1024]{1,0:T(8,128)(2,1)S(1)} collective-permute-done((bf16[32,1024]{1,0:T(8,128)(2,1)S(1)}, bf16[32,1024]{1,0:T(8,128)(2,1)S(1)}, u32[]{:S(2)}, u32[]{:S(2)}) %collective-permute-start.7) | collective-permute-done | bytes 65568 | tf_op jit(solution)/shard_map/ppermute | solution.py:27
  28.9 0.9 %weights.1 = (bf16[32,1024]{1,0:T(8,128)(2,1)S(1)}, bf16[32,128]{1,0:T(8,128)(2,1)S(1)}) custom-call(bf16[32,1024]{1,0:T(8,128)(2,1)S(1)} %get-tuple-element.45.after.refs_0_, bf16[32,1024]{1,0:T(8,128)(2,1)S(1)} %collective-permute-done.6.refs_1_, bf16[32,1024]{1,0:T(8,128)(2,1)S(1)} %collective-permute-done.7.refs_2_, ...), custom_call_target="tpu_custom_call" | custom-call | tf_op jit(solution)/shard_map/weights/pallas_call | solution.py:512
  29.8 1.9 %collective-permute-start.11 = (bf16[32,1024]{1,0:T(8,128)(2,1)S(1)}, bf16[32,1024]{1,0:T(8,128)(2,1)S(1)}, u32[]{:S(2)}, u32[]{:S(2)}) collective-permute-start(bf16[32,1024]{1,0:T(8,128)(2,1)S(1)} %get-tuple-element.52.refs_0_), channel_id=1, source_target_pairs={{0,2},{1,3},{2,0},{3,1},{4,6},{5,7},{6,4},{7,5},{8,10},{9,11},{10,... | collective-permute-start | bytes 196616 | tf_op jit(solution)/shard_map/ppermute | solution.py:27
  31.7 1.2 %collective-permute-start.10 = (bf16[32,1024]{1,0:T(8,128)(2,1)S(1)}, bf16[32,1024]{1,0:T(8,128)(2,1)S(1)}, u32[]{:S(2)}, u32[]{:S(2)}) collective-permute-start(bf16[32,1024]{1,0:T(8,128)(2,1)S(1)} %get-tuple-element.52.refs_0_), channel_id=1, source_target_pairs={{0,3},{1,2},{2,1},{3,0},{4,7},{5,6},{6,5},{7,4},{8,11},{9,10},{10,... | collective-permute-start | bytes 196616 | tf_op jit(solution)/shard_map/ppermute | solution.py:27
  33.3 2.3 %values.3 = (bf16[1024,512]{1,0:T(8,128)(2,1)S(1)}, bf16[1024,2048]{1,0:T(8,128)(2,1)S(1)}) custom-call(bf16[1024,1536]{1,0:T(8,128)(2,1)S(1)} %get-tuple-element.39.xa_ref, bf16[1536,2048]{1,0:T(8,128)(2,1)S(1)} %get-tuple-element.40.wa_ref, bf16[1024,512]{1,0:T(8,128)(2,1)S(1)} %get-tuple-element.49.xb_ref, ...), custom_call_target="tpu_custom_call" | custom-call | flops 1610612736 | bytes 8388608 | tf_op jit(solution)/shard_map/values/pallas_call | solution.py:267
  35.6 1.0 %collective-permute-done.11.refs_3_ = bf16[32,1024]{1,0:T(8,128)(2,1)S(1)} collective-permute-done((bf16[32,1024]{1,0:T(8,128)(2,1)S(1)}, bf16[32,1024]{1,0:T(8,128)(2,1)S(1)}, u32[]{:S(2)}, u32[]{:S(2)}) %collective-permute-start.11) | collective-permute-done | bytes 65568 | tf_op jit(solution)/shard_map/ppermute | solution.py:27
  36.6 1.3 %collective-permute-done.10.refs_2_ = bf16[32,1024]{1,0:T(8,128)(2,1)S(1)} collective-permute-done((bf16[32,1024]{1,0:T(8,128)(2,1)S(1)}, bf16[32,1024]{1,0:T(8,128)(2,1)S(1)}, u32[]{:S(2)}, u32[]{:S(2)}) %collective-permute-start.10) | collective-permute-done | bytes 65568 | tf_op jit(solution)/shard_map/ppermute | solution.py:27
  38.0 1.1 %weighted.1 = (bf16[8,32,128]{2,1,0:T(8,128)(2,1)S(1)}, bf16[8,32,128]{2,1,0:T(8,128)(2,1)S(1)}, bf16[8,32,128]{2,1,0:T(8,128)(2,1)S(1)}, bf16[8,32,128]{2,1,0:T(8,128)(2,1)S(1)}) custom-call(bf16[32,1024]{1,0:T(8,128)(2,1)S(1)} %get-tuple-element.52.refs_0_, bf16[32,1024]{1,0:T(8,128)(2,1)S(1)} %collective-permute-done.9.refs_1_, ...), custom_call_target="tpu_custom_call" | custom-call | flops 33554432 | bytes 8388608 | tf_op jit(solution)/shard_map/weighted/pallas_call | solution.py:566
  39.1 1.8 %collective-permute-start.12 = (bf16[8,32,128]{2,1,0:T(8,128)(2,1)S(1)}, bf16[8,32,128]{2,1,0:T(8,128)(2,1)S(1)}, u32[]{:S(2)}, u32[]{:S(2)}) collective-permute-start(bf16[8,32,128]{2,1,0:T(8,128)(2,1)S(1)} %get-tuple-element.56), channel_id=1, source_target_pairs={{0,2},{1,3},{2,0},{3,1},{4,6},{5,7},{6,4},{7,5},{8,10},{9,11},{10,... | collective-permute-start | bytes 196616 | tf_op jit(solution)/shard_map/ppermute | solution.py:27
  40.8 1.2 %collective-permute-start.13 = (bf16[8,32,128]{2,1,0:T(8,128)(2,1)S(1)}, bf16[8,32,128]{2,1,0:T(8,128)(2,1)S(1)}, u32[]{:S(2)}, u32[]{:S(2)}) collective-permute-start(bf16[8,32,128]{2,1,0:T(8,128)(2,1)S(1)} %get-tuple-element.57), channel_id=1, source_target_pairs={{0,3},{1,2},{2,1},{3,0},{4,7},{5,6},{6,5},{7,4},{8,11},{9,10},{10,... | collective-permute-start | bytes 196616 | tf_op jit(solution)/shard_map/ppermute | solution.py:27
  42.6 3.1 %collective-permute-done.12.refs_1_ = bf16[8,32,128]{2,1,0:T(8,128)(2,1)S(1)} collective-permute-done((bf16[8,32,128]{2,1,0:T(8,128)(2,1)S(1)}, bf16[8,32,128]{2,1,0:T(8,128)(2,1)S(1)}, u32[]{:S(2)}, u32[]{:S(2)}) %collective-permute-start.12) | collective-permute-done | bytes 65568 | tf_op jit(solution)/shard_map/ppermute | solution.py:27
  45.7 1.3 %collective-permute-done.13.refs_2_ = bf16[8,32,128]{2,1,0:T(8,128)(2,1)S(1)} collective-permute-done((bf16[8,32,128]{2,1,0:T(8,128)(2,1)S(1)}, bf16[8,32,128]{2,1,0:T(8,128)(2,1)S(1)}, u32[]{:S(2)}, u32[]{:S(2)}) %collective-permute-start.13) | collective-permute-done | bytes 65568 | tf_op jit(solution)/shard_map/ppermute | solution.py:27
  47.2 1.6 %collective-permute-start.17 = (bf16[9,32,128]{2,1,0:T(8,128)(2,1)S(1)}, bf16[9,32,128]{2,1,0:T(8,128)(2,1)S(1)}, u32[]{:S(2)}, u32[]{:S(2)}) collective-permute-start(bf16[9,32,128]{2,1,0:T(8,128)(2,1)S(1)} %summed.1.refs_0_), channel_id=1, source_target_pairs={{0,8},{4,12},{8,0},{12,4},{1,9},{5,13},{9,1},{13,5},{2,10},{6,14},... | collective-permute-start | bytes 221192 | tf_op jit(solution)/shard_map/ppermute | solution.py:27
  49.5 2.1 %collective-permute-done.17.refs_3_ = bf16[9,32,128]{2,1,0:T(8,128)(2,1)S(1)} collective-permute-done((bf16[9,32,128]{2,1,0:T(8,128)(2,1)S(1)}, bf16[9,32,128]{2,1,0:T(8,128)(2,1)S(1)}, u32[]{:S(2)}, u32[]{:S(2)}) %collective-permute-start.17) | collective-permute-done | bytes 73760 | tf_op jit(solution)/shard_map/ppermute | solution.py:27
  51.6 1.6 %collective-permute-done.16.refs_2_ = bf16[9,32,128]{2,1,0:T(8,128)(2,1)S(1)} collective-permute-done((bf16[9,32,128]{2,1,0:T(8,128)(2,1)S(1)}, bf16[9,32,128]{2,1,0:T(8,128)(2,1)S(1)}, u32[]{:S(2)}, u32[]{:S(2)}) %collective-permute-start.16) | collective-permute-done | bytes 73760 | tf_op jit(solution)/shard_map/ppermute | solution.py:27
  53.2 1.6 %output.1.refs_0_ = bf16[16,2048]{1,0:T(8,128)(2,1)S(1)} custom-call(bf16[9,32,128]{2,1,0:T(8,128)(2,1)S(1)} %summed.1.refs_0_, bf16[9,32,128]{2,1,0:T(8,128)(2,1)S(1)} %collective-permute-done.15.refs_1_, bf16[9,32,128]{2,1,0:T(8,128)(2,1)S(1)} %collective-permute-done.16.refs_2_, bf16[9,32,128]{2,1,0:T(8,128)(2,1)S(1)} %collective-permute-done.17.refs_3_, ...), custom_call_target="tpu_custom_call" | custom-call | tf_op jit(solution)/shard_map/output/pallas_call | solution.py:660
  54.8 1.1 %collective-permute-start.20 = (bf16[16,2048]{1,0:T(8,128)(2,1)S(1)}, bf16[16,2048]{1,0:T(8,128)(2,1)S(1)}, u32[]{:S(2)}, u32[]{:S(2)}) collective-permute-start(bf16[16,2048]{1,0:T(8,128)(2,1)S(1)} %output.1.refs_0_), channel_id=1, source_target_pairs={{0,2},{1,3},{2,0},{3,1},{4,6},{5,7},{6,4},{7,5},{8,10},{9,11},{10,... | collective-permute-start | bytes 196616 | tf_op jit(solution)/shard_map/ppermute | solution.py:27
  55.8 1.9 %collective-permute-start.19 = (bf16[16,2048]{1,0:T(8,128)(2,1)S(1)}, bf16[16,2048]{1,0:T(8,128)(2,1)S(1)}, u32[]{:S(2)}, u32[]{:S(2)}) collective-permute-start(bf16[16,2048]{1,0:T(8,128)(2,1)S(1)} %output.1.refs_0_), channel_id=1, source_target_pairs={{0,3},{1,2},{2,1},{3,0},{4,7},{5,6},{6,5},{7,4},{8,11},{9,10},{10,... | collective-permute-start | bytes 196616 | tf_op jit(solution)/shard_map/ppermute | solution.py:27
  58.2 4.5 %collective-permute-done.20.refs_3_ = bf16[16,2048]{1,0:T(8,128)(2,1)S(1)} collective-permute-done((bf16[16,2048]{1,0:T(8,128)(2,1)S(1)}, bf16[16,2048]{1,0:T(8,128)(2,1)S(1)}, u32[]{:S(2)}, u32[]{:S(2)}) %collective-permute-start.20) | collective-permute-done | bytes 65568 | tf_op jit(solution)/shard_map/ppermute | solution.py:27
  62.7 0.8 %collective-permute-done.18.refs_1_ = bf16[16,2048]{1,0:T(8,128)(2,1)S(1)} collective-permute-done((bf16[16,2048]{1,0:T(8,128)(2,1)S(1)}, bf16[16,2048]{1,0:T(8,128)(2,1)S(1)}, u32[]{:S(2)}, u32[]{:S(2)}) %collective-permute-start.18) | collective-permute-done | bytes 65568 | tf_op jit(solution)/shard_map/ppermute | solution.py:27
  63.5 0.7 %final.1 = f32[8,2,2048]{2,1,0:T(2,128)} custom-call(bf16[16,2048]{1,0:T(8,128)(2,1)S(1)} %output.1.refs_0_, bf16[16,2048]{1,0:T(8,128)(2,1)S(1)} %collective-permute-done.18.refs_1_, bf16[16,2048]{1,0:T(8,128)(2,1)S(1)} %collective-permute-done.19.refs_2_, bf16[16,2048]{1,0:T(8,128)(2,1)S(1)} %collective-permute-done.20.refs_3_, bf16[8,2,2048]{2,1,0:T(2,128)(2,1)S(1)} %copy-done), custom_call_target="tpu_custom_call" | custom-call | tf_op jit(solution)/shard_map/final/pallas_call | solution.py:684
  (25 shorter events, 3.6 us)
Async XLA Ops:
  0.7 11.4 %collective-permute-start.2 = (bf16[2,2,16,128]{3,2,1,0:T(8,128)(2,1)S(1)}, bf16[2,2,16,128]{3,2,1,0:T(8,128)(2,1)S(1)}, u32[]{:S(2)}, u32[]{:S(2)}) collective-permute-start(bf16[2,2,16,128]{3,2,1,0:T(8,128)(2,1)S(1)} %get-tuple-element.34.refs_0_), channel_id=1, source_target_pairs={{0,2},{1,3},{2,0},{3,1},{4,6},{5,7},{6,4},{7,5},{8,10},{9,11},{10,... | collective-permute-start | bytes 49160 | tf_op jit(solution)/shard_map/ppermute | solution.py:27
  4.8 7.3 %collective-permute-start.1 = (bf16[2,2,16,128]{3,2,1,0:T(8,128)(2,1)S(1)}, bf16[2,2,16,128]{3,2,1,0:T(8,128)(2,1)S(1)}, u32[]{:S(2)}, u32[]{:S(2)}) collective-permute-start(bf16[2,2,16,128]{3,2,1,0:T(8,128)(2,1)S(1)} %get-tuple-element.34.refs_0_), channel_id=1, source_target_pairs={{0,3},{1,2},{2,1},{3,0},{4,7},{5,6},{6,5},{7,4},{8,11},{9,10},{10,... | collective-permute-start | bytes 49160 | tf_op jit(solution)/shard_map/ppermute | solution.py:27
  6.2 5.9 %collective-permute-start = (bf16[2,2,16,128]{3,2,1,0:T(8,128)(2,1)S(1)}, bf16[2,2,16,128]{3,2,1,0:T(8,128)(2,1)S(1)}, u32[]{:S(2)}, u32[]{:S(2)}) collective-permute-start(bf16[2,2,16,128]{3,2,1,0:T(8,128)(2,1)S(1)} %get-tuple-element.34.refs_0_), channel_id=1, source_target_pairs={{0,1},{1,0},{2,3},{3,2},{4,5},{5,4},{6,7},{7,6},{8,9},{9,8},{10,11... | collective-permute-start | bytes 49160 | tf_op jit(solution)/shard_map/ppermute | solution.py:27
  12.3 5.8 %collective-permute-start.5 = (bf16[2,144,128]{2,1,0:T(8,128)(2,1)S(1)}, bf16[2,144,128]{2,1,0:T(8,128)(2,1)S(1)}, u32[]{:S(2)}, u32[]{:S(2)}) collective-permute-start(bf16[2,144,128]{2,1,0:T(8,128)(2,1)S(1)} %turned.1.after.refs_0_), channel_id=1, source_target_pairs={{0,8},{4,12},{8,0},{12,4},{1,9},{5,13},{9,1},{13,5},{2,10},{6,14},... | collective-permute-start | bytes 221192 | tf_op jit(solution)/shard_map/ppermute | solution.py:27
  13.8 4.4 %collective-permute-start.4 = (bf16[2,144,128]{2,1,0:T(8,128)(2,1)S(1)}, bf16[2,144,128]{2,1,0:T(8,128)(2,1)S(1)}, u32[]{:S(2)}, u32[]{:S(2)}) collective-permute-start(bf16[2,144,128]{2,1,0:T(8,128)(2,1)S(1)} %turned.1.after.refs_0_), channel_id=1, source_target_pairs={{0,12},{4,8},{8,4},{12,0},{1,13},{5,9},{9,5},{13,1},{2,14},{6,10},... | collective-permute-start | bytes 221192 | tf_op jit(solution)/shard_map/ppermute | solution.py:27
  13.8 4.4 %collective-permute-start.3 = (bf16[2,144,128]{2,1,0:T(8,128)(2,1)S(1)}, bf16[2,144,128]{2,1,0:T(8,128)(2,1)S(1)}, u32[]{:S(2)}, u32[]{:S(2)}) collective-permute-start(bf16[2,144,128]{2,1,0:T(8,128)(2,1)S(1)} %turned.1.after.refs_0_), channel_id=1, source_target_pairs={{0,4},{4,0},{8,12},{12,8},{1,5},{5,1},{9,13},{13,9},{2,6},{6,2},{1... | collective-permute-start | bytes 221192 | tf_op jit(solution)/shard_map/ppermute | solution.py:27
  19.6 7.1 %collective-permute-start.6 = (bf16[32,1024]{1,0:T(8,128)(2,1)S(1)}, bf16[32,1024]{1,0:T(8,128)(2,1)S(1)}, u32[]{:S(2)}, u32[]{:S(2)}) collective-permute-start(bf16[32,1024]{1,0:T(8,128)(2,1)S(1)} %get-tuple-element.46), channel_id=1, source_target_pairs={{0,2},{1,3},{2,0},{3,1},{4,6},{5,7},{6,4},{7,5},{8,10},{9,11},{10,... | collective-permute-start | bytes 196616 | tf_op jit(solution)/shard_map/ppermute | solution.py:27
  22.5 6.3 %collective-permute-start.7 = (bf16[32,1024]{1,0:T(8,128)(2,1)S(1)}, bf16[32,1024]{1,0:T(8,128)(2,1)S(1)}, u32[]{:S(2)}, u32[]{:S(2)}) collective-permute-start(bf16[32,1024]{1,0:T(8,128)(2,1)S(1)} %get-tuple-element.47), channel_id=1, source_target_pairs={{0,3},{1,2},{2,1},{3,0},{4,7},{5,6},{6,5},{7,4},{8,11},{9,10},{10,... | collective-permute-start | bytes 196616 | tf_op jit(solution)/shard_map/ppermute | solution.py:27
  23.8 5.1 %collective-permute-start.8 = (bf16[32,1024]{1,0:T(8,128)(2,1)S(1)}, bf16[32,1024]{1,0:T(8,128)(2,1)S(1)}, u32[]{:S(2)}, u32[]{:S(2)}) collective-permute-start(bf16[32,1024]{1,0:T(8,128)(2,1)S(1)} %get-tuple-element.48), channel_id=1, source_target_pairs={{0,1},{1,0},{2,3},{3,2},{4,5},{5,4},{6,7},{7,6},{8,9},{9,8},{10,11... | collective-permute-start | bytes 196616 | tf_op jit(solution)/shard_map/ppermute | solution.py:27
  29.8 6.8 %collective-permute-start.11 = (bf16[32,1024]{1,0:T(8,128)(2,1)S(1)}, bf16[32,1024]{1,0:T(8,128)(2,1)S(1)}, u32[]{:S(2)}, u32[]{:S(2)}) collective-permute-start(bf16[32,1024]{1,0:T(8,128)(2,1)S(1)} %get-tuple-element.52.refs_0_), channel_id=1, source_target_pairs={{0,2},{1,3},{2,0},{3,1},{4,6},{5,7},{6,4},{7,5},{8,10},{9,11},{10,... | collective-permute-start | bytes 196616 | tf_op jit(solution)/shard_map/ppermute | solution.py:27
  31.7 6.2 %collective-permute-start.10 = (bf16[32,1024]{1,0:T(8,128)(2,1)S(1)}, bf16[32,1024]{1,0:T(8,128)(2,1)S(1)}, u32[]{:S(2)}, u32[]{:S(2)}) collective-permute-start(bf16[32,1024]{1,0:T(8,128)(2,1)S(1)} %get-tuple-element.52.refs_0_), channel_id=1, source_target_pairs={{0,3},{1,2},{2,1},{3,0},{4,7},{5,6},{6,5},{7,4},{8,11},{9,10},{10,... | collective-permute-start | bytes 196616 | tf_op jit(solution)/shard_map/ppermute | solution.py:27
  32.9 5.1 %collective-permute-start.9 = (bf16[32,1024]{1,0:T(8,128)(2,1)S(1)}, bf16[32,1024]{1,0:T(8,128)(2,1)S(1)}, u32[]{:S(2)}, u32[]{:S(2)}) collective-permute-start(bf16[32,1024]{1,0:T(8,128)(2,1)S(1)} %get-tuple-element.52.refs_0_), channel_id=1, source_target_pairs={{0,1},{1,0},{2,3},{3,2},{4,5},{5,4},{6,7},{7,6},{8,9},{9,8},{10,11... | collective-permute-start | bytes 196616 | tf_op jit(solution)/shard_map/ppermute | solution.py:27
  39.1 6.6 %collective-permute-start.12 = (bf16[8,32,128]{2,1,0:T(8,128)(2,1)S(1)}, bf16[8,32,128]{2,1,0:T(8,128)(2,1)S(1)}, u32[]{:S(2)}, u32[]{:S(2)}) collective-permute-start(bf16[8,32,128]{2,1,0:T(8,128)(2,1)S(1)} %get-tuple-element.56), channel_id=1, source_target_pairs={{0,2},{1,3},{2,0},{3,1},{4,6},{5,7},{6,4},{7,5},{8,10},{9,11},{10,... | collective-permute-start | bytes 196616 | tf_op jit(solution)/shard_map/ppermute | solution.py:27
  40.8 6.2 %collective-permute-start.13 = (bf16[8,32,128]{2,1,0:T(8,128)(2,1)S(1)}, bf16[8,32,128]{2,1,0:T(8,128)(2,1)S(1)}, u32[]{:S(2)}, u32[]{:S(2)}) collective-permute-start(bf16[8,32,128]{2,1,0:T(8,128)(2,1)S(1)} %get-tuple-element.57), channel_id=1, source_target_pairs={{0,3},{1,2},{2,1},{3,0},{4,7},{5,6},{6,5},{7,4},{8,11},{9,10},{10,... | collective-permute-start | bytes 196616 | tf_op jit(solution)/shard_map/ppermute | solution.py:27
  42.1 5.0 %collective-permute-start.14 = (bf16[8,32,128]{2,1,0:T(8,128)(2,1)S(1)}, bf16[8,32,128]{2,1,0:T(8,128)(2,1)S(1)}, u32[]{:S(2)}, u32[]{:S(2)}) collective-permute-start(bf16[8,32,128]{2,1,0:T(8,128)(2,1)S(1)} %get-tuple-element.58), channel_id=1, source_target_pairs={{0,1},{1,0},{2,3},{3,2},{4,5},{5,4},{6,7},{7,6},{8,9},{9,8},{10,11... | collective-permute-start | bytes 196616 | tf_op jit(solution)/shard_map/ppermute | solution.py:27
  47.2 4.4 %collective-permute-start.17 = (bf16[9,32,128]{2,1,0:T(8,128)(2,1)S(1)}, bf16[9,32,128]{2,1,0:T(8,128)(2,1)S(1)}, u32[]{:S(2)}, u32[]{:S(2)}) collective-permute-start(bf16[9,32,128]{2,1,0:T(8,128)(2,1)S(1)} %summed.1.refs_0_), channel_id=1, source_target_pairs={{0,8},{4,12},{8,0},{12,4},{1,9},{5,13},{9,1},{13,5},{2,10},{6,14},... | collective-permute-start | bytes 221192 | tf_op jit(solution)/shard_map/ppermute | solution.py:27
  48.8 4.4 %collective-permute-start.16 = (bf16[9,32,128]{2,1,0:T(8,128)(2,1)S(1)}, bf16[9,32,128]{2,1,0:T(8,128)(2,1)S(1)}, u32[]{:S(2)}, u32[]{:S(2)}) collective-permute-start(bf16[9,32,128]{2,1,0:T(8,128)(2,1)S(1)} %summed.1.refs_0_), channel_id=1, source_target_pairs={{0,12},{4,8},{8,4},{12,0},{1,13},{5,9},{9,5},{13,1},{2,14},{6,10},... | collective-permute-start | bytes 221192 | tf_op jit(solution)/shard_map/ppermute | solution.py:27
  48.8 4.4 %collective-permute-start.15 = (bf16[9,32,128]{2,1,0:T(8,128)(2,1)S(1)}, bf16[9,32,128]{2,1,0:T(8,128)(2,1)S(1)}, u32[]{:S(2)}, u32[]{:S(2)}) collective-permute-start(bf16[9,32,128]{2,1,0:T(8,128)(2,1)S(1)} %summed.1.refs_0_), channel_id=1, source_target_pairs={{0,4},{4,0},{8,12},{12,8},{1,5},{5,1},{9,13},{13,9},{2,6},{6,2},{1... | collective-permute-start | bytes 221192 | tf_op jit(solution)/shard_map/ppermute | solution.py:27
  53.2 10.3 %copy-start = (bf16[8,2,2048]{2,1,0:T(2,128)(2,1)S(1)}, bf16[8,2,2048]{2,1,0:T(2,128)(2,1)}, u32[]{:S(2)}) copy-start(bf16[8,2,2048]{2,1,0:T(2,128)(2,1)} %refs_4_.1) | copy-start | bytes 196612
  54.8 8.0 %collective-permute-start.20 = (bf16[16,2048]{1,0:T(8,128)(2,1)S(1)}, bf16[16,2048]{1,0:T(8,128)(2,1)S(1)}, u32[]{:S(2)}, u32[]{:S(2)}) collective-permute-start(bf16[16,2048]{1,0:T(8,128)(2,1)S(1)} %output.1.refs_0_), channel_id=1, source_target_pairs={{0,2},{1,3},{2,0},{3,1},{4,6},{5,7},{6,4},{7,5},{8,10},{9,11},{10,... | collective-permute-start | bytes 196616 | tf_op jit(solution)/shard_map/ppermute | solution.py:27
  55.8 6.9 %collective-permute-start.19 = (bf16[16,2048]{1,0:T(8,128)(2,1)S(1)}, bf16[16,2048]{1,0:T(8,128)(2,1)S(1)}, u32[]{:S(2)}, u32[]{:S(2)}) collective-permute-start(bf16[16,2048]{1,0:T(8,128)(2,1)S(1)} %output.1.refs_0_), channel_id=1, source_target_pairs={{0,3},{1,2},{2,1},{3,0},{4,7},{5,6},{6,5},{7,4},{8,11},{9,10},{10,... | collective-permute-start | bytes 196616 | tf_op jit(solution)/shard_map/ppermute | solution.py:27
  57.7 5.8 %collective-permute-start.18 = (bf16[16,2048]{1,0:T(8,128)(2,1)S(1)}, bf16[16,2048]{1,0:T(8,128)(2,1)S(1)}, u32[]{:S(2)}, u32[]{:S(2)}) collective-permute-start(bf16[16,2048]{1,0:T(8,128)(2,1)S(1)} %output.1.refs_0_), channel_id=1, source_target_pairs={{0,1},{1,0},{2,3},{3,2},{4,5},{5,4},{6,7},{7,6},{8,9},{9,8},{10,11... | collective-permute-start | bytes 196616 | tf_op jit(solution)/shard_map/ppermute | solution.py:27

commit v16 on v15

--- a/solution.py
+++ b/solution.py
@@ -44,8 +44,13 @@
     return [chunks[0]] + [pairs(c, axis, d) for c, d in zip(chunks[1:], offsets[1:])]
 
 
-def gather(value, axis):
-    return [value] + [pairs(value, axis, d) for d in reverse(lax.axis_size(axis))[1:]]
+def gather(value, axis, offsets=None):
+    offsets = offsets or reverse(lax.axis_size(axis))
+    return [value] + [pairs(value, axis, d) for d in offsets[1:]]
+
+
+def falling(size):
+    return [0] + list(range(size - 1, 0, -1))
 
 
 def lane_freqs(rows):
@@ -136,7 +141,7 @@
 
 def add_block(x_ref, w_ref, rows, acc, out, fresh):
     tokens = x_ref.shape[0]
-    tall = tokens // 2
+    tall = tokens
     for pair in range(KVH // 2):
         weight = pair_columns(w_ref, rows, pair, 0)
         columns = slice(2 * pair * HD, 2 * (pair + 1) * HD)
@@ -200,7 +205,7 @@
 
 def keys_kernel(acc, xa_ref, wa_ref, x_hbm, w_hbm, cos_ref, sin_ref, after, k_ref, x_ref, w_ref, total, sems):
     tokens, size = x_ref.shape
-    tall = tokens // 2
+    tall = tokens
     (copies,) = copies_of(x_hbm, w_hbm, x_ref, w_ref, sems, 3 * size, size, 1)
     start(copies)
     add_block(xa_ref, wa_ref, slice(2 * size, 3 * size), acc, total, False)
@@ -285,36 +290,11 @@
     return jnp.concatenate([row[:, c : c + HD] for c in range(0, row.shape[1], HD)], axis=0)
 
 
-def prepare_kernel(q_ref, kv_ref, q_out, kv_out):
-    for r in range(q_ref.shape[0]):
-        q, kv = q_ref[r].astype(F32), kv_ref[r].astype(F32)
-        for n in range(q_ref.shape[1]):
-            q_out[r, n] = by_heads(q[n : n + 1]).astype(BF16)
-            kv_out[r, n] = by_heads(kv[n : n + 1])
-
-
-def prepare(new_query, new_keyval):
-    own_rows, new_count, columns = new_query.shape
-    shape = lambda a: (own_rows, new_count, a.shape[2] // HD, HD)
-    return pl.pallas_call(
-        prepare_kernel,
-        in_specs=[VMEM, VMEM],
-        out_specs=[VMEM, VMEM],
-        out_shape=[
-            jax.ShapeDtypeStruct(shape(new_query), BF16),
-            jax.ShapeDtypeStruct(shape(new_keyval), F32),
-        ],
-        compiler_params=pltpu.CompilerParams(vmem_limit_bytes=8 * MIB),
-        cost_estimate=pl.CostEstimate(flops=0, bytes_accessed=MIB, transcendentals=0),
-        name="prepare",
-    )(in_hbm(new_query), in_hbm(new_keyval))
-
-
 def turned_kernel(n_tp, *refs):
     kv_ref, cos_q, sin_q, out_ref = refs[n_tp:]
-    own_rows, new_count, heads, _ = refs[0].shape
+    own_rows, new_count, columns = refs[0].shape
     rows = new_count * GROUP
-    kv_local = heads // GROUP
+    kv_local = columns // HD // GROUP
     me, seq = lax.axis_index("tp"), lax.axis_index("seq")
     for r in range(own_rows):
         spots = [pl.ds((seq * own_rows + r) * new_count + n, 1) for n in range(new_count)]
@@ -324,16 +304,19 @@
             return value * turns[n][0] + pltpu.roll(value, HD // 2, 1) * turns[n][1]
 
         for d in range(n_tp):
-            blocks = [refs[d][r, n].astype(F32) for n in range(new_count)]
+            raw = refs[d][r].astype(F32)
+            blocks = [by_heads(raw[n : n + 1]) for n in range(new_count)]
             for g in range(kv_local):
                 parts = [turn(q[g * GROUP : (g + 1) * GROUP], n) for n, q in enumerate(blocks)]
-                at = ((me ^ reverse(n_tp)[d]) * kv_local + g) * rows
+                at = ((me ^ falling(n_tp)[d]) * kv_local + g) * rows
                 at = pl.ds(pl.multiple_of(at, rows), rows)
                 out_ref[r, at] = jnp.concatenate(parts, axis=0).astype(BF16)
+        raw = kv_ref[r].astype(F32)
         fresh = []
         for n in range(new_count):
-            row = lax.broadcasted_iota(jnp.int32, kv_ref.shape[2:], 0)
-            fresh.append(jnp.where(row % 2 == 0, turn(kv_ref[r, n], n), kv_ref[r, n]))
+            kv = by_heads(raw[n : n + 1])
+            row = lax.broadcasted_iota(jnp.int32, kv.shape, 0)
+            fresh.append(jnp.where(row % 2 == 0, turn(kv, n), kv))
         fresh.append(jnp.zeros((FRESH - new_count * 2 * kv_local, HD), F32))
         out_ref[r, KVH * rows :] = jnp.concatenate(fresh, axis=0).astype(BF16)
 
@@ -343,7 +326,7 @@
 
 def turned(pieces, fresh, cos_q, sin_q):
     n_tp = len(pieces)
-    own_rows, new_count, _, _ = pieces[0].shape
+    own_rows, new_count, _ = pieces[0].shape
     rows = KVH * GROUP * new_count + FRESH
     return pl.pallas_call(
         functools.partial(turned_kernel, n_tp),
@@ -698,12 +681,11 @@
     own_rows, new_count, _ = new_query.shape
     prompts = page_counts.shape[0]
     pages = prefill_states.shape[0] // PAGE * n_seq
-    query, new_kv = prepare(new_query, new_keyval)
-    query = gather(query, "tp")
+    query = gather(new_query, "tp", falling(n_tp))
     acc, xa, wa, cosine, sine, cos_q, sin_q, meta = load(
         prefill_states, kv_weight, page_counts, tail_tokens, pages, new_count
     )
-    new = turned(query, new_kv, cos_q, sin_q)
+    new = turned(query, new_keyval, cos_q, sin_q)
     k, xb, wb = rotated_keys(acc, xa, wa, prefill_states, kv_weight, cosine, sine, new)
     new = gather(new, "seq")
     scores = partial_scores(new, k, meta, prompts, n_tp)

time: 64.5 us -> 63.5 us (0.984)
    pallas_call x1 -> x0, Pallas kernels: 0.74 us -> none  [prepare(): pl.pallas_call(prepare_kernel, in_specs=[VMEM, VMEM], out_specs=[VMEM, VM...]
  transfers between devices with their start and end apart: 21 -> 21, of which waited for: 14 -> 14; matrix products, arithmetic and copies ran while one was open for 0% -> 0% of each run, Pallas kernels for 22% -> 23%
where the time goes in v16:
time: 63.5 us; the launch traced here: 63.4 us
  starting transfers between devices  24.8 us (39%)
  Pallas kernels  20.1 us (32%)
  waiting for transfers between devices  18.4 us (29%)
    ppermute x21, starting transfers between devices, pairs(): lax.ppermute(value, axis, [(i, i ^ d) for i in range(lax.axis_size(axis))])  24.8 us
    ppermute x21, waiting for transfers between devices, pairs(): lax.ppermute(value, axis, [(i, i ^ d) for i in range(lax.axis_size(axis))])  18.4 us
    pallas_call x1, Pallas kernels, load(): pl.pallas_call(functools.partial(load_kernel, pages, prompts, new_count),...  5.77 us
    pallas_call x2, Pallas kernels, project_values(): pl.pallas_call(functools.partial(values_kernel, first), in_specs=[VMEM] *...  4.68 us
    pallas_call x1, Pallas kernels, rotated_keys(): pl.pallas_call(keys_kernel, in_specs=[VMEM] * 3 + [hbm] * 2 + [VMEM] * 2...  3.68 us
    pallas_call x1, Pallas kernels, output_partial(): pl.pallas_call(functools.partial(output_kernel, n_seq), in_specs=[VMEM] *...  1.58 us
    pallas_call x1, Pallas kernels, partial_scores(): pl.pallas_call(functools.partial(scores_kernel, n_seq, n_tp), in_specs=[V...  1.35 us
  transfers between devices with their start and end apart: 21, of which 14 were waited for; matrix products, arithmetic and copies ran while one was open for 0% of the time, Pallas kernels for 23%

profile of v16, /device:TPU:0, one launch (start us, length us, event | category | flops | bytes accessed | tf_op | source)
XLA Modules:
  0.0 63.4 jit_solution(251398531559293300)
XLA Ops:
  0.0 4.0 %collective-permute-start.1 = (bf16[2,2,2048]{2,1,0:T(2,128)(2,1)}, bf16[2,2,2048]{2,1,0:T(2,128)(2,1)S(1)}, u32[]{:S(2)}, u32[]{:S(2)}) collective-permute-start(bf16[2,2,2048]{2,1,0:T(2,128)(2,1)} %refs_0_.1), channel_id=1, source_target_pairs={{0,2},{1,3},{2,0},{3,1},{4,6},{5,7},{6,4},{7,5},{8,10},{9,11},{10,... | collective-permute-start | bytes 49160 | tf_op jit(solution)/shard_map/ppermute | solution.py:27
  4.0 1.3 %collective-permute-start = (bf16[2,2,2048]{2,1,0:T(2,128)(2,1)}, bf16[2,2,2048]{2,1,0:T(2,128)(2,1)S(1)}, u32[]{:S(2)}, u32[]{:S(2)}) collective-permute-start(bf16[2,2,2048]{2,1,0:T(2,128)(2,1)} %refs_0_.1), channel_id=1, source_target_pairs={{0,3},{1,2},{2,1},{3,0},{4,7},{5,6},{6,5},{7,4},{8,11},{9,10},{10,... | collective-permute-start | bytes 49160 | tf_op jit(solution)/shard_map/ppermute | solution.py:27
  5.6 5.8 %load.1 = (f32[1024,1024]{1,0:T(8,128)S(1)}, bf16[1024,1536]{1,0:T(8,128)(2,1)S(1)}, bf16[1536,2048]{1,0:T(8,128)(2,1)S(1)}, f32[1024,128]{1,0:T(8,128)S(1)}, f3...) custom-call(bf16[1024,2048]{1,0:T(8,128)(2,1)} %x_hbm.3, ...), custom_call_target="tpu_custom_call" | custom-call | flops 2147483648 | bytes 9437184 | tf_op jit(solution)/shard_map/load/pallas_call | solution.py:181
  11.6 1.6 %collective-permute-start.5 = (bf16[2,144,128]{2,1,0:T(8,128)(2,1)S(1)}, bf16[2,144,128]{2,1,0:T(8,128)(2,1)S(1)}, u32[]{:S(2)}, u32[]{:S(2)}) collective-permute-start(bf16[2,144,128]{2,1,0:T(8,128)(2,1)S(1)} %turned.1.after.refs_0_), channel_id=1, source_target_pairs={{0,8},{4,12},{8,0},{12,4},{1,9},{5,13},{9,1},{13,5},{2,10},{6,14},... | collective-permute-start | bytes 221192 | tf_op jit(solution)/shard_map/ppermute | solution.py:27
  13.2 0.6 collective-permute-start.3
  13.8 3.7 %keys.1 = (bf16[1024,1024]{1,0:T(8,128)(2,1)S(1)}, bf16[1024,512]{1,0:T(8,128)(2,1)S(1)}, bf16[512,2048]{1,0:T(8,128)(2,1)S(1)}) custom-call(f32[1024,1024]{1,0:T(8,128)S(1)} %get-tuple-element.34.acc, bf16[1024,1536]{1,0:T(8,128)(2,1)S(1)} %get-tuple-element.35.xa_ref, bf16[1536,2048]{1,0:T(8,128)(2,1)S(1)} %get-tuple-element.36.wa_ref, ...), custom_call_target="tpu_custom_call" | custom-call | flops 2147483648 | bytes 8388608 | tf_op jit(solution)/shard_map/keys/pallas_call | solution.py:230
  17.6 1.3 %scores.1 = (bf16[32,1024]{1,0:T(8,128)(2,1)S(1)}, bf16[32,1024]{1,0:T(8,128)(2,1)S(1)}, bf16[32,1024]{1,0:T(8,128)(2,1)S(1)}, bf16[32,1024]{1,0:T(8,128)(2,1)S(1)}) custom-call(bf16[2,144,128]{2,1,0:T(8,128)(2,1)S(1)} %turned.1.after.refs_0_, bf16[2,144,128]{2,1,0:T(8,128)(2,1)S(1)} %collective-permute-done.3.refs_1_, ...), custom_call_target="tpu_custom_call" | custom-call | flops 33554432 | bytes 6291456 | tf_op jit(solution)/shard_map/scores/pallas_call | solution.py:383
  19.0 2.9 %collective-permute-start.6 = (bf16[32,1024]{1,0:T(8,128)(2,1)S(1)}, bf16[32,1024]{1,0:T(8,128)(2,1)S(1)}, u32[]{:S(2)}, u32[]{:S(2)}) collective-permute-start(bf16[32,1024]{1,0:T(8,128)(2,1)S(1)} %get-tuple-element.42), channel_id=1, source_target_pairs={{0,2},{1,3},{2,0},{3,1},{4,6},{5,7},{6,4},{7,5},{8,10},{9,11},{10,... | collective-permute-start | bytes 196616 | tf_op jit(solution)/shard_map/ppermute | solution.py:27
  21.8 1.3 %collective-permute-start.7 = (bf16[32,1024]{1,0:T(8,128)(2,1)S(1)}, bf16[32,1024]{1,0:T(8,128)(2,1)S(1)}, u32[]{:S(2)}, u32[]{:S(2)}) collective-permute-start(bf16[32,1024]{1,0:T(8,128)(2,1)S(1)} %get-tuple-element.43), channel_id=1, source_target_pairs={{0,3},{1,2},{2,1},{3,0},{4,7},{5,6},{6,5},{7,4},{8,11},{9,10},{10,... | collective-permute-start | bytes 196616 | tf_op jit(solution)/shard_map/ppermute | solution.py:27
  23.2 2.3 %values.2 = (bf16[1024,512]{1,0:T(8,128)(2,1)S(1)}, bf16[1024,2048]{1,0:T(8,128)(2,1)S(1)}) custom-call(bf16[1024,1536]{1,0:T(8,128)(2,1)S(1)} %get-tuple-element.35.xa_ref, bf16[1536,2048]{1,0:T(8,128)(2,1)S(1)} %get-tuple-element.36.wa_ref, bf16[1024,512]{1,0:T(8,128)(2,1)S(1)} %get-tuple-element.45.xb_ref, ...), custom_call_target="tpu_custom_call" | custom-call | flops 1610612736 | bytes 8388608 | tf_op jit(solution)/shard_map/values/pallas_call | solution.py:272
  26.1 2.1 %collective-permute-done.7.refs_2_ = bf16[32,1024]{1,0:T(8,128)(2,1)S(1)} collective-permute-done((bf16[32,1024]{1,0:T(8,128)(2,1)S(1)}, bf16[32,1024]{1,0:T(8,128)(2,1)S(1)}, u32[]{:S(2)}, u32[]{:S(2)}) %collective-permute-start.7) | collective-permute-done | bytes 65568 | tf_op jit(solution)/shard_map/ppermute | solution.py:27
  28.3 0.9 %weights.1 = (bf16[32,1024]{1,0:T(8,128)(2,1)S(1)}, bf16[32,128]{1,0:T(8,128)(2,1)S(1)}) custom-call(bf16[32,1024]{1,0:T(8,128)(2,1)S(1)} %get-tuple-element.41.after.refs_0_, bf16[32,1024]{1,0:T(8,128)(2,1)S(1)} %collective-permute-done.6.refs_1_, bf16[32,1024]{1,0:T(8,128)(2,1)S(1)} %collective-permute-done.7.refs_2_, ...), custom_call_target="tpu_custom_call" | custom-call | tf_op jit(solution)/shard_map/weights/pallas_call | solution.py:495
  29.1 1.9 %collective-permute-start.11 = (bf16[32,1024]{1,0:T(8,128)(2,1)S(1)}, bf16[32,1024]{1,0:T(8,128)(2,1)S(1)}, u32[]{:S(2)}, u32[]{:S(2)}) collective-permute-start(bf16[32,1024]{1,0:T(8,128)(2,1)S(1)} %get-tuple-element.48.refs_0_), channel_id=1, source_target_pairs={{0,2},{1,3},{2,0},{3,1},{4,6},{5,7},{6,4},{7,5},{8,10},{9,11},{10,... | collective-permute-start | bytes 196616 | tf_op jit(solution)/shard_map/ppermute | solution.py:27
  31.0 1.2 %collective-permute-start.10 = (bf16[32,1024]{1,0:T(8,128)(2,1)S(1)}, bf16[32,1024]{1,0:T(8,128)(2,1)S(1)}, u32[]{:S(2)}, u32[]{:S(2)}) collective-permute-start(bf16[32,1024]{1,0:T(8,128)(2,1)S(1)} %get-tuple-element.48.refs_0_), channel_id=1, source_target_pairs={{0,3},{1,2},{2,1},{3,0},{4,7},{5,6},{6,5},{7,4},{8,11},{9,10},{10,... | collective-permute-start | bytes 196616 | tf_op jit(solution)/shard_map/ppermute | solution.py:27
  32.6 2.3 %values.3 = (bf16[1024,512]{1,0:T(8,128)(2,1)S(1)}, bf16[1024,2048]{1,0:T(8,128)(2,1)S(1)}) custom-call(bf16[1024,1536]{1,0:T(8,128)(2,1)S(1)} %get-tuple-element.35.xa_ref, bf16[1536,2048]{1,0:T(8,128)(2,1)S(1)} %get-tuple-element.36.wa_ref, bf16[1024,512]{1,0:T(8,128)(2,1)S(1)} %get-tuple-element.45.xb_ref, ...), custom_call_target="tpu_custom_call" | custom-call | flops 1610612736 | bytes 8388608 | tf_op jit(solution)/shard_map/values/pallas_call | solution.py:272
  35.0 0.9 %collective-permute-done.11.refs_3_ = bf16[32,1024]{1,0:T(8,128)(2,1)S(1)} collective-permute-done((bf16[32,1024]{1,0:T(8,128)(2,1)S(1)}, bf16[32,1024]{1,0:T(8,128)(2,1)S(1)}, u32[]{:S(2)}, u32[]{:S(2)}) %collective-permute-start.11) | collective-permute-done | bytes 65568 | tf_op jit(solution)/shard_map/ppermute | solution.py:27
  35.9 1.3 %collective-permute-done.10.refs_2_ = bf16[32,1024]{1,0:T(8,128)(2,1)S(1)} collective-permute-done((bf16[32,1024]{1,0:T(8,128)(2,1)S(1)}, bf16[32,1024]{1,0:T(8,128)(2,1)S(1)}, u32[]{:S(2)}, u32[]{:S(2)}) %collective-permute-start.10) | collective-permute-done | bytes 65568 | tf_op jit(solution)/shard_map/ppermute | solution.py:27
  37.3 1.1 %weighted.1 = (bf16[8,32,128]{2,1,0:T(8,128)(2,1)S(1)}, bf16[8,32,128]{2,1,0:T(8,128)(2,1)S(1)}, bf16[8,32,128]{2,1,0:T(8,128)(2,1)S(1)}, bf16[8,32,128]{2,1,0:T(8,128)(2,1)S(1)}) custom-call(bf16[32,1024]{1,0:T(8,128)(2,1)S(1)} %get-tuple-element.48.refs_0_, bf16[32,1024]{1,0:T(8,128)(2,1)S(1)} %collective-permute-done.9.refs_1_, ...), custom_call_target="tpu_custom_call" | custom-call | flops 33554432 | bytes 8388608 | tf_op jit(solution)/shard_map/weighted/pallas_call | solution.py:549
  38.4 1.7 %collective-permute-start.12 = (bf16[8,32,128]{2,1,0:T(8,128)(2,1)S(1)}, bf16[8,32,128]{2,1,0:T(8,128)(2,1)S(1)}, u32[]{:S(2)}, u32[]{:S(2)}) collective-permute-start(bf16[8,32,128]{2,1,0:T(8,128)(2,1)S(1)} %get-tuple-element.52), channel_id=1, source_target_pairs={{0,2},{1,3},{2,0},{3,1},{4,6},{5,7},{6,4},{7,5},{8,10},{9,11},{10,... | collective-permute-start | bytes 196616 | tf_op jit(solution)/shard_map/ppermute | solution.py:27
  40.2 1.2 %collective-permute-start.13 = (bf16[8,32,128]{2,1,0:T(8,128)(2,1)S(1)}, bf16[8,32,128]{2,1,0:T(8,128)(2,1)S(1)}, u32[]{:S(2)}, u32[]{:S(2)}) collective-permute-start(bf16[8,32,128]{2,1,0:T(8,128)(2,1)S(1)} %get-tuple-element.53), channel_id=1, source_target_pairs={{0,3},{1,2},{2,1},{3,0},{4,7},{5,6},{6,5},{7,4},{8,11},{9,10},{10,... | collective-permute-start | bytes 196616 | tf_op jit(solution)/shard_map/ppermute | solution.py:27
  41.4 0.6 collective-permute-start.14
  42.0 3.1 %collective-permute-done.12.refs_1_ = bf16[8,32,128]{2,1,0:T(8,128)(2,1)S(1)} collective-permute-done((bf16[8,32,128]{2,1,0:T(8,128)(2,1)S(1)}, bf16[8,32,128]{2,1,0:T(8,128)(2,1)S(1)}, u32[]{:S(2)}, u32[]{:S(2)}) %collective-permute-start.12) | collective-permute-done | bytes 65568 | tf_op jit(solution)/shard_map/ppermute | solution.py:27
  45.1 1.3 %collective-permute-done.13.refs_2_ = bf16[8,32,128]{2,1,0:T(8,128)(2,1)S(1)} collective-permute-done((bf16[8,32,128]{2,1,0:T(8,128)(2,1)S(1)}, bf16[8,32,128]{2,1,0:T(8,128)(2,1)S(1)}, u32[]{:S(2)}, u32[]{:S(2)}) %collective-permute-start.13) | collective-permute-done | bytes 65568 | tf_op jit(solution)/shard_map/ppermute | solution.py:27
  46.5 1.7 %collective-permute-start.17 = (bf16[9,32,128]{2,1,0:T(8,128)(2,1)S(1)}, bf16[9,32,128]{2,1,0:T(8,128)(2,1)S(1)}, u32[]{:S(2)}, u32[]{:S(2)}) collective-permute-start(bf16[9,32,128]{2,1,0:T(8,128)(2,1)S(1)} %summed.1.refs_0_), channel_id=1, source_target_pairs={{0,8},{4,12},{8,0},{12,4},{1,9},{5,13},{9,1},{13,5},{2,10},{6,14},... | collective-permute-start | bytes 221192 | tf_op jit(solution)/shard_map/ppermute | solution.py:27
  48.9 2.1 %collective-permute-done.17.refs_3_ = bf16[9,32,128]{2,1,0:T(8,128)(2,1)S(1)} collective-permute-done((bf16[9,32,128]{2,1,0:T(8,128)(2,1)S(1)}, bf16[9,32,128]{2,1,0:T(8,128)(2,1)S(1)}, u32[]{:S(2)}, u32[]{:S(2)}) %collective-permute-start.17) | collective-permute-done | bytes 73760 | tf_op jit(solution)/shard_map/ppermute | solution.py:27
  50.9 1.6 %collective-permute-done.16.refs_2_ = bf16[9,32,128]{2,1,0:T(8,128)(2,1)S(1)} collective-permute-done((bf16[9,32,128]{2,1,0:T(8,128)(2,1)S(1)}, bf16[9,32,128]{2,1,0:T(8,128)(2,1)S(1)}, u32[]{:S(2)}, u32[]{:S(2)}) %collective-permute-start.16) | collective-permute-done | bytes 73760 | tf_op jit(solution)/shard_map/ppermute | solution.py:27
  52.5 1.6 %output.1.refs_0_ = bf16[16,2048]{1,0:T(8,128)(2,1)S(1)} custom-call(bf16[9,32,128]{2,1,0:T(8,128)(2,1)S(1)} %summed.1.refs_0_, bf16[9,32,128]{2,1,0:T(8,128)(2,1)S(1)} %collective-permute-done.15.refs_1_, bf16[9,32,128]{2,1,0:T(8,128)(2,1)S(1)} %collective-permute-done.16.refs_2_, bf16[9,32,128]{2,1,0:T(8,128)(2,1)S(1)} %collective-permute-done.17.refs_3_, ...), custom_call_target="tpu_custom_call" | custom-call | tf_op jit(solution)/shard_map/output/pallas_call | solution.py:643
  54.1 1.0 %collective-permute-start.20 = (bf16[16,2048]{1,0:T(8,128)(2,1)S(1)}, bf16[16,2048]{1,0:T(8,128)(2,1)S(1)}, u32[]{:S(2)}, u32[]{:S(2)}) collective-permute-start(bf16[16,2048]{1,0:T(8,128)(2,1)S(1)} %output.1.refs_0_), channel_id=1, source_target_pairs={{0,2},{1,3},{2,0},{3,1},{4,6},{5,7},{6,4},{7,5},{8,10},{9,11},{10,... | collective-permute-start | bytes 196616 | tf_op jit(solution)/shard_map/ppermute | solution.py:27
  55.1 1.9 %collective-permute-start.19 = (bf16[16,2048]{1,0:T(8,128)(2,1)S(1)}, bf16[16,2048]{1,0:T(8,128)(2,1)S(1)}, u32[]{:S(2)}, u32[]{:S(2)}) collective-permute-start(bf16[16,2048]{1,0:T(8,128)(2,1)S(1)} %output.1.refs_0_), channel_id=1, source_target_pairs={{0,3},{1,2},{2,1},{3,0},{4,7},{5,6},{6,5},{7,4},{8,11},{9,10},{10,... | collective-permute-start | bytes 196616 | tf_op jit(solution)/shard_map/ppermute | solution.py:27
  57.6 4.5 %collective-permute-done.20.refs_3_ = bf16[16,2048]{1,0:T(8,128)(2,1)S(1)} collective-permute-done((bf16[16,2048]{1,0:T(8,128)(2,1)S(1)}, bf16[16,2048]{1,0:T(8,128)(2,1)S(1)}, u32[]{:S(2)}, u32[]{:S(2)}) %collective-permute-start.20) | collective-permute-done | bytes 65568 | tf_op jit(solution)/shard_map/ppermute | solution.py:27
  62.1 0.6 collective-permute-done.18.refs_1_
  62.7 0.7 %final.1 = f32[8,2,2048]{2,1,0:T(2,128)} custom-call(bf16[16,2048]{1,0:T(8,128)(2,1)S(1)} %output.1.refs_0_, bf16[16,2048]{1,0:T(8,128)(2,1)S(1)} %collective-permute-done.18.refs_1_, bf16[16,2048]{1,0:T(8,128)(2,1)S(1)} %collective-permute-done.19.refs_2_, bf16[16,2048]{1,0:T(8,128)(2,1)S(1)} %collective-permute-done.20.refs_3_, bf16[8,2,2048]{2,1,0:T(2,128)(2,1)S(1)} %copy-done), custom_call_target="tpu_custom_call" | custom-call | tf_op jit(solution)/shard_map/final/pallas_call | solution.py:667
  (28 shorter events, 2.9 us)
Async XLA Ops:
  0.0 11.4 %copy-start.1 = (bf16[2,2,2048]{2,1,0:T(2,128)(2,1)S(1)}, bf16[2,2,2048]{2,1,0:T(2,128)(2,1)}, u32[]{:S(2)}) copy-start(bf16[2,2,2048]{2,1,0:T(2,128)(2,1)} %refs_0_.1) | copy-start | bytes 49156
  0.0 11.4 %copy-start.2 = (bf16[2,2,512]{2,1,0:T(2,128)(2,1)S(1)}, bf16[2,2,512]{2,1,0:T(2,128)(2,1)}, u32[]{:S(2)}) copy-start(bf16[2,2,512]{2,1,0:T(2,128)(2,1)} %refs_4_.2) | copy-start | bytes 12292
  0.0 11.4 %collective-permute-start.1 = (bf16[2,2,2048]{2,1,0:T(2,128)(2,1)}, bf16[2,2,2048]{2,1,0:T(2,128)(2,1)S(1)}, u32[]{:S(2)}, u32[]{:S(2)}) collective-permute-start(bf16[2,2,2048]{2,1,0:T(2,128)(2,1)} %refs_0_.1), channel_id=1, source_target_pairs={{0,2},{1,3},{2,0},{3,1},{4,6},{5,7},{6,4},{7,5},{8,10},{9,11},{10,... | collective-permute-start | bytes 49160 | tf_op jit(solution)/shard_map/ppermute | solution.py:27
  4.0 7.4 %collective-permute-start = (bf16[2,2,2048]{2,1,0:T(2,128)(2,1)}, bf16[2,2,2048]{2,1,0:T(2,128)(2,1)S(1)}, u32[]{:S(2)}, u32[]{:S(2)}) collective-permute-start(bf16[2,2,2048]{2,1,0:T(2,128)(2,1)} %refs_0_.1), channel_id=1, source_target_pairs={{0,3},{1,2},{2,1},{3,0},{4,7},{5,6},{6,5},{7,4},{8,11},{9,10},{10,... | collective-permute-start | bytes 49160 | tf_op jit(solution)/shard_map/ppermute | solution.py:27
  5.4 6.0 %collective-permute-start.2 = (bf16[2,2,2048]{2,1,0:T(2,128)(2,1)}, bf16[2,2,2048]{2,1,0:T(2,128)(2,1)S(1)}, u32[]{:S(2)}, u32[]{:S(2)}) collective-permute-start(bf16[2,2,2048]{2,1,0:T(2,128)(2,1)} %refs_0_.1), channel_id=1, source_target_pairs={{0,1},{1,0},{2,3},{3,2},{4,5},{5,4},{6,7},{7,6},{8,9},{9,8},{10,11... | collective-permute-start | bytes 49160 | tf_op jit(solution)/shard_map/ppermute | solution.py:27
  11.6 5.9 %collective-permute-start.5 = (bf16[2,144,128]{2,1,0:T(8,128)(2,1)S(1)}, bf16[2,144,128]{2,1,0:T(8,128)(2,1)S(1)}, u32[]{:S(2)}, u32[]{:S(2)}) collective-permute-start(bf16[2,144,128]{2,1,0:T(8,128)(2,1)S(1)} %turned.1.after.refs_0_), channel_id=1, source_target_pairs={{0,8},{4,12},{8,0},{12,4},{1,9},{5,13},{9,1},{13,5},{2,10},{6,14},... | collective-permute-start | bytes 221192 | tf_op jit(solution)/shard_map/ppermute | solution.py:27
  13.2 4.4 %collective-permute-start.4 = (bf16[2,144,128]{2,1,0:T(8,128)(2,1)S(1)}, bf16[2,144,128]{2,1,0:T(8,128)(2,1)S(1)}, u32[]{:S(2)}, u32[]{:S(2)}) collective-permute-start(bf16[2,144,128]{2,1,0:T(8,128)(2,1)S(1)} %turned.1.after.refs_0_), channel_id=1, source_target_pairs={{0,12},{4,8},{8,4},{12,0},{1,13},{5,9},{9,5},{13,1},{2,14},{6,10},... | collective-permute-start | bytes 221192 | tf_op jit(solution)/shard_map/ppermute | solution.py:27
  13.2 4.4 %collective-permute-start.3 = (bf16[2,144,128]{2,1,0:T(8,128)(2,1)S(1)}, bf16[2,144,128]{2,1,0:T(8,128)(2,1)S(1)}, u32[]{:S(2)}, u32[]{:S(2)}) collective-permute-start(bf16[2,144,128]{2,1,0:T(8,128)(2,1)S(1)} %turned.1.after.refs_0_), channel_id=1, source_target_pairs={{0,4},{4,0},{8,12},{12,8},{1,5},{5,1},{9,13},{13,9},{2,6},{6,2},{1... | collective-permute-start | bytes 221192 | tf_op jit(solution)/shard_map/ppermute | solution.py:27
  19.0 7.1 %collective-permute-start.6 = (bf16[32,1024]{1,0:T(8,128)(2,1)S(1)}, bf16[32,1024]{1,0:T(8,128)(2,1)S(1)}, u32[]{:S(2)}, u32[]{:S(2)}) collective-permute-start(bf16[32,1024]{1,0:T(8,128)(2,1)S(1)} %get-tuple-element.42), channel_id=1, source_target_pairs={{0,2},{1,3},{2,0},{3,1},{4,6},{5,7},{6,4},{7,5},{8,10},{9,11},{10,... | collective-permute-start | bytes 196616 | tf_op jit(solution)/shard_map/ppermute | solution.py:27
  21.8 6.3 %collective-permute-start.7 = (bf16[32,1024]{1,0:T(8,128)(2,1)S(1)}, bf16[32,1024]{1,0:T(8,128)(2,1)S(1)}, u32[]{:S(2)}, u32[]{:S(2)}) collective-permute-start(bf16[32,1024]{1,0:T(8,128)(2,1)S(1)} %get-tuple-element.43), channel_id=1, source_target_pairs={{0,3},{1,2},{2,1},{3,0},{4,7},{5,6},{6,5},{7,4},{8,11},{9,10},{10,... | collective-permute-start | bytes 196616 | tf_op jit(solution)/shard_map/ppermute | solution.py:27
  23.2 5.1 %collective-permute-start.8 = (bf16[32,1024]{1,0:T(8,128)(2,1)S(1)}, bf16[32,1024]{1,0:T(8,128)(2,1)S(1)}, u32[]{:S(2)}, u32[]{:S(2)}) collective-permute-start(bf16[32,1024]{1,0:T(8,128)(2,1)S(1)} %get-tuple-element.44), channel_id=1, source_target_pairs={{0,1},{1,0},{2,3},{3,2},{4,5},{5,4},{6,7},{7,6},{8,9},{9,8},{10,11... | collective-permute-start | bytes 196616 | tf_op jit(solution)/shard_map/ppermute | solution.py:27
  29.1 6.8 %collective-permute-start.11 = (bf16[32,1024]{1,0:T(8,128)(2,1)S(1)}, bf16[32,1024]{1,0:T(8,128)(2,1)S(1)}, u32[]{:S(2)}, u32[]{:S(2)}) collective-permute-start(bf16[32,1024]{1,0:T(8,128)(2,1)S(1)} %get-tuple-element.48.refs_0_), channel_id=1, source_target_pairs={{0,2},{1,3},{2,0},{3,1},{4,6},{5,7},{6,4},{7,5},{8,10},{9,11},{10,... | collective-permute-start | bytes 196616 | tf_op jit(solution)/shard_map/ppermute | solution.py:27
  31.0 6.2 %collective-permute-start.10 = (bf16[32,1024]{1,0:T(8,128)(2,1)S(1)}, bf16[32,1024]{1,0:T(8,128)(2,1)S(1)}, u32[]{:S(2)}, u32[]{:S(2)}) collective-permute-start(bf16[32,1024]{1,0:T(8,128)(2,1)S(1)} %get-tuple-element.48.refs_0_), channel_id=1, source_target_pairs={{0,3},{1,2},{2,1},{3,0},{4,7},{5,6},{6,5},{7,4},{8,11},{9,10},{10,... | collective-permute-start | bytes 196616 | tf_op jit(solution)/shard_map/ppermute | solution.py:27
  32.2 5.1 %collective-permute-start.9 = (bf16[32,1024]{1,0:T(8,128)(2,1)S(1)}, bf16[32,1024]{1,0:T(8,128)(2,1)S(1)}, u32[]{:S(2)}, u32[]{:S(2)}) collective-permute-start(bf16[32,1024]{1,0:T(8,128)(2,1)S(1)} %get-tuple-element.48.refs_0_), channel_id=1, source_target_pairs={{0,1},{1,0},{2,3},{3,2},{4,5},{5,4},{6,7},{7,6},{8,9},{9,8},{10,11... | collective-permute-start | bytes 196616 | tf_op jit(solution)/shard_map/ppermute | solution.py:27
  38.4 6.6 %collective-permute-start.12 = (bf16[8,32,128]{2,1,0:T(8,128)(2,1)S(1)}, bf16[8,32,128]{2,1,0:T(8,128)(2,1)S(1)}, u32[]{:S(2)}, u32[]{:S(2)}) collective-permute-start(bf16[8,32,128]{2,1,0:T(8,128)(2,1)S(1)} %get-tuple-element.52), channel_id=1, source_target_pairs={{0,2},{1,3},{2,0},{3,1},{4,6},{5,7},{6,4},{7,5},{8,10},{9,11},{10,... | collective-permute-start | bytes 196616 | tf_op jit(solution)/shard_map/ppermute | solution.py:27
  40.2 6.2 %collective-permute-start.13 = (bf16[8,32,128]{2,1,0:T(8,128)(2,1)S(1)}, bf16[8,32,128]{2,1,0:T(8,128)(2,1)S(1)}, u32[]{:S(2)}, u32[]{:S(2)}) collective-permute-start(bf16[8,32,128]{2,1,0:T(8,128)(2,1)S(1)} %get-tuple-element.53), channel_id=1, source_target_pairs={{0,3},{1,2},{2,1},{3,0},{4,7},{5,6},{6,5},{7,4},{8,11},{9,10},{10,... | collective-permute-start | bytes 196616 | tf_op jit(solution)/shard_map/ppermute | solution.py:27
  41.4 5.0 %collective-permute-start.14 = (bf16[8,32,128]{2,1,0:T(8,128)(2,1)S(1)}, bf16[8,32,128]{2,1,0:T(8,128)(2,1)S(1)}, u32[]{:S(2)}, u32[]{:S(2)}) collective-permute-start(bf16[8,32,128]{2,1,0:T(8,128)(2,1)S(1)} %get-tuple-element.54), channel_id=1, source_target_pairs={{0,1},{1,0},{2,3},{3,2},{4,5},{5,4},{6,7},{7,6},{8,9},{9,8},{10,11... | collective-permute-start | bytes 196616 | tf_op jit(solution)/shard_map/ppermute | solution.py:27
  46.5 4.4 %collective-permute-start.17 = (bf16[9,32,128]{2,1,0:T(8,128)(2,1)S(1)}, bf16[9,32,128]{2,1,0:T(8,128)(2,1)S(1)}, u32[]{:S(2)}, u32[]{:S(2)}) collective-permute-start(bf16[9,32,128]{2,1,0:T(8,128)(2,1)S(1)} %summed.1.refs_0_), channel_id=1, source_target_pairs={{0,8},{4,12},{8,0},{12,4},{1,9},{5,13},{9,1},{13,5},{2,10},{6,14},... | collective-permute-start | bytes 221192 | tf_op jit(solution)/shard_map/ppermute | solution.py:27
  48.2 4.3 %collective-permute-start.16 = (bf16[9,32,128]{2,1,0:T(8,128)(2,1)S(1)}, bf16[9,32,128]{2,1,0:T(8,128)(2,1)S(1)}, u32[]{:S(2)}, u32[]{:S(2)}) collective-permute-start(bf16[9,32,128]{2,1,0:T(8,128)(2,1)S(1)} %summed.1.refs_0_), channel_id=1, source_target_pairs={{0,12},{4,8},{8,4},{12,0},{1,13},{5,9},{9,5},{13,1},{2,14},{6,10},... | collective-permute-start | bytes 221192 | tf_op jit(solution)/shard_map/ppermute | solution.py:27
  48.2 4.3 %collective-permute-start.15 = (bf16[9,32,128]{2,1,0:T(8,128)(2,1)S(1)}, bf16[9,32,128]{2,1,0:T(8,128)(2,1)S(1)}, u32[]{:S(2)}, u32[]{:S(2)}) collective-permute-start(bf16[9,32,128]{2,1,0:T(8,128)(2,1)S(1)} %summed.1.refs_0_), channel_id=1, source_target_pairs={{0,4},{4,0},{8,12},{12,8},{1,5},{5,1},{9,13},{13,9},{2,6},{6,2},{1... | collective-permute-start | bytes 221192 | tf_op jit(solution)/shard_map/ppermute | solution.py:27
  52.5 10.2 %copy-start = (bf16[8,2,2048]{2,1,0:T(2,128)(2,1)S(1)}, bf16[8,2,2048]{2,1,0:T(2,128)(2,1)}, u32[]{:S(2)}) copy-start(bf16[8,2,2048]{2,1,0:T(2,128)(2,1)} %refs_4_.3) | copy-start | bytes 196612
  54.1 8.0 %collective-permute-start.20 = (bf16[16,2048]{1,0:T(8,128)(2,1)S(1)}, bf16[16,2048]{1,0:T(8,128)(2,1)S(1)}, u32[]{:S(2)}, u32[]{:S(2)}) collective-permute-start(bf16[16,2048]{1,0:T(8,128)(2,1)S(1)} %output.1.refs_0_), channel_id=1, source_target_pairs={{0,2},{1,3},{2,0},{3,1},{4,6},{5,7},{6,4},{7,5},{8,10},{9,11},{10,... | collective-permute-start | bytes 196616 | tf_op jit(solution)/shard_map/ppermute | solution.py:27
  55.1 7.0 %collective-permute-start.19 = (bf16[16,2048]{1,0:T(8,128)(2,1)S(1)}, bf16[16,2048]{1,0:T(8,128)(2,1)S(1)}, u32[]{:S(2)}, u32[]{:S(2)}) collective-permute-start(bf16[16,2048]{1,0:T(8,128)(2,1)S(1)} %output.1.refs_0_), channel_id=1, source_target_pairs={{0,3},{1,2},{2,1},{3,0},{4,7},{5,6},{6,5},{7,4},{8,11},{9,10},{10,... | collective-permute-start | bytes 196616 | tf_op jit(solution)/shard_map/ppermute | solution.py:27
  57.0 5.6 %collective-permute-start.18 = (bf16[16,2048]{1,0:T(8,128)(2,1)S(1)}, bf16[16,2048]{1,0:T(8,128)(2,1)S(1)}, u32[]{:S(2)}, u32[]{:S(2)}) collective-permute-start(bf16[16,2048]{1,0:T(8,128)(2,1)S(1)} %output.1.refs_0_), channel_id=1, source_target_pairs={{0,1},{1,0},{2,3},{3,2},{4,5},{5,4},{6,7},{7,6},{8,9},{9,8},{10,11... | collective-permute-start | bytes 196616 | tf_op jit(solution)/shard_map/ppermute | solution.py:27

commit v17 on v16

--- a/solution.py
+++ b/solution.py
@@ -141,7 +141,7 @@
 
 def add_block(x_ref, w_ref, rows, acc, out, fresh):
     tokens = x_ref.shape[0]
-    tall = tokens
+    tall = tokens // 2
     for pair in range(KVH // 2):
         weight = pair_columns(w_ref, rows, pair, 0)
         columns = slice(2 * pair * HD, 2 * (pair + 1) * HD)
@@ -205,7 +205,7 @@
 
 def keys_kernel(acc, xa_ref, wa_ref, x_hbm, w_hbm, cos_ref, sin_ref, after, k_ref, x_ref, w_ref, total, sems):
     tokens, size = x_ref.shape
-    tall = tokens
+    tall = tokens // 2
     (copies,) = copies_of(x_hbm, w_hbm, x_ref, w_ref, sems, 3 * size, size, 1)
     start(copies)
     add_block(xa_ref, wa_ref, slice(2 * size, 3 * size), acc, total, False)
@@ -507,9 +507,10 @@
 
 def weighted_kernel(n_tp, *refs):
     pieces = refs[:n_tp]
-    va_ref, vb_ref, meta = refs[n_tp : n_tp + 3]
-    outs = refs[n_tp + 3 : n_tp + 3 + n_tp]
-    ready, total = refs[n_tp + 3 + n_tp :]
+    va_ref, vb_ref, meta, stats_ref = refs[n_tp : n_tp + 4]
+    outs = refs[n_tp + 4 : n_tp + 4 + n_tp]
+    late_ref, ready, total = refs[n_tp + 4 + n_tp :]
+    late_ref[...] = stats_ref[...]
     rows_local, tokens_here = pieces[0].shape
     kv_local = KVH // n_tp
     rows = rows_local // kv_local
@@ -543,14 +544,15 @@
         outs[d][...] = total[:, own[d]].astype(BF16)
 
 
-def weighted_values(pieces, va, vb, meta, prompts):
+def weighted_values(pieces, va, vb, meta, stats, prompts):
     n_tp = len(pieces)
     rows, tokens = pieces[0].shape
     return pl.pallas_call(
         functools.partial(weighted_kernel, n_tp),
-        in_specs=[VMEM] * (n_tp + 2) + [SMEM],
-        out_specs=[VMEM] * n_tp,
-        out_shape=[jax.ShapeDtypeStruct((prompts, rows, HD), BF16)] * n_tp,
+        in_specs=[VMEM] * (n_tp + 2) + [SMEM, VMEM],
+        out_specs=[VMEM] * (n_tp + 1),
+        out_shape=[jax.ShapeDtypeStruct((prompts, rows, HD), BF16)] * n_tp
+        + [jax.ShapeDtypeStruct(stats.shape, stats.dtype)],
         scratch_shapes=[
             pltpu.VMEM((rows * n_tp, tokens), BF16),
             pltpu.VMEM((prompts, rows * n_tp, HD), F32),
@@ -560,50 +562,19 @@
             flops=2 * tokens * rows * n_tp * HD, bytes_accessed=8 * MIB, transcendentals=0
         ),
         name="weighted",
-    )(*pieces, va, vb, meta)
-
-
-def summed_kernel(n_tp, *refs):
-    chunks = refs[:n_tp]
-    stats_ref, out_ref = refs[n_tp:]
-    prompts = chunks[0].shape[0]
-    total = chunks[0][...].astype(F32)
-    for d in range(1, n_tp):
-        total = total + chunks[d][...].astype(F32)
-    out_ref[:prompts] = total.astype(BF16)
-    out_ref[prompts] = stats_ref[...]
-
-
-def summed(chunks, stats):
-    n_tp = len(chunks)
-    prompts, rows, _ = chunks[0].shape
-    return pl.pallas_call(
-        functools.partial(summed_kernel, n_tp),
-        in_specs=[VMEM] * (n_tp + 1),
-        out_specs=VMEM,
-        out_shape=jax.ShapeDtypeStruct((prompts + 1, rows, HD), BF16),
-        compiler_params=pltpu.CompilerParams(vmem_limit_bytes=8 * MIB),
-        cost_estimate=pl.CostEstimate(flops=0, bytes_accessed=4 * MIB, transcendentals=0),
-        name="summed",
-    )(*chunks, stats)
-
-
-def output_kernel(n_seq, *refs):
-    pieces = refs[:n_seq]
-    fresh_ref, value_ref, wa_ref, wb_ref, out_ref, held = refs[n_seq:]
-    more, rows_local, _ = pieces[0].shape
-    prompts = more - 1
-    new_count = fresh_ref.shape[0]
-    rows = new_count * GROUP
-    kv_local = rows_local // rows
-    heads = kv_local * GROUP
+    )(*pieces, va, vb, meta, stats)
+
+
+def merge_kernel(n_seq, prompts, *refs):
+    stats = refs[:n_seq]
+    fresh_ref, factor_ref, weight_ref = refs[n_seq:]
     tops, parts = [], []
-    for s in range(n_seq):
-        stats = pieces[s][prompts].astype(F32)
-        folded = stats + pltpu.roll(stats, HD - prompts, 1)
+    for piece in stats:
+        value = piece[...].astype(F32)
+        folded = value + pltpu.roll(value, HD - prompts, 1)
         tops.append(folded)
         parts.append(pltpu.roll(folded, HD - 2 * prompts, 1))
-    fresh = [fresh_ref[n] for n in range(new_count)]
+    fresh = [fresh_ref[n] for n in range(fresh_ref.shape[0])]
     top = fresh[0]
     for other in fresh[1:] + tops:
         top = jnp.maximum(top, other)
@@ -614,8 +585,56 @@
         total = total + w
     for f, part in zip(factors, parts):
         total = total + f * part
-    weights = [w / total for w in weights]
-    factors = [f / total for f in factors]
+    for n, w in enumerate(weights):
+        weight_ref[n] = w / total
+    for i, f in enumerate(factors):
+        factor_ref[i] = f / total
+
+
+def merge(stats, fresh, prompts):
+    n_seq = len(stats)
+    return pl.pallas_call(
+        functools.partial(merge_kernel, n_seq, prompts),
+        in_specs=[VMEM] * (n_seq + 1),
+        out_specs=[VMEM, VMEM],
+        out_shape=[
+            jax.ShapeDtypeStruct((n_seq,) + fresh.shape[1:], F32),
+            jax.ShapeDtypeStruct(fresh.shape, F32),
+        ],
+        compiler_params=pltpu.CompilerParams(vmem_limit_bytes=8 * MIB),
+        name="merge",
+    )(*stats, fresh)
+
+
+def summed_kernel(*refs):
+    total = refs[0][...].astype(F32)
+    for chunk in refs[1:-2]:
+        total = total + chunk[...].astype(F32)
+    refs[-1][...] = total.astype(BF16)
+
+
+def summed(chunks, after):
+    return pl.pallas_call(
+        summed_kernel,
+        in_specs=[VMEM] * len(chunks) + [ANY],
+        out_specs=VMEM,
+        out_shape=jax.ShapeDtypeStruct(chunks[0].shape, BF16),
+        compiler_params=pltpu.CompilerParams(vmem_limit_bytes=8 * MIB),
+        cost_estimate=pl.CostEstimate(flops=0, bytes_accessed=16 * MIB, transcendentals=0),
+        name="summed",
+    )(*chunks, after)
+
+
+def output_kernel(n_seq, *refs):
+    pieces = refs[:n_seq]
+    factor_ref, weight_ref, value_ref, wa_ref, wb_ref, out_ref, held = refs[n_seq:]
+    prompts, rows_local, _ = pieces[0].shape
+    new_count = weight_ref.shape[0]
+    rows = new_count * GROUP
+    kv_local = rows_local // rows
+    heads = kv_local * GROUP
+    factors = [factor_ref[s] for s in range(n_seq)]
+    weights = [weight_ref[n] for n in range(new_count)]
     for r in range(prompts):
         sums = jnp.zeros((rows_local, HD), F32)
         for s in range(n_seq):
@@ -635,20 +654,20 @@
     out_ref[...] = product.astype(BF16)
 
 
-def output_partial(pieces, fresh, values, weights):
+def output_partial(pieces, factors, fresh, values, weights):
     n_seq = len(pieces)
     new_count = fresh.shape[0]
-    prompts = pieces[0].shape[0] - 1
+    prompts = pieces[0].shape[0]
     depth, columns = weights[0].shape
     return pl.pallas_call(
         functools.partial(output_kernel, n_seq),
-        in_specs=[VMEM] * (n_seq + 4),
+        in_specs=[VMEM] * (n_seq + 5),
         out_specs=VMEM,
         out_shape=jax.ShapeDtypeStruct((prompts * new_count, columns), BF16),
         scratch_shapes=[pltpu.VMEM((2 * depth // HD, prompts * new_count, HD), F32)],
         compiler_params=pltpu.CompilerParams(vmem_limit_bytes=24 * MIB),
         name="output",
-    )(*pieces, fresh, values, *weights)
+    )(*pieces, factors, fresh, values, *weights)
 
 
 def final_kernel(n_tp, *refs):
@@ -693,9 +712,11 @@
     weights, stats = softmax_weights(exchange(scores, "tp"), meta, va, pages, prompts)
     vb, ob = project_values((xa, wa, xb, wb), out_weight, 1, stats)
     fresh, values = fresh_scores(new, stats, prompts, new_count, n_tp)
-    chunks = weighted_values(gather(weights, "tp"), va, vb, meta, prompts)
-    pieces = gather(summed(exchange(chunks, "tp"), stats), "seq")
-    partial = output_partial(pieces, fresh, values, (oa, ob))
+    *chunks, stats = weighted_values(gather(weights, "tp"), va, vb, meta, stats, prompts)
+    chunks = exchange(chunks, "tp")
+    factors, fresh = merge(gather(stats, "seq"), fresh, prompts)
+    pieces = gather(summed(chunks, factors), "seq")
+    partial = output_partial(pieces, factors, fresh, values, (oa, ob))
     return final_sum(gather(partial, "tp"), residual)
 
 

time: 63.5 us -> 64.7 us (1.019)
  starting transfers between devices: 24.8 us -> 26.7 us
    ppermute x21 -> x24, starting transfers between devices: 24.8 us -> 26.7 us  [pairs(): lax.ppermute(value, axis, [(i, i ^ d) for i in range(lax.axis_size(axis))])]
    ppermute x21 -> x24, waiting for transfers between devices: 18.4 us -> 17.8 us  [pairs(): lax.ppermute(value, axis, [(i, i ^ d) for i in range(lax.axis_size(axis))])]
  transfers between devices with their start and end apart: 21 -> 24, of which waited for: 14 -> 15; matrix products, arithmetic and copies ran while one was open for 0% -> 0% of each run, Pallas kernels for 23% -> 22%
where the time goes in v17:
time: 64.7 us; the launch traced here: 64.5 us
  starting transfers between devices  26.7 us (41%)
  Pallas kernels  19.9 us (31%)
  waiting for transfers between devices  17.8 us (28%)
    ppermute x24, starting transfers between devices, pairs(): lax.ppermute(value, axis, [(i, i ^ d) for i in range(lax.axis_size(axis))])  26.7 us
    ppermute x24, waiting for transfers between devices, pairs(): lax.ppermute(value, axis, [(i, i ^ d) for i in range(lax.axis_size(axis))])  17.8 us
    pallas_call x1, Pallas kernels, load(): pl.pallas_call(functools.partial(load_kernel, pages, prompts, new_count),...  5.68 us
    pallas_call x2, Pallas kernels, project_values(): pl.pallas_call(functools.partial(values_kernel, first), in_specs=[VMEM] *...  4.68 us
    pallas_call x1, Pallas kernels, rotated_keys(): pl.pallas_call(keys_kernel, in_specs=[VMEM] * 3 + [hbm] * 2 + [VMEM] * 2...  3.61 us
    pallas_call x1, Pallas kernels, output_partial(): pl.pallas_call(functools.partial(output_kernel, n_seq), in_specs=[VMEM] *...  1.43 us
    pallas_call x1, Pallas kernels, partial_scores(): pl.pallas_call(functools.partial(scores_kernel, n_seq, n_tp), in_specs=[V...  1.34 us
  transfers between devices with their start and end apart: 24, of which 15 were waited for; matrix products, arithmetic and copies ran while one was open for 0% of the time, Pallas kernels for 22%

profile of v17, /device:TPU:0, one launch (start us, length us, event | category | flops | bytes accessed | tf_op | source)
XLA Modules:
  0.0 64.5 jit_solution(12134921643079874801)
XLA Ops:
  0.0 4.0 %collective-permute-start.1 = (bf16[2,2,2048]{2,1,0:T(2,128)(2,1)}, bf16[2,2,2048]{2,1,0:T(2,128)(2,1)S(1)}, u32[]{:S(2)}, u32[]{:S(2)}) collective-permute-start(bf16[2,2,2048]{2,1,0:T(2,128)(2,1)} %refs_0_.1), channel_id=1, source_target_pairs={{0,2},{1,3},{2,0},{3,1},{4,6},{5,7},{6,4},{7,5},{8,10},{9,11},{10,... | collective-permute-start | bytes 49160 | tf_op jit(solution)/shard_map/ppermute | solution.py:27
  4.0 1.3 %collective-permute-start = (bf16[2,2,2048]{2,1,0:T(2,128)(2,1)}, bf16[2,2,2048]{2,1,0:T(2,128)(2,1)S(1)}, u32[]{:S(2)}, u32[]{:S(2)}) collective-permute-start(bf16[2,2,2048]{2,1,0:T(2,128)(2,1)} %refs_0_.1), channel_id=1, source_target_pairs={{0,3},{1,2},{2,1},{3,0},{4,7},{5,6},{6,5},{7,4},{8,11},{9,10},{10,... | collective-permute-start | bytes 49160 | tf_op jit(solution)/shard_map/ppermute | solution.py:27
  5.6 5.7 %load.1 = (f32[1024,1024]{1,0:T(8,128)S(1)}, bf16[1024,1536]{1,0:T(8,128)(2,1)S(1)}, bf16[1536,2048]{1,0:T(8,128)(2,1)S(1)}, f32[1024,128]{1,0:T(8,128)S(1)}, f3...) custom-call(bf16[1024,2048]{1,0:T(8,128)(2,1)} %x_hbm.3, ...), custom_call_target="tpu_custom_call" | custom-call | flops 2147483648 | bytes 9437184 | tf_op jit(solution)/shard_map/load/pallas_call | solution.py:181
  11.5 1.6 %collective-permute-start.5 = (bf16[2,144,128]{2,1,0:T(8,128)(2,1)S(1)}, bf16[2,144,128]{2,1,0:T(8,128)(2,1)S(1)}, u32[]{:S(2)}, u32[]{:S(2)}) collective-permute-start(bf16[2,144,128]{2,1,0:T(8,128)(2,1)S(1)} %turned.1.after.refs_0_), channel_id=1, source_target_pairs={{0,8},{4,12},{8,0},{12,4},{1,9},{5,13},{9,1},{13,5},{2,10},{6,14},... | collective-permute-start | bytes 221192 | tf_op jit(solution)/shard_map/ppermute | solution.py:27
  13.1 0.6 collective-permute-start.3
  13.7 3.6 %keys.1 = (bf16[1024,1024]{1,0:T(8,128)(2,1)S(1)}, bf16[1024,512]{1,0:T(8,128)(2,1)S(1)}, bf16[512,2048]{1,0:T(8,128)(2,1)S(1)}) custom-call(f32[1024,1024]{1,0:T(8,128)S(1)} %get-tuple-element.37.acc, bf16[1024,1536]{1,0:T(8,128)(2,1)S(1)} %get-tuple-element.38.xa_ref, bf16[1536,2048]{1,0:T(8,128)(2,1)S(1)} %get-tuple-element.39.wa_ref, ...), custom_call_target="tpu_custom_call" | custom-call | flops 2147483648 | bytes 8388608 | tf_op jit(solution)/shard_map/keys/pallas_call | solution.py:230
  17.5 1.3 %scores.1 = (bf16[32,1024]{1,0:T(8,128)(2,1)S(1)}, bf16[32,1024]{1,0:T(8,128)(2,1)S(1)}, bf16[32,1024]{1,0:T(8,128)(2,1)S(1)}, bf16[32,1024]{1,0:T(8,128)(2,1)S(1)}) custom-call(bf16[2,144,128]{2,1,0:T(8,128)(2,1)S(1)} %turned.1.after.refs_0_, bf16[2,144,128]{2,1,0:T(8,128)(2,1)S(1)} %collective-permute-done.3.refs_1_, ...), custom_call_target="tpu_custom_call" | custom-call | flops 33554432 | bytes 6291456 | tf_op jit(solution)/shard_map/scores/pallas_call | solution.py:383
  18.9 2.9 %collective-permute-start.6 = (bf16[32,1024]{1,0:T(8,128)(2,1)S(1)}, bf16[32,1024]{1,0:T(8,128)(2,1)S(1)}, u32[]{:S(2)}, u32[]{:S(2)}) collective-permute-start(bf16[32,1024]{1,0:T(8,128)(2,1)S(1)} %get-tuple-element.45), channel_id=1, source_target_pairs={{0,2},{1,3},{2,0},{3,1},{4,6},{5,7},{6,4},{7,5},{8,10},{9,11},{10,... | collective-permute-start | bytes 196616 | tf_op jit(solution)/shard_map/ppermute | solution.py:27
  21.7 1.3 %collective-permute-start.7 = (bf16[32,1024]{1,0:T(8,128)(2,1)S(1)}, bf16[32,1024]{1,0:T(8,128)(2,1)S(1)}, u32[]{:S(2)}, u32[]{:S(2)}) collective-permute-start(bf16[32,1024]{1,0:T(8,128)(2,1)S(1)} %get-tuple-element.46), channel_id=1, source_target_pairs={{0,3},{1,2},{2,1},{3,0},{4,7},{5,6},{6,5},{7,4},{8,11},{9,10},{10,... | collective-permute-start | bytes 196616 | tf_op jit(solution)/shard_map/ppermute | solution.py:27
  23.1 2.3 %values.2 = (bf16[1024,512]{1,0:T(8,128)(2,1)S(1)}, bf16[1024,2048]{1,0:T(8,128)(2,1)S(1)}) custom-call(bf16[1024,1536]{1,0:T(8,128)(2,1)S(1)} %get-tuple-element.38.xa_ref, bf16[1536,2048]{1,0:T(8,128)(2,1)S(1)} %get-tuple-element.39.wa_ref, bf16[1024,512]{1,0:T(8,128)(2,1)S(1)} %get-tuple-element.48.xb_ref, ...), custom_call_target="tpu_custom_call" | custom-call | flops 1610612736 | bytes 8388608 | tf_op jit(solution)/shard_map/values/pallas_call | solution.py:272
  26.0 2.1 %collective-permute-done.7.refs_2_ = bf16[32,1024]{1,0:T(8,128)(2,1)S(1)} collective-permute-done((bf16[32,1024]{1,0:T(8,128)(2,1)S(1)}, bf16[32,1024]{1,0:T(8,128)(2,1)S(1)}, u32[]{:S(2)}, u32[]{:S(2)}) %collective-permute-start.7) | collective-permute-done | bytes 65568 | tf_op jit(solution)/shard_map/ppermute | solution.py:27
  28.2 0.9 %weights.1 = (bf16[32,1024]{1,0:T(8,128)(2,1)S(1)}, bf16[32,128]{1,0:T(8,128)(2,1)S(1)}) custom-call(bf16[32,1024]{1,0:T(8,128)(2,1)S(1)} %get-tuple-element.44.after.refs_0_, bf16[32,1024]{1,0:T(8,128)(2,1)S(1)} %collective-permute-done.6.refs_1_, bf16[32,1024]{1,0:T(8,128)(2,1)S(1)} %collective-permute-done.7.refs_2_, ...), custom_call_target="tpu_custom_call" | custom-call | tf_op jit(solution)/shard_map/weights/pallas_call | solution.py:495
  29.0 1.9 %collective-permute-start.11 = (bf16[32,1024]{1,0:T(8,128)(2,1)S(1)}, bf16[32,1024]{1,0:T(8,128)(2,1)S(1)}, u32[]{:S(2)}, u32[]{:S(2)}) collective-permute-start(bf16[32,1024]{1,0:T(8,128)(2,1)S(1)} %get-tuple-element.51.refs_0_), channel_id=1, source_target_pairs={{0,2},{1,3},{2,0},{3,1},{4,6},{5,7},{6,4},{7,5},{8,10},{9,11},{10,... | collective-permute-start | bytes 196616 | tf_op jit(solution)/shard_map/ppermute | solution.py:27
  30.9 1.2 %collective-permute-start.10 = (bf16[32,1024]{1,0:T(8,128)(2,1)S(1)}, bf16[32,1024]{1,0:T(8,128)(2,1)S(1)}, u32[]{:S(2)}, u32[]{:S(2)}) collective-permute-start(bf16[32,1024]{1,0:T(8,128)(2,1)S(1)} %get-tuple-element.51.refs_0_), channel_id=1, source_target_pairs={{0,3},{1,2},{2,1},{3,0},{4,7},{5,6},{6,5},{7,4},{8,11},{9,10},{10,... | collective-permute-start | bytes 196616 | tf_op jit(solution)/shard_map/ppermute | solution.py:27
  32.5 2.3 %values.3 = (bf16[1024,512]{1,0:T(8,128)(2,1)S(1)}, bf16[1024,2048]{1,0:T(8,128)(2,1)S(1)}) custom-call(bf16[1024,1536]{1,0:T(8,128)(2,1)S(1)} %get-tuple-element.38.xa_ref, bf16[1536,2048]{1,0:T(8,128)(2,1)S(1)} %get-tuple-element.39.wa_ref, bf16[1024,512]{1,0:T(8,128)(2,1)S(1)} %get-tuple-element.48.xb_ref, ...), custom_call_target="tpu_custom_call" | custom-call | flops 1610612736 | bytes 8388608 | tf_op jit(solution)/shard_map/values/pallas_call | solution.py:272
  34.9 1.0 %collective-permute-done.11.refs_3_ = bf16[32,1024]{1,0:T(8,128)(2,1)S(1)} collective-permute-done((bf16[32,1024]{1,0:T(8,128)(2,1)S(1)}, bf16[32,1024]{1,0:T(8,128)(2,1)S(1)}, u32[]{:S(2)}, u32[]{:S(2)}) %collective-permute-start.11) | collective-permute-done | bytes 65568 | tf_op jit(solution)/shard_map/ppermute | solution.py:27
  35.9 1.2 %collective-permute-done.10.refs_2_ = bf16[32,1024]{1,0:T(8,128)(2,1)S(1)} collective-permute-done((bf16[32,1024]{1,0:T(8,128)(2,1)S(1)}, bf16[32,1024]{1,0:T(8,128)(2,1)S(1)}, u32[]{:S(2)}, u32[]{:S(2)}) %collective-permute-start.10) | collective-permute-done | bytes 65568 | tf_op jit(solution)/shard_map/ppermute | solution.py:27
  37.3 1.1 %weighted.1 = (bf16[8,32,128]{2,1,0:T(8,128)(2,1)S(1)}, bf16[8,32,128]{2,1,0:T(8,128)(2,1)S(1)}, bf16[8,32,128]{2,1,0:T(8,128)(2,1)S(1)}, bf16[8,32,128]{2,1,0:T(8,128)(2,1)S(1)}, bf16[32,128]{1,0:T(8,128)(2,1)S(1)}) custom-call(bf16[32,1024]{1,0:T(8,128)(2,1)S(1)} %get-tuple-element.51.refs_0_, bf16[32,1024]{1,0:T(8,128)(2,1)S(1)} %collective-permute-done.9.refs_1_, ...), custom_call_target="tpu_custom_call" | custom-call | flops 33554432 | bytes 8388608 | tf_op jit(solution)/shard_map/weighted/pallas_call | solution.py:550
  38.4 1.8 %collective-permute-start.12 = (bf16[8,32,128]{2,1,0:T(8,128)(2,1)S(1)}, bf16[8,32,128]{2,1,0:T(8,128)(2,1)S(1)}, u32[]{:S(2)}, u32[]{:S(2)}) collective-permute-start(bf16[8,32,128]{2,1,0:T(8,128)(2,1)S(1)} %get-tuple-element.55), channel_id=1, source_target_pairs={{0,2},{1,3},{2,0},{3,1},{4,6},{5,7},{6,4},{7,5},{8,10},{9,11},{10,... | collective-permute-start | bytes 196616 | tf_op jit(solution)/shard_map/ppermute | solution.py:27
  40.2 1.2 %collective-permute-start.13 = (bf16[8,32,128]{2,1,0:T(8,128)(2,1)S(1)}, bf16[8,32,128]{2,1,0:T(8,128)(2,1)S(1)}, u32[]{:S(2)}, u32[]{:S(2)}) collective-permute-start(bf16[8,32,128]{2,1,0:T(8,128)(2,1)S(1)} %get-tuple-element.56), channel_id=1, source_target_pairs={{0,3},{1,2},{2,1},{3,0},{4,7},{5,6},{6,5},{7,4},{8,11},{9,10},{10,... | collective-permute-start | bytes 196616 | tf_op jit(solution)/shard_map/ppermute | solution.py:27
  42.0 1.5 %collective-permute-start.17 = (bf16[32,128]{1,0:T(8,128)(2,1)S(1)}, bf16[32,128]{1,0:T(8,128)(2,1)S(1)}, u32[]{:S(2)}, u32[]{:S(2)}) collective-permute-start(bf16[32,128]{1,0:T(8,128)(2,1)S(1)} %get-tuple-element.58.refs_0_), channel_id=1, source_target_pairs={{0,8},{4,12},{8,0},{12,4},{1,9},{5,13},{9,1},{13,5},{2,10},{6,14},... | collective-permute-start | bytes 24584 | tf_op jit(solution)/shard_map/ppermute | solution.py:27
  43.5 2.1 %collective-permute-done.17.refs_3_ = bf16[32,128]{1,0:T(8,128)(2,1)S(1)} collective-permute-done((bf16[32,128]{1,0:T(8,128)(2,1)S(1)}, bf16[32,128]{1,0:T(8,128)(2,1)S(1)}, u32[]{:S(2)}, u32[]{:S(2)}) %collective-permute-start.17) | collective-permute-done | bytes 8224 | tf_op jit(solution)/shard_map/ppermute | solution.py:27
  45.8 0.8 %collective-permute-done.16.refs_2_ = bf16[32,128]{1,0:T(8,128)(2,1)S(1)} collective-permute-done((bf16[32,128]{1,0:T(8,128)(2,1)S(1)}, bf16[32,128]{1,0:T(8,128)(2,1)S(1)}, u32[]{:S(2)}, u32[]{:S(2)}) %collective-permute-start.16) | collective-permute-done | bytes 8224 | tf_op jit(solution)/shard_map/ppermute | solution.py:27
  47.0 1.6 %collective-permute-start.20 = (bf16[8,32,128]{2,1,0:T(8,128)(2,1)S(1)}, bf16[8,32,128]{2,1,0:T(8,128)(2,1)S(1)}, u32[]{:S(2)}, u32[]{:S(2)}) collective-permute-start(bf16[8,32,128]{2,1,0:T(8,128)(2,1)S(1)} %summed.1.refs_0_), channel_id=1, source_target_pairs={{0,8},{4,12},{8,0},{12,4},{1,9},{5,13},{9,1},{13,5},{2,10},{6,14},... | collective-permute-start | bytes 196616 | tf_op jit(solution)/shard_map/ppermute | solution.py:27
  49.2 2.1 %collective-permute-done.20.refs_3_ = bf16[8,32,128]{2,1,0:T(8,128)(2,1)S(1)} collective-permute-done((bf16[8,32,128]{2,1,0:T(8,128)(2,1)S(1)}, bf16[8,32,128]{2,1,0:T(8,128)(2,1)S(1)}, u32[]{:S(2)}, u32[]{:S(2)}) %collective-permute-start.20) | collective-permute-done | bytes 65568 | tf_op jit(solution)/shard_map/ppermute | solution.py:27
  51.4 1.6 %collective-permute-done.19.refs_2_ = bf16[8,32,128]{2,1,0:T(8,128)(2,1)S(1)} collective-permute-done((bf16[8,32,128]{2,1,0:T(8,128)(2,1)S(1)}, bf16[8,32,128]{2,1,0:T(8,128)(2,1)S(1)}, u32[]{:S(2)}, u32[]{:S(2)}) %collective-permute-start.19) | collective-permute-done | bytes 65568 | tf_op jit(solution)/shard_map/ppermute | solution.py:27
  53.0 1.4 %output.1.refs_0_ = bf16[16,2048]{1,0:T(8,128)(2,1)S(1)} custom-call(bf16[8,32,128]{2,1,0:T(8,128)(2,1)S(1)} %summed.1.refs_0_, bf16[8,32,128]{2,1,0:T(8,128)(2,1)S(1)} %collective-permute-done.18.refs_1_, bf16[8,32,128]{2,1,0:T(8,128)(2,1)S(1)} %collective-permute-done.19.refs_2_, bf16[8,32,128]{2,1,0:T(8,128)(2,1)S(1)} %collective-permute-done.20.refs_3_, ...), custom_call_target="tpu_custom_call" | custom-call | tf_op jit(solution)/shard_map/output/pallas_call | solution.py:662
  54.4 2.6 %collective-permute-start.23 = (bf16[16,2048]{1,0:T(8,128)(2,1)S(1)}, bf16[16,2048]{1,0:T(8,128)(2,1)S(1)}, u32[]{:S(2)}, u32[]{:S(2)}) collective-permute-start(bf16[16,2048]{1,0:T(8,128)(2,1)S(1)} %output.1.refs_0_), channel_id=1, source_target_pairs={{0,2},{1,3},{2,0},{3,1},{4,6},{5,7},{6,4},{7,5},{8,10},{9,11},{10,... | collective-permute-start | bytes 196616 | tf_op jit(solution)/shard_map/ppermute | solution.py:27
  57.0 1.2 %collective-permute-start.22 = (bf16[16,2048]{1,0:T(8,128)(2,1)S(1)}, bf16[16,2048]{1,0:T(8,128)(2,1)S(1)}, u32[]{:S(2)}, u32[]{:S(2)}) collective-permute-start(bf16[16,2048]{1,0:T(8,128)(2,1)S(1)} %output.1.refs_0_), channel_id=1, source_target_pairs={{0,3},{1,2},{2,1},{3,0},{4,7},{5,6},{6,5},{7,4},{8,11},{9,10},{10,... | collective-permute-start | bytes 196616 | tf_op jit(solution)/shard_map/ppermute | solution.py:27
  58.3 4.1 %collective-permute-done.23.refs_3_ = bf16[16,2048]{1,0:T(8,128)(2,1)S(1)} collective-permute-done((bf16[16,2048]{1,0:T(8,128)(2,1)S(1)}, bf16[16,2048]{1,0:T(8,128)(2,1)S(1)}, u32[]{:S(2)}, u32[]{:S(2)}) %collective-permute-start.23) | collective-permute-done | bytes 65568 | tf_op jit(solution)/shard_map/ppermute | solution.py:27
  62.4 1.0 %collective-permute-done.22.refs_2_ = bf16[16,2048]{1,0:T(8,128)(2,1)S(1)} collective-permute-done((bf16[16,2048]{1,0:T(8,128)(2,1)S(1)}, bf16[16,2048]{1,0:T(8,128)(2,1)S(1)}, u32[]{:S(2)}, u32[]{:S(2)}) %collective-permute-start.22) | collective-permute-done | bytes 65568 | tf_op jit(solution)/shard_map/ppermute | solution.py:27
  63.8 0.7 %final.1 = f32[8,2,2048]{2,1,0:T(2,128)} custom-call(bf16[16,2048]{1,0:T(8,128)(2,1)S(1)} %output.1.refs_0_, bf16[16,2048]{1,0:T(8,128)(2,1)S(1)} %collective-permute-done.21.refs_1_, bf16[16,2048]{1,0:T(8,128)(2,1)S(1)} %collective-permute-done.22.refs_2_, bf16[16,2048]{1,0:T(8,128)(2,1)S(1)} %collective-permute-done.23.refs_3_, bf16[8,2,2048]{2,1,0:T(2,128)(2,1)S(1)} %copy-done), custom_call_target="tpu_custom_call" | custom-call | tf_op jit(solution)/shard_map/final/pallas_call | solution.py:686
  (35 shorter events, 3.9 us)
Async XLA Ops:
  0.0 11.3 %copy-start.1 = (bf16[2,2,2048]{2,1,0:T(2,128)(2,1)S(1)}, bf16[2,2,2048]{2,1,0:T(2,128)(2,1)}, u32[]{:S(2)}) copy-start(bf16[2,2,2048]{2,1,0:T(2,128)(2,1)} %refs_0_.1) | copy-start | bytes 49156
  0.0 11.4 %copy-start.2 = (bf16[2,2,512]{2,1,0:T(2,128)(2,1)S(1)}, bf16[2,2,512]{2,1,0:T(2,128)(2,1)}, u32[]{:S(2)}) copy-start(bf16[2,2,512]{2,1,0:T(2,128)(2,1)} %refs_4_.2) | copy-start | bytes 12292
  0.0 11.3 %collective-permute-start.1 = (bf16[2,2,2048]{2,1,0:T(2,128)(2,1)}, bf16[2,2,2048]{2,1,0:T(2,128)(2,1)S(1)}, u32[]{:S(2)}, u32[]{:S(2)}) collective-permute-start(bf16[2,2,2048]{2,1,0:T(2,128)(2,1)} %refs_0_.1), channel_id=1, source_target_pairs={{0,2},{1,3},{2,0},{3,1},{4,6},{5,7},{6,4},{7,5},{8,10},{9,11},{10,... | collective-permute-start | bytes 49160 | tf_op jit(solution)/shard_map/ppermute | solution.py:27
  4.0 7.3 %collective-permute-start = (bf16[2,2,2048]{2,1,0:T(2,128)(2,1)}, bf16[2,2,2048]{2,1,0:T(2,128)(2,1)S(1)}, u32[]{:S(2)}, u32[]{:S(2)}) collective-permute-start(bf16[2,2,2048]{2,1,0:T(2,128)(2,1)} %refs_0_.1), channel_id=1, source_target_pairs={{0,3},{1,2},{2,1},{3,0},{4,7},{5,6},{6,5},{7,4},{8,11},{9,10},{10,... | collective-permute-start | bytes 49160 | tf_op jit(solution)/shard_map/ppermute | solution.py:27
  5.4 5.9 %collective-permute-start.2 = (bf16[2,2,2048]{2,1,0:T(2,128)(2,1)}, bf16[2,2,2048]{2,1,0:T(2,128)(2,1)S(1)}, u32[]{:S(2)}, u32[]{:S(2)}) collective-permute-start(bf16[2,2,2048]{2,1,0:T(2,128)(2,1)} %refs_0_.1), channel_id=1, source_target_pairs={{0,1},{1,0},{2,3},{3,2},{4,5},{5,4},{6,7},{7,6},{8,9},{9,8},{10,11... | collective-permute-start | bytes 49160 | tf_op jit(solution)/shard_map/ppermute | solution.py:27
  11.5 5.8 %collective-permute-start.5 = (bf16[2,144,128]{2,1,0:T(8,128)(2,1)S(1)}, bf16[2,144,128]{2,1,0:T(8,128)(2,1)S(1)}, u32[]{:S(2)}, u32[]{:S(2)}) collective-permute-start(bf16[2,144,128]{2,1,0:T(8,128)(2,1)S(1)} %turned.1.after.refs_0_), channel_id=1, source_target_pairs={{0,8},{4,12},{8,0},{12,4},{1,9},{5,13},{9,1},{13,5},{2,10},{6,14},... | collective-permute-start | bytes 221192 | tf_op jit(solution)/shard_map/ppermute | solution.py:27
  13.1 4.4 %collective-permute-start.4 = (bf16[2,144,128]{2,1,0:T(8,128)(2,1)S(1)}, bf16[2,144,128]{2,1,0:T(8,128)(2,1)S(1)}, u32[]{:S(2)}, u32[]{:S(2)}) collective-permute-start(bf16[2,144,128]{2,1,0:T(8,128)(2,1)S(1)} %turned.1.after.refs_0_), channel_id=1, source_target_pairs={{0,12},{4,8},{8,4},{12,0},{1,13},{5,9},{9,5},{13,1},{2,14},{6,10},... | collective-permute-start | bytes 221192 | tf_op jit(solution)/shard_map/ppermute | solution.py:27
  13.1 4.4 %collective-permute-start.3 = (bf16[2,144,128]{2,1,0:T(8,128)(2,1)S(1)}, bf16[2,144,128]{2,1,0:T(8,128)(2,1)S(1)}, u32[]{:S(2)}, u32[]{:S(2)}) collective-permute-start(bf16[2,144,128]{2,1,0:T(8,128)(2,1)S(1)} %turned.1.after.refs_0_), channel_id=1, source_target_pairs={{0,4},{4,0},{8,12},{12,8},{1,5},{5,1},{9,13},{13,9},{2,6},{6,2},{1... | collective-permute-start | bytes 221192 | tf_op jit(solution)/shard_map/ppermute | solution.py:27
  18.9 7.1 %collective-permute-start.6 = (bf16[32,1024]{1,0:T(8,128)(2,1)S(1)}, bf16[32,1024]{1,0:T(8,128)(2,1)S(1)}, u32[]{:S(2)}, u32[]{:S(2)}) collective-permute-start(bf16[32,1024]{1,0:T(8,128)(2,1)S(1)} %get-tuple-element.45), channel_id=1, source_target_pairs={{0,2},{1,3},{2,0},{3,1},{4,6},{5,7},{6,4},{7,5},{8,10},{9,11},{10,... | collective-permute-start | bytes 196616 | tf_op jit(solution)/shard_map/ppermute | solution.py:27
  21.7 6.3 %collective-permute-start.7 = (bf16[32,1024]{1,0:T(8,128)(2,1)S(1)}, bf16[32,1024]{1,0:T(8,128)(2,1)S(1)}, u32[]{:S(2)}, u32[]{:S(2)}) collective-permute-start(bf16[32,1024]{1,0:T(8,128)(2,1)S(1)} %get-tuple-element.46), channel_id=1, source_target_pairs={{0,3},{1,2},{2,1},{3,0},{4,7},{5,6},{6,5},{7,4},{8,11},{9,10},{10,... | collective-permute-start | bytes 196616 | tf_op jit(solution)/shard_map/ppermute | solution.py:27
  23.1 5.1 %collective-permute-start.8 = (bf16[32,1024]{1,0:T(8,128)(2,1)S(1)}, bf16[32,1024]{1,0:T(8,128)(2,1)S(1)}, u32[]{:S(2)}, u32[]{:S(2)}) collective-permute-start(bf16[32,1024]{1,0:T(8,128)(2,1)S(1)} %get-tuple-element.47), channel_id=1, source_target_pairs={{0,1},{1,0},{2,3},{3,2},{4,5},{5,4},{6,7},{7,6},{8,9},{9,8},{10,11... | collective-permute-start | bytes 196616 | tf_op jit(solution)/shard_map/ppermute | solution.py:27
  29.0 6.9 %collective-permute-start.11 = (bf16[32,1024]{1,0:T(8,128)(2,1)S(1)}, bf16[32,1024]{1,0:T(8,128)(2,1)S(1)}, u32[]{:S(2)}, u32[]{:S(2)}) collective-permute-start(bf16[32,1024]{1,0:T(8,128)(2,1)S(1)} %get-tuple-element.51.refs_0_), channel_id=1, source_target_pairs={{0,2},{1,3},{2,0},{3,1},{4,6},{5,7},{6,4},{7,5},{8,10},{9,11},{10,... | collective-permute-start | bytes 196616 | tf_op jit(solution)/shard_map/ppermute | solution.py:27
  30.9 6.2 %collective-permute-start.10 = (bf16[32,1024]{1,0:T(8,128)(2,1)S(1)}, bf16[32,1024]{1,0:T(8,128)(2,1)S(1)}, u32[]{:S(2)}, u32[]{:S(2)}) collective-permute-start(bf16[32,1024]{1,0:T(8,128)(2,1)S(1)} %get-tuple-element.51.refs_0_), channel_id=1, source_target_pairs={{0,3},{1,2},{2,1},{3,0},{4,7},{5,6},{6,5},{7,4},{8,11},{9,10},{10,... | collective-permute-start | bytes 196616 | tf_op jit(solution)/shard_map/ppermute | solution.py:27
  32.1 5.2 %collective-permute-start.9 = (bf16[32,1024]{1,0:T(8,128)(2,1)S(1)}, bf16[32,1024]{1,0:T(8,128)(2,1)S(1)}, u32[]{:S(2)}, u32[]{:S(2)}) collective-permute-start(bf16[32,1024]{1,0:T(8,128)(2,1)S(1)} %get-tuple-element.51.refs_0_), channel_id=1, source_target_pairs={{0,1},{1,0},{2,3},{3,2},{4,5},{5,4},{6,7},{7,6},{8,9},{9,8},{10,11... | collective-permute-start | bytes 196616 | tf_op jit(solution)/shard_map/ppermute | solution.py:27
  38.4 8.6 %collective-permute-start.12 = (bf16[8,32,128]{2,1,0:T(8,128)(2,1)S(1)}, bf16[8,32,128]{2,1,0:T(8,128)(2,1)S(1)}, u32[]{:S(2)}, u32[]{:S(2)}) collective-permute-start(bf16[8,32,128]{2,1,0:T(8,128)(2,1)S(1)} %get-tuple-element.55), channel_id=1, source_target_pairs={{0,2},{1,3},{2,0},{3,1},{4,6},{5,7},{6,4},{7,5},{8,10},{9,11},{10,... | collective-permute-start | bytes 196616 | tf_op jit(solution)/shard_map/ppermute | solution.py:27
  40.2 6.8 %collective-permute-start.13 = (bf16[8,32,128]{2,1,0:T(8,128)(2,1)S(1)}, bf16[8,32,128]{2,1,0:T(8,128)(2,1)S(1)}, u32[]{:S(2)}, u32[]{:S(2)}) collective-permute-start(bf16[8,32,128]{2,1,0:T(8,128)(2,1)S(1)} %get-tuple-element.56), channel_id=1, source_target_pairs={{0,3},{1,2},{2,1},{3,0},{4,7},{5,6},{6,5},{7,4},{8,11},{9,10},{10,... | collective-permute-start | bytes 196616 | tf_op jit(solution)/shard_map/ppermute | solution.py:27
  41.4 5.6 %collective-permute-start.14 = (bf16[8,32,128]{2,1,0:T(8,128)(2,1)S(1)}, bf16[8,32,128]{2,1,0:T(8,128)(2,1)S(1)}, u32[]{:S(2)}, u32[]{:S(2)}) collective-permute-start(bf16[8,32,128]{2,1,0:T(8,128)(2,1)S(1)} %get-tuple-element.57), channel_id=1, source_target_pairs={{0,1},{1,0},{2,3},{3,2},{4,5},{5,4},{6,7},{7,6},{8,9},{9,8},{10,11... | collective-permute-start | bytes 196616 | tf_op jit(solution)/shard_map/ppermute | solution.py:27
  42.0 3.7 %collective-permute-start.17 = (bf16[32,128]{1,0:T(8,128)(2,1)S(1)}, bf16[32,128]{1,0:T(8,128)(2,1)S(1)}, u32[]{:S(2)}, u32[]{:S(2)}) collective-permute-start(bf16[32,128]{1,0:T(8,128)(2,1)S(1)} %get-tuple-element.58.refs_0_), channel_id=1, source_target_pairs={{0,8},{4,12},{8,0},{12,4},{1,9},{5,13},{9,1},{13,5},{2,10},{6,14},... | collective-permute-start | bytes 24584 | tf_op jit(solution)/shard_map/ppermute | solution.py:27
  43.5 3.1 %collective-permute-start.16 = (bf16[32,128]{1,0:T(8,128)(2,1)S(1)}, bf16[32,128]{1,0:T(8,128)(2,1)S(1)}, u32[]{:S(2)}, u32[]{:S(2)}) collective-permute-start(bf16[32,128]{1,0:T(8,128)(2,1)S(1)} %get-tuple-element.58.refs_0_), channel_id=1, source_target_pairs={{0,12},{4,8},{8,4},{12,0},{1,13},{5,9},{9,5},{13,1},{2,14},{6,10},... | collective-permute-start | bytes 24584 | tf_op jit(solution)/shard_map/ppermute | solution.py:27
  45.6 1.2 %collective-permute-start.15 = (bf16[32,128]{1,0:T(8,128)(2,1)S(1)}, bf16[32,128]{1,0:T(8,128)(2,1)S(1)}, u32[]{:S(2)}, u32[]{:S(2)}) collective-permute-start(bf16[32,128]{1,0:T(8,128)(2,1)S(1)} %get-tuple-element.58.refs_0_), channel_id=1, source_target_pairs={{0,4},{4,0},{8,12},{12,8},{1,5},{5,1},{9,13},{13,9},{2,6},{6,2},{1... | collective-permute-start | bytes 24584 | tf_op jit(solution)/shard_map/ppermute | solution.py:27
  47.0 4.3 %collective-permute-start.20 = (bf16[8,32,128]{2,1,0:T(8,128)(2,1)S(1)}, bf16[8,32,128]{2,1,0:T(8,128)(2,1)S(1)}, u32[]{:S(2)}, u32[]{:S(2)}) collective-permute-start(bf16[8,32,128]{2,1,0:T(8,128)(2,1)S(1)} %summed.1.refs_0_), channel_id=1, source_target_pairs={{0,8},{4,12},{8,0},{12,4},{1,9},{5,13},{9,1},{13,5},{2,10},{6,14},... | collective-permute-start | bytes 196616 | tf_op jit(solution)/shard_map/ppermute | solution.py:27
  48.6 4.3 %collective-permute-start.19 = (bf16[8,32,128]{2,1,0:T(8,128)(2,1)S(1)}, bf16[8,32,128]{2,1,0:T(8,128)(2,1)S(1)}, u32[]{:S(2)}, u32[]{:S(2)}) collective-permute-start(bf16[8,32,128]{2,1,0:T(8,128)(2,1)S(1)} %summed.1.refs_0_), channel_id=1, source_target_pairs={{0,12},{4,8},{8,4},{12,0},{1,13},{5,9},{9,5},{13,1},{2,14},{6,10},... | collective-permute-start | bytes 196616 | tf_op jit(solution)/shard_map/ppermute | solution.py:27
  48.6 4.3 %collective-permute-start.18 = (bf16[8,32,128]{2,1,0:T(8,128)(2,1)S(1)}, bf16[8,32,128]{2,1,0:T(8,128)(2,1)S(1)}, u32[]{:S(2)}, u32[]{:S(2)}) collective-permute-start(bf16[8,32,128]{2,1,0:T(8,128)(2,1)S(1)} %summed.1.refs_0_), channel_id=1, source_target_pairs={{0,4},{4,0},{8,12},{12,8},{1,5},{5,1},{9,13},{13,9},{2,6},{6,2},{1... | collective-permute-start | bytes 196616 | tf_op jit(solution)/shard_map/ppermute | solution.py:27
  53.0 10.8 %copy-start = (bf16[8,2,2048]{2,1,0:T(2,128)(2,1)S(1)}, bf16[8,2,2048]{2,1,0:T(2,128)(2,1)}, u32[]{:S(2)}) copy-start(bf16[8,2,2048]{2,1,0:T(2,128)(2,1)} %refs_4_.3) | copy-start | bytes 196612
  54.4 7.9 %collective-permute-start.23 = (bf16[16,2048]{1,0:T(8,128)(2,1)S(1)}, bf16[16,2048]{1,0:T(8,128)(2,1)S(1)}, u32[]{:S(2)}, u32[]{:S(2)}) collective-permute-start(bf16[16,2048]{1,0:T(8,128)(2,1)S(1)} %output.1.refs_0_), channel_id=1, source_target_pairs={{0,2},{1,3},{2,0},{3,1},{4,6},{5,7},{6,4},{7,5},{8,10},{9,11},{10,... | collective-permute-start | bytes 196616 | tf_op jit(solution)/shard_map/ppermute | solution.py:27
  57.0 6.4 %collective-permute-start.22 = (bf16[16,2048]{1,0:T(8,128)(2,1)S(1)}, bf16[16,2048]{1,0:T(8,128)(2,1)S(1)}, u32[]{:S(2)}, u32[]{:S(2)}) collective-permute-start(bf16[16,2048]{1,0:T(8,128)(2,1)S(1)} %output.1.refs_0_), channel_id=1, source_target_pairs={{0,3},{1,2},{2,1},{3,0},{4,7},{5,6},{6,5},{7,4},{8,11},{9,10},{10,... | collective-permute-start | bytes 196616 | tf_op jit(solution)/shard_map/ppermute | solution.py:27
  58.3 5.5 %collective-permute-start.21 = (bf16[16,2048]{1,0:T(8,128)(2,1)S(1)}, bf16[16,2048]{1,0:T(8,128)(2,1)S(1)}, u32[]{:S(2)}, u32[]{:S(2)}) collective-permute-start(bf16[16,2048]{1,0:T(8,128)(2,1)S(1)} %output.1.refs_0_), channel_id=1, source_target_pairs={{0,1},{1,0},{2,3},{3,2},{4,5},{5,4},{6,7},{7,6},{8,9},{9,8},{10,11... | collective-permute-start | bytes 196616 | tf_op jit(solution)/shard_map/ppermute | solution.py:27

commit v18 on v16

--- a/solution.py
+++ b/solution.py
@@ -141,7 +141,7 @@
 
 def add_block(x_ref, w_ref, rows, acc, out, fresh):
     tokens = x_ref.shape[0]
-    tall = tokens
+    tall = tokens // 2
     for pair in range(KVH // 2):
         weight = pair_columns(w_ref, rows, pair, 0)
         columns = slice(2 * pair * HD, 2 * (pair + 1) * HD)
@@ -205,7 +205,7 @@
 
 def keys_kernel(acc, xa_ref, wa_ref, x_hbm, w_hbm, cos_ref, sin_ref, after, k_ref, x_ref, w_ref, total, sems):
     tokens, size = x_ref.shape
-    tall = tokens
+    tall = tokens // 2
     (copies,) = copies_of(x_hbm, w_hbm, x_ref, w_ref, sems, 3 * size, size, 1)
     start(copies)
     add_block(xa_ref, wa_ref, slice(2 * size, 3 * size), acc, total, False)

time: 63.5 us -> 63.8 us (level)
  transfers between devices with their start and end apart: 21 -> 21, of which waited for: 14 -> 14; matrix products, arithmetic and copies ran while one was open for 0% -> 0% of each run, Pallas kernels for 23% -> 22%
where the time goes in v18:
time: 63.8 us; the launch traced here: 63.7 us
  starting transfers between devices  24.8 us (39%)
  Pallas kernels  19.9 us (31%)
  waiting for transfers between devices  18.8 us (29%)
    ppermute x21, starting transfers between devices, pairs(): lax.ppermute(value, axis, [(i, i ^ d) for i in range(lax.axis_size(axis))])  24.8 us
    ppermute x21, waiting for transfers between devices, pairs(): lax.ppermute(value, axis, [(i, i ^ d) for i in range(lax.axis_size(axis))])  18.8 us
    pallas_call x1, Pallas kernels, load(): pl.pallas_call(functools.partial(load_kernel, pages, prompts, new_count),...  5.68 us
    pallas_call x2, Pallas kernels, project_values(): pl.pallas_call(functools.partial(values_kernel, first), in_specs=[VMEM] *...  4.68 us
    pallas_call x1, Pallas kernels, rotated_keys(): pl.pallas_call(keys_kernel, in_specs=[VMEM] * 3 + [hbm] * 2 + [VMEM] * 2...  3.61 us
    pallas_call x1, Pallas kernels, output_partial(): pl.pallas_call(functools.partial(output_kernel, n_seq), in_specs=[VMEM] *...  1.58 us
    pallas_call x1, Pallas kernels, partial_scores(): pl.pallas_call(functools.partial(scores_kernel, n_seq, n_tp), in_specs=[V...  1.34 us
  transfers between devices with their start and end apart: 21, of which 14 were waited for; matrix products, arithmetic and copies ran while one was open for 0% of the time, Pallas kernels for 22%

profile of v18, /device:TPU:0, one launch (start us, length us, event | category | flops | bytes accessed | tf_op | source)
XLA Modules:
  0.0 63.7 jit_solution(17067108432037868314)
XLA Ops:
  0.0 4.0 %collective-permute-start.1 = (bf16[2,2,2048]{2,1,0:T(2,128)(2,1)}, bf16[2,2,2048]{2,1,0:T(2,128)(2,1)S(1)}, u32[]{:S(2)}, u32[]{:S(2)}) collective-permute-start(bf16[2,2,2048]{2,1,0:T(2,128)(2,1)} %refs_0_.1), channel_id=1, source_target_pairs={{0,2},{1,3},{2,0},{3,1},{4,6},{5,7},{6,4},{7,5},{8,10},{9,11},{10,... | collective-permute-start | bytes 49160 | tf_op jit(solution)/shard_map/ppermute | solution.py:27
  4.0 1.3 %collective-permute-start = (bf16[2,2,2048]{2,1,0:T(2,128)(2,1)}, bf16[2,2,2048]{2,1,0:T(2,128)(2,1)S(1)}, u32[]{:S(2)}, u32[]{:S(2)}) collective-permute-start(bf16[2,2,2048]{2,1,0:T(2,128)(2,1)} %refs_0_.1), channel_id=1, source_target_pairs={{0,3},{1,2},{2,1},{3,0},{4,7},{5,6},{6,5},{7,4},{8,11},{9,10},{10,... | collective-permute-start | bytes 49160 | tf_op jit(solution)/shard_map/ppermute | solution.py:27
  5.6 5.7 %load.1 = (f32[1024,1024]{1,0:T(8,128)S(1)}, bf16[1024,1536]{1,0:T(8,128)(2,1)S(1)}, bf16[1536,2048]{1,0:T(8,128)(2,1)S(1)}, f32[1024,128]{1,0:T(8,128)S(1)}, f3...) custom-call(bf16[1024,2048]{1,0:T(8,128)(2,1)} %x_hbm.3, ...), custom_call_target="tpu_custom_call" | custom-call | flops 2147483648 | bytes 9437184 | tf_op jit(solution)/shard_map/load/pallas_call | solution.py:181
  11.5 1.6 %collective-permute-start.5 = (bf16[2,144,128]{2,1,0:T(8,128)(2,1)S(1)}, bf16[2,144,128]{2,1,0:T(8,128)(2,1)S(1)}, u32[]{:S(2)}, u32[]{:S(2)}) collective-permute-start(bf16[2,144,128]{2,1,0:T(8,128)(2,1)S(1)} %turned.1.after.refs_0_), channel_id=1, source_target_pairs={{0,8},{4,12},{8,0},{12,4},{1,9},{5,13},{9,1},{13,5},{2,10},{6,14},... | collective-permute-start | bytes 221192 | tf_op jit(solution)/shard_map/ppermute | solution.py:27
  13.1 0.6 collective-permute-start.3
  13.7 3.6 %keys.1 = (bf16[1024,1024]{1,0:T(8,128)(2,1)S(1)}, bf16[1024,512]{1,0:T(8,128)(2,1)S(1)}, bf16[512,2048]{1,0:T(8,128)(2,1)S(1)}) custom-call(f32[1024,1024]{1,0:T(8,128)S(1)} %get-tuple-element.34.acc, bf16[1024,1536]{1,0:T(8,128)(2,1)S(1)} %get-tuple-element.35.xa_ref, bf16[1536,2048]{1,0:T(8,128)(2,1)S(1)} %get-tuple-element.36.wa_ref, ...), custom_call_target="tpu_custom_call" | custom-call | flops 2147483648 | bytes 8388608 | tf_op jit(solution)/shard_map/keys/pallas_call | solution.py:230
  17.5 1.3 %scores.1 = (bf16[32,1024]{1,0:T(8,128)(2,1)S(1)}, bf16[32,1024]{1,0:T(8,128)(2,1)S(1)}, bf16[32,1024]{1,0:T(8,128)(2,1)S(1)}, bf16[32,1024]{1,0:T(8,128)(2,1)S(1)}) custom-call(bf16[2,144,128]{2,1,0:T(8,128)(2,1)S(1)} %turned.1.after.refs_0_, bf16[2,144,128]{2,1,0:T(8,128)(2,1)S(1)} %collective-permute-done.3.refs_1_, ...), custom_call_target="tpu_custom_call" | custom-call | flops 33554432 | bytes 6291456 | tf_op jit(solution)/shard_map/scores/pallas_call | solution.py:383
  18.9 2.9 %collective-permute-start.6 = (bf16[32,1024]{1,0:T(8,128)(2,1)S(1)}, bf16[32,1024]{1,0:T(8,128)(2,1)S(1)}, u32[]{:S(2)}, u32[]{:S(2)}) collective-permute-start(bf16[32,1024]{1,0:T(8,128)(2,1)S(1)} %get-tuple-element.42), channel_id=1, source_target_pairs={{0,2},{1,3},{2,0},{3,1},{4,6},{5,7},{6,4},{7,5},{8,10},{9,11},{10,... | collective-permute-start | bytes 196616 | tf_op jit(solution)/shard_map/ppermute | solution.py:27
  21.7 1.3 %collective-permute-start.7 = (bf16[32,1024]{1,0:T(8,128)(2,1)S(1)}, bf16[32,1024]{1,0:T(8,128)(2,1)S(1)}, u32[]{:S(2)}, u32[]{:S(2)}) collective-permute-start(bf16[32,1024]{1,0:T(8,128)(2,1)S(1)} %get-tuple-element.43), channel_id=1, source_target_pairs={{0,3},{1,2},{2,1},{3,0},{4,7},{5,6},{6,5},{7,4},{8,11},{9,10},{10,... | collective-permute-start | bytes 196616 | tf_op jit(solution)/shard_map/ppermute | solution.py:27
  23.1 2.3 %values.2 = (bf16[1024,512]{1,0:T(8,128)(2,1)S(1)}, bf16[1024,2048]{1,0:T(8,128)(2,1)S(1)}) custom-call(bf16[1024,1536]{1,0:T(8,128)(2,1)S(1)} %get-tuple-element.35.xa_ref, bf16[1536,2048]{1,0:T(8,128)(2,1)S(1)} %get-tuple-element.36.wa_ref, bf16[1024,512]{1,0:T(8,128)(2,1)S(1)} %get-tuple-element.45.xb_ref, ...), custom_call_target="tpu_custom_call" | custom-call | flops 1610612736 | bytes 8388608 | tf_op jit(solution)/shard_map/values/pallas_call | solution.py:272
  26.0 2.1 %collective-permute-done.7.refs_2_ = bf16[32,1024]{1,0:T(8,128)(2,1)S(1)} collective-permute-done((bf16[32,1024]{1,0:T(8,128)(2,1)S(1)}, bf16[32,1024]{1,0:T(8,128)(2,1)S(1)}, u32[]{:S(2)}, u32[]{:S(2)}) %collective-permute-start.7) | collective-permute-done | bytes 65568 | tf_op jit(solution)/shard_map/ppermute | solution.py:27
  28.2 0.9 %weights.1 = (bf16[32,1024]{1,0:T(8,128)(2,1)S(1)}, bf16[32,128]{1,0:T(8,128)(2,1)S(1)}) custom-call(bf16[32,1024]{1,0:T(8,128)(2,1)S(1)} %get-tuple-element.41.after.refs_0_, bf16[32,1024]{1,0:T(8,128)(2,1)S(1)} %collective-permute-done.6.refs_1_, bf16[32,1024]{1,0:T(8,128)(2,1)S(1)} %collective-permute-done.7.refs_2_, ...), custom_call_target="tpu_custom_call" | custom-call | tf_op jit(solution)/shard_map/weights/pallas_call | solution.py:495
  29.0 1.9 %collective-permute-start.11 = (bf16[32,1024]{1,0:T(8,128)(2,1)S(1)}, bf16[32,1024]{1,0:T(8,128)(2,1)S(1)}, u32[]{:S(2)}, u32[]{:S(2)}) collective-permute-start(bf16[32,1024]{1,0:T(8,128)(2,1)S(1)} %get-tuple-element.48.refs_0_), channel_id=1, source_target_pairs={{0,2},{1,3},{2,0},{3,1},{4,6},{5,7},{6,4},{7,5},{8,10},{9,11},{10,... | collective-permute-start | bytes 196616 | tf_op jit(solution)/shard_map/ppermute | solution.py:27
  30.9 1.2 %collective-permute-start.10 = (bf16[32,1024]{1,0:T(8,128)(2,1)S(1)}, bf16[32,1024]{1,0:T(8,128)(2,1)S(1)}, u32[]{:S(2)}, u32[]{:S(2)}) collective-permute-start(bf16[32,1024]{1,0:T(8,128)(2,1)S(1)} %get-tuple-element.48.refs_0_), channel_id=1, source_target_pairs={{0,3},{1,2},{2,1},{3,0},{4,7},{5,6},{6,5},{7,4},{8,11},{9,10},{10,... | collective-permute-start | bytes 196616 | tf_op jit(solution)/shard_map/ppermute | solution.py:27
  32.5 2.3 %values.3 = (bf16[1024,512]{1,0:T(8,128)(2,1)S(1)}, bf16[1024,2048]{1,0:T(8,128)(2,1)S(1)}) custom-call(bf16[1024,1536]{1,0:T(8,128)(2,1)S(1)} %get-tuple-element.35.xa_ref, bf16[1536,2048]{1,0:T(8,128)(2,1)S(1)} %get-tuple-element.36.wa_ref, bf16[1024,512]{1,0:T(8,128)(2,1)S(1)} %get-tuple-element.45.xb_ref, ...), custom_call_target="tpu_custom_call" | custom-call | flops 1610612736 | bytes 8388608 | tf_op jit(solution)/shard_map/values/pallas_call | solution.py:272
  34.9 1.0 %collective-permute-done.11.refs_3_ = bf16[32,1024]{1,0:T(8,128)(2,1)S(1)} collective-permute-done((bf16[32,1024]{1,0:T(8,128)(2,1)S(1)}, bf16[32,1024]{1,0:T(8,128)(2,1)S(1)}, u32[]{:S(2)}, u32[]{:S(2)}) %collective-permute-start.11) | collective-permute-done | bytes 65568 | tf_op jit(solution)/shard_map/ppermute | solution.py:27
  35.9 1.2 %collective-permute-done.10.refs_2_ = bf16[32,1024]{1,0:T(8,128)(2,1)S(1)} collective-permute-done((bf16[32,1024]{1,0:T(8,128)(2,1)S(1)}, bf16[32,1024]{1,0:T(8,128)(2,1)S(1)}, u32[]{:S(2)}, u32[]{:S(2)}) %collective-permute-start.10) | collective-permute-done | bytes 65568 | tf_op jit(solution)/shard_map/ppermute | solution.py:27
  37.3 1.1 %weighted.1 = (bf16[8,32,128]{2,1,0:T(8,128)(2,1)S(1)}, bf16[8,32,128]{2,1,0:T(8,128)(2,1)S(1)}, bf16[8,32,128]{2,1,0:T(8,128)(2,1)S(1)}, bf16[8,32,128]{2,1,0:T(8,128)(2,1)S(1)}) custom-call(bf16[32,1024]{1,0:T(8,128)(2,1)S(1)} %get-tuple-element.48.refs_0_, bf16[32,1024]{1,0:T(8,128)(2,1)S(1)} %collective-permute-done.9.refs_1_, ...), custom_call_target="tpu_custom_call" | custom-call | flops 33554432 | bytes 8388608 | tf_op jit(solution)/shard_map/weighted/pallas_call | solution.py:549
  38.4 1.7 %collective-permute-start.12 = (bf16[8,32,128]{2,1,0:T(8,128)(2,1)S(1)}, bf16[8,32,128]{2,1,0:T(8,128)(2,1)S(1)}, u32[]{:S(2)}, u32[]{:S(2)}) collective-permute-start(bf16[8,32,128]{2,1,0:T(8,128)(2,1)S(1)} %get-tuple-element.52), channel_id=1, source_target_pairs={{0,2},{1,3},{2,0},{3,1},{4,6},{5,7},{6,4},{7,5},{8,10},{9,11},{10,... | collective-permute-start | bytes 196616 | tf_op jit(solution)/shard_map/ppermute | solution.py:27
  40.2 1.2 %collective-permute-start.13 = (bf16[8,32,128]{2,1,0:T(8,128)(2,1)S(1)}, bf16[8,32,128]{2,1,0:T(8,128)(2,1)S(1)}, u32[]{:S(2)}, u32[]{:S(2)}) collective-permute-start(bf16[8,32,128]{2,1,0:T(8,128)(2,1)S(1)} %get-tuple-element.53), channel_id=1, source_target_pairs={{0,3},{1,2},{2,1},{3,0},{4,7},{5,6},{6,5},{7,4},{8,11},{9,10},{10,... | collective-permute-start | bytes 196616 | tf_op jit(solution)/shard_map/ppermute | solution.py:27
  42.0 3.1 %collective-permute-done.12.refs_1_ = bf16[8,32,128]{2,1,0:T(8,128)(2,1)S(1)} collective-permute-done((bf16[8,32,128]{2,1,0:T(8,128)(2,1)S(1)}, bf16[8,32,128]{2,1,0:T(8,128)(2,1)S(1)}, u32[]{:S(2)}, u32[]{:S(2)}) %collective-permute-start.12) | collective-permute-done | bytes 65568 | tf_op jit(solution)/shard_map/ppermute | solution.py:27
  45.0 1.3 %collective-permute-done.13.refs_2_ = bf16[8,32,128]{2,1,0:T(8,128)(2,1)S(1)} collective-permute-done((bf16[8,32,128]{2,1,0:T(8,128)(2,1)S(1)}, bf16[8,32,128]{2,1,0:T(8,128)(2,1)S(1)}, u32[]{:S(2)}, u32[]{:S(2)}) %collective-permute-start.13) | collective-permute-done | bytes 65568 | tf_op jit(solution)/shard_map/ppermute | solution.py:27
  46.5 1.6 %collective-permute-start.17 = (bf16[9,32,128]{2,1,0:T(8,128)(2,1)S(1)}, bf16[9,32,128]{2,1,0:T(8,128)(2,1)S(1)}, u32[]{:S(2)}, u32[]{:S(2)}) collective-permute-start(bf16[9,32,128]{2,1,0:T(8,128)(2,1)S(1)} %summed.1.refs_0_), channel_id=1, source_target_pairs={{0,8},{4,12},{8,0},{12,4},{1,9},{5,13},{9,1},{13,5},{2,10},{6,14},... | collective-permute-start | bytes 221192 | tf_op jit(solution)/shard_map/ppermute | solution.py:27
  48.1 0.6 collective-permute-start.15
  48.8 2.1 %collective-permute-done.17.refs_3_ = bf16[9,32,128]{2,1,0:T(8,128)(2,1)S(1)} collective-permute-done((bf16[9,32,128]{2,1,0:T(8,128)(2,1)S(1)}, bf16[9,32,128]{2,1,0:T(8,128)(2,1)S(1)}, u32[]{:S(2)}, u32[]{:S(2)}) %collective-permute-start.17) | collective-permute-done | bytes 73760 | tf_op jit(solution)/shard_map/ppermute | solution.py:27
  50.9 1.6 %collective-permute-done.16.refs_2_ = bf16[9,32,128]{2,1,0:T(8,128)(2,1)S(1)} collective-permute-done((bf16[9,32,128]{2,1,0:T(8,128)(2,1)S(1)}, bf16[9,32,128]{2,1,0:T(8,128)(2,1)S(1)}, u32[]{:S(2)}, u32[]{:S(2)}) %collective-permute-start.16) | collective-permute-done | bytes 73760 | tf_op jit(solution)/shard_map/ppermute | solution.py:27
  52.5 1.6 %output.1.refs_0_ = bf16[16,2048]{1,0:T(8,128)(2,1)S(1)} custom-call(bf16[9,32,128]{2,1,0:T(8,128)(2,1)S(1)} %summed.1.refs_0_, bf16[9,32,128]{2,1,0:T(8,128)(2,1)S(1)} %collective-permute-done.15.refs_1_, bf16[9,32,128]{2,1,0:T(8,128)(2,1)S(1)} %collective-permute-done.16.refs_2_, bf16[9,32,128]{2,1,0:T(8,128)(2,1)S(1)} %collective-permute-done.17.refs_3_, ...), custom_call_target="tpu_custom_call" | custom-call | tf_op jit(solution)/shard_map/output/pallas_call | solution.py:643
  54.1 1.0 %collective-permute-start.20 = (bf16[16,2048]{1,0:T(8,128)(2,1)S(1)}, bf16[16,2048]{1,0:T(8,128)(2,1)S(1)}, u32[]{:S(2)}, u32[]{:S(2)}) collective-permute-start(bf16[16,2048]{1,0:T(8,128)(2,1)S(1)} %output.1.refs_0_), channel_id=1, source_target_pairs={{0,2},{1,3},{2,0},{3,1},{4,6},{5,7},{6,4},{7,5},{8,10},{9,11},{10,... | collective-permute-start | bytes 196616 | tf_op jit(solution)/shard_map/ppermute | solution.py:27
  55.1 1.9 %collective-permute-start.19 = (bf16[16,2048]{1,0:T(8,128)(2,1)S(1)}, bf16[16,2048]{1,0:T(8,128)(2,1)S(1)}, u32[]{:S(2)}, u32[]{:S(2)}) collective-permute-start(bf16[16,2048]{1,0:T(8,128)(2,1)S(1)} %output.1.refs_0_), channel_id=1, source_target_pairs={{0,3},{1,2},{2,1},{3,0},{4,7},{5,6},{6,5},{7,4},{8,11},{9,10},{10,... | collective-permute-start | bytes 196616 | tf_op jit(solution)/shard_map/ppermute | solution.py:27
  57.6 4.5 %collective-permute-done.20.refs_3_ = bf16[16,2048]{1,0:T(8,128)(2,1)S(1)} collective-permute-done((bf16[16,2048]{1,0:T(8,128)(2,1)S(1)}, bf16[16,2048]{1,0:T(8,128)(2,1)S(1)}, u32[]{:S(2)}, u32[]{:S(2)}) %collective-permute-start.20) | collective-permute-done | bytes 65568 | tf_op jit(solution)/shard_map/ppermute | solution.py:27
  62.0 0.9 %collective-permute-done.18.refs_1_ = bf16[16,2048]{1,0:T(8,128)(2,1)S(1)} collective-permute-done((bf16[16,2048]{1,0:T(8,128)(2,1)S(1)}, bf16[16,2048]{1,0:T(8,128)(2,1)S(1)}, u32[]{:S(2)}, u32[]{:S(2)}) %collective-permute-start.18) | collective-permute-done | bytes 65568 | tf_op jit(solution)/shard_map/ppermute | solution.py:27
  62.9 0.7 %final.1 = f32[8,2,2048]{2,1,0:T(2,128)} custom-call(bf16[16,2048]{1,0:T(8,128)(2,1)S(1)} %output.1.refs_0_, bf16[16,2048]{1,0:T(8,128)(2,1)S(1)} %collective-permute-done.18.refs_1_, bf16[16,2048]{1,0:T(8,128)(2,1)S(1)} %collective-permute-done.19.refs_2_, bf16[16,2048]{1,0:T(8,128)(2,1)S(1)} %collective-permute-done.20.refs_3_, bf16[8,2,2048]{2,1,0:T(2,128)(2,1)S(1)} %copy-done), custom_call_target="tpu_custom_call" | custom-call | tf_op jit(solution)/shard_map/final/pallas_call | solution.py:667
  (28 shorter events, 3.1 us)
Async XLA Ops:
  0.0 11.3 %copy-start.1 = (bf16[2,2,2048]{2,1,0:T(2,128)(2,1)S(1)}, bf16[2,2,2048]{2,1,0:T(2,128)(2,1)}, u32[]{:S(2)}) copy-start(bf16[2,2,2048]{2,1,0:T(2,128)(2,1)} %refs_0_.1) | copy-start | bytes 49156
  0.0 11.4 %copy-start.2 = (bf16[2,2,512]{2,1,0:T(2,128)(2,1)S(1)}, bf16[2,2,512]{2,1,0:T(2,128)(2,1)}, u32[]{:S(2)}) copy-start(bf16[2,2,512]{2,1,0:T(2,128)(2,1)} %refs_4_.2) | copy-start | bytes 12292
  0.0 11.3 %collective-permute-start.1 = (bf16[2,2,2048]{2,1,0:T(2,128)(2,1)}, bf16[2,2,2048]{2,1,0:T(2,128)(2,1)S(1)}, u32[]{:S(2)}, u32[]{:S(2)}) collective-permute-start(bf16[2,2,2048]{2,1,0:T(2,128)(2,1)} %refs_0_.1), channel_id=1, source_target_pairs={{0,2},{1,3},{2,0},{3,1},{4,6},{5,7},{6,4},{7,5},{8,10},{9,11},{10,... | collective-permute-start | bytes 49160 | tf_op jit(solution)/shard_map/ppermute | solution.py:27
  4.0 7.3 %collective-permute-start = (bf16[2,2,2048]{2,1,0:T(2,128)(2,1)}, bf16[2,2,2048]{2,1,0:T(2,128)(2,1)S(1)}, u32[]{:S(2)}, u32[]{:S(2)}) collective-permute-start(bf16[2,2,2048]{2,1,0:T(2,128)(2,1)} %refs_0_.1), channel_id=1, source_target_pairs={{0,3},{1,2},{2,1},{3,0},{4,7},{5,6},{6,5},{7,4},{8,11},{9,10},{10,... | collective-permute-start | bytes 49160 | tf_op jit(solution)/shard_map/ppermute | solution.py:27
  5.4 5.9 %collective-permute-start.2 = (bf16[2,2,2048]{2,1,0:T(2,128)(2,1)}, bf16[2,2,2048]{2,1,0:T(2,128)(2,1)S(1)}, u32[]{:S(2)}, u32[]{:S(2)}) collective-permute-start(bf16[2,2,2048]{2,1,0:T(2,128)(2,1)} %refs_0_.1), channel_id=1, source_target_pairs={{0,1},{1,0},{2,3},{3,2},{4,5},{5,4},{6,7},{7,6},{8,9},{9,8},{10,11... | collective-permute-start | bytes 49160 | tf_op jit(solution)/shard_map/ppermute | solution.py:27
  11.5 5.8 %collective-permute-start.5 = (bf16[2,144,128]{2,1,0:T(8,128)(2,1)S(1)}, bf16[2,144,128]{2,1,0:T(8,128)(2,1)S(1)}, u32[]{:S(2)}, u32[]{:S(2)}) collective-permute-start(bf16[2,144,128]{2,1,0:T(8,128)(2,1)S(1)} %turned.1.after.refs_0_), channel_id=1, source_target_pairs={{0,8},{4,12},{8,0},{12,4},{1,9},{5,13},{9,1},{13,5},{2,10},{6,14},... | collective-permute-start | bytes 221192 | tf_op jit(solution)/shard_map/ppermute | solution.py:27
  13.1 4.4 %collective-permute-start.4 = (bf16[2,144,128]{2,1,0:T(8,128)(2,1)S(1)}, bf16[2,144,128]{2,1,0:T(8,128)(2,1)S(1)}, u32[]{:S(2)}, u32[]{:S(2)}) collective-permute-start(bf16[2,144,128]{2,1,0:T(8,128)(2,1)S(1)} %turned.1.after.refs_0_), channel_id=1, source_target_pairs={{0,12},{4,8},{8,4},{12,0},{1,13},{5,9},{9,5},{13,1},{2,14},{6,10},... | collective-permute-start | bytes 221192 | tf_op jit(solution)/shard_map/ppermute | solution.py:27
  13.1 4.4 %collective-permute-start.3 = (bf16[2,144,128]{2,1,0:T(8,128)(2,1)S(1)}, bf16[2,144,128]{2,1,0:T(8,128)(2,1)S(1)}, u32[]{:S(2)}, u32[]{:S(2)}) collective-permute-start(bf16[2,144,128]{2,1,0:T(8,128)(2,1)S(1)} %turned.1.after.refs_0_), channel_id=1, source_target_pairs={{0,4},{4,0},{8,12},{12,8},{1,5},{5,1},{9,13},{13,9},{2,6},{6,2},{1... | collective-permute-start | bytes 221192 | tf_op jit(solution)/shard_map/ppermute | solution.py:27
  18.9 7.1 %collective-permute-start.6 = (bf16[32,1024]{1,0:T(8,128)(2,1)S(1)}, bf16[32,1024]{1,0:T(8,128)(2,1)S(1)}, u32[]{:S(2)}, u32[]{:S(2)}) collective-permute-start(bf16[32,1024]{1,0:T(8,128)(2,1)S(1)} %get-tuple-element.42), channel_id=1, source_target_pairs={{0,2},{1,3},{2,0},{3,1},{4,6},{5,7},{6,4},{7,5},{8,10},{9,11},{10,... | collective-permute-start | bytes 196616 | tf_op jit(solution)/shard_map/ppermute | solution.py:27
  21.7 6.3 %collective-permute-start.7 = (bf16[32,1024]{1,0:T(8,128)(2,1)S(1)}, bf16[32,1024]{1,0:T(8,128)(2,1)S(1)}, u32[]{:S(2)}, u32[]{:S(2)}) collective-permute-start(bf16[32,1024]{1,0:T(8,128)(2,1)S(1)} %get-tuple-element.43), channel_id=1, source_target_pairs={{0,3},{1,2},{2,1},{3,0},{4,7},{5,6},{6,5},{7,4},{8,11},{9,10},{10,... | collective-permute-start | bytes 196616 | tf_op jit(solution)/shard_map/ppermute | solution.py:27
  23.1 5.1 %collective-permute-start.8 = (bf16[32,1024]{1,0:T(8,128)(2,1)S(1)}, bf16[32,1024]{1,0:T(8,128)(2,1)S(1)}, u32[]{:S(2)}, u32[]{:S(2)}) collective-permute-start(bf16[32,1024]{1,0:T(8,128)(2,1)S(1)} %get-tuple-element.44), channel_id=1, source_target_pairs={{0,1},{1,0},{2,3},{3,2},{4,5},{5,4},{6,7},{7,6},{8,9},{9,8},{10,11... | collective-permute-start | bytes 196616 | tf_op jit(solution)/shard_map/ppermute | solution.py:27
  29.0 6.9 %collective-permute-start.11 = (bf16[32,1024]{1,0:T(8,128)(2,1)S(1)}, bf16[32,1024]{1,0:T(8,128)(2,1)S(1)}, u32[]{:S(2)}, u32[]{:S(2)}) collective-permute-start(bf16[32,1024]{1,0:T(8,128)(2,1)S(1)} %get-tuple-element.48.refs_0_), channel_id=1, source_target_pairs={{0,2},{1,3},{2,0},{3,1},{4,6},{5,7},{6,4},{7,5},{8,10},{9,11},{10,... | collective-permute-start | bytes 196616 | tf_op jit(solution)/shard_map/ppermute | solution.py:27
  30.9 6.2 %collective-permute-start.10 = (bf16[32,1024]{1,0:T(8,128)(2,1)S(1)}, bf16[32,1024]{1,0:T(8,128)(2,1)S(1)}, u32[]{:S(2)}, u32[]{:S(2)}) collective-permute-start(bf16[32,1024]{1,0:T(8,128)(2,1)S(1)} %get-tuple-element.48.refs_0_), channel_id=1, source_target_pairs={{0,3},{1,2},{2,1},{3,0},{4,7},{5,6},{6,5},{7,4},{8,11},{9,10},{10,... | collective-permute-start | bytes 196616 | tf_op jit(solution)/shard_map/ppermute | solution.py:27
  32.1 5.2 %collective-permute-start.9 = (bf16[32,1024]{1,0:T(8,128)(2,1)S(1)}, bf16[32,1024]{1,0:T(8,128)(2,1)S(1)}, u32[]{:S(2)}, u32[]{:S(2)}) collective-permute-start(bf16[32,1024]{1,0:T(8,128)(2,1)S(1)} %get-tuple-element.48.refs_0_), channel_id=1, source_target_pairs={{0,1},{1,0},{2,3},{3,2},{4,5},{5,4},{6,7},{7,6},{8,9},{9,8},{10,11... | collective-permute-start | bytes 196616 | tf_op jit(solution)/shard_map/ppermute | solution.py:27
  38.4 6.6 %collective-permute-start.12 = (bf16[8,32,128]{2,1,0:T(8,128)(2,1)S(1)}, bf16[8,32,128]{2,1,0:T(8,128)(2,1)S(1)}, u32[]{:S(2)}, u32[]{:S(2)}) collective-permute-start(bf16[8,32,128]{2,1,0:T(8,128)(2,1)S(1)} %get-tuple-element.52), channel_id=1, source_target_pairs={{0,2},{1,3},{2,0},{3,1},{4,6},{5,7},{6,4},{7,5},{8,10},{9,11},{10,... | collective-permute-start | bytes 196616 | tf_op jit(solution)/shard_map/ppermute | solution.py:27
  40.2 6.2 %collective-permute-start.13 = (bf16[8,32,128]{2,1,0:T(8,128)(2,1)S(1)}, bf16[8,32,128]{2,1,0:T(8,128)(2,1)S(1)}, u32[]{:S(2)}, u32[]{:S(2)}) collective-permute-start(bf16[8,32,128]{2,1,0:T(8,128)(2,1)S(1)} %get-tuple-element.53), channel_id=1, source_target_pairs={{0,3},{1,2},{2,1},{3,0},{4,7},{5,6},{6,5},{7,4},{8,11},{9,10},{10,... | collective-permute-start | bytes 196616 | tf_op jit(solution)/shard_map/ppermute | solution.py:27
  41.4 5.0 %collective-permute-start.14 = (bf16[8,32,128]{2,1,0:T(8,128)(2,1)S(1)}, bf16[8,32,128]{2,1,0:T(8,128)(2,1)S(1)}, u32[]{:S(2)}, u32[]{:S(2)}) collective-permute-start(bf16[8,32,128]{2,1,0:T(8,128)(2,1)S(1)} %get-tuple-element.54), channel_id=1, source_target_pairs={{0,1},{1,0},{2,3},{3,2},{4,5},{5,4},{6,7},{7,6},{8,9},{9,8},{10,11... | collective-permute-start | bytes 196616 | tf_op jit(solution)/shard_map/ppermute | solution.py:27
  46.5 4.4 %collective-permute-start.17 = (bf16[9,32,128]{2,1,0:T(8,128)(2,1)S(1)}, bf16[9,32,128]{2,1,0:T(8,128)(2,1)S(1)}, u32[]{:S(2)}, u32[]{:S(2)}) collective-permute-start(bf16[9,32,128]{2,1,0:T(8,128)(2,1)S(1)} %summed.1.refs_0_), channel_id=1, source_target_pairs={{0,8},{4,12},{8,0},{12,4},{1,9},{5,13},{9,1},{13,5},{2,10},{6,14},... | collective-permute-start | bytes 221192 | tf_op jit(solution)/shard_map/ppermute | solution.py:27
  48.1 4.4 %collective-permute-start.16 = (bf16[9,32,128]{2,1,0:T(8,128)(2,1)S(1)}, bf16[9,32,128]{2,1,0:T(8,128)(2,1)S(1)}, u32[]{:S(2)}, u32[]{:S(2)}) collective-permute-start(bf16[9,32,128]{2,1,0:T(8,128)(2,1)S(1)} %summed.1.refs_0_), channel_id=1, source_target_pairs={{0,12},{4,8},{8,4},{12,0},{1,13},{5,9},{9,5},{13,1},{2,14},{6,10},... | collective-permute-start | bytes 221192 | tf_op jit(solution)/shard_map/ppermute | solution.py:27
  48.1 4.4 %collective-permute-start.15 = (bf16[9,32,128]{2,1,0:T(8,128)(2,1)S(1)}, bf16[9,32,128]{2,1,0:T(8,128)(2,1)S(1)}, u32[]{:S(2)}, u32[]{:S(2)}) collective-permute-start(bf16[9,32,128]{2,1,0:T(8,128)(2,1)S(1)} %summed.1.refs_0_), channel_id=1, source_target_pairs={{0,4},{4,0},{8,12},{12,8},{1,5},{5,1},{9,13},{13,9},{2,6},{6,2},{1... | collective-permute-start | bytes 221192 | tf_op jit(solution)/shard_map/ppermute | solution.py:27
  52.5 10.5 %copy-start = (bf16[8,2,2048]{2,1,0:T(2,128)(2,1)S(1)}, bf16[8,2,2048]{2,1,0:T(2,128)(2,1)}, u32[]{:S(2)}) copy-start(bf16[8,2,2048]{2,1,0:T(2,128)(2,1)} %refs_4_.3) | copy-start | bytes 196612
  54.1 8.0 %collective-permute-start.20 = (bf16[16,2048]{1,0:T(8,128)(2,1)S(1)}, bf16[16,2048]{1,0:T(8,128)(2,1)S(1)}, u32[]{:S(2)}, u32[]{:S(2)}) collective-permute-start(bf16[16,2048]{1,0:T(8,128)(2,1)S(1)} %output.1.refs_0_), channel_id=1, source_target_pairs={{0,2},{1,3},{2,0},{3,1},{4,6},{5,7},{6,4},{7,5},{8,10},{9,11},{10,... | collective-permute-start | bytes 196616 | tf_op jit(solution)/shard_map/ppermute | solution.py:27
  55.1 6.9 %collective-permute-start.19 = (bf16[16,2048]{1,0:T(8,128)(2,1)S(1)}, bf16[16,2048]{1,0:T(8,128)(2,1)S(1)}, u32[]{:S(2)}, u32[]{:S(2)}) collective-permute-start(bf16[16,2048]{1,0:T(8,128)(2,1)S(1)} %output.1.refs_0_), channel_id=1, source_target_pairs={{0,3},{1,2},{2,1},{3,0},{4,7},{5,6},{6,5},{7,4},{8,11},{9,10},{10,... | collective-permute-start | bytes 196616 | tf_op jit(solution)/shard_map/ppermute | solution.py:27
  57.0 5.9 %collective-permute-start.18 = (bf16[16,2048]{1,0:T(8,128)(2,1)S(1)}, bf16[16,2048]{1,0:T(8,128)(2,1)S(1)}, u32[]{:S(2)}, u32[]{:S(2)}) collective-permute-start(bf16[16,2048]{1,0:T(8,128)(2,1)S(1)} %output.1.refs_0_), channel_id=1, source_target_pairs={{0,1},{1,0},{2,3},{3,2},{4,5},{5,4},{6,7},{7,6},{8,9},{9,8},{10,11... | collective-permute-start | bytes 196616 | tf_op jit(solution)/shard_map/ppermute | solution.py:27

commit v19 on v18

--- a/solution.py
+++ b/solution.py
@@ -152,12 +152,19 @@
 
 
 def load_kernel(pages, prompts, new_count, x_hbm, w_hbm, counts, tails, *refs):
-    acc, x_ref, w_ref, cos_ref, sin_ref, cos_q, sin_q, meta, sems = refs
+    acc, x_ref, w_ref, cos_ref, sin_ref, cos_q, sin_q, meta, sems = refs[:9]
+    counts_s, tails_s, small_sems = refs[9:]
     tokens = x_ref.shape[0]
     size = x_ref.shape[1] // 3
     copies = copies_of(x_hbm, w_hbm, x_ref, w_ref, sems, 0, size, 3)
     start(copies[0])
-    page_table(pages, prompts, counts, tails, meta)
+    small = [
+        pltpu.make_async_copy(counts, counts_s, small_sems.at[0]),
+        pltpu.make_async_copy(tails, tails_s, small_sems.at[1]),
+    ]
+    start(small)
+    wait(small)
+    page_table(pages, prompts, counts_s, tails_s, meta)
     rotation_tables(pages, tokens // PAGE, meta, cos_ref, sin_ref)
     spots = [meta[3 * pages + r] + n for r in range(prompts) for n in range(new_count)]
     angles = by_row(len(spots), spots) * lane_freqs(len(spots))
@@ -180,7 +187,7 @@
     hbm = pl.BlockSpec(memory_space=pltpu.HBM)
     return pl.pallas_call(
         functools.partial(load_kernel, pages, prompts, new_count),
-        in_specs=[hbm, hbm, SMEM, SMEM],
+        in_specs=[hbm] * 4,
         out_specs=[VMEM] * 7 + [SMEM],
         out_shape=[
             pltpu.VMEM((tokens, KVH * HD), F32),
@@ -192,7 +199,12 @@
             pltpu.VMEM((prompts * new_count, HD), F32),
             jax.ShapeDtypeStruct((3 * pages + prompts,), jnp.int32),
         ],
-        scratch_shapes=[pltpu.SemaphoreType.DMA((6,))],
+        scratch_shapes=[
+            pltpu.SemaphoreType.DMA((6,)),
+            pltpu.SMEM((prompts,), jnp.int32),
+            pltpu.SMEM((prompts,), jnp.int32),
+            pltpu.SemaphoreType.DMA((2,)),
+        ],
         compiler_params=pltpu.CompilerParams(vmem_limit_bytes=28 * MIB),
         cost_estimate=pl.CostEstimate(
             flops=tokens * depth * KVH * HD,

time: 63.8 us -> 63.3 us (level)
  no operation moved by 1% of the time
where the time goes in v19:
time: 63.3 us; the launch traced here: 63.1 us
  starting transfers between devices  24.8 us (39%)
  Pallas kernels  19.4 us (31%)
  waiting for transfers between devices  18.8 us (30%)
    ppermute x21, starting transfers between devices, pairs(): lax.ppermute(value, axis, [(i, i ^ d) for i in range(lax.axis_size(axis))])  24.8 us
    ppermute x21, waiting for transfers between devices, pairs(): lax.ppermute(value, axis, [(i, i ^ d) for i in range(lax.axis_size(axis))])  18.8 us
    pallas_call x1, Pallas kernels, load(): pl.pallas_call(functools.partial(load_kernel, pages, prompts, new_count),...  5.15 us
    pallas_call x2, Pallas kernels, project_values(): pl.pallas_call(functools.partial(values_kernel, first), in_specs=[VMEM] *...  4.68 us
    pallas_call x1, Pallas kernels, rotated_keys(): pl.pallas_call(keys_kernel, in_specs=[VMEM] * 3 + [hbm] * 2 + [VMEM] * 2...  3.61 us
    pallas_call x1, Pallas kernels, output_partial(): pl.pallas_call(functools.partial(output_kernel, n_seq), in_specs=[VMEM] *...  1.58 us
    pallas_call x1, Pallas kernels, partial_scores(): pl.pallas_call(functools.partial(scores_kernel, n_seq, n_tp), in_specs=[V...  1.34 us
  transfers between devices with their start and end apart: 21, of which 14 were waited for; matrix products, arithmetic and copies ran while one was open for 0% of the time, Pallas kernels for 22%

profile of v19, /device:TPU:0, one launch (start us, length us, event | category | flops | bytes accessed | tf_op | source)
XLA Modules:
  0.0 63.1 jit_solution(7170100753213669905)
XLA Ops:
  0.0 4.0 %collective-permute-start.1 = (bf16[2,2,2048]{2,1,0:T(2,128)(2,1)}, bf16[2,2,2048]{2,1,0:T(2,128)(2,1)S(1)}, u32[]{:S(2)}, u32[]{:S(2)}) collective-permute-start(bf16[2,2,2048]{2,1,0:T(2,128)(2,1)} %refs_0_.1), channel_id=1, source_target_pairs={{0,2},{1,3},{2,0},{3,1},{4,6},{5,7},{6,4},{7,5},{8,10},{9,11},{10,... | collective-permute-start | bytes 49160 | tf_op jit(solution)/shard_map/ppermute | solution.py:27
  4.0 1.3 %collective-permute-start = (bf16[2,2,2048]{2,1,0:T(2,128)(2,1)}, bf16[2,2,2048]{2,1,0:T(2,128)(2,1)S(1)}, u32[]{:S(2)}, u32[]{:S(2)}) collective-permute-start(bf16[2,2,2048]{2,1,0:T(2,128)(2,1)} %refs_0_.1), channel_id=1, source_target_pairs={{0,3},{1,2},{2,1},{3,0},{4,7},{5,6},{6,5},{7,4},{8,11},{9,10},{10,... | collective-permute-start | bytes 49160 | tf_op jit(solution)/shard_map/ppermute | solution.py:27
  5.6 5.2 %load.1 = (f32[1024,1024]{1,0:T(8,128)S(1)}, bf16[1024,1536]{1,0:T(8,128)(2,1)S(1)}, bf16[1536,2048]{1,0:T(8,128)(2,1)S(1)}, f32[1024,128]{1,0:T(8,128)S(1)}, f3...) custom-call(bf16[1024,2048]{1,0:T(8,128)(2,1)} %x_hbm.3, ...), custom_call_target="tpu_custom_call" | custom-call | flops 2147483648 | bytes 9437184 | tf_op jit(solution)/shard_map/load/pallas_call | solution.py:188
  11.0 1.6 %collective-permute-start.5 = (bf16[2,144,128]{2,1,0:T(8,128)(2,1)S(1)}, bf16[2,144,128]{2,1,0:T(8,128)(2,1)S(1)}, u32[]{:S(2)}, u32[]{:S(2)}) collective-permute-start(bf16[2,144,128]{2,1,0:T(8,128)(2,1)S(1)} %turned.1.after.refs_0_), channel_id=1, source_target_pairs={{0,8},{4,12},{8,0},{12,4},{1,9},{5,13},{9,1},{13,5},{2,10},{6,14},... | collective-permute-start | bytes 221192 | tf_op jit(solution)/shard_map/ppermute | solution.py:27
  12.6 0.6 collective-permute-start.3
  13.2 3.6 %keys.1 = (bf16[1024,1024]{1,0:T(8,128)(2,1)S(1)}, bf16[1024,512]{1,0:T(8,128)(2,1)S(1)}, bf16[512,2048]{1,0:T(8,128)(2,1)S(1)}) custom-call(f32[1024,1024]{1,0:T(8,128)S(1)} %get-tuple-element.34.acc, bf16[1024,1536]{1,0:T(8,128)(2,1)S(1)} %get-tuple-element.35.xa_ref, bf16[1536,2048]{1,0:T(8,128)(2,1)S(1)} %get-tuple-element.36.wa_ref, ...), custom_call_target="tpu_custom_call" | custom-call | flops 2147483648 | bytes 8388608 | tf_op jit(solution)/shard_map/keys/pallas_call | solution.py:242
  17.0 1.3 %scores.1 = (bf16[32,1024]{1,0:T(8,128)(2,1)S(1)}, bf16[32,1024]{1,0:T(8,128)(2,1)S(1)}, bf16[32,1024]{1,0:T(8,128)(2,1)S(1)}, bf16[32,1024]{1,0:T(8,128)(2,1)S(1)}) custom-call(bf16[2,144,128]{2,1,0:T(8,128)(2,1)S(1)} %turned.1.after.refs_0_, bf16[2,144,128]{2,1,0:T(8,128)(2,1)S(1)} %collective-permute-done.3.refs_1_, ...), custom_call_target="tpu_custom_call" | custom-call | flops 33554432 | bytes 6291456 | tf_op jit(solution)/shard_map/scores/pallas_call | solution.py:395
  18.3 2.9 %collective-permute-start.6 = (bf16[32,1024]{1,0:T(8,128)(2,1)S(1)}, bf16[32,1024]{1,0:T(8,128)(2,1)S(1)}, u32[]{:S(2)}, u32[]{:S(2)}) collective-permute-start(bf16[32,1024]{1,0:T(8,128)(2,1)S(1)} %get-tuple-element.42), channel_id=1, source_target_pairs={{0,2},{1,3},{2,0},{3,1},{4,6},{5,7},{6,4},{7,5},{8,10},{9,11},{10,... | collective-permute-start | bytes 196616 | tf_op jit(solution)/shard_map/ppermute | solution.py:27
  21.2 1.3 %collective-permute-start.7 = (bf16[32,1024]{1,0:T(8,128)(2,1)S(1)}, bf16[32,1024]{1,0:T(8,128)(2,1)S(1)}, u32[]{:S(2)}, u32[]{:S(2)}) collective-permute-start(bf16[32,1024]{1,0:T(8,128)(2,1)S(1)} %get-tuple-element.43), channel_id=1, source_target_pairs={{0,3},{1,2},{2,1},{3,0},{4,7},{5,6},{6,5},{7,4},{8,11},{9,10},{10,... | collective-permute-start | bytes 196616 | tf_op jit(solution)/shard_map/ppermute | solution.py:27
  22.6 2.3 %values.2 = (bf16[1024,512]{1,0:T(8,128)(2,1)S(1)}, bf16[1024,2048]{1,0:T(8,128)(2,1)S(1)}) custom-call(bf16[1024,1536]{1,0:T(8,128)(2,1)S(1)} %get-tuple-element.35.xa_ref, bf16[1536,2048]{1,0:T(8,128)(2,1)S(1)} %get-tuple-element.36.wa_ref, bf16[1024,512]{1,0:T(8,128)(2,1)S(1)} %get-tuple-element.45.xb_ref, ...), custom_call_target="tpu_custom_call" | custom-call | flops 1610612736 | bytes 8388608 | tf_op jit(solution)/shard_map/values/pallas_call | solution.py:284
  25.4 2.1 %collective-permute-done.7.refs_2_ = bf16[32,1024]{1,0:T(8,128)(2,1)S(1)} collective-permute-done((bf16[32,1024]{1,0:T(8,128)(2,1)S(1)}, bf16[32,1024]{1,0:T(8,128)(2,1)S(1)}, u32[]{:S(2)}, u32[]{:S(2)}) %collective-permute-start.7) | collective-permute-done | bytes 65568 | tf_op jit(solution)/shard_map/ppermute | solution.py:27
  27.6 0.9 %weights.1 = (bf16[32,1024]{1,0:T(8,128)(2,1)S(1)}, bf16[32,128]{1,0:T(8,128)(2,1)S(1)}) custom-call(bf16[32,1024]{1,0:T(8,128)(2,1)S(1)} %get-tuple-element.41.after.refs_0_, bf16[32,1024]{1,0:T(8,128)(2,1)S(1)} %collective-permute-done.6.refs_1_, bf16[32,1024]{1,0:T(8,128)(2,1)S(1)} %collective-permute-done.7.refs_2_, ...), custom_call_target="tpu_custom_call" | custom-call | tf_op jit(solution)/shard_map/weights/pallas_call | solution.py:507
  28.5 1.9 %collective-permute-start.11 = (bf16[32,1024]{1,0:T(8,128)(2,1)S(1)}, bf16[32,1024]{1,0:T(8,128)(2,1)S(1)}, u32[]{:S(2)}, u32[]{:S(2)}) collective-permute-start(bf16[32,1024]{1,0:T(8,128)(2,1)S(1)} %get-tuple-element.48.refs_0_), channel_id=1, source_target_pairs={{0,2},{1,3},{2,0},{3,1},{4,6},{5,7},{6,4},{7,5},{8,10},{9,11},{10,... | collective-permute-start | bytes 196616 | tf_op jit(solution)/shard_map/ppermute | solution.py:27
  30.4 1.2 %collective-permute-start.10 = (bf16[32,1024]{1,0:T(8,128)(2,1)S(1)}, bf16[32,1024]{1,0:T(8,128)(2,1)S(1)}, u32[]{:S(2)}, u32[]{:S(2)}) collective-permute-start(bf16[32,1024]{1,0:T(8,128)(2,1)S(1)} %get-tuple-element.48.refs_0_), channel_id=1, source_target_pairs={{0,3},{1,2},{2,1},{3,0},{4,7},{5,6},{6,5},{7,4},{8,11},{9,10},{10,... | collective-permute-start | bytes 196616 | tf_op jit(solution)/shard_map/ppermute | solution.py:27
  32.0 2.3 %values.3 = (bf16[1024,512]{1,0:T(8,128)(2,1)S(1)}, bf16[1024,2048]{1,0:T(8,128)(2,1)S(1)}) custom-call(bf16[1024,1536]{1,0:T(8,128)(2,1)S(1)} %get-tuple-element.35.xa_ref, bf16[1536,2048]{1,0:T(8,128)(2,1)S(1)} %get-tuple-element.36.wa_ref, bf16[1024,512]{1,0:T(8,128)(2,1)S(1)} %get-tuple-element.45.xb_ref, ...), custom_call_target="tpu_custom_call" | custom-call | flops 1610612736 | bytes 8388608 | tf_op jit(solution)/shard_map/values/pallas_call | solution.py:284
  34.4 1.0 %collective-permute-done.11.refs_3_ = bf16[32,1024]{1,0:T(8,128)(2,1)S(1)} collective-permute-done((bf16[32,1024]{1,0:T(8,128)(2,1)S(1)}, bf16[32,1024]{1,0:T(8,128)(2,1)S(1)}, u32[]{:S(2)}, u32[]{:S(2)}) %collective-permute-start.11) | collective-permute-done | bytes 65568 | tf_op jit(solution)/shard_map/ppermute | solution.py:27
  35.4 1.2 %collective-permute-done.10.refs_2_ = bf16[32,1024]{1,0:T(8,128)(2,1)S(1)} collective-permute-done((bf16[32,1024]{1,0:T(8,128)(2,1)S(1)}, bf16[32,1024]{1,0:T(8,128)(2,1)S(1)}, u32[]{:S(2)}, u32[]{:S(2)}) %collective-permute-start.10) | collective-permute-done | bytes 65568 | tf_op jit(solution)/shard_map/ppermute | solution.py:27
  36.8 1.1 %weighted.1 = (bf16[8,32,128]{2,1,0:T(8,128)(2,1)S(1)}, bf16[8,32,128]{2,1,0:T(8,128)(2,1)S(1)}, bf16[8,32,128]{2,1,0:T(8,128)(2,1)S(1)}, bf16[8,32,128]{2,1,0:T(8,128)(2,1)S(1)}) custom-call(bf16[32,1024]{1,0:T(8,128)(2,1)S(1)} %get-tuple-element.48.refs_0_, bf16[32,1024]{1,0:T(8,128)(2,1)S(1)} %collective-permute-done.9.refs_1_, ...), custom_call_target="tpu_custom_call" | custom-call | flops 33554432 | bytes 8388608 | tf_op jit(solution)/shard_map/weighted/pallas_call | solution.py:561
  37.9 1.8 %collective-permute-start.12 = (bf16[8,32,128]{2,1,0:T(8,128)(2,1)S(1)}, bf16[8,32,128]{2,1,0:T(8,128)(2,1)S(1)}, u32[]{:S(2)}, u32[]{:S(2)}) collective-permute-start(bf16[8,32,128]{2,1,0:T(8,128)(2,1)S(1)} %get-tuple-element.52), channel_id=1, source_target_pairs={{0,2},{1,3},{2,0},{3,1},{4,6},{5,7},{6,4},{7,5},{8,10},{9,11},{10,... | collective-permute-start | bytes 196616 | tf_op jit(solution)/shard_map/ppermute | solution.py:27
  39.6 1.2 %collective-permute-start.13 = (bf16[8,32,128]{2,1,0:T(8,128)(2,1)S(1)}, bf16[8,32,128]{2,1,0:T(8,128)(2,1)S(1)}, u32[]{:S(2)}, u32[]{:S(2)}) collective-permute-start(bf16[8,32,128]{2,1,0:T(8,128)(2,1)S(1)} %get-tuple-element.53), channel_id=1, source_target_pairs={{0,3},{1,2},{2,1},{3,0},{4,7},{5,6},{6,5},{7,4},{8,11},{9,10},{10,... | collective-permute-start | bytes 196616 | tf_op jit(solution)/shard_map/ppermute | solution.py:27
  41.4 3.1 %collective-permute-done.12.refs_1_ = bf16[8,32,128]{2,1,0:T(8,128)(2,1)S(1)} collective-permute-done((bf16[8,32,128]{2,1,0:T(8,128)(2,1)S(1)}, bf16[8,32,128]{2,1,0:T(8,128)(2,1)S(1)}, u32[]{:S(2)}, u32[]{:S(2)}) %collective-permute-start.12) | collective-permute-done | bytes 65568 | tf_op jit(solution)/shard_map/ppermute | solution.py:27
  44.5 1.3 %collective-permute-done.13.refs_2_ = bf16[8,32,128]{2,1,0:T(8,128)(2,1)S(1)} collective-permute-done((bf16[8,32,128]{2,1,0:T(8,128)(2,1)S(1)}, bf16[8,32,128]{2,1,0:T(8,128)(2,1)S(1)}, u32[]{:S(2)}, u32[]{:S(2)}) %collective-permute-start.13) | collective-permute-done | bytes 65568 | tf_op jit(solution)/shard_map/ppermute | solution.py:27
  46.0 1.6 %collective-permute-start.17 = (bf16[9,32,128]{2,1,0:T(8,128)(2,1)S(1)}, bf16[9,32,128]{2,1,0:T(8,128)(2,1)S(1)}, u32[]{:S(2)}, u32[]{:S(2)}) collective-permute-start(bf16[9,32,128]{2,1,0:T(8,128)(2,1)S(1)} %summed.1.refs_0_), channel_id=1, source_target_pairs={{0,8},{4,12},{8,0},{12,4},{1,9},{5,13},{9,1},{13,5},{2,10},{6,14},... | collective-permute-start | bytes 221192 | tf_op jit(solution)/shard_map/ppermute | solution.py:27
  47.5 0.6 collective-permute-start.15
  48.3 2.1 %collective-permute-done.17.refs_3_ = bf16[9,32,128]{2,1,0:T(8,128)(2,1)S(1)} collective-permute-done((bf16[9,32,128]{2,1,0:T(8,128)(2,1)S(1)}, bf16[9,32,128]{2,1,0:T(8,128)(2,1)S(1)}, u32[]{:S(2)}, u32[]{:S(2)}) %collective-permute-start.17) | collective-permute-done | bytes 73760 | tf_op jit(solution)/shard_map/ppermute | solution.py:27
  50.4 1.6 %collective-permute-done.16.refs_2_ = bf16[9,32,128]{2,1,0:T(8,128)(2,1)S(1)} collective-permute-done((bf16[9,32,128]{2,1,0:T(8,128)(2,1)S(1)}, bf16[9,32,128]{2,1,0:T(8,128)(2,1)S(1)}, u32[]{:S(2)}, u32[]{:S(2)}) %collective-permute-start.16) | collective-permute-done | bytes 73760 | tf_op jit(solution)/shard_map/ppermute | solution.py:27
  52.0 1.6 %output.1.refs_0_ = bf16[16,2048]{1,0:T(8,128)(2,1)S(1)} custom-call(bf16[9,32,128]{2,1,0:T(8,128)(2,1)S(1)} %summed.1.refs_0_, bf16[9,32,128]{2,1,0:T(8,128)(2,1)S(1)} %collective-permute-done.15.refs_1_, bf16[9,32,128]{2,1,0:T(8,128)(2,1)S(1)} %collective-permute-done.16.refs_2_, bf16[9,32,128]{2,1,0:T(8,128)(2,1)S(1)} %collective-permute-done.17.refs_3_, ...), custom_call_target="tpu_custom_call" | custom-call | tf_op jit(solution)/shard_map/output/pallas_call | solution.py:655
  53.5 1.0 %collective-permute-start.20 = (bf16[16,2048]{1,0:T(8,128)(2,1)S(1)}, bf16[16,2048]{1,0:T(8,128)(2,1)S(1)}, u32[]{:S(2)}, u32[]{:S(2)}) collective-permute-start(bf16[16,2048]{1,0:T(8,128)(2,1)S(1)} %output.1.refs_0_), channel_id=1, source_target_pairs={{0,2},{1,3},{2,0},{3,1},{4,6},{5,7},{6,4},{7,5},{8,10},{9,11},{10,... | collective-permute-start | bytes 196616 | tf_op jit(solution)/shard_map/ppermute | solution.py:27
  54.6 1.9 %collective-permute-start.19 = (bf16[16,2048]{1,0:T(8,128)(2,1)S(1)}, bf16[16,2048]{1,0:T(8,128)(2,1)S(1)}, u32[]{:S(2)}, u32[]{:S(2)}) collective-permute-start(bf16[16,2048]{1,0:T(8,128)(2,1)S(1)} %output.1.refs_0_), channel_id=1, source_target_pairs={{0,3},{1,2},{2,1},{3,0},{4,7},{5,6},{6,5},{7,4},{8,11},{9,10},{10,... | collective-permute-start | bytes 196616 | tf_op jit(solution)/shard_map/ppermute | solution.py:27
  57.0 4.5 %collective-permute-done.20.refs_3_ = bf16[16,2048]{1,0:T(8,128)(2,1)S(1)} collective-permute-done((bf16[16,2048]{1,0:T(8,128)(2,1)S(1)}, bf16[16,2048]{1,0:T(8,128)(2,1)S(1)}, u32[]{:S(2)}, u32[]{:S(2)}) %collective-permute-start.20) | collective-permute-done | bytes 65568 | tf_op jit(solution)/shard_map/ppermute | solution.py:27
  61.5 0.9 %collective-permute-done.18.refs_1_ = bf16[16,2048]{1,0:T(8,128)(2,1)S(1)} collective-permute-done((bf16[16,2048]{1,0:T(8,128)(2,1)S(1)}, bf16[16,2048]{1,0:T(8,128)(2,1)S(1)}, u32[]{:S(2)}, u32[]{:S(2)}) %collective-permute-start.18) | collective-permute-done | bytes 65568 | tf_op jit(solution)/shard_map/ppermute | solution.py:27
  62.4 0.7 %final.1 = f32[8,2,2048]{2,1,0:T(2,128)} custom-call(bf16[16,2048]{1,0:T(8,128)(2,1)S(1)} %output.1.refs_0_, bf16[16,2048]{1,0:T(8,128)(2,1)S(1)} %collective-permute-done.18.refs_1_, bf16[16,2048]{1,0:T(8,128)(2,1)S(1)} %collective-permute-done.19.refs_2_, bf16[16,2048]{1,0:T(8,128)(2,1)S(1)} %collective-permute-done.20.refs_3_, bf16[8,2,2048]{2,1,0:T(2,128)(2,1)S(1)} %copy-done), custom_call_target="tpu_custom_call" | custom-call | tf_op jit(solution)/shard_map/final/pallas_call | solution.py:679
  (28 shorter events, 3.1 us)
Async XLA Ops:
  0.0 10.8 %copy-start.1 = (bf16[2,2,2048]{2,1,0:T(2,128)(2,1)S(1)}, bf16[2,2,2048]{2,1,0:T(2,128)(2,1)}, u32[]{:S(2)}) copy-start(bf16[2,2,2048]{2,1,0:T(2,128)(2,1)} %refs_0_.1) | copy-start | bytes 49156
  0.0 10.8 %copy-start.2 = (bf16[2,2,512]{2,1,0:T(2,128)(2,1)S(1)}, bf16[2,2,512]{2,1,0:T(2,128)(2,1)}, u32[]{:S(2)}) copy-start(bf16[2,2,512]{2,1,0:T(2,128)(2,1)} %refs_4_.2) | copy-start | bytes 12292
  0.0 10.8 %collective-permute-start.1 = (bf16[2,2,2048]{2,1,0:T(2,128)(2,1)}, bf16[2,2,2048]{2,1,0:T(2,128)(2,1)S(1)}, u32[]{:S(2)}, u32[]{:S(2)}) collective-permute-start(bf16[2,2,2048]{2,1,0:T(2,128)(2,1)} %refs_0_.1), channel_id=1, source_target_pairs={{0,2},{1,3},{2,0},{3,1},{4,6},{5,7},{6,4},{7,5},{8,10},{9,11},{10,... | collective-permute-start | bytes 49160 | tf_op jit(solution)/shard_map/ppermute | solution.py:27
  4.0 6.8 %collective-permute-start = (bf16[2,2,2048]{2,1,0:T(2,128)(2,1)}, bf16[2,2,2048]{2,1,0:T(2,128)(2,1)S(1)}, u32[]{:S(2)}, u32[]{:S(2)}) collective-permute-start(bf16[2,2,2048]{2,1,0:T(2,128)(2,1)} %refs_0_.1), channel_id=1, source_target_pairs={{0,3},{1,2},{2,1},{3,0},{4,7},{5,6},{6,5},{7,4},{8,11},{9,10},{10,... | collective-permute-start | bytes 49160 | tf_op jit(solution)/shard_map/ppermute | solution.py:27
  5.4 5.4 %collective-permute-start.2 = (bf16[2,2,2048]{2,1,0:T(2,128)(2,1)}, bf16[2,2,2048]{2,1,0:T(2,128)(2,1)S(1)}, u32[]{:S(2)}, u32[]{:S(2)}) collective-permute-start(bf16[2,2,2048]{2,1,0:T(2,128)(2,1)} %refs_0_.1), channel_id=1, source_target_pairs={{0,1},{1,0},{2,3},{3,2},{4,5},{5,4},{6,7},{7,6},{8,9},{9,8},{10,11... | collective-permute-start | bytes 49160 | tf_op jit(solution)/shard_map/ppermute | solution.py:27
  11.0 5.8 %collective-permute-start.5 = (bf16[2,144,128]{2,1,0:T(8,128)(2,1)S(1)}, bf16[2,144,128]{2,1,0:T(8,128)(2,1)S(1)}, u32[]{:S(2)}, u32[]{:S(2)}) collective-permute-start(bf16[2,144,128]{2,1,0:T(8,128)(2,1)S(1)} %turned.1.after.refs_0_), channel_id=1, source_target_pairs={{0,8},{4,12},{8,0},{12,4},{1,9},{5,13},{9,1},{13,5},{2,10},{6,14},... | collective-permute-start | bytes 221192 | tf_op jit(solution)/shard_map/ppermute | solution.py:27
  12.6 4.4 %collective-permute-start.4 = (bf16[2,144,128]{2,1,0:T(8,128)(2,1)S(1)}, bf16[2,144,128]{2,1,0:T(8,128)(2,1)S(1)}, u32[]{:S(2)}, u32[]{:S(2)}) collective-permute-start(bf16[2,144,128]{2,1,0:T(8,128)(2,1)S(1)} %turned.1.after.refs_0_), channel_id=1, source_target_pairs={{0,12},{4,8},{8,4},{12,0},{1,13},{5,9},{9,5},{13,1},{2,14},{6,10},... | collective-permute-start | bytes 221192 | tf_op jit(solution)/shard_map/ppermute | solution.py:27
  12.6 4.4 %collective-permute-start.3 = (bf16[2,144,128]{2,1,0:T(8,128)(2,1)S(1)}, bf16[2,144,128]{2,1,0:T(8,128)(2,1)S(1)}, u32[]{:S(2)}, u32[]{:S(2)}) collective-permute-start(bf16[2,144,128]{2,1,0:T(8,128)(2,1)S(1)} %turned.1.after.refs_0_), channel_id=1, source_target_pairs={{0,4},{4,0},{8,12},{12,8},{1,5},{5,1},{9,13},{13,9},{2,6},{6,2},{1... | collective-permute-start | bytes 221192 | tf_op jit(solution)/shard_map/ppermute | solution.py:27
  18.3 7.1 %collective-permute-start.6 = (bf16[32,1024]{1,0:T(8,128)(2,1)S(1)}, bf16[32,1024]{1,0:T(8,128)(2,1)S(1)}, u32[]{:S(2)}, u32[]{:S(2)}) collective-permute-start(bf16[32,1024]{1,0:T(8,128)(2,1)S(1)} %get-tuple-element.42), channel_id=1, source_target_pairs={{0,2},{1,3},{2,0},{3,1},{4,6},{5,7},{6,4},{7,5},{8,10},{9,11},{10,... | collective-permute-start | bytes 196616 | tf_op jit(solution)/shard_map/ppermute | solution.py:27
  21.2 6.3 %collective-permute-start.7 = (bf16[32,1024]{1,0:T(8,128)(2,1)S(1)}, bf16[32,1024]{1,0:T(8,128)(2,1)S(1)}, u32[]{:S(2)}, u32[]{:S(2)}) collective-permute-start(bf16[32,1024]{1,0:T(8,128)(2,1)S(1)} %get-tuple-element.43), channel_id=1, source_target_pairs={{0,3},{1,2},{2,1},{3,0},{4,7},{5,6},{6,5},{7,4},{8,11},{9,10},{10,... | collective-permute-start | bytes 196616 | tf_op jit(solution)/shard_map/ppermute | solution.py:27
  22.6 5.1 %collective-permute-start.8 = (bf16[32,1024]{1,0:T(8,128)(2,1)S(1)}, bf16[32,1024]{1,0:T(8,128)(2,1)S(1)}, u32[]{:S(2)}, u32[]{:S(2)}) collective-permute-start(bf16[32,1024]{1,0:T(8,128)(2,1)S(1)} %get-tuple-element.44), channel_id=1, source_target_pairs={{0,1},{1,0},{2,3},{3,2},{4,5},{5,4},{6,7},{7,6},{8,9},{9,8},{10,11... | collective-permute-start | bytes 196616 | tf_op jit(solution)/shard_map/ppermute | solution.py:27
  28.5 6.9 %collective-permute-start.11 = (bf16[32,1024]{1,0:T(8,128)(2,1)S(1)}, bf16[32,1024]{1,0:T(8,128)(2,1)S(1)}, u32[]{:S(2)}, u32[]{:S(2)}) collective-permute-start(bf16[32,1024]{1,0:T(8,128)(2,1)S(1)} %get-tuple-element.48.refs_0_), channel_id=1, source_target_pairs={{0,2},{1,3},{2,0},{3,1},{4,6},{5,7},{6,4},{7,5},{8,10},{9,11},{10,... | collective-permute-start | bytes 196616 | tf_op jit(solution)/shard_map/ppermute | solution.py:27
  30.4 6.2 %collective-permute-start.10 = (bf16[32,1024]{1,0:T(8,128)(2,1)S(1)}, bf16[32,1024]{1,0:T(8,128)(2,1)S(1)}, u32[]{:S(2)}, u32[]{:S(2)}) collective-permute-start(bf16[32,1024]{1,0:T(8,128)(2,1)S(1)} %get-tuple-element.48.refs_0_), channel_id=1, source_target_pairs={{0,3},{1,2},{2,1},{3,0},{4,7},{5,6},{6,5},{7,4},{8,11},{9,10},{10,... | collective-permute-start | bytes 196616 | tf_op jit(solution)/shard_map/ppermute | solution.py:27
  31.6 5.2 %collective-permute-start.9 = (bf16[32,1024]{1,0:T(8,128)(2,1)S(1)}, bf16[32,1024]{1,0:T(8,128)(2,1)S(1)}, u32[]{:S(2)}, u32[]{:S(2)}) collective-permute-start(bf16[32,1024]{1,0:T(8,128)(2,1)S(1)} %get-tuple-element.48.refs_0_), channel_id=1, source_target_pairs={{0,1},{1,0},{2,3},{3,2},{4,5},{5,4},{6,7},{7,6},{8,9},{9,8},{10,11... | collective-permute-start | bytes 196616 | tf_op jit(solution)/shard_map/ppermute | solution.py:27
  37.9 6.6 %collective-permute-start.12 = (bf16[8,32,128]{2,1,0:T(8,128)(2,1)S(1)}, bf16[8,32,128]{2,1,0:T(8,128)(2,1)S(1)}, u32[]{:S(2)}, u32[]{:S(2)}) collective-permute-start(bf16[8,32,128]{2,1,0:T(8,128)(2,1)S(1)} %get-tuple-element.52), channel_id=1, source_target_pairs={{0,2},{1,3},{2,0},{3,1},{4,6},{5,7},{6,4},{7,5},{8,10},{9,11},{10,... | collective-permute-start | bytes 196616 | tf_op jit(solution)/shard_map/ppermute | solution.py:27
  39.6 6.2 %collective-permute-start.13 = (bf16[8,32,128]{2,1,0:T(8,128)(2,1)S(1)}, bf16[8,32,128]{2,1,0:T(8,128)(2,1)S(1)}, u32[]{:S(2)}, u32[]{:S(2)}) collective-permute-start(bf16[8,32,128]{2,1,0:T(8,128)(2,1)S(1)} %get-tuple-element.53), channel_id=1, source_target_pairs={{0,3},{1,2},{2,1},{3,0},{4,7},{5,6},{6,5},{7,4},{8,11},{9,10},{10,... | collective-permute-start | bytes 196616 | tf_op jit(solution)/shard_map/ppermute | solution.py:27
  40.9 5.0 %collective-permute-start.14 = (bf16[8,32,128]{2,1,0:T(8,128)(2,1)S(1)}, bf16[8,32,128]{2,1,0:T(8,128)(2,1)S(1)}, u32[]{:S(2)}, u32[]{:S(2)}) collective-permute-start(bf16[8,32,128]{2,1,0:T(8,128)(2,1)S(1)} %get-tuple-element.54), channel_id=1, source_target_pairs={{0,1},{1,0},{2,3},{3,2},{4,5},{5,4},{6,7},{7,6},{8,9},{9,8},{10,11... | collective-permute-start | bytes 196616 | tf_op jit(solution)/shard_map/ppermute | solution.py:27
  46.0 4.4 %collective-permute-start.17 = (bf16[9,32,128]{2,1,0:T(8,128)(2,1)S(1)}, bf16[9,32,128]{2,1,0:T(8,128)(2,1)S(1)}, u32[]{:S(2)}, u32[]{:S(2)}) collective-permute-start(bf16[9,32,128]{2,1,0:T(8,128)(2,1)S(1)} %summed.1.refs_0_), channel_id=1, source_target_pairs={{0,8},{4,12},{8,0},{12,4},{1,9},{5,13},{9,1},{13,5},{2,10},{6,14},... | collective-permute-start | bytes 221192 | tf_op jit(solution)/shard_map/ppermute | solution.py:27
  47.5 4.4 %collective-permute-start.16 = (bf16[9,32,128]{2,1,0:T(8,128)(2,1)S(1)}, bf16[9,32,128]{2,1,0:T(8,128)(2,1)S(1)}, u32[]{:S(2)}, u32[]{:S(2)}) collective-permute-start(bf16[9,32,128]{2,1,0:T(8,128)(2,1)S(1)} %summed.1.refs_0_), channel_id=1, source_target_pairs={{0,12},{4,8},{8,4},{12,0},{1,13},{5,9},{9,5},{13,1},{2,14},{6,10},... | collective-permute-start | bytes 221192 | tf_op jit(solution)/shard_map/ppermute | solution.py:27
  47.5 4.4 %collective-permute-start.15 = (bf16[9,32,128]{2,1,0:T(8,128)(2,1)S(1)}, bf16[9,32,128]{2,1,0:T(8,128)(2,1)S(1)}, u32[]{:S(2)}, u32[]{:S(2)}) collective-permute-start(bf16[9,32,128]{2,1,0:T(8,128)(2,1)S(1)} %summed.1.refs_0_), channel_id=1, source_target_pairs={{0,4},{4,0},{8,12},{12,8},{1,5},{5,1},{9,13},{13,9},{2,6},{6,2},{1... | collective-permute-start | bytes 221192 | tf_op jit(solution)/shard_map/ppermute | solution.py:27
  52.0 10.5 %copy-start = (bf16[8,2,2048]{2,1,0:T(2,128)(2,1)S(1)}, bf16[8,2,2048]{2,1,0:T(2,128)(2,1)}, u32[]{:S(2)}) copy-start(bf16[8,2,2048]{2,1,0:T(2,128)(2,1)} %refs_4_.3) | copy-start | bytes 196612
  53.5 8.0 %collective-permute-start.20 = (bf16[16,2048]{1,0:T(8,128)(2,1)S(1)}, bf16[16,2048]{1,0:T(8,128)(2,1)S(1)}, u32[]{:S(2)}, u32[]{:S(2)}) collective-permute-start(bf16[16,2048]{1,0:T(8,128)(2,1)S(1)} %output.1.refs_0_), channel_id=1, source_target_pairs={{0,2},{1,3},{2,0},{3,1},{4,6},{5,7},{6,4},{7,5},{8,10},{9,11},{10,... | collective-permute-start | bytes 196616 | tf_op jit(solution)/shard_map/ppermute | solution.py:27
  54.6 6.9 %collective-permute-start.19 = (bf16[16,2048]{1,0:T(8,128)(2,1)S(1)}, bf16[16,2048]{1,0:T(8,128)(2,1)S(1)}, u32[]{:S(2)}, u32[]{:S(2)}) collective-permute-start(bf16[16,2048]{1,0:T(8,128)(2,1)S(1)} %output.1.refs_0_), channel_id=1, source_target_pairs={{0,3},{1,2},{2,1},{3,0},{4,7},{5,6},{6,5},{7,4},{8,11},{9,10},{10,... | collective-permute-start | bytes 196616 | tf_op jit(solution)/shard_map/ppermute | solution.py:27
  56.5 5.9 %collective-permute-start.18 = (bf16[16,2048]{1,0:T(8,128)(2,1)S(1)}, bf16[16,2048]{1,0:T(8,128)(2,1)S(1)}, u32[]{:S(2)}, u32[]{:S(2)}) collective-permute-start(bf16[16,2048]{1,0:T(8,128)(2,1)S(1)} %output.1.refs_0_), channel_id=1, source_target_pairs={{0,1},{1,0},{2,3},{3,2},{4,5},{5,4},{6,7},{7,6},{8,9},{9,8},{10,11... | collective-permute-start | bytes 196616 | tf_op jit(solution)/shard_map/ppermute | solution.py:27

commit v20 on v19

--- a/solution.py
+++ b/solution.py
@@ -354,7 +354,9 @@
     new = refs[:n_seq]
     k_ref, meta = refs[n_seq : n_seq + 2]
     outs = refs[n_seq + 2 : n_seq + 2 + n_tp]
-    all_q, ready = refs[n_seq + 2 + n_tp :]
+    all_q, ready, table, sem = refs[n_seq + 2 + n_tp :]
+    copy = pltpu.make_async_copy(meta, table, sem)
+    copy.start()
     own_rows = new[0].shape[0]
     local_pages = k_ref.shape[0] // PAGE
     all_rows = all_q.shape[1]
@@ -371,8 +373,9 @@
             request = (seq ^ reverse(n_seq)[ds]) * own_rows + rr
             all_q[request, :, :HD] = jnp.where(even, q, 0.0).astype(BF16)
             all_q[request, :, HD:] = jnp.where(even, 0.0, q).astype(BF16)
+    copy.wait()
     for p in range(0, local_pages, 2):
-        requests = [meta[first + p], meta[first + p + 1]]
+        requests = [table[first + p], table[first + p + 1]]
         tokens = slice(p * PAGE, (p + 2) * PAGE)
         for pair in range(KVH // 2):
             k = k_ref[tokens, 2 * pair * HD : 2 * (pair + 1) * HD]
@@ -394,19 +397,21 @@
     rows = all_rows // n_tp
     return pl.pallas_call(
         functools.partial(scores_kernel, n_seq, n_tp),
-        in_specs=[VMEM] * (n_seq + 1) + [SMEM],
+        in_specs=[VMEM] * (n_seq + 1) + [pl.BlockSpec(memory_space=pltpu.HBM)],
         out_specs=[VMEM] * n_tp,
         out_shape=[jax.ShapeDtypeStruct((rows, tokens), BF16)] * n_tp,
         scratch_shapes=[
             pltpu.VMEM((prompts, all_rows, 2 * HD), BF16),
             pltpu.VMEM((all_rows, tokens), BF16),
+            pltpu.SMEM(meta.shape, jnp.int32),
+            pltpu.SemaphoreType.DMA,
         ],
         compiler_params=pltpu.CompilerParams(vmem_limit_bytes=24 * MIB),
         cost_estimate=pl.CostEstimate(
             flops=2 * tokens * all_rows * HD, bytes_accessed=6 * MIB, transcendentals=0
         ),
         name="scores",
-    )(*new, k, meta)
+    )(*new, k, in_hbm(meta))
 
 
 def fresh_kernel(n_seq, *refs):
@@ -521,7 +526,9 @@
     pieces = refs[:n_tp]
     va_ref, vb_ref, meta = refs[n_tp : n_tp + 3]
     outs = refs[n_tp + 3 : n_tp + 3 + n_tp]
-    ready, total = refs[n_tp + 3 + n_tp :]
+    ready, total, table, sem = refs[n_tp + 3 + n_tp :]
+    copy = pltpu.make_async_copy(meta, table, sem)
+    copy.start()
     rows_local, tokens_here = pieces[0].shape
     kv_local = KVH // n_tp
     rows = rows_local // kv_local
@@ -535,8 +542,9 @@
     total[...] = jnp.zeros_like(total)
     half = va_ref.shape[1] // HD
     none = jnp.zeros((2 * rows, PAGE), BF16)
+    copy.wait()
     for p in range(0, local_pages, 2):
-        requests = [meta[first + p], meta[first + p + 1]]
+        requests = [table[first + p], table[first + p + 1]]
         tokens = slice(p * PAGE, (p + 2) * PAGE)
         for pair in range(KVH // 2):
             head = 2 * pair
@@ -560,19 +568,21 @@
     rows, tokens = pieces[0].shape
     return pl.pallas_call(
         functools.partial(weighted_kernel, n_tp),
-        in_specs=[VMEM] * (n_tp + 2) + [SMEM],
+        in_specs=[VMEM] * (n_tp + 2) + [pl.BlockSpec(memory_space=pltpu.HBM)],
         out_specs=[VMEM] * n_tp,
         out_shape=[jax.ShapeDtypeStruct((prompts, rows, HD), BF16)] * n_tp,
         scratch_shapes=[
             pltpu.VMEM((rows * n_tp, tokens), BF16),
             pltpu.VMEM((prompts, rows * n_tp, HD), F32),
+            pltpu.SMEM(meta.shape, jnp.int32),
+            pltpu.SemaphoreType.DMA,
         ],
         compiler_params=pltpu.CompilerParams(vmem_limit_bytes=24 * MIB),
         cost_estimate=pl.CostEstimate(
             flops=2 * tokens * rows * n_tp * HD, bytes_accessed=8 * MIB, transcendentals=0
         ),
         name="weighted",
-    )(*pieces, va, vb, meta)
+    )(*pieces, va, vb, in_hbm(meta))
 
 
 def summed_kernel(n_tp, *refs):

time: 63.3 us -> 63.5 us (level)
  transfers between devices with their start and end apart: 21 -> 21, of which waited for: 14 -> 14; matrix products, arithmetic and copies ran while one was open for 0% -> 0% of each run, Pallas kernels for 22% -> 21%
where the time goes in v20:
time: 63.5 us; the launch traced here: 63.3 us
  starting transfers between devices  24.8 us (39%)
  Pallas kernels  19.6 us (31%)
  waiting for transfers between devices  18.8 us (30%)
    ppermute x21, starting transfers between devices, pairs(): lax.ppermute(value, axis, [(i, i ^ d) for i in range(lax.axis_size(axis))])  24.8 us
    ppermute x21, waiting for transfers between devices, pairs(): lax.ppermute(value, axis, [(i, i ^ d) for i in range(lax.axis_size(axis))])  18.8 us
    pallas_call x1, Pallas kernels, load(): pl.pallas_call(functools.partial(load_kernel, pages, prompts, new_count),...  5.15 us
    pallas_call x2, Pallas kernels, project_values(): pl.pallas_call(functools.partial(values_kernel, first), in_specs=[VMEM] *...  4.68 us
    pallas_call x1, Pallas kernels, rotated_keys(): pl.pallas_call(keys_kernel, in_specs=[VMEM] * 3 + [hbm] * 2 + [VMEM] * 2...  3.62 us
    pallas_call x1, Pallas kernels, output_partial(): pl.pallas_call(functools.partial(output_kernel, n_seq), in_specs=[VMEM] *...  1.58 us
    pallas_call x1, Pallas kernels, partial_scores(): pl.pallas_call(functools.partial(scores_kernel, n_seq, n_tp), in_specs=[V...  1.45 us
  transfers between devices with their start and end apart: 21, of which 14 were waited for; matrix products, arithmetic and copies ran while one was open for 0% of the time, Pallas kernels for 21%

profile of v20, /device:TPU:0, one launch (start us, length us, event | category | flops | bytes accessed | tf_op | source)
XLA Modules:
  0.0 63.3 jit_solution(10150442043247931020)
XLA Ops:
  0.0 4.0 %collective-permute-start.1 = (bf16[2,2,2048]{2,1,0:T(2,128)(2,1)}, bf16[2,2,2048]{2,1,0:T(2,128)(2,1)S(1)}, u32[]{:S(2)}, u32[]{:S(2)}) collective-permute-start(bf16[2,2,2048]{2,1,0:T(2,128)(2,1)} %refs_0_.1), channel_id=1, source_target_pairs={{0,2},{1,3},{2,0},{3,1},{4,6},{5,7},{6,4},{7,5},{8,10},{9,11},{10,... | collective-permute-start | bytes 49160 | tf_op jit(solution)/shard_map/ppermute | solution.py:27
  4.0 1.3 %collective-permute-start = (bf16[2,2,2048]{2,1,0:T(2,128)(2,1)}, bf16[2,2,2048]{2,1,0:T(2,128)(2,1)S(1)}, u32[]{:S(2)}, u32[]{:S(2)}) collective-permute-start(bf16[2,2,2048]{2,1,0:T(2,128)(2,1)} %refs_0_.1), channel_id=1, source_target_pairs={{0,3},{1,2},{2,1},{3,0},{4,7},{5,6},{6,5},{7,4},{8,11},{9,10},{10,... | collective-permute-start | bytes 49160 | tf_op jit(solution)/shard_map/ppermute | solution.py:27
  5.6 5.2 %load.1 = (f32[1024,1024]{1,0:T(8,128)S(1)}, bf16[1024,1536]{1,0:T(8,128)(2,1)S(1)}, bf16[1536,2048]{1,0:T(8,128)(2,1)S(1)}, f32[1024,128]{1,0:T(8,128)S(1)}, f3...) custom-call(bf16[1024,2048]{1,0:T(8,128)(2,1)} %x_hbm.3, ...), custom_call_target="tpu_custom_call" | custom-call | flops 2147483648 | bytes 9437184 | tf_op jit(solution)/shard_map/load/pallas_call | solution.py:188
  11.0 1.6 %collective-permute-start.5 = (bf16[2,144,128]{2,1,0:T(8,128)(2,1)S(1)}, bf16[2,144,128]{2,1,0:T(8,128)(2,1)S(1)}, u32[]{:S(2)}, u32[]{:S(2)}) collective-permute-start(bf16[2,144,128]{2,1,0:T(8,128)(2,1)S(1)} %turned.1.after.refs_0_), channel_id=1, source_target_pairs={{0,8},{4,12},{8,0},{12,4},{1,9},{5,13},{9,1},{13,5},{2,10},{6,14},... | collective-permute-start | bytes 221192 | tf_op jit(solution)/shard_map/ppermute | solution.py:27
  12.6 0.6 collective-permute-start.3
  13.2 3.6 %keys.1 = (bf16[1024,1024]{1,0:T(8,128)(2,1)S(1)}, bf16[1024,512]{1,0:T(8,128)(2,1)S(1)}, bf16[512,2048]{1,0:T(8,128)(2,1)S(1)}) custom-call(f32[1024,1024]{1,0:T(8,128)S(1)} %get-tuple-element.34.acc, bf16[1024,1536]{1,0:T(8,128)(2,1)S(1)} %get-tuple-element.35.xa_ref, bf16[1536,2048]{1,0:T(8,128)(2,1)S(1)} %get-tuple-element.36.wa_ref, ...), custom_call_target="tpu_custom_call" | custom-call | flops 2147483648 | bytes 8388608 | tf_op jit(solution)/shard_map/keys/pallas_call | solution.py:242
  17.0 1.4 %scores.1 = (bf16[32,1024]{1,0:T(8,128)(2,1)S(1)}, bf16[32,1024]{1,0:T(8,128)(2,1)S(1)}, bf16[32,1024]{1,0:T(8,128)(2,1)S(1)}, bf16[32,1024]{1,0:T(8,128)(2,1)S(1)}) custom-call(bf16[2,144,128]{2,1,0:T(8,128)(2,1)S(1)} %turned.1.after.refs_0_, bf16[2,144,128]{2,1,0:T(8,128)(2,1)S(1)} %collective-permute-done.3.refs_1_, ...), custom_call_target="tpu_custom_call" | custom-call | flops 33554432 | bytes 6291456 | tf_op jit(solution)/shard_map/scores/pallas_call | solution.py:398
  18.5 2.9 %collective-permute-start.6 = (bf16[32,1024]{1,0:T(8,128)(2,1)S(1)}, bf16[32,1024]{1,0:T(8,128)(2,1)S(1)}, u32[]{:S(2)}, u32[]{:S(2)}) collective-permute-start(bf16[32,1024]{1,0:T(8,128)(2,1)S(1)} %get-tuple-element.42), channel_id=1, source_target_pairs={{0,2},{1,3},{2,0},{3,1},{4,6},{5,7},{6,4},{7,5},{8,10},{9,11},{10,... | collective-permute-start | bytes 196616 | tf_op jit(solution)/shard_map/ppermute | solution.py:27
  21.3 1.3 %collective-permute-start.7 = (bf16[32,1024]{1,0:T(8,128)(2,1)S(1)}, bf16[32,1024]{1,0:T(8,128)(2,1)S(1)}, u32[]{:S(2)}, u32[]{:S(2)}) collective-permute-start(bf16[32,1024]{1,0:T(8,128)(2,1)S(1)} %get-tuple-element.43), channel_id=1, source_target_pairs={{0,3},{1,2},{2,1},{3,0},{4,7},{5,6},{6,5},{7,4},{8,11},{9,10},{10,... | collective-permute-start | bytes 196616 | tf_op jit(solution)/shard_map/ppermute | solution.py:27
  22.7 2.3 %values.2 = (bf16[1024,512]{1,0:T(8,128)(2,1)S(1)}, bf16[1024,2048]{1,0:T(8,128)(2,1)S(1)}) custom-call(bf16[1024,1536]{1,0:T(8,128)(2,1)S(1)} %get-tuple-element.35.xa_ref, bf16[1536,2048]{1,0:T(8,128)(2,1)S(1)} %get-tuple-element.36.wa_ref, bf16[1024,512]{1,0:T(8,128)(2,1)S(1)} %get-tuple-element.45.xb_ref, ...), custom_call_target="tpu_custom_call" | custom-call | flops 1610612736 | bytes 8388608 | tf_op jit(solution)/shard_map/values/pallas_call | solution.py:284
  25.5 2.1 %collective-permute-done.7.refs_2_ = bf16[32,1024]{1,0:T(8,128)(2,1)S(1)} collective-permute-done((bf16[32,1024]{1,0:T(8,128)(2,1)S(1)}, bf16[32,1024]{1,0:T(8,128)(2,1)S(1)}, u32[]{:S(2)}, u32[]{:S(2)}) %collective-permute-start.7) | collective-permute-done | bytes 65568 | tf_op jit(solution)/shard_map/ppermute | solution.py:27
  27.8 0.9 %weights.1 = (bf16[32,1024]{1,0:T(8,128)(2,1)S(1)}, bf16[32,128]{1,0:T(8,128)(2,1)S(1)}) custom-call(bf16[32,1024]{1,0:T(8,128)(2,1)S(1)} %get-tuple-element.41.after.refs_0_, bf16[32,1024]{1,0:T(8,128)(2,1)S(1)} %collective-permute-done.6.refs_1_, bf16[32,1024]{1,0:T(8,128)(2,1)S(1)} %collective-permute-done.7.refs_2_, ...), custom_call_target="tpu_custom_call" | custom-call | tf_op jit(solution)/shard_map/weights/pallas_call | solution.py:512
  28.6 1.9 %collective-permute-start.11 = (bf16[32,1024]{1,0:T(8,128)(2,1)S(1)}, bf16[32,1024]{1,0:T(8,128)(2,1)S(1)}, u32[]{:S(2)}, u32[]{:S(2)}) collective-permute-start(bf16[32,1024]{1,0:T(8,128)(2,1)S(1)} %get-tuple-element.48.refs_0_), channel_id=1, source_target_pairs={{0,2},{1,3},{2,0},{3,1},{4,6},{5,7},{6,4},{7,5},{8,10},{9,11},{10,... | collective-permute-start | bytes 196616 | tf_op jit(solution)/shard_map/ppermute | solution.py:27
  30.5 1.2 %collective-permute-start.10 = (bf16[32,1024]{1,0:T(8,128)(2,1)S(1)}, bf16[32,1024]{1,0:T(8,128)(2,1)S(1)}, u32[]{:S(2)}, u32[]{:S(2)}) collective-permute-start(bf16[32,1024]{1,0:T(8,128)(2,1)S(1)} %get-tuple-element.48.refs_0_), channel_id=1, source_target_pairs={{0,3},{1,2},{2,1},{3,0},{4,7},{5,6},{6,5},{7,4},{8,11},{9,10},{10,... | collective-permute-start | bytes 196616 | tf_op jit(solution)/shard_map/ppermute | solution.py:27
  32.1 2.3 %values.3 = (bf16[1024,512]{1,0:T(8,128)(2,1)S(1)}, bf16[1024,2048]{1,0:T(8,128)(2,1)S(1)}) custom-call(bf16[1024,1536]{1,0:T(8,128)(2,1)S(1)} %get-tuple-element.35.xa_ref, bf16[1536,2048]{1,0:T(8,128)(2,1)S(1)} %get-tuple-element.36.wa_ref, bf16[1024,512]{1,0:T(8,128)(2,1)S(1)} %get-tuple-element.45.xb_ref, ...), custom_call_target="tpu_custom_call" | custom-call | flops 1610612736 | bytes 8388608 | tf_op jit(solution)/shard_map/values/pallas_call | solution.py:284
  34.5 1.0 %collective-permute-done.11.refs_3_ = bf16[32,1024]{1,0:T(8,128)(2,1)S(1)} collective-permute-done((bf16[32,1024]{1,0:T(8,128)(2,1)S(1)}, bf16[32,1024]{1,0:T(8,128)(2,1)S(1)}, u32[]{:S(2)}, u32[]{:S(2)}) %collective-permute-start.11) | collective-permute-done | bytes 65568 | tf_op jit(solution)/shard_map/ppermute | solution.py:27
  35.5 1.2 %collective-permute-done.10.refs_2_ = bf16[32,1024]{1,0:T(8,128)(2,1)S(1)} collective-permute-done((bf16[32,1024]{1,0:T(8,128)(2,1)S(1)}, bf16[32,1024]{1,0:T(8,128)(2,1)S(1)}, u32[]{:S(2)}, u32[]{:S(2)}) %collective-permute-start.10) | collective-permute-done | bytes 65568 | tf_op jit(solution)/shard_map/ppermute | solution.py:27
  36.9 1.2 %weighted.1 = (bf16[8,32,128]{2,1,0:T(8,128)(2,1)S(1)}, bf16[8,32,128]{2,1,0:T(8,128)(2,1)S(1)}, bf16[8,32,128]{2,1,0:T(8,128)(2,1)S(1)}, bf16[8,32,128]{2,1,0:T(8,128)(2,1)S(1)}) custom-call(bf16[32,1024]{1,0:T(8,128)(2,1)S(1)} %get-tuple-element.48.refs_0_, bf16[32,1024]{1,0:T(8,128)(2,1)S(1)} %collective-permute-done.9.refs_1_, ...), custom_call_target="tpu_custom_call" | custom-call | flops 33554432 | bytes 8388608 | tf_op jit(solution)/shard_map/weighted/pallas_call | solution.py:569
  38.1 1.8 %collective-permute-start.12 = (bf16[8,32,128]{2,1,0:T(8,128)(2,1)S(1)}, bf16[8,32,128]{2,1,0:T(8,128)(2,1)S(1)}, u32[]{:S(2)}, u32[]{:S(2)}) collective-permute-start(bf16[8,32,128]{2,1,0:T(8,128)(2,1)S(1)} %get-tuple-element.52), channel_id=1, source_target_pairs={{0,2},{1,3},{2,0},{3,1},{4,6},{5,7},{6,4},{7,5},{8,10},{9,11},{10,... | collective-permute-start | bytes 196616 | tf_op jit(solution)/shard_map/ppermute | solution.py:27
  39.8 1.2 %collective-permute-start.13 = (bf16[8,32,128]{2,1,0:T(8,128)(2,1)S(1)}, bf16[8,32,128]{2,1,0:T(8,128)(2,1)S(1)}, u32[]{:S(2)}, u32[]{:S(2)}) collective-permute-start(bf16[8,32,128]{2,1,0:T(8,128)(2,1)S(1)} %get-tuple-element.53), channel_id=1, source_target_pairs={{0,3},{1,2},{2,1},{3,0},{4,7},{5,6},{6,5},{7,4},{8,11},{9,10},{10,... | collective-permute-start | bytes 196616 | tf_op jit(solution)/shard_map/ppermute | solution.py:27
  41.6 3.1 %collective-permute-done.12.refs_1_ = bf16[8,32,128]{2,1,0:T(8,128)(2,1)S(1)} collective-permute-done((bf16[8,32,128]{2,1,0:T(8,128)(2,1)S(1)}, bf16[8,32,128]{2,1,0:T(8,128)(2,1)S(1)}, u32[]{:S(2)}, u32[]{:S(2)}) %collective-permute-start.12) | collective-permute-done | bytes 65568 | tf_op jit(solution)/shard_map/ppermute | solution.py:27
  44.7 1.3 %collective-permute-done.13.refs_2_ = bf16[8,32,128]{2,1,0:T(8,128)(2,1)S(1)} collective-permute-done((bf16[8,32,128]{2,1,0:T(8,128)(2,1)S(1)}, bf16[8,32,128]{2,1,0:T(8,128)(2,1)S(1)}, u32[]{:S(2)}, u32[]{:S(2)}) %collective-permute-start.13) | collective-permute-done | bytes 65568 | tf_op jit(solution)/shard_map/ppermute | solution.py:27
  46.2 1.6 %collective-permute-start.17 = (bf16[9,32,128]{2,1,0:T(8,128)(2,1)S(1)}, bf16[9,32,128]{2,1,0:T(8,128)(2,1)S(1)}, u32[]{:S(2)}, u32[]{:S(2)}) collective-permute-start(bf16[9,32,128]{2,1,0:T(8,128)(2,1)S(1)} %summed.1.refs_0_), channel_id=1, source_target_pairs={{0,8},{4,12},{8,0},{12,4},{1,9},{5,13},{9,1},{13,5},{2,10},{6,14},... | collective-permute-start | bytes 221192 | tf_op jit(solution)/shard_map/ppermute | solution.py:27
  47.8 0.6 collective-permute-start.15
  48.5 2.1 %collective-permute-done.17.refs_3_ = bf16[9,32,128]{2,1,0:T(8,128)(2,1)S(1)} collective-permute-done((bf16[9,32,128]{2,1,0:T(8,128)(2,1)S(1)}, bf16[9,32,128]{2,1,0:T(8,128)(2,1)S(1)}, u32[]{:S(2)}, u32[]{:S(2)}) %collective-permute-start.17) | collective-permute-done | bytes 73760 | tf_op jit(solution)/shard_map/ppermute | solution.py:27
  50.6 1.6 %collective-permute-done.16.refs_2_ = bf16[9,32,128]{2,1,0:T(8,128)(2,1)S(1)} collective-permute-done((bf16[9,32,128]{2,1,0:T(8,128)(2,1)S(1)}, bf16[9,32,128]{2,1,0:T(8,128)(2,1)S(1)}, u32[]{:S(2)}, u32[]{:S(2)}) %collective-permute-start.16) | collective-permute-done | bytes 73760 | tf_op jit(solution)/shard_map/ppermute | solution.py:27
  52.2 1.6 %output.1.refs_0_ = bf16[16,2048]{1,0:T(8,128)(2,1)S(1)} custom-call(bf16[9,32,128]{2,1,0:T(8,128)(2,1)S(1)} %summed.1.refs_0_, bf16[9,32,128]{2,1,0:T(8,128)(2,1)S(1)} %collective-permute-done.15.refs_1_, bf16[9,32,128]{2,1,0:T(8,128)(2,1)S(1)} %collective-permute-done.16.refs_2_, bf16[9,32,128]{2,1,0:T(8,128)(2,1)S(1)} %collective-permute-done.17.refs_3_, ...), custom_call_target="tpu_custom_call" | custom-call | tf_op jit(solution)/shard_map/output/pallas_call | solution.py:665
  53.7 1.1 %collective-permute-start.20 = (bf16[16,2048]{1,0:T(8,128)(2,1)S(1)}, bf16[16,2048]{1,0:T(8,128)(2,1)S(1)}, u32[]{:S(2)}, u32[]{:S(2)}) collective-permute-start(bf16[16,2048]{1,0:T(8,128)(2,1)S(1)} %output.1.refs_0_), channel_id=1, source_target_pairs={{0,2},{1,3},{2,0},{3,1},{4,6},{5,7},{6,4},{7,5},{8,10},{9,11},{10,... | collective-permute-start | bytes 196616 | tf_op jit(solution)/shard_map/ppermute | solution.py:27
  54.8 1.9 %collective-permute-start.19 = (bf16[16,2048]{1,0:T(8,128)(2,1)S(1)}, bf16[16,2048]{1,0:T(8,128)(2,1)S(1)}, u32[]{:S(2)}, u32[]{:S(2)}) collective-permute-start(bf16[16,2048]{1,0:T(8,128)(2,1)S(1)} %output.1.refs_0_), channel_id=1, source_target_pairs={{0,3},{1,2},{2,1},{3,0},{4,7},{5,6},{6,5},{7,4},{8,11},{9,10},{10,... | collective-permute-start | bytes 196616 | tf_op jit(solution)/shard_map/ppermute | solution.py:27
  57.2 4.5 %collective-permute-done.20.refs_3_ = bf16[16,2048]{1,0:T(8,128)(2,1)S(1)} collective-permute-done((bf16[16,2048]{1,0:T(8,128)(2,1)S(1)}, bf16[16,2048]{1,0:T(8,128)(2,1)S(1)}, u32[]{:S(2)}, u32[]{:S(2)}) %collective-permute-start.20) | collective-permute-done | bytes 65568 | tf_op jit(solution)/shard_map/ppermute | solution.py:27
  61.7 0.8 %collective-permute-done.18.refs_1_ = bf16[16,2048]{1,0:T(8,128)(2,1)S(1)} collective-permute-done((bf16[16,2048]{1,0:T(8,128)(2,1)S(1)}, bf16[16,2048]{1,0:T(8,128)(2,1)S(1)}, u32[]{:S(2)}, u32[]{:S(2)}) %collective-permute-start.18) | collective-permute-done | bytes 65568 | tf_op jit(solution)/shard_map/ppermute | solution.py:27
  62.6 0.7 %final.1 = f32[8,2,2048]{2,1,0:T(2,128)} custom-call(bf16[16,2048]{1,0:T(8,128)(2,1)S(1)} %output.1.refs_0_, bf16[16,2048]{1,0:T(8,128)(2,1)S(1)} %collective-permute-done.18.refs_1_, bf16[16,2048]{1,0:T(8,128)(2,1)S(1)} %collective-permute-done.19.refs_2_, bf16[16,2048]{1,0:T(8,128)(2,1)S(1)} %collective-permute-done.20.refs_3_, bf16[8,2,2048]{2,1,0:T(2,128)(2,1)S(1)} %copy-done), custom_call_target="tpu_custom_call" | custom-call | tf_op jit(solution)/shard_map/final/pallas_call | solution.py:689
  (32 shorter events, 3.1 us)
Async XLA Ops:
  0.0 10.8 %copy-start.1 = (bf16[2,2,2048]{2,1,0:T(2,128)(2,1)S(1)}, bf16[2,2,2048]{2,1,0:T(2,128)(2,1)}, u32[]{:S(2)}) copy-start(bf16[2,2,2048]{2,1,0:T(2,128)(2,1)} %refs_0_.1) | copy-start | bytes 49156
  0.0 10.8 %copy-start.4 = (bf16[2,2,512]{2,1,0:T(2,128)(2,1)S(1)}, bf16[2,2,512]{2,1,0:T(2,128)(2,1)}, u32[]{:S(2)}) copy-start(bf16[2,2,512]{2,1,0:T(2,128)(2,1)} %refs_4_.2) | copy-start | bytes 12292
  0.0 10.8 %collective-permute-start.1 = (bf16[2,2,2048]{2,1,0:T(2,128)(2,1)}, bf16[2,2,2048]{2,1,0:T(2,128)(2,1)S(1)}, u32[]{:S(2)}, u32[]{:S(2)}) collective-permute-start(bf16[2,2,2048]{2,1,0:T(2,128)(2,1)} %refs_0_.1), channel_id=1, source_target_pairs={{0,2},{1,3},{2,0},{3,1},{4,6},{5,7},{6,4},{7,5},{8,10},{9,11},{10,... | collective-permute-start | bytes 49160 | tf_op jit(solution)/shard_map/ppermute | solution.py:27
  4.0 6.8 %collective-permute-start = (bf16[2,2,2048]{2,1,0:T(2,128)(2,1)}, bf16[2,2,2048]{2,1,0:T(2,128)(2,1)S(1)}, u32[]{:S(2)}, u32[]{:S(2)}) collective-permute-start(bf16[2,2,2048]{2,1,0:T(2,128)(2,1)} %refs_0_.1), channel_id=1, source_target_pairs={{0,3},{1,2},{2,1},{3,0},{4,7},{5,6},{6,5},{7,4},{8,11},{9,10},{10,... | collective-permute-start | bytes 49160 | tf_op jit(solution)/shard_map/ppermute | solution.py:27
  5.4 5.4 %collective-permute-start.2 = (bf16[2,2,2048]{2,1,0:T(2,128)(2,1)}, bf16[2,2,2048]{2,1,0:T(2,128)(2,1)S(1)}, u32[]{:S(2)}, u32[]{:S(2)}) collective-permute-start(bf16[2,2,2048]{2,1,0:T(2,128)(2,1)} %refs_0_.1), channel_id=1, source_target_pairs={{0,1},{1,0},{2,3},{3,2},{4,5},{5,4},{6,7},{7,6},{8,9},{9,8},{10,11... | collective-permute-start | bytes 49160 | tf_op jit(solution)/shard_map/ppermute | solution.py:27
  10.8 2.4 %copy-start.2 = (s32[104]{0:T(128)}, s32[104]{0:T(128)S(1)}, u32[]{:S(2)}) copy-start(s32[104]{0:T(128)S(1)} %get-tuple-element.40.refs_5_.refs_4_.refs_6_) | copy-start | bytes 1252
  11.0 5.8 %collective-permute-start.5 = (bf16[2,144,128]{2,1,0:T(8,128)(2,1)S(1)}, bf16[2,144,128]{2,1,0:T(8,128)(2,1)S(1)}, u32[]{:S(2)}, u32[]{:S(2)}) collective-permute-start(bf16[2,144,128]{2,1,0:T(8,128)(2,1)S(1)} %turned.1.after.refs_0_), channel_id=1, source_target_pairs={{0,8},{4,12},{8,0},{12,4},{1,9},{5,13},{9,1},{13,5},{2,10},{6,14},... | collective-permute-start | bytes 221192 | tf_op jit(solution)/shard_map/ppermute | solution.py:27
  12.6 4.4 %collective-permute-start.4 = (bf16[2,144,128]{2,1,0:T(8,128)(2,1)S(1)}, bf16[2,144,128]{2,1,0:T(8,128)(2,1)S(1)}, u32[]{:S(2)}, u32[]{:S(2)}) collective-permute-start(bf16[2,144,128]{2,1,0:T(8,128)(2,1)S(1)} %turned.1.after.refs_0_), channel_id=1, source_target_pairs={{0,12},{4,8},{8,4},{12,0},{1,13},{5,9},{9,5},{13,1},{2,14},{6,10},... | collective-permute-start | bytes 221192 | tf_op jit(solution)/shard_map/ppermute | solution.py:27
  12.6 4.4 %collective-permute-start.3 = (bf16[2,144,128]{2,1,0:T(8,128)(2,1)S(1)}, bf16[2,144,128]{2,1,0:T(8,128)(2,1)S(1)}, u32[]{:S(2)}, u32[]{:S(2)}) collective-permute-start(bf16[2,144,128]{2,1,0:T(8,128)(2,1)S(1)} %turned.1.after.refs_0_), channel_id=1, source_target_pairs={{0,4},{4,0},{8,12},{12,8},{1,5},{5,1},{9,13},{13,9},{2,6},{6,2},{1... | collective-permute-start | bytes 221192 | tf_op jit(solution)/shard_map/ppermute | solution.py:27
  18.5 7.1 %collective-permute-start.6 = (bf16[32,1024]{1,0:T(8,128)(2,1)S(1)}, bf16[32,1024]{1,0:T(8,128)(2,1)S(1)}, u32[]{:S(2)}, u32[]{:S(2)}) collective-permute-start(bf16[32,1024]{1,0:T(8,128)(2,1)S(1)} %get-tuple-element.42), channel_id=1, source_target_pairs={{0,2},{1,3},{2,0},{3,1},{4,6},{5,7},{6,4},{7,5},{8,10},{9,11},{10,... | collective-permute-start | bytes 196616 | tf_op jit(solution)/shard_map/ppermute | solution.py:27
  21.3 6.3 %collective-permute-start.7 = (bf16[32,1024]{1,0:T(8,128)(2,1)S(1)}, bf16[32,1024]{1,0:T(8,128)(2,1)S(1)}, u32[]{:S(2)}, u32[]{:S(2)}) collective-permute-start(bf16[32,1024]{1,0:T(8,128)(2,1)S(1)} %get-tuple-element.43), channel_id=1, source_target_pairs={{0,3},{1,2},{2,1},{3,0},{4,7},{5,6},{6,5},{7,4},{8,11},{9,10},{10,... | collective-permute-start | bytes 196616 | tf_op jit(solution)/shard_map/ppermute | solution.py:27
  22.7 5.1 %collective-permute-start.8 = (bf16[32,1024]{1,0:T(8,128)(2,1)S(1)}, bf16[32,1024]{1,0:T(8,128)(2,1)S(1)}, u32[]{:S(2)}, u32[]{:S(2)}) collective-permute-start(bf16[32,1024]{1,0:T(8,128)(2,1)S(1)} %get-tuple-element.44), channel_id=1, source_target_pairs={{0,1},{1,0},{2,3},{3,2},{4,5},{5,4},{6,7},{7,6},{8,9},{9,8},{10,11... | collective-permute-start | bytes 196616 | tf_op jit(solution)/shard_map/ppermute | solution.py:27
  22.7 5.1 %copy-start.3 = (s32[104]{0:T(128)S(1)}, s32[104]{0:T(128)}, u32[]{:S(2)}) copy-start(s32[104]{0:T(128)} %copy-done.2) | copy-start | bytes 1252
  28.6 6.9 %collective-permute-start.11 = (bf16[32,1024]{1,0:T(8,128)(2,1)S(1)}, bf16[32,1024]{1,0:T(8,128)(2,1)S(1)}, u32[]{:S(2)}, u32[]{:S(2)}) collective-permute-start(bf16[32,1024]{1,0:T(8,128)(2,1)S(1)} %get-tuple-element.48.refs_0_), channel_id=1, source_target_pairs={{0,2},{1,3},{2,0},{3,1},{4,6},{5,7},{6,4},{7,5},{8,10},{9,11},{10,... | collective-permute-start | bytes 196616 | tf_op jit(solution)/shard_map/ppermute | solution.py:27
  30.5 6.2 %collective-permute-start.10 = (bf16[32,1024]{1,0:T(8,128)(2,1)S(1)}, bf16[32,1024]{1,0:T(8,128)(2,1)S(1)}, u32[]{:S(2)}, u32[]{:S(2)}) collective-permute-start(bf16[32,1024]{1,0:T(8,128)(2,1)S(1)} %get-tuple-element.48.refs_0_), channel_id=1, source_target_pairs={{0,3},{1,2},{2,1},{3,0},{4,7},{5,6},{6,5},{7,4},{8,11},{9,10},{10,... | collective-permute-start | bytes 196616 | tf_op jit(solution)/shard_map/ppermute | solution.py:27
  31.7 5.2 %collective-permute-start.9 = (bf16[32,1024]{1,0:T(8,128)(2,1)S(1)}, bf16[32,1024]{1,0:T(8,128)(2,1)S(1)}, u32[]{:S(2)}, u32[]{:S(2)}) collective-permute-start(bf16[32,1024]{1,0:T(8,128)(2,1)S(1)} %get-tuple-element.48.refs_0_), channel_id=1, source_target_pairs={{0,1},{1,0},{2,3},{3,2},{4,5},{5,4},{6,7},{7,6},{8,9},{9,8},{10,11... | collective-permute-start | bytes 196616 | tf_op jit(solution)/shard_map/ppermute | solution.py:27
  38.1 6.6 %collective-permute-start.12 = (bf16[8,32,128]{2,1,0:T(8,128)(2,1)S(1)}, bf16[8,32,128]{2,1,0:T(8,128)(2,1)S(1)}, u32[]{:S(2)}, u32[]{:S(2)}) collective-permute-start(bf16[8,32,128]{2,1,0:T(8,128)(2,1)S(1)} %get-tuple-element.52), channel_id=1, source_target_pairs={{0,2},{1,3},{2,0},{3,1},{4,6},{5,7},{6,4},{7,5},{8,10},{9,11},{10,... | collective-permute-start | bytes 196616 | tf_op jit(solution)/shard_map/ppermute | solution.py:27
  39.8 6.2 %collective-permute-start.13 = (bf16[8,32,128]{2,1,0:T(8,128)(2,1)S(1)}, bf16[8,32,128]{2,1,0:T(8,128)(2,1)S(1)}, u32[]{:S(2)}, u32[]{:S(2)}) collective-permute-start(bf16[8,32,128]{2,1,0:T(8,128)(2,1)S(1)} %get-tuple-element.53), channel_id=1, source_target_pairs={{0,3},{1,2},{2,1},{3,0},{4,7},{5,6},{6,5},{7,4},{8,11},{9,10},{10,... | collective-permute-start | bytes 196616 | tf_op jit(solution)/shard_map/ppermute | solution.py:27
  41.1 5.0 %collective-permute-start.14 = (bf16[8,32,128]{2,1,0:T(8,128)(2,1)S(1)}, bf16[8,32,128]{2,1,0:T(8,128)(2,1)S(1)}, u32[]{:S(2)}, u32[]{:S(2)}) collective-permute-start(bf16[8,32,128]{2,1,0:T(8,128)(2,1)S(1)} %get-tuple-element.54), channel_id=1, source_target_pairs={{0,1},{1,0},{2,3},{3,2},{4,5},{5,4},{6,7},{7,6},{8,9},{9,8},{10,11... | collective-permute-start | bytes 196616 | tf_op jit(solution)/shard_map/ppermute | solution.py:27
  46.2 4.4 %collective-permute-start.17 = (bf16[9,32,128]{2,1,0:T(8,128)(2,1)S(1)}, bf16[9,32,128]{2,1,0:T(8,128)(2,1)S(1)}, u32[]{:S(2)}, u32[]{:S(2)}) collective-permute-start(bf16[9,32,128]{2,1,0:T(8,128)(2,1)S(1)} %summed.1.refs_0_), channel_id=1, source_target_pairs={{0,8},{4,12},{8,0},{12,4},{1,9},{5,13},{9,1},{13,5},{2,10},{6,14},... | collective-permute-start | bytes 221192 | tf_op jit(solution)/shard_map/ppermute | solution.py:27
  47.8 4.4 %collective-permute-start.16 = (bf16[9,32,128]{2,1,0:T(8,128)(2,1)S(1)}, bf16[9,32,128]{2,1,0:T(8,128)(2,1)S(1)}, u32[]{:S(2)}, u32[]{:S(2)}) collective-permute-start(bf16[9,32,128]{2,1,0:T(8,128)(2,1)S(1)} %summed.1.refs_0_), channel_id=1, source_target_pairs={{0,12},{4,8},{8,4},{12,0},{1,13},{5,9},{9,5},{13,1},{2,14},{6,10},... | collective-permute-start | bytes 221192 | tf_op jit(solution)/shard_map/ppermute | solution.py:27
  47.8 4.4 %collective-permute-start.15 = (bf16[9,32,128]{2,1,0:T(8,128)(2,1)S(1)}, bf16[9,32,128]{2,1,0:T(8,128)(2,1)S(1)}, u32[]{:S(2)}, u32[]{:S(2)}) collective-permute-start(bf16[9,32,128]{2,1,0:T(8,128)(2,1)S(1)} %summed.1.refs_0_), channel_id=1, source_target_pairs={{0,4},{4,0},{8,12},{12,8},{1,5},{5,1},{9,13},{13,9},{2,6},{6,2},{1... | collective-permute-start | bytes 221192 | tf_op jit(solution)/shard_map/ppermute | solution.py:27
  52.2 10.4 %copy-start = (bf16[8,2,2048]{2,1,0:T(2,128)(2,1)S(1)}, bf16[8,2,2048]{2,1,0:T(2,128)(2,1)}, u32[]{:S(2)}) copy-start(bf16[8,2,2048]{2,1,0:T(2,128)(2,1)} %refs_4_.3) | copy-start | bytes 196612
  53.7 8.0 %collective-permute-start.20 = (bf16[16,2048]{1,0:T(8,128)(2,1)S(1)}, bf16[16,2048]{1,0:T(8,128)(2,1)S(1)}, u32[]{:S(2)}, u32[]{:S(2)}) collective-permute-start(bf16[16,2048]{1,0:T(8,128)(2,1)S(1)} %output.1.refs_0_), channel_id=1, source_target_pairs={{0,2},{1,3},{2,0},{3,1},{4,6},{5,7},{6,4},{7,5},{8,10},{9,11},{10,... | collective-permute-start | bytes 196616 | tf_op jit(solution)/shard_map/ppermute | solution.py:27
  54.8 6.9 %collective-permute-start.19 = (bf16[16,2048]{1,0:T(8,128)(2,1)S(1)}, bf16[16,2048]{1,0:T(8,128)(2,1)S(1)}, u32[]{:S(2)}, u32[]{:S(2)}) collective-permute-start(bf16[16,2048]{1,0:T(8,128)(2,1)S(1)} %output.1.refs_0_), channel_id=1, source_target_pairs={{0,3},{1,2},{2,1},{3,0},{4,7},{5,6},{6,5},{7,4},{8,11},{9,10},{10,... | collective-permute-start | bytes 196616 | tf_op jit(solution)/shard_map/ppermute | solution.py:27
  56.7 5.9 %collective-permute-start.18 = (bf16[16,2048]{1,0:T(8,128)(2,1)S(1)}, bf16[16,2048]{1,0:T(8,128)(2,1)S(1)}, u32[]{:S(2)}, u32[]{:S(2)}) collective-permute-start(bf16[16,2048]{1,0:T(8,128)(2,1)S(1)} %output.1.refs_0_), channel_id=1, source_target_pairs={{0,1},{1,0},{2,3},{3,2},{4,5},{5,4},{6,7},{7,6},{8,9},{9,8},{10,11... | collective-permute-start | bytes 196616 | tf_op jit(solution)/shard_map/ppermute | solution.py:27
